TPU v7x, 32 devices: a whole 2x2x4 slice. The times are simulated.
32 devices in a mesh: rep: 8 (over y, x, core), shard: 4 (over z).
Axes of the slice: x: 2, y: 2, z: 4, core: 2. Of those that a mesh axis runs over, the one named last changes fastest.
Arguments:
- tokens: bfloat16 [5120, 1536], P(('rep', 'shard')), may hold values from -6 to 6
- segment_ids: int32 [8, 640], P('rep'), may hold values from 0 to 2, never falling along the last dimension, each value on 1 to 512 neighbouring positions
- first_gain: bfloat16 [1536], P('shard'), may hold values from 0.5 to 1.5
- input_weight: bfloat16 [1536, 2048], P('shard'), may hold values from -0.15625 to 0.15625
- input_bias: bfloat16 [2048], P('shard'), may hold values from -0.625 to 0.625
- output_weight: bfloat16 [1536, 1536], P('shard'), may hold values from -0.875 to 0.875
- second_gain: bfloat16 [1536], P('shard'), may hold values from 0.5 to 1.5
- gate_weight: bfloat16 [1536, 8960], P('shard'), may hold values from -0.15625 to 0.15625
- up_weight: bfloat16 [1536, 8960], P('shard'), may hold values from -0.15625 to 0.15625
- down_weight: bfloat16 [8960, 1536], P('shard'), may hold values from -0.0625 to 0.0625
- output_cotangent: bfloat16 [5120, 1536], P(('rep', 'shard')), may hold values from -6 to 6
Outputs:
- block_out: bfloat16 [5120, 1536], P(('rep', 'shard'))
- tokens_gradient: bfloat16 [5120, 1536], P(('rep', 'shard'))
- first_gain_gradient: float32 [1536], P('shard')
- input_weight_gradient: float32 [1536, 2048], P('shard')
- input_bias_gradient: float32 [1792], P('shard')
- value_bias_gradient: float32 [256], P('shard')
- output_weight_gradient: float32 [1536, 1536], P('shard')
- second_gain_gradient: float32 [1536], P('shard')
- gate_weight_gradient: float32 [1536, 8960], P('shard')
- up_weight_gradient: float32 [1536, 8960], P('shard')
- down_weight_gradient: float32 [8960, 1536], P('shard')
Inputs may be any that keep to these rules, and one draw needn't show every extreme that they name: `segment_ids`: in every row the numbers never fall and each of 0 to 2 appears; a sequence has 1 to 512 tokens, and in every row one has exactly 512.
All inputs are finite; a program needn't handle non-finite values.
Results may differ from a plain program's by a relative error of at most 0.02.
Values may be sent and summed in bfloat16 or wider, within the bound.
No kernel may reach another device: no remote copies, remote signals or barrier semaphores. Data moves between devices by JAX's collectives and lax.ppermute only.
A program may use at most 448 MiB of HBM per device.

v0:
```python
import math

import jax
import jax.numpy as jnp
from jax import lax
from jax.sharding import PartitionSpec as P

QH = 12
KVH = 2
HD = 128
SEQS = 3


EPSILON = 1e-06
LOG_THETA = math.log(1000000.0)
MASKED = -1e30


def rope_tables(places, head_width):
    half_width = head_width // 2
    frequency = jnp.exp(jnp.arange(half_width, dtype=jnp.float32) * (-2.0 * LOG_THETA / head_width))
    angles = places.astype(jnp.float32)[:, None] * frequency[None, :]
    angles = jnp.concatenate([angles, angles], axis=-1)
    return (jnp.cos(angles), jnp.sin(angles))


def positions(segments):
    labels = jnp.arange(SEQS, dtype=jnp.int32)
    starts = jnp.sum((segments[None, :] < labels[:, None]).astype(jnp.int32), axis=1)
    own_start = jnp.sum(jnp.where(segments[:, None] == labels[None, :], starts[None, :], 0), axis=1)
    return jnp.arange(segments.shape[0], dtype=jnp.int32) - own_start


def rotate(field_rows, cosine_table, sine_table):
    half_width = field_rows.shape[-1] // 2
    turned = jnp.concatenate([-field_rows[..., half_width:], field_rows[..., :half_width]], axis=-1)
    return field_rows * cosine_table[:, None, :] + turned * sine_table[:, None, :]


def rotate_back(gradient, cosine_table, sine_table):
    half_width = gradient.shape[-1] // 2
    moved_part = gradient * sine_table[:, None, :]
    turned = jnp.concatenate([moved_part[..., half_width:], -moved_part[..., :half_width]], axis=-1)
    return gradient * cosine_table[:, None, :] + turned


def transposed_times(left_side, right_side):
    return lax.dot_general(
        left_side, right_side, (((0,), (0,)), ((), ())), preferred_element_type=jnp.float32
    )


def times_transposed(left_side, right_side):
    return lax.dot_general(
        left_side, right_side, (((1,), (1,)), ((), ())), preferred_element_type=jnp.float32
    )


def norm_back(normed_gradient, unit_rows, inverse_rms, gain_row):
    scaled = normed_gradient * gain_row
    return inverse_rms * (scaled - unit_rows * jnp.mean(scaled * unit_rows, axis=-1, keepdims=True))


def on_device(
    tokens,
    segment_ids,
    first_gain,
    input_weight,
    input_bias,
    output_weight,
    second_gain,
    gate_weight,
    up_weight,
    down_weight,
    output_cotangent,
):
    shards = lax.axis_size("shard")
    my_rank = lax.axis_index("shard")
    own_rows = tokens.shape[0]
    segments = segment_ids[0]
    group_rows = segments.shape[0]
    per_group = QH // KVH
    query_width = QH * HD
    pair_width = KVH * HD
    score_scale = 1.0 / math.sqrt(HD)
    first_row = my_rank * own_rows
    places = positions(segments)
    own_segments = lax.dynamic_slice_in_dim(segments, first_row, own_rows)
    cosine_table, sine_table = rope_tables(
        lax.dynamic_slice_in_dim(places, first_row, own_rows), HD
    )
    wide_tokens = tokens.astype(jnp.float32)
    inverse_one = lax.rsqrt(jnp.mean(wide_tokens * wide_tokens, axis=-1, keepdims=True) + EPSILON)
    unit_one = wide_tokens * inverse_one
    input_matrix, output_matrix, gathered_bias, gathered_gain = (
        lax.all_gather(input_weight, "shard", axis=0, tiled=True),
        lax.all_gather(output_weight, "shard", axis=0, tiled=True),
        lax.all_gather(input_bias, "shard", axis=0, tiled=True),
        lax.all_gather(first_gain, "shard", axis=0, tiled=True),
    )
    gain_one = gathered_gain.astype(jnp.float32)
    normed_one = (unit_one * gain_one).astype(jnp.bfloat16)
    projected = jnp.dot(
        normed_one, input_matrix, preferred_element_type=jnp.float32
    ) + gathered_bias.astype(jnp.float32)
    queries = rotate(
        projected[:, :query_width].reshape(own_rows, QH, HD), cosine_table, sine_table
    ).astype(jnp.bfloat16)
    key_part = rotate(
        projected[:, query_width : query_width + pair_width].reshape(own_rows, KVH, HD),
        cosine_table,
        sine_table,
    )
    own_pairs = jnp.concatenate(
        [key_part.reshape(own_rows, pair_width), projected[:, query_width + pair_width :]], axis=1
    ).astype(jnp.bfloat16)
    all_pairs = lax.all_gather(own_pairs, "shard", axis=0, tiled=True)
    candidates = [
        option
        for option in range(1, shards + 1)
        if shards % option == 0 and option * own_rows >= 512
    ]
    per_step = candidates[0]
    block_rows = per_step * own_rows
    block_count = group_rows // block_rows
    pair_blocks = all_pairs.reshape(block_count, block_rows, 2 * pair_width)
    segment_blocks = segments.reshape(block_count, block_rows)
    index_blocks = jnp.arange(group_rows, dtype=jnp.int32).reshape(block_count, block_rows)
    block_inputs = (pair_blocks, segment_blocks, index_blocks)
    query_index = first_row + jnp.arange(own_rows, dtype=jnp.int32)
    grouped_queries = queries.reshape(own_rows, KVH, per_group, HD)

    def block_scores(inputs):
        pair_rows, block_segments, block_index = inputs
        block_keys = pair_rows[:, :pair_width].reshape(block_rows, KVH, HD)
        block_values = pair_rows[:, pair_width:].reshape(block_rows, KVH, HD)
        raw_scores = (
            jnp.einsum(
                "tkgd,jkd->kgtj", grouped_queries, block_keys, preferred_element_type=jnp.float32
            )
            * score_scale
        )
        allowed = (own_segments[:, None] == block_segments[None, :]) & (
            block_index[None, :] <= query_index[:, None]
        )
        return (raw_scores, allowed[None, None], block_keys, block_values)

    def max_pass(running, inputs):
        running_max, running_sum = running
        raw_scores, allowed, block_keys, block_values = block_scores(inputs)
        masked = jnp.where(allowed, raw_scores, MASKED)
        new_max = jnp.maximum(running_max, jnp.max(masked, axis=-1))
        running_sum = running_sum * jnp.exp(running_max - new_max) + jnp.sum(
            jnp.exp(masked - new_max[..., None]), axis=-1
        )
        return ((new_max, running_sum), None)

    start_max = jnp.full((KVH, per_group, own_rows), MASKED, jnp.float32)
    (top_score, score_sum), unused_out = lax.scan(
        max_pass, (start_max, jnp.zeros_like(start_max)), block_inputs
    )
    log_norm = top_score + jnp.log(score_sum)

    def value_pass(running, inputs):
        attended, remainder = running
        raw_scores, allowed, block_keys, block_values = block_scores(inputs)
        shares = jnp.where(allowed, jnp.exp(raw_scores - log_norm[..., None]), 0.0)
        shares_low = shares.astype(jnp.bfloat16)
        leftover = (shares - shares_low.astype(jnp.float32)).astype(jnp.bfloat16)
        attended = attended + jnp.einsum(
            "kgtj,jkd->tkgd", shares_low, block_values, preferred_element_type=jnp.float32
        )
        remainder = remainder + jnp.einsum(
            "kgtj,jkd->tkgd", leftover, block_values, preferred_element_type=jnp.float32
        )
        return ((attended, remainder), None)

    start_sum = jnp.zeros((own_rows, KVH, per_group, HD), jnp.float32)
    (attended, remainder), unused_out = lax.scan(value_pass, (start_sum, start_sum), block_inputs)
    exact_sum = attended + remainder
    attention_low = attended.reshape(own_rows, query_width).astype(jnp.bfloat16)
    hidden = wide_tokens + jnp.dot(attention_low, output_matrix, preferred_element_type=jnp.float32)
    gate_matrix, up_matrix, down_matrix, second_gathered = (
        lax.all_gather(gate_weight, "shard", axis=0, tiled=True),
        lax.all_gather(up_weight, "shard", axis=0, tiled=True),
        lax.all_gather(down_weight, "shard", axis=0, tiled=True),
        lax.all_gather(second_gain, "shard", axis=0, tiled=True),
    )
    gain_two = second_gathered.astype(jnp.float32)
    inverse_two = lax.rsqrt(jnp.mean(hidden * hidden, axis=-1, keepdims=True) + EPSILON)
    unit_two = hidden * inverse_two
    normed_two = (unit_two * gain_two).astype(jnp.bfloat16)
    gate_linear = jnp.dot(normed_two, gate_matrix, preferred_element_type=jnp.float32)
    up_linear = jnp.dot(normed_two, up_matrix, preferred_element_type=jnp.float32)
    gate_sigmoid = jax.nn.sigmoid(gate_linear)
    gate_output = gate_linear * gate_sigmoid
    inner_act = (gate_output * up_linear).astype(jnp.bfloat16)
    block_out = (
        hidden + jnp.dot(inner_act, down_matrix, preferred_element_type=jnp.float32)
    ).astype(jnp.bfloat16)
    gate_matrix, up_matrix, down_matrix = (
        lax.all_gather(gate_weight, "shard", axis=0, tiled=True),
        lax.all_gather(up_weight, "shard", axis=0, tiled=True),
        lax.all_gather(down_weight, "shard", axis=0, tiled=True),
    )
    out_wide = output_cotangent.astype(jnp.float32)
    inner_gradient = times_transposed(output_cotangent, down_matrix)
    down_gradient = lax.psum_scatter(
        transposed_times(inner_act, output_cotangent).astype(jnp.bfloat16),
        "shard",
        scatter_dimension=0,
        tiled=True,
    )
    gate_gradient_rows = (
        inner_gradient * up_linear * gate_sigmoid * (1.0 + gate_linear * (1.0 - gate_sigmoid))
    ).astype(jnp.bfloat16)
    up_gradient_rows = (inner_gradient * gate_output).astype(jnp.bfloat16)
    normed_two_gradient = times_transposed(gate_gradient_rows, gate_matrix) + times_transposed(
        up_gradient_rows, up_matrix
    )
    both_gradients = jnp.concatenate([gate_gradient_rows, up_gradient_rows], axis=1)
    hidden_units = gate_weight.shape[1]
    gate_up_gradient = lax.psum_scatter(
        transposed_times(normed_two, both_gradients).astype(jnp.bfloat16),
        "shard",
        scatter_dimension=0,
        tiled=True,
    )
    gain_two_gradient = jnp.sum(normed_two_gradient * unit_two, axis=0)
    hidden_gradient = out_wide + norm_back(normed_two_gradient, unit_two, inverse_two, gain_two)
    branch_gradient = hidden_gradient.astype(jnp.bfloat16)
    input_matrix, output_matrix = (
        lax.all_gather(input_weight, "shard", axis=0, tiled=True),
        lax.all_gather(output_weight, "shard", axis=0, tiled=True),
    )
    output_gradient = lax.psum_scatter(
        transposed_times(attention_low, branch_gradient).astype(jnp.bfloat16),
        "shard",
        scatter_dimension=0,
        tiled=True,
    )
    attention_gradient = times_transposed(branch_gradient, output_matrix).astype(jnp.bfloat16)
    grouped_gradient = attention_gradient.reshape(own_rows, KVH, per_group, HD)
    share_dot = jnp.transpose(
        jnp.sum(grouped_gradient.astype(jnp.float32) * exact_sum, axis=-1), (1, 2, 0)
    )

    def grad_pass(query_gradient, inputs):
        raw_scores, allowed, block_keys, block_values = block_scores(inputs)
        shares = jnp.where(allowed, jnp.exp(raw_scores - log_norm[..., None]), 0.0)
        shares_low = shares.astype(jnp.bfloat16)
        share_gradient = jnp.einsum(
            "tkgd,jkd->kgtj", grouped_gradient, block_values, preferred_element_type=jnp.float32
        )
        score_gradient = (shares * (share_gradient - share_dot[..., None])).astype(jnp.bfloat16)
        query_gradient = query_gradient + jnp.einsum(
            "kgtj,jkd->tkgd", score_gradient, block_keys, preferred_element_type=jnp.float32
        )
        key_gradient = (
            jnp.einsum(
                "kgtj,tkgd->jkd",
                score_gradient,
                grouped_queries,
                preferred_element_type=jnp.float32,
            )
            * score_scale
        )
        value_gradient = jnp.einsum(
            "kgtj,tkgd->jkd", shares_low, grouped_gradient, preferred_element_type=jnp.float32
        )
        return (
            query_gradient,
            jnp.concatenate(
                [
                    key_gradient.reshape(block_rows, pair_width),
                    value_gradient.reshape(block_rows, pair_width),
                ],
                axis=1,
            ),
        )

    query_gradient, pair_gradient_blocks = lax.scan(grad_pass, start_sum, block_inputs)
    pair_gradients = lax.psum_scatter(
        pair_gradient_blocks.reshape(group_rows, 2 * pair_width).astype(jnp.bfloat16),
        "shard",
        scatter_dimension=0,
        tiled=True,
    ).astype(jnp.float32)
    query_back = rotate_back(
        (query_gradient * score_scale).reshape(own_rows, QH, HD), cosine_table, sine_table
    ).reshape(own_rows, query_width)
    key_back = rotate_back(
        pair_gradients[:, :pair_width].reshape(own_rows, KVH, HD), cosine_table, sine_table
    ).reshape(own_rows, pair_width)
    projected_gradient = jnp.concatenate(
        [query_back, key_back, pair_gradients[:, pair_width:]], axis=1
    ).astype(jnp.bfloat16)
    bias_gradient = jnp.sum(projected_gradient.astype(jnp.float32), axis=0)
    bias_split = query_width + pair_width
    normed_one_gradient = times_transposed(projected_gradient, input_matrix)
    input_gradient = lax.psum_scatter(
        transposed_times(normed_one, projected_gradient).astype(jnp.bfloat16),
        "shard",
        scatter_dimension=0,
        tiled=True,
    )
    gain_one_gradient = jnp.sum(normed_one_gradient * unit_one, axis=0)
    tokens_gradient = (
        hidden_gradient + norm_back(normed_one_gradient, unit_one, inverse_one, gain_one)
    ).astype(jnp.bfloat16)
    small_sums = (
        lax.psum_scatter(gain_one_gradient, "shard", scatter_dimension=0, tiled=True),
        lax.psum_scatter(gain_two_gradient, "shard", scatter_dimension=0, tiled=True),
        lax.psum_scatter(bias_gradient[:bias_split], "shard", scatter_dimension=0, tiled=True),
        lax.psum_scatter(bias_gradient[bias_split:], "shard", scatter_dimension=0, tiled=True),
    )
    totals = (
        lax.psum(input_gradient, "rep").astype(jnp.float32),
        lax.psum(output_gradient, "rep").astype(jnp.float32),
        lax.psum(gate_up_gradient, "rep").astype(jnp.float32),
        lax.psum(down_gradient, "rep").astype(jnp.float32),
        lax.psum(small_sums[0].astype(jnp.bfloat16), "rep").astype(jnp.float32),
        lax.psum(small_sums[1].astype(jnp.bfloat16), "rep").astype(jnp.float32),
        lax.psum(small_sums[2].astype(jnp.bfloat16), "rep").astype(jnp.float32),
        lax.psum(small_sums[3].astype(jnp.bfloat16), "rep").astype(jnp.float32),
    )
    return (
        block_out,
        tokens_gradient,
        totals[4],
        totals[0],
        totals[6],
        totals[7],
        totals[1],
        totals[5],
        totals[2][:, :hidden_units],
        totals[2][:, hidden_units:],
        totals[3],
    )


def solution(mesh):
    placed = (
        P(("rep", "shard"), None),
        P("rep", None),
        P("shard"),
        P("shard", None),
        P("shard"),
        P("shard", None),
        P("shard"),
        P("shard", None),
        P("shard", None),
        P("shard", None),
        P(("rep", "shard"), None),
    )
    return jax.shard_map(
        on_device,
        mesh=mesh,
        in_specs=placed,
        out_specs=(
            P(("rep", "shard"), None),
            P(("rep", "shard"), None),
            P("shard"),
            P("shard", None),
            P("shard"),
            P("shard"),
            P("shard", None),
            P("shard"),
            P("shard", None),
            P("shard", None),
            P("shard", None),
        ),
        check_vma=False,
    )
```

profile of v0, /device:TPU:0, one launch (start us, length us, event | category | flops | bytes accessed | tf_op | source)
XLA Modules:
  0.0 3600.1 jit_solution(6588939777055080525)
XLA Ops:
  10.7 13.6 all-gather.1
  24.3 12.1 all-gather
  36.5 13.6 all-gather.2
  52.0 75.8 %all-gather.9.cloned.1.call-done = bf16[1536,2048]{1,0:T(8,128)(2,1)} async-done(((bf16[384,2048]{1,0:T(8,128)(2,1)}), bf16[1536,2048]{1,0:T(8,128)(2,1)}) %all-gather.9.cloned.1.call-update) | async-done | bytes 6291472 | tf_op jit(solution)/shard_map/all_gather | solution.py:96
  136.2 28.0 all_gather.35
  189.0 36.9 %all-gather.11.cloned.1.call-done = bf16[1536,1536]{1,0:T(8,128)(2,1)} async-done(((bf16[384,1536]{1,0:T(8,128)(2,1)}), bf16[1536,1536]{1,0:T(8,128)(2,1)}) %all-gather.11.cloned.1.call-update) | async-done | bytes 4718608 | tf_op jit(solution)/shard_map/all_gather | solution.py:97
  229.5 461.6 %all-gather.13.cloned.1.call-done = bf16[1536,8960]{1,0:T(8,128)(2,1)} async-done(((bf16[384,8960]{1,0:T(8,128)(2,1)}), bf16[1536,8960]{1,0:T(8,128)(2,1)}) %all-gather.13.cloned.1.call-update) | async-done | bytes 27525136 | tf_op jit(solution)/shard_map/all_gather | solution.py:184
  691.0 17.2 fusion.71
  708.2 445.9 %all-gather.15.cloned.1.call-done = bf16[1536,8960]{1,0:T(8,128)(2,1)} async-done(((bf16[384,8960]{1,0:T(8,128)(2,1)}), bf16[1536,8960]{1,0:T(8,128)(2,1)}) %all-gather.15.cloned.1.call-update) | async-done | bytes 27525136 | tf_op jit(solution)/shard_map/all_gather | solution.py:185
  1154.1 16.2 fusion.72
  1170.3 446.8 %all-gather.17.cloned.1.call-done = bf16[8960,1536]{1,0:T(8,128)(2,1)} async-done(((bf16[2240,1536]{1,0:T(8,128)(2,1)}), bf16[8960,1536]{1,0:T(8,128)(2,1)}) %all-gather.17.cloned.1.call-update) | async-done | bytes 27525136 | tf_op jit(solution)/shard_map/all_gather | solution.py:186
  1617.2 19.8 multiply_convert_fusion
  1637.0 14.9 fusion.73
  1651.9 16.1 multiply_reduce_fusion
  1669.6 4.0 convolution_convert_fusion.4
  1675.1 4.8 fusion.24
  1683.0 4.5 fusion.5
  1705.1 6.2 reduce-scatter.6.cloned.1.call-done
  1713.8 4.6 convolution_convert_fusion.2
  1719.6 14.8 convolution_convert_fusion.1
  1735.4 23.9 convolution_convert_fusion
  1759.7 38.6 %reduce-scatter.10.cloned.1.call-done = bf16[384,1536]{1,0:T(8,128)(2,1)} async-done(((bf16[1536,1536]{1,0:T(8,128)(2,1)}), bf16[384,1536]{1,0:T(8,128)(2,1)}) %reduce-scatter.10.cloned.1.call-update) | async-done | bytes 1179664 | tf_op jit(solution)/shard_map/reduce_scatter | solution.py:236
  1798.3 114.2 %reduce-scatter.8.cloned.1.call-done = bf16[384,2048]{1,0:T(8,128)(2,1)} async-done(((bf16[1536,2048]{1,0:T(8,128)(2,1)}), bf16[384,2048]{1,0:T(8,128)(2,1)}) %reduce-scatter.8.cloned.1.call-update) | async-done | bytes 1572880 | tf_op jit(solution)/shard_map/reduce_scatter | solution.py:301
  1912.5 455.0 %reduce-scatter.14.cloned.1.call-done = bf16[2240,1536]{1,0:T(8,128)(2,1)} async-done(((bf16[8960,1536]{1,0:T(8,128)(2,1)}), bf16[2240,1536]{1,0:T(8,128)(2,1)}) %reduce-scatter.14.cloned.1.call-update) | async-done | bytes 6881296 | tf_op jit(solution)/shard_map/reduce_scatter | solution.py:208
  2367.5 901.0 %reduce-scatter.12.cloned.1.call-done = bf16[384,17920]{1,0:T(8,128)(2,1)} async-done(((bf16[1536,17920]{1,0:T(8,128)(2,1)}), bf16[384,17920]{1,0:T(8,128)(2,1)}) %reduce-scatter.12.cloned.1.call-update) | async-done | bytes 13762576 | tf_op jit(solution)/shard_map/reduce_scatter | solution.py:223
  3271.7 16.2 fusion.12
  3288.1 5.4 fusion.32
  3293.5 20.1 all-reduce.4
  3313.9 12.4 all-reduce.5
  3329.6 235.9 %all-reduce.9.cloned.1.call-done = (bf16[384,2048]{1,0:T(8,128)(2,1)}, bf16[384,1536]{1,0:T(8,128)(2,1)}, bf16[384,17920]{1,0:T(8,128)(2,1)}, bf16[2240,1536]{1,0:T(8,128)(2,1)}) async-done(((bf16[384,2048]{1,0:T(8,128)(2,1)}, bf16[384,1536]{1,0:T(8,128)(2,1)}, bf16[384,17920]{1,0:T(8,128)(2,1)}, bf16[2240,1536]{1,0:T(8,128)(2,1)}), (bf16[384,2048]{1,0:T(8,128)(2,1)}, bf16[384,1536]{1,0:T(8,128)(2,1)}, ...) | async-done | bytes 23396368 | tf_op jit(solution)/shard_map/psum | solution.py:318
  3570.8 15.4 fusion.66
  3586.2 7.1 convert_element_type.178
  (204 shorter events, 80.5 us)
Async XLA Ops:
  7.2 120.7 %all-gather.9.cloned.1.call-start = ((), (), s32[]{:S(2)}) async-start(), calls=%async_computation.5 | async-start | bytes 7864320 | tf_op jit(solution)/shard_map/all_gather | solution.py:96
  7.9 218.0 %all-gather.11.cloned.1.call-start = ((), (), s32[]{:S(2)}) async-start(), calls=%async_computation.6 | async-start | bytes 5898240 | tf_op jit(solution)/shard_map/all_gather | solution.py:97
  8.7 682.4 %all-gather.13.cloned.1.call-start = ((), (), s32[]{:S(2)}) async-start(), calls=%async_computation.7 | async-start | bytes 34406400 | tf_op jit(solution)/shard_map/all_gather | solution.py:184
  9.4 1144.7 %all-gather.15.cloned.1.call-start = ((), (), s32[]{:S(2)}) async-start(), calls=%async_computation.8 | async-start | bytes 34406400 | tf_op jit(solution)/shard_map/all_gather | solution.py:185
  10.0 14.3 copy-start.37
  10.0 26.4 copy-start.35
  10.0 26.4 copy-start.38
  10.0 41.0 %copy-start.1 = (bf16[160,1536]{1,0:T(8,128)(2,1)S(1)}, bf16[160,1536]{1,0:T(8,128)(2,1)}, u32[]{:S(2)}) copy-start(bf16[160,1536]{1,0:T(8,128)(2,1)} %param.11) | copy-start | bytes 1474564
  10.0 1607.1 %all-gather.17.cloned.1.call-start = ((), (), s32[]{:S(2)}) async-start(), calls=%async_computation.9 | async-start | bytes 34406400 | tf_op jit(solution)/shard_map/all_gather | solution.py:186
  10.6 1700.6 %reduce-scatter.6.cloned.1.call-start = ((), (), s32[]{:S(2)}) async-start(), calls=%async_computation.10 | async-start | bytes 819200 | tf_op jit(solution)/shard_map/reduce_scatter | solution.py:283
  51.0 83.9 %copy-start.17 = (f32[160,128]{1,0:T(8,128)}, f32[160,128]{1,0:T(8,128)S(1)}, u32[]{:S(2)}) copy-start(f32[160,128]{1,0:T(8,128)S(1)} %get-tuple-element.138) | copy-start | bytes 245764
  51.0 84.1 %copy-start.27 = (f32[160,128]{1,0:T(8,128)}, f32[160,128]{1,0:T(8,128)S(1)}, u32[]{:S(2)}) copy-start(f32[160,128]{1,0:T(8,128)S(1)} %get-tuple-element.137) | copy-start | bytes 245764
  135.2 33.5 copy-start.25
  167.3 11.9 copy-start.9
  189.0 40.3 %copy-start.7 = (bf16[160,1536]{1,0:T(8,128)(2,1)}, bf16[160,1536]{1,0:T(8,128)(2,1)S(1)}, u32[]{:S(2)}) copy-start(bf16[160,1536]{1,0:T(8,128)(2,1)S(1)} %convert_element_type.147) | copy-start | bytes 1474564
  229.3 1438.8 %copy-start.3 = (f32[160,1536]{1,0:T(8,128)}, f32[160,1536]{1,0:T(8,128)S(1)}, u32[]{:S(2)}) copy-start(f32[160,1536]{1,0:T(8,128)S(1)} %get-tuple-element.142) | copy-start | bytes 2949124
  229.5 924.6 %copy-start.5 = (bf16[160,1536]{1,0:T(8,128)(2,1)}, bf16[160,1536]{1,0:T(8,128)(2,1)S(1)}, u32[]{:S(2)}) copy-start(bf16[160,1536]{1,0:T(8,128)(2,1)S(1)} %multiply_convert_fusion.3) | copy-start | bytes 1474564
  708.2 908.9 %copy-start.19 = (bf16[160,1536]{1,0:T(8,128)(2,1)S(1)}, bf16[160,1536]{1,0:T(8,128)(2,1)}, u32[]{:S(2)}) copy-start(bf16[160,1536]{1,0:T(8,128)(2,1)} %param.21) | copy-start | bytes 1474564
  1651.9 16.2 copy-start.20
  1668.1 7.0 copy-start.23
  1673.7 6.2 slice-start
  1690.7 107.6 %reduce-scatter.10.cloned.1.call-start = ((), (), s32[]{:S(2)}) async-start(), calls=%async_computation.12 | async-start | bytes 5898240 | tf_op jit(solution)/shard_map/reduce_scatter | solution.py:236
  1694.4 7.7 copy-start.18
  1694.4 218.0 %reduce-scatter.8.cloned.1.call-start = ((), (), s32[]{:S(2)}) async-start(), calls=%async_computation.11 | async-start | bytes 7864320 | tf_op jit(solution)/shard_map/reduce_scatter | solution.py:301
  1703.2 9.6 copy-start.26
  1705.0 13.4 copy-start.10
  1718.4 649.1 %reduce-scatter.14.cloned.1.call-start = ((), (), s32[]{:S(2)}) async-start(), calls=%async_computation.14 | async-start | bytes 34406400 | tf_op jit(solution)/shard_map/reduce_scatter | solution.py:208
  1734.4 1534.1 %reduce-scatter.12.cloned.1.call-start = ((), (), s32[]{:S(2)}) async-start(), calls=%async_computation.13 | async-start | bytes 68812800 | tf_op jit(solution)/shard_map/reduce_scatter | solution.py:223
  1759.4 1806.2 %all-reduce.9.cloned.1.call-start = ((), (), s32[]{:S(2)}) async-start(), calls=%async_computation.15 | async-start | bytes 46792704 | tf_op jit(solution)/shard_map/psum | solution.py:318
  3271.7 16.2 copy-start.11
  3569.1 17.1 slice-start.2
  3570.8 15.4 slice-start.3
  (23 other events, 62.0 us)
Sparse Core Ops, SparseCore 0:
  9.6 118.2 all-gather.8
  129.4 96.4 all-gather.10
  227.5 463.5 all-gather.12
  692.5 461.5 all-gather.14
  1155.5 461.5 all-gather.16
  1690.8 20.3 reduce-scatter.5
  1714.1 84.1 reduce-scatter.9
  1801.1 111.2 reduce-scatter.7
  1914.8 452.6 reduce-scatter.13
  2369.8 898.6 reduce-scatter.11
  3272.8 292.6 all-reduce.8
where the time goes:
time: 3600 us
  waiting for transfers between devices  3220 us (89%)
  matrix products  182 us (5%)
  blocking collectives  99.7 us (3%)
  local copies, waits for them, and re-layouts  47.1 us (1%)
    reduce_scatter x1, waiting for transfers between devices, on_device(): lax.psum_scatter(transposed_times(normed_two, both_gradients).astype(jnp....  901 us
    all_gather x1, waiting for transfers between devices, on_device(): lax.all_gather(gate_weight, 'shard', axis=0, tiled=True)  462 us
    reduce_scatter x1, waiting for transfers between devices, on_device(): lax.psum_scatter(transposed_times(inner_act, output_cotangent).astype(jnp...  455 us
    all_gather x1, waiting for transfers between devices, on_device(): lax.all_gather(down_weight, 'shard', axis=0, tiled=True)  447 us
    all_gather x1, waiting for transfers between devices, on_device(): lax.all_gather(up_weight, 'shard', axis=0, tiled=True)  446 us
    psum x1, waiting for transfers between devices, on_device(): lax.psum(input_gradient, 'rep').astype(jnp.float32)  236 us
    reduce_scatter x1, waiting for transfers between devices, on_device(): lax.psum_scatter(transposed_times(normed_one, projected_gradient).astype(...  114 us
    all_gather x1, waiting for transfers between devices, on_device(): lax.all_gather(input_weight, 'shard', axis=0, tiled=True)  75.8 us
  transfers between devices with their start and end apart: 11, of which 11 were waited for; matrix products, arithmetic and copies ran while one was open for 4% of the time, Pallas kernels for 0%

commit v1 on v0

v1 whole, which is shorter than its diff:
```python
import math

import jax
import jax.numpy as jnp
from jax import lax
from jax.sharding import PartitionSpec as P

QH = 12
KVH = 2
HD = 128
SEQS = 3


EPSILON = 1e-06
LOG_THETA = math.log(1000000.0)
MASKED = -1e30


def rope_tables(places, head_width):
    half_width = head_width // 2
    frequency = jnp.exp(jnp.arange(half_width, dtype=jnp.float32) * (-2.0 * LOG_THETA / head_width))
    angles = places.astype(jnp.float32)[:, None] * frequency[None, :]
    angles = jnp.concatenate([angles, angles], axis=-1)
    return (jnp.cos(angles), jnp.sin(angles))


def positions(segments):
    labels = jnp.arange(SEQS, dtype=jnp.int32)
    starts = jnp.sum((segments[None, :] < labels[:, None]).astype(jnp.int32), axis=1)
    own_start = jnp.sum(jnp.where(segments[:, None] == labels[None, :], starts[None, :], 0), axis=1)
    return jnp.arange(segments.shape[0], dtype=jnp.int32) - own_start


def rotate(field_rows, cosine_table, sine_table):
    half_width = field_rows.shape[-1] // 2
    turned = jnp.concatenate([-field_rows[..., half_width:], field_rows[..., :half_width]], axis=-1)
    return field_rows * cosine_table[:, None, :] + turned * sine_table[:, None, :]


def rotate_back(gradient, cosine_table, sine_table):
    half_width = gradient.shape[-1] // 2
    moved_part = gradient * sine_table[:, None, :]
    turned = jnp.concatenate([moved_part[..., half_width:], -moved_part[..., :half_width]], axis=-1)
    return gradient * cosine_table[:, None, :] + turned


def transposed_times(left_side, right_side):
    return lax.dot_general(
        left_side, right_side, (((0,), (0,)), ((), ())), preferred_element_type=jnp.float32
    )


def times_transposed(left_side, right_side):
    return lax.dot_general(
        left_side, right_side, (((1,), (1,)), ((), ())), preferred_element_type=jnp.float32
    )


def norm_back(normed_gradient, unit_rows, inverse_rms, gain_row):
    scaled = normed_gradient * gain_row
    return inverse_rms * (scaled - unit_rows * jnp.mean(scaled * unit_rows, axis=-1, keepdims=True))


class Line:
    def __init__(self, name, size, place, pairs, crossed=False):
        self.name, self.size, self.place, self.pairs = name, size, place, pairs
        self.crossed = crossed

    def shift(self, value, step):
        return lax.ppermute(value, self.name, self.pairs(step % self.size))

    def behind(self, step):
        return lax.rem(self.place + (self.size - step % self.size), self.size)

    def ahead(self, step):
        return lax.rem(self.place + step % self.size, self.size)


def make_lines(reps, shards):
    inner = 2 if reps % 4 == 0 else 1
    outer = reps // (2 * inner)
    square = inner == outer

    def split(index):
        core, b, a = index % 2, (index // 2) % inner, index // (2 * inner)
        return core, b, a

    def join(core, b, a):
        return (a * inner + b) * 2 + core

    def first_pairs(step):
        pairs = []
        for index in range(reps):
            core, b, a = split(index)
            if square and core == 0:
                pairs.append((index, join(core, (b + step) % inner, a)))
            else:
                pairs.append((index, join(core, b, (a + step) % outer)))
        return pairs

    def second_pairs(step):
        pairs = []
        for index in range(reps):
            core, b, a = split(index)
            if square and core == 0:
                pairs.append((index, join(core, b, (a + step) % outer)))
            else:
                pairs.append((index, join(core, (b + step) % inner, a)))
        return pairs

    def core_pairs(step):
        pairs = []
        for index in range(reps):
            core, b, a = split(index)
            pairs.append((index, join((core + step) % 2, b, a)))
        return pairs

    def shard_pairs(step):
        return [(index, (index + step) % shards) for index in range(shards)]

    core, b, a = split(lax.axis_index("rep"))
    first, second = (jnp.where(core == 0, b, a), jnp.where(core == 0, a, b)) if square else (a, b)
    return (
        Line("shard", shards, lax.axis_index("shard"), shard_pairs),
        Line("rep", 2, core, core_pairs, square),
        Line("rep", outer, first, first_pairs),
        Line("rep", inner, second, second_pairs),
    )


def pick(array, index, axis):
    return lax.dynamic_index_in_dim(array, index, axis, keepdims=False)


def put(array, piece, index, axis):
    return lax.dynamic_update_index_in_dim(array, piece, index, axis)


def stack_by_place(pieces, line, axis=0):
    shape = list(pieces[0].shape)
    shape.insert(axis, line.size)
    held = jnp.zeros(shape, pieces[0].dtype)
    for step, piece in enumerate(pieces):
        held = put(held, piece, line.behind(step), axis)
    return held


def gather_line(value, line):
    return [value] + [line.shift(value, step) for step in range(1, line.size)]


def sum_line(blocks, line, axis):
    total = pick(blocks, line.place, axis).astype(jnp.float32)
    for step in range(1, line.size):
        total = total + line.shift(pick(blocks, line.ahead(step), axis), step).astype(jnp.float32)
    return total.astype(blocks.dtype)


def gather_rep(piece, core, first, second):
    held = [(0, 0, piece)]
    for step in range(1, second.size):
        held.append((0, step, second.shift(piece, step)))
    for step in range(1, first.size):
        held += [(step, at, first.shift(value, step)) for zero, at, value in held if zero == 0]
    placed = [
        (core.place, first.behind(one), second.behind(two), value) for one, two, value in held
    ]
    there, here = (second, first) if core.crossed else (first, second)
    for one, two, value in held:
        placed.append(
            (core.behind(1), there.behind(one), here.behind(two), core.shift(value, 1))
        )
    return [((c * first.size + f) * second.size + s, value) for c, f, s, value in placed]


def sum_rep(blocks, axis, core, first, second):
    shape = blocks.shape
    blocks = blocks.reshape(shape[:axis] + (2, first.size, second.size) + shape[axis + 1 :])
    for line in (core, first, second):
        blocks = sum_line(blocks, line, axis)
    return blocks


def on_device(
    tokens,
    segment_ids,
    first_gain,
    input_weight,
    input_bias,
    output_weight,
    second_gain,
    gate_weight,
    up_weight,
    down_weight,
    output_cotangent,
):
    bf16, f32 = jnp.bfloat16, jnp.float32
    shards, reps = lax.axis_size("shard"), lax.axis_size("rep")
    shard, core, first, second = make_lines(reps, shards)
    rep_place = (core.place * first.size + first.place) * second.size + second.place
    own_rows, width = tokens.shape
    segments = segment_ids[0]
    per_group = QH // KVH
    query_width = QH * HD
    pair_width = KVH * HD
    score_scale = 1.0 / math.sqrt(HD)
    first_row = shard.place * own_rows
    part_rows = input_weight.shape[0] // reps
    hidden_units = gate_weight.shape[1]
    block_units = hidden_units // shards

    def gather_weight(weight):
        piece = pick(weight.reshape(reps, part_rows, weight.shape[1]), rep_place, 0)
        column = stack_by_place(gather_line(piece, shard), shard)
        whole = jnp.zeros((shards, reps, part_rows, weight.shape[1]), weight.dtype)
        for place, value in gather_rep(column, core, first, second):
            whole = put(whole, value, place, 1)
        return whole.reshape(width, weight.shape[1])

    def gather_column_blocks(weights):
        pieces = jnp.stack(
            [
                pick(weight.reshape(reps, part_rows, hidden_units), rep_place, 0)
                .reshape(part_rows, shards, block_units)
                .transpose(1, 0, 2)
                for weight in weights
            ],
            axis=1,
        )
        rows = [pick(pieces, shard.place, 0)] + [
            shard.shift(pick(pieces, shard.ahead(step), 0), step) for step in range(1, shards)
        ]
        column = stack_by_place(rows, shard, 1)
        wholes = [jnp.zeros((shards, reps, part_rows, block_units), bf16) for _ in weights]
        for place, value in gather_rep(column, core, first, second):
            wholes = [put(whole, value[at], place, 1) for at, whole in enumerate(wholes)]
        return [whole.reshape(width, block_units) for whole in wholes]

    input_matrix = gather_weight(input_weight)
    shard_vectors = jnp.concatenate([first_gain, second_gain, input_bias])
    vector_rows = stack_by_place(gather_line(shard_vectors, shard), shard)
    own_gain = first_gain.shape[0]
    gain_one = vector_rows[:, :own_gain].reshape(width).astype(f32)
    gain_two = vector_rows[:, own_gain : 2 * own_gain].reshape(width).astype(f32)
    shift_row = vector_rows[:, 2 * own_gain :].reshape(-1).astype(f32)

    places = positions(segments)
    own_segments = lax.dynamic_slice_in_dim(segments, first_row, own_rows)
    cosine_table, sine_table = rope_tables(
        lax.dynamic_slice_in_dim(places, first_row, own_rows), HD
    )
    wide_tokens = tokens.astype(f32)
    inverse_one = lax.rsqrt(jnp.mean(wide_tokens * wide_tokens, axis=-1, keepdims=True) + EPSILON)
    unit_one = wide_tokens * inverse_one
    normed_one = (unit_one * gain_one).astype(bf16)
    output_matrix = gather_weight(output_weight)
    gate_matrix, up_matrix = gather_column_blocks([gate_weight, up_weight])

    projected = jnp.dot(normed_one, input_matrix, preferred_element_type=f32) + shift_row
    queries = rotate(
        projected[:, :query_width].reshape(own_rows, QH, HD), cosine_table, sine_table
    ).astype(bf16)
    key_part = rotate(
        projected[:, query_width : query_width + pair_width].reshape(own_rows, KVH, HD),
        cosine_table,
        sine_table,
    )
    own_pairs = jnp.concatenate(
        [key_part.reshape(own_rows, pair_width), projected[:, query_width + pair_width :]], axis=1
    ).astype(bf16)
    pairs = jnp.concatenate(gather_line(own_pairs, shard), axis=0)
    group_rows = pairs.shape[0]
    row_index = jnp.arange(own_rows, dtype=jnp.int32)
    key_index = jnp.concatenate([shard.behind(step) * own_rows + row_index for step in range(shards)])
    key_segments = jnp.concatenate(
        [
            lax.dynamic_slice_in_dim(segments, shard.behind(step) * own_rows, own_rows)
            for step in range(shards)
        ]
    )
    query_index = first_row + row_index
    allowed = (own_segments[:, None] == key_segments[None, :]) & (
        key_index[None, :] <= query_index[:, None]
    )
    grouped_queries = queries.reshape(own_rows, KVH, per_group, HD)
    keys = pairs[:, :pair_width].reshape(group_rows, KVH, HD)
    values = pairs[:, pair_width:].reshape(group_rows, KVH, HD)
    raw_scores = (
        jnp.einsum("tkgd,jkd->kgtj", grouped_queries, keys, preferred_element_type=f32)
        * score_scale
    )
    masked = jnp.where(allowed[None, None], raw_scores, MASKED)
    top_score = jnp.max(masked, axis=-1, keepdims=True)
    log_norm = top_score + jnp.log(jnp.sum(jnp.exp(masked - top_score), axis=-1, keepdims=True))
    shares = jnp.where(allowed[None, None], jnp.exp(masked - log_norm), 0.0)
    shares_low = shares.astype(bf16)
    attention_low = (
        jnp.einsum("kgtj,jkd->tkgd", shares_low, values, preferred_element_type=f32)
        .reshape(own_rows, query_width)
        .astype(bf16)
    )
    hidden = wide_tokens + jnp.dot(attention_low, output_matrix, preferred_element_type=f32)
    inverse_two = lax.rsqrt(jnp.mean(hidden * hidden, axis=-1, keepdims=True) + EPSILON)
    unit_two = hidden * inverse_two
    normed_two = (unit_two * gain_two).astype(bf16)

    cotangents = jnp.concatenate(gather_line(output_cotangent, shard), axis=0)
    group_normed = jnp.concatenate(gather_line(normed_two, shard), axis=0)

    def sum_rows(rows):
        blocks = rows.reshape(shards, own_rows, width)
        total = blocks[0]
        for step in range(1, shards):
            total = total + shard.shift(blocks[step].astype(bf16), shards - step).astype(f32)
        return total

    gate_linear = jnp.dot(group_normed, gate_matrix, preferred_element_type=f32)
    up_linear = jnp.dot(group_normed, up_matrix, preferred_element_type=f32)
    gate_sigmoid = jax.nn.sigmoid(gate_linear)
    gate_output = gate_linear * gate_sigmoid
    inner_act = (gate_output * up_linear).astype(bf16)
    inner_gradient = times_transposed(cotangents, down_weight)

    down_blocks = transposed_times(inner_act, cotangents).astype(bf16)
    down_piece = sum_rep(
        down_blocks.reshape(reps, block_units // reps, width), 0, core, first, second
    )

    gate_gradient_rows = (
        inner_gradient * up_linear * gate_sigmoid * (1.0 + gate_linear * (1.0 - gate_sigmoid))
    ).astype(bf16)
    up_gradient_rows = (inner_gradient * gate_output).astype(bf16)
    normed_two_gradient = sum_rows(
        times_transposed(gate_gradient_rows, gate_matrix)
        + times_transposed(up_gradient_rows, up_matrix)
    )

    def column_gradient(gradient_rows):
        partial = transposed_times(group_normed, gradient_rows).astype(bf16)
        piece = sum_rep(
            partial.reshape(shards, reps, part_rows, block_units), 1, core, first, second
        )
        rows = [pick(piece, shard.place, 0)] + [
            shard.shift(pick(piece, shard.ahead(step), 0), step) for step in range(1, shards)
        ]
        return (
            stack_by_place(rows, shard).transpose(1, 0, 2).reshape(part_rows, shards * block_units)
        )

    def spread(piece):
        rows = piece.shape[0]
        whole = jnp.zeros((reps,) + piece.shape, f32)
        for place, value in gather_rep(piece, core, first, second):
            whole = put(whole, value.astype(f32), place, 0)
        return whole.reshape(reps * rows, piece.shape[1])

    gate_piece = column_gradient(gate_gradient_rows)
    up_piece = column_gradient(up_gradient_rows)
    down_total = spread(down_piece)
    gate_total = spread(gate_piece)
    up_total = spread(up_piece)
    block_out = (
        hidden + sum_rows(jnp.dot(inner_act, down_weight, preferred_element_type=f32))
    ).astype(bf16)

    gain_two_gradient = jnp.sum(normed_two_gradient * unit_two, axis=0)
    hidden_gradient = output_cotangent.astype(f32) + norm_back(
        normed_two_gradient, unit_two, inverse_two, gain_two
    )
    branch_gradient = hidden_gradient.astype(bf16)

    def row_gradient(partial):
        columns = partial.shape[1]
        piece = sum_rep(
            partial.astype(bf16).reshape(shards, reps, part_rows, columns), 1, core, first, second
        )
        return spread(sum_line(piece, shard, 0))

    output_total = row_gradient(transposed_times(attention_low, branch_gradient))
    attention_gradient = times_transposed(branch_gradient, output_matrix).astype(bf16)
    grouped_gradient = attention_gradient.reshape(own_rows, KVH, per_group, HD)
    share_gradient = jnp.einsum(
        "tkgd,jkd->kgtj", grouped_gradient, values, preferred_element_type=f32
    )
    share_dot = jnp.sum(shares * share_gradient, axis=-1, keepdims=True)
    score_gradient = (shares * (share_gradient - share_dot)).astype(bf16)
    query_gradient = jnp.einsum(
        "kgtj,jkd->tkgd", score_gradient, keys, preferred_element_type=f32
    )
    key_gradient = (
        jnp.einsum("kgtj,tkgd->jkd", score_gradient, grouped_queries, preferred_element_type=f32)
        * score_scale
    )
    value_gradient = jnp.einsum(
        "kgtj,tkgd->jkd", shares_low, grouped_gradient, preferred_element_type=f32
    )
    pair_blocks = jnp.concatenate(
        [
            key_gradient.reshape(group_rows, pair_width),
            value_gradient.reshape(group_rows, pair_width),
        ],
        axis=1,
    ).reshape(shards, own_rows, 2 * pair_width)
    pair_gradients = pair_blocks[0]
    for step in range(1, shards):
        pair_gradients = pair_gradients + shard.shift(
            pair_blocks[step].astype(bf16), shards - step
        ).astype(f32)
    query_back = rotate_back(
        (query_gradient * score_scale).reshape(own_rows, QH, HD), cosine_table, sine_table
    ).reshape(own_rows, query_width)
    key_back = rotate_back(
        pair_gradients[:, :pair_width].reshape(own_rows, KVH, HD), cosine_table, sine_table
    ).reshape(own_rows, pair_width)
    projected_gradient = jnp.concatenate(
        [query_back, key_back, pair_gradients[:, pair_width:]], axis=1
    ).astype(bf16)
    input_total = row_gradient(transposed_times(normed_one, projected_gradient))
    bias_gradient = jnp.sum(projected_gradient.astype(f32), axis=0)
    bias_split = query_width + pair_width
    normed_one_gradient = times_transposed(projected_gradient, input_matrix)
    gain_one_gradient = jnp.sum(normed_one_gradient * unit_one, axis=0)
    tokens_gradient = (
        hidden_gradient + norm_back(normed_one_gradient, unit_one, inverse_one, gain_one)
    ).astype(bf16)

    small_parts = (
        gain_one_gradient,
        gain_two_gradient,
        bias_gradient[:bias_split],
        bias_gradient[bias_split:],
    )
    small_rows = jnp.concatenate([part.reshape(shards, -1) for part in small_parts], axis=1)
    small = sum_line(small_rows, shard, 0)
    for line in (core, first, second):
        total = small
        for step in range(1, line.size):
            total = total + line.shift(small, step)
        small = total
    small_totals, at = [], 0
    for part in small_parts:
        size = part.shape[0] // shards
        small_totals.append(small[at : at + size])
        at += size
    return (
        block_out,
        tokens_gradient,
        small_totals[0],
        input_total,
        small_totals[2],
        small_totals[3],
        output_total,
        small_totals[1],
        gate_total,
        up_total,
        down_total,
    )


def solution(mesh):
    placed = (
        P(("rep", "shard"), None),
        P("rep", None),
        P("shard"),
        P("shard", None),
        P("shard"),
        P("shard", None),
        P("shard"),
        P("shard", None),
        P("shard", None),
        P("shard", None),
        P(("rep", "shard"), None),
    )
    return jax.shard_map(
        on_device,
        mesh=mesh,
        in_specs=placed,
        out_specs=(
            P(("rep", "shard"), None),
            P(("rep", "shard"), None),
            P("shard"),
            P("shard", None),
            P("shard"),
            P("shard"),
            P("shard", None),
            P("shard"),
            P("shard", None),
            P("shard", None),
            P("shard", None),
        ),
        check_vma=False,
    )
```

time: 3600 us -> 902 us (0.25)
  waiting for transfers between devices: 3220 us -> 342 us
  local copies, waits for them, and re-layouts: 47.1 us -> 206 us
  starting transfers between devices: 0.69 us -> 117 us
  blocking collectives: 99.7 us -> 0 us
  other arithmetic: 32.5 us -> 100 us
  matrix products: 182 us -> 125 us
    reduce_scatter x5 -> x0, waiting for transfers between devices: 1520 us -> none  [the longest x1 901 us: on_device(): lax.psum_scatter(transposed_times(normed_two, both_gradients).astype(jnp....]
    all_gather x5 -> x0, waiting for transfers between devices: 1470 us -> none  [the longest x1 462 us: on_device(): lax.all_gather(gate_weight, 'shard', axis=0, tiled=True)]
    ppermute x0 -> x119, waiting for transfers between devices: none -> 342 us  [shift(): return lax.ppermute(value, self.name, self.pairs(step % self.size))]
    psum x1 -> x0, waiting for transfers between devices: 236 us -> none  [on_device(): lax.psum(input_gradient, 'rep').astype(jnp.float32)]
    ppermute x0 -> x119, starting transfers between devices: none -> 117 us  [shift(): return lax.ppermute(value, self.name, self.pairs(step % self.size))]
    all_gather x4 -> x0, blocking collectives: 67.3 us -> none  [the longest x1 28 us: on_device(): all_pairs = lax.all_gather(own_pairs, 'shard', axis=0, tiled=True)]
    dynamic_update_slice x0 -> x49, local copies, waits for them, and re-layouts: none -> 57.9 us  [put(): return lax.dynamic_update_index_in_dim(array, piece, index, axis)]
    dynamic_update_slice x0 -> x38, other arithmetic: none -> 40.8 us  [put(): return lax.dynamic_update_index_in_dim(array, piece, index, axis)]
  transfers between devices with their start and end apart: 11 -> 119, of which waited for: 11 -> 44; matrix products, arithmetic and copies ran while one was open for 4% -> 39% of each run, Pallas kernels for 0% -> 0%
where the time goes in v1:
time: 902 us; the launch traced here: 893 us
  waiting for transfers between devices  342 us (38%)
  local copies, waits for them, and re-layouts  206 us (23%)
  matrix products  125 us (14%)
  starting transfers between devices  117 us (13%)
  other arithmetic  100 us (11%)
    ppermute x119, waiting for transfers between devices, shift(): return lax.ppermute(value, self.name, self.pairs(step % self.size))  342 us
    ppermute x119, starting transfers between devices, shift(): return lax.ppermute(value, self.name, self.pairs(step % self.size))  117 us
    dynamic_update_slice x49, local copies, waits for them, and re-layouts, put(): return lax.dynamic_update_index_in_dim(array, piece, index, axis)  57.9 us
    dynamic_update_slice x38, other arithmetic, put(): return lax.dynamic_update_index_in_dim(array, piece, index, axis)  40.8 us
    dot_general x5, matrix products, times_transposed(): lax.dot_general(left_side, right_side, (((1,), (1,)), ((), ())), preferre...  33.2 us
    dot_general x5, matrix products, transposed_times(): lax.dot_general(left_side, right_side, (((0,), (0,)), ((), ())), preferre...  30.6 us
    squeeze x21, local copies, waits for them, and re-layouts, pick(): return lax.dynamic_index_in_dim(array, index, axis, keepdims=False)  25.6 us
    unnamed x172, local copies, waits for them, and re-layouts  22.4 us
  transfers between devices with their start and end apart: 119, of which 44 were waited for; matrix products, arithmetic and copies ran while one was open for 39% of the time, Pallas kernels for 0%

profile of v1, /device:TPU:0, one launch (start us, length us, event | category | flops | bytes accessed | tf_op | source)
XLA Modules:
  0.0 893.2 jit_solution(14125141422031684876)
XLA Ops:
  31.6 7.0 fusion.45
  74.5 33.7 %collective-permute-done.29 = bf16[2,48,2240]{2,1,0:T(8,128)(2,1)S(1)} collective-permute-done((bf16[2,48,2240]{2,1,0:T(8,128)(2,1)S(1)}, bf16[2,48,2240]{2,1,0:T(8,128)(2,1)S(1)}, u32[]{:S(2)}, u32[]{:S(2)}) %collective-permute-start.29) | collective-permute-done | bytes 430112 | tf_op jit(solution)/shard_map/ppermute | solution.py:70
  109.5 26.6 %collective-permute-done.30 = bf16[2,48,2240]{2,1,0:T(8,128)(2,1)S(1)} collective-permute-done((bf16[2,48,2240]{2,1,0:T(8,128)(2,1)S(1)}, bf16[2,48,2240]{2,1,0:T(8,128)(2,1)S(1)}, u32[]{:S(2)}, u32[]{:S(2)}) %collective-permute-start.30) | collective-permute-done | bytes 430112 | tf_op jit(solution)/shard_map/ppermute | solution.py:70
  138.4 7.1 collective-permute-done.31
  155.9 9.9 %fusion.117 = f32[640,2240]{0,1:T(8,128)} fusion(bf16[640,1536]{1,0:T(8,128)(2,1)} %constant_dynamic-update-slice_fusion.2, bf16[2240,1536]{1,0:T(8,128)(2,1)} %param.20), kind=kOutput, calls=%fused_computation.350 | convolution fusion | flops 4404019200 | bytes 14581760 | tf_op jit(solution)/shard_map/dot_general | solution.py:54
  175.5 13.2 %collective-permute-done.21 = bf16[4,48,1536]{2,1,0:T(8,128)(2,1)S(1)} collective-permute-done((bf16[4,48,1536]{2,1,0:T(8,128)(2,1)}, bf16[4,48,1536]{2,1,0:T(8,128)(2,1)S(1)}, u32[]{:S(2)}, u32[]{:S(2)}) %collective-permute-start.21) | collective-permute-done | bytes 589856 | tf_op jit(solution)/shard_map/ppermute | solution.py:70
  192.5 32.5 %collective-permute-done.8 = bf16[4,48,2048]{2,1,0:T(8,128)(2,1)S(1)} collective-permute-done((bf16[4,48,2048]{2,1,0:T(8,128)(2,1)S(1)}, bf16[4,48,2048]{2,1,0:T(8,128)(2,1)S(1)}, u32[]{:S(2)}, u32[]{:S(2)}) %collective-permute-start.8) | collective-permute-done | bytes 786464 | tf_op jit(solution)/shard_map/ppermute | solution.py:70
  296.3 30.4 %collective-permute-done.27 = bf16[160,1536]{1,0:T(8,128)(2,1)S(1)} collective-permute-done((bf16[160,1536]{1,0:T(8,128)(2,1)S(1)}, bf16[160,1536]{1,0:T(8,128)(2,1)S(1)}, u32[]{:S(2)}, u32[]{:S(2)}) %collective-permute-start.27) | collective-permute-done | bytes 491552 | tf_op jit(solution)/shard_map/ppermute | solution.py:70
  326.7 10.0 %fusion.101 = f32[640,2240]{0,1:T(8,128)} fusion(bf16[1536,2240]{1,0:T(8,128)(2,1)} %bitcast.588, bf16[160,1536]{1,0:T(8,128)(2,1)S(1)} %collective-permute-done.28, bf16[160,1536]{1,0:T(8,128)(2,1)S(1)} %collective-permute-done.27, bf16[160,1536]{1,0:T(8,128)(2,1)S(1)} %collective-permute-done.26, bf16[160,1536]{1,0:T(8,128)(2,1)S(1)} %multiply_convert_fusion.3), kind=kOutput, calls=%fused_computation.338 | convolution fusion | flops 4411883520 | bytes 14581760 | tf_op jit(solution)/shard_map/dot_general | solution.py:318
  336.7 21.0 %multiply_convert_fusion.1 = (bf16[640,2240]{0,1:T(8,128)(2,1)}, bf16[640,2240]{0,1:T(8,128)(2,1)}, bf16[640,2240]{0,1:T(8,128)(2,1)}) fusion(f32[640,2240]{0,1:T(8,128)} %fusion.117, f32[640,2240]{0,1:T(8,128)} %fusion.101, bf16[1536,2240]{1,0:T(8,128)(2,1)} %bitcast.584, bf16[160,1536]{1,0:T(8,128)(2,1)S(1)} %collective-permute-done.28, ...), kind=kOutput, calls=%fused_computation.14 | convolution fusion | flops 4433387520 | bytes 28917760 | tf_op jit(solution)/shard_map/dot_general | solution.py:317
  357.7 10.7 %fusion.116 = (bf16[640,1536]{1,0:T(8,128)(2,1)S(1)}, f32[640,1536]{1,0:T(8,128)}) fusion(bf16[640,2240]{0,1:T(8,128)(2,1)} %get-tuple-element.28, bf16[2240,1536]{1,0:T(8,128)(2,1)} %param.20), kind=kOutput, calls=%fused_computation.349 | convolution fusion | flops 4405002240 | bytes 15646720 | tf_op jit(solution)/shard_map/dot_general | solution.py:363
  368.5 7.9 convolution_convert_fusion.2
  376.4 6.8 fusion.118
  383.2 8.8 fusion.115
  400.3 7.7 convolution_convert_fusion.1
  408.0 10.2 %copy.257 = bf16[1536,2240]{1,0:T(8,128)(2,1)} copy(bf16[1536,2240]{0,1:T(8,128)(2,1)} %convolution_convert_fusion.1) | data formatting | bytes 13762560 | tf_op jit(solution)/shard_map/convert_element_type | solution.py:339
  422.4 9.5 %convolution_convert_fusion = bf16[1536,2240]{0,1:T(8,128)(2,1)} fusion(bf16[640,2240]{0,1:T(8,128)(2,1)} %get-tuple-element.27, bf16[160,1536]{1,0:T(8,128)(2,1)S(1)} %copy-done.55, bf16[160,1536]{1,0:T(8,128)(2,1)S(1)} %copy-done.58, bf16[160,1536]{1,0:T(8,128)(2,1)S(1)} %copy-done.61, bf16[160,1536]{1,0:T(8,128)(2,1)S(1)} %multiply_convert_fusion.3), kind=kOutput, calls=%fused_computation | convolution fusion | flops 4415324160 | bytes 11714560 | tf_op jit(solution)/shard_map/dot_general | solution.py:48
  434.0 10.2 %copy.262 = bf16[1536,2240]{1,0:T(8,128)(2,1)} copy(bf16[1536,2240]{0,1:T(8,128)(2,1)} %convolution_convert_fusion) | data formatting | bytes 13762560 | tf_op jit(solution)/shard_map/convert_element_type | solution.py:339
  454.2 16.9 %collective-permute-done.40 = bf16[160,1536]{1,0:T(8,128)(2,1)} collective-permute-done((bf16[160,1536]{1,0:T(8,128)(2,1)}, bf16[160,1536]{1,0:T(8,128)(2,1)}, u32[]{:S(2)}, u32[]{:S(2)}) %collective-permute-start.40) | collective-permute-done | bytes 491552 | tf_op jit(solution)/shard_map/ppermute | solution.py:70
  499.5 9.9 %collective-permute-start.50 = (bf16[160,512]{1,0:T(8,128)(2,1)}, bf16[160,512]{1,0:T(8,128)(2,1)}, u32[]{:S(2)}, u32[]{:S(2)}) collective-permute-start(bf16[160,512]{1,0:T(8,128)(2,1)} %get-tuple-element.75), channel_id=1, source_target_pairs={{0,1},{1,2},{2,3},{3,0},{4,5},{5,6},{6,7},{7,4},{8,9},{9,10},{10,1... | collective-permute-start | bytes 491528 | tf_op jit(solution)/shard_map/ppermute | solution.py:70
  579.9 10.6 %collective-permute-done.72 = bf16[4,48,1536]{2,1,0:T(8,128)(2,1)S(1)} collective-permute-done((bf16[4,48,1536]{2,1,0:T(8,128)(2,1)S(1)}, bf16[4,48,1536]{2,1,0:T(8,128)(2,1)S(1)}, u32[]{:S(2)}, u32[]{:S(2)}) %collective-permute-start.72) | collective-permute-done | bytes 589856 | tf_op jit(solution)/shard_map/ppermute | solution.py:70
  599.6 7.0 collective-permute-done.74
  614.6 40.4 %collective-permute-done.77 = bf16[48,1536]{1,0:T(8,128)(2,1)S(1)} collective-permute-done((bf16[48,1536]{1,0:T(8,128)(2,1)S(1)}, bf16[48,1536]{1,0:T(8,128)(2,1)S(1)}, u32[]{:S(2)}, u32[]{:S(2)}) %collective-permute-start.77) | collective-permute-done | bytes 147488 | tf_op jit(solution)/shard_map/ppermute | solution.py:70
  672.0 24.8 %collective-permute-done.111 = bf16[280,1536]{1,0:T(8,128)(2,1)S(1)} collective-permute-done((bf16[280,1536]{1,0:T(8,128)(2,1)S(1)}, bf16[280,1536]{1,0:T(8,128)(2,1)S(1)}, u32[]{:S(2)}, u32[]{:S(2)}) %collective-permute-start.111) | collective-permute-done | bytes 860192 | tf_op jit(solution)/shard_map/ppermute | solution.py:70
  696.8 6.9 broadcast_in_dim.615
  718.9 6.1 dynamic_update_slice.376
  760.7 6.3 broadcast.149.clone
  787.1 6.3 broadcast.149.clone.1
  829.8 13.4 %collective-permute-done.102 = bf16[48,8960]{1,0:T(8,128)(2,1)S(1)} collective-permute-done((bf16[48,8960]{1,0:T(8,128)(2,1)S(1)}, bf16[48,8960]{1,0:T(8,128)(2,1)S(1)}, u32[]{:S(2)}, u32[]{:S(2)}) %collective-permute-start.102) | collective-permute-done | bytes 860192 | tf_op jit(solution)/shard_map/ppermute | solution.py:70
  846.1 10.1 %collective-permute-done.114 = bf16[280,1536]{1,0:T(8,128)(2,1)S(1)} collective-permute-done((bf16[280,1536]{1,0:T(8,128)(2,1)}, bf16[280,1536]{1,0:T(8,128)(2,1)S(1)}, u32[]{:S(2)}, u32[]{:S(2)}) %collective-permute-start.114) | collective-permute-done | bytes 860192 | tf_op jit(solution)/shard_map/ppermute | solution.py:70
  862.6 7.8 collective-permute-done.91
  876.4 6.8 collective-permute-done.104
  (663 shorter events, 453.5 us)
Async XLA Ops:
  3.4 63.1 %collective-permute-start.3 = (bf16[48,2048]{1,0:T(8,128)(2,1)}, bf16[48,2048]{1,0:T(8,128)(2,1)}, u32[]{:S(2)}, u32[]{:S(2)}) collective-permute-start(bf16[48,2048]{1,0:T(8,128)(2,1)} %get-tuple-element.53), channel_id=1, source_target_pairs={{0,1},{1,2},{2,3},{3,0},{4,5},{5,6},{6,7},{7,4},{8,9},{9,10},{10,1... | collective-permute-start | bytes 589832 | tf_op jit(solution)/shard_map/ppermute | solution.py:70
  6.4 62.6 %collective-permute-start.4 = (bf16[48,2048]{1,0:T(8,128)(2,1)}, bf16[48,2048]{1,0:T(8,128)(2,1)}, u32[]{:S(2)}, u32[]{:S(2)}) collective-permute-start(bf16[48,2048]{1,0:T(8,128)(2,1)} %get-tuple-element.53), channel_id=1, source_target_pairs={{0,2},{1,3},{2,0},{3,1},{4,6},{5,7},{6,4},{7,5},{8,10},{9,11},{10,... | collective-permute-start | bytes 589832 | tf_op jit(solution)/shard_map/ppermute | solution.py:70
  60.7 90.5 %collective-permute-start.42 = (bf16[160,1536]{1,0:T(8,128)(2,1)}, bf16[160,1536]{1,0:T(8,128)(2,1)S(1)}, u32[]{:S(2)}, u32[]{:S(2)}) collective-permute-start(bf16[160,1536]{1,0:T(8,128)(2,1)} %param.21), channel_id=1, source_target_pairs={{0,1},{1,2},{2,3},{3,0},{4,5},{5,6},{6,7},{7,4},{8,9},{9,10},{10,1... | collective-permute-start | bytes 1474568 | tf_op jit(solution)/shard_map/ppermute | solution.py:70
  62.5 89.7 %collective-permute-start.43 = (bf16[160,1536]{1,0:T(8,128)(2,1)}, bf16[160,1536]{1,0:T(8,128)(2,1)S(1)}, u32[]{:S(2)}, u32[]{:S(2)}) collective-permute-start(bf16[160,1536]{1,0:T(8,128)(2,1)} %param.21), channel_id=1, source_target_pairs={{0,2},{1,3},{2,0},{3,1},{4,6},{5,7},{6,4},{7,5},{8,10},{9,11},{10,... | collective-permute-start | bytes 1474568 | tf_op jit(solution)/shard_map/ppermute | solution.py:70
  66.5 88.0 %collective-permute-start.44 = (bf16[160,1536]{1,0:T(8,128)(2,1)S(1)}, bf16[160,1536]{1,0:T(8,128)(2,1)S(1)}, u32[]{:S(2)}, u32[]{:S(2)}) collective-permute-start(bf16[160,1536]{1,0:T(8,128)(2,1)S(1)} %copy-done.20), channel_id=1, source_target_pairs={{0,3},{1,0},{2,1},{3,2},{4,7},{5,4},{6,5},{7,6},{8,11},{9,8},{10,9... | collective-permute-start | bytes 1474568 | tf_op jit(solution)/shard_map/ppermute | solution.py:70
  71.8 64.3 %collective-permute-start.30 = (bf16[2,48,2240]{2,1,0:T(8,128)(2,1)S(1)}, bf16[2,48,2240]{2,1,0:T(8,128)(2,1)S(1)}, u32[]{:S(2)}, u32[]{:S(2)}) collective-permute-start(bf16[2,48,2240]{2,1,0:T(8,128)(2,1)S(1)} %bitcast.615), channel_id=1, source_target_pairs={{0,2},{1,3},{2,0},{3,1},{4,6},{5,7},{6,4},{7,5},{8,10},{9,11},{10,... | collective-permute-start | bytes 1290248 | tf_op jit(solution)/shard_map/ppermute | solution.py:70
  165.8 59.6 %collective-permute-start.9 = (bf16[4,48,2048]{2,1,0:T(8,128)(2,1)}, bf16[4,48,2048]{2,1,0:T(8,128)(2,1)S(1)}, u32[]{:S(2)}, u32[]{:S(2)}) collective-permute-start(bf16[4,48,2048]{2,1,0:T(8,128)(2,1)} %bitcast_dynamic-update-slice_fusion.20), channel_id=1, source_target_pairs={{0,4},{4,0},{8,12},{12,8},{16,20},{20,16},{24,28},{28,24},{1,5},{5... | collective-permute-start | bytes 2359304 | tf_op jit(solution)/shard_map/ppermute | solution.py:70
  166.9 62.4 %collective-permute-start.32 = (bf16[2,4,48,2240]{3,2,1,0:T(8,128)(2,1)}, bf16[2,4,48,2240]{3,2,1,0:T(8,128)(2,1)}, u32[]{:S(2)}, u32[]{:S(2)}) collective-permute-start(bf16[2,4,48,2240]{3,2,1,0:T(8,128)(2,1)} %bitcast_dynamic-update-slice_fusion.17), channel_id=1, source_target_pairs={{0,16},{4,12},{8,24},{12,4},{16,0},{20,28},{24,8},{28,20},{1,17},{... | collective-permute-start | bytes 5160968 | tf_op jit(solution)/shard_map/ppermute | solution.py:70
  174.3 58.5 %collective-permute-start.33 = (bf16[2,4,48,2240]{3,2,1,0:T(8,128)(2,1)}, bf16[2,4,48,2240]{3,2,1,0:T(8,128)(2,1)}, u32[]{:S(2)}, u32[]{:S(2)}) collective-permute-start(bf16[2,4,48,2240]{3,2,1,0:T(8,128)(2,1)} %bitcast_dynamic-update-slice_fusion.17), channel_id=1, source_target_pairs={{0,8},{4,20},{8,0},{12,28},{16,24},{20,4},{24,16},{28,12},{1,9},{5... | collective-permute-start | bytes 5160968 | tf_op jit(solution)/shard_map/ppermute | solution.py:70
  191.8 94.9 %collective-permute-start.35 = (bf16[2,4,48,2240]{3,2,1,0:T(8,128)(2,1)}, bf16[2,4,48,2240]{3,2,1,0:T(8,128)(2,1)}, u32[]{:S(2)}, u32[]{:S(2)}) collective-permute-start(bf16[2,4,48,2240]{3,2,1,0:T(8,128)(2,1)} %bitcast_dynamic-update-slice_fusion.17), channel_id=1, source_target_pairs={{0,4},{4,0},{8,12},{12,8},{16,20},{20,16},{24,28},{28,24},{1,5},{5... | collective-permute-start | bytes 5160968 | tf_op jit(solution)/shard_map/ppermute | solution.py:70
  229.4 53.4 %collective-permute-start.34 = (bf16[2,4,48,2240]{3,2,1,0:T(8,128)(2,1)}, bf16[2,4,48,2240]{3,2,1,0:T(8,128)(2,1)}, u32[]{:S(2)}, u32[]{:S(2)}) collective-permute-start(bf16[2,4,48,2240]{3,2,1,0:T(8,128)(2,1)} %collective-permute-done.32), channel_id=1, source_target_pairs={{0,8},{4,20},{8,0},{12,28},{16,24},{20,4},{24,16},{28,12},{1,9},{5... | collective-permute-start | bytes 5160968 | tf_op jit(solution)/shard_map/ppermute | solution.py:70
  282.8 43.9 %collective-permute-start.27 = (bf16[160,1536]{1,0:T(8,128)(2,1)S(1)}, bf16[160,1536]{1,0:T(8,128)(2,1)S(1)}, u32[]{:S(2)}, u32[]{:S(2)}) collective-permute-start(bf16[160,1536]{1,0:T(8,128)(2,1)S(1)} %multiply_convert_fusion.3), channel_id=1, source_target_pairs={{0,2},{1,3},{2,0},{3,1},{4,6},{5,7},{6,4},{7,5},{8,10},{9,11},{10,... | collective-permute-start | bytes 1474568 | tf_op jit(solution)/shard_map/ppermute | solution.py:70
  393.2 55.1 %collective-permute-start.47 = (bf16[160,1536]{1,0:T(8,128)(2,1)}, bf16[160,1536]{1,0:T(8,128)(2,1)}, u32[]{:S(2)}, u32[]{:S(2)}) collective-permute-start(bf16[160,1536]{1,0:T(8,128)(2,1)} %get-tuple-element.30), channel_id=1, source_target_pairs={{0,1},{1,2},{2,3},{3,0},{4,5},{5,6},{6,7},{7,4},{8,9},{9,10},{10,1... | collective-permute-start | bytes 1474568 | tf_op jit(solution)/shard_map/ppermute | solution.py:70
  393.2 58.1 %collective-permute-start.46 = (bf16[160,1536]{1,0:T(8,128)(2,1)}, bf16[160,1536]{1,0:T(8,128)(2,1)}, u32[]{:S(2)}, u32[]{:S(2)}) collective-permute-start(bf16[160,1536]{1,0:T(8,128)(2,1)} %get-tuple-element.31), channel_id=1, source_target_pairs={{0,2},{1,3},{2,0},{3,1},{4,6},{5,7},{6,4},{7,5},{8,10},{9,11},{10,... | collective-permute-start | bytes 1474568 | tf_op jit(solution)/shard_map/ppermute | solution.py:70
  394.3 57.0 %collective-permute-start.45 = (bf16[160,1536]{1,0:T(8,128)(2,1)}, bf16[160,1536]{1,0:T(8,128)(2,1)}, u32[]{:S(2)}, u32[]{:S(2)}) collective-permute-start(bf16[160,1536]{1,0:T(8,128)(2,1)} %get-tuple-element.29), channel_id=1, source_target_pairs={{0,3},{1,0},{2,1},{3,2},{4,7},{5,4},{6,5},{7,6},{8,11},{9,8},{10,9... | collective-permute-start | bytes 1474568 | tf_op jit(solution)/shard_map/ppermute | solution.py:70
  398.4 55.8 %collective-permute-start.41 = (bf16[160,1536]{1,0:T(8,128)(2,1)}, bf16[160,1536]{1,0:T(8,128)(2,1)S(1)}, u32[]{:S(2)}, u32[]{:S(2)}) collective-permute-start(bf16[160,1536]{1,0:T(8,128)(2,1)} %get-tuple-element.33), channel_id=1, source_target_pairs={{0,1},{1,2},{2,3},{3,0},{4,5},{5,6},{6,7},{7,4},{8,9},{9,10},{10,1... | collective-permute-start | bytes 1474568 | tf_op jit(solution)/shard_map/ppermute | solution.py:70
  398.8 72.3 %collective-permute-start.40 = (bf16[160,1536]{1,0:T(8,128)(2,1)}, bf16[160,1536]{1,0:T(8,128)(2,1)}, u32[]{:S(2)}, u32[]{:S(2)}) collective-permute-start(bf16[160,1536]{1,0:T(8,128)(2,1)} %get-tuple-element.34), channel_id=1, source_target_pairs={{0,2},{1,3},{2,0},{3,1},{4,6},{5,7},{6,4},{7,5},{8,10},{9,11},{10,... | collective-permute-start | bytes 1474568 | tf_op jit(solution)/shard_map/ppermute | solution.py:70
  451.2 105.5 %collective-permute-start.83 = (bf16[4,2,2,48,2240]{4,3,2,1,0:T(8,128)(2,1)}, bf16[4,2,2,48,2240]{4,3,2,1,0:T(8,128)(2,1)}, u32[]{:S(2)}, u32[]{:S(2)}) collective-permute-start(bf16[4,2,2,48,2240]{4,3,2,1,0:T(8,128)(2,1)} %dynamic-slice_bitcast_fusion.1), channel_id=1, source_target_pairs={{0,4},{4,0},{8,12},{12,8},{16,20},{20,16},{24,28},{28,24},{1,5},{5... | collective-permute-start | bytes 10321928 | tf_op jit(solution)/shard_map/ppermute | solution.py:70
  550.5 44.0 %collective-permute-start.57 = (bf16[4,2,2,48,2048]{4,3,2,1,0:T(8,128)(2,1)}, bf16[4,2,2,48,2048]{4,3,2,1,0:T(8,128)(2,1)}, u32[]{:S(2)}, u32[]{:S(2)}) collective-permute-start(bf16[4,2,2,48,2048]{4,3,2,1,0:T(8,128)(2,1)} %dynamic-slice_bitcast_fusion.3), channel_id=1, source_target_pairs={{0,4},{4,0},{8,12},{12,8},{16,20},{20,16},{24,28},{28,24},{1,5},{5... | collective-permute-start | bytes 9437192 | tf_op jit(solution)/shard_map/ppermute | solution.py:70
  561.6 102.8 %collective-permute-start.84 = (bf16[4,2,48,2240]{3,2,1,0:T(8,128)(2,1)}, bf16[4,2,48,2240]{3,2,1,0:T(8,128)(2,1)S(1)}, u32[]{:S(2)}, u32[]{:S(2)}) collective-permute-start(bf16[4,2,48,2240]{3,2,1,0:T(8,128)(2,1)} %dynamic-slice_bitcast_fusion.6), channel_id=1, source_target_pairs={{0,8},{4,20},{8,0},{12,28},{16,24},{20,4},{24,16},{28,12},{1,9},{5... | collective-permute-start | bytes 5160968 | tf_op jit(solution)/shard_map/ppermute | solution.py:70
  565.5 101.1 %collective-permute-start.97 = (bf16[4,2,48,2240]{3,2,1,0:T(8,128)(2,1)S(1)}, bf16[4,2,48,2240]{3,2,1,0:T(8,128)(2,1)S(1)}, u32[]{:S(2)}, u32[]{:S(2)}) collective-permute-start(bf16[4,2,48,2240]{3,2,1,0:T(8,128)(2,1)S(1)} %dynamic-slice_bitcast_fusion.5), channel_id=1, source_target_pairs={{0,8},{4,20},{8,0},{12,28},{16,24},{20,4},{24,16},{28,12},{1,9},{5... | collective-permute-start | bytes 5160968 | tf_op jit(solution)/shard_map/ppermute | solution.py:70
  598.8 68.8 %collective-permute-start.110 = (bf16[2,280,1536]{2,1,0:T(8,128)(2,1)S(1)}, bf16[2,280,1536]{2,1,0:T(8,128)(2,1)S(1)}, u32[]{:S(2)}, u32[]{:S(2)}) collective-permute-start(bf16[2,280,1536]{2,1,0:T(8,128)(2,1)S(1)} %dynamic-slice_bitcast_fusion.7), channel_id=1, source_target_pairs={{0,8},{4,20},{8,0},{12,28},{16,24},{20,4},{24,16},{28,12},{1,9},{5... | collective-permute-start | bytes 5160968 | tf_op jit(solution)/shard_map/ppermute | solution.py:70
  608.8 61.2 %collective-permute-start.58 = (bf16[4,2,48,2048]{3,2,1,0:T(8,128)(2,1)S(1)}, bf16[4,2,48,2048]{3,2,1,0:T(8,128)(2,1)S(1)}, u32[]{:S(2)}, u32[]{:S(2)}) collective-permute-start(bf16[4,2,48,2048]{3,2,1,0:T(8,128)(2,1)S(1)} %dynamic-slice_bitcast_fusion.8), channel_id=1, source_target_pairs={{0,8},{4,20},{8,0},{12,28},{16,24},{20,4},{24,16},{28,12},{1,9},{5... | collective-permute-start | bytes 4718600 | tf_op jit(solution)/shard_map/ppermute | solution.py:70
  665.0 42.6 %collective-permute-start.85 = (bf16[4,48,2240]{2,1,0:T(8,128)(2,1)S(1)}, bf16[4,48,2240]{2,1,0:T(8,128)(2,1)S(1)}, u32[]{:S(2)}, u32[]{:S(2)}) collective-permute-start(bf16[4,48,2240]{2,1,0:T(8,128)(2,1)S(1)} %dynamic-slice_bitcast_fusion.11), channel_id=1, source_target_pairs={{0,16},{4,12},{8,24},{12,4},{16,0},{20,28},{24,8},{28,20},{1,17},{... | collective-permute-start | bytes 2580488 | tf_op jit(solution)/shard_map/ppermute | solution.py:70
  667.2 43.8 %collective-permute-start.98 = (bf16[4,48,2240]{2,1,0:T(8,128)(2,1)S(1)}, bf16[4,48,2240]{2,1,0:T(8,128)(2,1)S(1)}, u32[]{:S(2)}, u32[]{:S(2)}) collective-permute-start(bf16[4,48,2240]{2,1,0:T(8,128)(2,1)S(1)} %dynamic-slice_bitcast_fusion.10), channel_id=1, source_target_pairs={{0,16},{4,12},{8,24},{12,4},{16,0},{20,28},{24,8},{28,20},{1,17},{... | collective-permute-start | bytes 2580488 | tf_op jit(solution)/shard_map/ppermute | solution.py:70
  671.6 53.5 %collective-permute-start.59 = (bf16[4,48,2048]{2,1,0:T(8,128)(2,1)}, bf16[4,48,2048]{2,1,0:T(8,128)(2,1)}, u32[]{:S(2)}, u32[]{:S(2)}) collective-permute-start(bf16[4,48,2048]{2,1,0:T(8,128)(2,1)} %dynamic-slice_bitcast_fusion.13), channel_id=1, source_target_pairs={{0,16},{4,12},{8,24},{12,4},{16,0},{20,28},{24,8},{28,20},{1,17},{... | collective-permute-start | bytes 2359304 | tf_op jit(solution)/shard_map/ppermute | solution.py:70
  705.6 110.0 %collective-permute-start.112 = (bf16[280,1536]{1,0:T(8,128)(2,1)}, bf16[280,1536]{1,0:T(8,128)(2,1)}, u32[]{:S(2)}, u32[]{:S(2)}) collective-permute-start(bf16[280,1536]{1,0:T(8,128)(2,1)} %get-tuple-element.20), channel_id=1, source_target_pairs={{0,16},{4,12},{8,24},{12,4},{16,0},{20,28},{24,8},{28,20},{1,17},{... | collective-permute-start | bytes 2580488 | tf_op jit(solution)/shard_map/ppermute | solution.py:70
  707.1 111.0 %collective-permute-start.113 = (bf16[280,1536]{1,0:T(8,128)(2,1)}, bf16[280,1536]{1,0:T(8,128)(2,1)}, u32[]{:S(2)}, u32[]{:S(2)}) collective-permute-start(bf16[280,1536]{1,0:T(8,128)(2,1)} %get-tuple-element.20), channel_id=1, source_target_pairs={{0,8},{4,20},{8,0},{12,28},{16,24},{20,4},{24,16},{28,12},{1,9},{5... | collective-permute-start | bytes 2580488 | tf_op jit(solution)/shard_map/ppermute | solution.py:70
  781.0 76.7 %collective-permute-start.115 = (bf16[280,1536]{1,0:T(8,128)(2,1)}, bf16[280,1536]{1,0:T(8,128)(2,1)S(1)}, u32[]{:S(2)}, u32[]{:S(2)}) collective-permute-start(bf16[280,1536]{1,0:T(8,128)(2,1)} %get-tuple-element.20), channel_id=1, source_target_pairs={{0,4},{4,0},{8,12},{12,8},{16,20},{20,16},{24,28},{28,24},{1,5},{5... | collective-permute-start | bytes 2580488 | tf_op jit(solution)/shard_map/ppermute | solution.py:70
  781.0 41.3 %collective-permute-start.89 = (bf16[48,8960]{1,0:T(8,128)(2,1)}, bf16[48,8960]{1,0:T(8,128)(2,1)S(1)}, u32[]{:S(2)}, u32[]{:S(2)}) collective-permute-start(bf16[48,8960]{1,0:T(8,128)(2,1)} %reshape.458), channel_id=1, source_target_pairs={{0,16},{4,12},{8,24},{12,4},{16,0},{20,28},{24,8},{28,20},{1,17},{... | collective-permute-start | bytes 2580488 | tf_op jit(solution)/shard_map/ppermute | solution.py:70
  815.6 56.4 %collective-permute-start.92 = (bf16[48,8960]{1,0:T(8,128)(2,1)S(1)}, bf16[48,8960]{1,0:T(8,128)(2,1)S(1)}, u32[]{:S(2)}, u32[]{:S(2)}) collective-permute-start(bf16[48,8960]{1,0:T(8,128)(2,1)S(1)} %copy-done.26), channel_id=1, source_target_pairs={{0,4},{4,0},{8,12},{12,8},{16,20},{20,16},{24,28},{28,24},{1,5},{5... | collective-permute-start | bytes 2580488 | tf_op jit(solution)/shard_map/ppermute | solution.py:70
  828.5 56.0 %collective-permute-start.105 = (bf16[48,8960]{1,0:T(8,128)(2,1)S(1)}, bf16[48,8960]{1,0:T(8,128)(2,1)S(1)}, u32[]{:S(2)}, u32[]{:S(2)}) collective-permute-start(bf16[48,8960]{1,0:T(8,128)(2,1)S(1)} %copy-done.27), channel_id=1, source_target_pairs={{0,4},{4,0},{8,12},{12,8},{16,20},{20,16},{24,28},{28,24},{1,5},{5... | collective-permute-start | bytes 2580488 | tf_op jit(solution)/shard_map/ppermute | solution.py:70
  (168 other events, 2572.3 us)

commit v2 on v1

--- a/solution.py
+++ b/solution.py
@@ -3,6 +3,8 @@
 import jax
 import jax.numpy as jnp
 from jax import lax
+from jax.experimental import pallas as pl
+from jax.experimental.pallas import tpu as pltpu
 from jax.sharding import PartitionSpec as P
 
 QH = 12
@@ -14,6 +16,8 @@
 EPSILON = 1e-06
 LOG_THETA = math.log(1000000.0)
 MASKED = -1e30
+VMEM_LIMIT = 56 * 1024 * 1024
+TILE = 512
 
 
 def rope_tables(places, head_width):
@@ -136,49 +140,279 @@
     return lax.dynamic_update_index_in_dim(array, piece, index, axis)
 
 
-def stack_by_place(pieces, line, axis=0):
-    shape = list(pieces[0].shape)
-    shape.insert(axis, line.size)
-    held = jnp.zeros(shape, pieces[0].dtype)
-    for step, piece in enumerate(pieces):
-        held = put(held, piece, line.behind(step), axis)
-    return held
+def in_place_order(pieces, line):
+    ordered = []
+    for place in range(line.size):
+        chosen = pieces[0]
+        for step in range(1, line.size):
+            chosen = jnp.where(line.behind(step) == place, pieces[step], chosen)
+        ordered.append(chosen)
+    return ordered
+
+
+def tie(*arrays):
+    return lax.optimization_barrier(arrays)
 
 
 def gather_line(value, line):
     return [value] + [line.shift(value, step) for step in range(1, line.size)]
 
 
-def sum_line(blocks, line, axis):
+def send_sums(blocks, line, axis):
+    return [line.shift(pick(blocks, line.ahead(step), axis), step) for step in range(1, line.size)]
+
+
+def add_sums(blocks, line, axis, arrived):
     total = pick(blocks, line.place, axis).astype(jnp.float32)
-    for step in range(1, line.size):
-        total = total + line.shift(pick(blocks, line.ahead(step), axis), step).astype(jnp.float32)
+    for block in arrived:
+        total = total + block.astype(jnp.float32)
     return total.astype(blocks.dtype)
 
 
-def gather_rep(piece, core, first, second):
-    held = [(0, 0, piece)]
-    for step in range(1, second.size):
-        held.append((0, step, second.shift(piece, step)))
-    for step in range(1, first.size):
-        held += [(step, at, first.shift(value, step)) for zero, at, value in held if zero == 0]
-    placed = [
-        (core.place, first.behind(one), second.behind(two), value) for one, two, value in held
-    ]
-    there, here = (second, first) if core.crossed else (first, second)
-    for one, two, value in held:
-        placed.append(
-            (core.behind(1), there.behind(one), here.behind(two), core.shift(value, 1))
+class Spread:
+    def __init__(self, piece, core, first, second):
+        self.lines = core, first, second
+        self.held = [(0, 0, piece)]
+        for step in range(1, second.size):
+            self.held.append((0, step, second.shift(piece, step)))
+        for step in range(1, first.size):
+            self.held.append((step, 0, first.shift(piece, step)))
+
+    def arrived(self):
+        return [value for one, two, value in self.held[1:]]
+
+    def replace(self, values):
+        self.held = self.held[:1] + [
+            (one, two, value) for (one, two, old), value in zip(self.held[1:], values)
+        ]
+
+    def further(self):
+        core, first, second = self.lines
+        for step in range(1, first.size):
+            for one, two, value in [entry for entry in self.held if entry[0] == 0 and entry[1]]:
+                self.held.append((step, two, first.shift(value, step)))
+
+    def finish(self):
+        core, first, second = self.lines
+        placed = [
+            (core.place, first.behind(one), second.behind(two), value)
+            for one, two, value in self.held
+        ]
+        there, here = (second, first) if core.crossed else (first, second)
+        for one, two, value in self.held:
+            placed.append(
+                (core.behind(1), there.behind(one), here.behind(two), core.shift(value, 1))
+            )
+        places = [(c * first.size + f) * second.size + s for c, f, s, value in placed]
+        return jnp.stack(places).astype(jnp.int32), [value for c, f, s, value in placed]
+
+
+def place_blocks(order, places, pieces):
+    reps, shards = len(pieces), pieces[0].shape[0]
+    block = pieces[0].shape[1:]
+
+    def body(order_ref, places_ref, *refs):
+        sources, (out_ref, held, in_sems, out_sems) = refs[:reps], refs[reps:]
+        loads = [
+            [
+                pltpu.make_async_copy(
+                    sources[r].at[k], held.at[k, places_ref[r]], in_sems.at[r, k]
+                )
+                for r in range(reps)
+            ]
+            for k in range(shards)
+        ]
+        stores = [
+            pltpu.make_async_copy(held.at[k], out_ref.at[order_ref[k]], out_sems.at[k])
+            for k in range(shards)
+        ]
+        for k in range(shards):
+            for r in range(reps):
+                loads[k][r].start()
+        for k in range(shards):
+            for r in range(reps):
+                loads[k][r].wait()
+            stores[k].start()
+        for store in stores:
+            store.wait()
+
+    return pl.pallas_call(
+        body,
+        out_shape=jax.ShapeDtypeStruct((shards, reps) + block, pieces[0].dtype),
+        in_specs=[pl.BlockSpec(memory_space=pltpu.SMEM)] * 2
+        + [pl.BlockSpec(memory_space=pl.ANY)] * reps,
+        out_specs=pl.BlockSpec(memory_space=pl.ANY),
+        scratch_shapes=[
+            pltpu.VMEM((shards, reps) + block, pieces[0].dtype),
+            pltpu.SemaphoreType.DMA((reps, shards)),
+            pltpu.SemaphoreType.DMA((shards,)),
+        ],
+        compiler_params=pltpu.CompilerParams(vmem_limit_bytes=VMEM_LIMIT),
+        name="place_blocks",
+    )(order, places, *pieces)
+
+
+def widen_pieces(places, pieces):
+    reps = len(pieces)
+    rows, columns = pieces[0].shape
+    strip = next(size for size in (16, 8, rows) if rows % size == 0)
+
+    def body(places_ref, *refs):
+        sources, (out_ref, narrow, wide, in_sems, out_sems) = refs[:reps], refs[reps:]
+        loads = [
+            pltpu.make_async_copy(sources[r], narrow.at[r], in_sems.at[r]) for r in range(reps)
+        ]
+        stores = [
+            pltpu.make_async_copy(wide.at[r], out_ref.at[places_ref[r]], out_sems.at[r])
+            for r in range(reps)
+        ]
+        for load in loads:
+            load.start()
+        for r in range(reps):
+            loads[r].wait()
+
+            def convert(at, carry):
+                cut = pl.ds(pl.multiple_of(at * strip, strip), strip)
+                wide[r, cut, :] = narrow[r, cut, :].astype(jnp.float32)
+                return carry
+
+            lax.fori_loop(0, rows // strip, convert, 0)
+            stores[r].start()
+        for store in stores:
+            store.wait()
+
+    return pl.pallas_call(
+        body,
+        out_shape=jax.ShapeDtypeStruct((reps, rows, columns), jnp.float32),
+        in_specs=[pl.BlockSpec(memory_space=pltpu.SMEM)]
+        + [pl.BlockSpec(memory_space=pl.ANY)] * reps,
+        out_specs=pl.BlockSpec(memory_space=pl.ANY),
+        scratch_shapes=[
+            pltpu.VMEM((reps, rows, columns), jnp.bfloat16),
+            pltpu.VMEM((reps, rows, columns), jnp.float32),
+            pltpu.SemaphoreType.DMA((reps,)),
+            pltpu.SemaphoreType.DMA((reps,)),
+        ],
+        compiler_params=pltpu.CompilerParams(vmem_limit_bytes=VMEM_LIMIT),
+        name="widen_pieces",
+    )(places, *pieces).reshape(reps * rows, columns)
+
+
+def resident(shape):
+    return pl.BlockSpec(shape, lambda i: (0, 0), pipeline_mode=pl.Buffered(1))
+
+
+def cost(flops):
+    return pl.CostEstimate(flops=flops, bytes_accessed=0, transcendentals=0)
+
+
+def feed_forward(rows, cotangents, gate_matrix, up_matrix, down_matrix):
+    count, width = rows.shape
+    units = gate_matrix.shape[1]
+
+    def body(rows_ref, cotangents_ref, gate_ref, up_ref, down_ref, inner_ref, d_gate_ref, d_up_ref):
+        gate = jnp.dot(rows_ref[...], gate_ref[...], preferred_element_type=jnp.float32)
+        up = jnp.dot(rows_ref[...], up_ref[...], preferred_element_type=jnp.float32)
+        sigmoid = jax.nn.sigmoid(gate)
+        silu = gate * sigmoid
+        inner_ref[...] = (silu * up).astype(jnp.bfloat16)
+        d_inner = times_transposed(cotangents_ref[...], down_ref[...])
+        d_up_ref[...] = (d_inner * silu).astype(jnp.bfloat16)
+        d_gate_ref[...] = (d_inner * up * sigmoid * (1.0 + gate * (1.0 - sigmoid))).astype(
+            jnp.bfloat16
         )
-    return [((c * first.size + f) * second.size + s, value) for c, f, s, value in placed]
-
-
-def sum_rep(blocks, axis, core, first, second):
-    shape = blocks.shape
-    blocks = blocks.reshape(shape[:axis] + (2, first.size, second.size) + shape[axis + 1 :])
-    for line in (core, first, second):
-        blocks = sum_line(blocks, line, axis)
-    return blocks
+
+    columns = pl.BlockSpec((width, TILE), lambda i: (0, i))
+    results = pl.BlockSpec((count, TILE), lambda i: (0, i))
+    return pl.pallas_call(
+        body,
+        grid=(pl.cdiv(units, TILE),),
+        out_shape=[jax.ShapeDtypeStruct((count, units), jnp.bfloat16)] * 3,
+        in_specs=[
+            resident((count, width)),
+            resident((count, width)),
+            columns,
+            columns,
+            pl.BlockSpec((TILE, width), lambda i: (i, 0)),
+        ],
+        out_specs=[results] * 3,
+        compiler_params=pltpu.CompilerParams(vmem_limit_bytes=VMEM_LIMIT),
+        cost_estimate=cost(2 * count * width * units),
+        name="feed_forward",
+    )(rows, cotangents, gate_matrix, up_matrix, down_matrix)
+
+
+def split_gradient(left, right, groups, core_place):
+    count, rows = left.shape
+    columns = right.shape[1]
+    half = rows // (2 * groups)
+
+    def body(core_ref, left_ref, right_ref, other_ref, own_ref, turned):
+        @pl.when(pl.program_id(0) == 0)
+        def turn():
+            turned[...] = left_ref[...].T
+
+        core = core_ref[0]
+        for out_ref, which in ((other_ref, 1 - core), (own_ref, core)):
+            for group in range(groups):
+                at = pl.multiple_of((2 * group + which) * half, 16)
+                out_ref[group * half : (group + 1) * half, :] = jnp.dot(
+                    turned[pl.ds(at, half), :], right_ref[...], preferred_element_type=jnp.float32
+                ).astype(jnp.bfloat16)
+
+    results = pl.BlockSpec((rows // 2, TILE), lambda i: (0, i))
+    return pl.pallas_call(
+        body,
+        grid=(pl.cdiv(columns, TILE),),
+        out_shape=[jax.ShapeDtypeStruct((rows // 2, columns), jnp.bfloat16)] * 2,
+        in_specs=[
+            pl.BlockSpec(memory_space=pltpu.SMEM),
+            resident((count, rows)),
+            pl.BlockSpec((count, TILE), lambda i: (0, i)),
+        ],
+        out_specs=[results] * 2,
+        scratch_shapes=[pltpu.VMEM((rows, count), jnp.bfloat16)],
+        compiler_params=pltpu.CompilerParams(vmem_limit_bytes=VMEM_LIMIT),
+        cost_estimate=cost(count * rows * columns),
+        name="split_gradient",
+    )(core_place.reshape(1).astype(jnp.int32), left, right)
+
+
+def rows_product(lefts, rights, turned, blocks):
+    count, depth = lefts[0].shape
+    columns = rights[0].shape[0 if turned else 1]
+    pairs, part = len(lefts), count // blocks
+
+    def body(*refs):
+        total = None
+        for left_ref, right_ref in zip(refs[:pairs], refs[pairs : 2 * pairs]):
+            if turned:
+                product = times_transposed(left_ref[...], right_ref[...])
+            else:
+                product = jnp.dot(
+                    left_ref[...], right_ref[...], preferred_element_type=jnp.float32
+                )
+            total = product if total is None else total + product
+        for block in range(blocks):
+            refs[2 * pairs + block][...] = total[block * part : (block + 1) * part].astype(
+                jnp.bfloat16
+            )
+
+    right_spec = (
+        pl.BlockSpec((TILE, depth), lambda i: (i, 0))
+        if turned
+        else pl.BlockSpec((depth, TILE), lambda i: (0, i))
+    )
+    return pl.pallas_call(
+        body,
+        grid=(pl.cdiv(columns, TILE),),
+        out_shape=[jax.ShapeDtypeStruct((part, columns), jnp.bfloat16)] * blocks,
+        in_specs=[resident((count, depth))] * pairs + [right_spec] * pairs,
+        out_specs=[pl.BlockSpec((part, TILE), lambda i: (0, i))] * blocks,
+        compiler_params=pltpu.CompilerParams(vmem_limit_bytes=VMEM_LIMIT),
+        cost_estimate=cost(pairs * count * depth * columns),
+        name="rows_product",
+    )(*lefts, *rights)
 
 
 def on_device(
@@ -209,41 +443,41 @@
     hidden_units = gate_weight.shape[1]
     block_units = hidden_units // shards
 
-    def gather_weight(weight):
-        piece = pick(weight.reshape(reps, part_rows, weight.shape[1]), rep_place, 0)
-        column = stack_by_place(gather_line(piece, shard), shard)
-        whole = jnp.zeros((shards, reps, part_rows, weight.shape[1]), weight.dtype)
-        for place, value in gather_rep(column, core, first, second):
-            whole = put(whole, value, place, 1)
-        return whole.reshape(width, weight.shape[1])
-
-    def gather_column_blocks(weights):
-        pieces = jnp.stack(
+    z_order = jnp.stack([shard.behind(step) for step in range(shards)]).astype(jnp.int32)
+
+    def weight_piece(weight):
+        return pick(weight.reshape(reps, part_rows, weight.shape[1]), rep_place, 0)
+
+    def column_pieces(weights):
+        return jnp.stack(
             [
-                pick(weight.reshape(reps, part_rows, hidden_units), rep_place, 0)
-                .reshape(part_rows, shards, block_units)
-                .transpose(1, 0, 2)
+                weight_piece(weight).reshape(part_rows, shards, block_units).transpose(1, 0, 2)
                 for weight in weights
             ],
             axis=1,
         )
-        rows = [pick(pieces, shard.place, 0)] + [
-            shard.shift(pick(pieces, shard.ahead(step), 0), step) for step in range(1, shards)
-        ]
-        column = stack_by_place(rows, shard, 1)
-        wholes = [jnp.zeros((shards, reps, part_rows, block_units), bf16) for _ in weights]
-        for place, value in gather_rep(column, core, first, second):
-            wholes = [put(whole, value[at], place, 1) for at, whole in enumerate(wholes)]
-        return [whole.reshape(width, block_units) for whole in wholes]
-
-    input_matrix = gather_weight(input_weight)
+
+    input_rows = gather_line(weight_piece(input_weight), shard)
     shard_vectors = jnp.concatenate([first_gain, second_gain, input_bias])
-    vector_rows = stack_by_place(gather_line(shard_vectors, shard), shard)
+    vector_rows = jnp.stack(in_place_order(gather_line(shard_vectors, shard), shard))
     own_gain = first_gain.shape[0]
     gain_one = vector_rows[:, :own_gain].reshape(width).astype(f32)
     gain_two = vector_rows[:, own_gain : 2 * own_gain].reshape(width).astype(f32)
     shift_row = vector_rows[:, 2 * own_gain :].reshape(-1).astype(f32)
 
+    output_piece, gate_weight, up_weight, *input_rows = tie(
+        weight_piece(output_weight), gate_weight, up_weight, *input_rows
+    )
+    output_rows = gather_line(output_piece, shard)
+    input_spread = Spread(jnp.stack(input_rows), core, first, second)
+    columns = column_pieces([gate_weight, up_weight])
+    columns, *output_rows = tie(columns, *output_rows)
+    column_rows = [pick(columns, shard.place, 0)] + [
+        shard.shift(pick(columns, shard.ahead(step), 0), step) for step in range(1, shards)
+    ]
+    input_spread.further()
+    input_matrix = place_blocks(z_order, *input_spread.finish()).reshape(width, -1)
+
     places = positions(segments)
     own_segments = lax.dynamic_slice_in_dim(segments, first_row, own_rows)
     cosine_table, sine_table = rope_tables(
@@ -253,9 +487,8 @@
     inverse_one = lax.rsqrt(jnp.mean(wide_tokens * wide_tokens, axis=-1, keepdims=True) + EPSILON)
     unit_one = wide_tokens * inverse_one
     normed_one = (unit_one * gain_one).astype(bf16)
-    output_matrix = gather_weight(output_weight)
-    gate_matrix, up_matrix = gather_column_blocks([gate_weight, up_weight])
-
+    output_column, input_matrix = tie(jnp.stack(output_rows), input_matrix)
+    output_spread = Spread(output_column, core, first, second)
     projected = jnp.dot(normed_one, input_matrix, preferred_element_type=f32) + shift_row
     queries = rotate(
         projected[:, :query_width].reshape(own_rows, QH, HD), cosine_table, sine_table
@@ -268,7 +501,22 @@
     own_pairs = jnp.concatenate(
         [key_part.reshape(own_rows, pair_width), projected[:, query_width + pair_width :]], axis=1
     ).astype(bf16)
-    pairs = jnp.concatenate(gather_line(own_pairs, shard), axis=0)
+    pair_rows = gather_line(own_pairs, shard)
+    output_spread.further()
+    output_matrix = place_blocks(z_order, *output_spread.finish()).reshape(width, width)
+    gate_up_column, output_matrix = tie(jnp.stack(column_rows, axis=1), output_matrix)
+    gate_up_spread = Spread(gate_up_column, core, first, second)
+    gate_up_spread.further()
+    gate_up_places, gate_up_pieces = gate_up_spread.finish()
+    gate_matrix, up_matrix = (
+        place_blocks(z_order, gate_up_places, [piece[at] for piece in gate_up_pieces]).reshape(
+            width, block_units
+        )
+        for at in range(2)
+    )
+    output_cotangent, *pair_rows = tie(output_cotangent, *pair_rows)
+    cotangents = jnp.concatenate(gather_line(output_cotangent, shard), axis=0)
+    pairs = jnp.concatenate(pair_rows, axis=0)
     group_rows = pairs.shape[0]
     row_index = jnp.arange(own_rows, dtype=jnp.int32)
     key_index = jnp.concatenate([shard.behind(step) * own_rows + row_index for step in range(shards)])
@@ -304,80 +552,86 @@
     unit_two = hidden * inverse_two
     normed_two = (unit_two * gain_two).astype(bf16)
 
-    cotangents = jnp.concatenate(gather_line(output_cotangent, shard), axis=0)
     group_normed = jnp.concatenate(gather_line(normed_two, shard), axis=0)
 
-    def sum_rows(rows):
-        blocks = rows.reshape(shards, own_rows, width)
-        total = blocks[0]
-        for step in range(1, shards):
-            total = total + shard.shift(blocks[step].astype(bf16), shards - step).astype(f32)
+    def send_rows(rows):
+        return [
+            shard.shift(rows[step].astype(bf16), shards - step) for step in range(1, shards)
+        ]
+
+    def add_rows(own, arrived):
+        total = own.astype(f32)
+        for block in arrived:
+            total = total + block.astype(f32)
         return total
 
-    gate_linear = jnp.dot(group_normed, gate_matrix, preferred_element_type=f32)
-    up_linear = jnp.dot(group_normed, up_matrix, preferred_element_type=f32)
-    gate_sigmoid = jax.nn.sigmoid(gate_linear)
-    gate_output = gate_linear * gate_sigmoid
-    inner_act = (gate_output * up_linear).astype(bf16)
-    inner_gradient = times_transposed(cotangents, down_weight)
-
-    down_blocks = transposed_times(inner_act, cotangents).astype(bf16)
-    down_piece = sum_rep(
-        down_blocks.reshape(reps, block_units // reps, width), 0, core, first, second
-    )
-
-    gate_gradient_rows = (
-        inner_gradient * up_linear * gate_sigmoid * (1.0 + gate_linear * (1.0 - gate_sigmoid))
-    ).astype(bf16)
-    up_gradient_rows = (inner_gradient * gate_output).astype(bf16)
-    normed_two_gradient = sum_rows(
-        times_transposed(gate_gradient_rows, gate_matrix)
-        + times_transposed(up_gradient_rows, up_matrix)
-    )
-
-    def column_gradient(gradient_rows):
-        partial = transposed_times(group_normed, gradient_rows).astype(bf16)
-        piece = sum_rep(
-            partial.reshape(shards, reps, part_rows, block_units), 1, core, first, second
-        )
-        rows = [pick(piece, shard.place, 0)] + [
-            shard.shift(pick(piece, shard.ahead(step), 0), step) for step in range(1, shards)
-        ]
-        return (
-            stack_by_place(rows, shard).transpose(1, 0, 2).reshape(part_rows, shards * block_units)
-        )
-
-    def spread(piece):
-        rows = piece.shape[0]
-        whole = jnp.zeros((reps,) + piece.shape, f32)
-        for place, value in gather_rep(piece, core, first, second):
-            whole = put(whole, value.astype(f32), place, 0)
-        return whole.reshape(reps * rows, piece.shape[1])
-
-    gate_piece = column_gradient(gate_gradient_rows)
-    up_piece = column_gradient(up_gradient_rows)
-    down_total = spread(down_piece)
-    gate_total = spread(gate_piece)
-    up_total = spread(up_piece)
-    block_out = (
-        hidden + sum_rows(jnp.dot(inner_act, down_weight, preferred_element_type=f32))
-    ).astype(bf16)
-
+    def by_columns(piece):
+        rows = [pick(piece, shard.place, 0)] + send_sums(piece, shard, 0)
+        return jnp.concatenate(in_place_order(rows, shard), axis=1)
+
+    plane = (first.size, second.size)
+
+    def add_half(own, arrived, shape):
+        return (own.astype(f32) + arrived.astype(f32)).astype(bf16).reshape(shape)
+
+    by_rows = (shards,) + plane + (part_rows, block_units)
+    by_units = plane + (block_units // reps, width)
+
+    inner_act, gate_gradient_rows, up_gradient_rows = feed_forward(
+        group_normed, cotangents, gate_matrix, up_matrix, down_weight
+    )
+
+    down_sent, down_own = split_gradient(inner_act, cotangents, 1, core.place)
+    gate_gradient_rows, up_gradient_rows, down_own = tie(
+        gate_gradient_rows, up_gradient_rows, down_own
+    )
+    down_arrived = core.shift(down_sent, 1)
+    normed_own, *normed_partial = rows_product(
+        (gate_gradient_rows, up_gradient_rows), (gate_matrix, up_matrix), True, shards
+    )
+    normed_arrived = send_rows([None] + normed_partial)
+
+    down_arrived, normed_own = tie(down_arrived, normed_own)
+    down_sum = add_half(down_own, down_arrived, by_units)
+    group_normed, down_sum = tie(group_normed, down_sum)
+    down_first = send_sums(down_sum, first, 0)
+    gate_sent, gate_own = split_gradient(group_normed, gate_gradient_rows, shards, core.place)
+    up_gradient_rows, gate_own = tie(up_gradient_rows, gate_own)
+    gate_arrived = core.shift(gate_sent, 1)
+    up_sent, up_own = split_gradient(group_normed, up_gradient_rows, shards, core.place)
+    gate_arrived, up_own = tie(gate_arrived, up_own)
+    up_arrived = core.shift(up_sent, 1)
+    gate_sum = add_half(gate_own, gate_arrived, by_rows)
+    *down_first, gate_sum = tie(*down_first, gate_sum)
+    gate_first = send_sums(gate_sum, first, 1)
+    down_sum = add_sums(down_sum, first, 0, down_first)
+    up_arrived, down_sum = tie(up_arrived, down_sum)
+    down_second = send_sums(down_sum, second, 0)
+    up_sum = add_half(up_own, up_arrived, by_rows)
+    *gate_first, up_sum = tie(*gate_first, up_sum)
+    up_first = send_sums(up_sum, first, 1)
+    gate_sum = add_sums(gate_sum, first, 1, gate_first)
+    *down_second, gate_sum = tie(*down_second, gate_sum)
+    gate_second = send_sums(gate_sum, second, 1)
+    down_piece = add_sums(down_sum, second, 0, down_second)
+
+    *normed_arrived, down_piece = tie(*normed_arrived, down_piece)
+    down_spread = Spread(down_piece, core, first, second)
+    normed_two_gradient = add_rows(normed_own, normed_arrived)
     gain_two_gradient = jnp.sum(normed_two_gradient * unit_two, axis=0)
     hidden_gradient = output_cotangent.astype(f32) + norm_back(
         normed_two_gradient, unit_two, inverse_two, gain_two
     )
     branch_gradient = hidden_gradient.astype(bf16)
-
-    def row_gradient(partial):
-        columns = partial.shape[1]
-        piece = sum_rep(
-            partial.astype(bf16).reshape(shards, reps, part_rows, columns), 1, core, first, second
-        )
-        return spread(sum_line(piece, shard, 0))
-
-    output_total = row_gradient(transposed_times(attention_low, branch_gradient))
+    *up_first, branch_gradient = tie(*up_first, branch_gradient)
+    up_sum = add_sums(up_sum, first, 1, up_first)
+
     attention_gradient = times_transposed(branch_gradient, output_matrix).astype(bf16)
+    *gate_second, attention_gradient, up_sum = tie(*gate_second, attention_gradient, up_sum)
+    up_second = send_sums(up_sum, second, 1)
+    gate_sum = add_sums(gate_sum, second, 1, gate_second)
+    gate_piece = by_columns(gate_sum)
+
     grouped_gradient = attention_gradient.reshape(own_rows, KVH, per_group, HD)
     share_gradient = jnp.einsum(
         "tkgd,jkd->kgtj", grouped_gradient, values, preferred_element_type=f32
@@ -401,11 +655,26 @@
         ],
         axis=1,
     ).reshape(shards, own_rows, 2 * pair_width)
-    pair_gradients = pair_blocks[0]
-    for step in range(1, shards):
-        pair_gradients = pair_gradients + shard.shift(
-            pair_blocks[step].astype(bf16), shards - step
-        ).astype(f32)
+    pair_own = pair_blocks[0]
+    pair_arrived = send_rows(pair_blocks)
+
+    *down_moved, pair_own = tie(*down_spread.arrived(), pair_own)
+    down_spread.replace(down_moved)
+    down_spread.further()
+    output_sent, output_own = split_gradient(
+        attention_low, branch_gradient, shards, core.place
+    )
+    output_arrived = core.shift(output_sent, 1)
+    *up_second, gate_piece, pair_own = tie(*up_second, gate_piece, pair_own)
+    gate_spread = Spread(gate_piece, core, first, second)
+    up_sum = add_sums(up_sum, second, 1, up_second)
+    up_piece = by_columns(up_sum)
+    output_arrived, up_sum, output_own = tie(output_arrived, up_sum, output_own)
+    output_sum = add_half(output_own, output_arrived, (shards,) + plane + (part_rows, width))
+    output_first = send_sums(output_sum, first, 1)
+
+    *pair_arrived, output_sum = tie(*pair_arrived, output_sum)
+    pair_gradients = add_rows(pair_own, pair_arrived)
     query_back = rotate_back(
         (query_gradient * score_scale).reshape(own_rows, QH, HD), cosine_table, sine_table
     ).reshape(own_rows, query_width)
@@ -415,14 +684,67 @@
     projected_gradient = jnp.concatenate(
         [query_back, key_back, pair_gradients[:, pair_width:]], axis=1
     ).astype(bf16)
-    input_total = row_gradient(transposed_times(normed_one, projected_gradient))
+    *down_moved, projected_gradient = tie(*down_spread.arrived(), projected_gradient)
+    down_spread.replace(down_moved)
+    down_places, down_pieces = down_spread.finish()
+    input_sent, input_own = split_gradient(normed_one, projected_gradient, shards, core.place)
+    input_arrived = core.shift(input_sent, 1)
+    up_spread = Spread(up_piece, core, first, second)
+
+    *gate_moved, input_own = tie(*gate_spread.arrived(), input_own)
+    gate_spread.replace(gate_moved)
+    gate_spread.further()
+    *output_first, input_own = tie(*output_first, input_own)
+    output_sum = add_sums(output_sum, first, 1, output_first)
+    output_second = send_sums(output_sum, second, 1)
     bias_gradient = jnp.sum(projected_gradient.astype(f32), axis=0)
     bias_split = query_width + pair_width
     normed_one_gradient = times_transposed(projected_gradient, input_matrix)
+    normed_one_gradient, input_arrived, input_own = tie(
+        normed_one_gradient, input_arrived, input_own
+    )
+    input_sum = add_half(
+        input_own, input_arrived, (shards,) + plane + (part_rows, projected_gradient.shape[1])
+    )
+    input_first = send_sums(input_sum, first, 1)
     gain_one_gradient = jnp.sum(normed_one_gradient * unit_one, axis=0)
     tokens_gradient = (
         hidden_gradient + norm_back(normed_one_gradient, unit_one, inverse_one, gain_one)
     ).astype(bf16)
+
+    inner_act, input_sum = tie(inner_act, input_sum)
+    block_own, *block_partial = rows_product((inner_act,), (down_weight,), False, shards)
+    block_arrived = send_rows([None] + block_partial)
+    down_total = widen_pieces(down_places, down_pieces)
+    *input_first, down_total, block_own = tie(*input_first, down_total, block_own)
+    input_sum = add_sums(input_sum, first, 1, input_first)
+    input_second = send_sums(input_sum, second, 1)
+    *output_second, input_sum = tie(*output_second, input_sum)
+    output_sum = add_sums(output_sum, second, 1, output_second)
+    output_piece = add_sums(output_sum, shard, 0, send_sums(output_sum, shard, 0))
+    *gate_moved, input_sum = tie(*gate_spread.arrived(), input_sum)
+    gate_spread.replace(gate_moved)
+    gate_places, gate_pieces = gate_spread.finish()
+    *input_second, output_sum = tie(*input_second, output_sum)
+    input_sum = add_sums(input_sum, second, 1, input_second)
+    input_shard = send_sums(input_sum, shard, 0)
+    *up_moved, input_sum = tie(*up_spread.arrived(), input_sum)
+    up_spread.replace(up_moved)
+    up_spread.further()
+    gate_total = widen_pieces(gate_places, gate_pieces)
+    output_spread = Spread(output_piece, core, first, second)
+    output_spread.further()
+    up_places, up_pieces = up_spread.finish()
+    block_out = add_rows(hidden, [block_own] + block_arrived).astype(bf16)
+    output_total = widen_pieces(*output_spread.finish())
+    input_shard, gate_total, block_out = (
+        lambda *parts: (parts[:-2], parts[-2], parts[-1])
+    )(*tie(*input_shard, gate_total, block_out))
+    input_piece = add_sums(input_sum, shard, 0, input_shard)
+    input_spread = Spread(input_piece, core, first, second)
+    input_spread.further()
+    up_total = widen_pieces(up_places, up_pieces)
+    input_total = widen_pieces(*input_spread.finish())
 
     small_parts = (
         gain_one_gradient,
@@ -431,7 +753,7 @@
         bias_gradient[bias_split:],
     )
     small_rows = jnp.concatenate([part.reshape(shards, -1) for part in small_parts], axis=1)
-    small = sum_line(small_rows, shard, 0)
+    small = add_sums(small_rows, shard, 0, send_sums(small_rows, shard, 0))
     for line in (core, first, second):
         total = small
         for step in range(1, line.size):

time: 902 us -> 760 us (0.84)
  Pallas kernels: 0 us -> 141 us
  local copies, waits for them, and re-layouts: 206 us -> 108 us
  matrix products: 125 us -> 29.3 us
  waiting for transfers between devices: 342 us -> 257 us
  other arithmetic: 100 us -> 78.2 us
  starting transfers between devices: 117 us -> 134 us
    pallas_call x0 -> x17, Pallas kernels: none -> 141 us  [the longest x5 40.8 us: split_gradient(): pl.pallas_call(body, grid=(pl.cdiv(columns, TILE),), out_shape=[jax.Shape...]
    ppermute x119, waiting for transfers between devices: 342 us -> 257 us  [shift(): return lax.ppermute(value, self.name, self.pairs(step % self.size))]
    dot_general x8 -> x0, matrix products: 72.4 us -> none  [the longest x5 30.6 us: transposed_times(): lax.dot_general(left_side, right_side, (((0,), (0,)), ((), ())), preferre...]
    dynamic_update_slice x49 -> x0, local copies, waits for them, and re-layouts: 57.9 us -> none  [put(): return lax.dynamic_update_index_in_dim(array, piece, index, axis)]
    dynamic_update_slice x38 -> x0, other arithmetic: 40.8 us -> none  [put(): return lax.dynamic_update_index_in_dim(array, piece, index, axis)]
    dot_general x5 -> x2, matrix products: 33.2 us -> 6.98 us  [times_transposed(): lax.dot_general(left_side, right_side, (((1,), (1,)), ((), ())), preferre...]
    convert_element_type x4 -> x0, local copies, waits for them, and re-layouts: 25.4 us -> none  [the longest x2 20.4 us: column_gradient(): partial = transposed_times(group_normed, gradient_rows).astype(bf16)]
    broadcast_in_dim x19 -> x0, local copies, waits for them, and re-layouts: 20.6 us -> none  [the longest x10 9.44 us: put(): return lax.dynamic_update_index_in_dim(array, piece, index, axis)]
  transfers between devices with their start and end apart: 119 -> 119, of which waited for: 44 -> 32; matrix products, arithmetic and copies ran while one was open for 39% -> 25% of each run, Pallas kernels for 0% -> 8%
where the time goes in v2:
time: 760 us; the launch traced here: 751 us
  waiting for transfers between devices  257 us (34%)
  Pallas kernels  141 us (19%)
  starting transfers between devices  134 us (18%)
  local copies, waits for them, and re-layouts  108 us (14%)
  other arithmetic  78.2 us (10%)
  matrix products  29.3 us (4%)
    ppermute x119, waiting for transfers between devices, shift(): return lax.ppermute(value, self.name, self.pairs(step % self.size))  257 us
    ppermute x119, starting transfers between devices, shift(): return lax.ppermute(value, self.name, self.pairs(step % self.size))  134 us
    pallas_call x5, Pallas kernels, split_gradient(): pl.pallas_call(body, grid=(pl.cdiv(columns, TILE),), out_shape=[jax.Shape...  40.8 us
    pallas_call x5, Pallas kernels, widen_pieces(): pl.pallas_call(body, out_shape=jax.ShapeDtypeStruct((reps, rows, columns)...  28.5 us
    pallas_call x4, Pallas kernels, place_blocks(): pl.pallas_call(body, out_shape=jax.ShapeDtypeStruct((shards, reps) + bloc...  25.2 us
    pallas_call x2, Pallas kernels, rows_product(): pl.pallas_call(body, grid=(pl.cdiv(columns, TILE),), out_shape=[jax.Shape...  23.2 us
    pallas_call x1, Pallas kernels, feed_forward(): pl.pallas_call(body, grid=(pl.cdiv(units, TILE),), out_shape=[jax.ShapeDt...  22.8 us
    unnamed x190, local copies, waits for them, and re-layouts  21.8 us
  transfers between devices with their start and end apart: 119, of which 32 were waited for; matrix products, arithmetic and copies ran while one was open for 25% of the time, Pallas kernels for 8%

profile of v2, /device:TPU:0, one launch (start us, length us, event | category | flops | bytes accessed | tf_op | source)
XLA Modules:
  0.0 750.7 jit_solution(6561801271435129161)
XLA Ops:
  54.7 12.6 %collective-permute-done.2 = bf16[1280]{0:T(1024)(128)(2,1)S(1)} collective-permute-done((bf16[1280]{0:T(1024)(128)(2,1)S(1)}, bf16[1280]{0:T(1024)(128)(2,1)S(1)}, u32[]{:S(2)}, u32[]{:S(2)}) %collective-permute-start.2) | collective-permute-done | bytes 2592 | tf_op jit(solution)/shard_map/ppermute | solution.py:74
  68.3 10.2 %collective-permute-start.19 = (bf16[2,48,2240]{2,1,0:T(8,128)(2,1)}, bf16[2,48,2240]{2,1,0:T(8,128)(2,1)}, u32[]{:S(2)}, u32[]{:S(2)}) collective-permute-start(bf16[2,48,2240]{2,1,0:T(8,128)(2,1)} %bitcast.314), channel_id=1, source_target_pairs={{0,1},{1,2},{2,3},{3,0},{4,5},{5,6},{6,7},{7,4},{8,9},{9,10},{10,1... | collective-permute-start | bytes 1290248 | tf_op jit(solution)/shard_map/ppermute | solution.py:74
  78.5 7.4 collective-permute-done.20
  91.7 6.3 place_blocks.4
  142.9 18.5 %collective-permute-done.33 = bf16[160,1536]{1,0:T(8,128)(2,1)} collective-permute-done((bf16[160,1536]{1,0:T(8,128)(2,1)}, bf16[160,1536]{1,0:T(8,128)(2,1)}, u32[]{:S(2)}, u32[]{:S(2)}) %collective-permute-start.33) | collective-permute-done | bytes 491552 | tf_op jit(solution)/shard_map/ppermute | solution.py:74
  176.6 9.0 %collective-permute-start.31 = (bf16[160,1536]{1,0:T(8,128)(2,1)S(1)}, bf16[160,1536]{1,0:T(8,128)(2,1)S(1)}, u32[]{:S(2)}, u32[]{:S(2)}) collective-permute-start(bf16[160,1536]{1,0:T(8,128)(2,1)S(1)} %multiply_convert_fusion), channel_id=1, source_target_pairs={{0,3},{1,0},{2,1},{3,2},{4,7},{5,4},{6,5},{7,6},{8,11},{9,8},{10,9... | collective-permute-start | bytes 1474568 | tf_op jit(solution)/shard_map/ppermute | solution.py:74
  188.0 9.3 %collective-permute-done.31 = bf16[160,1536]{1,0:T(8,128)(2,1)S(1)} collective-permute-done((bf16[160,1536]{1,0:T(8,128)(2,1)S(1)}, bf16[160,1536]{1,0:T(8,128)(2,1)S(1)}, u32[]{:S(2)}, u32[]{:S(2)}) %collective-permute-start.31) | collective-permute-done | bytes 491552 | tf_op jit(solution)/shard_map/ppermute | solution.py:74
  197.3 29.6 %collective-permute-done.30 = bf16[160,1536]{1,0:T(8,128)(2,1)S(1)} collective-permute-done((bf16[160,1536]{1,0:T(8,128)(2,1)S(1)}, bf16[160,1536]{1,0:T(8,128)(2,1)S(1)}, u32[]{:S(2)}, u32[]{:S(2)}) %collective-permute-start.30) | collective-permute-done | bytes 491552 | tf_op jit(solution)/shard_map/ppermute | solution.py:74
  234.3 16.5 %collective-permute-done.37 = bf16[2,4,48,2240]{3,2,1,0:T(8,128)(2,1)S(1)} collective-permute-done((bf16[2,4,48,2240]{3,2,1,0:T(8,128)(2,1)S(1)}, bf16[2,4,48,2240]{3,2,1,0:T(8,128)(2,1)S(1)}, u32[]{:S(2)}, u32[]{:S(2)}) %collective-permute-start.37) | collective-permute-done | bytes 1720352 | tf_op jit(solution)/shard_map/ppermute | solution.py:74
  256.3 7.0 place_blocks.6
  263.3 7.0 place_blocks.7
  270.3 22.8 %feed_forward.1 = (bf16[640,2240]{1,0:T(8,128)(2,1)}, bf16[640,2240]{1,0:T(8,128)(2,1)}, bf16[640,2240]{1,0:T(8,128)(2,1)}) custom-call(bf16[640,1536]{1,0:T(8,128)(2,1)} %pad_maximum_fusion.rows_ref.left_ref, bf16[640,1536]{1,0:T(8,128)(2,1)} %copy-done.31, bf16[1536,2240]{1,0:T(8,128)(2,1)} %bitcast.320, bf16[1536,2240]{1,0:T(8,128)(2,1)} %bitcast.322, ...), custom_call_target="tpu_custom_call" | custom-call | flops 4404019200 | tf_op jit(solution)/shard_map/feed_forward/pallas_call | solution.py:327
  293.1 9.8 %split_gradient.5 = (bf16[1120,1536]{1,0:T(8,128)(2,1)}, bf16[1120,1536]{1,0:T(8,128)(2,1)}) custom-call(s32[1]{0:T(128)} %bitcast.core_ref, bf16[640,2240]{1,0:T(8,128)(2,1)} %get-tuple-element.215.left_ref.refs_0_, bf16[640,1536]{1,0:T(8,128)(2,1)} %copy-done.31), custom_call_target="tpu_custom_call" | custom-call | flops 2202009600 | tf_op jit(solution)/shard_map/split_gradient/pallas_call | solution.py:364
  303.4 14.8 %rows_product.2 = (bf16[160,1536]{1,0:T(8,128)(2,1)}, bf16[160,1536]{1,0:T(8,128)(2,1)}, bf16[160,1536]{1,0:T(8,128)(2,1)}, bf16[160,1536]{1,0:T(8,128)(2,1)}) custom-call(bf16[640,2240]{1,0:T(8,128)(2,1)} %get-tuple-element.152.refs_0_.right_ref, bf16[640,2240]{1,0:T(8,128)(2,1)} %get-tuple-element.158.refs_1_.right_ref, bf16[1536,2240]{1,0:T(8,128)(2,1)} %bitcast.321, ...), custom_call_target="tpu_custom_call" | custom-call | flops 4404019200 | tf_op jit(solution)/shard_map/rows_product/pallas_call | solution.py:406
  322.9 10.5 %split_gradient.6 = (bf16[768,2240]{1,0:T(8,128)(2,1)}, bf16[768,2240]{1,0:T(8,128)(2,1)}) custom-call(s32[1]{0:T(128)} %bitcast.core_ref, bf16[640,1536]{1,0:T(8,128)(2,1)} %pad_maximum_fusion.rows_ref.left_ref, bf16[640,2240]{1,0:T(8,128)(2,1)} %get-tuple-element.152.refs_0_.right_ref), custom_call_target="tpu_custom_call" | custom-call | flops 2202009600 | tf_op jit(solution)/shard_map/split_gradient/pallas_call | solution.py:364
  339.1 10.6 %split_gradient.7 = (bf16[768,2240]{1,0:T(8,128)(2,1)}, bf16[768,2240]{1,0:T(8,128)(2,1)}) custom-call(s32[1]{0:T(128)} %bitcast.core_ref, bf16[640,1536]{1,0:T(8,128)(2,1)} %pad_maximum_fusion.rows_ref.left_ref, bf16[640,2240]{1,0:T(8,128)(2,1)} %get-tuple-element.158.refs_1_.right_ref), custom_call_target="tpu_custom_call" | custom-call | flops 2202009600 | tf_op jit(solution)/shard_map/split_gradient/pallas_call | solution.py:364
  349.7 5.7 copy.156
  365.2 5.8 copy.158
  375.0 6.0 collective-permute-done.44
  397.6 17.2 %collective-permute-done.47 = bf16[4,2,48,2240]{3,2,0,1:T(8,128)(2,1)} collective-permute-done((bf16[4,2,48,2240]{3,2,0,1:T(8,128)(2,1)}, bf16[4,2,48,2240]{3,2,0,1:T(8,128)(2,1)}, u32[]{:S(2)}, u32[]{:S(2)}) %collective-permute-start.47) | collective-permute-done | bytes 1720352 | tf_op jit(solution)/shard_map/ppermute | solution.py:74
  428.5 29.4 %collective-permute-done.49 = bf16[4,2,48,2240]{3,2,0,1:T(8,128)(2,1)S(1)} collective-permute-done((bf16[4,2,48,2240]{3,2,0,1:T(8,128)(2,1)S(1)}, bf16[4,2,48,2240]{3,2,0,1:T(8,128)(2,1)S(1)}, u32[]{:S(2)}, u32[]{:S(2)}) %collective-permute-start.49) | collective-permute-done | bytes 1720352 | tf_op jit(solution)/shard_map/ppermute | solution.py:74
  551.4 10.8 %collective-permute-done.93 = bf16[48,2240]{1,0:T(8,128)(2,1)S(1)} collective-permute-done((bf16[48,2240]{1,0:T(8,128)(2,1)}, bf16[48,2240]{1,0:T(8,128)(2,1)S(1)}, u32[]{:S(2)}, u32[]{:S(2)}) %collective-permute-start.93) | collective-permute-done | bytes 215072 | tf_op jit(solution)/shard_map/ppermute | solution.py:74
  572.8 6.0 collective-permute-done.67
  587.3 7.3 widen_pieces.5
  607.0 8.4 %rows_product.3 = (bf16[160,1536]{1,0:T(8,128)(2,1)}, bf16[160,1536]{1,0:T(8,128)(2,1)}, bf16[160,1536]{1,0:T(8,128)(2,1)}, bf16[160,1536]{1,0:T(8,128)(2,1)}) custom-call(bf16[640,2240]{1,0:T(8,128)(2,1)} %get-tuple-element.215.left_ref.refs_0_, bf16[2240,1536]{1,0:T(8,128)(2,1)} %refs_1_.1), custom_call_target="tpu_custom_call" | custom-call | flops 2202009600 | tf_op jit(solution)/shard_map/rows_product/pallas_call | solution.py:406
  631.9 19.9 %collective-permute-done.84 = bf16[160,1536]{1,0:T(8,128)(2,1)S(1)} collective-permute-done((bf16[160,1536]{1,0:T(8,128)(2,1)}, bf16[160,1536]{1,0:T(8,128)(2,1)S(1)}, u32[]{:S(2)}, u32[]{:S(2)}) %collective-permute-start.84) | collective-permute-done | bytes 491552 | tf_op jit(solution)/shard_map/ppermute | solution.py:74
  655.2 8.5 %collective-permute-done.75 = bf16[4,48,2048]{2,1,0:T(8,128)(2,1)S(1)} collective-permute-done((bf16[4,48,2048]{2,1,0:T(8,128)(2,1)S(1)}, bf16[4,48,2048]{2,1,0:T(8,128)(2,1)S(1)}, u32[]{:S(2)}, u32[]{:S(2)}) %collective-permute-start.75) | collective-permute-done | bytes 786464 | tf_op jit(solution)/shard_map/ppermute | solution.py:74
  664.3 9.8 %collective-permute-start.106 = (bf16[48,1536]{1,0:T(8,128)(2,1)S(1)}, bf16[48,1536]{1,0:T(8,128)(2,1)S(1)}, u32[]{:S(2)}, u32[]{:S(2)}) collective-permute-start(bf16[48,1536]{1,0:T(8,128)(2,1)S(1)} %get-tuple-element.296), channel_id=1, source_target_pairs={{0,3},{1,0},{2,1},{3,2},{4,7},{5,4},{6,5},{7,6},{8,11},{9,8},{10,9... | collective-permute-start | bytes 442376 | tf_op jit(solution)/shard_map/ppermute | solution.py:74
  678.4 8.8 %collective-permute-done.105 = bf16[48,1536]{1,0:T(8,128)(2,1)S(1)} collective-permute-done((bf16[48,1536]{1,0:T(8,128)(2,1)S(1)}, bf16[48,1536]{1,0:T(8,128)(2,1)S(1)}, u32[]{:S(2)}, u32[]{:S(2)}) %collective-permute-start.105) | collective-permute-done | bytes 147488 | tf_op jit(solution)/shard_map/ppermute | solution.py:74
  694.6 7.3 widen_pieces.6
  707.9 12.6 %collective-permute-done.109.refs_3_ = bf16[48,1536]{1,0:T(8,128)(2,1)S(1)} collective-permute-done((bf16[48,1536]{1,0:T(8,128)(2,1)S(1)}, bf16[48,1536]{1,0:T(8,128)(2,1)S(1)}, u32[]{:S(2)}, u32[]{:S(2)}) %collective-permute-start.109) | collective-permute-done | bytes 147488 | tf_op jit(solution)/shard_map/ppermute | solution.py:74
  742.7 7.4 widen_pieces.9
  (588 shorter events, 374.9 us)
Async XLA Ops:
  11.7 38.2 %collective-permute-start = (bf16[1280]{0:T(1024)(128)(2,1)S(1)}, bf16[1280]{0:T(1024)(128)(2,1)S(1)}, u32[]{:S(2)}, u32[]{:S(2)}) collective-permute-start(bf16[1280]{0:T(1024)(128)(2,1)S(1)} %dynamic-update-slice.10), channel_id=1, source_target_pairs={{0,3},{1,0},{2,1},{3,2},{4,7},{5,4},{6,5},{7,6},{8,11},{9,8},{10,9... | collective-permute-start | bytes 7688 | tf_op jit(solution)/shard_map/ppermute | solution.py:74
  36.1 49.8 %collective-permute-start.10 = (bf16[4,48,2048]{2,1,0:T(8,128)(2,1)}, bf16[4,48,2048]{2,1,0:T(8,128)(2,1)S(1)}, u32[]{:S(2)}, u32[]{:S(2)}) collective-permute-start(bf16[4,48,2048]{2,1,0:T(8,128)(2,1)} %pad_maximum_fusion.5.refs_0_), channel_id=1, source_target_pairs={{0,8},{4,20},{8,0},{12,28},{16,24},{20,4},{24,16},{28,12},{1,9},{5... | collective-permute-start | bytes 2359304 | tf_op jit(solution)/shard_map/ppermute | solution.py:74
  43.0 43.4 %collective-permute-start.11 = (bf16[4,48,2048]{2,1,0:T(8,128)(2,1)}, bf16[4,48,2048]{2,1,0:T(8,128)(2,1)}, u32[]{:S(2)}, u32[]{:S(2)}) collective-permute-start(bf16[4,48,2048]{2,1,0:T(8,128)(2,1)} %collective-permute-done.9.refs_1_), channel_id=1, source_target_pairs={{0,8},{4,20},{8,0},{12,28},{16,24},{20,4},{24,16},{28,12},{1,9},{5... | collective-permute-start | bytes 2359304 | tf_op jit(solution)/shard_map/ppermute | solution.py:74
  49.9 36.0 %collective-permute-start.20 = (bf16[2,48,2240]{2,1,0:T(8,128)(2,1)}, bf16[2,48,2240]{2,1,0:T(8,128)(2,1)}, u32[]{:S(2)}, u32[]{:S(2)}) collective-permute-start(bf16[2,48,2240]{2,1,0:T(8,128)(2,1)} %bitcast.313), channel_id=1, source_target_pairs={{0,2},{1,3},{2,0},{3,1},{4,6},{5,7},{6,4},{7,5},{8,10},{9,11},{10,... | collective-permute-start | bytes 1290248 | tf_op jit(solution)/shard_map/ppermute | solution.py:74
  126.6 34.8 %collective-permute-start.33 = (bf16[160,1536]{1,0:T(8,128)(2,1)}, bf16[160,1536]{1,0:T(8,128)(2,1)}, u32[]{:S(2)}, u32[]{:S(2)}) collective-permute-start(bf16[160,1536]{1,0:T(8,128)(2,1)} %param.21), channel_id=1, source_target_pairs={{0,2},{1,3},{2,0},{3,1},{4,6},{5,7},{6,4},{7,5},{8,10},{9,11},{10,... | collective-permute-start | bytes 1474568 | tf_op jit(solution)/shard_map/ppermute | solution.py:74
  127.1 36.9 %collective-permute-start.34 = (bf16[160,1536]{1,0:T(8,128)(2,1)}, bf16[160,1536]{1,0:T(8,128)(2,1)}, u32[]{:S(2)}, u32[]{:S(2)}) collective-permute-start(bf16[160,1536]{1,0:T(8,128)(2,1)} %param.21), channel_id=1, source_target_pairs={{0,3},{1,0},{2,1},{3,2},{4,7},{5,4},{6,5},{7,6},{8,11},{9,8},{10,9... | collective-permute-start | bytes 1474568 | tf_op jit(solution)/shard_map/ppermute | solution.py:74
  172.1 56.1 %collective-permute-start.35 = (bf16[2,4,48,2240]{3,2,1,0:T(8,128)(2,1)S(1)}, bf16[2,4,48,2240]{3,2,1,0:T(8,128)(2,1)S(1)}, u32[]{:S(2)}, u32[]{:S(2)}) collective-permute-start(bf16[2,4,48,2240]{3,2,1,0:T(8,128)(2,1)S(1)} %copy-done.10), channel_id=1, source_target_pairs={{0,16},{4,12},{8,24},{12,4},{16,0},{20,28},{24,8},{28,20},{1,17},{... | collective-permute-start | bytes 5160968 | tf_op jit(solution)/shard_map/ppermute | solution.py:74
  185.6 41.3 %collective-permute-start.30 = (bf16[160,1536]{1,0:T(8,128)(2,1)S(1)}, bf16[160,1536]{1,0:T(8,128)(2,1)S(1)}, u32[]{:S(2)}, u32[]{:S(2)}) collective-permute-start(bf16[160,1536]{1,0:T(8,128)(2,1)S(1)} %multiply_convert_fusion), channel_id=1, source_target_pairs={{0,2},{1,3},{2,0},{3,1},{4,6},{5,7},{6,4},{7,5},{8,10},{9,11},{10,... | collective-permute-start | bytes 1474568 | tf_op jit(solution)/shard_map/ppermute | solution.py:74
  185.6 41.3 %collective-permute-start.29 = (bf16[160,1536]{1,0:T(8,128)(2,1)S(1)}, bf16[160,1536]{1,0:T(8,128)(2,1)S(1)}, u32[]{:S(2)}, u32[]{:S(2)}) collective-permute-start(bf16[160,1536]{1,0:T(8,128)(2,1)S(1)} %multiply_convert_fusion), channel_id=1, source_target_pairs={{0,1},{1,2},{2,3},{3,0},{4,5},{5,6},{6,7},{7,4},{8,9},{9,10},{10,1... | collective-permute-start | bytes 1474568 | tf_op jit(solution)/shard_map/ppermute | solution.py:74
  186.2 45.0 %collective-permute-start.36 = (bf16[2,4,48,2240]{3,2,1,0:T(8,128)(2,1)S(1)}, bf16[2,4,48,2240]{3,2,1,0:T(8,128)(2,1)S(1)}, u32[]{:S(2)}, u32[]{:S(2)}) collective-permute-start(bf16[2,4,48,2240]{3,2,1,0:T(8,128)(2,1)S(1)} %copy-done.10), channel_id=1, source_target_pairs={{0,8},{4,20},{8,0},{12,28},{16,24},{20,4},{24,16},{28,12},{1,9},{5... | collective-permute-start | bytes 5160968 | tf_op jit(solution)/shard_map/ppermute | solution.py:74
  197.3 35.7 %collective-permute-start.38 = (bf16[2,4,48,2240]{3,2,1,0:T(8,128)(2,1)S(1)}, bf16[2,4,48,2240]{3,2,1,0:T(8,128)(2,1)S(1)}, u32[]{:S(2)}, u32[]{:S(2)}) collective-permute-start(bf16[2,4,48,2240]{3,2,1,0:T(8,128)(2,1)S(1)} %copy-done.10), channel_id=1, source_target_pairs={{0,4},{4,0},{8,12},{12,8},{16,20},{20,16},{24,28},{28,24},{1,5},{5... | collective-permute-start | bytes 5160968 | tf_op jit(solution)/shard_map/ppermute | solution.py:74
  355.5 30.7 %collective-permute-start.43 = (bf16[768,2240]{0,1:T(8,128)(2,1)}, bf16[768,2240]{0,1:T(8,128)(2,1)}, u32[]{:S(2)}, u32[]{:S(2)}) collective-permute-start(bf16[768,2240]{0,1:T(8,128)(2,1)} %copy.156), channel_id=1, source_target_pairs={{0,4},{4,0},{8,12},{12,8},{16,20},{20,16},{24,28},{28,24},{1,5},{5... | collective-permute-start | bytes 10321928 | tf_op jit(solution)/shard_map/ppermute | solution.py:74
  360.2 60.6 %collective-permute-start.50 = (bf16[160,1536]{1,0:T(8,128)(2,1)}, bf16[160,1536]{1,0:T(8,128)(2,1)}, u32[]{:S(2)}, u32[]{:S(2)}) collective-permute-start(bf16[160,1536]{1,0:T(8,128)(2,1)} %get-tuple-element.174), channel_id=1, source_target_pairs={{0,3},{1,0},{2,1},{3,2},{4,7},{5,4},{6,5},{7,6},{8,11},{9,8},{10,9... | collective-permute-start | bytes 1474568 | tf_op jit(solution)/shard_map/ppermute | solution.py:74
  360.2 60.6 %collective-permute-start.51 = (bf16[160,1536]{1,0:T(8,128)(2,1)}, bf16[160,1536]{1,0:T(8,128)(2,1)}, u32[]{:S(2)}, u32[]{:S(2)}) collective-permute-start(bf16[160,1536]{1,0:T(8,128)(2,1)} %get-tuple-element.175), channel_id=1, source_target_pairs={{0,2},{1,3},{2,0},{3,1},{4,6},{5,7},{6,4},{7,5},{8,10},{9,11},{10,... | collective-permute-start | bytes 1474568 | tf_op jit(solution)/shard_map/ppermute | solution.py:74
  363.2 57.6 %collective-permute-start.52 = (bf16[160,1536]{1,0:T(8,128)(2,1)}, bf16[160,1536]{1,0:T(8,128)(2,1)}, u32[]{:S(2)}, u32[]{:S(2)}) collective-permute-start(bf16[160,1536]{1,0:T(8,128)(2,1)} %get-tuple-element.176), channel_id=1, source_target_pairs={{0,1},{1,2},{2,3},{3,0},{4,5},{5,6},{6,7},{7,4},{8,9},{9,10},{10,1... | collective-permute-start | bytes 1474568 | tf_op jit(solution)/shard_map/ppermute | solution.py:74
  382.7 32.1 %collective-permute-start.47 = (bf16[4,2,48,2240]{3,2,0,1:T(8,128)(2,1)}, bf16[4,2,48,2240]{3,2,0,1:T(8,128)(2,1)}, u32[]{:S(2)}, u32[]{:S(2)}) collective-permute-start(bf16[4,2,48,2240]{3,2,0,1:T(8,128)(2,1)} %copy_bitcast_fusion.1), channel_id=1, source_target_pairs={{0,8},{4,20},{8,0},{12,28},{16,24},{20,4},{24,16},{28,12},{1,9},{5... | collective-permute-start | bytes 5160968 | tf_op jit(solution)/shard_map/ppermute | solution.py:74
  387.1 29.6 %collective-permute-start.46 = (bf16[280,1536]{1,0:T(8,128)(2,1)}, bf16[280,1536]{1,0:T(8,128)(2,1)}, u32[]{:S(2)}, u32[]{:S(2)}) collective-permute-start(bf16[280,1536]{1,0:T(8,128)(2,1)} %dynamic-slice_bitcast_fusion.3), channel_id=1, source_target_pairs={{0,16},{4,12},{8,24},{12,4},{16,0},{20,28},{24,8},{28,20},{1,17},{... | collective-permute-start | bytes 2580488 | tf_op jit(solution)/shard_map/ppermute | solution.py:74
  416.8 41.1 %collective-permute-start.49 = (bf16[4,2,48,2240]{3,2,0,1:T(8,128)(2,1)S(1)}, bf16[4,2,48,2240]{3,2,0,1:T(8,128)(2,1)S(1)}, u32[]{:S(2)}, u32[]{:S(2)}) collective-permute-start(bf16[4,2,48,2240]{3,2,0,1:T(8,128)(2,1)S(1)} %copy_bitcast_fusion), channel_id=1, source_target_pairs={{0,8},{4,20},{8,0},{12,28},{16,24},{20,4},{24,16},{28,12},{1,9},{5... | collective-permute-start | bytes 5160968 | tf_op jit(solution)/shard_map/ppermute | solution.py:74
  420.8 67.1 %collective-permute-start.57 = (bf16[280,1536]{1,0:T(8,128)(2,1)}, bf16[280,1536]{1,0:T(8,128)(2,1)}, u32[]{:S(2)}, u32[]{:S(2)}) collective-permute-start(bf16[280,1536]{1,0:T(8,128)(2,1)} %fusion.12.refs_0_), channel_id=1, source_target_pairs={{0,16},{4,12},{8,24},{12,4},{16,0},{20,28},{24,8},{28,20},{1,17},{... | collective-permute-start | bytes 2580488 | tf_op jit(solution)/shard_map/ppermute | solution.py:74
  421.7 66.2 %collective-permute-start.58 = (bf16[280,1536]{1,0:T(8,128)(2,1)}, bf16[280,1536]{1,0:T(8,128)(2,1)}, u32[]{:S(2)}, u32[]{:S(2)}) collective-permute-start(bf16[280,1536]{1,0:T(8,128)(2,1)} %fusion.12.refs_0_), channel_id=1, source_target_pairs={{0,8},{4,20},{8,0},{12,28},{16,24},{20,4},{24,16},{28,12},{1,9},{5... | collective-permute-start | bytes 2580488 | tf_op jit(solution)/shard_map/ppermute | solution.py:74
  422.3 39.9 %collective-permute-start.48 = (bf16[4,48,2240]{2,1,0:T(8,128)(2,1)S(1)}, bf16[4,48,2240]{2,1,0:T(8,128)(2,1)}, u32[]{:S(2)}, u32[]{:S(2)}) collective-permute-start(bf16[4,48,2240]{2,1,0:T(8,128)(2,1)S(1)} %dynamic-slice_bitcast_fusion.2), channel_id=1, source_target_pairs={{0,16},{4,12},{8,24},{12,4},{16,0},{20,28},{24,8},{28,20},{1,17},{... | collective-permute-start | bytes 2580488 | tf_op jit(solution)/shard_map/ppermute | solution.py:74
  487.9 36.3 %collective-permute-start.65 = (bf16[768,1536]{1,0:T(8,128)(2,1)}, bf16[768,1536]{1,0:T(8,128)(2,1)}, u32[]{:S(2)}, u32[]{:S(2)}) collective-permute-start(bf16[768,1536]{1,0:T(8,128)(2,1)} %get-tuple-element.192), channel_id=1, source_target_pairs={{0,4},{4,0},{8,12},{12,8},{16,20},{20,16},{24,28},{28,24},{1,5},{5... | collective-permute-start | bytes 7077896 | tf_op jit(solution)/shard_map/ppermute | solution.py:74
  489.1 30.7 %collective-permute-start.53 = (bf16[4,48,2240]{2,1,0:T(8,128)(2,1)}, bf16[4,48,2240]{2,1,0:T(8,128)(2,1)}, u32[]{:S(2)}, u32[]{:S(2)}) collective-permute-start(bf16[4,48,2240]{2,1,0:T(8,128)(2,1)} %dynamic-slice_bitcast_fusion.1), channel_id=1, source_target_pairs={{0,16},{4,12},{8,24},{12,4},{16,0},{20,28},{24,8},{28,20},{1,17},{... | collective-permute-start | bytes 2580488 | tf_op jit(solution)/shard_map/ppermute | solution.py:74
  537.4 41.3 %collective-permute-start.69 = (bf16[768,2048]{1,0:T(8,128)(2,1)}, bf16[768,2048]{1,0:T(8,128)(2,1)}, u32[]{:S(2)}, u32[]{:S(2)}) collective-permute-start(bf16[768,2048]{1,0:T(8,128)(2,1)} %get-tuple-element.207), channel_id=1, source_target_pairs={{0,4},{4,0},{8,12},{12,8},{16,20},{20,16},{24,28},{28,24},{1,5},{5... | collective-permute-start | bytes 9437192 | tf_op jit(solution)/shard_map/ppermute | solution.py:74
  584.9 38.6 %collective-permute-start.70 = (bf16[4,2,48,2048]{3,2,0,1:T(8,128)(2,1)}, bf16[4,2,48,2048]{3,2,0,1:T(8,128)(2,1)}, u32[]{:S(2)}, u32[]{:S(2)}) collective-permute-start(bf16[4,2,48,2048]{3,2,0,1:T(8,128)(2,1)} %copy_bitcast_fusion.2), channel_id=1, source_target_pairs={{0,8},{4,20},{8,0},{12,28},{16,24},{20,4},{24,16},{28,12},{1,9},{5... | collective-permute-start | bytes 4718600 | tf_op jit(solution)/shard_map/ppermute | solution.py:74
  586.7 39.5 %collective-permute-start.66 = (bf16[48,8960]{1,0:T(8,128)(2,1)}, bf16[48,8960]{1,0:T(8,128)(2,1)}, u32[]{:S(2)}, u32[]{:S(2)}) collective-permute-start(bf16[48,8960]{1,0:T(8,128)(2,1)} %collective-permute-done.59.refs_1_), channel_id=1, source_target_pairs={{0,8},{4,20},{8,0},{12,28},{16,24},{20,4},{24,16},{28,12},{1,9},{5... | collective-permute-start | bytes 2580488 | tf_op jit(solution)/shard_map/ppermute | solution.py:74
  621.2 30.6 %collective-permute-start.84 = (bf16[160,1536]{1,0:T(8,128)(2,1)}, bf16[160,1536]{1,0:T(8,128)(2,1)S(1)}, u32[]{:S(2)}, u32[]{:S(2)}) collective-permute-start(bf16[160,1536]{1,0:T(8,128)(2,1)} %get-tuple-element.227), channel_id=1, source_target_pairs={{0,2},{1,3},{2,0},{3,1},{4,6},{5,7},{6,4},{7,5},{8,10},{9,11},{10,... | collective-permute-start | bytes 1474568 | tf_op jit(solution)/shard_map/ppermute | solution.py:74
  623.5 29.4 %collective-permute-start.83 = (bf16[160,1536]{1,0:T(8,128)(2,1)}, bf16[160,1536]{1,0:T(8,128)(2,1)S(1)}, u32[]{:S(2)}, u32[]{:S(2)}) collective-permute-start(bf16[160,1536]{1,0:T(8,128)(2,1)} %get-tuple-element.226), channel_id=1, source_target_pairs={{0,3},{1,0},{2,1},{3,2},{4,7},{5,4},{6,5},{7,6},{8,11},{9,8},{10,9... | collective-permute-start | bytes 1474568 | tf_op jit(solution)/shard_map/ppermute | solution.py:74
  626.1 37.6 %collective-permute-start.79 = (bf16[48,8960]{1,0:T(8,128)(2,1)}, bf16[48,8960]{1,0:T(8,128)(2,1)S(1)}, u32[]{:S(2)}, u32[]{:S(2)}) collective-permute-start(bf16[48,8960]{1,0:T(8,128)(2,1)} %concatenate.82.refs_0_), channel_id=1, source_target_pairs={{0,4},{4,0},{8,12},{12,8},{16,20},{20,16},{24,28},{28,24},{1,5},{5... | collective-permute-start | bytes 2580488 | tf_op jit(solution)/shard_map/ppermute | solution.py:74
  626.2 38.0 %collective-permute-start.95 = (bf16[48,8960]{1,0:T(8,128)(2,1)S(1)}, bf16[48,8960]{1,0:T(8,128)(2,1)S(1)}, u32[]{:S(2)}, u32[]{:S(2)}) collective-permute-start(bf16[48,8960]{1,0:T(8,128)(2,1)S(1)} %copy-done.29), channel_id=1, source_target_pairs={{0,16},{4,12},{8,24},{12,4},{16,0},{20,28},{24,8},{28,20},{1,17},{... | collective-permute-start | bytes 2580488 | tf_op jit(solution)/shard_map/ppermute | solution.py:74
  631.7 42.7 %collective-permute-start.96 = (bf16[48,8960]{1,0:T(8,128)(2,1)S(1)}, bf16[48,8960]{1,0:T(8,128)(2,1)S(1)}, u32[]{:S(2)}, u32[]{:S(2)}) collective-permute-start(bf16[48,8960]{1,0:T(8,128)(2,1)S(1)} %copy-done.29), channel_id=1, source_target_pairs={{0,8},{4,20},{8,0},{12,28},{16,24},{20,4},{24,16},{28,12},{1,9},{5... | collective-permute-start | bytes 2580488 | tf_op jit(solution)/shard_map/ppermute | solution.py:74
  652.9 37.6 %collective-permute-start.80 = (bf16[48,8960]{1,0:T(8,128)(2,1)}, bf16[48,8960]{1,0:T(8,128)(2,1)S(1)}, u32[]{:S(2)}, u32[]{:S(2)}) collective-permute-start(bf16[48,8960]{1,0:T(8,128)(2,1)} %collective-permute-done.59.refs_1_), channel_id=1, source_target_pairs={{0,4},{4,0},{8,12},{12,8},{16,20},{20,16},{24,28},{28,24},{1,5},{5... | collective-permute-start | bytes 2580488 | tf_op jit(solution)/shard_map/ppermute | solution.py:74
  (175 other events, 2513.7 us)

commit v3 on v2

v3 whole, which is shorter than its diff:
```python
import math

import jax
import jax.numpy as jnp
from jax import lax
from jax.experimental import pallas as pl
from jax.experimental.pallas import tpu as pltpu
from jax.sharding import PartitionSpec as P

QH = 12
KVH = 2
HD = 128
SEQS = 3


EPSILON = 1e-06
LOG_THETA = math.log(1000000.0)
MASKED = -1e30
VMEM_LIMIT = 56 * 1024 * 1024
TILE = 512
COST = pl.CostEstimate(flops=1, bytes_accessed=1, transcendentals=0)


def rope_tables(places, head_width):
    half_width = head_width // 2
    frequency = jnp.exp(jnp.arange(half_width, dtype=jnp.float32) * (-2.0 * LOG_THETA / head_width))
    angles = places.astype(jnp.float32)[:, None] * frequency[None, :]
    angles = jnp.concatenate([angles, angles], axis=-1)
    return (jnp.cos(angles), jnp.sin(angles))


def positions(segments):
    labels = jnp.arange(SEQS, dtype=jnp.int32)
    starts = jnp.sum((segments[None, :] < labels[:, None]).astype(jnp.int32), axis=1)
    own_start = jnp.sum(jnp.where(segments[:, None] == labels[None, :], starts[None, :], 0), axis=1)
    return jnp.arange(segments.shape[0], dtype=jnp.int32) - own_start


def rotate(field_rows, cosine_table, sine_table):
    half_width = field_rows.shape[-1] // 2
    turned = jnp.concatenate([-field_rows[..., half_width:], field_rows[..., :half_width]], axis=-1)
    return field_rows * cosine_table[:, None, :] + turned * sine_table[:, None, :]


def transposed_times(left_side, right_side):
    return lax.dot_general(
        left_side, right_side, (((0,), (0,)), ((), ())), preferred_element_type=jnp.float32
    )


def times_transposed(left_side, right_side):
    return lax.dot_general(
        left_side, right_side, (((1,), (1,)), ((), ())), preferred_element_type=jnp.float32
    )


def norm_back(normed_gradient, unit_rows, inverse_rms, gain_row):
    scaled = normed_gradient * gain_row
    return inverse_rms * (scaled - unit_rows * jnp.mean(scaled * unit_rows, axis=-1, keepdims=True))


class Line:
    def __init__(self, name, size, place, pairs, crossed=False):
        self.name, self.size, self.place, self.pairs = name, size, place, pairs
        self.crossed = crossed

    def shift(self, value, step):
        return lax.ppermute(value, self.name, self.pairs(step % self.size))

    def behind(self, step):
        return lax.rem(self.place + (self.size - step % self.size), self.size)

    def ahead(self, step):
        return lax.rem(self.place + step % self.size, self.size)


def make_lines(reps, shards):
    inner = 2 if reps % 4 == 0 else 1
    outer = reps // (2 * inner)
    square = inner == outer

    def split(index):
        core, b, a = index % 2, (index // 2) % inner, index // (2 * inner)
        return core, b, a

    def join(core, b, a):
        return (a * inner + b) * 2 + core

    def first_pairs(step):
        pairs = []
        for index in range(reps):
            core, b, a = split(index)
            if square and core == 0:
                pairs.append((index, join(core, (b + step) % inner, a)))
            else:
                pairs.append((index, join(core, b, (a + step) % outer)))
        return pairs

    def second_pairs(step):
        pairs = []
        for index in range(reps):
            core, b, a = split(index)
            if square and core == 0:
                pairs.append((index, join(core, b, (a + step) % outer)))
            else:
                pairs.append((index, join(core, (b + step) % inner, a)))
        return pairs

    def core_pairs(step):
        pairs = []
        for index in range(reps):
            core, b, a = split(index)
            pairs.append((index, join((core + step) % 2, b, a)))
        return pairs

    def shard_pairs(step):
        return [(index, (index + step) % shards) for index in range(shards)]

    core, b, a = split(lax.axis_index("rep"))
    first, second = (jnp.where(core == 0, b, a), jnp.where(core == 0, a, b)) if square else (a, b)
    return (
        Line("shard", shards, lax.axis_index("shard"), shard_pairs),
        Line("rep", 2, core, core_pairs, square),
        Line("rep", outer, first, first_pairs),
        Line("rep", inner, second, second_pairs),
    )


def pick(array, index, axis):
    return lax.dynamic_index_in_dim(array, index, axis, keepdims=False)


def put(array, piece, index, axis):
    return lax.dynamic_update_index_in_dim(array, piece, index, axis)


def in_place_order(pieces, line):
    ordered = []
    for place in range(line.size):
        chosen = pieces[0]
        for step in range(1, line.size):
            chosen = jnp.where(line.behind(step) == place, pieces[step], chosen)
        ordered.append(chosen)
    return ordered


def tie(*arrays):
    return lax.optimization_barrier(arrays)


def gather_line(value, line):
    return [value] + [line.shift(value, step) for step in range(1, line.size)]


class Clock:
    def __init__(self):
        self.token = jnp.zeros((8, 128), jnp.float32)

    def __call__(self, *arrays):
        self.token, *arrays = tie(self.token, *arrays)
        return arrays


def total_of(terms):
    total = terms[0].astype(jnp.float32)
    for term in terms[1:]:
        total = total + term.astype(jnp.float32)
    return total


class Halving:
    def __init__(self, clock, terms, axis):
        self.clock, self.terms, self.axis = clock, terms, axis

    def send(self, line):
        self.moving = [
            line.shift(
                total_of([pick(term, line.ahead(step), self.axis) for term in self.terms]).astype(
                    jnp.bfloat16
                ),
                step,
            )
            for step in range(1, line.size)
        ]
        self.terms = [pick(term, line.place, self.axis) for term in self.terms]

    def receive(self):
        self.terms = self.terms + self.clock(*self.moving)


class Spread:
    def __init__(self, clock, piece, core, first, second):
        self.clock, self.lines = clock, (core, first, second)
        self.own = piece
        self.across = {(0, two): second.shift(piece, two) for two in range(1, second.size)}
        self.along = {(one, 0): first.shift(piece, one) for one in range(1, first.size)}
        self.here = {(0, 0): piece}
        self.there = {(0, 0): core.shift(piece, 1)}

    def arrive(self, group):
        for key, value in zip(group, self.clock(*group.values())):
            self.here[key] = value
            self.there[key] = self.lines[0].shift(value, 1)

    def further(self):
        self.arrive(self.across)
        self.beyond = {
            (one, two): self.lines[1].shift(self.here[0, two], one)
            for one in range(1, self.lines[1].size)
            for two in range(1, self.lines[2].size)
        }

    def over(self):
        self.arrive(self.along)
        self.arrive(self.beyond)

    def finish(self):
        core, first, second = self.lines
        placed = [
            (core.place, first.behind(one), second.behind(two), value)
            for (one, two), value in self.here.items()
        ]
        far, near = (second, first) if core.crossed else (first, second)
        others = self.clock(*self.there.values())
        for (one, two), value in zip(self.there, others):
            placed.append((core.behind(1), far.behind(one), near.behind(two), value))
        places = [(c * first.size + f) * second.size + s for c, f, s, value in placed]
        return jnp.stack(places).astype(jnp.int32), [value for c, f, s, value in placed]


def place_blocks(order, places, pieces):
    reps = len(pieces)
    groups, shards = pieces[0].shape[:2]
    block = pieces[0].shape[2:]
    whole = (shards, reps) + block

    def body(order_ref, places_ref, *refs):
        sources, outs, (held, in_sems, out_sems) = (
            refs[:reps],
            refs[reps : reps + groups],
            refs[reps + groups :],
        )
        slabs = [(g, k) for g in range(groups) for k in range(shards)]

        def load(g, k, r):
            return pltpu.make_async_copy(
                sources[r].at[g, k], held.at[g, k, places_ref[r]], in_sems.at[g, k, r]
            )

        def store(g, k):
            return pltpu.make_async_copy(
                held.at[g, k], outs[g].at[order_ref[k]], out_sems.at[g, k]
            )

        for g, k in slabs:
            for r in range(reps):
                load(g, k, r).start()
        for g, k in slabs:
            for r in range(reps):
                load(g, k, r).wait()
            store(g, k).start()
        for g, k in slabs:
            store(g, k).wait()

    return pl.pallas_call(
        body,
        out_shape=[jax.ShapeDtypeStruct(whole, pieces[0].dtype)] * groups,
        in_specs=[pl.BlockSpec(memory_space=pltpu.SMEM)] * 2
        + [pl.BlockSpec(memory_space=pl.ANY)] * reps,
        out_specs=[pl.BlockSpec(memory_space=pl.ANY)] * groups,
        scratch_shapes=[
            pltpu.VMEM((groups,) + whole, pieces[0].dtype),
            pltpu.SemaphoreType.DMA((groups, shards, reps)),
            pltpu.SemaphoreType.DMA((groups, shards)),
        ],
        compiler_params=pltpu.CompilerParams(vmem_limit_bytes=VMEM_LIMIT),
        cost_estimate=COST,
        name="place_blocks",
    )(order, places, *pieces)


def widen_pieces(places, pieces):
    reps = len(pieces)
    rows, columns = pieces[0].shape
    strip = next(size for size in (16, 8, rows) if rows % size == 0)

    def body(places_ref, *refs):
        sources, (out_ref, narrow, wide, in_sems, out_sems) = refs[:reps], refs[reps:]
        loads = [
            pltpu.make_async_copy(sources[r], narrow.at[r], in_sems.at[r]) for r in range(reps)
        ]
        stores = [
            pltpu.make_async_copy(wide.at[r], out_ref.at[places_ref[r]], out_sems.at[r])
            for r in range(reps)
        ]
        for load in loads:
            load.start()
        for r in range(reps):
            loads[r].wait()

            def convert(at, carry):
                cut = pl.ds(pl.multiple_of(at * strip, strip), strip)
                wide[r, cut, :] = narrow[r, cut, :].astype(jnp.float32)
                return carry

            lax.fori_loop(0, rows // strip, convert, 0)
            stores[r].start()
        for store in stores:
            store.wait()

    return pl.pallas_call(
        body,
        out_shape=jax.ShapeDtypeStruct((reps, rows, columns), jnp.float32),
        in_specs=[pl.BlockSpec(memory_space=pltpu.SMEM)]
        + [pl.BlockSpec(memory_space=pl.ANY)] * reps,
        out_specs=pl.BlockSpec(memory_space=pl.ANY),
        scratch_shapes=[
            pltpu.VMEM((reps, rows, columns), jnp.bfloat16),
            pltpu.VMEM((reps, rows, columns), jnp.float32),
            pltpu.SemaphoreType.DMA((reps,)),
            pltpu.SemaphoreType.DMA((reps,)),
        ],
        compiler_params=pltpu.CompilerParams(vmem_limit_bytes=VMEM_LIMIT),
        cost_estimate=COST,
        name="widen_pieces",
    )(places, *pieces).reshape(reps * rows, columns)


def resident(shape):
    return pl.BlockSpec(shape, lambda i: (0, 0), pipeline_mode=pl.Buffered(1))


def feed_forward(rows, cotangents, gate_matrix, up_matrix, down_matrix):
    count, width = rows.shape
    units = gate_matrix.shape[1]

    def body(rows_ref, cotangents_ref, gate_ref, up_ref, down_ref, inner_ref, d_gate_ref, d_up_ref):
        gate = jnp.dot(rows_ref[...], gate_ref[...], preferred_element_type=jnp.float32)
        up = jnp.dot(rows_ref[...], up_ref[...], preferred_element_type=jnp.float32)
        sigmoid = jax.nn.sigmoid(gate)
        silu = gate * sigmoid
        inner_ref[...] = (silu * up).astype(jnp.bfloat16)
        d_inner = times_transposed(cotangents_ref[...], down_ref[...])
        d_up_ref[...] = (d_inner * silu).astype(jnp.bfloat16)
        d_gate_ref[...] = (d_inner * up * sigmoid * (1.0 + gate * (1.0 - sigmoid))).astype(
            jnp.bfloat16
        )

    columns = pl.BlockSpec((width, TILE), lambda i: (0, i))
    results = pl.BlockSpec((count, TILE), lambda i: (0, i))
    return pl.pallas_call(
        body,
        grid=(pl.cdiv(units, TILE),),
        out_shape=[jax.ShapeDtypeStruct((count, units), jnp.bfloat16)] * 3,
        in_specs=[
            resident((count, width)),
            resident((count, width)),
            columns,
            columns,
            pl.BlockSpec((TILE, width), lambda i: (i, 0)),
        ],
        out_specs=[results] * 3,
        compiler_params=pltpu.CompilerParams(vmem_limit_bytes=VMEM_LIMIT),
        cost_estimate=COST,
        name="feed_forward",
    )(rows, cotangents, gate_matrix, up_matrix, down_matrix)


def split_gradient(left, right, groups, core_place):
    count, rows = left.shape
    columns = right.shape[1]
    half = rows // (2 * groups)

    def body(core_ref, left_ref, right_ref, other_ref, own_ref, turned):
        @pl.when(pl.program_id(0) == 0)
        def turn():
            whole = left_ref[...].T
            for group in range(groups):
                for which in range(2):
                    at = (2 * group + which) * half
                    turned[which, group * half : (group + 1) * half, :] = whole[at : at + half]

        core = core_ref[0]
        for out_ref, which in ((other_ref, 1 - core), (own_ref, core)):
            product = jnp.dot(turned[which], right_ref[...], preferred_element_type=jnp.float32)
            for group in range(groups):
                out_ref[group] = product[group * half : (group + 1) * half].astype(jnp.bfloat16)

    return pl.pallas_call(
        body,
        grid=(pl.cdiv(columns, TILE),),
        out_shape=[jax.ShapeDtypeStruct((groups, half, columns), jnp.bfloat16)] * 2,
        in_specs=[
            pl.BlockSpec(memory_space=pltpu.SMEM),
            resident((count, rows)),
            pl.BlockSpec((count, TILE), lambda i: (0, i)),
        ],
        out_specs=[pl.BlockSpec((groups, half, TILE), lambda i: (0, 0, i))] * 2,
        scratch_shapes=[pltpu.VMEM((2, rows // 2, count), jnp.bfloat16)],
        compiler_params=pltpu.CompilerParams(vmem_limit_bytes=VMEM_LIMIT),
        cost_estimate=COST,
        name="split_gradient",
    )(core_place.reshape(1).astype(jnp.int32), left, right)


def rows_product(lefts, rights, turned, blocks):
    count, depth = lefts[0].shape
    columns = rights[0].shape[0 if turned else 1]
    pairs, part = len(lefts), count // blocks

    def body(*refs):
        total = None
        for left_ref, right_ref in zip(refs[:pairs], refs[pairs : 2 * pairs]):
            if turned:
                product = times_transposed(left_ref[...], right_ref[...])
            else:
                product = jnp.dot(
                    left_ref[...], right_ref[...], preferred_element_type=jnp.float32
                )
            total = product if total is None else total + product
        for block in range(blocks):
            refs[2 * pairs + block][...] = total[block * part : (block + 1) * part].astype(
                jnp.bfloat16
            )

    right_spec = (
        pl.BlockSpec((TILE, depth), lambda i: (i, 0))
        if turned
        else pl.BlockSpec((depth, TILE), lambda i: (0, i))
    )
    return pl.pallas_call(
        body,
        grid=(pl.cdiv(columns, TILE),),
        out_shape=[jax.ShapeDtypeStruct((part, columns), jnp.bfloat16)] * blocks,
        in_specs=[resident((count, depth))] * pairs + [right_spec] * pairs,
        out_specs=[pl.BlockSpec((part, TILE), lambda i: (0, i))] * blocks,
        compiler_params=pltpu.CompilerParams(vmem_limit_bytes=VMEM_LIMIT),
        cost_estimate=COST,
        name="rows_product",
    )(*lefts, *rights)


def kept_bias(row_segments, row_index, key_segments, key_index):
    kept = (row_segments == key_segments) & (key_index <= row_index)
    return jnp.where(kept, 0.0, MASKED)


def in_vmem(count):
    return [pl.BlockSpec(memory_space=pltpu.VMEM)] * count


def attention_forward(projected, cosine, signed_sine, pairs, rows, keys):
    count = projected.shape[0]
    per_group = QH // KVH
    scale = 1.0 / math.sqrt(HD)
    shape = (KVH, per_group * count, HD)

    def body(projected_ref, cosine_ref, sine_ref, pairs_ref, rows_ref, keys_ref, queries_ref, out_ref):
        bias = kept_bias(rows_ref[:, 0:1], rows_ref[:, 1:2], keys_ref[0:1, :], keys_ref[1:2, :])
        for k in range(KVH):
            for h in range(per_group):
                at = (k * per_group + h) * HD
                field = projected_ref[:, at : at + HD]
                queries_ref[k, h * count : (h + 1) * count, :] = (
                    field * cosine_ref[...] + pltpu.roll(field, HD // 2, 1) * sine_ref[...]
                ).astype(jnp.bfloat16)
            keys_here = pairs_ref[:, k * HD : (k + 1) * HD]
            values_here = pairs_ref[:, (KVH + k) * HD : (KVH + k + 1) * HD]
            scores = times_transposed(queries_ref[k], keys_here) * scale + bias
            powers = jnp.exp(scores - jnp.max(scores, axis=1, keepdims=True))
            shares = powers * (1.0 / jnp.sum(powers, axis=1, keepdims=True))
            result = jnp.dot(
                shares.astype(jnp.bfloat16), values_here, preferred_element_type=jnp.float32
            ).astype(jnp.bfloat16)
            for h in range(per_group):
                at = (k * per_group + h) * HD
                out_ref[:, at : at + HD] = result[h * count : (h + 1) * count]

    return pl.pallas_call(
        body,
        out_shape=[
            jax.ShapeDtypeStruct(shape, jnp.bfloat16),
            jax.ShapeDtypeStruct((count, QH * HD), jnp.bfloat16),
        ],
        in_specs=in_vmem(6),
        out_specs=in_vmem(2),
        compiler_params=pltpu.CompilerParams(vmem_limit_bytes=VMEM_LIMIT),
        cost_estimate=COST,
        name="attention_forward",
    )(projected, cosine, signed_sine, pairs, rows, keys)


def attention_backward(queries, gradient, pairs, cosine, signed_sine, rows, keys, blocks):
    count = gradient.shape[0]
    per_group = QH // KVH
    scale = 1.0 / math.sqrt(HD)
    group_rows = pairs.shape[0]
    part = group_rows // blocks

    def body(queries_ref, gradient_ref, pairs_ref, cosine_ref, sine_ref, rows_ref, keys_ref, d_ref, *outs):
        block_refs, stacked = outs[:blocks], outs[blocks]
        bias = kept_bias(rows_ref[0:1, :], rows_ref[1:2, :], keys_ref[:, 0:1], keys_ref[:, 1:2])
        for k in range(KVH):
            for h in range(per_group):
                at = (k * per_group + h) * HD
                stacked[h * count : (h + 1) * count, :] = gradient_ref[:, at : at + HD]
            keys_here = pairs_ref[:, k * HD : (k + 1) * HD]
            values_here = pairs_ref[:, (KVH + k) * HD : (KVH + k + 1) * HD]
            scores = times_transposed(keys_here, queries_ref[k]) * scale + bias
            powers = jnp.exp(scores - jnp.max(scores, axis=0, keepdims=True))
            shares = powers * (1.0 / jnp.sum(powers, axis=0, keepdims=True))
            d_shares = times_transposed(values_here, stacked[...])
            dots = jnp.sum(shares * d_shares, axis=0, keepdims=True)
            d_scores = (shares * (d_shares - dots)).astype(jnp.bfloat16)
            d_keys = jnp.dot(d_scores, queries_ref[k], preferred_element_type=jnp.float32) * scale
            d_values = jnp.dot(
                shares.astype(jnp.bfloat16), stacked[...], preferred_element_type=jnp.float32
            )
            for block in range(blocks):
                cut = slice(block * part, (block + 1) * part)
                block_refs[block][:, k * HD : (k + 1) * HD] = d_keys[cut].astype(jnp.bfloat16)
                block_refs[block][:, (KVH + k) * HD : (KVH + k + 1) * HD] = d_values[cut].astype(
                    jnp.bfloat16
                )
            d_queries = transposed_times(d_scores, keys_here) * scale
            for h in range(per_group):
                at = (k * per_group + h) * HD
                field = d_queries[h * count : (h + 1) * count]
                d_ref[:, at : at + HD] = (
                    field * cosine_ref[...] - pltpu.roll(field, HD // 2, 1) * sine_ref[...]
                ).astype(jnp.bfloat16)

    return pl.pallas_call(
        body,
        out_shape=[jax.ShapeDtypeStruct((count, QH * HD), jnp.bfloat16)]
        + [jax.ShapeDtypeStruct((part, 2 * KVH * HD), jnp.bfloat16)] * blocks,
        in_specs=in_vmem(7),
        out_specs=in_vmem(1 + blocks),
        scratch_shapes=[pltpu.VMEM((per_group * count, HD), jnp.bfloat16)],
        compiler_params=pltpu.CompilerParams(vmem_limit_bytes=VMEM_LIMIT),
        cost_estimate=COST,
        name="attention_backward",
    )(queries, gradient, pairs, cosine, signed_sine, rows, keys)


def join_projected(d_queries, pair_terms, cosine, signed_sine):
    count, query_width = d_queries.shape
    pair_width = KVH * HD
    terms = len(pair_terms)

    def body(d_queries_ref, cosine_ref, sine_ref, *refs):
        term_refs, out_ref, sum_ref = refs[:terms], refs[terms], refs[terms + 1]
        out_ref[:, :query_width] = d_queries_ref[...]
        for at in range(0, 2 * pair_width, HD):
            field = total_of([term[:, at : at + HD] for term in term_refs])
            if at < pair_width:
                field = field * cosine_ref[...] - pltpu.roll(field, HD // 2, 1) * sine_ref[...]
            out_ref[:, query_width + at : query_width + at + HD] = field.astype(jnp.bfloat16)
        sum_ref[...] = jnp.sum(out_ref[...].astype(jnp.float32), axis=0, keepdims=True)

    return pl.pallas_call(
        body,
        out_shape=[
            jax.ShapeDtypeStruct((count, query_width + 2 * pair_width), jnp.bfloat16),
            jax.ShapeDtypeStruct((1, query_width + 2 * pair_width), jnp.float32),
        ],
        in_specs=in_vmem(3 + terms),
        out_specs=in_vmem(2),
        cost_estimate=COST,
        name="join_projected",
    )(d_queries, cosine, signed_sine, *pair_terms)


def on_device(
    tokens,
    segment_ids,
    first_gain,
    input_weight,
    input_bias,
    output_weight,
    second_gain,
    gate_weight,
    up_weight,
    down_weight,
    output_cotangent,
):
    bf16, f32 = jnp.bfloat16, jnp.float32
    shards, reps = lax.axis_size("shard"), lax.axis_size("rep")
    shard, core, first, second = make_lines(reps, shards)
    plane = (first.size, second.size)
    rep_place = (core.place * first.size + first.place) * second.size + second.place
    own_rows, width = tokens.shape
    segments = segment_ids[0]
    per_group = QH // KVH
    query_width = QH * HD
    pair_width = KVH * HD
    first_row = shard.place * own_rows
    part_rows = input_weight.shape[0] // reps
    hidden_units = gate_weight.shape[1]
    block_units = hidden_units // shards
    by_rows = (shards,) + plane + (part_rows,)
    clock = Clock()
    z_order = jnp.stack([shard.behind(step) for step in range(shards)]).astype(jnp.int32)

    def weight_piece(weight):
        return pick(weight.reshape(reps, part_rows, weight.shape[1]), rep_place, 0)

    def column_piece(weight):
        return weight_piece(weight).reshape(part_rows, shards, block_units).transpose(1, 0, 2)

    def spread(piece):
        return Spread(clock, piece, core, first, second)

    def send_rows(rows):
        return [shard.shift(row, shards - step) for step, row in enumerate(rows, 1)]

    def place_sends(blocks):
        return [pick(blocks, shard.place, 0)] + [
            shard.shift(pick(blocks, shard.ahead(step), 0), step) for step in range(1, shards)
        ]

    shard_vectors = jnp.concatenate([first_gain, second_gain, input_bias])
    vector_moving = gather_line(shard_vectors, shard)
    input_moving = gather_line(weight_piece(input_weight), shard)
    input_rows = clock(*input_moving)
    input_spread = spread(jnp.stack(input_rows)[None])
    output_piece, gate_weight, up_weight = clock(
        weight_piece(output_weight), gate_weight, up_weight
    )
    output_moving = gather_line(output_piece, shard)
    (columns,) = clock(jnp.stack([column_piece(gate_weight), column_piece(up_weight)], axis=1))
    column_moving = place_sends(columns)
    vector_rows = jnp.stack(in_place_order(clock(*vector_moving), shard))
    own_gain = first_gain.shape[0]
    gain_one = vector_rows[:, :own_gain].reshape(width).astype(f32)
    gain_two = vector_rows[:, own_gain : 2 * own_gain].reshape(width).astype(f32)
    shift_row = vector_rows[:, 2 * own_gain :].reshape(-1).astype(f32)

    places = positions(segments)
    cosine_table, sine_table = rope_tables(
        lax.dynamic_slice_in_dim(places, first_row, own_rows), HD
    )
    signed_sine = jnp.concatenate(
        [-sine_table[:, : HD // 2], sine_table[:, HD // 2 :]], axis=1
    )
    own_segments = lax.dynamic_slice_in_dim(segments, first_row, own_rows)
    row_index = jnp.arange(own_rows, dtype=jnp.int32)
    key_index = jnp.concatenate([shard.behind(step) * own_rows + row_index for step in range(shards)])
    key_segments = jnp.concatenate(
        [
            lax.dynamic_slice_in_dim(segments, shard.behind(step) * own_rows, own_rows)
            for step in range(shards)
        ]
    )
    key_marks = jnp.stack([key_segments, key_index])
    row_marks = jnp.tile(jnp.stack([own_segments, first_row + row_index]), (1, per_group))

    wide_tokens = tokens.astype(f32)
    inverse_one = lax.rsqrt(jnp.mean(wide_tokens * wide_tokens, axis=-1, keepdims=True) + EPSILON)
    unit_one = wide_tokens * inverse_one
    (normed_one,) = clock((unit_one * gain_one).astype(bf16))

    input_spread.further()
    input_spread.over()
    output_spread = spread(jnp.stack(clock(*output_moving))[None])
    (input_matrix,) = place_blocks(z_order, *input_spread.finish())
    (input_matrix,) = clock(input_matrix.reshape(width, -1))
    projected = jnp.dot(normed_one, input_matrix, preferred_element_type=f32) + shift_row
    key_part = rotate(
        projected[:, query_width : query_width + pair_width].reshape(own_rows, KVH, HD),
        cosine_table,
        sine_table,
    )
    (own_pairs,) = clock(
        jnp.concatenate(
            [key_part.reshape(own_rows, pair_width), projected[:, query_width + pair_width :]],
            axis=1,
        ).astype(bf16)
    )
    pair_moving = gather_line(own_pairs, shard)
    output_spread.further()
    output_spread.over()
    pairs = jnp.concatenate(clock(*pair_moving), axis=0)
    (output_cotangent,) = clock(output_cotangent)
    cotangent_moving = gather_line(output_cotangent, shard)
    queries, attention_low = attention_forward(
        projected, cosine_table, signed_sine, pairs, row_marks.T, key_marks
    )
    (output_matrix,) = place_blocks(z_order, *output_spread.finish())
    output_matrix, attention_low = clock(output_matrix.reshape(width, width), attention_low)
    hidden = wide_tokens + jnp.dot(attention_low, output_matrix, preferred_element_type=f32)
    inverse_two = lax.rsqrt(jnp.mean(hidden * hidden, axis=-1, keepdims=True) + EPSILON)
    unit_two = hidden * inverse_two
    (normed_two,) = clock((unit_two * gain_two).astype(bf16))
    normed_moving = gather_line(normed_two, shard)
    gate_up_spread = spread(jnp.stack(clock(*column_moving), axis=1))
    gate_up_spread.further()
    gate_up_spread.over()
    gate_matrix, up_matrix = place_blocks(z_order, *gate_up_spread.finish())
    gate_matrix, up_matrix = clock(
        gate_matrix.reshape(width, block_units), up_matrix.reshape(width, block_units)
    )
    cotangents = jnp.concatenate(clock(*cotangent_moving), axis=0)
    group_normed = jnp.concatenate(clock(*normed_moving), axis=0)

    inner_act, d_gate, d_up = clock(
        *feed_forward(group_normed, cotangents, gate_matrix, up_matrix, down_weight)
    )

    def start_halving(left, right, groups, shape, axis):
        sent, own = clock(*split_gradient(left, right, groups, core.place))
        halving = Halving(clock, [own.reshape(shape)], axis)
        halving.moving = [core.shift(sent, 1).reshape(shape)]
        return halving

    down = start_halving(
        inner_act, cotangents, 1, plane + (block_units // reps, width), 0
    )
    normed_own, *normed_partial = clock(
        *rows_product((d_gate, d_up), (gate_matrix, up_matrix), True, shards)
    )
    normed_arriving = send_rows(normed_partial)
    down.receive()
    down.send(first)
    gate = start_halving(group_normed, d_gate, shards, by_rows + (block_units,), 1)
    up = start_halving(group_normed, d_up, shards, by_rows + (block_units,), 1)
    gate.receive()
    gate.send(first)
    down.receive()
    down.send(second)
    up.receive()
    up.send(first)
    gate.receive()
    gate.send(second)
    down.receive()
    down_spread = spread(total_of(down.terms).astype(bf16))

    normed_two_gradient = total_of([normed_own] + clock(*normed_arriving))
    gain_two_gradient = jnp.sum(normed_two_gradient * unit_two, axis=0)
    hidden_gradient = output_cotangent.astype(f32) + norm_back(
        normed_two_gradient, unit_two, inverse_two, gain_two
    )
    (branch_gradient,) = clock(hidden_gradient.astype(bf16))
    up.receive()
    up.send(second)
    (attention_gradient,) = clock(times_transposed(branch_gradient, output_matrix).astype(bf16))
    d_queries, pair_own, *pair_partial = clock(
        *attention_backward(
            queries,
            attention_gradient,
            pairs,
            cosine_table,
            signed_sine,
            row_marks,
            key_marks.T,
            shards,
        )
    )
    pair_arriving = send_rows(pair_partial)
    output = start_halving(attention_low, branch_gradient, shards, by_rows + (width,), 1)
    down_spread.further()
    gate.receive()
    gate_moving = place_sends(total_of(gate.terms).astype(bf16))
    output.receive()
    output.send(first)
    up.receive()
    up_moving = place_sends(total_of(up.terms).astype(bf16))
    pair_terms = [pair_own] + clock(*pair_arriving)
    projected_gradient, bias_sum = clock(
        *join_projected(d_queries, pair_terms, cosine_table, signed_sine)
    )
    projected = start_halving(
        normed_one, projected_gradient, shards, by_rows + (projected_gradient.shape[1],), 1
    )
    down_spread.over()

    def side_by_side(moving):
        rows = clock(*moving)
        return jnp.concatenate(in_place_order(rows, shard), axis=1)

    gate_spread = spread(side_by_side(gate_moving))
    projected.receive()
    projected.send(first)
    normed_one_gradient = times_transposed(projected_gradient, input_matrix)
    gain_one_gradient = jnp.sum(normed_one_gradient * unit_one, axis=0)
    (tokens_gradient,) = clock(
        (
            hidden_gradient + norm_back(normed_one_gradient, unit_one, inverse_one, gain_one)
        ).astype(bf16)
    )
    bias_gradient = bias_sum[0]
    bias_split = query_width + pair_width
    small_parts = (
        gain_one_gradient,
        gain_two_gradient,
        bias_gradient[:bias_split],
        bias_gradient[bias_split:],
    )
    (small_rows,) = clock(
        jnp.concatenate([part.reshape(shards, -1) for part in small_parts], axis=1)
    )
    small_moving = place_sends(small_rows)
    block_own, *block_partial = clock(*rows_product((inner_act,), (down_weight,), False, shards))
    block_arriving = send_rows(block_partial)
    up_spread = spread(side_by_side(up_moving))
    output.receive()
    output.send(second)
    gate_spread.further()
    projected.receive()
    projected.send(second)
    small = total_of(clock(*small_moving))
    small_moving = [core.shift(small, 1)]
    down_total, *small_moving = clock(widen_pieces(*down_spread.finish()), *small_moving)
    small = total_of([small] + small_moving)
    small_moving = [first.shift(small, step) for step in range(1, first.size)]
    output.receive()
    output_moving = place_sends(total_of(output.terms).astype(bf16))
    gate_spread.over()
    projected.receive()
    projected_moving = place_sends(total_of(projected.terms).astype(bf16))
    small = total_of([small] + clock(*small_moving))
    small_moving = [second.shift(small, step) for step in range(1, second.size)]
    up_spread.further()
    output_spread = spread(total_of(clock(*output_moving)).astype(bf16))
    (gate_total,) = clock(widen_pieces(*gate_spread.finish()))
    input_spread = spread(total_of(clock(*projected_moving)).astype(bf16))
    up_spread.over()
    output_spread.further()
    input_spread.further()
    small = total_of([small] + clock(*small_moving))
    (block_out,) = clock(total_of([hidden, block_own] + clock(*block_arriving)).astype(bf16))
    (up_total,) = clock(widen_pieces(*up_spread.finish()))
    output_spread.over()
    input_spread.over()
    (output_total,) = clock(widen_pieces(*output_spread.finish()))
    (input_total,) = clock(widen_pieces(*input_spread.finish()))

    small = small + clock.token[0, 0]
    small_totals, at = [], 0
    for part in small_parts:
        size = part.shape[0] // shards
        small_totals.append(small[at : at + size])
        at += size
    return (
        block_out,
        tokens_gradient,
        small_totals[0],
        input_total,
        small_totals[2],
        small_totals[3],
        output_total,
        small_totals[1],
        gate_total,
        up_total,
        down_total,
    )


def solution(mesh):
    placed = (
        P(("rep", "shard"), None),
        P("rep", None),
        P("shard"),
        P("shard", None),
        P("shard"),
        P("shard", None),
        P("shard"),
        P("shard", None),
        P("shard", None),
        P("shard", None),
        P(("rep", "shard"), None),
    )
    return jax.shard_map(
        on_device,
        mesh=mesh,
        in_specs=placed,
        out_specs=(
            P(("rep", "shard"), None),
            P(("rep", "shard"), None),
            P("shard"),
            P("shard", None),
            P("shard"),
            P("shard"),
            P("shard", None),
            P("shard"),
            P("shard", None),
            P("shard", None),
            P("shard", None),
        ),
        check_vma=False,
    )
```

time: 760 us -> 791 us (1.041)
  starting transfers between devices: 134 us -> 215 us
  local copies, waits for them, and re-layouts: 108 us -> 44.1 us
  waiting for transfers between devices: 257 us -> 283 us
  matrix products: 29.3 us -> 14.1 us
  Pallas kernels: 141 us -> 154 us
  other arithmetic: 78.2 us -> 68.8 us
    ppermute x119, starting transfers between devices: 134 us -> 215 us  [shift(): return lax.ppermute(value, self.name, self.pairs(step % self.size))]
    ppermute x119, waiting for transfers between devices: 257 us -> 283 us  [shift(): return lax.ppermute(value, self.name, self.pairs(step % self.size))]
    dot_general x6 -> x0, matrix products: 15 us -> none  [the longest x1 4.96 us: on_device(): jnp.einsum('tkgd,jkd->kgtj', grouped_gradient, values, preferred_element_...]
    pallas_call x4 -> x6, Pallas kernels: 25.2 us -> 38.3 us  [the longest x3 22.8 us: place_blocks(): pl.pallas_call(body, out_shape=[jax.ShapeDtypeStruct(whole, pieces[0].dty...]
    pallas_call x2 -> x0, local copies, waits for them, and re-layouts: 11.5 us -> none  [split_gradient(): pl.pallas_call(body, grid=(pl.cdiv(columns, TILE),), out_shape=[jax.Shape...]
    optimization_barrier x2 -> x0, local copies, waits for them, and re-layouts: 11.4 us -> none  [tie(): return lax.optimization_barrier(arrays)]
    squeeze x16 -> x6, local copies, waits for them, and re-layouts: 13.6 us -> 2.74 us  [pick(): return lax.dynamic_index_in_dim(array, index, axis, keepdims=False)]
    squeeze x8 -> x0, local copies, waits for them, and re-layouts: 10.8 us -> none  [on_device(): piece[at]]
  transfers between devices with their start and end apart: 119 -> 119, of which waited for: 32 -> 37; matrix products, arithmetic and copies ran while one was open for 25% -> 14% of each run, Pallas kernels for 8% -> 14%
where the time goes in v3:
time: 791 us; the launch traced here: 782 us
  waiting for transfers between devices  283 us (36%)
  starting transfers between devices  215 us (27%)
  Pallas kernels  154 us (19%)
  other arithmetic  68.8 us (9%)
  local copies, waits for them, and re-layouts  44.1 us (6%)
  matrix products  14.1 us (2%)
    ppermute x119, waiting for transfers between devices, shift(): return lax.ppermute(value, self.name, self.pairs(step % self.size))  283 us
    ppermute x119, starting transfers between devices, shift(): return lax.ppermute(value, self.name, self.pairs(step % self.size))  215 us
    pallas_call x5, Pallas kernels, split_gradient(): pl.pallas_call(body, grid=(pl.cdiv(columns, TILE),), out_shape=[jax.Shape...  41.6 us
    pallas_call x5, Pallas kernels, widen_pieces(): pl.pallas_call(body, out_shape=jax.ShapeDtypeStruct((reps, rows, columns)...  28.4 us
    convert_element_type x10, other arithmetic, send(): total_of([pick(term, line.ahead(step), self.axis) for term in self.terms])  28.3 us
    pallas_call x2, Pallas kernels, rows_product(): pl.pallas_call(body, grid=(pl.cdiv(columns, TILE),), out_shape=[jax.Shape...  23 us
    pallas_call x3, Pallas kernels, place_blocks(): pl.pallas_call(body, out_shape=[jax.ShapeDtypeStruct(whole, pieces[0].dty...  22.8 us
    pallas_call x1, Pallas kernels, feed_forward(): pl.pallas_call(body, grid=(pl.cdiv(units, TILE),), out_shape=[jax.ShapeDt...  22.3 us
  transfers between devices with their start and end apart: 119, of which 37 were waited for; matrix products, arithmetic and copies ran while one was open for 14% of the time, Pallas kernels for 14%

profile of v3, /device:TPU:0, one launch (start us, length us, event | category | flops | bytes accessed | tf_op | source)
XLA Modules:
  0.0 782.1 jit_solution(10572827707541633785)
XLA Ops:
  32.1 10.2 %collective-permute-done.6.refs_1_ = bf16[1,4,48,2048]{3,2,1,0:T(8,128)(2,1)} collective-permute-done((bf16[1,4,48,2048]{3,2,1,0:T(8,128)(2,1)}, bf16[1,4,48,2048]{3,2,1,0:T(8,128)(2,1)}, u32[]{:S(2)}, u32[]{:S(2)}) %collective-permute-start.6) | collective-permute-done | bytes 786464 | tf_op jit(solution)/shard_map/ppermute | solution.py:68
  63.0 6.7 collective-permute-start.11
  135.9 13.0 %collective-permute-done.27 = bf16[2,48,2240]{2,1,0:T(8,128)(2,1)S(1)} collective-permute-done((bf16[2,48,2240]{2,1,0:T(8,128)(2,1)S(1)}, bf16[2,48,2240]{2,1,0:T(8,128)(2,1)S(1)}, u32[]{:S(2)}, u32[]{:S(2)}) %collective-permute-start.27) | collective-permute-done | bytes 430112 | tf_op jit(solution)/shard_map/ppermute | solution.py:68
  151.1 39.4 %collective-permute-done.29.refs_1_ = bf16[2,4,48,2240]{3,2,1,0:T(8,128)(2,1)S(1)} collective-permute-done((bf16[2,4,48,2240]{3,2,1,0:T(8,128)(2,1)S(1)}, bf16[2,4,48,2240]{3,2,1,0:T(8,128)(2,1)S(1)}, u32[]{:S(2)}, u32[]{:S(2)}) %collective-permute-start.29) | collective-permute-done | bytes 1720352 | tf_op jit(solution)/shard_map/ppermute | solution.py:68
  192.1 20.9 %collective-permute-done.31.refs_3_ = bf16[2,4,48,2240]{3,2,1,0:T(8,128)(2,1)S(1)} collective-permute-done((bf16[2,4,48,2240]{3,2,1,0:T(8,128)(2,1)S(1)}, bf16[2,4,48,2240]{3,2,1,0:T(8,128)(2,1)S(1)}, u32[]{:S(2)}, u32[]{:S(2)}) %collective-permute-start.31) | collective-permute-done | bytes 1720352 | tf_op jit(solution)/shard_map/ppermute | solution.py:68
  213.0 10.1 %collective-permute-start.36 = (bf16[160,1536]{1,0:T(8,128)(2,1)S(1)}, bf16[160,1536]{1,0:T(8,128)(2,1)S(1)}, u32[]{:S(2)}, u32[]{:S(2)}) collective-permute-start(bf16[160,1536]{1,0:T(8,128)(2,1)S(1)} %copy-done.18), channel_id=1, source_target_pairs={{0,1},{1,2},{2,3},{3,0},{4,5},{5,6},{6,7},{7,4},{8,9},{9,10},{10,1... | collective-permute-start | bytes 1474568 | tf_op jit(solution)/shard_map/ppermute | solution.py:68
  223.1 12.6 %collective-permute-done.36 = bf16[160,1536]{1,0:T(8,128)(2,1)S(1)} collective-permute-done((bf16[160,1536]{1,0:T(8,128)(2,1)S(1)}, bf16[160,1536]{1,0:T(8,128)(2,1)S(1)}, u32[]{:S(2)}, u32[]{:S(2)}) %collective-permute-start.36) | collective-permute-done | bytes 491552 | tf_op jit(solution)/shard_map/ppermute | solution.py:68
  245.8 11.7 %place_blocks.5 = (bf16[4,8,48,2240]{3,2,1,0:T(8,128)(2,1)}, bf16[4,8,48,2240]{3,2,1,0:T(8,128)(2,1)}) custom-call(s32[4]{0:T(128)} %pad_add_fusion.4.order_ref, s32[8]{0:T(128)} %stack.214.places_ref, bf16[2,4,48,2240]{3,2,1,0:T(8,128)(2,1)} %copy-done.6, bf16[2,4,48,2240]{3,2,1,0:T(8,128)(2,1)} %copy-done.20, bf16[2,4,48,2240]{3,2,1,0:T(8,128)(2,1)} %copy-done.21, ...), custom_call_target="tpu_custom_call" | custom-call | flops 1 | bytes 1 | tf_op jit(solution)/shard_map/place_blocks/pallas_call | solution.py:265
  257.4 22.9 %collective-permute-done.37 = bf16[160,1536]{1,0:T(8,128)(2,1)S(1)} collective-permute-done((bf16[160,1536]{1,0:T(8,128)(2,1)S(1)}, bf16[160,1536]{1,0:T(8,128)(2,1)S(1)}, u32[]{:S(2)}, u32[]{:S(2)}) %collective-permute-start.37) | collective-permute-done | bytes 491552 | tf_op jit(solution)/shard_map/ppermute | solution.py:68
  280.4 22.4 %collective-permute-done.40 = bf16[160,1536]{1,0:T(8,128)(2,1)} collective-permute-done((bf16[160,1536]{1,0:T(8,128)(2,1)S(1)}, bf16[160,1536]{1,0:T(8,128)(2,1)}, u32[]{:S(2)}, u32[]{:S(2)}) %collective-permute-start.40) | collective-permute-done | bytes 491552 | tf_op jit(solution)/shard_map/ppermute | solution.py:68
  308.8 22.3 %feed_forward.1 = (bf16[640,2240]{1,0:T(8,128)(2,1)}, bf16[640,2240]{1,0:T(8,128)(2,1)}, bf16[640,2240]{1,0:T(8,128)(2,1)}) custom-call(bf16[640,1536]{1,0:T(8,128)(2,1)} %copy-done.2, bf16[640,1536]{1,0:T(8,128)(2,1)} %copy-done.3, bf16[1536,2240]{1,0:T(8,128)(2,1)} %bitcast.219, bf16[1536,2240]{1,0:T(8,128)(2,1)} %bitcast.221, bf16[2240,1536]{1,0:T(8,128)(2,1)} %refs_1_.1), custom_call_target="tpu_custom_call" | custom-call | flops 1 | bytes 1 | tf_op jit(solution)/shard_map/feed_forward/pallas_call | solution.py:351
  331.2 9.9 %split_gradient.5 = (bf16[1,1120,1536]{2,1,0:T(8,128)(2,1)}, bf16[1,1120,1536]{2,1,0:T(8,128)(2,1)}) custom-call(s32[1]{0:T(128)} %bitcast.45.core_ref, bf16[640,2240]{1,0:T(8,128)(2,1)} %get-tuple-element.415.left_ref.refs_0_, bf16[640,1536]{1,0:T(8,128)(2,1)} %copy-done.3), custom_call_target="tpu_custom_call" | custom-call | flops 1 | bytes 1 | tf_op jit(solution)/shard_map/split_gradient/pallas_call | solution.py:389
  341.1 10.5 %split_gradient.6 = (bf16[4,192,2240]{2,1,0:T(8,128)(2,1)}, bf16[4,192,2240]{2,1,0:T(8,128)(2,1)}) custom-call(s32[1]{0:T(128)} %bitcast.45.core_ref, bf16[640,1536]{1,0:T(8,128)(2,1)} %copy-done.2, bf16[640,2240]{1,0:T(8,128)(2,1)} %get-tuple-element.419.refs_0_.right_ref), custom_call_target="tpu_custom_call" | custom-call | flops 1 | bytes 1 | tf_op jit(solution)/shard_map/split_gradient/pallas_call | solution.py:389
  351.6 14.6 %rows_product.2 = (bf16[160,1536]{1,0:T(8,128)(2,1)}, bf16[160,1536]{1,0:T(8,128)(2,1)}, bf16[160,1536]{1,0:T(8,128)(2,1)}, bf16[160,1536]{1,0:T(8,128)(2,1)}) custom-call(bf16[640,2240]{1,0:T(8,128)(2,1)} %get-tuple-element.419.refs_0_.right_ref, bf16[640,2240]{1,0:T(8,128)(2,1)} %get-tuple-element.420.refs_1_.right_ref, bf16[1536,2240]{1,0:T(8,128)(2,1)} %bitcast.220, ...), custom_call_target="tpu_custom_call" | custom-call | flops 1 | bytes 1 | tf_op jit(solution)/shard_map/rows_product/pallas_call | solution.py:431
  366.8 11.1 %split_gradient.7 = (bf16[4,192,2240]{2,1,0:T(8,128)(2,1)}, bf16[4,192,2240]{2,1,0:T(8,128)(2,1)}) custom-call(s32[1]{0:T(128)} %bitcast.45.core_ref, bf16[640,1536]{1,0:T(8,128)(2,1)} %copy-done.2, bf16[640,2240]{1,0:T(8,128)(2,1)} %get-tuple-element.420.refs_1_.right_ref), custom_call_target="tpu_custom_call" | custom-call | flops 1 | bytes 1 | tf_op jit(solution)/shard_map/split_gradient/pallas_call | solution.py:389
  387.4 11.7 %collective-permute-start.48 = (bf16[160,1536]{1,0:T(8,128)(2,1)}, bf16[160,1536]{1,0:T(8,128)(2,1)S(1)}, u32[]{:S(2)}, u32[]{:S(2)}) collective-permute-start(bf16[160,1536]{1,0:T(8,128)(2,1)} %get-tuple-element.446), channel_id=1, source_target_pairs={{0,3},{1,0},{2,1},{3,2},{4,7},{5,4},{6,5},{7,6},{8,11},{9,8},{10,9... | collective-permute-start | bytes 1474568 | tf_op jit(solution)/shard_map/ppermute | solution.py:68
  404.5 10.9 %collective-permute-start.50 = (bf16[160,1536]{1,0:T(8,128)(2,1)}, bf16[160,1536]{1,0:T(8,128)(2,1)}, u32[]{:S(2)}, u32[]{:S(2)}) collective-permute-start(bf16[160,1536]{1,0:T(8,128)(2,1)} %get-tuple-element.448), channel_id=1, source_target_pairs={{0,1},{1,2},{2,3},{3,0},{4,5},{5,6},{6,7},{7,4},{8,9},{9,10},{10,1... | collective-permute-start | bytes 1474568 | tf_op jit(solution)/shard_map/ppermute | solution.py:68
  428.9 8.7 %collective-permute-done.47 = bf16[280,1536]{1,0:T(8,128)(2,1)} collective-permute-done((bf16[280,1536]{1,0:T(8,128)(2,1)}, bf16[280,1536]{1,0:T(8,128)(2,1)}, u32[]{:S(2)}, u32[]{:S(2)}) %collective-permute-start.47) | collective-permute-done | bytes 860192 | tf_op jit(solution)/shard_map/ppermute | solution.py:68
  454.9 7.5 attention_backward.1
  472.6 12.4 %collective-permute-start.56 = (bf16[160,512]{1,0:T(8,128)(2,1)S(1)}, bf16[160,512]{1,0:T(8,128)(2,1)S(1)}, u32[]{:S(2)}, u32[]{:S(2)}) collective-permute-start(bf16[160,512]{1,0:T(8,128)(2,1)S(1)} %copy-done.91), channel_id=1, source_target_pairs={{0,3},{1,0},{2,1},{3,2},{4,7},{5,4},{6,5},{7,6},{8,11},{9,8},{10,9... | collective-permute-start | bytes 491528 | tf_op jit(solution)/shard_map/ppermute | solution.py:68
  489.0 10.8 %collective-permute-start.58 = (bf16[160,512]{1,0:T(8,128)(2,1)S(1)}, bf16[160,512]{1,0:T(8,128)(2,1)S(1)}, u32[]{:S(2)}, u32[]{:S(2)}) collective-permute-start(bf16[160,512]{1,0:T(8,128)(2,1)S(1)} %copy-done.89), channel_id=1, source_target_pairs={{0,1},{1,2},{2,3},{3,0},{4,5},{5,6},{6,7},{7,4},{8,9},{9,10},{10,1... | collective-permute-start | bytes 491528 | tf_op jit(solution)/shard_map/ppermute | solution.py:68
  516.5 12.4 %collective-permute-start.61 = (bf16[48,2240]{1,0:T(8,128)(2,1)}, bf16[48,2240]{1,0:T(8,128)(2,1)S(1)}, u32[]{:S(2)}, u32[]{:S(2)}) collective-permute-start(bf16[48,2240]{1,0:T(8,128)(2,1)} %get-tuple-element.653), channel_id=1, source_target_pairs={{0,1},{1,2},{2,3},{3,0},{4,5},{5,6},{6,7},{7,4},{8,9},{9,10},{10,1... | collective-permute-start | bytes 645128 | tf_op jit(solution)/shard_map/ppermute | solution.py:68
  536.5 9.3 %collective-permute-done.62 = bf16[48,2240]{1,0:T(8,128)(2,1)S(1)} collective-permute-done((bf16[48,2240]{1,0:T(8,128)(2,1)}, bf16[48,2240]{1,0:T(8,128)(2,1)S(1)}, u32[]{:S(2)}, u32[]{:S(2)}) %collective-permute-start.62) | collective-permute-done | bytes 215072 | tf_op jit(solution)/shard_map/ppermute | solution.py:68
  580.1 6.6 collective-permute-done.66
  595.2 8.4 %rows_product.3 = (bf16[160,1536]{1,0:T(8,128)(2,1)}, bf16[160,1536]{1,0:T(8,128)(2,1)}, bf16[160,1536]{1,0:T(8,128)(2,1)}, bf16[160,1536]{1,0:T(8,128)(2,1)}) custom-call(bf16[640,2240]{1,0:T(8,128)(2,1)} %get-tuple-element.415.left_ref.refs_0_, bf16[2240,1536]{1,0:T(8,128)(2,1)} %refs_1_.1), custom_call_target="tpu_custom_call" | custom-call | flops 1 | bytes 1 | tf_op jit(solution)/shard_map/rows_product/pallas_call | solution.py:431
  614.5 8.7 %collective-permute-done.79 = bf16[4,48,1536]{2,1,0:T(8,128)(2,1)S(1)} collective-permute-done((bf16[4,48,1536]{2,1,0:T(8,128)(2,1)S(1)}, bf16[4,48,1536]{2,1,0:T(8,128)(2,1)S(1)}, u32[]{:S(2)}, u32[]{:S(2)}) %collective-permute-start.79) | collective-permute-done | bytes 589856 | tf_op jit(solution)/shard_map/ppermute | solution.py:68
  628.4 7.3 widen_pieces.5
  637.5 12.2 %collective-permute-done.81.refs_3_ = bf16[48,8960]{1,0:T(8,128)(2,1)} collective-permute-done((bf16[48,8960]{1,0:T(8,128)(2,1)}, bf16[48,8960]{1,0:T(8,128)(2,1)}, u32[]{:S(2)}, u32[]{:S(2)}) %collective-permute-start.81) | collective-permute-done | bytes 860192 | tf_op jit(solution)/shard_map/ppermute | solution.py:68
  684.6 17.7 %collective-permute-start.101 = (bf16[160,1536]{1,0:T(8,128)(2,1)}, bf16[160,1536]{1,0:T(8,128)(2,1)}, u32[]{:S(2)}, u32[]{:S(2)}) collective-permute-start(bf16[160,1536]{1,0:T(8,128)(2,1)} %get-tuple-element.579), channel_id=1, source_target_pairs={{0,2},{1,3},{2,0},{3,1},{4,6},{5,7},{6,4},{7,5},{8,10},{9,11},{10,... | collective-permute-start | bytes 1474568 | tf_op jit(solution)/shard_map/ppermute | solution.py:68
  705.6 7.3 widen_pieces.6
  714.8 19.9 %collective-permute-done.101 = bf16[160,1536]{1,0:T(8,128)(2,1)} collective-permute-done((bf16[160,1536]{1,0:T(8,128)(2,1)}, bf16[160,1536]{1,0:T(8,128)(2,1)}, u32[]{:S(2)}, u32[]{:S(2)}) %collective-permute-start.101) | collective-permute-done | bytes 491552 | tf_op jit(solution)/shard_map/ppermute | solution.py:68
  759.7 7.3 widen_pieces.7
  (551 shorter events, 362.0 us)
Async XLA Ops:
  149.2 41.4 %collective-permute-start.29 = (bf16[2,4,48,2240]{3,2,1,0:T(8,128)(2,1)S(1)}, bf16[2,4,48,2240]{3,2,1,0:T(8,128)(2,1)S(1)}, u32[]{:S(2)}, u32[]{:S(2)}) collective-permute-start(bf16[2,4,48,2240]{3,2,1,0:T(8,128)(2,1)S(1)} %pad_maximum_fusion.1.refs_0_), channel_id=1, source_target_pairs={{0,16},{4,12},{8,24},{12,4},{16,0},{20,28},{24,8},{28,20},{1,17},{... | collective-permute-start | bytes 5160968 | tf_op jit(solution)/shard_map/ppermute | solution.py:68
  150.2 41.8 %collective-permute-start.30 = (bf16[2,4,48,2240]{3,2,1,0:T(8,128)(2,1)S(1)}, bf16[2,4,48,2240]{3,2,1,0:T(8,128)(2,1)S(1)}, u32[]{:S(2)}, u32[]{:S(2)}) collective-permute-start(bf16[2,4,48,2240]{3,2,1,0:T(8,128)(2,1)S(1)} %pad_maximum_fusion.1.refs_0_), channel_id=1, source_target_pairs={{0,8},{4,20},{8,0},{12,28},{16,24},{20,4},{24,16},{28,12},{1,9},{5... | collective-permute-start | bytes 5160968 | tf_op jit(solution)/shard_map/ppermute | solution.py:68
  191.5 44.9 %collective-permute-start.32 = (bf16[2,4,48,2240]{3,2,1,0:T(8,128)(2,1)S(1)}, bf16[2,4,48,2240]{3,2,1,0:T(8,128)(2,1)S(1)}, u32[]{:S(2)}, u32[]{:S(2)}) collective-permute-start(bf16[2,4,48,2240]{3,2,1,0:T(8,128)(2,1)S(1)} %pad_maximum_fusion.1.refs_0_), channel_id=1, source_target_pairs={{0,4},{4,0},{8,12},{12,8},{16,20},{20,16},{24,28},{28,24},{1,5},{5... | collective-permute-start | bytes 5160968 | tf_op jit(solution)/shard_map/ppermute | solution.py:68
  191.5 47.6 %collective-permute-start.33 = (bf16[2,4,48,2240]{3,2,1,0:T(8,128)(2,1)S(1)}, bf16[2,4,48,2240]{3,2,1,0:T(8,128)(2,1)S(1)}, u32[]{:S(2)}, u32[]{:S(2)}) collective-permute-start(bf16[2,4,48,2240]{3,2,1,0:T(8,128)(2,1)S(1)} %collective-permute-done.29.refs_1_), channel_id=1, source_target_pairs={{0,4},{4,0},{8,12},{12,8},{16,20},{20,16},{24,28},{28,24},{1,5},{5... | collective-permute-start | bytes 5160968 | tf_op jit(solution)/shard_map/ppermute | solution.py:68
  192.0 47.1 %collective-permute-start.34 = (bf16[2,4,48,2240]{3,2,1,0:T(8,128)(2,1)S(1)}, bf16[2,4,48,2240]{3,2,1,0:T(8,128)(2,1)S(1)}, u32[]{:S(2)}, u32[]{:S(2)}) collective-permute-start(bf16[2,4,48,2240]{3,2,1,0:T(8,128)(2,1)S(1)} %collective-permute-done.30.refs_2_), channel_id=1, source_target_pairs={{0,4},{4,0},{8,12},{12,8},{16,20},{20,16},{24,28},{28,24},{1,5},{5... | collective-permute-start | bytes 5160968 | tf_op jit(solution)/shard_map/ppermute | solution.py:68
  235.7 44.7 %collective-permute-start.37 = (bf16[160,1536]{1,0:T(8,128)(2,1)S(1)}, bf16[160,1536]{1,0:T(8,128)(2,1)S(1)}, u32[]{:S(2)}, u32[]{:S(2)}) collective-permute-start(bf16[160,1536]{1,0:T(8,128)(2,1)S(1)} %copy-done.18), channel_id=1, source_target_pairs={{0,2},{1,3},{2,0},{3,1},{4,6},{5,7},{6,4},{7,5},{8,10},{9,11},{10,... | collective-permute-start | bytes 1474568 | tf_op jit(solution)/shard_map/ppermute | solution.py:68
  236.4 43.9 %collective-permute-start.38 = (bf16[160,1536]{1,0:T(8,128)(2,1)S(1)}, bf16[160,1536]{1,0:T(8,128)(2,1)S(1)}, u32[]{:S(2)}, u32[]{:S(2)}) collective-permute-start(bf16[160,1536]{1,0:T(8,128)(2,1)S(1)} %copy-done.18), channel_id=1, source_target_pairs={{0,3},{1,0},{2,1},{3,2},{4,7},{5,4},{6,5},{7,6},{8,11},{9,8},{10,9... | collective-permute-start | bytes 1474568 | tf_op jit(solution)/shard_map/ppermute | solution.py:68
  239.1 41.3 %collective-permute-start.39 = (bf16[160,1536]{1,0:T(8,128)(2,1)S(1)}, bf16[160,1536]{1,0:T(8,128)(2,1)S(1)}, u32[]{:S(2)}, u32[]{:S(2)}) collective-permute-start(bf16[160,1536]{1,0:T(8,128)(2,1)S(1)} %multiply_convert_fusion), channel_id=1, source_target_pairs={{0,1},{1,2},{2,3},{3,0},{4,5},{5,6},{6,7},{7,4},{8,9},{9,10},{10,1... | collective-permute-start | bytes 1474568 | tf_op jit(solution)/shard_map/ppermute | solution.py:68
  239.1 63.7 %collective-permute-start.40 = (bf16[160,1536]{1,0:T(8,128)(2,1)S(1)}, bf16[160,1536]{1,0:T(8,128)(2,1)}, u32[]{:S(2)}, u32[]{:S(2)}) collective-permute-start(bf16[160,1536]{1,0:T(8,128)(2,1)S(1)} %multiply_convert_fusion), channel_id=1, source_target_pairs={{0,2},{1,3},{2,0},{3,1},{4,6},{5,7},{6,4},{7,5},{8,10},{9,11},{10,... | collective-permute-start | bytes 1474568 | tf_op jit(solution)/shard_map/ppermute | solution.py:68
  242.1 60.6 %collective-permute-start.41 = (bf16[160,1536]{1,0:T(8,128)(2,1)S(1)}, bf16[160,1536]{1,0:T(8,128)(2,1)}, u32[]{:S(2)}, u32[]{:S(2)}) collective-permute-start(bf16[160,1536]{1,0:T(8,128)(2,1)S(1)} %multiply_convert_fusion), channel_id=1, source_target_pairs={{0,3},{1,0},{2,1},{3,2},{4,7},{5,4},{6,5},{7,6},{8,11},{9,8},{10,9... | collective-permute-start | bytes 1474568 | tf_op jit(solution)/shard_map/ppermute | solution.py:68
  377.9 37.5 %collective-permute-start.45 = (bf16[4,192,2240]{2,1,0:T(8,128)(2,1)}, bf16[4,192,2240]{2,1,0:T(8,128)(2,1)}, u32[]{:S(2)}, u32[]{:S(2)}) collective-permute-start(bf16[4,192,2240]{2,1,0:T(8,128)(2,1)} %get-tuple-element.439), channel_id=1, source_target_pairs={{0,4},{4,0},{8,12},{12,8},{16,20},{20,16},{24,28},{28,24},{1,5},{5... | collective-permute-start | bytes 10321928 | tf_op jit(solution)/shard_map/ppermute | solution.py:68
  386.3 40.5 %collective-permute-start.46 = (bf16[4,2,48,2240]{3,2,0,1:T(8,128)(2,1)}, bf16[4,2,48,2240]{3,2,0,1:T(8,128)(2,1)}, u32[]{:S(2)}, u32[]{:S(2)}) collective-permute-start(bf16[4,2,48,2240]{3,2,0,1:T(8,128)(2,1)} %fusion), channel_id=1, source_target_pairs={{0,8},{4,20},{8,0},{12,28},{16,24},{20,4},{24,16},{28,12},{1,9},{5... | collective-permute-start | bytes 5160968 | tf_op jit(solution)/shard_map/ppermute | solution.py:68
  387.4 50.2 %collective-permute-start.48 = (bf16[160,1536]{1,0:T(8,128)(2,1)}, bf16[160,1536]{1,0:T(8,128)(2,1)S(1)}, u32[]{:S(2)}, u32[]{:S(2)}) collective-permute-start(bf16[160,1536]{1,0:T(8,128)(2,1)} %get-tuple-element.446), channel_id=1, source_target_pairs={{0,3},{1,0},{2,1},{3,2},{4,7},{5,4},{6,5},{7,6},{8,11},{9,8},{10,9... | collective-permute-start | bytes 1474568 | tf_op jit(solution)/shard_map/ppermute | solution.py:68
  399.1 43.0 %collective-permute-start.49 = (bf16[160,1536]{1,0:T(8,128)(2,1)}, bf16[160,1536]{1,0:T(8,128)(2,1)}, u32[]{:S(2)}, u32[]{:S(2)}) collective-permute-start(bf16[160,1536]{1,0:T(8,128)(2,1)} %get-tuple-element.447), channel_id=1, source_target_pairs={{0,2},{1,3},{2,0},{3,1},{4,6},{5,7},{6,4},{7,5},{8,10},{9,11},{10,... | collective-permute-start | bytes 1474568 | tf_op jit(solution)/shard_map/ppermute | solution.py:68
  404.5 37.5 %collective-permute-start.50 = (bf16[160,1536]{1,0:T(8,128)(2,1)}, bf16[160,1536]{1,0:T(8,128)(2,1)}, u32[]{:S(2)}, u32[]{:S(2)}) collective-permute-start(bf16[160,1536]{1,0:T(8,128)(2,1)} %get-tuple-element.448), channel_id=1, source_target_pairs={{0,1},{1,2},{2,3},{3,0},{4,5},{5,6},{6,7},{7,4},{8,9},{9,10},{10,1... | collective-permute-start | bytes 1474568 | tf_op jit(solution)/shard_map/ppermute | solution.py:68
  462.4 37.5 %collective-permute-start.54 = (bf16[4,192,1536]{2,1,0:T(8,128)(2,1)}, bf16[4,192,1536]{2,1,0:T(8,128)(2,1)}, u32[]{:S(2)}, u32[]{:S(2)}) collective-permute-start(bf16[4,192,1536]{2,1,0:T(8,128)(2,1)} %get-tuple-element.475), channel_id=1, source_target_pairs={{0,4},{4,0},{8,12},{12,8},{16,20},{20,16},{24,28},{28,24},{1,5},{5... | collective-permute-start | bytes 7077896 | tf_op jit(solution)/shard_map/ppermute | solution.py:68
  499.8 30.6 %collective-permute-start.59 = (bf16[280,1536]{1,0:T(8,128)(2,1)}, bf16[280,1536]{1,0:T(8,128)(2,1)}, u32[]{:S(2)}, u32[]{:S(2)}) collective-permute-start(bf16[280,1536]{1,0:T(8,128)(2,1)} %fusion.10.refs_0_), channel_id=1, source_target_pairs={{0,8},{4,20},{8,0},{12,28},{16,24},{20,4},{24,16},{28,12},{1,9},{5... | collective-permute-start | bytes 2580488 | tf_op jit(solution)/shard_map/ppermute | solution.py:68
  500.7 30.6 %collective-permute-start.60 = (bf16[280,1536]{1,0:T(8,128)(2,1)}, bf16[280,1536]{1,0:T(8,128)(2,1)}, u32[]{:S(2)}, u32[]{:S(2)}) collective-permute-start(bf16[280,1536]{1,0:T(8,128)(2,1)} %collective-permute-done.52.refs_1_), channel_id=1, source_target_pairs={{0,8},{4,20},{8,0},{12,28},{16,24},{20,4},{24,16},{28,12},{1,9},{5... | collective-permute-start | bytes 2580488 | tf_op jit(solution)/shard_map/ppermute | solution.py:68
  513.2 41.5 %collective-permute-start.64 = (bf16[4,192,2048]{2,1,0:T(8,128)(2,1)}, bf16[4,192,2048]{2,1,0:T(8,128)(2,1)}, u32[]{:S(2)}, u32[]{:S(2)}) collective-permute-start(bf16[4,192,2048]{2,1,0:T(8,128)(2,1)} %get-tuple-element.500), channel_id=1, source_target_pairs={{0,4},{4,0},{8,12},{12,8},{16,20},{20,16},{24,28},{28,24},{1,5},{5... | collective-permute-start | bytes 9437192 | tf_op jit(solution)/shard_map/ppermute | solution.py:68
  548.9 54.8 %collective-permute-start.68 = (bf16[4,2,48,1536]{3,2,0,1:T(8,128)(2,1)}, bf16[4,2,48,1536]{3,2,0,1:T(8,128)(2,1)}, u32[]{:S(2)}, u32[]{:S(2)}) collective-permute-start(bf16[4,2,48,1536]{3,2,0,1:T(8,128)(2,1)} %fusion.20), channel_id=1, source_target_pairs={{0,8},{4,20},{8,0},{12,28},{16,24},{20,4},{24,16},{28,12},{1,9},{5... | collective-permute-start | bytes 3538952 | tf_op jit(solution)/shard_map/ppermute | solution.py:68
  557.9 46.8 %collective-permute-start.70 = (bf16[4,2,48,2048]{3,2,0,1:T(8,128)(2,1)}, bf16[4,2,48,2048]{3,2,0,1:T(8,128)(2,1)}, u32[]{:S(2)}, u32[]{:S(2)}) collective-permute-start(bf16[4,2,48,2048]{3,2,0,1:T(8,128)(2,1)} %fusion.12), channel_id=1, source_target_pairs={{0,8},{4,20},{8,0},{12,28},{16,24},{20,4},{24,16},{28,12},{1,9},{5... | collective-permute-start | bytes 4718600 | tf_op jit(solution)/shard_map/ppermute | solution.py:68
  565.0 38.7 %collective-permute-start.69 = (bf16[48,8960]{1,0:T(8,128)(2,1)}, bf16[48,8960]{1,0:T(8,128)(2,1)}, u32[]{:S(2)}, u32[]{:S(2)}) collective-permute-start(bf16[48,8960]{1,0:T(8,128)(2,1)} %concatenate.59.refs_0_), channel_id=1, source_target_pairs={{0,16},{4,12},{8,24},{12,4},{16,0},{20,28},{24,8},{28,20},{1,17},{... | collective-permute-start | bytes 2580488 | tf_op jit(solution)/shard_map/ppermute | solution.py:68
  613.4 37.5 %collective-permute-start.88 = (bf16[48,8960]{1,0:T(8,128)(2,1)S(1)}, bf16[48,8960]{1,0:T(8,128)(2,1)}, u32[]{:S(2)}, u32[]{:S(2)}) collective-permute-start(bf16[48,8960]{1,0:T(8,128)(2,1)S(1)} %copy-done.11), channel_id=1, source_target_pairs={{0,4},{4,0},{8,12},{12,8},{16,20},{20,16},{24,28},{28,24},{1,5},{5... | collective-permute-start | bytes 2580488 | tf_op jit(solution)/shard_map/ppermute | solution.py:68
  613.5 36.2 %collective-permute-start.81 = (bf16[48,8960]{1,0:T(8,128)(2,1)}, bf16[48,8960]{1,0:T(8,128)(2,1)}, u32[]{:S(2)}, u32[]{:S(2)}) collective-permute-start(bf16[48,8960]{1,0:T(8,128)(2,1)} %collective-permute-done.69.refs_1_), channel_id=1, source_target_pairs={{0,8},{4,20},{8,0},{12,28},{16,24},{20,4},{24,16},{28,12},{1,9},{5... | collective-permute-start | bytes 2580488 | tf_op jit(solution)/shard_map/ppermute | solution.py:68
  660.2 52.7 %collective-permute-start.95 = (bf16[48,8960]{1,0:T(8,128)(2,1)S(1)}, bf16[48,8960]{1,0:T(8,128)(2,1)S(1)}, u32[]{:S(2)}, u32[]{:S(2)}) collective-permute-start(bf16[48,8960]{1,0:T(8,128)(2,1)S(1)} %concatenate.60.refs_0_), channel_id=1, source_target_pairs={{0,8},{4,20},{8,0},{12,28},{16,24},{20,4},{24,16},{28,12},{1,9},{5... | collective-permute-start | bytes 2580488 | tf_op jit(solution)/shard_map/ppermute | solution.py:68
  667.1 46.0 %collective-permute-start.96 = (bf16[48,8960]{1,0:T(8,128)(2,1)S(1)}, bf16[48,8960]{1,0:T(8,128)(2,1)S(1)}, u32[]{:S(2)}, u32[]{:S(2)}) collective-permute-start(bf16[48,8960]{1,0:T(8,128)(2,1)S(1)} %collective-permute-done.84.refs_1_), channel_id=1, source_target_pairs={{0,8},{4,20},{8,0},{12,28},{16,24},{20,4},{24,16},{28,12},{1,9},{5... | collective-permute-start | bytes 2580488 | tf_op jit(solution)/shard_map/ppermute | solution.py:68
  672.2 30.1 %collective-permute-start.94 = (bf16[48,2048]{1,0:T(8,128)(2,1)S(1)}, bf16[48,2048]{1,0:T(8,128)(2,1)S(1)}, u32[]{:S(2)}, u32[]{:S(2)}) collective-permute-start(bf16[48,2048]{1,0:T(8,128)(2,1)S(1)} %get-tuple-element.655), channel_id=1, source_target_pairs={{0,3},{1,0},{2,1},{3,2},{4,7},{5,4},{6,5},{7,6},{8,11},{9,8},{10,9... | collective-permute-start | bytes 589832 | tf_op jit(solution)/shard_map/ppermute | solution.py:68
  677.7 35.9 %collective-permute-start.100 = (bf16[160,1536]{1,0:T(8,128)(2,1)}, bf16[160,1536]{1,0:T(8,128)(2,1)S(1)}, u32[]{:S(2)}, u32[]{:S(2)}) collective-permute-start(bf16[160,1536]{1,0:T(8,128)(2,1)} %get-tuple-element.578), channel_id=1, source_target_pairs={{0,3},{1,0},{2,1},{3,2},{4,7},{5,4},{6,5},{7,6},{8,11},{9,8},{10,9... | collective-permute-start | bytes 1474568 | tf_op jit(solution)/shard_map/ppermute | solution.py:68
  684.6 50.1 %collective-permute-start.101 = (bf16[160,1536]{1,0:T(8,128)(2,1)}, bf16[160,1536]{1,0:T(8,128)(2,1)}, u32[]{:S(2)}, u32[]{:S(2)}) collective-permute-start(bf16[160,1536]{1,0:T(8,128)(2,1)} %get-tuple-element.579), channel_id=1, source_target_pairs={{0,2},{1,3},{2,0},{3,1},{4,6},{5,7},{6,4},{7,5},{8,10},{9,11},{10,... | collective-permute-start | bytes 1474568 | tf_op jit(solution)/shard_map/ppermute | solution.py:68
  702.3 32.3 %collective-permute-start.102 = (bf16[160,1536]{1,0:T(8,128)(2,1)}, bf16[160,1536]{1,0:T(8,128)(2,1)}, u32[]{:S(2)}, u32[]{:S(2)}) collective-permute-start(bf16[160,1536]{1,0:T(8,128)(2,1)} %get-tuple-element.580), channel_id=1, source_target_pairs={{0,1},{1,2},{2,3},{3,0},{4,5},{5,6},{6,7},{7,4},{8,9},{9,10},{10,1... | collective-permute-start | bytes 1474568 | tf_op jit(solution)/shard_map/ppermute | solution.py:68
  713.0 36.0 %collective-permute-start.103 = (bf16[48,8960]{1,0:T(8,128)(2,1)S(1)}, bf16[48,8960]{1,0:T(8,128)(2,1)S(1)}, u32[]{:S(2)}, u32[]{:S(2)}) collective-permute-start(bf16[48,8960]{1,0:T(8,128)(2,1)S(1)} %concatenate.60.refs_0_), channel_id=1, source_target_pairs={{0,4},{4,0},{8,12},{12,8},{16,20},{20,16},{24,28},{28,24},{1,5},{5... | collective-permute-start | bytes 2580488 | tf_op jit(solution)/shard_map/ppermute | solution.py:68
  713.1 41.0 %collective-permute-start.104 = (bf16[48,8960]{1,0:T(8,128)(2,1)S(1)}, bf16[48,8960]{1,0:T(8,128)(2,1)S(1)}, u32[]{:S(2)}, u32[]{:S(2)}) collective-permute-start(bf16[48,8960]{1,0:T(8,128)(2,1)S(1)} %collective-permute-done.84.refs_1_), channel_id=1, source_target_pairs={{0,4},{4,0},{8,12},{12,8},{16,20},{20,16},{24,28},{28,24},{1,5},{5... | collective-permute-start | bytes 2580488 | tf_op jit(solution)/shard_map/ppermute | solution.py:68
  (183 other events, 2972.4 us)

commit v4 on v3

--- a/solution.py
+++ b/solution.py
@@ -160,6 +160,9 @@
         self.token, *arrays = tie(self.token, *arrays)
         return arrays
 
+    def run(self, step, *arrays):
+        return self(*step(*self(*arrays)))
+
 
 def total_of(terms):
     total = terms[0].astype(jnp.float32)
@@ -168,51 +171,106 @@
     return total
 
 
+def add_chosen(chosen, *terms):
+    count = len(terms)
+    groups, places, rows, columns = terms[0].shape
+    chosen = jnp.stack([jnp.stack(line) for line in chosen]).astype(jnp.int32)
+    slots = chosen.shape[1]
+
+    def body(chosen_ref, *refs):
+        refs[count][...] = total_of([ref[...] for ref in refs[:count]]).astype(jnp.bfloat16)
+
+    return pl.pallas_call(
+        body,
+        out_shape=jax.ShapeDtypeStruct((groups, slots, rows, columns), jnp.bfloat16),
+        grid_spec=pltpu.PrefetchScalarGridSpec(
+            num_scalar_prefetch=1,
+            grid=(groups, slots),
+            in_specs=[
+                pl.BlockSpec(
+                    (1, 1, rows, columns), lambda z, j, at, t=t: (z, at[t, j], 0, 0)
+                )
+                for t in range(count)
+            ],
+            out_specs=pl.BlockSpec((1, 1, rows, columns), lambda z, j, at: (z, j, 0, 0)),
+        ),
+        compiler_params=pltpu.CompilerParams(vmem_limit_bytes=VMEM_LIMIT),
+        cost_estimate=COST,
+        name="add_chosen",
+    )(chosen, *terms)
+
+
 class Halving:
-    def __init__(self, clock, terms, axis):
-        self.clock, self.terms, self.axis = clock, terms, axis
-
-    def send(self, line):
-        self.moving = [
-            line.shift(
-                total_of([pick(term, line.ahead(step), self.axis) for term in self.terms]).astype(
-                    jnp.bfloat16
-                ),
-                step,
-            )
-            for step in range(1, line.size)
-        ]
-        self.terms = [pick(term, line.place, self.axis) for term in self.terms]
-
-    def receive(self):
-        self.terms = self.terms + self.clock(*self.moving)
+    def __init__(self, clock, sent, own, core, first, second):
+        self.clock, self.first, self.second = clock, first, second
+        self.own = own
+        self.moving = [core.shift(sent, 1)]
+
+    def chosen(self, one, two):
+        return one * self.second.size + two
+
+    def along_first(self):
+        (arrived,) = self.clock(*self.moving)
+        self.halves = [self.own, arrived]
+        self.moving = []
+        for step in range(1, self.first.size):
+            one = self.first.ahead(step)
+            slots = [self.chosen(one, two) for two in range(self.second.size)]
+            (block,) = self.clock(add_chosen([slots] * 2, *self.halves))
+            self.moving.append(self.first.shift(block, step))
+
+    def along_second(self):
+        self.quarters = self.clock(*self.moving)
+        self.moving = []
+        for step in range(1, self.second.size):
+            two = self.second.ahead(step)
+            slots = [[self.chosen(self.first.place, two)]] * 2 + [[two]] * len(self.quarters)
+            (block,) = self.clock(add_chosen(slots, *self.halves, *self.quarters))
+            self.moving.append(self.second.shift(block, step))
+
+    def finish(self):
+        eighths = self.clock(*self.moving)
+        two = self.second.place
+        zero = jnp.zeros((), jnp.int32)
+        slots = (
+            [[self.chosen(self.first.place, two)]] * 2
+            + [[two]] * len(self.quarters)
+            + [[zero]] * len(eighths)
+        )
+        (block,) = self.clock(add_chosen(slots, *self.halves, *self.quarters, *eighths))
+        return block[:, 0]
 
 
 class Spread:
     def __init__(self, clock, piece, core, first, second):
         self.clock, self.lines = clock, (core, first, second)
-        self.own = piece
         self.across = {(0, two): second.shift(piece, two) for two in range(1, second.size)}
         self.along = {(one, 0): first.shift(piece, one) for one in range(1, first.size)}
         self.here = {(0, 0): piece}
         self.there = {(0, 0): core.shift(piece, 1)}
 
-    def arrive(self, group):
-        for key, value in zip(group, self.clock(*group.values())):
+    def waits(self):
+        if hasattr(self, "beyond"):
+            return list(self.beyond.values())
+        return list(self.across.values()) + list(self.along.values())
+
+    def arrive(self, group, values):
+        for key, value in zip(group, values):
             self.here[key] = value
             self.there[key] = self.lines[0].shift(value, 1)
 
-    def further(self):
-        self.arrive(self.across)
+    def further(self, *values):
+        values = values or self.clock(*self.waits())
+        self.arrive(list(self.across) + list(self.along), values)
         self.beyond = {
             (one, two): self.lines[1].shift(self.here[0, two], one)
             for one in range(1, self.lines[1].size)
             for two in range(1, self.lines[2].size)
         }
 
-    def over(self):
-        self.arrive(self.along)
-        self.arrive(self.beyond)
+    def over(self, *values):
+        values = values or self.clock(*self.waits())
+        self.arrive(self.beyond, values)
 
     def finish(self):
         core, first, second = self.lines
@@ -228,7 +286,7 @@
         return jnp.stack(places).astype(jnp.int32), [value for c, f, s, value in placed]
 
 
-def place_blocks(order, places, pieces):
+def place_blocks(order, places, *pieces):
     reps = len(pieces)
     groups, shards = pieces[0].shape[:2]
     block = pieces[0].shape[2:]
@@ -279,7 +337,7 @@
     )(order, places, *pieces)
 
 
-def widen_pieces(places, pieces):
+def widen_pieces(places, *pieces):
     reps = len(pieces)
     rows, columns = pieces[0].shape
     strip = next(size for size in (16, 8, rows) if rows % size == 0)
@@ -308,7 +366,7 @@
         for store in stores:
             store.wait()
 
-    return pl.pallas_call(
+    result = pl.pallas_call(
         body,
         out_shape=jax.ShapeDtypeStruct((reps, rows, columns), jnp.float32),
         in_specs=[pl.BlockSpec(memory_space=pltpu.SMEM)]
@@ -323,7 +381,8 @@
         compiler_params=pltpu.CompilerParams(vmem_limit_bytes=VMEM_LIMIT),
         cost_estimate=COST,
         name="widen_pieces",
-    )(places, *pieces).reshape(reps * rows, columns)
+    )(places, *pieces)
+    return (result.reshape(reps * rows, columns),)
 
 
 def resident(shape):
@@ -587,7 +646,6 @@
     bf16, f32 = jnp.bfloat16, jnp.float32
     shards, reps = lax.axis_size("shard"), lax.axis_size("rep")
     shard, core, first, second = make_lines(reps, shards)
-    plane = (first.size, second.size)
     rep_place = (core.place * first.size + first.place) * second.size + second.place
     own_rows, width = tokens.shape
     segments = segment_ids[0]
@@ -598,7 +656,6 @@
     part_rows = input_weight.shape[0] // reps
     hidden_units = gate_weight.shape[1]
     block_units = hidden_units // shards
-    by_rows = (shards,) + plane + (part_rows,)
     clock = Clock()
     z_order = jnp.stack([shard.behind(step) for step in range(shards)]).astype(jnp.int32)
 
@@ -610,6 +667,10 @@
 
     def spread(piece):
         return Spread(clock, piece, core, first, second)
+
+    def flat_of(spread_pieces):
+        at, pieces = spread_pieces.finish()
+        return [at] + pieces
 
     def send_rows(rows):
         return [shard.shift(row, shards - step) for step, row in enumerate(rows, 1)]
@@ -622,20 +683,20 @@
     shard_vectors = jnp.concatenate([first_gain, second_gain, input_bias])
     vector_moving = gather_line(shard_vectors, shard)
     input_moving = gather_line(weight_piece(input_weight), shard)
-    input_rows = clock(*input_moving)
+    columns = [column_piece(gate_weight), column_piece(up_weight)]
+    output_piece = weight_piece(output_weight)
+    arrived = clock(*vector_moving, *input_moving, *columns, output_piece)
+    vectors, input_rows = arrived[:shards], arrived[shards : 2 * shards]
+    *columns, output_piece = arrived[2 * shards :]
+
     input_spread = spread(jnp.stack(input_rows)[None])
-    output_piece, gate_weight, up_weight = clock(
-        weight_piece(output_weight), gate_weight, up_weight
-    )
     output_moving = gather_line(output_piece, shard)
-    (columns,) = clock(jnp.stack([column_piece(gate_weight), column_piece(up_weight)], axis=1))
-    column_moving = place_sends(columns)
-    vector_rows = jnp.stack(in_place_order(clock(*vector_moving), shard))
+    cotangent_arrived = [output_cotangent, shard.shift(output_cotangent, 1)]
+    vector_rows = jnp.stack(in_place_order(vectors, shard))
     own_gain = first_gain.shape[0]
     gain_one = vector_rows[:, :own_gain].reshape(width).astype(f32)
     gain_two = vector_rows[:, own_gain : 2 * own_gain].reshape(width).astype(f32)
     shift_row = vector_rows[:, 2 * own_gain :].reshape(-1).astype(f32)
-
     places = positions(segments)
     cosine_table, sine_table = rope_tables(
         lax.dynamic_slice_in_dim(places, first_row, own_rows), HD
@@ -654,17 +715,44 @@
     )
     key_marks = jnp.stack([key_segments, key_index])
     row_marks = jnp.tile(jnp.stack([own_segments, first_row + row_index]), (1, per_group))
-
     wide_tokens = tokens.astype(f32)
     inverse_one = lax.rsqrt(jnp.mean(wide_tokens * wide_tokens, axis=-1, keepdims=True) + EPSILON)
     unit_one = wide_tokens * inverse_one
-    (normed_one,) = clock((unit_one * gain_one).astype(bf16))
-
-    input_spread.further()
-    input_spread.over()
-    output_spread = spread(jnp.stack(clock(*output_moving))[None])
-    (input_matrix,) = place_blocks(z_order, *input_spread.finish())
-    (input_matrix,) = clock(input_matrix.reshape(width, -1))
+    normed_one = (unit_one * gain_one).astype(bf16)
+    (
+        normed_one,
+        cosine_table,
+        sine_table,
+        signed_sine,
+        key_marks,
+        row_marks,
+    ) = clock(normed_one, cosine_table, sine_table, signed_sine, key_marks, row_marks)
+
+    def together(*groups):
+        flat = clock(*[array for group in groups for array in group])
+        parts, at = [], 0
+        for group in groups:
+            parts.append(flat[at : at + len(group)])
+            at += len(group)
+        return parts
+
+    arrived, output_rows, (moved,) = together(
+        input_spread.waits(), output_moving, cotangent_arrived[1:]
+    )
+    cotangent_arrived[1] = moved
+    input_spread.further(*arrived)
+    output_spread = spread(jnp.stack(output_rows)[None])
+    gate_moving = place_sends(columns[0])
+    arrived, output_arrived, gate_rows = together(
+        input_spread.waits(), output_spread.waits(), gate_moving
+    )
+    input_spread.over(*arrived)
+    output_spread.further(*output_arrived)
+    input_places, input_pieces = input_spread.finish()
+    gate_spread = spread(jnp.stack(gate_rows)[None])
+    up_moving = place_sends(columns[1])
+    (input_matrix,) = clock.run(place_blocks, z_order, input_places, *input_pieces)
+    input_matrix = input_matrix.reshape(width, -1)
     projected = jnp.dot(normed_one, input_matrix, preferred_element_type=f32) + shift_row
     key_part = rotate(
         projected[:, query_width : query_width + pair_width].reshape(own_rows, KVH, HD),
@@ -678,62 +766,83 @@
         ).astype(bf16)
     )
     pair_moving = gather_line(own_pairs, shard)
-    output_spread.further()
-    output_spread.over()
-    pairs = jnp.concatenate(clock(*pair_moving), axis=0)
-    (output_cotangent,) = clock(output_cotangent)
-    cotangent_moving = gather_line(output_cotangent, shard)
-    queries, attention_low = attention_forward(
-        projected, cosine_table, signed_sine, pairs, row_marks.T, key_marks
-    )
-    (output_matrix,) = place_blocks(z_order, *output_spread.finish())
-    output_matrix, attention_low = clock(output_matrix.reshape(width, width), attention_low)
+    pair_rows, output_arrived, gate_arrived, up_rows = together(
+        pair_moving, output_spread.waits(), gate_spread.waits(), up_moving
+    )
+    pairs = jnp.concatenate(pair_rows, axis=0)
+    output_spread.over(*output_arrived)
+    gate_spread.further(*gate_arrived)
+    up_spread = spread(jnp.stack(up_rows)[None])
+    last = shards - 1
+    cotangent_arrived += [None] * (shards - 2)
+    if last > 1:
+        cotangent_arrived[last] = shard.shift(output_cotangent, last)
+    queries, attention_low = clock.run(
+        attention_forward, projected, cosine_table, signed_sine, pairs, row_marks.T, key_marks
+    )
+    output_places, output_pieces = output_spread.finish()
+    (output_matrix,) = clock.run(place_blocks, z_order, output_places, *output_pieces)
+    output_matrix = output_matrix.reshape(width, width)
     hidden = wide_tokens + jnp.dot(attention_low, output_matrix, preferred_element_type=f32)
     inverse_two = lax.rsqrt(jnp.mean(hidden * hidden, axis=-1, keepdims=True) + EPSILON)
     unit_two = hidden * inverse_two
     (normed_two,) = clock((unit_two * gain_two).astype(bf16))
-    normed_moving = gather_line(normed_two, shard)
-    gate_up_spread = spread(jnp.stack(clock(*column_moving), axis=1))
-    gate_up_spread.further()
-    gate_up_spread.over()
-    gate_matrix, up_matrix = place_blocks(z_order, *gate_up_spread.finish())
-    gate_matrix, up_matrix = clock(
-        gate_matrix.reshape(width, block_units), up_matrix.reshape(width, block_units)
-    )
-    cotangents = jnp.concatenate(clock(*cotangent_moving), axis=0)
-    group_normed = jnp.concatenate(clock(*normed_moving), axis=0)
-
-    inner_act, d_gate, d_up = clock(
-        *feed_forward(group_normed, cotangents, gate_matrix, up_matrix, down_weight)
-    )
-
-    def start_halving(left, right, groups, shape, axis):
-        sent, own = clock(*split_gradient(left, right, groups, core.place))
-        halving = Halving(clock, [own.reshape(shape)], axis)
-        halving.moving = [core.shift(sent, 1).reshape(shape)]
-        return halving
-
-    down = start_halving(
-        inner_act, cotangents, 1, plane + (block_units // reps, width), 0
-    )
-    normed_own, *normed_partial = clock(
-        *rows_product((d_gate, d_up), (gate_matrix, up_matrix), True, shards)
+    normed_arrived = gather_line(normed_two, shard)
+    for step in range(2, last):
+        cotangent_arrived[step] = shard.shift(output_cotangent, step)
+    gate_arrived, up_arrived = together(gate_spread.waits(), up_spread.waits())
+    gate_spread.over(*gate_arrived)
+    up_spread.further(*up_arrived)
+    edge = [1] if last == 1 else [1, last]
+    up_arrived, normed_edge, (moved,) = together(
+        up_spread.waits(), [normed_arrived[step] for step in edge], [cotangent_arrived[last]]
+    )
+    up_spread.over(*up_arrived)
+    cotangent_arrived[last] = moved
+    for step, value in zip(edge, normed_edge):
+        normed_arrived[step] = value
+    gate_places, gate_pieces = gate_spread.finish()
+    (gate_matrix,) = clock.run(place_blocks, z_order, gate_places, *gate_pieces)
+    up_places, up_pieces = up_spread.finish()
+    (up_matrix,) = clock.run(place_blocks, z_order, up_places, *up_pieces)
+    gate_matrix = gate_matrix.reshape(width, block_units)
+    up_matrix = up_matrix.reshape(width, block_units)
+    normed_arrived, cotangent_arrived = together(normed_arrived, cotangent_arrived)
+    cotangents = jnp.concatenate(cotangent_arrived, axis=0)
+    group_normed = jnp.concatenate(normed_arrived, axis=0)
+
+    inner_act, d_gate, d_up = clock.run(
+        feed_forward, group_normed, cotangents, gate_matrix, up_matrix, down_weight
+    )
+
+    def start_halving(left, right, groups):
+        sent, own = clock.run(
+            lambda left, right: split_gradient(left, right, groups, core.place), left, right
+        )
+        shape = (groups, first.size * second.size, -1, right.shape[1])
+        return Halving(clock, sent.reshape(shape), own.reshape(shape), core, first, second)
+
+    def side_by_side(moving):
+        rows = clock(*moving)
+        return clock(jnp.concatenate(in_place_order(rows, shard), axis=1))[0]
+
+    down = start_halving(inner_act, cotangents, 1)
+    normed_own, *normed_partial = clock.run(
+        lambda *operands: rows_product(operands[:2], operands[2:], True, shards),
+        d_gate,
+        d_up,
+        gate_matrix,
+        up_matrix,
     )
     normed_arriving = send_rows(normed_partial)
-    down.receive()
-    down.send(first)
-    gate = start_halving(group_normed, d_gate, shards, by_rows + (block_units,), 1)
-    up = start_halving(group_normed, d_up, shards, by_rows + (block_units,), 1)
-    gate.receive()
-    gate.send(first)
-    down.receive()
-    down.send(second)
-    up.receive()
-    up.send(first)
-    gate.receive()
-    gate.send(second)
-    down.receive()
-    down_spread = spread(total_of(down.terms).astype(bf16))
+    down.along_first()
+    gate = start_halving(group_normed, d_gate, shards)
+    up = start_halving(group_normed, d_up, shards)
+    gate.along_first()
+    down.along_second()
+    up.along_first()
+    gate.along_second()
+    down_spread = spread(down.finish()[0])
 
     normed_two_gradient = total_of([normed_own] + clock(*normed_arriving))
     gain_two_gradient = jnp.sum(normed_two_gradient * unit_two, axis=0)
@@ -741,46 +850,46 @@
         normed_two_gradient, unit_two, inverse_two, gain_two
     )
     (branch_gradient,) = clock(hidden_gradient.astype(bf16))
-    up.receive()
-    up.send(second)
     (attention_gradient,) = clock(times_transposed(branch_gradient, output_matrix).astype(bf16))
-    d_queries, pair_own, *pair_partial = clock(
-        *attention_backward(
-            queries,
-            attention_gradient,
-            pairs,
-            cosine_table,
-            signed_sine,
-            row_marks,
-            key_marks.T,
-            shards,
-        )
+    d_queries, pair_own, *pair_partial = clock.run(
+        lambda *operands: attention_backward(*operands, shards),
+        queries,
+        attention_gradient,
+        pairs,
+        cosine_table,
+        signed_sine,
+        row_marks,
+        key_marks.T,
     )
     pair_arriving = send_rows(pair_partial)
-    output = start_halving(attention_low, branch_gradient, shards, by_rows + (width,), 1)
+    up.along_second()
+    output = start_halving(attention_low, branch_gradient, shards)
+    gate_moving = place_sends(gate.finish())
+    output.along_first()
     down_spread.further()
-    gate.receive()
-    gate_moving = place_sends(total_of(gate.terms).astype(bf16))
-    output.receive()
-    output.send(first)
-    up.receive()
-    up_moving = place_sends(total_of(up.terms).astype(bf16))
+    up_moving = place_sends(up.finish())
     pair_terms = [pair_own] + clock(*pair_arriving)
-    projected_gradient, bias_sum = clock(
-        *join_projected(d_queries, pair_terms, cosine_table, signed_sine)
-    )
-    projected = start_halving(
-        normed_one, projected_gradient, shards, by_rows + (projected_gradient.shape[1],), 1
-    )
+    projected_gradient, bias_sum = clock.run(
+        lambda *operands: join_projected(operands[0], operands[3:], *operands[1:3]),
+        d_queries,
+        cosine_table,
+        signed_sine,
+        *pair_terms,
+    )
+    projected = start_halving(normed_one, projected_gradient, shards)
+    gate_spread = spread(side_by_side(gate_moving))
+    projected.along_first()
+    block_own, *block_partial = clock.run(
+        lambda left, right: rows_product((left,), (right,), False, shards), inner_act, down_weight
+    )
+    output.along_second()
     down_spread.over()
-
-    def side_by_side(moving):
-        rows = clock(*moving)
-        return jnp.concatenate(in_place_order(rows, shard), axis=1)
-
-    gate_spread = spread(side_by_side(gate_moving))
-    projected.receive()
-    projected.send(first)
+    up_piece = side_by_side(up_moving)
+    block_arriving = send_rows(block_partial)
+    projected.along_second()
+    up_spread = spread(up_piece)
+    gate_spread.further()
+    projected_gradient, hidden_gradient = clock(projected_gradient, hidden_gradient)
     normed_one_gradient = times_transposed(projected_gradient, input_matrix)
     gain_one_gradient = jnp.sum(normed_one_gradient * unit_one, axis=0)
     (tokens_gradient,) = clock(
@@ -800,40 +909,30 @@
         jnp.concatenate([part.reshape(shards, -1) for part in small_parts], axis=1)
     )
     small_moving = place_sends(small_rows)
-    block_own, *block_partial = clock(*rows_product((inner_act,), (down_weight,), False, shards))
-    block_arriving = send_rows(block_partial)
-    up_spread = spread(side_by_side(up_moving))
-    output.receive()
-    output.send(second)
-    gate_spread.further()
-    projected.receive()
-    projected.send(second)
+    output_moving = place_sends(output.finish())
+    projected_moving = place_sends(projected.finish())
+    gate_spread.over()
+    (down_total,) = clock.run(widen_pieces, *flat_of(down_spread))
     small = total_of(clock(*small_moving))
     small_moving = [core.shift(small, 1)]
-    down_total, *small_moving = clock(widen_pieces(*down_spread.finish()), *small_moving)
-    small = total_of([small] + small_moving)
+    output_spread = spread(clock(total_of(clock(*output_moving)).astype(bf16))[0])
+    input_spread = spread(clock(total_of(clock(*projected_moving)).astype(bf16))[0])
+    up_spread.further()
+    small = total_of([small] + clock(*small_moving))
     small_moving = [first.shift(small, step) for step in range(1, first.size)]
-    output.receive()
-    output_moving = place_sends(total_of(output.terms).astype(bf16))
-    gate_spread.over()
-    projected.receive()
-    projected_moving = place_sends(total_of(projected.terms).astype(bf16))
+    (gate_total,) = clock.run(widen_pieces, *flat_of(gate_spread))
+    output_spread.further()
+    input_spread.further()
+    up_spread.over()
     small = total_of([small] + clock(*small_moving))
     small_moving = [second.shift(small, step) for step in range(1, second.size)]
-    up_spread.further()
-    output_spread = spread(total_of(clock(*output_moving)).astype(bf16))
-    (gate_total,) = clock(widen_pieces(*gate_spread.finish()))
-    input_spread = spread(total_of(clock(*projected_moving)).astype(bf16))
-    up_spread.over()
-    output_spread.further()
-    input_spread.further()
-    small = total_of([small] + clock(*small_moving))
     (block_out,) = clock(total_of([hidden, block_own] + clock(*block_arriving)).astype(bf16))
-    (up_total,) = clock(widen_pieces(*up_spread.finish()))
     output_spread.over()
     input_spread.over()
-    (output_total,) = clock(widen_pieces(*output_spread.finish()))
-    (input_total,) = clock(widen_pieces(*input_spread.finish()))
+    (up_total,) = clock.run(widen_pieces, *flat_of(up_spread))
+    small = total_of([small] + clock(*small_moving))
+    (output_total,) = clock.run(widen_pieces, *flat_of(output_spread))
+    (input_total,) = clock.run(widen_pieces, *flat_of(input_spread))
 
     small = small + clock.token[0, 0]
     small_totals, at = [], 0

time: 791 us -> 780 us (0.986)
  starting transfers between devices: 215 us -> 122 us
  Pallas kernels: 154 us -> 232 us
  other arithmetic: 68.8 us -> 29.6 us
  local copies, waits for them, and re-layouts: 44.1 us -> 66 us
  waiting for transfers between devices: 283 us -> 304 us
    ppermute x119 -> x129, starting transfers between devices: 215 us -> 122 us  [shift(): return lax.ppermute(value, self.name, self.pairs(step % self.size))]
    pallas_call x0 -> x15, Pallas kernels: none -> 76.3 us  [add_chosen(): pl.pallas_call(body, out_shape=jax.ShapeDtypeStruct((groups, slots, rows,...]
    convert_element_type x18 -> x3, other arithmetic: 43.1 us -> 1.04 us  [the longest x1 0.84 us: on_device(): normed_one = (unit_one * gain_one).astype(bf16)]
    ppermute x119 -> x129, waiting for transfers between devices: 283 us -> 304 us  [shift(): return lax.ppermute(value, self.name, self.pairs(step % self.size))]
    unnamed x208 -> x262, local copies, waits for them, and re-layouts: 19.5 us -> 32.1 us
    pallas_call x3 -> x4, Pallas kernels: 22.8 us -> 25.2 us  [place_blocks(): pl.pallas_call(body, out_shape=[jax.ShapeDtypeStruct(whole, pieces[0].dty...]
  transfers between devices with their start and end apart: 119 -> 129, of which waited for: 37 -> 40; matrix products, arithmetic and copies ran while one was open for 14% -> 10% of each run, Pallas kernels for 14% -> 21%
where the time goes in v4:
time: 780 us; the launch traced here: 770 us
  waiting for transfers between devices  304 us (39%)
  Pallas kernels  232 us (30%)
  starting transfers between devices  122 us (16%)
  local copies, waits for them, and re-layouts  66 us (8%)
  other arithmetic  29.6 us (4%)
  matrix products  14 us (2%)
    ppermute x129, waiting for transfers between devices, shift(): return lax.ppermute(value, self.name, self.pairs(step % self.size))  304 us
    ppermute x129, starting transfers between devices, shift(): return lax.ppermute(value, self.name, self.pairs(step % self.size))  122 us
    pallas_call x15, Pallas kernels, add_chosen(): pl.pallas_call(body, out_shape=jax.ShapeDtypeStruct((groups, slots, rows,...  76.3 us
    pallas_call x5, Pallas kernels, split_gradient(): pl.pallas_call(body, grid=(pl.cdiv(columns, TILE),), out_shape=[jax.Shape...  40.8 us
    unnamed x262, local copies, waits for them, and re-layouts  32.1 us
    pallas_call x5, Pallas kernels, widen_pieces(): pl.pallas_call(body, out_shape=jax.ShapeDtypeStruct((reps, rows, columns)...  28.4 us
    pallas_call x4, Pallas kernels, place_blocks(): pl.pallas_call(body, out_shape=[jax.ShapeDtypeStruct(whole, pieces[0].dty...  25.2 us
    pallas_call x2, Pallas kernels, rows_product(): pl.pallas_call(body, grid=(pl.cdiv(columns, TILE),), out_shape=[jax.Shape...  23 us
  transfers between devices with their start and end apart: 129, of which 40 were waited for; matrix products, arithmetic and copies ran while one was open for 10% of the time, Pallas kernels for 21%

profile of v4, /device:TPU:0, one launch (start us, length us, event | category | flops | bytes accessed | tf_op | source)
XLA Modules:
  0.0 769.6 jit_solution(14170880923113282429)
XLA Ops:
  38.8 8.4 %collective-permute-done.8 = bf16[48,1536]{1,0:T(8,128)(2,1)S(1)} collective-permute-done((bf16[48,1536]{1,0:T(8,128)(2,1)}, bf16[48,1536]{1,0:T(8,128)(2,1)S(1)}, u32[]{:S(2)}, u32[]{:S(2)}) %collective-permute-start.8) | collective-permute-done | bytes 147488 | tf_op jit(solution)/shard_map/ppermute | solution.py:68
  153.6 18.2 %collective-permute-done.35.refs_3_ = bf16[1,4,48,2240]{3,2,1,0:T(8,128)(2,1)S(1)} collective-permute-done((bf16[1,4,48,2240]{3,2,1,0:T(8,128)(2,1)}, bf16[1,4,48,2240]{3,2,1,0:T(8,128)(2,1)S(1)}, u32[]{:S(2)}, u32[]{:S(2)}) %collective-permute-start.35) | collective-permute-done | bytes 860192 | tf_op jit(solution)/shard_map/ppermute | solution.py:68
  177.5 10.3 %collective-permute-done.40 = bf16[160,1536]{1,0:T(8,128)(2,1)} collective-permute-done((bf16[160,1536]{1,0:T(8,128)(2,1)S(1)}, bf16[160,1536]{1,0:T(8,128)(2,1)}, u32[]{:S(2)}, u32[]{:S(2)}) %collective-permute-start.40) | collective-permute-done | bytes 491552 | tf_op jit(solution)/shard_map/ppermute | solution.py:68
  194.6 7.0 place_blocks.6
  201.7 7.0 place_blocks.7
  208.7 17.5 %collective-permute-done.51 = bf16[160,1536]{1,0:T(8,128)(2,1)S(1)} collective-permute-done((bf16[160,1536]{1,0:T(8,128)(2,1)S(1)}, bf16[160,1536]{1,0:T(8,128)(2,1)S(1)}, u32[]{:S(2)}, u32[]{:S(2)}) %collective-permute-start.51) | collective-permute-done | bytes 491552 | tf_op jit(solution)/shard_map/ppermute | solution.py:68
  227.0 9.2 %collective-permute-done.50 = bf16[160,1536]{1,0:T(8,128)(2,1)} collective-permute-done((bf16[160,1536]{1,0:T(8,128)(2,1)S(1)}, bf16[160,1536]{1,0:T(8,128)(2,1)}, u32[]{:S(2)}, u32[]{:S(2)}) %collective-permute-start.50) | collective-permute-done | bytes 491552 | tf_op jit(solution)/shard_map/ppermute | solution.py:68
  242.4 22.4 %feed_forward.1 = (bf16[640,2240]{1,0:T(8,128)(2,1)}, bf16[640,2240]{1,0:T(8,128)(2,1)}, bf16[640,2240]{1,0:T(8,128)(2,1)}) custom-call(bf16[640,1536]{1,0:T(8,128)(2,1)} %copy-done.10, bf16[640,1536]{1,0:T(8,128)(2,1)} %copy-done.11, bf16[1536,2240]{1,0:T(8,128)(2,1)} %bitcast.160, bf16[1536,2240]{1,0:T(8,128)(2,1)} %bitcast.162, bf16[2240,1536]{1,0:T(8,128)(2,1)} %refs_1_), custom_call_target="tpu_custom_call" | custom-call | flops 1 | bytes 1 | tf_op jit(solution)/shard_map/feed_forward/pallas_call | solution.py:410
  264.7 9.9 %split_gradient.5 = (bf16[1,1120,1536]{2,1,0:T(8,128)(2,1)}, bf16[1,1120,1536]{2,1,0:T(8,128)(2,1)}) custom-call(s32[1]{0:T(128)} %bitcast.49.core_ref, bf16[640,2240]{1,0:T(8,128)(2,1)} %get-tuple-element.821.left_ref.refs_0_, bf16[640,1536]{1,0:T(8,128)(2,1)} %copy-done.11), custom_call_target="tpu_custom_call" | custom-call | flops 1 | bytes 1 | tf_op jit(solution)/shard_map/split_gradient/pallas_call | solution.py:448
  275.3 14.6 %rows_product.2 = (bf16[160,1536]{1,0:T(8,128)(2,1)}, bf16[160,1536]{1,0:T(8,128)(2,1)}, bf16[160,1536]{1,0:T(8,128)(2,1)}, bf16[160,1536]{1,0:T(8,128)(2,1)}) custom-call(bf16[640,2240]{1,0:T(8,128)(2,1)} %get-tuple-element.697.refs_0_.right_ref, bf16[640,2240]{1,0:T(8,128)(2,1)} %get-tuple-element.703.refs_1_.right_ref, bf16[1536,2240]{1,0:T(8,128)(2,1)} %bitcast.161, ...), custom_call_target="tpu_custom_call" | custom-call | flops 1 | bytes 1 | tf_op jit(solution)/shard_map/rows_product/pallas_call | solution.py:490
  295.5 10.5 %split_gradient.6 = (bf16[4,192,2240]{2,1,0:T(8,128)(2,1)}, bf16[4,192,2240]{2,1,0:T(8,128)(2,1)}) custom-call(s32[1]{0:T(128)} %bitcast.49.core_ref, bf16[640,1536]{1,0:T(8,128)(2,1)} %copy-done.10, bf16[640,2240]{1,0:T(8,128)(2,1)} %get-tuple-element.697.refs_0_.right_ref), custom_call_target="tpu_custom_call" | custom-call | flops 1 | bytes 1 | tf_op jit(solution)/shard_map/split_gradient/pallas_call | solution.py:448
  306.5 10.5 %split_gradient.7 = (bf16[4,192,2240]{2,1,0:T(8,128)(2,1)}, bf16[4,192,2240]{2,1,0:T(8,128)(2,1)}) custom-call(s32[1]{0:T(128)} %bitcast.49.core_ref, bf16[640,1536]{1,0:T(8,128)(2,1)} %copy-done.10, bf16[640,2240]{1,0:T(8,128)(2,1)} %get-tuple-element.703.refs_1_.right_ref), custom_call_target="tpu_custom_call" | custom-call | flops 1 | bytes 1 | tf_op jit(solution)/shard_map/split_gradient/pallas_call | solution.py:448
  319.6 6.8 add_chosen.16
  329.6 9.8 %collective-permute-done.54.refs_2_ = bf16[1,2,280,1536]{3,2,1,0:T(8,128)(2,1)} collective-permute-done((bf16[1,2,280,1536]{3,2,1,0:T(8,128)(2,1)}, bf16[1,2,280,1536]{3,2,1,0:T(8,128)(2,1)}, u32[]{:S(2)}, u32[]{:S(2)}) %collective-permute-start.54) | collective-permute-done | bytes 1720352 | tf_op jit(solution)/shard_map/ppermute | solution.py:68
  347.6 6.8 add_chosen.18
  354.4 13.1 %collective-permute-done.56.refs_2_ = bf16[4,2,48,2240]{3,2,1,0:T(8,128)(2,1)} collective-permute-done((bf16[4,2,48,2240]{3,2,1,0:T(8,128)(2,1)}, bf16[4,2,48,2240]{3,2,1,0:T(8,128)(2,1)}, u32[]{:S(2)}, u32[]{:S(2)}) %collective-permute-start.56) | collective-permute-done | bytes 1720352 | tf_op jit(solution)/shard_map/ppermute | solution.py:68
  379.8 7.1 collective-permute-done.59
  394.1 7.5 attention_backward.1
  415.9 17.5 %collective-permute-done.62.refs_3_ = bf16[4,1,48,2240]{3,2,1,0:T(8,128)(2,1)S(1)} collective-permute-done((bf16[4,1,48,2240]{3,2,1,0:T(8,128)(2,1)S(1)}, bf16[4,1,48,2240]{3,2,1,0:T(8,128)(2,1)S(1)}, u32[]{:S(2)}, u32[]{:S(2)}) %collective-permute-start.62) | collective-permute-done | bytes 860192 | tf_op jit(solution)/shard_map/ppermute | solution.py:68
  433.4 10.2 %collective-permute-done.64.refs_1_ = bf16[280,1536]{1,0:T(8,128)(2,1)} collective-permute-done((bf16[280,1536]{1,0:T(8,128)(2,1)}, bf16[280,1536]{1,0:T(8,128)(2,1)}, u32[]{:S(2)}, u32[]{:S(2)}) %collective-permute-start.64) | collective-permute-done | bytes 860192 | tf_op jit(solution)/shard_map/ppermute | solution.py:68
  452.1 6.4 add_chosen.23
  484.8 9.2 %collective-permute-done.71 = bf16[48,2240]{1,0:T(8,128)(2,1)S(1)} collective-permute-done((bf16[48,2240]{1,0:T(8,128)(2,1)S(1)}, bf16[48,2240]{1,0:T(8,128)(2,1)S(1)}, u32[]{:S(2)}, u32[]{:S(2)}) %collective-permute-start.71) | collective-permute-done | bytes 215072 | tf_op jit(solution)/shard_map/ppermute | solution.py:68
  498.8 6.8 add_chosen.25
  519.6 37.8 %collective-permute-done.75.refs_3_ = bf16[280,1536]{1,0:T(8,128)(2,1)} collective-permute-done((bf16[280,1536]{1,0:T(8,128)(2,1)}, bf16[280,1536]{1,0:T(8,128)(2,1)}, u32[]{:S(2)}, u32[]{:S(2)}) %collective-permute-start.75) | collective-permute-done | bytes 860192 | tf_op jit(solution)/shard_map/ppermute | solution.py:68
  566.4 8.4 %rows_product.3 = (bf16[160,1536]{1,0:T(8,128)(2,1)}, bf16[160,1536]{1,0:T(8,128)(2,1)}, bf16[160,1536]{1,0:T(8,128)(2,1)}, bf16[160,1536]{1,0:T(8,128)(2,1)}) custom-call(bf16[640,2240]{1,0:T(8,128)(2,1)} %get-tuple-element.821.left_ref.refs_0_, bf16[2240,1536]{1,0:T(8,128)(2,1)} %refs_1_), custom_call_target="tpu_custom_call" | custom-call | flops 1 | bytes 1 | tf_op jit(solution)/shard_map/rows_product/pallas_call | solution.py:490
  613.5 22.8 %collective-permute-done.83.refs_3_ = bf16[4,1,48,2048]{3,2,1,0:T(8,128)(2,1)} collective-permute-done((bf16[4,1,48,2048]{3,2,1,0:T(8,128)(2,1)}, bf16[4,1,48,2048]{3,2,1,0:T(8,128)(2,1)}, u32[]{:S(2)}, u32[]{:S(2)}) %collective-permute-start.83) | collective-permute-done | bytes 786464 | tf_op jit(solution)/shard_map/ppermute | solution.py:68
  661.0 7.3 widen_pieces.5
  670.8 12.6 %collective-permute-done.111 = bf16[160,1536]{1,0:T(8,128)(2,1)S(1)} collective-permute-done((bf16[160,1536]{1,0:T(8,128)(2,1)}, bf16[160,1536]{1,0:T(8,128)(2,1)S(1)}, u32[]{:S(2)}, u32[]{:S(2)}) %collective-permute-start.111) | collective-permute-done | bytes 491552 | tf_op jit(solution)/shard_map/ppermute | solution.py:68
  684.0 16.9 %collective-permute-done.112 = bf16[160,1536]{1,0:T(8,128)(2,1)S(1)} collective-permute-done((bf16[160,1536]{1,0:T(8,128)(2,1)}, bf16[160,1536]{1,0:T(8,128)(2,1)S(1)}, u32[]{:S(2)}, u32[]{:S(2)}) %collective-permute-start.112) | collective-permute-done | bytes 491552 | tf_op jit(solution)/shard_map/ppermute | solution.py:68
  711.3 6.8 collective-permute-done.108.refs_2_
  720.8 7.3 widen_pieces.6
  750.1 7.3 widen_pieces.7
  (633 shorter events, 392.9 us)
Async XLA Ops:
  94.3 32.1 %collective-permute-start.26 = (bf16[1,4,48,2240]{3,2,1,0:T(8,128)(2,1)}, bf16[1,4,48,2240]{3,2,1,0:T(8,128)(2,1)}, u32[]{:S(2)}, u32[]{:S(2)}) collective-permute-start(bf16[1,4,48,2240]{3,2,1,0:T(8,128)(2,1)} %maximum_bitcast_fusion.refs_0_), channel_id=1, source_target_pairs={{0,16},{4,12},{8,24},{12,4},{16,0},{20,28},{24,8},{28,20},{1,17},{... | collective-permute-start | bytes 2580488 | tf_op jit(solution)/shard_map/ppermute | solution.py:68
  95.8 30.6 %collective-permute-start.27 = (bf16[1,4,48,2240]{3,2,1,0:T(8,128)(2,1)}, bf16[1,4,48,2240]{3,2,1,0:T(8,128)(2,1)}, u32[]{:S(2)}, u32[]{:S(2)}) collective-permute-start(bf16[1,4,48,2240]{3,2,1,0:T(8,128)(2,1)} %maximum_bitcast_fusion.refs_0_), channel_id=1, source_target_pairs={{0,8},{4,20},{8,0},{12,28},{16,24},{20,4},{24,16},{28,12},{1,9},{5... | collective-permute-start | bytes 2580488 | tf_op jit(solution)/shard_map/ppermute | solution.py:68
  126.4 50.7 %collective-permute-start.41 = (bf16[160,1536]{1,0:T(8,128)(2,1)S(1)}, bf16[160,1536]{1,0:T(8,128)(2,1)}, u32[]{:S(2)}, u32[]{:S(2)}) collective-permute-start(bf16[160,1536]{1,0:T(8,128)(2,1)S(1)} %copy-done.30), channel_id=1, source_target_pairs={{0,3},{1,0},{2,1},{3,2},{4,7},{5,4},{6,5},{7,6},{8,11},{9,8},{10,9... | collective-permute-start | bytes 1474568 | tf_op jit(solution)/shard_map/ppermute | solution.py:68
  140.3 31.6 %collective-permute-start.36 = (bf16[1,4,48,2240]{3,2,1,0:T(8,128)(2,1)S(1)}, bf16[1,4,48,2240]{3,2,1,0:T(8,128)(2,1)S(1)}, u32[]{:S(2)}, u32[]{:S(2)}) collective-permute-start(bf16[1,4,48,2240]{3,2,1,0:T(8,128)(2,1)S(1)} %maximum_bitcast_fusion.1.refs_0_), channel_id=1, source_target_pairs={{0,16},{4,12},{8,24},{12,4},{16,0},{20,28},{24,8},{28,20},{1,17},{... | collective-permute-start | bytes 2580488 | tf_op jit(solution)/shard_map/ppermute | solution.py:68
  141.5 30.4 %collective-permute-start.37 = (bf16[1,4,48,2240]{3,2,1,0:T(8,128)(2,1)S(1)}, bf16[1,4,48,2240]{3,2,1,0:T(8,128)(2,1)S(1)}, u32[]{:S(2)}, u32[]{:S(2)}) collective-permute-start(bf16[1,4,48,2240]{3,2,1,0:T(8,128)(2,1)S(1)} %maximum_bitcast_fusion.1.refs_0_), channel_id=1, source_target_pairs={{0,8},{4,20},{8,0},{12,28},{16,24},{20,4},{24,16},{28,12},{1,9},{5... | collective-permute-start | bytes 2580488 | tf_op jit(solution)/shard_map/ppermute | solution.py:68
  190.2 36.0 %collective-permute-start.51 = (bf16[160,1536]{1,0:T(8,128)(2,1)S(1)}, bf16[160,1536]{1,0:T(8,128)(2,1)S(1)}, u32[]{:S(2)}, u32[]{:S(2)}) collective-permute-start(bf16[160,1536]{1,0:T(8,128)(2,1)S(1)} %copy-done.30), channel_id=1, source_target_pairs={{0,2},{1,3},{2,0},{3,1},{4,6},{5,7},{6,4},{7,5},{8,10},{9,11},{10,... | collective-permute-start | bytes 1474568 | tf_op jit(solution)/shard_map/ppermute | solution.py:68
  193.7 42.5 %collective-permute-start.50 = (bf16[160,1536]{1,0:T(8,128)(2,1)S(1)}, bf16[160,1536]{1,0:T(8,128)(2,1)}, u32[]{:S(2)}, u32[]{:S(2)}) collective-permute-start(bf16[160,1536]{1,0:T(8,128)(2,1)S(1)} %multiply_convert_fusion), channel_id=1, source_target_pairs={{0,2},{1,3},{2,0},{3,1},{4,6},{5,7},{6,4},{7,5},{8,10},{9,11},{10,... | collective-permute-start | bytes 1474568 | tf_op jit(solution)/shard_map/ppermute | solution.py:68
  326.4 41.1 %collective-permute-start.56 = (bf16[4,2,48,2240]{3,2,1,0:T(8,128)(2,1)}, bf16[4,2,48,2240]{3,2,1,0:T(8,128)(2,1)}, u32[]{:S(2)}, u32[]{:S(2)}) collective-permute-start(bf16[4,2,48,2240]{3,2,1,0:T(8,128)(2,1)} %add_chosen.16), channel_id=1, source_target_pairs={{0,8},{4,20},{8,0},{12,28},{16,24},{20,4},{24,16},{28,12},{1,9},{5... | collective-permute-start | bytes 5160968 | tf_op jit(solution)/shard_map/ppermute | solution.py:68
  342.9 32.8 %collective-permute-start.57 = (bf16[1,1,280,1536]{3,2,1,0:T(8,128)(2,1)}, bf16[1,1,280,1536]{3,2,1,0:T(8,128)(2,1)}, u32[]{:S(2)}, u32[]{:S(2)}) collective-permute-start(bf16[1,1,280,1536]{3,2,1,0:T(8,128)(2,1)} %add_chosen.17), channel_id=1, source_target_pairs={{0,16},{4,12},{8,24},{12,4},{16,0},{20,28},{24,8},{28,20},{1,17},{... | collective-permute-start | bytes 2580488 | tf_op jit(solution)/shard_map/ppermute | solution.py:68
  343.4 36.4 %collective-permute-start.58 = (bf16[160,1536]{1,0:T(8,128)(2,1)}, bf16[160,1536]{1,0:T(8,128)(2,1)}, u32[]{:S(2)}, u32[]{:S(2)}) collective-permute-start(bf16[160,1536]{1,0:T(8,128)(2,1)} %get-tuple-element.729), channel_id=1, source_target_pairs={{0,3},{1,0},{2,1},{3,2},{4,7},{5,4},{6,5},{7,6},{8,11},{9,8},{10,9... | collective-permute-start | bytes 1474568 | tf_op jit(solution)/shard_map/ppermute | solution.py:68
  345.8 41.1 %collective-permute-start.59 = (bf16[160,1536]{1,0:T(8,128)(2,1)}, bf16[160,1536]{1,0:T(8,128)(2,1)}, u32[]{:S(2)}, u32[]{:S(2)}) collective-permute-start(bf16[160,1536]{1,0:T(8,128)(2,1)} %get-tuple-element.730), channel_id=1, source_target_pairs={{0,2},{1,3},{2,0},{3,1},{4,6},{5,7},{6,4},{7,5},{8,10},{9,11},{10,... | collective-permute-start | bytes 1474568 | tf_op jit(solution)/shard_map/ppermute | solution.py:68
  345.8 41.1 %collective-permute-start.60 = (bf16[160,1536]{1,0:T(8,128)(2,1)}, bf16[160,1536]{1,0:T(8,128)(2,1)}, u32[]{:S(2)}, u32[]{:S(2)}) collective-permute-start(bf16[160,1536]{1,0:T(8,128)(2,1)} %get-tuple-element.731), channel_id=1, source_target_pairs={{0,1},{1,2},{2,3},{3,0},{4,5},{5,6},{6,7},{7,4},{8,9},{9,10},{10,1... | collective-permute-start | bytes 1474568 | tf_op jit(solution)/shard_map/ppermute | solution.py:68
  367.5 34.1 %collective-permute-start.61 = (bf16[4,2,48,2240]{3,2,1,0:T(8,128)(2,1)}, bf16[4,2,48,2240]{3,2,1,0:T(8,128)(2,1)S(1)}, u32[]{:S(2)}, u32[]{:S(2)}) collective-permute-start(bf16[4,2,48,2240]{3,2,1,0:T(8,128)(2,1)} %add_chosen.18), channel_id=1, source_target_pairs={{0,8},{4,20},{8,0},{12,28},{16,24},{20,4},{24,16},{28,12},{1,9},{5... | collective-permute-start | bytes 5160968 | tf_op jit(solution)/shard_map/ppermute | solution.py:68
  412.0 35.2 %collective-permute-start.63 = (bf16[4,4,48,1536]{3,2,1,0:T(8,128)(2,1)}, bf16[4,4,48,1536]{3,2,1,0:T(8,128)(2,1)S(1)}, u32[]{:S(2)}, u32[]{:S(2)}) collective-permute-start(bf16[4,4,48,1536]{3,2,1,0:T(8,128)(2,1)} %bitcast.220), channel_id=1, source_target_pairs={{0,4},{4,0},{8,12},{12,8},{16,20},{20,16},{24,28},{28,24},{1,5},{5... | collective-permute-start | bytes 7077896 | tf_op jit(solution)/shard_map/ppermute | solution.py:68
  412.4 31.2 %collective-permute-start.64 = (bf16[280,1536]{1,0:T(8,128)(2,1)}, bf16[280,1536]{1,0:T(8,128)(2,1)}, u32[]{:S(2)}, u32[]{:S(2)}) collective-permute-start(bf16[280,1536]{1,0:T(8,128)(2,1)} %bitcast.66.refs_0_), channel_id=1, source_target_pairs={{0,16},{4,12},{8,24},{12,4},{16,0},{20,28},{24,8},{28,20},{1,17},{... | collective-permute-start | bytes 2580488 | tf_op jit(solution)/shard_map/ppermute | solution.py:68
  414.1 44.4 %collective-permute-start.65 = (bf16[280,1536]{1,0:T(8,128)(2,1)}, bf16[280,1536]{1,0:T(8,128)(2,1)}, u32[]{:S(2)}, u32[]{:S(2)}) collective-permute-start(bf16[280,1536]{1,0:T(8,128)(2,1)} %bitcast.66.refs_0_), channel_id=1, source_target_pairs={{0,8},{4,20},{8,0},{12,28},{16,24},{20,4},{24,16},{28,12},{1,9},{5... | collective-permute-start | bytes 2580488 | tf_op jit(solution)/shard_map/ppermute | solution.py:68
  414.7 43.7 %collective-permute-start.66 = (bf16[4,1,48,2240]{3,2,1,0:T(8,128)(2,1)}, bf16[4,1,48,2240]{3,2,1,0:T(8,128)(2,1)S(1)}, u32[]{:S(2)}, u32[]{:S(2)}) collective-permute-start(bf16[4,1,48,2240]{3,2,1,0:T(8,128)(2,1)} %add_chosen.21), channel_id=1, source_target_pairs={{0,16},{4,12},{8,24},{12,4},{16,0},{20,28},{24,8},{28,20},{1,17},{... | collective-permute-start | bytes 2580488 | tf_op jit(solution)/shard_map/ppermute | solution.py:68
  433.4 30.7 %collective-permute-start.67 = (bf16[160,512]{1,0:T(8,128)(2,1)S(1)}, bf16[160,512]{1,0:T(8,128)(2,1)S(1)}, u32[]{:S(2)}, u32[]{:S(2)}) collective-permute-start(bf16[160,512]{1,0:T(8,128)(2,1)S(1)} %copy-done.116), channel_id=1, source_target_pairs={{0,3},{1,0},{2,1},{3,2},{4,7},{5,4},{6,5},{7,6},{8,11},{9,8},{10,9... | collective-permute-start | bytes 491528 | tf_op jit(solution)/shard_map/ppermute | solution.py:68
  505.6 74.2 %collective-permute-start.79 = (bf16[4,2,48,2048]{3,2,1,0:T(8,128)(2,1)}, bf16[4,2,48,2048]{3,2,1,0:T(8,128)(2,1)S(1)}, u32[]{:S(2)}, u32[]{:S(2)}) collective-permute-start(bf16[4,2,48,2048]{3,2,1,0:T(8,128)(2,1)} %add_chosen.25), channel_id=1, source_target_pairs={{0,8},{4,20},{8,0},{12,28},{16,24},{20,4},{24,16},{28,12},{1,9},{5... | collective-permute-start | bytes 4718600 | tf_op jit(solution)/shard_map/ppermute | solution.py:68
  506.3 55.4 %collective-permute-start.74 = (bf16[4,2,48,1536]{3,2,1,0:T(8,128)(2,1)}, bf16[4,2,48,1536]{3,2,1,0:T(8,128)(2,1)S(1)}, u32[]{:S(2)}, u32[]{:S(2)}) collective-permute-start(bf16[4,2,48,1536]{3,2,1,0:T(8,128)(2,1)} %add_chosen.23), channel_id=1, source_target_pairs={{0,8},{4,20},{8,0},{12,28},{16,24},{20,4},{24,16},{28,12},{1,9},{5... | collective-permute-start | bytes 3538952 | tf_op jit(solution)/shard_map/ppermute | solution.py:68
  507.7 49.8 %collective-permute-start.75 = (bf16[280,1536]{1,0:T(8,128)(2,1)}, bf16[280,1536]{1,0:T(8,128)(2,1)}, u32[]{:S(2)}, u32[]{:S(2)}) collective-permute-start(bf16[280,1536]{1,0:T(8,128)(2,1)} %collective-permute-done.64.refs_1_), channel_id=1, source_target_pairs={{0,8},{4,20},{8,0},{12,28},{16,24},{20,4},{24,16},{28,12},{1,9},{5... | collective-permute-start | bytes 2580488 | tf_op jit(solution)/shard_map/ppermute | solution.py:68
  515.0 75.0 %collective-permute-start.80 = (bf16[48,8960]{1,0:T(8,128)(2,1)}, bf16[48,8960]{1,0:T(8,128)(2,1)}, u32[]{:S(2)}, u32[]{:S(2)}) collective-permute-start(bf16[48,8960]{1,0:T(8,128)(2,1)} %concatenate.50.refs_0_), channel_id=1, source_target_pairs={{0,16},{4,12},{8,24},{12,4},{16,0},{20,28},{24,8},{28,20},{1,17},{... | collective-permute-start | bytes 2580488 | tf_op jit(solution)/shard_map/ppermute | solution.py:68
  518.2 72.3 %collective-permute-start.81 = (bf16[48,8960]{1,0:T(8,128)(2,1)}, bf16[48,8960]{1,0:T(8,128)(2,1)}, u32[]{:S(2)}, u32[]{:S(2)}) collective-permute-start(bf16[48,8960]{1,0:T(8,128)(2,1)} %concatenate.50.refs_0_), channel_id=1, source_target_pairs={{0,8},{4,20},{8,0},{12,28},{16,24},{20,4},{24,16},{28,12},{1,9},{5... | collective-permute-start | bytes 2580488 | tf_op jit(solution)/shard_map/ppermute | solution.py:68
  595.3 73.0 %collective-permute-start.98 = (bf16[48,8960]{1,0:T(8,128)(2,1)S(1)}, bf16[48,8960]{1,0:T(8,128)(2,1)S(1)}, u32[]{:S(2)}, u32[]{:S(2)}) collective-permute-start(bf16[48,8960]{1,0:T(8,128)(2,1)S(1)} %concatenate.51.refs_0_), channel_id=1, source_target_pairs={{0,16},{4,12},{8,24},{12,4},{16,0},{20,28},{24,8},{28,20},{1,17},{... | collective-permute-start | bytes 2580488 | tf_op jit(solution)/shard_map/ppermute | solution.py:68
  596.5 71.9 %collective-permute-start.99 = (bf16[48,8960]{1,0:T(8,128)(2,1)S(1)}, bf16[48,8960]{1,0:T(8,128)(2,1)S(1)}, u32[]{:S(2)}, u32[]{:S(2)}) collective-permute-start(bf16[48,8960]{1,0:T(8,128)(2,1)S(1)} %concatenate.51.refs_0_), channel_id=1, source_target_pairs={{0,8},{4,20},{8,0},{12,28},{16,24},{20,4},{24,16},{28,12},{1,9},{5... | collective-permute-start | bytes 2580488 | tf_op jit(solution)/shard_map/ppermute | solution.py:68
  597.2 39.0 %collective-permute-start.83 = (bf16[4,1,48,2048]{3,2,1,0:T(8,128)(2,1)}, bf16[4,1,48,2048]{3,2,1,0:T(8,128)(2,1)}, u32[]{:S(2)}, u32[]{:S(2)}) collective-permute-start(bf16[4,1,48,2048]{3,2,1,0:T(8,128)(2,1)} %add_chosen.27), channel_id=1, source_target_pairs={{0,16},{4,12},{8,24},{12,4},{16,0},{20,28},{24,8},{28,20},{1,17},{... | collective-permute-start | bytes 2359304 | tf_op jit(solution)/shard_map/ppermute | solution.py:68
  600.9 56.2 %collective-permute-start.84 = (bf16[48,8960]{1,0:T(8,128)(2,1)}, bf16[48,8960]{1,0:T(8,128)(2,1)}, u32[]{:S(2)}, u32[]{:S(2)}) collective-permute-start(bf16[48,8960]{1,0:T(8,128)(2,1)} %collective-permute-done.80.refs_1_), channel_id=1, source_target_pairs={{0,8},{4,20},{8,0},{12,28},{16,24},{20,4},{24,16},{28,12},{1,9},{5... | collective-permute-start | bytes 2580488 | tf_op jit(solution)/shard_map/ppermute | solution.py:68
  668.6 32.3 %collective-permute-start.112 = (bf16[160,1536]{1,0:T(8,128)(2,1)}, bf16[160,1536]{1,0:T(8,128)(2,1)S(1)}, u32[]{:S(2)}, u32[]{:S(2)}) collective-permute-start(bf16[160,1536]{1,0:T(8,128)(2,1)} %get-tuple-element.931), channel_id=1, source_target_pairs={{0,2},{1,3},{2,0},{3,1},{4,6},{5,7},{6,4},{7,5},{8,10},{9,11},{10,... | collective-permute-start | bytes 1474568 | tf_op jit(solution)/shard_map/ppermute | solution.py:68
  668.6 32.3 %collective-permute-start.102 = (bf16[48,8960]{1,0:T(8,128)(2,1)}, bf16[48,8960]{1,0:T(8,128)(2,1)S(1)}, u32[]{:S(2)}, u32[]{:S(2)}) collective-permute-start(bf16[48,8960]{1,0:T(8,128)(2,1)} %collective-permute-done.80.refs_1_), channel_id=1, source_target_pairs={{0,4},{4,0},{8,12},{12,8},{16,20},{20,16},{24,28},{28,24},{1,5},{5... | collective-permute-start | bytes 2580488 | tf_op jit(solution)/shard_map/ppermute | solution.py:68
  669.1 32.6 %collective-permute-start.103 = (bf16[48,8960]{1,0:T(8,128)(2,1)}, bf16[48,8960]{1,0:T(8,128)(2,1)S(1)}, u32[]{:S(2)}, u32[]{:S(2)}) collective-permute-start(bf16[48,8960]{1,0:T(8,128)(2,1)} %collective-permute-done.81.refs_2_), channel_id=1, source_target_pairs={{0,4},{4,0},{8,12},{12,8},{16,20},{20,16},{24,28},{28,24},{1,5},{5... | collective-permute-start | bytes 2580488 | tf_op jit(solution)/shard_map/ppermute | solution.py:68
  670.8 32.7 %collective-permute-start.105 = (bf16[48,1536]{1,0:T(8,128)(2,1)S(1)}, bf16[48,1536]{1,0:T(8,128)(2,1)}, u32[]{:S(2)}, u32[]{:S(2)}) collective-permute-start(bf16[48,1536]{1,0:T(8,128)(2,1)S(1)} %add_convert_fusion.2.refs_0_), channel_id=1, source_target_pairs={{0,16},{4,12},{8,24},{12,4},{16,0},{20,28},{24,8},{28,20},{1,17},{... | collective-permute-start | bytes 442376 | tf_op jit(solution)/shard_map/ppermute | solution.py:68
  703.3 30.5 %collective-permute-start.116 = (bf16[48,8960]{1,0:T(8,128)(2,1)S(1)}, bf16[48,8960]{1,0:T(8,128)(2,1)S(1)}, u32[]{:S(2)}, u32[]{:S(2)}) collective-permute-start(bf16[48,8960]{1,0:T(8,128)(2,1)S(1)} %concatenate.51.refs_0_), channel_id=1, source_target_pairs={{0,4},{4,0},{8,12},{12,8},{16,20},{20,16},{24,28},{28,24},{1,5},{5... | collective-permute-start | bytes 2580488 | tf_op jit(solution)/shard_map/ppermute | solution.py:68
  (218 other events, 3279.5 us)

commit v5 on v4

--- a/solution.py
+++ b/solution.py
@@ -124,6 +124,17 @@
         Line("rep", outer, first, first_pairs),
         Line("rep", inner, second, second_pairs),
     )
+
+
+def rep_places(reps):
+    inner = 2 if reps % 4 == 0 else 1
+    outer = reps // (2 * inner)
+    places = []
+    for index in range(reps):
+        core, b, a = index % 2, (index // 2) % inner, index // (2 * inner)
+        one, two = (b, a) if inner == outer and core == 0 else (a, b)
+        places.append((core * outer + one) * inner + two)
+    return places
 
 
 def pick(array, index, axis):
@@ -247,21 +258,17 @@
         self.across = {(0, two): second.shift(piece, two) for two in range(1, second.size)}
         self.along = {(one, 0): first.shift(piece, one) for one in range(1, first.size)}
         self.here = {(0, 0): piece}
-        self.there = {(0, 0): core.shift(piece, 1)}
 
     def waits(self):
+        if hasattr(self, "there"):
+            return [self.there]
         if hasattr(self, "beyond"):
             return list(self.beyond.values())
         return list(self.across.values()) + list(self.along.values())
 
-    def arrive(self, group, values):
-        for key, value in zip(group, values):
-            self.here[key] = value
-            self.there[key] = self.lines[0].shift(value, 1)
-
     def further(self, *values):
         values = values or self.clock(*self.waits())
-        self.arrive(list(self.across) + list(self.along), values)
+        self.here.update(zip(list(self.across) + list(self.along), values))
         self.beyond = {
             (one, two): self.lines[1].shift(self.here[0, two], one)
             for one in range(1, self.lines[1].size)
@@ -270,82 +277,108 @@
 
     def over(self, *values):
         values = values or self.clock(*self.waits())
-        self.arrive(self.beyond, values)
-
-    def finish(self):
+        self.here.update(zip(self.beyond, values))
+        (stacked,) = self.clock(jnp.stack(list(self.here.values())))
+        self.there = self.lines[0].shift(stacked, 1)
+
+    def finish(self, *values):
         core, first, second = self.lines
-        placed = [
-            (core.place, first.behind(one), second.behind(two), value)
-            for (one, two), value in self.here.items()
-        ]
+        (others,) = values or self.clock(*self.waits())
+        placed = [(core.place, first.behind(one), second.behind(two)) for one, two in self.here]
         far, near = (second, first) if core.crossed else (first, second)
-        others = self.clock(*self.there.values())
-        for (one, two), value in zip(self.there, others):
-            placed.append((core.behind(1), far.behind(one), near.behind(two), value))
-        places = [(c * first.size + f) * second.size + s for c, f, s, value in placed]
-        return jnp.stack(places).astype(jnp.int32), [value for c, f, s, value in placed]
-
-
-def place_blocks(order, places, *pieces):
-    reps = len(pieces)
+        placed += [(core.behind(1), far.behind(one), near.behind(two)) for one, two in self.here]
+        places = [(c * first.size + f) * second.size + s for c, f, s in placed]
+        return [jnp.stack(places).astype(jnp.int32), others] + list(self.here.values())
+
+
+def piece_of(r, sources):
+    return sources[r] if r < len(sources) - 1 else sources[-1].at[r - len(sources) + 1]
+
+
+def place_blocks(order, places, others, *pieces):
+    reps = 2 * len(pieces)
     groups, shards = pieces[0].shape[:2]
     block = pieces[0].shape[2:]
+
+    def body(order_ref, places_ref, *refs):
+        sources, rest = refs[: len(pieces) + 1], refs[len(pieces) + 1 :]
+        move_blocks(
+            lambda g, k, r: piece_of(r, sources).at[g, k],
+            lambda r: places_ref[r],
+            order_ref,
+            rest[:groups],
+            *rest[groups:],
+        )
+
+    return blocks_call(body, 2, len(pieces) + 1, groups, shards, reps, block)(
+        order, places, *pieces, others
+    )
+
+
+def place_gathered(order, gathered):
+    reps, shards, groups = gathered.shape[:3]
+
+    def body(order_ref, source, *rest):
+        move_blocks(
+            lambda g, k, r: source.at[r, k, g], lambda r: r, order_ref, rest[:groups], *rest[groups:]
+        )
+
+    return blocks_call(body, 1, 1, groups, shards, reps, gathered.shape[3:])(order, gathered)
+
+
+def move_blocks(source_of, place_of, order_ref, outs, held, in_sems, out_sems):
+    groups, shards, reps = in_sems.shape
+    slabs = [(g, k) for g in range(groups) for k in range(shards)]
+
+    def load(g, k, r):
+        return pltpu.make_async_copy(
+            source_of(g, k, r), held.at[g, k, place_of(r)], in_sems.at[g, k, r]
+        )
+
+    def store(g, k):
+        return pltpu.make_async_copy(held.at[g, k], outs[g].at[order_ref[k]], out_sems.at[g, k])
+
+    for g, k in slabs:
+        for r in range(reps):
+            load(g, k, r).start()
+    for g, k in slabs:
+        for r in range(reps):
+            load(g, k, r).wait()
+        store(g, k).start()
+    for g, k in slabs:
+        store(g, k).wait()
+
+
+def blocks_call(body, scalars, sources, groups, shards, reps, block):
     whole = (shards, reps) + block
-
-    def body(order_ref, places_ref, *refs):
-        sources, outs, (held, in_sems, out_sems) = (
-            refs[:reps],
-            refs[reps : reps + groups],
-            refs[reps + groups :],
-        )
-        slabs = [(g, k) for g in range(groups) for k in range(shards)]
-
-        def load(g, k, r):
-            return pltpu.make_async_copy(
-                sources[r].at[g, k], held.at[g, k, places_ref[r]], in_sems.at[g, k, r]
-            )
-
-        def store(g, k):
-            return pltpu.make_async_copy(
-                held.at[g, k], outs[g].at[order_ref[k]], out_sems.at[g, k]
-            )
-
-        for g, k in slabs:
-            for r in range(reps):
-                load(g, k, r).start()
-        for g, k in slabs:
-            for r in range(reps):
-                load(g, k, r).wait()
-            store(g, k).start()
-        for g, k in slabs:
-            store(g, k).wait()
-
     return pl.pallas_call(
         body,
-        out_shape=[jax.ShapeDtypeStruct(whole, pieces[0].dtype)] * groups,
-        in_specs=[pl.BlockSpec(memory_space=pltpu.SMEM)] * 2
-        + [pl.BlockSpec(memory_space=pl.ANY)] * reps,
+        out_shape=[jax.ShapeDtypeStruct(whole, jnp.bfloat16)] * groups,
+        in_specs=[pl.BlockSpec(memory_space=pltpu.SMEM)] * scalars
+        + [pl.BlockSpec(memory_space=pl.ANY)] * sources,
         out_specs=[pl.BlockSpec(memory_space=pl.ANY)] * groups,
         scratch_shapes=[
-            pltpu.VMEM((groups,) + whole, pieces[0].dtype),
+            pltpu.VMEM((groups,) + whole, jnp.bfloat16),
             pltpu.SemaphoreType.DMA((groups, shards, reps)),
             pltpu.SemaphoreType.DMA((groups, shards)),
         ],
         compiler_params=pltpu.CompilerParams(vmem_limit_bytes=VMEM_LIMIT),
         cost_estimate=COST,
         name="place_blocks",
-    )(order, places, *pieces)
-
-
-def widen_pieces(places, *pieces):
-    reps = len(pieces)
+    )
+
+
+def widen_pieces(places, others, *pieces):
+    reps = 2 * len(pieces)
     rows, columns = pieces[0].shape
     strip = next(size for size in (16, 8, rows) if rows % size == 0)
 
     def body(places_ref, *refs):
-        sources, (out_ref, narrow, wide, in_sems, out_sems) = refs[:reps], refs[reps:]
+        sources = refs[: len(pieces) + 1]
+        out_ref, narrow, wide, in_sems, out_sems = refs[len(pieces) + 1 :]
         loads = [
-            pltpu.make_async_copy(sources[r], narrow.at[r], in_sems.at[r]) for r in range(reps)
+            pltpu.make_async_copy(piece_of(r, sources), narrow.at[r], in_sems.at[r])
+            for r in range(reps)
         ]
         stores = [
             pltpu.make_async_copy(wide.at[r], out_ref.at[places_ref[r]], out_sems.at[r])
@@ -370,7 +403,7 @@
         body,
         out_shape=jax.ShapeDtypeStruct((reps, rows, columns), jnp.float32),
         in_specs=[pl.BlockSpec(memory_space=pltpu.SMEM)]
-        + [pl.BlockSpec(memory_space=pl.ANY)] * reps,
+        + [pl.BlockSpec(memory_space=pl.ANY)] * (len(pieces) + 1),
         out_specs=pl.BlockSpec(memory_space=pl.ANY),
         scratch_shapes=[
             pltpu.VMEM((reps, rows, columns), jnp.bfloat16),
@@ -381,7 +414,7 @@
         compiler_params=pltpu.CompilerParams(vmem_limit_bytes=VMEM_LIMIT),
         cost_estimate=COST,
         name="widen_pieces",
-    )(places, *pieces)
+    )(places, *pieces, others)
     return (result.reshape(reps * rows, columns),)
 
 
@@ -460,6 +493,39 @@
         cost_estimate=COST,
         name="split_gradient",
     )(core_place.reshape(1).astype(jnp.int32), left, right)
+
+
+def ordered_gradient(left, right, shards, order):
+    reps = len(order)
+    count, rows = left.shape
+    columns = right.shape[1]
+    part = rows // (shards * reps)
+
+    def body(left_ref, right_ref, out_ref, turned):
+        @pl.when(pl.program_id(0) == 0)
+        def turn():
+            turned[...] = left_ref[...].T
+
+        product = jnp.dot(turned[...], right_ref[...], preferred_element_type=jnp.float32)
+        for z in range(shards):
+            for r in range(reps):
+                at = (z * reps + order[r]) * part
+                out_ref[r, z] = product[at : at + part].astype(jnp.bfloat16)
+
+    return pl.pallas_call(
+        body,
+        grid=(pl.cdiv(columns, TILE),),
+        out_shape=[jax.ShapeDtypeStruct((reps, shards, part, columns), jnp.bfloat16)],
+        in_specs=[
+            resident((count, rows)),
+            pl.BlockSpec((count, TILE), lambda i: (0, i)),
+        ],
+        out_specs=[pl.BlockSpec((reps, shards, part, TILE), lambda i: (0, 0, 0, i))],
+        scratch_shapes=[pltpu.VMEM((rows, count), jnp.bfloat16)],
+        compiler_params=pltpu.CompilerParams(vmem_limit_bytes=VMEM_LIMIT),
+        cost_estimate=COST,
+        name="ordered_gradient",
+    )(left, right)
 
 
 def rows_product(lefts, rights, turned, blocks):
@@ -659,18 +725,14 @@
     clock = Clock()
     z_order = jnp.stack([shard.behind(step) for step in range(shards)]).astype(jnp.int32)
 
-    def weight_piece(weight):
-        return pick(weight.reshape(reps, part_rows, weight.shape[1]), rep_place, 0)
-
-    def column_piece(weight):
-        return weight_piece(weight).reshape(part_rows, shards, block_units).transpose(1, 0, 2)
+    def weight_piece(weight, place):
+        return pick(weight.reshape(reps, part_rows, weight.shape[1]), place, 0)
+
+    def column_piece(weight, place):
+        return weight_piece(weight, place).reshape(part_rows, shards, block_units).transpose(1, 0, 2)
 
     def spread(piece):
         return Spread(clock, piece, core, first, second)
-
-    def flat_of(spread_pieces):
-        at, pieces = spread_pieces.finish()
-        return [at] + pieces
 
     def send_rows(rows):
         return [shard.shift(row, shards - step) for step, row in enumerate(rows, 1)]
@@ -680,23 +742,35 @@
             shard.shift(pick(blocks, shard.ahead(step), 0), step) for step in range(1, shards)
         ]
 
+    def together(*groups):
+        flat = clock(*[array for group in groups for array in group])
+        parts, at = [], 0
+        for group in groups:
+            parts.append(flat[at : at + len(group)])
+            at += len(group)
+        return parts
+
+    rep_index = lax.axis_index("rep")
+    input_matrix = lax.all_gather(
+        weight_piece(input_weight, rep_index), ("shard", "rep"), axis=0, tiled=True
+    )
     shard_vectors = jnp.concatenate([first_gain, second_gain, input_bias])
     vector_moving = gather_line(shard_vectors, shard)
-    input_moving = gather_line(weight_piece(input_weight), shard)
-    columns = [column_piece(gate_weight), column_piece(up_weight)]
-    output_piece = weight_piece(output_weight)
-    arrived = clock(*vector_moving, *input_moving, *columns, output_piece)
-    vectors, input_rows = arrived[:shards], arrived[shards : 2 * shards]
-    *columns, output_piece = arrived[2 * shards :]
-
-    input_spread = spread(jnp.stack(input_rows)[None])
+    output_piece = weight_piece(output_weight, rep_place)
+    vectors, (output_piece,) = together(vector_moving, [output_piece])
     output_moving = gather_line(output_piece, shard)
-    cotangent_arrived = [output_cotangent, shard.shift(output_cotangent, 1)]
     vector_rows = jnp.stack(in_place_order(vectors, shard))
     own_gain = first_gain.shape[0]
     gain_one = vector_rows[:, :own_gain].reshape(width).astype(f32)
     gain_two = vector_rows[:, own_gain : 2 * own_gain].reshape(width).astype(f32)
     shift_row = vector_rows[:, 2 * own_gain :].reshape(-1).astype(f32)
+    columns = jnp.stack(
+        [column_piece(gate_weight, rep_index), column_piece(up_weight, rep_index)], axis=1
+    )
+    output_rows, (columns,) = together(output_moving, [columns])
+    output_spread = spread(jnp.stack(output_rows)[None])
+    column_moving = place_sends(columns)
+
     places = positions(segments)
     cosine_table, sine_table = rope_tables(
         lax.dynamic_slice_in_dim(places, first_row, own_rows), HD
@@ -727,32 +801,19 @@
         key_marks,
         row_marks,
     ) = clock(normed_one, cosine_table, sine_table, signed_sine, key_marks, row_marks)
-
-    def together(*groups):
-        flat = clock(*[array for group in groups for array in group])
-        parts, at = [], 0
-        for group in groups:
-            parts.append(flat[at : at + len(group)])
-            at += len(group)
-        return parts
-
-    arrived, output_rows, (moved,) = together(
-        input_spread.waits(), output_moving, cotangent_arrived[1:]
-    )
-    cotangent_arrived[1] = moved
-    input_spread.further(*arrived)
-    output_spread = spread(jnp.stack(output_rows)[None])
-    gate_moving = place_sends(columns[0])
-    arrived, output_arrived, gate_rows = together(
-        input_spread.waits(), output_spread.waits(), gate_moving
-    )
-    input_spread.over(*arrived)
-    output_spread.further(*output_arrived)
-    input_places, input_pieces = input_spread.finish()
-    gate_spread = spread(jnp.stack(gate_rows)[None])
-    up_moving = place_sends(columns[1])
-    (input_matrix,) = clock.run(place_blocks, z_order, input_places, *input_pieces)
-    input_matrix = input_matrix.reshape(width, -1)
+    output_spread.further()
+    output_arrived, column_rows = together(output_spread.waits(), column_moving)
+    output_spread.over(*output_arrived)
+    gate_up = lax.all_gather(jnp.stack(column_rows)[None], "rep", axis=0, tiled=True)
+    (output_matrix,) = clock.run(place_blocks, z_order, *output_spread.finish())
+    output_matrix = output_matrix.reshape(width, width)
+
+    cotangent_arrived = [output_cotangent] + [None] * (shards - 1)
+    far = list(range(2, shards - 1))
+    near = sorted({1, shards - 1})
+    for step in far:
+        cotangent_arrived[step] = shard.shift(output_cotangent, step)
+    (input_matrix,) = clock(input_matrix)
     projected = jnp.dot(normed_one, input_matrix, preferred_element_type=f32) + shift_row
     key_part = rotate(
         projected[:, query_width : query_width + pair_width].reshape(own_rows, KVH, HD),
@@ -765,51 +826,27 @@
             axis=1,
         ).astype(bf16)
     )
-    pair_moving = gather_line(own_pairs, shard)
-    pair_rows, output_arrived, gate_arrived, up_rows = together(
-        pair_moving, output_spread.waits(), gate_spread.waits(), up_moving
-    )
+    pair_rows, moved = together(
+        gather_line(own_pairs, shard), [cotangent_arrived[step] for step in far]
+    )
+    for step, value in zip(far, moved):
+        cotangent_arrived[step] = value
     pairs = jnp.concatenate(pair_rows, axis=0)
-    output_spread.over(*output_arrived)
-    gate_spread.further(*gate_arrived)
-    up_spread = spread(jnp.stack(up_rows)[None])
-    last = shards - 1
-    cotangent_arrived += [None] * (shards - 2)
-    if last > 1:
-        cotangent_arrived[last] = shard.shift(output_cotangent, last)
+    for step in near:
+        cotangent_arrived[step] = shard.shift(output_cotangent, step)
     queries, attention_low = clock.run(
         attention_forward, projected, cosine_table, signed_sine, pairs, row_marks.T, key_marks
     )
-    output_places, output_pieces = output_spread.finish()
-    (output_matrix,) = clock.run(place_blocks, z_order, output_places, *output_pieces)
-    output_matrix = output_matrix.reshape(width, width)
     hidden = wide_tokens + jnp.dot(attention_low, output_matrix, preferred_element_type=f32)
     inverse_two = lax.rsqrt(jnp.mean(hidden * hidden, axis=-1, keepdims=True) + EPSILON)
     unit_two = hidden * inverse_two
     (normed_two,) = clock((unit_two * gain_two).astype(bf16))
-    normed_arrived = gather_line(normed_two, shard)
-    for step in range(2, last):
-        cotangent_arrived[step] = shard.shift(output_cotangent, step)
-    gate_arrived, up_arrived = together(gate_spread.waits(), up_spread.waits())
-    gate_spread.over(*gate_arrived)
-    up_spread.further(*up_arrived)
-    edge = [1] if last == 1 else [1, last]
-    up_arrived, normed_edge, (moved,) = together(
-        up_spread.waits(), [normed_arrived[step] for step in edge], [cotangent_arrived[last]]
-    )
-    up_spread.over(*up_arrived)
-    cotangent_arrived[last] = moved
-    for step, value in zip(edge, normed_edge):
-        normed_arrived[step] = value
-    gate_places, gate_pieces = gate_spread.finish()
-    (gate_matrix,) = clock.run(place_blocks, z_order, gate_places, *gate_pieces)
-    up_places, up_pieces = up_spread.finish()
-    (up_matrix,) = clock.run(place_blocks, z_order, up_places, *up_pieces)
+    normed_arrived, cotangent_arrived = together(gather_line(normed_two, shard), cotangent_arrived)
+    cotangents = jnp.concatenate(cotangent_arrived, axis=0)
+    group_normed = jnp.concatenate(normed_arrived, axis=0)
+    gate_matrix, up_matrix = clock.run(place_gathered, z_order, gate_up)
     gate_matrix = gate_matrix.reshape(width, block_units)
     up_matrix = up_matrix.reshape(width, block_units)
-    normed_arrived, cotangent_arrived = together(normed_arrived, cotangent_arrived)
-    cotangents = jnp.concatenate(cotangent_arrived, axis=0)
-    group_normed = jnp.concatenate(normed_arrived, axis=0)
 
     inner_act, d_gate, d_up = clock.run(
         feed_forward, group_normed, cotangents, gate_matrix, up_matrix, down_weight
@@ -822,11 +859,16 @@
         shape = (groups, first.size * second.size, -1, right.shape[1])
         return Halving(clock, sent.reshape(shape), own.reshape(shape), core, first, second)
 
-    def side_by_side(moving):
-        rows = clock(*moving)
+    def side_by_side(rows):
         return clock(jnp.concatenate(in_place_order(rows, shard), axis=1))[0]
 
-    down = start_halving(inner_act, cotangents, 1)
+    def sum_over_rep(blocks):
+        return lax.psum_scatter(blocks, "rep", scatter_dimension=0, tiled=True)
+
+    (down_blocks,) = clock.run(
+        lambda left, right: ordered_gradient(left, right, 1, list(range(reps))), inner_act, cotangents
+    )
+    down_piece = sum_over_rep(down_blocks.reshape(block_units, width))
     normed_own, *normed_partial = clock.run(
         lambda *operands: rows_product(operands[:2], operands[2:], True, shards),
         d_gate,
@@ -835,14 +877,14 @@
         up_matrix,
     )
     normed_arriving = send_rows(normed_partial)
-    down.along_first()
-    gate = start_halving(group_normed, d_gate, shards)
     up = start_halving(group_normed, d_up, shards)
-    gate.along_first()
-    down.along_second()
+    (gate_blocks,) = clock.run(
+        lambda left, right: ordered_gradient(left, right, shards, rep_places(reps)), group_normed, d_gate
+    )
     up.along_first()
-    gate.along_second()
-    down_spread = spread(down.finish()[0])
+    (down_piece,) = clock(down_piece)
+    gate_piece = sum_over_rep(gate_blocks.reshape(width, block_units))
+    up.along_second()
 
     normed_two_gradient = total_of([normed_own] + clock(*normed_arriving))
     gain_two_gradient = jnp.sum(normed_two_gradient * unit_two, axis=0)
@@ -862,13 +904,14 @@
         key_marks.T,
     )
     pair_arriving = send_rows(pair_partial)
-    up.along_second()
     output = start_halving(attention_low, branch_gradient, shards)
-    gate_moving = place_sends(gate.finish())
+    up_blocks = up.finish()
     output.along_first()
-    down_spread.further()
-    up_moving = place_sends(up.finish())
+    block_own, *block_partial = clock.run(
+        lambda left, right: rows_product((left,), (right,), False, shards), inner_act, down_weight
+    )
     pair_terms = [pair_own] + clock(*pair_arriving)
+    up_moving = place_sends(up_blocks)
     projected_gradient, bias_sum = clock.run(
         lambda *operands: join_projected(operands[0], operands[3:], *operands[1:3]),
         d_queries,
@@ -877,18 +920,11 @@
         *pair_terms,
     )
     projected = start_halving(normed_one, projected_gradient, shards)
-    gate_spread = spread(side_by_side(gate_moving))
+    output.along_second()
     projected.along_first()
-    block_own, *block_partial = clock.run(
-        lambda left, right: rows_product((left,), (right,), False, shards), inner_act, down_weight
-    )
-    output.along_second()
-    down_spread.over()
-    up_piece = side_by_side(up_moving)
-    block_arriving = send_rows(block_partial)
-    projected.along_second()
-    up_spread = spread(up_piece)
-    gate_spread.further()
+    up_rows = clock(*up_moving)
+    up_spread = spread(side_by_side(up_rows))
+    output_blocks = output.finish()
     projected_gradient, hidden_gradient = clock(projected_gradient, hidden_gradient)
     normed_one_gradient = times_transposed(projected_gradient, input_matrix)
     gain_one_gradient = jnp.sum(normed_one_gradient * unit_one, axis=0)
@@ -905,34 +941,42 @@
         bias_gradient[:bias_split],
         bias_gradient[bias_split:],
     )
-    (small_rows,) = clock(
+    (small,) = clock(
         jnp.concatenate([part.reshape(shards, -1) for part in small_parts], axis=1)
     )
-    small_moving = place_sends(small_rows)
-    output_moving = place_sends(output.finish())
-    projected_moving = place_sends(projected.finish())
+    projected.along_second()
+    up_spread.further()
+    output_moving = place_sends(output_blocks)
+    input_blocks = projected.finish()
+    output_sum = clock(total_of(clock(*output_moving)).astype(bf16))[0]
+    input_moving = place_sends(input_blocks)
+    up_spread.over()
+    input_sum = clock(total_of(clock(*input_moving)).astype(bf16))[0]
+    (gate_piece,) = clock(gate_piece)
+    down_spread = lax.all_gather(down_piece, "rep", axis=0, tiled=True)
+    gate_moving = place_sends(gate_piece.reshape(shards, part_rows, block_units))
+    (up_total,) = clock.run(widen_pieces, *up_spread.finish())
+    gate_rows = clock(*gate_moving)
+    gate_spread = spread(side_by_side(gate_rows))
+    output_spread = spread(output_sum)
+    output_spread.further()
+    block_arriving = send_rows(block_partial)
+    output_spread.over()
+    gate_spread.further()
+    input_spread = spread(input_sum)
+    (output_total,) = clock.run(widen_pieces, *output_spread.finish())
+    input_spread.further()
     gate_spread.over()
-    (down_total,) = clock.run(widen_pieces, *flat_of(down_spread))
-    small = total_of(clock(*small_moving))
-    small_moving = [core.shift(small, 1)]
-    output_spread = spread(clock(total_of(clock(*output_moving)).astype(bf16))[0])
-    input_spread = spread(clock(total_of(clock(*projected_moving)).astype(bf16))[0])
-    up_spread.further()
-    small = total_of([small] + clock(*small_moving))
-    small_moving = [first.shift(small, step) for step in range(1, first.size)]
-    (gate_total,) = clock.run(widen_pieces, *flat_of(gate_spread))
-    output_spread.further()
-    input_spread.further()
-    up_spread.over()
-    small = total_of([small] + clock(*small_moving))
-    small_moving = [second.shift(small, step) for step in range(1, second.size)]
+    input_spread.over()
     (block_out,) = clock(total_of([hidden, block_own] + clock(*block_arriving)).astype(bf16))
-    output_spread.over()
-    input_spread.over()
-    (up_total,) = clock.run(widen_pieces, *flat_of(up_spread))
-    small = total_of([small] + clock(*small_moving))
-    (output_total,) = clock.run(widen_pieces, *flat_of(output_spread))
-    (input_total,) = clock.run(widen_pieces, *flat_of(input_spread))
+    (input_total,) = clock.run(widen_pieces, *input_spread.finish())
+    for line in (core, first, second):
+        small = total_of(
+            [small] + clock(*[line.shift(small, step) for step in range(1, line.size)])
+        )
+    small = total_of(clock(*place_sends(small)))
+    (gate_total,) = clock.run(widen_pieces, *gate_spread.finish())
+    down_total = clock(down_spread)[0].astype(f32)
 
     small = small + clock.token[0, 0]
     small_totals, at = [], 0

time: 780 us -> 734 us (0.941)
  Pallas kernels: 232 us -> 189 us
  local copies, waits for them, and re-layouts: 66 us -> 42.4 us
  starting transfers between devices: 122 us -> 105 us
  other arithmetic: 29.6 us -> 42.9 us
  between operations: 2.9 us -> 15.4 us
  waiting for transfers between devices: 304 us -> 314 us
    pallas_call x15 -> x9, Pallas kernels: 76.3 us -> 47.8 us  [add_chosen(): pl.pallas_call(body, out_shape=jax.ShapeDtypeStruct((groups, slots, rows,...]
    reduce_scatter x0 -> x2, waiting for transfers between devices: none -> 27.8 us  [sum_over_rep(): return lax.psum_scatter(blocks, 'rep', scatter_dimension=0, tiled=True)]
    pallas_call x5 -> x3, Pallas kernels: 40.8 us -> 20.4 us  [split_gradient(): pl.pallas_call(body, grid=(pl.cdiv(columns, TILE),), out_shape=[jax.Shape...]
    ppermute x129 -> x74, waiting for transfers between devices: 304 us -> 286 us  [shift(): return lax.ppermute(value, self.name, self.pairs(step % self.size))]
    ppermute x129 -> x74, starting transfers between devices: 122 us -> 105 us  [shift(): return lax.ppermute(value, self.name, self.pairs(step % self.size))]
    unnamed x262 -> x120, local copies, waits for them, and re-layouts: 32.1 us -> 17.7 us
    another operation x1 -> x9, other arithmetic: 0.04 us -> 13.6 us  [the longest x6 9.69 us: over(): stacked, = self.clock(jnp.stack(list(self.here.values())))]
    pallas_call x4, Pallas kernels: 25.2 us -> 37.3 us  [the longest x2 20.8 us: ordered_gradient(): pl.pallas_call(body, grid=(pl.cdiv(columns, TILE),), out_shape=[jax.Shape...]
  transfers between devices with their start and end apart: 129 -> 79, of which waited for: 40 -> 30; matrix products, arithmetic and copies ran while one was open for 10% -> 11% of each run, Pallas kernels for 21% -> 20%
where the time goes in v5:
time: 734 us; the launch traced here: 725 us
  waiting for transfers between devices  314 us (43%)
  Pallas kernels  189 us (26%)
  starting transfers between devices  105 us (14%)
  other arithmetic  42.9 us (6%)
  local copies, waits for them, and re-layouts  42.4 us (6%)
  matrix products  16.9 us (2%)
  between operations  15.4 us (2%)
    ppermute x74, waiting for transfers between devices, shift(): return lax.ppermute(value, self.name, self.pairs(step % self.size))  286 us
    ppermute x74, starting transfers between devices, shift(): return lax.ppermute(value, self.name, self.pairs(step % self.size))  105 us
    pallas_call x9, Pallas kernels, add_chosen(): pl.pallas_call(body, out_shape=jax.ShapeDtypeStruct((groups, slots, rows,...  47.8 us
    reduce_scatter x2, waiting for transfers between devices, sum_over_rep(): return lax.psum_scatter(blocks, 'rep', scatter_dimension=0, tiled=True)  27.8 us
    pallas_call x2, Pallas kernels, rows_product(): pl.pallas_call(body, grid=(pl.cdiv(columns, TILE),), out_shape=[jax.Shape...  23.7 us
    pallas_call x1, Pallas kernels, feed_forward(): pl.pallas_call(body, grid=(pl.cdiv(units, TILE),), out_shape=[jax.ShapeDt...  22.4 us
    pallas_call x4, Pallas kernels, widen_pieces(): pl.pallas_call(body, out_shape=jax.ShapeDtypeStruct((reps, rows, columns)...  21.2 us
    pallas_call x2, Pallas kernels, ordered_gradient(): pl.pallas_call(body, grid=(pl.cdiv(columns, TILE),), out_shape=[jax.Shape...  20.8 us
  transfers between devices with their start and end apart: 79, of which 30 were waited for; matrix products, arithmetic and copies ran while one was open for 11% of the time, Pallas kernels for 20%

profile of v5, /device:TPU:0, one launch (start us, length us, event | category | flops | bytes accessed | tf_op | source)
XLA Modules:
  0.0 725.5 jit_solution(17622587500522513069)
XLA Ops:
  38.1 18.1 %collective-permute-done.4 = bf16[48,1536]{1,0:T(8,128)(2,1)S(1)} collective-permute-done((bf16[48,1536]{1,0:T(8,128)(2,1)S(1)}, bf16[48,1536]{1,0:T(8,128)(2,1)S(1)}, u32[]{:S(2)}, u32[]{:S(2)}) %collective-permute-start.4) | collective-permute-done | bytes 147488 | tf_op jit(solution)/shard_map/ppermute | solution.py:68
  61.4 14.2 %collective-permute-done.7.refs_2_ = bf16[1,4,48,1536]{3,2,1,0:T(8,128)(2,1)S(1)} collective-permute-done((bf16[1,4,48,1536]{3,2,1,0:T(8,128)(2,1)}, bf16[1,4,48,1536]{3,2,1,0:T(8,128)(2,1)S(1)}, u32[]{:S(2)}, u32[]{:S(2)}) %collective-permute-start.7) | collective-permute-done | bytes 589856 | tf_op jit(solution)/shard_map/ppermute | solution.py:68
  75.6 9.1 %collective-permute-done.6.refs_1_ = bf16[1,4,48,1536]{3,2,1,0:T(8,128)(2,1)} collective-permute-done((bf16[1,4,48,1536]{3,2,1,0:T(8,128)(2,1)}, bf16[1,4,48,1536]{3,2,1,0:T(8,128)(2,1)}, u32[]{:S(2)}, u32[]{:S(2)}) %collective-permute-start.6) | collective-permute-done | bytes 589856 | tf_op jit(solution)/shard_map/ppermute | solution.py:68
  92.5 11.1 %collective-permute-done.9 = bf16[2,48,2240]{2,1,0:T(8,128)(2,1)S(1)} collective-permute-done((bf16[2,48,2240]{2,1,0:T(8,128)(2,1)S(1)}, bf16[2,48,2240]{2,1,0:T(8,128)(2,1)S(1)}, u32[]{:S(2)}, u32[]{:S(2)}) %collective-permute-start.9) | collective-permute-done | bytes 430112 | tf_op jit(solution)/shard_map/ppermute | solution.py:68
  103.5 10.9 %collective-permute-done.10 = bf16[2,48,2240]{2,1,0:T(8,128)(2,1)S(1)} collective-permute-done((bf16[2,48,2240]{2,1,0:T(8,128)(2,1)S(1)}, bf16[2,48,2240]{2,1,0:T(8,128)(2,1)S(1)}, u32[]{:S(2)}, u32[]{:S(2)}) %collective-permute-start.10) | collective-permute-done | bytes 430112 | tf_op jit(solution)/shard_map/ppermute | solution.py:68
  137.9 11.2 %collective-permute-start.15 = (bf16[160,512]{1,0:T(8,128)(2,1)S(1)}, bf16[160,512]{1,0:T(8,128)(2,1)S(1)}, u32[]{:S(2)}, u32[]{:S(2)}) collective-permute-start(bf16[160,512]{1,0:T(8,128)(2,1)S(1)} %pad_maximum_fusion.8), channel_id=1, source_target_pairs={{0,3},{1,0},{2,1},{3,2},{4,7},{5,4},{6,5},{7,6},{8,11},{9,8},{10,9... | collective-permute-start | bytes 491528 | tf_op jit(solution)/shard_map/ppermute | solution.py:68
  154.0 9.9 %collective-permute-done.14 = bf16[160,512]{1,0:T(8,128)(2,1)S(1)} collective-permute-done((bf16[160,512]{1,0:T(8,128)(2,1)S(1)}, bf16[160,512]{1,0:T(8,128)(2,1)S(1)}, u32[]{:S(2)}, u32[]{:S(2)}) %collective-permute-start.14) | collective-permute-done | bytes 163872 | tf_op jit(solution)/shard_map/ppermute | solution.py:68
  177.3 11.6 %collective-permute-start.18 = (bf16[160,1536]{1,0:T(8,128)(2,1)S(1)}, bf16[160,1536]{1,0:T(8,128)(2,1)S(1)}, u32[]{:S(2)}, u32[]{:S(2)}) collective-permute-start(bf16[160,1536]{1,0:T(8,128)(2,1)S(1)} %multiply_convert_fusion), channel_id=1, source_target_pairs={{0,2},{1,3},{2,0},{3,1},{4,6},{5,7},{6,4},{7,5},{8,10},{9,11},{10,... | collective-permute-start | bytes 1474568 | tf_op jit(solution)/shard_map/ppermute | solution.py:68
  196.9 33.5 %collective-permute-done.18 = bf16[160,1536]{1,0:T(8,128)(2,1)S(1)} collective-permute-done((bf16[160,1536]{1,0:T(8,128)(2,1)S(1)}, bf16[160,1536]{1,0:T(8,128)(2,1)S(1)}, u32[]{:S(2)}, u32[]{:S(2)}) %collective-permute-start.18) | collective-permute-done | bytes 491552 | tf_op jit(solution)/shard_map/ppermute | solution.py:68
  236.0 11.7 %place_blocks.3 = (bf16[4,8,48,2240]{3,2,1,0:T(8,128)(2,1)}, bf16[4,8,48,2240]{3,2,1,0:T(8,128)(2,1)}) custom-call(s32[4]{0:T(128)} %pad_add_fusion.5.order_ref, bf16[8,4,2,48,2240]{4,3,2,1,0:T(8,128)(2,1)} %bitcast.176), custom_call_target="tpu_custom_call" | custom-call | flops 1 | bytes 1 | tf_op jit(solution)/shard_map/place_blocks/pallas_call | solution.py:326
  247.6 22.4 %feed_forward.1 = (bf16[640,2240]{1,0:T(8,128)(2,1)}, bf16[640,2240]{1,0:T(8,128)(2,1)}, bf16[640,2240]{1,0:T(8,128)(2,1)}) custom-call(bf16[640,1536]{1,0:T(8,128)(2,1)} %copy-done.2, bf16[640,1536]{1,0:T(8,128)(2,1)} %constant_dynamic-update-slice_fusion.8.cotangents_ref.right_ref, bf16[1536,2240]{1,0:T(8,128)(2,1)} %bitcast.162, ...), custom_call_target="tpu_custom_call" | custom-call | flops 1 | bytes 1 | tf_op jit(solution)/shard_map/feed_forward/pallas_call | solution.py:443
  270.0 10.1 %ordered_gradient.2 = bf16[8,1,280,1536]{3,2,1,0:T(8,128)(2,1)} custom-call(bf16[640,2240]{1,0:T(8,128)(2,1)} %get-tuple-element.550.left_ref.refs_0_, bf16[640,1536]{1,0:T(8,128)(2,1)} %constant_dynamic-update-slice_fusion.8.cotangents_ref.right_ref), custom_call_target="tpu_custom_call" | custom-call | flops 1 | bytes 1 | tf_op jit(solution)/shard_map/ordered_gradient/pallas_call | solution.py:515
  280.2 15.2 %rows_product.2 = (bf16[160,1536]{1,0:T(8,128)(2,1)}, bf16[160,1536]{1,0:T(8,128)(2,1)}, bf16[160,1536]{1,0:T(8,128)(2,1)}, bf16[160,1536]{1,0:T(8,128)(2,1)}) custom-call(bf16[640,2240]{1,0:T(8,128)(2,1)} %get-tuple-element.494.refs_0_.right_ref, bf16[640,2240]{1,0:T(8,128)(2,1)} %get-tuple-element.488.refs_1_.right_ref, bf16[1536,2240]{1,0:T(8,128)(2,1)} %bitcast.163, ...), custom_call_target="tpu_custom_call" | custom-call | flops 1 | bytes 1 | tf_op jit(solution)/shard_map/rows_product/pallas_call | solution.py:556
  295.4 10.5 %split_gradient.3 = (bf16[4,192,2240]{2,1,0:T(8,128)(2,1)}, bf16[4,192,2240]{2,1,0:T(8,128)(2,1)}) custom-call(s32[1]{0:T(128)} %bitcast.44.core_ref, bf16[640,1536]{1,0:T(8,128)(2,1)} %copy-done.2, bf16[640,2240]{1,0:T(8,128)(2,1)} %get-tuple-element.488.refs_1_.right_ref), custom_call_target="tpu_custom_call" | custom-call | flops 1 | bytes 1 | tf_op jit(solution)/shard_map/split_gradient/pallas_call | solution.py:481
  306.6 10.6 %ordered_gradient.3 = bf16[8,4,48,2240]{3,2,1,0:T(8,128)(2,1)} custom-call(bf16[640,1536]{1,0:T(8,128)(2,1)} %copy-done.2, bf16[640,2240]{1,0:T(8,128)(2,1)} %get-tuple-element.494.refs_0_.right_ref), custom_call_target="tpu_custom_call" | custom-call | flops 1 | bytes 1 | tf_op jit(solution)/shard_map/ordered_gradient/pallas_call | solution.py:515
  317.2 6.9 add_chosen.9
  329.6 27.8 %reduce-scatter.3.cloned.1.call-done = bf16[280,1536]{1,0:T(8,128)(2,1)} async-done(((bf16[2240,1536]{1,0:T(8,128)(2,1)}), bf16[280,1536]{1,0:T(8,128)(2,1)}) %reduce-scatter.3.cloned.1.call-update) | async-done | bytes 860176 | tf_op jit(solution)/shard_map/reduce_scatter | solution.py:866
  375.0 7.7 %attention_backward.1 = (bf16[160,1536]{1,0:T(8,128)(2,1)}, bf16[160,512]{1,0:T(8,128)(2,1)}, bf16[160,512]{1,0:T(8,128)(2,1)}, bf16[160,512]{1,0:T(8,128)(2,1)}, bf16[160,512]{1,0:T(8,128)(2,1)}) custom-call(bf16[2,960,128]{2,1,0:T(8,128)(2,1)} %get-tuple-element.521.queries_ref, bf16[160,1536]{1,0:T(8,128)(2,1)} %convolution_convert_fusion.gradient_ref, ...), custom_call_target="tpu_custom_call" | custom-call | flops 1 | bytes 1 | tf_op jit(solution)/shard_map/attention_backward/pallas_call | solution.py:658
  394.8 20.6 %collective-permute-done.27.refs_3_ = bf16[4,1,48,2240]{3,2,1,0:T(8,128)(2,1)S(1)} collective-permute-done((bf16[4,1,48,2240]{3,2,1,0:T(8,128)(2,1)S(1)}, bf16[4,1,48,2240]{3,2,1,0:T(8,128)(2,1)S(1)}, u32[]{:S(2)}, u32[]{:S(2)}) %collective-permute-start.27) | collective-permute-done | bytes 860192 | tf_op jit(solution)/shard_map/ppermute | solution.py:68
  427.8 8.5 %rows_product.3 = (bf16[160,1536]{1,0:T(8,128)(2,1)}, bf16[160,1536]{1,0:T(8,128)(2,1)}, bf16[160,1536]{1,0:T(8,128)(2,1)}, bf16[160,1536]{1,0:T(8,128)(2,1)}) custom-call(bf16[640,2240]{1,0:T(8,128)(2,1)} %get-tuple-element.550.left_ref.refs_0_, bf16[2240,1536]{1,0:T(8,128)(2,1)} %refs_1_), custom_call_target="tpu_custom_call" | custom-call | flops 1 | bytes 1 | tf_op jit(solution)/shard_map/rows_product/pallas_call | solution.py:556
  453.0 8.1 %collective-permute-done.32.refs_2_ = bf16[4,2,48,1536]{3,2,1,0:T(8,128)(2,1)S(1)} collective-permute-done((bf16[4,2,48,1536]{3,2,1,0:T(8,128)(2,1)}, bf16[4,2,48,1536]{3,2,1,0:T(8,128)(2,1)S(1)}, u32[]{:S(2)}, u32[]{:S(2)}) %collective-permute-start.32) | collective-permute-done | bytes 1179680 | tf_op jit(solution)/shard_map/ppermute | solution.py:68
  494.3 10.5 %collective-permute-done.38.refs_2_ = bf16[4,2,48,2048]{3,2,1,0:T(8,128)(2,1)} collective-permute-done((bf16[4,2,48,2048]{3,2,1,0:T(8,128)(2,1)}, bf16[4,2,48,2048]{3,2,1,0:T(8,128)(2,1)}, u32[]{:S(2)}, u32[]{:S(2)}) %collective-permute-start.38) | collective-permute-done | bytes 1572896 | tf_op jit(solution)/shard_map/ppermute | solution.py:68
  510.2 6.8 collective-permute-done.40.refs_2_
  544.2 13.4 %collective-permute-done.47 = bf16[48,2048]{1,0:T(8,128)(2,1)S(1)} collective-permute-done((bf16[48,2048]{1,0:T(8,128)(2,1)S(1)}, bf16[48,2048]{1,0:T(8,128)(2,1)S(1)}, u32[]{:S(2)}, u32[]{:S(2)}) %collective-permute-start.47) | collective-permute-done | bytes 196640 | tf_op jit(solution)/shard_map/ppermute | solution.py:68
  561.6 7.4 %widen_pieces.4 = f32[8,48,8960]{2,1,0:T(8,128)} custom-call(s32[8]{0:T(128)} %stack.299.places_ref, bf16[48,8960]{1,0:T(8,128)(2,1)} %copy-done.5, bf16[48,8960]{1,0:T(8,128)(2,1)} %collective-permute-done.39.refs_1_, bf16[48,8960]{1,0:T(8,128)(2,1)} %collective-permute-done.40.refs_2_, bf16[48,8960]{1,0:T(8,128)(2,1)} %copy-done.15, ...), custom_call_target="tpu_custom_call" | custom-call | flops 1 | bytes 1 | tf_op jit(solution)/shard_map/widen_pieces/pallas_call | solution.py:402
  569.0 10.5 %collective-permute-done.51 = bf16[48,2240]{1,0:T(8,128)(2,1)S(1)} collective-permute-done((bf16[48,2240]{1,0:T(8,128)(2,1)S(1)}, bf16[48,2240]{1,0:T(8,128)(2,1)S(1)}, u32[]{:S(2)}, u32[]{:S(2)}) %collective-permute-start.51) | collective-permute-done | bytes 215072 | tf_op jit(solution)/shard_map/ppermute | solution.py:68
  584.3 21.1 %collective-permute-done.54.refs_2_ = bf16[48,1536]{1,0:T(8,128)(2,1)S(1)} collective-permute-done((bf16[48,1536]{1,0:T(8,128)(2,1)S(1)}, bf16[48,1536]{1,0:T(8,128)(2,1)S(1)}, u32[]{:S(2)}, u32[]{:S(2)}) %collective-permute-start.54) | collective-permute-done | bytes 147488 | tf_op jit(solution)/shard_map/ppermute | solution.py:68
  617.2 10.5 %collective-permute-done.60.refs_2_ = bf16[48,2048]{1,0:T(8,128)(2,1)S(1)} collective-permute-done((bf16[48,2048]{1,0:T(8,128)(2,1)S(1)}, bf16[48,2048]{1,0:T(8,128)(2,1)S(1)}, u32[]{:S(2)}, u32[]{:S(2)}) %collective-permute-start.60) | collective-permute-done | bytes 196640 | tf_op jit(solution)/shard_map/ppermute | solution.py:68
  636.7 7.9 %collective-permute-done.63 = bf16[160,1536]{1,0:T(8,128)(2,1)S(1)} collective-permute-done((bf16[160,1536]{1,0:T(8,128)(2,1)S(1)}, bf16[160,1536]{1,0:T(8,128)(2,1)S(1)}, u32[]{:S(2)}, u32[]{:S(2)}) %collective-permute-start.63) | collective-permute-done | bytes 491552 | tf_op jit(solution)/shard_map/ppermute | solution.py:68
  644.5 32.3 %collective-permute-done.64 = bf16[160,1536]{1,0:T(8,128)(2,1)S(1)} collective-permute-done((bf16[160,1536]{1,0:T(8,128)(2,1)S(1)}, bf16[160,1536]{1,0:T(8,128)(2,1)S(1)}, u32[]{:S(2)}, u32[]{:S(2)}) %collective-permute-start.64) | collective-permute-done | bytes 491552 | tf_op jit(solution)/shard_map/ppermute | solution.py:68
  698.0 7.3 %widen_pieces.7 = f32[8,48,8960]{2,1,0:T(8,128)} custom-call(s32[8]{0:T(128)} %stack.299.places_ref, bf16[48,8960]{1,0:T(8,128)(2,1)} %copy-done.4, bf16[48,8960]{1,0:T(8,128)(2,1)} %copy-done.13, bf16[48,8960]{1,0:T(8,128)(2,1)} %copy-done.12, bf16[48,8960]{1,0:T(8,128)(2,1)} %copy-done.14, bf16[4,48,8960]{2,1,0:T(8,128)(2,1)} %copy-done.11), custom_call_target="tpu_custom_call" | custom-call | flops 1 | bytes 1 | tf_op jit(solution)/shard_map/widen_pieces/pallas_call | solution.py:402
  708.3 10.2 %convert_element_type.152 = f32[2240,1536]{1,0:T(8,128)} convert(bf16[2240,1536]{1,0:T(8,128)(2,1)} %all-gather.6.cloned.1.call-done) | non-fusion elementwise | flops 3440640 | bytes 20643840 | tf_op jit(solution)/shard_map/convert_element_type | solution.py:979
  (390 shorter events, 282.1 us)
Async XLA Ops:
  7.2 125.1 %all-gather.8.cloned.1.call-start = ((), (), s32[]{:S(2)}) async-start(), calls=%async_computation.5 | async-start | bytes 6488064 | tf_op jit(solution)/shard_map/all_gather | solution.py:754
  9.3 226.7 %all-gather.10.cloned.1.call-start = ((), (), s32[]{:S(2)}) async-start(), calls=%async_computation.6 | async-start | bytes 15925248 | tf_op jit(solution)/shard_map/all_gather | solution.py:807
  58.6 26.0 %collective-permute-start.6 = (bf16[1,4,48,1536]{3,2,1,0:T(8,128)(2,1)}, bf16[1,4,48,1536]{3,2,1,0:T(8,128)(2,1)}, u32[]{:S(2)}, u32[]{:S(2)}) collective-permute-start(bf16[1,4,48,1536]{3,2,1,0:T(8,128)(2,1)} %get-tuple-element.402.refs_0_), channel_id=1, source_target_pairs={{0,16},{4,12},{8,24},{12,4},{16,0},{20,28},{24,8},{28,20},{1,17},{... | collective-permute-start | bytes 1769480 | tf_op jit(solution)/shard_map/ppermute | solution.py:68
  84.7 29.8 %collective-permute-start.8 = (bf16[1,4,48,1536]{3,2,1,0:T(8,128)(2,1)}, bf16[1,4,48,1536]{3,2,1,0:T(8,128)(2,1)}, u32[]{:S(2)}, u32[]{:S(2)}) collective-permute-start(bf16[1,4,48,1536]{3,2,1,0:T(8,128)(2,1)} %collective-permute-done.6.refs_1_), channel_id=1, source_target_pairs={{0,8},{4,20},{8,0},{12,28},{16,24},{20,4},{24,16},{28,12},{1,9},{5... | collective-permute-start | bytes 1769480 | tf_op jit(solution)/shard_map/ppermute | solution.py:68
  115.9 241.5 %reduce-scatter.3.cloned.1.call-start = ((), (), s32[]{:S(2)}) async-start(), calls=%async_computation.2 | async-start | bytes 7741440 | tf_op jit(solution)/shard_map/reduce_scatter | solution.py:866
  119.4 34.6 %collective-permute-start.16 = (bf16[160,1536]{1,0:T(8,128)(2,1)}, bf16[160,1536]{1,0:T(8,128)(2,1)}, u32[]{:S(2)}, u32[]{:S(2)}) collective-permute-start(bf16[160,1536]{1,0:T(8,128)(2,1)} %param.21), channel_id=1, source_target_pairs={{0,2},{1,3},{2,0},{3,1},{4,6},{5,7},{6,4},{7,5},{8,10},{9,11},{10,... | collective-permute-start | bytes 1474568 | tf_op jit(solution)/shard_map/ppermute | solution.py:68
  149.8 41.3 %collective-permute-start.21 = (bf16[160,1536]{1,0:T(8,128)(2,1)}, bf16[160,1536]{1,0:T(8,128)(2,1)S(1)}, u32[]{:S(2)}, u32[]{:S(2)}) collective-permute-start(bf16[160,1536]{1,0:T(8,128)(2,1)} %param.21), channel_id=1, source_target_pairs={{0,3},{1,0},{2,1},{3,2},{4,7},{5,4},{6,5},{7,6},{8,11},{9,8},{10,9... | collective-permute-start | bytes 1474568 | tf_op jit(solution)/shard_map/ppermute | solution.py:68
  154.0 37.1 %collective-permute-start.20 = (bf16[160,1536]{1,0:T(8,128)(2,1)}, bf16[160,1536]{1,0:T(8,128)(2,1)S(1)}, u32[]{:S(2)}, u32[]{:S(2)}) collective-permute-start(bf16[160,1536]{1,0:T(8,128)(2,1)} %param.21), channel_id=1, source_target_pairs={{0,1},{1,2},{2,3},{3,0},{4,5},{5,6},{6,7},{7,4},{8,9},{9,10},{10,1... | collective-permute-start | bytes 1474568 | tf_op jit(solution)/shard_map/ppermute | solution.py:68
  177.3 53.1 %collective-permute-start.18 = (bf16[160,1536]{1,0:T(8,128)(2,1)S(1)}, bf16[160,1536]{1,0:T(8,128)(2,1)S(1)}, u32[]{:S(2)}, u32[]{:S(2)}) collective-permute-start(bf16[160,1536]{1,0:T(8,128)(2,1)S(1)} %multiply_convert_fusion), channel_id=1, source_target_pairs={{0,2},{1,3},{2,0},{3,1},{4,6},{5,7},{6,4},{7,5},{8,10},{9,11},{10,... | collective-permute-start | bytes 1474568 | tf_op jit(solution)/shard_map/ppermute | solution.py:68
  189.0 41.5 %collective-permute-start.17 = (bf16[160,1536]{1,0:T(8,128)(2,1)S(1)}, bf16[160,1536]{1,0:T(8,128)(2,1)S(1)}, u32[]{:S(2)}, u32[]{:S(2)}) collective-permute-start(bf16[160,1536]{1,0:T(8,128)(2,1)S(1)} %multiply_convert_fusion), channel_id=1, source_target_pairs={{0,1},{1,2},{2,3},{3,0},{4,5},{5,6},{6,7},{7,4},{8,9},{9,10},{10,1... | collective-permute-start | bytes 1474568 | tf_op jit(solution)/shard_map/ppermute | solution.py:68
  280.2 277.6 %reduce-scatter.5.cloned.1.call-start = ((), (), s32[]{:S(2)}) async-start(), calls=%async_computation.3 | async-start | bytes 7962624 | tf_op jit(solution)/shard_map/reduce_scatter | solution.py:866
  324.1 33.3 %collective-permute-start.23 = (bf16[4,2,48,2240]{3,2,1,0:T(8,128)(2,1)}, bf16[4,2,48,2240]{3,2,1,0:T(8,128)(2,1)}, u32[]{:S(2)}, u32[]{:S(2)}) collective-permute-start(bf16[4,2,48,2240]{3,2,1,0:T(8,128)(2,1)} %add_chosen.9), channel_id=1, source_target_pairs={{0,8},{4,20},{8,0},{12,28},{16,24},{20,4},{24,16},{28,12},{1,9},{5... | collective-permute-start | bytes 5160968 | tf_op jit(solution)/shard_map/ppermute | solution.py:68
  325.5 379.8 %all-gather.6.cloned.1.call-start = ((), (), s32[]{:S(2)}) async-start(), calls=%async_computation.4 | async-start | bytes 7741440 | tf_op jit(solution)/shard_map/all_gather | solution.py:956
  325.6 36.8 %collective-permute-start.24 = (bf16[160,1536]{1,0:T(8,128)(2,1)}, bf16[160,1536]{1,0:T(8,128)(2,1)S(1)}, u32[]{:S(2)}, u32[]{:S(2)}) collective-permute-start(bf16[160,1536]{1,0:T(8,128)(2,1)} %get-tuple-element.507), channel_id=1, source_target_pairs={{0,3},{1,0},{2,1},{3,2},{4,7},{5,4},{6,5},{7,6},{8,11},{9,8},{10,9... | collective-permute-start | bytes 1474568 | tf_op jit(solution)/shard_map/ppermute | solution.py:68
  325.7 42.5 %collective-permute-start.25 = (bf16[160,1536]{1,0:T(8,128)(2,1)}, bf16[160,1536]{1,0:T(8,128)(2,1)S(1)}, u32[]{:S(2)}, u32[]{:S(2)}) collective-permute-start(bf16[160,1536]{1,0:T(8,128)(2,1)} %get-tuple-element.508), channel_id=1, source_target_pairs={{0,2},{1,3},{2,0},{3,1},{4,6},{5,7},{6,4},{7,5},{8,10},{9,11},{10,... | collective-permute-start | bytes 1474568 | tf_op jit(solution)/shard_map/ppermute | solution.py:68
  325.7 42.4 %collective-permute-start.26 = (bf16[160,1536]{1,0:T(8,128)(2,1)}, bf16[160,1536]{1,0:T(8,128)(2,1)}, u32[]{:S(2)}, u32[]{:S(2)}) collective-permute-start(bf16[160,1536]{1,0:T(8,128)(2,1)} %get-tuple-element.509), channel_id=1, source_target_pairs={{0,1},{1,2},{2,3},{3,0},{4,5},{5,6},{6,7},{7,4},{8,9},{9,10},{10,1... | collective-permute-start | bytes 1474568 | tf_op jit(solution)/shard_map/ppermute | solution.py:68
  387.4 34.1 %collective-permute-start.28 = (bf16[4,4,48,1536]{3,2,1,0:T(8,128)(2,1)}, bf16[4,4,48,1536]{3,2,1,0:T(8,128)(2,1)}, u32[]{:S(2)}, u32[]{:S(2)}) collective-permute-start(bf16[4,4,48,1536]{3,2,1,0:T(8,128)(2,1)} %bitcast.224), channel_id=1, source_target_pairs={{0,4},{4,0},{8,12},{12,8},{16,20},{20,16},{24,28},{28,24},{1,5},{5... | collective-permute-start | bytes 7077896 | tf_op jit(solution)/shard_map/ppermute | solution.py:68
  387.4 28.1 %collective-permute-start.27 = (bf16[4,1,48,2240]{3,2,1,0:T(8,128)(2,1)S(1)}, bf16[4,1,48,2240]{3,2,1,0:T(8,128)(2,1)S(1)}, u32[]{:S(2)}, u32[]{:S(2)}) collective-permute-start(bf16[4,1,48,2240]{3,2,1,0:T(8,128)(2,1)S(1)} %copy-done.26), channel_id=1, source_target_pairs={{0,16},{4,12},{8,24},{12,4},{16,0},{20,28},{24,8},{28,20},{1,17},{... | collective-permute-start | bytes 2580488 | tf_op jit(solution)/shard_map/ppermute | solution.py:68
  388.2 48.1 %collective-permute-start.29 = (bf16[160,512]{1,0:T(8,128)(2,1)}, bf16[160,512]{1,0:T(8,128)(2,1)S(1)}, u32[]{:S(2)}, u32[]{:S(2)}) collective-permute-start(bf16[160,512]{1,0:T(8,128)(2,1)} %get-tuple-element.557), channel_id=1, source_target_pairs={{0,3},{1,0},{2,1},{3,2},{4,7},{5,4},{6,5},{7,6},{8,11},{9,8},{10,9... | collective-permute-start | bytes 491528 | tf_op jit(solution)/shard_map/ppermute | solution.py:68
  388.2 48.1 %collective-permute-start.30 = (bf16[160,512]{1,0:T(8,128)(2,1)}, bf16[160,512]{1,0:T(8,128)(2,1)}, u32[]{:S(2)}, u32[]{:S(2)}) collective-permute-start(bf16[160,512]{1,0:T(8,128)(2,1)} %get-tuple-element.558), channel_id=1, source_target_pairs={{0,2},{1,3},{2,0},{3,1},{4,6},{5,7},{6,4},{7,5},{8,10},{9,11},{10,... | collective-permute-start | bytes 491528 | tf_op jit(solution)/shard_map/ppermute | solution.py:68
  392.1 44.3 %collective-permute-start.31 = (bf16[160,512]{1,0:T(8,128)(2,1)}, bf16[160,512]{1,0:T(8,128)(2,1)}, u32[]{:S(2)}, u32[]{:S(2)}) collective-permute-start(bf16[160,512]{1,0:T(8,128)(2,1)} %get-tuple-element.559), channel_id=1, source_target_pairs={{0,1},{1,2},{2,3},{3,0},{4,5},{5,6},{6,7},{7,4},{8,9},{9,10},{10,1... | collective-permute-start | bytes 491528 | tf_op jit(solution)/shard_map/ppermute | solution.py:68
  448.1 26.0 %collective-permute-start.35 = (bf16[48,2240]{1,0:T(8,128)(2,1)}, bf16[48,2240]{1,0:T(8,128)(2,1)S(1)}, u32[]{:S(2)}, u32[]{:S(2)}) collective-permute-start(bf16[48,2240]{1,0:T(8,128)(2,1)} %get-tuple-element.770), channel_id=1, source_target_pairs={{0,2},{1,3},{2,0},{3,1},{4,6},{5,7},{6,4},{7,5},{8,10},{9,11},{10,... | collective-permute-start | bytes 645128 | tf_op jit(solution)/shard_map/ppermute | solution.py:68
  474.8 29.9 %collective-permute-start.38 = (bf16[4,2,48,2048]{3,2,1,0:T(8,128)(2,1)}, bf16[4,2,48,2048]{3,2,1,0:T(8,128)(2,1)}, u32[]{:S(2)}, u32[]{:S(2)}) collective-permute-start(bf16[4,2,48,2048]{3,2,1,0:T(8,128)(2,1)} %add_chosen.14), channel_id=1, source_target_pairs={{0,8},{4,20},{8,0},{12,28},{16,24},{20,4},{24,16},{28,12},{1,9},{5... | collective-permute-start | bytes 4718600 | tf_op jit(solution)/shard_map/ppermute | solution.py:68
  479.0 38.1 %collective-permute-start.40 = (bf16[48,8960]{1,0:T(8,128)(2,1)S(1)}, bf16[48,8960]{1,0:T(8,128)(2,1)}, u32[]{:S(2)}, u32[]{:S(2)}) collective-permute-start(bf16[48,8960]{1,0:T(8,128)(2,1)S(1)} %concatenate.50.refs_0_), channel_id=1, source_target_pairs={{0,8},{4,20},{8,0},{12,28},{16,24},{20,4},{24,16},{28,12},{1,9},{5... | collective-permute-start | bytes 2580488 | tf_op jit(solution)/shard_map/ppermute | solution.py:68
  480.2 36.8 %collective-permute-start.39 = (bf16[48,8960]{1,0:T(8,128)(2,1)S(1)}, bf16[48,8960]{1,0:T(8,128)(2,1)}, u32[]{:S(2)}, u32[]{:S(2)}) collective-permute-start(bf16[48,8960]{1,0:T(8,128)(2,1)S(1)} %concatenate.50.refs_0_), channel_id=1, source_target_pairs={{0,16},{4,12},{8,24},{12,4},{16,0},{20,28},{24,8},{28,20},{1,17},{... | collective-permute-start | bytes 2580488 | tf_op jit(solution)/shard_map/ppermute | solution.py:68
  580.2 30.5 %collective-permute-start.57 = (bf16[48,8960]{1,0:T(8,128)(2,1)S(1)}, bf16[48,8960]{1,0:T(8,128)(2,1)S(1)}, u32[]{:S(2)}, u32[]{:S(2)}) collective-permute-start(bf16[48,8960]{1,0:T(8,128)(2,1)S(1)} %concatenate.52.refs_0_), channel_id=1, source_target_pairs={{0,8},{4,20},{8,0},{12,28},{16,24},{20,4},{24,16},{28,12},{1,9},{5... | collective-permute-start | bytes 2580488 | tf_op jit(solution)/shard_map/ppermute | solution.py:68
  581.3 29.4 %collective-permute-start.56 = (bf16[48,8960]{1,0:T(8,128)(2,1)S(1)}, bf16[48,8960]{1,0:T(8,128)(2,1)S(1)}, u32[]{:S(2)}, u32[]{:S(2)}) collective-permute-start(bf16[48,8960]{1,0:T(8,128)(2,1)S(1)} %concatenate.52.refs_0_), channel_id=1, source_target_pairs={{0,16},{4,12},{8,24},{12,4},{16,0},{20,28},{24,8},{28,20},{1,17},{... | collective-permute-start | bytes 2580488 | tf_op jit(solution)/shard_map/ppermute | solution.py:68
  630.7 65.5 %collective-permute-start.73 = (bf16[4,48,8960]{2,1,0:T(8,128)(2,1)}, bf16[4,48,8960]{2,1,0:T(8,128)(2,1)S(1)}, u32[]{:S(2)}, u32[]{:S(2)}) collective-permute-start(bf16[4,48,8960]{2,1,0:T(8,128)(2,1)} %pad_maximum_fusion.1), channel_id=1, source_target_pairs={{0,4},{4,0},{8,12},{12,8},{16,20},{20,16},{24,28},{28,24},{1,5},{5... | collective-permute-start | bytes 10321928 | tf_op jit(solution)/shard_map/ppermute | solution.py:68
  631.1 45.8 %collective-permute-start.64 = (bf16[160,1536]{1,0:T(8,128)(2,1)S(1)}, bf16[160,1536]{1,0:T(8,128)(2,1)S(1)}, u32[]{:S(2)}, u32[]{:S(2)}) collective-permute-start(bf16[160,1536]{1,0:T(8,128)(2,1)S(1)} %copy-done.48), channel_id=1, source_target_pairs={{0,2},{1,3},{2,0},{3,1},{4,6},{5,7},{6,4},{7,5},{8,10},{9,11},{10,... | collective-permute-start | bytes 1474568 | tf_op jit(solution)/shard_map/ppermute | solution.py:68
  633.6 43.3 %collective-permute-start.65 = (bf16[160,1536]{1,0:T(8,128)(2,1)S(1)}, bf16[160,1536]{1,0:T(8,128)(2,1)S(1)}, u32[]{:S(2)}, u32[]{:S(2)}) collective-permute-start(bf16[160,1536]{1,0:T(8,128)(2,1)S(1)} %copy-done.47), channel_id=1, source_target_pairs={{0,1},{1,2},{2,3},{3,0},{4,5},{5,6},{6,7},{7,4},{8,9},{9,10},{10,1... | collective-permute-start | bytes 1474568 | tf_op jit(solution)/shard_map/ppermute | solution.py:68
  636.6 41.4 %collective-permute-start.66 = (bf16[4,48,2048]{2,1,0:T(8,128)(2,1)S(1)}, bf16[4,48,2048]{2,1,0:T(8,128)(2,1)S(1)}, u32[]{:S(2)}, u32[]{:S(2)}) collective-permute-start(bf16[4,48,2048]{2,1,0:T(8,128)(2,1)S(1)} %pad_maximum_fusion.5), channel_id=1, source_target_pairs={{0,4},{4,0},{8,12},{12,8},{16,20},{20,16},{24,28},{28,24},{1,5},{5... | collective-permute-start | bytes 2359304 | tf_op jit(solution)/shard_map/ppermute | solution.py:68
  644.5 37.8 %collective-permute-start.67 = (f32[4,1280]{1,0:T(4,128)S(1)}, f32[4,1280]{1,0:T(4,128)S(1)}, u32[]{:S(2)}, u32[]{:S(2)}) collective-permute-start(f32[4,1280]{1,0:T(4,128)S(1)} %concatenate.51), channel_id=1, source_target_pairs={{0,4},{4,0},{8,12},{12,8},{16,20},{20,16},{24,28},{28,24},{1,5},{5... | collective-permute-start | bytes 61448 | tf_op jit(solution)/shard_map/ppermute | solution.py:68
  (99 other events, 1852.1 us)
Sparse Core Ops, SparseCore 0:
  11.5 89.8 all-gather.7
  116.0 89.8 all-gather.9
  280.3 77.0 reduce-scatter.2
  361.7 71.0 reduce-scatter.4
  522.8 47.6 all-gather.5

commit v6 on v5

--- a/solution.py
+++ b/solution.py
@@ -71,7 +71,7 @@
         return lax.rem(self.place + (self.size - step % self.size), self.size)
 
     def ahead(self, step):
-        return lax.rem(self.place + step % self.size, self.size)
+        return lax.rem(self.place + step % self.size, self.size) if step else self.place
 
 
 def make_lines(reps, shards):
@@ -182,74 +182,32 @@
     return total
 
 
-def add_chosen(chosen, *terms):
-    count = len(terms)
-    groups, places, rows, columns = terms[0].shape
-    chosen = jnp.stack([jnp.stack(line) for line in chosen]).astype(jnp.int32)
-    slots = chosen.shape[1]
-
-    def body(chosen_ref, *refs):
-        refs[count][...] = total_of([ref[...] for ref in refs[:count]]).astype(jnp.bfloat16)
-
-    return pl.pallas_call(
-        body,
-        out_shape=jax.ShapeDtypeStruct((groups, slots, rows, columns), jnp.bfloat16),
-        grid_spec=pltpu.PrefetchScalarGridSpec(
-            num_scalar_prefetch=1,
-            grid=(groups, slots),
-            in_specs=[
-                pl.BlockSpec(
-                    (1, 1, rows, columns), lambda z, j, at, t=t: (z, at[t, j], 0, 0)
-                )
-                for t in range(count)
-            ],
-            out_specs=pl.BlockSpec((1, 1, rows, columns), lambda z, j, at: (z, j, 0, 0)),
-        ),
-        compiler_params=pltpu.CompilerParams(vmem_limit_bytes=VMEM_LIMIT),
-        cost_estimate=COST,
-        name="add_chosen",
-    )(chosen, *terms)
-
-
 class Halving:
     def __init__(self, clock, sent, own, core, first, second):
         self.clock, self.first, self.second = clock, first, second
-        self.own = own
+        self.terms = [own]
         self.moving = [core.shift(sent, 1)]
 
-    def chosen(self, one, two):
-        return one * self.second.size + two
+    def along(self, line):
+        self.terms = self.terms + self.clock(*self.moving)
+        blocks = [
+            total_of([pick(term, line.ahead(step), 1) for term in self.terms]).astype(jnp.bfloat16)
+            for step in range(1, line.size)
+        ]
+        self.moving = [
+            line.shift(block, step) for step, block in enumerate(self.clock(*blocks), 1)
+        ]
+        self.terms = [pick(term, line.place, 1) for term in self.terms]
 
     def along_first(self):
-        (arrived,) = self.clock(*self.moving)
-        self.halves = [self.own, arrived]
-        self.moving = []
-        for step in range(1, self.first.size):
-            one = self.first.ahead(step)
-            slots = [self.chosen(one, two) for two in range(self.second.size)]
-            (block,) = self.clock(add_chosen([slots] * 2, *self.halves))
-            self.moving.append(self.first.shift(block, step))
+        self.along(self.first)
 
     def along_second(self):
-        self.quarters = self.clock(*self.moving)
-        self.moving = []
-        for step in range(1, self.second.size):
-            two = self.second.ahead(step)
-            slots = [[self.chosen(self.first.place, two)]] * 2 + [[two]] * len(self.quarters)
-            (block,) = self.clock(add_chosen(slots, *self.halves, *self.quarters))
-            self.moving.append(self.second.shift(block, step))
+        self.along(self.second)
 
     def finish(self):
-        eighths = self.clock(*self.moving)
-        two = self.second.place
-        zero = jnp.zeros((), jnp.int32)
-        slots = (
-            [[self.chosen(self.first.place, two)]] * 2
-            + [[two]] * len(self.quarters)
-            + [[zero]] * len(eighths)
-        )
-        (block,) = self.clock(add_chosen(slots, *self.halves, *self.quarters, *eighths))
-        return block[:, 0]
+        self.terms = self.terms + self.clock(*self.moving)
+        return self.clock(total_of(self.terms).astype(jnp.bfloat16))[0]
 
 
 class Spread:
@@ -425,25 +383,50 @@
 def feed_forward(rows, cotangents, gate_matrix, up_matrix, down_matrix):
     count, width = rows.shape
     units = gate_matrix.shape[1]
-
-    def body(rows_ref, cotangents_ref, gate_ref, up_ref, down_ref, inner_ref, d_gate_ref, d_up_ref):
+    steps = pl.cdiv(units, TILE)
+    slabs = next(size for size in range(min(steps, width // 128), 0, -1) if width % (128 * size) == 0)
+    slab = width // slabs
+
+    def body(
+        rows_ref,
+        cotangents_ref,
+        gate_ref,
+        up_ref,
+        down_ref,
+        inner_ref,
+        d_gate_ref,
+        d_up_ref,
+        turned_rows_ref,
+        turned_inner_ref,
+    ):
         gate = jnp.dot(rows_ref[...], gate_ref[...], preferred_element_type=jnp.float32)
         up = jnp.dot(rows_ref[...], up_ref[...], preferred_element_type=jnp.float32)
         sigmoid = jax.nn.sigmoid(gate)
         silu = gate * sigmoid
-        inner_ref[...] = (silu * up).astype(jnp.bfloat16)
+        inner = (silu * up).astype(jnp.bfloat16)
+        inner_ref[...] = inner
+        turned_inner_ref[...] = inner.T
         d_inner = times_transposed(cotangents_ref[...], down_ref[...])
         d_up_ref[...] = (d_inner * silu).astype(jnp.bfloat16)
         d_gate_ref[...] = (d_inner * up * sigmoid * (1.0 + gate * (1.0 - sigmoid))).astype(
             jnp.bfloat16
         )
+        for step in range(slabs):
+
+            @pl.when(pl.program_id(0) == step)
+            def turn():
+                turned_rows_ref[...] = rows_ref[:, step * slab : (step + 1) * slab].T
 
     columns = pl.BlockSpec((width, TILE), lambda i: (0, i))
     results = pl.BlockSpec((count, TILE), lambda i: (0, i))
     return pl.pallas_call(
         body,
-        grid=(pl.cdiv(units, TILE),),
-        out_shape=[jax.ShapeDtypeStruct((count, units), jnp.bfloat16)] * 3,
+        grid=(steps,),
+        out_shape=[jax.ShapeDtypeStruct((count, units), jnp.bfloat16)] * 3
+        + [
+            jax.ShapeDtypeStruct((width, count), jnp.bfloat16),
+            jax.ShapeDtypeStruct((units, count), jnp.bfloat16),
+        ],
         in_specs=[
             resident((count, width)),
             resident((count, width)),
@@ -451,7 +434,11 @@
             columns,
             pl.BlockSpec((TILE, width), lambda i: (i, 0)),
         ],
-        out_specs=[results] * 3,
+        out_specs=[results] * 3
+        + [
+            pl.BlockSpec((slab, count), lambda i: (jnp.minimum(i, slabs - 1), 0)),
+            pl.BlockSpec((TILE, count), lambda i: (i, 0)),
+        ],
         compiler_params=pltpu.CompilerParams(vmem_limit_bytes=VMEM_LIMIT),
         cost_estimate=COST,
         name="feed_forward",
@@ -459,22 +446,20 @@
 
 
 def split_gradient(left, right, groups, core_place):
-    count, rows = left.shape
+    rows, count = left.shape
     columns = right.shape[1]
     half = rows // (2 * groups)
 
-    def body(core_ref, left_ref, right_ref, other_ref, own_ref, turned):
-        @pl.when(pl.program_id(0) == 0)
-        def turn():
-            whole = left_ref[...].T
-            for group in range(groups):
-                for which in range(2):
-                    at = (2 * group + which) * half
-                    turned[which, group * half : (group + 1) * half, :] = whole[at : at + half]
-
+    def body(core_ref, left_ref, right_ref, other_ref, own_ref):
         core = core_ref[0]
         for out_ref, which in ((other_ref, 1 - core), (own_ref, core)):
-            product = jnp.dot(turned[which], right_ref[...], preferred_element_type=jnp.float32)
+            halves = [
+                left_ref[pl.ds(pl.multiple_of((2 * group + which) * half, 16), half), :]
+                for group in range(groups)
+            ]
+            product = jnp.dot(
+                jnp.concatenate(halves, axis=0), right_ref[...], preferred_element_type=jnp.float32
+            )
             for group in range(groups):
                 out_ref[group] = product[group * half : (group + 1) * half].astype(jnp.bfloat16)
 
@@ -484,11 +469,10 @@
         out_shape=[jax.ShapeDtypeStruct((groups, half, columns), jnp.bfloat16)] * 2,
         in_specs=[
             pl.BlockSpec(memory_space=pltpu.SMEM),
-            resident((count, rows)),
+            resident((rows, count)),
             pl.BlockSpec((count, TILE), lambda i: (0, i)),
         ],
         out_specs=[pl.BlockSpec((groups, half, TILE), lambda i: (0, 0, i))] * 2,
-        scratch_shapes=[pltpu.VMEM((2, rows // 2, count), jnp.bfloat16)],
         compiler_params=pltpu.CompilerParams(vmem_limit_bytes=VMEM_LIMIT),
         cost_estimate=COST,
         name="split_gradient",
@@ -497,16 +481,12 @@
 
 def ordered_gradient(left, right, shards, order):
     reps = len(order)
-    count, rows = left.shape
+    rows, count = left.shape
     columns = right.shape[1]
     part = rows // (shards * reps)
 
-    def body(left_ref, right_ref, out_ref, turned):
-        @pl.when(pl.program_id(0) == 0)
-        def turn():
-            turned[...] = left_ref[...].T
-
-        product = jnp.dot(turned[...], right_ref[...], preferred_element_type=jnp.float32)
+    def body(left_ref, right_ref, out_ref):
+        product = jnp.dot(left_ref[...], right_ref[...], preferred_element_type=jnp.float32)
         for z in range(shards):
             for r in range(reps):
                 at = (z * reps + order[r]) * part
@@ -517,11 +497,10 @@
         grid=(pl.cdiv(columns, TILE),),
         out_shape=[jax.ShapeDtypeStruct((reps, shards, part, columns), jnp.bfloat16)],
         in_specs=[
-            resident((count, rows)),
+            resident((rows, count)),
             pl.BlockSpec((count, TILE), lambda i: (0, i)),
         ],
         out_specs=[pl.BlockSpec((reps, shards, part, TILE), lambda i: (0, 0, 0, i))],
-        scratch_shapes=[pltpu.VMEM((rows, count), jnp.bfloat16)],
         compiler_params=pltpu.CompilerParams(vmem_limit_bytes=VMEM_LIMIT),
         cost_estimate=COST,
         name="ordered_gradient",
@@ -737,10 +716,11 @@
     def send_rows(rows):
         return [shard.shift(row, shards - step) for step, row in enumerate(rows, 1)]
 
-    def place_sends(blocks):
-        return [pick(blocks, shard.place, 0)] + [
-            shard.shift(pick(blocks, shard.ahead(step), 0), step) for step in range(1, shards)
-        ]
+    def sends_of(blocks):
+        return [pick(blocks, shard.ahead(step), 0) for step in range(shards)]
+
+    def shift_blocks(blocks):
+        return [blocks[0]] + [shard.shift(block, step) for step, block in enumerate(blocks[1:], 1)]
 
     def together(*groups):
         flat = clock(*[array for group in groups for array in group])
@@ -751,25 +731,27 @@
         return parts
 
     rep_index = lax.axis_index("rep")
-    input_matrix = lax.all_gather(
-        weight_piece(input_weight, rep_index), ("shard", "rep"), axis=0, tiled=True
-    )
     shard_vectors = jnp.concatenate([first_gain, second_gain, input_bias])
-    vector_moving = gather_line(shard_vectors, shard)
-    output_piece = weight_piece(output_weight, rep_place)
-    vectors, (output_piece,) = together(vector_moving, [output_piece])
-    output_moving = gather_line(output_piece, shard)
-    vector_rows = jnp.stack(in_place_order(vectors, shard))
+    vector_row = jnp.pad(shard_vectors, (0, input_weight.shape[1] - shard_vectors.shape[0]))
+    input_moving = gather_line(
+        jnp.concatenate([weight_piece(input_weight, rep_place), vector_row[None]], axis=0), shard
+    )
+    output_piece = weight_piece(output_weight, rep_index)
+    gate_blocks = sends_of(column_piece(gate_weight, rep_index))
+    up_blocks = sends_of(column_piece(up_weight, rep_place))
+    input_rows, gate_blocks, up_blocks, (output_piece,) = together(
+        input_moving, gate_blocks, up_blocks, [output_piece]
+    )
+    input_spread = spread(jnp.stack([rows[:part_rows] for rows in input_rows])[None])
+    output_matrix = lax.all_gather(output_piece, ("shard", "rep"), axis=0, tiled=True)
+    gate_moving = shift_blocks(gate_blocks)
+    vector_rows = jnp.stack(in_place_order([rows[part_rows] for rows in input_rows], shard))
     own_gain = first_gain.shape[0]
     gain_one = vector_rows[:, :own_gain].reshape(width).astype(f32)
     gain_two = vector_rows[:, own_gain : 2 * own_gain].reshape(width).astype(f32)
-    shift_row = vector_rows[:, 2 * own_gain :].reshape(-1).astype(f32)
-    columns = jnp.stack(
-        [column_piece(gate_weight, rep_index), column_piece(up_weight, rep_index)], axis=1
-    )
-    output_rows, (columns,) = together(output_moving, [columns])
-    output_spread = spread(jnp.stack(output_rows)[None])
-    column_moving = place_sends(columns)
+    shift_row = (
+        vector_rows[:, 2 * own_gain : shard_vectors.shape[0]].reshape(-1).astype(f32)
+    )
 
     places = positions(segments)
     cosine_table, sine_table = rope_tables(
@@ -801,19 +783,18 @@
         key_marks,
         row_marks,
     ) = clock(normed_one, cosine_table, sine_table, signed_sine, key_marks, row_marks)
-    output_spread.further()
-    output_arrived, column_rows = together(output_spread.waits(), column_moving)
-    output_spread.over(*output_arrived)
-    gate_up = lax.all_gather(jnp.stack(column_rows)[None], "rep", axis=0, tiled=True)
-    (output_matrix,) = clock.run(place_blocks, z_order, *output_spread.finish())
-    output_matrix = output_matrix.reshape(width, width)
-
-    cotangent_arrived = [output_cotangent] + [None] * (shards - 1)
+
     far = list(range(2, shards - 1))
-    near = sorted({1, shards - 1})
-    for step in far:
-        cotangent_arrived[step] = shard.shift(output_cotangent, step)
-    (input_matrix,) = clock(input_matrix)
+    cotangent_arrived = [output_cotangent, shard.shift(output_cotangent, 1)] + [None] * (shards - 2)
+    input_spread.further()
+    input_arrived, gate_rows, (cotangent_arrived[1],) = together(
+        input_spread.waits(), gate_moving, cotangent_arrived[1:2]
+    )
+    input_spread.over(*input_arrived)
+    gate_gathered = lax.all_gather(jnp.stack(gate_rows)[None, :, None], "rep", axis=0, tiled=True)
+    up_moving = shift_blocks(up_blocks)
+    (input_matrix,) = clock.run(place_blocks, z_order, *input_spread.finish())
+    input_matrix = input_matrix.reshape(width, -1)
     projected = jnp.dot(normed_one, input_matrix, preferred_element_type=f32) + shift_row
     key_part = rotate(
         projected[:, query_width : query_width + pair_width].reshape(own_rows, KVH, HD),
@@ -826,29 +807,36 @@
             axis=1,
         ).astype(bf16)
     )
-    pair_rows, moved = together(
-        gather_line(own_pairs, shard), [cotangent_arrived[step] for step in far]
-    )
-    for step, value in zip(far, moved):
-        cotangent_arrived[step] = value
+    up_rows = clock(*up_moving)
+    pair_moving = gather_line(own_pairs, shard)
+    up_spread = spread(jnp.stack(up_rows)[None])
+    pair_rows, up_arrived = together(pair_moving, up_spread.waits())
     pairs = jnp.concatenate(pair_rows, axis=0)
-    for step in near:
+    up_spread.further(*up_arrived)
+    for step in far:
         cotangent_arrived[step] = shard.shift(output_cotangent, step)
     queries, attention_low = clock.run(
         attention_forward, projected, cosine_table, signed_sine, pairs, row_marks.T, key_marks
     )
+    output_matrix, attention_low = clock(output_matrix, attention_low)
     hidden = wide_tokens + jnp.dot(attention_low, output_matrix, preferred_element_type=f32)
     inverse_two = lax.rsqrt(jnp.mean(hidden * hidden, axis=-1, keepdims=True) + EPSILON)
     unit_two = hidden * inverse_two
     (normed_two,) = clock((unit_two * gain_two).astype(bf16))
-    normed_arrived, cotangent_arrived = together(gather_line(normed_two, shard), cotangent_arrived)
+    normed_moving = gather_line(normed_two, shard)
+    up_spread.over()
+    up_arrived = clock(*up_spread.waits())
+    if shards > 2:
+        cotangent_arrived[-1] = shard.shift(output_cotangent, shards - 1)
+    (up_matrix,) = clock.run(place_blocks, z_order, *up_spread.finish(*up_arrived))
+    up_matrix = up_matrix.reshape(width, block_units)
+    (gate_matrix,) = clock.run(place_gathered, z_order, gate_gathered)
+    gate_matrix = gate_matrix.reshape(width, block_units)
+    normed_arrived, cotangent_arrived = together(normed_moving, cotangent_arrived)
     cotangents = jnp.concatenate(cotangent_arrived, axis=0)
     group_normed = jnp.concatenate(normed_arrived, axis=0)
-    gate_matrix, up_matrix = clock.run(place_gathered, z_order, gate_up)
-    gate_matrix = gate_matrix.reshape(width, block_units)
-    up_matrix = up_matrix.reshape(width, block_units)
-
-    inner_act, d_gate, d_up = clock.run(
+
+    inner_act, d_gate, d_up, turned_normed, turned_inner = clock.run(
         feed_forward, group_normed, cotangents, gate_matrix, up_matrix, down_weight
     )
 
@@ -856,7 +844,7 @@
         sent, own = clock.run(
             lambda left, right: split_gradient(left, right, groups, core.place), left, right
         )
-        shape = (groups, first.size * second.size, -1, right.shape[1])
+        shape = (groups, first.size, second.size, -1, right.shape[1])
         return Halving(clock, sent.reshape(shape), own.reshape(shape), core, first, second)
 
     def side_by_side(rows):
@@ -865,8 +853,13 @@
     def sum_over_rep(blocks):
         return lax.psum_scatter(blocks, "rep", scatter_dimension=0, tiled=True)
 
+    def row_sum(arrived):
+        return clock(total_of(arrived).astype(bf16))[0]
+
     (down_blocks,) = clock.run(
-        lambda left, right: ordered_gradient(left, right, 1, list(range(reps))), inner_act, cotangents
+        lambda left, right: ordered_gradient(left, right, 1, list(range(reps))),
+        turned_inner,
+        cotangents,
     )
     down_piece = sum_over_rep(down_blocks.reshape(block_units, width))
     normed_own, *normed_partial = clock.run(
@@ -877,13 +870,22 @@
         up_matrix,
     )
     normed_arriving = send_rows(normed_partial)
-    up = start_halving(group_normed, d_up, shards)
+    up = start_halving(turned_normed, d_up, shards)
     (gate_blocks,) = clock.run(
-        lambda left, right: ordered_gradient(left, right, shards, rep_places(reps)), group_normed, d_gate
-    )
+        lambda left, right: ordered_gradient(left, right, shards, rep_places(reps)),
+        turned_normed,
+        d_gate,
+    )
+    gate_piece = sum_over_rep(gate_blocks.reshape(width, block_units))
     up.along_first()
-    (down_piece,) = clock(down_piece)
-    gate_piece = sum_over_rep(gate_blocks.reshape(width, block_units))
+    block_own, *block_partial = clock.run(
+        lambda left, right: rows_product((left,), (right,), False, shards), inner_act, down_weight
+    )
+    block_arrived = [None] * len(block_partial)
+
+    def move_block(at):
+        block_arrived[at] = shard.shift(block_partial[at], shards - 1 - at)
+
     up.along_second()
 
     normed_two_gradient = total_of([normed_own] + clock(*normed_arriving))
@@ -904,14 +906,12 @@
         key_marks.T,
     )
     pair_arriving = send_rows(pair_partial)
-    output = start_halving(attention_low, branch_gradient, shards)
+    output = start_halving(clock(attention_low.T)[0], branch_gradient, shards)
     up_blocks = up.finish()
     output.along_first()
-    block_own, *block_partial = clock.run(
-        lambda left, right: rows_product((left,), (right,), False, shards), inner_act, down_weight
-    )
+    (down_piece,) = clock(down_piece)
+    down_gathered = lax.all_gather(down_piece, "rep", axis=0, tiled=True)
     pair_terms = [pair_own] + clock(*pair_arriving)
-    up_moving = place_sends(up_blocks)
     projected_gradient, bias_sum = clock.run(
         lambda *operands: join_projected(operands[0], operands[3:], *operands[1:3]),
         d_queries,
@@ -919,11 +919,13 @@
         signed_sine,
         *pair_terms,
     )
-    projected = start_halving(normed_one, projected_gradient, shards)
+    projected = start_halving(clock(normed_one.T)[0], projected_gradient, shards)
+    up_moving = shift_blocks(clock(*sends_of(up_blocks)))
     output.along_second()
     projected.along_first()
     up_rows = clock(*up_moving)
     up_spread = spread(side_by_side(up_rows))
+    move_block(0)
     output_blocks = output.finish()
     projected_gradient, hidden_gradient = clock(projected_gradient, hidden_gradient)
     normed_one_gradient = times_transposed(projected_gradient, input_matrix)
@@ -945,38 +947,44 @@
         jnp.concatenate([part.reshape(shards, -1) for part in small_parts], axis=1)
     )
     projected.along_second()
-    up_spread.further()
-    output_moving = place_sends(output_blocks)
-    input_blocks = projected.finish()
-    output_sum = clock(total_of(clock(*output_moving)).astype(bf16))[0]
-    input_moving = place_sends(input_blocks)
+    up_arrived, block_arrived[:1] = together(up_spread.waits(), block_arrived[:1])
+    up_spread.further(*up_arrived)
+    output_moving = shift_blocks(clock(*sends_of(output_blocks)))
+    input_blocks = clock(*sends_of(projected.finish()))
+    output_sum = row_sum(clock(*output_moving))
+    input_moving = shift_blocks(input_blocks)
     up_spread.over()
-    input_sum = clock(total_of(clock(*input_moving)).astype(bf16))[0]
+    input_sum = row_sum(clock(*input_moving))
+    input_spread = spread(input_sum)
+    up_arrived = clock(*up_spread.waits())
     (gate_piece,) = clock(gate_piece)
-    down_spread = lax.all_gather(down_piece, "rep", axis=0, tiled=True)
-    gate_moving = place_sends(gate_piece.reshape(shards, part_rows, block_units))
-    (up_total,) = clock.run(widen_pieces, *up_spread.finish())
-    gate_rows = clock(*gate_moving)
-    gate_spread = spread(side_by_side(gate_rows))
+    gate_moving = shift_blocks(
+        clock(*sends_of(gate_piece.reshape(shards, part_rows, block_units)))
+    )
+    (up_total,) = clock.run(widen_pieces, *up_spread.finish(*up_arrived))
+    input_spread.further()
+    for at in range(1, len(block_partial) - 1):
+        move_block(at)
+    input_spread.over()
+    gate_spread = spread(side_by_side(clock(*gate_moving)))
     output_spread = spread(output_sum)
+    (input_total,) = clock.run(widen_pieces, *input_spread.finish())
+    block_arrived[1:-1] = clock(*block_arrived[1:-1])
     output_spread.further()
-    block_arriving = send_rows(block_partial)
+    gate_spread.further()
+    move_block(len(block_partial) - 1)
     output_spread.over()
-    gate_spread.further()
-    input_spread = spread(input_sum)
-    (output_total,) = clock.run(widen_pieces, *output_spread.finish())
-    input_spread.further()
-    gate_spread.over()
-    input_spread.over()
-    (block_out,) = clock(total_of([hidden, block_own] + clock(*block_arriving)).astype(bf16))
-    (input_total,) = clock.run(widen_pieces, *input_spread.finish())
     for line in (core, first, second):
         small = total_of(
             [small] + clock(*[line.shift(small, step) for step in range(1, line.size)])
         )
-    small = total_of(clock(*place_sends(small)))
+    small_moving = shift_blocks(clock(*sends_of(small)))
+    gate_spread.over()
+    small = total_of(clock(*small_moving))
+    (output_total,) = clock.run(widen_pieces, *output_spread.finish())
+    down_total = clock(clock(down_gathered)[0].astype(f32))[0]
+    (block_out,) = clock(total_of([hidden, block_own] + clock(*block_arrived)).astype(bf16))
     (gate_total,) = clock.run(widen_pieces, *gate_spread.finish())
-    down_total = clock(down_spread)[0].astype(f32)
 
     small = small + clock.token[0, 0]
     small_totals, at = [], 0

time: 734 us -> 771 us (1.050)
  Pallas kernels: 189 us -> 144 us
  local copies, waits for them, and re-layouts: 42.4 us -> 86.8 us
  other arithmetic: 42.9 us -> 78.3 us
  waiting for transfers between devices: 314 us -> 299 us
  starting transfers between devices: 105 us -> 119 us
    pallas_call x10 -> x1, Pallas kernels: 70.2 us -> 23.6 us  [feed_forward(): pl.pallas_call(body, grid=(steps,), out_shape=[jax.ShapeDtypeStruct((coun...]
    optimization_barrier x2 -> x17, local copies, waits for them, and re-layouts: 1.95 us -> 30.7 us  [tie(): return lax.optimization_barrier(arrays)]
    reduce_scatter x2, waiting for transfers between devices: 27.8 us -> 0.01 us  [sum_over_rep(): return lax.psum_scatter(blocks, 'rep', scatter_dimension=0, tiled=True)]
    convert_element_type x4 -> x13, other arithmetic: 12.5 us -> 38.1 us  [the longest x6 17.8 us: along(): total_of([pick(term, line.ahead(step), 1) for term in self.terms])]
    ppermute x74 -> x78, starting transfers between devices: 105 us -> 119 us  [shift(): return lax.ppermute(value, self.name, self.pairs(step % self.size))]
    ppermute x74 -> x78, waiting for transfers between devices: 286 us -> 299 us  [shift(): return lax.ppermute(value, self.name, self.pairs(step % self.size))]
    reshape x0 -> x3, local copies, waits for them, and re-layouts: none -> 11.3 us  [start_halving(): sent.reshape(shape)]
    pallas_call x1 -> x2, Pallas kernels: 4.86 us -> 13.3 us  [place_blocks(): blocks_call(body, 2, len(pieces) + 1, groups, shards, reps, block)]
  transfers between devices with their start and end apart: 79 -> 83, of which waited for: 30 -> 31; matrix products, arithmetic and copies ran while one was open for 11% -> 20% of each run, Pallas kernels for 20% -> 14%
where the time goes in v6:
time: 771 us; the launch traced here: 760 us
  waiting for transfers between devices  299 us (39%)
  Pallas kernels  144 us (19%)
  starting transfers between devices  119 us (15%)
  local copies, waits for them, and re-layouts  86.8 us (11%)
  other arithmetic  78.3 us (10%)
  matrix products  17 us (2%)
  between operations  15.6 us (2%)
    ppermute x78, waiting for transfers between devices, shift(): return lax.ppermute(value, self.name, self.pairs(step % self.size))  299 us
    ppermute x78, starting transfers between devices, shift(): return lax.ppermute(value, self.name, self.pairs(step % self.size))  119 us
    optimization_barrier x17, local copies, waits for them, and re-layouts, tie(): return lax.optimization_barrier(arrays)  30.7 us
    pallas_call x2, Pallas kernels, rows_product(): pl.pallas_call(body, grid=(pl.cdiv(columns, TILE),), out_shape=[jax.Shape...  24.2 us
    pallas_call x1, Pallas kernels, feed_forward(): pl.pallas_call(body, grid=(steps,), out_shape=[jax.ShapeDtypeStruct((coun...  23.6 us
    pallas_call x4, Pallas kernels, widen_pieces(): pl.pallas_call(body, out_shape=jax.ShapeDtypeStruct((reps, rows, columns)...  21.3 us
    unnamed x141, local copies, waits for them, and re-layouts  20.4 us
    pallas_call x3, Pallas kernels, split_gradient(): pl.pallas_call(body, grid=(pl.cdiv(columns, TILE),), out_shape=[jax.Shape...  19.6 us
  transfers between devices with their start and end apart: 83, of which 31 were waited for; matrix products, arithmetic and copies ran while one was open for 20% of the time, Pallas kernels for 14%

profile of v6, /device:TPU:0, one launch (start us, length us, event | category | flops | bytes accessed | tf_op | source)
XLA Modules:
  0.0 760.4 jit_solution(5023981735666742885)
XLA Ops:
  47.6 14.6 %collective-permute-done.4.refs_2_ = bf16[1,4,48,2048]{3,2,1,0:T(8,128)(2,1)S(1)} collective-permute-done((bf16[1,4,48,2048]{3,2,1,0:T(8,128)(2,1)}, bf16[1,4,48,2048]{3,2,1,0:T(8,128)(2,1)S(1)}, u32[]{:S(2)}, u32[]{:S(2)}) %collective-permute-start.4) | collective-permute-done | bytes 786464 | tf_op jit(solution)/shard_map/ppermute | solution.py:68
  70.2 18.4 %collective-permute-done.6 = bf16[48,2240]{1,0:T(8,128)(2,1)S(1)} collective-permute-done((bf16[48,2240]{1,0:T(8,128)(2,1)}, bf16[48,2240]{1,0:T(8,128)(2,1)S(1)}, u32[]{:S(2)}, u32[]{:S(2)}) %collective-permute-start.6) | collective-permute-done | bytes 215072 | tf_op jit(solution)/shard_map/ppermute | solution.py:68
  88.6 6.7 collective-permute-done.7
  102.7 9.4 %collective-permute-start.11 = (bf16[48,2240]{1,0:T(8,128)(2,1)}, bf16[48,2240]{1,0:T(8,128)(2,1)}, u32[]{:S(2)}, u32[]{:S(2)}) collective-permute-start(bf16[48,2240]{1,0:T(8,128)(2,1)} %bitcast.278), channel_id=1, source_target_pairs={{0,1},{1,2},{2,3},{3,0},{4,5},{5,6},{6,7},{7,4},{8,9},{9,10},{10,1... | collective-permute-start | bytes 645128 | tf_op jit(solution)/shard_map/ppermute | solution.py:68
  144.8 11.7 %collective-permute-done.15 = bf16[160,512]{1,0:T(8,128)(2,1)S(1)} collective-permute-done((bf16[160,512]{1,0:T(8,128)(2,1)S(1)}, bf16[160,512]{1,0:T(8,128)(2,1)S(1)}, u32[]{:S(2)}, u32[]{:S(2)}) %collective-permute-start.15) | collective-permute-done | bytes 163872 | tf_op jit(solution)/shard_map/ppermute | solution.py:68
  156.5 10.0 %collective-permute-done.18.refs_2_ = bf16[1,4,48,2240]{3,2,1,0:T(8,128)(2,1)S(1)} collective-permute-done((bf16[1,4,48,2240]{3,2,1,0:T(8,128)(2,1)}, bf16[1,4,48,2240]{3,2,1,0:T(8,128)(2,1)S(1)}, u32[]{:S(2)}, u32[]{:S(2)}) %collective-permute-start.18) | collective-permute-done | bytes 860192 | tf_op jit(solution)/shard_map/ppermute | solution.py:68
  200.3 7.0 place_blocks.4
  207.4 7.0 place_blocks.5
  214.4 34.9 %collective-permute-done.24 = bf16[160,1536]{1,0:T(8,128)(2,1)} collective-permute-done((bf16[160,1536]{1,0:T(8,128)(2,1)}, bf16[160,1536]{1,0:T(8,128)(2,1)}, u32[]{:S(2)}, u32[]{:S(2)}) %collective-permute-start.24) | collective-permute-done | bytes 491552 | tf_op jit(solution)/shard_map/ppermute | solution.py:68
  249.3 20.7 %collective-permute-done.22 = bf16[160,1536]{1,0:T(8,128)(2,1)} collective-permute-done((bf16[160,1536]{1,0:T(8,128)(2,1)}, bf16[160,1536]{1,0:T(8,128)(2,1)}, u32[]{:S(2)}, u32[]{:S(2)}) %collective-permute-start.22) | collective-permute-done | bytes 491552 | tf_op jit(solution)/shard_map/ppermute | solution.py:68
  290.8 23.6 %feed_forward.1 = (bf16[640,2240]{1,0:T(8,128)(2,1)}, bf16[640,2240]{1,0:T(8,128)(2,1)}, bf16[640,2240]{1,0:T(8,128)(2,1)}, bf16[1536,640]{1,0:T(8,128)(2,1)}, bf16[2240,640]{1,0:T(8,128)(2,1)}) custom-call(bf16[640,1536]{1,0:T(8,128)(2,1)} %copy.169.rows_ref, bf16[640,1536]{1,0:T(8,128)(2,1)} %constant_dynamic-update-slice_fusion.4.cotangents_ref.right_ref, ...), custom_call_target="tpu_custom_call" | custom-call | flops 1 | bytes 1 | tf_op jit(solution)/shard_map/feed_forward/pallas_call | solution.py:422
  314.4 9.3 %ordered_gradient.2 = bf16[8,1,280,1536]{3,2,1,0:T(8,128)(2,1)} custom-call(bf16[2240,640]{1,0:T(8,128)(2,1)} %get-tuple-element.557.left_ref, bf16[640,1536]{1,0:T(8,128)(2,1)} %constant_dynamic-update-slice_fusion.4.cotangents_ref.right_ref), custom_call_target="tpu_custom_call" | custom-call | flops 1 | bytes 1 | tf_op jit(solution)/shard_map/ordered_gradient/pallas_call | solution.py:495
  323.8 15.2 %rows_product.2 = (bf16[160,1536]{1,0:T(8,128)(2,1)}, bf16[160,1536]{1,0:T(8,128)(2,1)}, bf16[160,1536]{1,0:T(8,128)(2,1)}, bf16[160,1536]{1,0:T(8,128)(2,1)}) custom-call(bf16[640,2240]{1,0:T(8,128)(2,1)} %get-tuple-element.581.refs_0_.right_ref, bf16[640,2240]{1,0:T(8,128)(2,1)} %get-tuple-element.575.refs_1_.right_ref, bf16[1536,2240]{1,0:T(8,128)(2,1)} %bitcast.222, ...), custom_call_target="tpu_custom_call" | custom-call | flops 1 | bytes 1 | tf_op jit(solution)/shard_map/rows_product/pallas_call | solution.py:535
  339.1 9.9 %split_gradient.3 = (bf16[4,192,2240]{2,1,0:T(8,128)(2,1)}, bf16[4,192,2240]{2,1,0:T(8,128)(2,1)}) custom-call(s32[1]{0:T(128)} %bitcast.49.core_ref, bf16[1536,640]{1,0:T(8,128)(2,1)} %get-tuple-element.580.left_ref, bf16[640,2240]{1,0:T(8,128)(2,1)} %get-tuple-element.575.refs_1_.right_ref), custom_call_target="tpu_custom_call" | custom-call | flops 1 | bytes 1 | tf_op jit(solution)/shard_map/split_gradient/pallas_call | solution.py:466
  353.0 10.2 %ordered_gradient.3 = bf16[8,4,48,2240]{3,2,1,0:T(8,128)(2,1)} custom-call(bf16[1536,640]{1,0:T(8,128)(2,1)} %get-tuple-element.580.left_ref, bf16[640,2240]{1,0:T(8,128)(2,1)} %get-tuple-element.581.refs_0_.right_ref), custom_call_target="tpu_custom_call" | custom-call | flops 1 | bytes 1 | tf_op jit(solution)/shard_map/ordered_gradient/pallas_call | solution.py:495
  375.9 9.0 %rows_product.3 = (bf16[160,1536]{1,0:T(8,128)(2,1)}, bf16[160,1536]{1,0:T(8,128)(2,1)}, bf16[160,1536]{1,0:T(8,128)(2,1)}, bf16[160,1536]{1,0:T(8,128)(2,1)}) custom-call(bf16[640,2240]{1,0:T(8,128)(2,1)} %get-tuple-element.590.refs_0_, bf16[2240,1536]{1,0:T(8,128)(2,1)} %refs_1_), custom_call_target="tpu_custom_call" | custom-call | flops 1 | bytes 1 | tf_op jit(solution)/shard_map/rows_product/pallas_call | solution.py:535
  384.9 13.6 %collective-permute-done.27 = bf16[4,2,48,2240]{3,2,0,1:T(8,128)(2,1)} collective-permute-done((bf16[4,2,48,2240]{3,2,0,1:T(8,128)(2,1)}, bf16[4,2,48,2240]{3,2,0,1:T(8,128)(2,1)}, u32[]{:S(2)}, u32[]{:S(2)}) %collective-permute-start.27) | collective-permute-done | bytes 1720352 | tf_op jit(solution)/shard_map/ppermute | solution.py:68
  401.4 10.2 %collective-permute-done.29 = bf16[160,1536]{1,0:T(8,128)(2,1)} collective-permute-done((bf16[160,1536]{1,0:T(8,128)(2,1)}, bf16[160,1536]{1,0:T(8,128)(2,1)}, u32[]{:S(2)}, u32[]{:S(2)}) %collective-permute-start.29) | collective-permute-done | bytes 491552 | tf_op jit(solution)/shard_map/ppermute | solution.py:68
  426.8 7.6 attention_backward.1
  448.3 8.3 %collective-permute-done.31 = bf16[4,48,2240]{2,1,0:T(8,128)(2,1)} collective-permute-done((bf16[4,48,2240]{2,1,0:T(8,128)(2,1)}, bf16[4,48,2240]{2,1,0:T(8,128)(2,1)}, u32[]{:S(2)}, u32[]{:S(2)}) %collective-permute-start.31) | collective-permute-done | bytes 860192 | tf_op jit(solution)/shard_map/ppermute | solution.py:68
  478.2 13.7 %collective-permute-done.36 = bf16[4,2,48,1536]{3,2,0,1:T(8,128)(2,1)} collective-permute-done((bf16[4,2,48,1536]{3,2,0,1:T(8,128)(2,1)}, bf16[4,2,48,1536]{3,2,0,1:T(8,128)(2,1)}, u32[]{:S(2)}, u32[]{:S(2)}) %collective-permute-start.36) | collective-permute-done | bytes 1179680 | tf_op jit(solution)/shard_map/ppermute | solution.py:68
  527.6 22.7 %collective-permute-done.42 = bf16[4,2,48,2048]{3,2,0,1:T(8,128)(2,1)} collective-permute-done((bf16[4,2,48,2048]{3,2,0,1:T(8,128)(2,1)}, bf16[4,2,48,2048]{3,2,0,1:T(8,128)(2,1)}, u32[]{:S(2)}, u32[]{:S(2)}) %collective-permute-start.42) | collective-permute-done | bytes 1572896 | tf_op jit(solution)/shard_map/ppermute | solution.py:68
  554.2 6.3 collective-permute-start.45
  560.6 10.2 %collective-permute-done.45 = bf16[160,1536]{1,0:T(8,128)(2,1)} collective-permute-done((bf16[160,1536]{1,0:T(8,128)(2,1)}, bf16[160,1536]{1,0:T(8,128)(2,1)}, u32[]{:S(2)}, u32[]{:S(2)}) %collective-permute-start.45) | collective-permute-done | bytes 491552 | tf_op jit(solution)/shard_map/ppermute | solution.py:68
  601.1 7.9 %collective-permute-done.52 = bf16[48,2048]{1,0:T(8,128)(2,1)S(1)} collective-permute-done((bf16[48,2048]{1,0:T(8,128)(2,1)S(1)}, bf16[48,2048]{1,0:T(8,128)(2,1)S(1)}, u32[]{:S(2)}, u32[]{:S(2)}) %collective-permute-start.52) | collective-permute-done | bytes 196640 | tf_op jit(solution)/shard_map/ppermute | solution.py:68
  615.0 7.3 widen_pieces.4
  634.9 8.0 %collective-permute-done.59 = bf16[48,2240]{1,0:T(8,128)(2,1)S(1)} collective-permute-done((bf16[48,2240]{1,0:T(8,128)(2,1)S(1)}, bf16[48,2240]{1,0:T(8,128)(2,1)S(1)}, u32[]{:S(2)}, u32[]{:S(2)}) %collective-permute-start.59) | collective-permute-done | bytes 215072 | tf_op jit(solution)/shard_map/ppermute | solution.py:68
  657.0 16.1 %collective-permute-done.62 = bf16[160,1536]{1,0:T(8,128)(2,1)S(1)} collective-permute-done((bf16[160,1536]{1,0:T(8,128)(2,1)}, bf16[160,1536]{1,0:T(8,128)(2,1)S(1)}, u32[]{:S(2)}, u32[]{:S(2)}) %collective-permute-start.62) | collective-permute-done | bytes 491552 | tf_op jit(solution)/shard_map/ppermute | solution.py:68
  675.8 12.3 %collective-permute-done.67.refs_3_ = bf16[48,1536]{1,0:T(8,128)(2,1)S(1)} collective-permute-done((bf16[48,1536]{1,0:T(8,128)(2,1)S(1)}, bf16[48,1536]{1,0:T(8,128)(2,1)S(1)}, u32[]{:S(2)}, u32[]{:S(2)}) %collective-permute-start.67) | collective-permute-done | bytes 147488 | tf_op jit(solution)/shard_map/ppermute | solution.py:68
  704.0 11.2 %collective-permute-done.72 = f32[1280]{0:T(1024)S(1)} collective-permute-done((f32[1280]{0:T(1024)S(1)}, f32[1280]{0:T(1024)S(1)}, u32[]{:S(2)}, u32[]{:S(2)}) %collective-permute-start.72) | collective-permute-done | bytes 5152 | tf_op jit(solution)/shard_map/ppermute | solution.py:68
  722.5 10.1 %convert_element_type.347 = f32[2240,1536]{1,0:T(8,128)} convert(bf16[2240,1536]{1,0:T(8,128)(2,1)} %all-gather.7.cloned.1.call-done) | non-fusion elementwise | flops 3440640 | bytes 20643840 | tf_op jit(solution)/shard_map/convert_element_type | solution.py:985
  743.1 7.4 widen_pieces.7
  (436 shorter events, 354.0 us)
Async XLA Ops:
  7.2 168.7 %all-gather.5.cloned.1.call-start = ((), (), s32[]{:S(2)}) async-start(), calls=%async_computation.2 | async-start | bytes 4866048 | tf_op jit(solution)/shard_map/all_gather | solution.py:746
  33.4 173.9 %all-gather.9.cloned.1.call-start = ((), (), s32[]{:S(2)}) async-start(), calls=%async_computation.6 | async-start | bytes 7962624 | tf_op jit(solution)/shard_map/all_gather | solution.py:794
  62.3 33.1 %collective-permute-start.5 = (bf16[1,4,48,2048]{3,2,1,0:T(8,128)(2,1)S(1)}, bf16[1,4,48,2048]{3,2,1,0:T(8,128)(2,1)S(1)}, u32[]{:S(2)}, u32[]{:S(2)}) collective-permute-start(bf16[1,4,48,2048]{3,2,1,0:T(8,128)(2,1)S(1)} %collective-permute-done.3.refs_1_), channel_id=1, source_target_pairs={{0,8},{4,20},{8,0},{12,28},{16,24},{20,4},{24,16},{28,12},{1,9},{5... | collective-permute-start | bytes 2359304 | tf_op jit(solution)/shard_map/ppermute | solution.py:68
  64.6 30.8 %collective-permute-start.9 = (bf16[160,1536]{1,0:T(8,128)(2,1)}, bf16[160,1536]{1,0:T(8,128)(2,1)S(1)}, u32[]{:S(2)}, u32[]{:S(2)}) collective-permute-start(bf16[160,1536]{1,0:T(8,128)(2,1)} %param.21), channel_id=1, source_target_pairs={{0,1},{1,2},{2,3},{3,0},{4,5},{5,6},{6,7},{7,4},{8,9},{9,10},{10,1... | collective-permute-start | bytes 1474568 | tf_op jit(solution)/shard_map/ppermute | solution.py:68
  67.8 27.6 %collective-permute-start.7 = (bf16[48,2240]{1,0:T(8,128)(2,1)}, bf16[48,2240]{1,0:T(8,128)(2,1)S(1)}, u32[]{:S(2)}, u32[]{:S(2)}) collective-permute-start(bf16[48,2240]{1,0:T(8,128)(2,1)} %bitcast.280), channel_id=1, source_target_pairs={{0,2},{1,3},{2,0},{3,1},{4,6},{5,7},{6,4},{7,5},{8,10},{9,11},{10,... | collective-permute-start | bytes 645128 | tf_op jit(solution)/shard_map/ppermute | solution.py:68
  69.0 26.4 %collective-permute-start.8 = (bf16[48,2240]{1,0:T(8,128)(2,1)}, bf16[48,2240]{1,0:T(8,128)(2,1)S(1)}, u32[]{:S(2)}, u32[]{:S(2)}) collective-permute-start(bf16[48,2240]{1,0:T(8,128)(2,1)} %bitcast.279), channel_id=1, source_target_pairs={{0,3},{1,0},{2,1},{3,2},{4,7},{5,4},{6,5},{7,6},{8,11},{9,8},{10,9... | collective-permute-start | bytes 645128 | tf_op jit(solution)/shard_map/ppermute | solution.py:68
  97.5 365.1 %reduce-scatter.3.cloned.1.call-start = ((), (), s32[]{:S(2)}) async-start(), calls=%async_computation.3 | async-start | bytes 7741440 | tf_op jit(solution)/shard_map/reduce_scatter | solution.py:854
  102.7 24.2 %collective-permute-start.11 = (bf16[48,2240]{1,0:T(8,128)(2,1)}, bf16[48,2240]{1,0:T(8,128)(2,1)}, u32[]{:S(2)}, u32[]{:S(2)}) collective-permute-start(bf16[48,2240]{1,0:T(8,128)(2,1)} %bitcast.278), channel_id=1, source_target_pairs={{0,1},{1,2},{2,3},{3,0},{4,5},{5,6},{6,7},{7,4},{8,9},{9,10},{10,1... | collective-permute-start | bytes 645128 | tf_op jit(solution)/shard_map/ppermute | solution.py:68
  133.7 32.8 %collective-permute-start.18 = (bf16[1,4,48,2240]{3,2,1,0:T(8,128)(2,1)}, bf16[1,4,48,2240]{3,2,1,0:T(8,128)(2,1)S(1)}, u32[]{:S(2)}, u32[]{:S(2)}) collective-permute-start(bf16[1,4,48,2240]{3,2,1,0:T(8,128)(2,1)} %get-tuple-element.516.refs_0_), channel_id=1, source_target_pairs={{0,8},{4,20},{8,0},{12,28},{16,24},{20,4},{24,16},{28,12},{1,9},{5... | collective-permute-start | bytes 2580488 | tf_op jit(solution)/shard_map/ppermute | solution.py:68
  134.9 33.8 %collective-permute-start.17 = (bf16[1,4,48,2240]{3,2,1,0:T(8,128)(2,1)}, bf16[1,4,48,2240]{3,2,1,0:T(8,128)(2,1)}, u32[]{:S(2)}, u32[]{:S(2)}) collective-permute-start(bf16[1,4,48,2240]{3,2,1,0:T(8,128)(2,1)} %get-tuple-element.516.refs_0_), channel_id=1, source_target_pairs={{0,16},{4,12},{8,24},{12,4},{16,0},{20,28},{24,8},{28,20},{1,17},{... | collective-permute-start | bytes 2580488 | tf_op jit(solution)/shard_map/ppermute | solution.py:68
  190.4 24.0 %collective-permute-start.25 = (bf16[160,1536]{1,0:T(8,128)(2,1)}, bf16[160,1536]{1,0:T(8,128)(2,1)}, u32[]{:S(2)}, u32[]{:S(2)}) collective-permute-start(bf16[160,1536]{1,0:T(8,128)(2,1)} %param.21), channel_id=1, source_target_pairs={{0,3},{1,0},{2,1},{3,2},{4,7},{5,4},{6,5},{7,6},{8,11},{9,8},{10,9... | collective-permute-start | bytes 1474568 | tf_op jit(solution)/shard_map/ppermute | solution.py:68
  193.7 55.6 %collective-permute-start.24 = (bf16[160,1536]{1,0:T(8,128)(2,1)}, bf16[160,1536]{1,0:T(8,128)(2,1)}, u32[]{:S(2)}, u32[]{:S(2)}) collective-permute-start(bf16[160,1536]{1,0:T(8,128)(2,1)} %param.21), channel_id=1, source_target_pairs={{0,2},{1,3},{2,0},{3,1},{4,6},{5,7},{6,4},{7,5},{8,10},{9,11},{10,... | collective-permute-start | bytes 1474568 | tf_op jit(solution)/shard_map/ppermute | solution.py:68
  195.9 53.4 %collective-permute-start.23 = (bf16[160,1536]{1,0:T(8,128)(2,1)}, bf16[160,1536]{1,0:T(8,128)(2,1)}, u32[]{:S(2)}, u32[]{:S(2)}) collective-permute-start(bf16[160,1536]{1,0:T(8,128)(2,1)} %copy.163), channel_id=1, source_target_pairs={{0,3},{1,0},{2,1},{3,2},{4,7},{5,4},{6,5},{7,6},{8,11},{9,8},{10,9... | collective-permute-start | bytes 1474568 | tf_op jit(solution)/shard_map/ppermute | solution.py:68
  196.8 73.1 %collective-permute-start.22 = (bf16[160,1536]{1,0:T(8,128)(2,1)}, bf16[160,1536]{1,0:T(8,128)(2,1)}, u32[]{:S(2)}, u32[]{:S(2)}) collective-permute-start(bf16[160,1536]{1,0:T(8,128)(2,1)} %copy.163), channel_id=1, source_target_pairs={{0,2},{1,3},{2,0},{3,1},{4,6},{5,7},{6,4},{7,5},{8,10},{9,11},{10,... | collective-permute-start | bytes 1474568 | tf_op jit(solution)/shard_map/ppermute | solution.py:68
  197.7 72.3 %collective-permute-start.21 = (bf16[160,1536]{1,0:T(8,128)(2,1)}, bf16[160,1536]{1,0:T(8,128)(2,1)}, u32[]{:S(2)}, u32[]{:S(2)}) collective-permute-start(bf16[160,1536]{1,0:T(8,128)(2,1)} %copy.163), channel_id=1, source_target_pairs={{0,1},{1,2},{2,3},{3,0},{4,5},{5,6},{6,7},{7,4},{8,9},{9,10},{10,1... | collective-permute-start | bytes 1474568 | tf_op jit(solution)/shard_map/ppermute | solution.py:68
  323.8 289.9 %reduce-scatter.5.cloned.1.call-start = ((), (), s32[]{:S(2)}) async-start(), calls=%async_computation.4 | async-start | bytes 7962624 | tf_op jit(solution)/shard_map/reduce_scatter | solution.py:854
  366.4 32.1 %collective-permute-start.27 = (bf16[4,2,48,2240]{3,2,0,1:T(8,128)(2,1)}, bf16[4,2,48,2240]{3,2,0,1:T(8,128)(2,1)}, u32[]{:S(2)}, u32[]{:S(2)}) collective-permute-start(bf16[4,2,48,2240]{3,2,0,1:T(8,128)(2,1)} %fusion.4), channel_id=1, source_target_pairs={{0,8},{4,20},{8,0},{12,28},{16,24},{20,4},{24,16},{28,12},{1,9},{5... | collective-permute-start | bytes 5160968 | tf_op jit(solution)/shard_map/ppermute | solution.py:68
  366.5 34.9 %collective-permute-start.28 = (bf16[160,1536]{1,0:T(8,128)(2,1)}, bf16[160,1536]{1,0:T(8,128)(2,1)}, u32[]{:S(2)}, u32[]{:S(2)}) collective-permute-start(bf16[160,1536]{1,0:T(8,128)(2,1)} %get-tuple-element.601), channel_id=1, source_target_pairs={{0,3},{1,0},{2,1},{3,2},{4,7},{5,4},{6,5},{7,6},{8,11},{9,8},{10,9... | collective-permute-start | bytes 1474568 | tf_op jit(solution)/shard_map/ppermute | solution.py:68
  366.6 45.1 %collective-permute-start.29 = (bf16[160,1536]{1,0:T(8,128)(2,1)}, bf16[160,1536]{1,0:T(8,128)(2,1)}, u32[]{:S(2)}, u32[]{:S(2)}) collective-permute-start(bf16[160,1536]{1,0:T(8,128)(2,1)} %get-tuple-element.602), channel_id=1, source_target_pairs={{0,2},{1,3},{2,0},{3,1},{4,6},{5,7},{6,4},{7,5},{8,10},{9,11},{10,... | collective-permute-start | bytes 1474568 | tf_op jit(solution)/shard_map/ppermute | solution.py:68
  368.0 43.6 %collective-permute-start.30 = (bf16[160,1536]{1,0:T(8,128)(2,1)}, bf16[160,1536]{1,0:T(8,128)(2,1)}, u32[]{:S(2)}, u32[]{:S(2)}) collective-permute-start(bf16[160,1536]{1,0:T(8,128)(2,1)} %get-tuple-element.603), channel_id=1, source_target_pairs={{0,1},{1,2},{2,3},{3,0},{4,5},{5,6},{6,7},{7,4},{8,9},{9,10},{10,1... | collective-permute-start | bytes 1474568 | tf_op jit(solution)/shard_map/ppermute | solution.py:68
  375.8 346.6 %all-gather.7.cloned.1.call-start = ((), (), s32[]{:S(2)}) async-start(), calls=%async_computation.5 | async-start | bytes 7741440 | tf_op jit(solution)/shard_map/all_gather | solution.py:913
  475.5 25.3 %collective-permute-start.37 = (bf16[4,2,2,48,2048]{4,3,0,2,1:T(8,128)(2,1)}, bf16[4,2,2,48,2048]{4,3,0,2,1:T(8,128)(2,1)}, u32[]{:S(2)}, u32[]{:S(2)}) collective-permute-start(bf16[4,2,2,48,2048]{4,3,0,2,1:T(8,128)(2,1)} %copy.185), channel_id=1, source_target_pairs={{0,4},{4,0},{8,12},{12,8},{16,20},{20,16},{24,28},{28,24},{1,5},{5... | collective-permute-start | bytes 9437192 | tf_op jit(solution)/shard_map/ppermute | solution.py:68
  513.3 57.4 %collective-permute-start.44 = (bf16[48,8960]{1,0:T(8,128)(2,1)}, bf16[48,8960]{1,0:T(8,128)(2,1)}, u32[]{:S(2)}, u32[]{:S(2)}) collective-permute-start(bf16[48,8960]{1,0:T(8,128)(2,1)} %concatenate.54.refs_0_), channel_id=1, source_target_pairs={{0,8},{4,20},{8,0},{12,28},{16,24},{20,4},{24,16},{28,12},{1,9},{5... | collective-permute-start | bytes 2580488 | tf_op jit(solution)/shard_map/ppermute | solution.py:68
  514.5 56.3 %collective-permute-start.43 = (bf16[48,8960]{1,0:T(8,128)(2,1)}, bf16[48,8960]{1,0:T(8,128)(2,1)}, u32[]{:S(2)}, u32[]{:S(2)}) collective-permute-start(bf16[48,8960]{1,0:T(8,128)(2,1)} %concatenate.54.refs_0_), channel_id=1, source_target_pairs={{0,16},{4,12},{8,24},{12,4},{16,0},{20,28},{24,8},{28,20},{1,17},{... | collective-permute-start | bytes 2580488 | tf_op jit(solution)/shard_map/ppermute | solution.py:68
  515.6 34.7 %collective-permute-start.42 = (bf16[4,2,48,2048]{3,2,0,1:T(8,128)(2,1)}, bf16[4,2,48,2048]{3,2,0,1:T(8,128)(2,1)}, u32[]{:S(2)}, u32[]{:S(2)}) collective-permute-start(bf16[4,2,48,2048]{3,2,0,1:T(8,128)(2,1)} %fusion.16), channel_id=1, source_target_pairs={{0,8},{4,20},{8,0},{12,28},{16,24},{20,4},{24,16},{28,12},{1,9},{5... | collective-permute-start | bytes 4718600 | tf_op jit(solution)/shard_map/ppermute | solution.py:68
  553.2 23.6 %collective-permute-start.46 = (bf16[4,48,2048]{2,1,0:T(8,128)(2,1)}, bf16[4,48,2048]{2,1,0:T(8,128)(2,1)S(1)}, u32[]{:S(2)}, u32[]{:S(2)}) collective-permute-start(bf16[4,48,2048]{2,1,0:T(8,128)(2,1)} %fusion.19), channel_id=1, source_target_pairs={{0,16},{4,12},{8,24},{12,4},{16,0},{20,28},{24,8},{28,20},{1,17},{... | collective-permute-start | bytes 2359304 | tf_op jit(solution)/shard_map/ppermute | solution.py:68
  645.2 27.8 %collective-permute-start.66 = (bf16[48,8960]{1,0:T(8,128)(2,1)S(1)}, bf16[48,8960]{1,0:T(8,128)(2,1)S(1)}, u32[]{:S(2)}, u32[]{:S(2)}) collective-permute-start(bf16[48,8960]{1,0:T(8,128)(2,1)S(1)} %concatenate.56.refs_0_), channel_id=1, source_target_pairs={{0,8},{4,20},{8,0},{12,28},{16,24},{20,4},{24,16},{28,12},{1,9},{5... | collective-permute-start | bytes 2580488 | tf_op jit(solution)/shard_map/ppermute | solution.py:68
  645.7 27.4 %collective-permute-start.65 = (bf16[48,8960]{1,0:T(8,128)(2,1)S(1)}, bf16[48,8960]{1,0:T(8,128)(2,1)S(1)}, u32[]{:S(2)}, u32[]{:S(2)}) collective-permute-start(bf16[48,8960]{1,0:T(8,128)(2,1)S(1)} %concatenate.56.refs_0_), channel_id=1, source_target_pairs={{0,16},{4,12},{8,24},{12,4},{16,0},{20,28},{24,8},{28,20},{1,17},{... | collective-permute-start | bytes 2580488 | tf_op jit(solution)/shard_map/ppermute | solution.py:68
  647.3 25.8 %collective-permute-start.62 = (bf16[160,1536]{1,0:T(8,128)(2,1)}, bf16[160,1536]{1,0:T(8,128)(2,1)S(1)}, u32[]{:S(2)}, u32[]{:S(2)}) collective-permute-start(bf16[160,1536]{1,0:T(8,128)(2,1)} %get-tuple-element.790), channel_id=1, source_target_pairs={{0,2},{1,3},{2,0},{3,1},{4,6},{5,7},{6,4},{7,5},{8,10},{9,11},{10,... | collective-permute-start | bytes 1474568 | tf_op jit(solution)/shard_map/ppermute | solution.py:68
  673.8 23.0 %collective-permute-start.71 = (bf16[48,8960]{1,0:T(8,128)(2,1)S(1)}, bf16[48,8960]{1,0:T(8,128)(2,1)S(1)}, u32[]{:S(2)}, u32[]{:S(2)}) collective-permute-start(bf16[48,8960]{1,0:T(8,128)(2,1)S(1)} %collective-permute-done.65.refs_1_), channel_id=1, source_target_pairs={{0,8},{4,20},{8,0},{12,28},{16,24},{20,4},{24,16},{28,12},{1,9},{5... | collective-permute-start | bytes 2580488 | tf_op jit(solution)/shard_map/ppermute | solution.py:68
  699.1 44.0 %collective-permute-start.77 = (bf16[4,48,8960]{2,1,0:T(8,128)(2,1)}, bf16[4,48,8960]{2,1,0:T(8,128)(2,1)}, u32[]{:S(2)}, u32[]{:S(2)}) collective-permute-start(bf16[4,48,8960]{2,1,0:T(8,128)(2,1)} %pad_maximum_fusion.2), channel_id=1, source_target_pairs={{0,4},{4,0},{8,12},{12,8},{16,20},{20,16},{24,28},{28,24},{1,5},{5... | collective-permute-start | bytes 10321928 | tf_op jit(solution)/shard_map/ppermute | solution.py:68
  699.6 32.9 %collective-permute-start.76 = (bf16[160,1536]{1,0:T(8,128)(2,1)}, bf16[160,1536]{1,0:T(8,128)(2,1)}, u32[]{:S(2)}, u32[]{:S(2)}) collective-permute-start(bf16[160,1536]{1,0:T(8,128)(2,1)} %get-tuple-element.836), channel_id=1, source_target_pairs={{0,1},{1,2},{2,3},{3,0},{4,5},{5,6},{6,7},{7,4},{8,9},{9,10},{10,1... | collective-permute-start | bytes 1474568 | tf_op jit(solution)/shard_map/ppermute | solution.py:68
  (112 other events, 1717.4 us)
Sparse Core Ops, SparseCore 0:
  33.5 82.6 all-gather.4
  118.7 64.8 all-gather.8
  323.9 70.9 reduce-scatter.2
  399.2 69.4 reduce-scatter.4
  560.6 48.0 all-gather.6

commit v7 on v6

--- a/solution.py
+++ b/solution.py
@@ -166,6 +166,7 @@
 class Clock:
     def __init__(self):
         self.token = jnp.zeros((8, 128), jnp.float32)
+        self.open = 0
 
     def __call__(self, *arrays):
         self.token, *arrays = tie(self.token, *arrays)
@@ -173,6 +174,19 @@
 
     def run(self, step, *arrays):
         return self(*step(*self(*arrays)))
+
+    def send(self, line, values, steps):
+        self.open += len(values)
+        return [line.shift(value, step) for value, step in zip(self(*values), steps)]
+
+    def wait(self, *groups):
+        flat = self(*[array for group in groups for array in group])
+        self.open -= len(flat)
+        parts, at = [], 0
+        for group in groups:
+            parts.append(flat[at : at + len(group)])
+            at += len(group)
+        return parts
 
 
 def total_of(terms):
@@ -186,17 +200,17 @@
     def __init__(self, clock, sent, own, core, first, second):
         self.clock, self.first, self.second = clock, first, second
         self.terms = [own]
-        self.moving = [core.shift(sent, 1)]
+        self.moving = clock.send(core, [sent], [1])
 
     def along(self, line):
-        self.terms = self.terms + self.clock(*self.moving)
+        (arrived,) = self.clock.wait(self.moving)
+        self.terms = self.terms + arrived
+        steps = range(1, line.size)
         blocks = [
             total_of([pick(term, line.ahead(step), 1) for term in self.terms]).astype(jnp.bfloat16)
-            for step in range(1, line.size)
+            for step in steps
         ]
-        self.moving = [
-            line.shift(block, step) for step, block in enumerate(self.clock(*blocks), 1)
-        ]
+        self.moving = self.clock.send(line, blocks, steps)
         self.terms = [pick(term, line.place, 1) for term in self.terms]
 
     def along_first(self):
@@ -206,70 +220,53 @@
         self.along(self.second)
 
     def finish(self):
-        self.terms = self.terms + self.clock(*self.moving)
-        return self.clock(total_of(self.terms).astype(jnp.bfloat16))[0]
+        (arrived,) = self.clock.wait(self.moving)
+        return self.clock(total_of(self.terms + arrived).astype(jnp.bfloat16))[0]
 
 
 class Spread:
     def __init__(self, clock, piece, core, first, second):
         self.clock, self.lines = clock, (core, first, second)
-        self.across = {(0, two): second.shift(piece, two) for two in range(1, second.size)}
-        self.along = {(one, 0): first.shift(piece, one) for one in range(1, first.size)}
-        self.here = {(0, 0): piece}
-
-    def waits(self):
-        if hasattr(self, "there"):
-            return [self.there]
-        if hasattr(self, "beyond"):
-            return list(self.beyond.values())
-        return list(self.across.values()) + list(self.along.values())
-
-    def further(self, *values):
-        values = values or self.clock(*self.waits())
-        self.here.update(zip(list(self.across) + list(self.along), values))
-        self.beyond = {
-            (one, two): self.lines[1].shift(self.here[0, two], one)
-            for one in range(1, self.lines[1].size)
-            for two in range(1, self.lines[2].size)
-        }
-
-    def over(self, *values):
-        values = values or self.clock(*self.waits())
-        self.here.update(zip(self.beyond, values))
-        (stacked,) = self.clock(jnp.stack(list(self.here.values())))
-        self.there = self.lines[0].shift(stacked, 1)
-
-    def finish(self, *values):
+        self.pieces = [piece]
+        self.moving = clock.send(second, [piece], range(1, 2)) if second.size == 2 else []
+
+    def further(self):
         core, first, second = self.lines
-        (others,) = values or self.clock(*self.waits())
-        placed = [(core.place, first.behind(one), second.behind(two)) for one, two in self.here]
+        if self.moving:
+            (arrived,) = self.clock.wait(self.moving)
+            self.pieces = self.pieces + arrived
+        steps = range(1, first.size)
+        self.moving = self.clock.send(first, [jnp.stack(self.pieces)] * len(steps), steps)
+
+    def over(self):
+        core, first, second = self.lines
+        (arrived,) = self.clock.wait(self.moving)
+        rows = [jnp.stack(self.pieces)] + arrived
+        self.pieces = jnp.concatenate(rows, axis=0)
+        self.moving = self.clock.send(core, [self.pieces], [1])
+
+    def finish(self):
+        core, first, second = self.lines
+        ((others,),) = self.clock.wait(self.moving)
+        offsets = [(one, two) for one in range(first.size) for two in range(second.size)]
+        placed = [(core.place, first.behind(one), second.behind(two)) for one, two in offsets]
         far, near = (second, first) if core.crossed else (first, second)
-        placed += [(core.behind(1), far.behind(one), near.behind(two)) for one, two in self.here]
+        placed += [(core.behind(1), far.behind(one), near.behind(two)) for one, two in offsets]
         places = [(c * first.size + f) * second.size + s for c, f, s in placed]
-        return [jnp.stack(places).astype(jnp.int32), others] + list(self.here.values())
-
-
-def piece_of(r, sources):
-    return sources[r] if r < len(sources) - 1 else sources[-1].at[r - len(sources) + 1]
-
-
-def place_blocks(order, places, others, *pieces):
-    reps = 2 * len(pieces)
-    groups, shards = pieces[0].shape[:2]
-    block = pieces[0].shape[2:]
-
-    def body(order_ref, places_ref, *refs):
-        sources, rest = refs[: len(pieces) + 1], refs[len(pieces) + 1 :]
-        move_blocks(
-            lambda g, k, r: piece_of(r, sources).at[g, k],
-            lambda r: places_ref[r],
-            order_ref,
-            rest[:groups],
-            *rest[groups:],
-        )
-
-    return blocks_call(body, 2, len(pieces) + 1, groups, shards, reps, block)(
-        order, places, *pieces, others
+        return [jnp.stack(places).astype(jnp.int32), self.pieces, others]
+
+
+def place_blocks(order, places, pieces, others):
+    half, groups, shards = pieces.shape[:3]
+
+    def body(order_ref, places_ref, pieces_ref, others_ref, *rest):
+        def source_of(g, k, r):
+            return (pieces_ref if r < half else others_ref).at[r % half, g, k]
+
+        move_blocks(source_of, lambda r: places_ref[r], order_ref, rest[:groups], *rest[groups:])
+
+    return blocks_call(body, 2, 2, groups, shards, 2 * half, pieces.shape[3:])(
+        order, places, pieces, others
     )
 
 
@@ -326,16 +323,16 @@
     )
 
 
-def widen_pieces(places, others, *pieces):
-    reps = 2 * len(pieces)
-    rows, columns = pieces[0].shape
+def widen_pieces(places, pieces, others):
+    half, rows, columns = pieces.shape
+    reps = 2 * half
     strip = next(size for size in (16, 8, rows) if rows % size == 0)
 
-    def body(places_ref, *refs):
-        sources = refs[: len(pieces) + 1]
-        out_ref, narrow, wide, in_sems, out_sems = refs[len(pieces) + 1 :]
+    def body(places_ref, pieces_ref, others_ref, out_ref, narrow, wide, in_sems, out_sems):
         loads = [
-            pltpu.make_async_copy(piece_of(r, sources), narrow.at[r], in_sems.at[r])
+            pltpu.make_async_copy(
+                (pieces_ref if r < half else others_ref).at[r % half], narrow.at[r], in_sems.at[r]
+            )
             for r in range(reps)
         ]
         stores = [
@@ -361,7 +358,7 @@
         body,
         out_shape=jax.ShapeDtypeStruct((reps, rows, columns), jnp.float32),
         in_specs=[pl.BlockSpec(memory_space=pltpu.SMEM)]
-        + [pl.BlockSpec(memory_space=pl.ANY)] * (len(pieces) + 1),
+        + [pl.BlockSpec(memory_space=pl.ANY)] * 2,
         out_specs=pl.BlockSpec(memory_space=pl.ANY),
         scratch_shapes=[
             pltpu.VMEM((reps, rows, columns), jnp.bfloat16),
@@ -372,7 +369,7 @@
         compiler_params=pltpu.CompilerParams(vmem_limit_bytes=VMEM_LIMIT),
         cost_estimate=COST,
         name="widen_pieces",
-    )(places, *pieces, others)
+    )(places, pieces, others)
     return (result.reshape(reps * rows, columns),)
 
 
@@ -445,16 +442,25 @@
     )(rows, cotangents, gate_matrix, up_matrix, down_matrix)
 
 
-def split_gradient(left, right, groups, core_place):
-    rows, count = left.shape
+def split_gradient(left, right, groups, core_place, turned):
+    rows, count = left.shape if turned else left.shape[::-1]
     columns = right.shape[1]
     half = rows // (2 * groups)
 
-    def body(core_ref, left_ref, right_ref, other_ref, own_ref):
+    def body(core_ref, left_ref, right_ref, other_ref, own_ref, *scratch):
+        if turned:
+            rows_ref = left_ref
+        else:
+            (rows_ref,) = scratch
+
+            @pl.when(pl.program_id(0) == 0)
+            def turn():
+                rows_ref[...] = left_ref[...].T
+
         core = core_ref[0]
         for out_ref, which in ((other_ref, 1 - core), (own_ref, core)):
             halves = [
-                left_ref[pl.ds(pl.multiple_of((2 * group + which) * half, 16), half), :]
+                rows_ref[pl.ds(pl.multiple_of((2 * group + which) * half, 16), half), :]
                 for group in range(groups)
             ]
             product = jnp.dot(
@@ -469,10 +475,11 @@
         out_shape=[jax.ShapeDtypeStruct((groups, half, columns), jnp.bfloat16)] * 2,
         in_specs=[
             pl.BlockSpec(memory_space=pltpu.SMEM),
-            resident((rows, count)),
+            resident(left.shape),
             pl.BlockSpec((count, TILE), lambda i: (0, i)),
         ],
         out_specs=[pl.BlockSpec((groups, half, TILE), lambda i: (0, 0, i))] * 2,
+        scratch_shapes=[] if turned else [pltpu.VMEM((rows, count), jnp.bfloat16)],
         compiler_params=pltpu.CompilerParams(vmem_limit_bytes=VMEM_LIMIT),
         cost_estimate=COST,
         name="split_gradient",
@@ -713,38 +720,35 @@
     def spread(piece):
         return Spread(clock, piece, core, first, second)
 
-    def send_rows(rows):
-        return [shard.shift(row, shards - step) for step, row in enumerate(rows, 1)]
-
-    def sends_of(blocks):
+    def blocks_of(blocks):
         return [pick(blocks, shard.ahead(step), 0) for step in range(shards)]
 
-    def shift_blocks(blocks):
-        return [blocks[0]] + [shard.shift(block, step) for step, block in enumerate(blocks[1:], 1)]
-
-    def together(*groups):
-        flat = clock(*[array for group in groups for array in group])
-        parts, at = [], 0
-        for group in groups:
-            parts.append(flat[at : at + len(group)])
-            at += len(group)
-        return parts
+    steps = range(1, shards)
+
+    def send_blocks(blocks):
+        return clock.send(shard, blocks[1:], steps)
+
+    def send_around(value):
+        return clock.send(shard, [value] * len(steps), steps)
+
+    def send_back(rows):
+        return clock.send(shard, rows, [shards - step for step in steps])
 
     rep_index = lax.axis_index("rep")
     shard_vectors = jnp.concatenate([first_gain, second_gain, input_bias])
     vector_row = jnp.pad(shard_vectors, (0, input_weight.shape[1] - shard_vectors.shape[0]))
-    input_moving = gather_line(
-        jnp.concatenate([weight_piece(input_weight, rep_place), vector_row[None]], axis=0), shard
-    )
-    output_piece = weight_piece(output_weight, rep_index)
-    gate_blocks = sends_of(column_piece(gate_weight, rep_index))
-    up_blocks = sends_of(column_piece(up_weight, rep_place))
-    input_rows, gate_blocks, up_blocks, (output_piece,) = together(
-        input_moving, gate_blocks, up_blocks, [output_piece]
-    )
+    own_input = jnp.concatenate([weight_piece(input_weight, rep_place), vector_row[None]], axis=0)
+    input_moving = send_around(own_input)
+    output_piece, *gate_blocks = clock(
+        weight_piece(output_weight, rep_index), *blocks_of(column_piece(gate_weight, rep_index))
+    )
+    up_blocks = clock(*blocks_of(column_piece(up_weight, rep_place)))
+    (input_rows,) = clock.wait(input_moving)
+    input_rows = [own_input] + input_rows
     input_spread = spread(jnp.stack([rows[:part_rows] for rows in input_rows])[None])
-    output_matrix = lax.all_gather(output_piece, ("shard", "rep"), axis=0, tiled=True)
-    gate_moving = shift_blocks(gate_blocks)
+    output_matrix = lax.all_gather(clock(output_piece)[0], ("shard", "rep"), axis=0, tiled=True)
+    gate_moving = send_blocks(gate_blocks)
+
     vector_rows = jnp.stack(in_place_order([rows[part_rows] for rows in input_rows], shard))
     own_gain = first_gain.shape[0]
     gain_one = vector_rows[:, :own_gain].reshape(width).astype(f32)
@@ -752,7 +756,6 @@
     shift_row = (
         vector_rows[:, 2 * own_gain : shard_vectors.shape[0]].reshape(-1).astype(f32)
     )
-
     places = positions(segments)
     cosine_table, sine_table = rope_tables(
         lax.dynamic_slice_in_dim(places, first_row, own_rows), HD
@@ -784,15 +787,13 @@
         row_marks,
     ) = clock(normed_one, cosine_table, sine_table, signed_sine, key_marks, row_marks)
 
-    far = list(range(2, shards - 1))
-    cotangent_arrived = [output_cotangent, shard.shift(output_cotangent, 1)] + [None] * (shards - 2)
     input_spread.further()
-    input_arrived, gate_rows, (cotangent_arrived[1],) = together(
-        input_spread.waits(), gate_moving, cotangent_arrived[1:2]
-    )
-    input_spread.over(*input_arrived)
-    gate_gathered = lax.all_gather(jnp.stack(gate_rows)[None, :, None], "rep", axis=0, tiled=True)
-    up_moving = shift_blocks(up_blocks)
+    (gate_rows,) = clock.wait(gate_moving)
+    gate_gathered = lax.all_gather(
+        clock(jnp.stack(gate_blocks[:1] + gate_rows))[0][None, :, None], "rep", axis=0, tiled=True
+    )
+    up_moving = send_blocks(up_blocks)
+    input_spread.over()
     (input_matrix,) = clock.run(place_blocks, z_order, *input_spread.finish())
     input_matrix = input_matrix.reshape(width, -1)
     projected = jnp.dot(normed_one, input_matrix, preferred_element_type=f32) + shift_row
@@ -807,14 +808,15 @@
             axis=1,
         ).astype(bf16)
     )
-    up_rows = clock(*up_moving)
-    pair_moving = gather_line(own_pairs, shard)
-    up_spread = spread(jnp.stack(up_rows)[None])
-    pair_rows, up_arrived = together(pair_moving, up_spread.waits())
-    pairs = jnp.concatenate(pair_rows, axis=0)
-    up_spread.further(*up_arrived)
-    for step in far:
-        cotangent_arrived[step] = shard.shift(output_cotangent, step)
+    (up_rows,) = clock.wait(up_moving)
+    pair_moving = send_around(own_pairs)
+    up_spread = spread(jnp.stack(up_blocks[:1] + up_rows)[None])
+    (pair_rows,) = clock.wait(pair_moving)
+    pairs = jnp.concatenate([own_pairs] + pair_rows, axis=0)
+    far = list(range(2, shards - 1))
+    near = sorted({1, shards - 1})
+    far_moving = clock.send(shard, [output_cotangent] * len(far), far)
+    up_spread.further()
     queries, attention_low = clock.run(
         attention_forward, projected, cosine_table, signed_sine, pairs, row_marks.T, key_marks
     )
@@ -823,26 +825,31 @@
     inverse_two = lax.rsqrt(jnp.mean(hidden * hidden, axis=-1, keepdims=True) + EPSILON)
     unit_two = hidden * inverse_two
     (normed_two,) = clock((unit_two * gain_two).astype(bf16))
-    normed_moving = gather_line(normed_two, shard)
+    normed_moving = send_around(normed_two)
     up_spread.over()
-    up_arrived = clock(*up_spread.waits())
-    if shards > 2:
-        cotangent_arrived[-1] = shard.shift(output_cotangent, shards - 1)
-    (up_matrix,) = clock.run(place_blocks, z_order, *up_spread.finish(*up_arrived))
+    (far_arrived,) = clock.wait(far_moving)
+    near_moving = clock.send(shard, [output_cotangent] * (len(near) - 1), near[1:])
+    (up_matrix,) = clock.run(place_blocks, z_order, *up_spread.finish())
+    near_moving = clock.send(shard, [output_cotangent], near[:1]) + near_moving
     up_matrix = up_matrix.reshape(width, block_units)
     (gate_matrix,) = clock.run(place_gathered, z_order, gate_gathered)
     gate_matrix = gate_matrix.reshape(width, block_units)
-    normed_arrived, cotangent_arrived = together(normed_moving, cotangent_arrived)
-    cotangents = jnp.concatenate(cotangent_arrived, axis=0)
-    group_normed = jnp.concatenate(normed_arrived, axis=0)
+    normed_arrived, near_arrived = clock.wait(normed_moving, near_moving)
+    group_normed = jnp.concatenate([normed_two] + normed_arrived, axis=0)
+    cotangent_arrived = dict(zip(near + far, near_arrived + far_arrived))
+    cotangents = jnp.concatenate(
+        [output_cotangent] + [cotangent_arrived[step] for step in steps], axis=0
+    )
 
     inner_act, d_gate, d_up, turned_normed, turned_inner = clock.run(
         feed_forward, group_normed, cotangents, gate_matrix, up_matrix, down_weight
     )
 
-    def start_halving(left, right, groups):
+    def start_halving(left, right, groups, turned):
         sent, own = clock.run(
-            lambda left, right: split_gradient(left, right, groups, core.place), left, right
+            lambda left, right: split_gradient(left, right, groups, core.place, turned),
+            left,
+            right,
         )
         shape = (groups, first.size, second.size, -1, right.shape[1])
         return Halving(clock, sent.reshape(shape), own.reshape(shape), core, first, second)
@@ -852,9 +859,6 @@
 
     def sum_over_rep(blocks):
         return lax.psum_scatter(blocks, "rep", scatter_dimension=0, tiled=True)
-
-    def row_sum(arrived):
-        return clock(total_of(arrived).astype(bf16))[0]
 
     (down_blocks,) = clock.run(
         lambda left, right: ordered_gradient(left, right, 1, list(range(reps))),
@@ -869,8 +873,8 @@
         gate_matrix,
         up_matrix,
     )
-    normed_arriving = send_rows(normed_partial)
-    up = start_halving(turned_normed, d_up, shards)
+    normed_moving = send_back(normed_partial)
+    up = start_halving(turned_normed, d_up, shards, True)
     (gate_blocks,) = clock.run(
         lambda left, right: ordered_gradient(left, right, shards, rep_places(reps)),
         turned_normed,
@@ -881,14 +885,13 @@
     block_own, *block_partial = clock.run(
         lambda left, right: rows_product((left,), (right,), False, shards), inner_act, down_weight
     )
-    block_arrived = [None] * len(block_partial)
-
-    def move_block(at):
-        block_arrived[at] = shard.shift(block_partial[at], shards - 1 - at)
+
+    def send_block(at):
+        return clock.send(shard, [block_partial[at]], [shards - 1 - at])
 
     up.along_second()
-
-    normed_two_gradient = total_of([normed_own] + clock(*normed_arriving))
+    (normed_arrived,) = clock.wait(normed_moving)
+    normed_two_gradient = total_of([normed_own] + normed_arrived)
     gain_two_gradient = jnp.sum(normed_two_gradient * unit_two, axis=0)
     hidden_gradient = output_cotangent.astype(f32) + norm_back(
         normed_two_gradient, unit_two, inverse_two, gain_two
@@ -905,28 +908,29 @@
         row_marks,
         key_marks.T,
     )
-    pair_arriving = send_rows(pair_partial)
-    output = start_halving(clock(attention_low.T)[0], branch_gradient, shards)
-    up_blocks = up.finish()
+    pair_moving = send_back(pair_partial)
+    output = start_halving(attention_low, branch_gradient, shards, False)
+    up_blocks = clock(*blocks_of(up.finish()))
     output.along_first()
     (down_piece,) = clock(down_piece)
     down_gathered = lax.all_gather(down_piece, "rep", axis=0, tiled=True)
-    pair_terms = [pair_own] + clock(*pair_arriving)
+    (pair_arrived,) = clock.wait(pair_moving)
+    up_moving = send_blocks(up_blocks)
     projected_gradient, bias_sum = clock.run(
         lambda *operands: join_projected(operands[0], operands[3:], *operands[1:3]),
         d_queries,
         cosine_table,
         signed_sine,
-        *pair_terms,
-    )
-    projected = start_halving(clock(normed_one.T)[0], projected_gradient, shards)
-    up_moving = shift_blocks(clock(*sends_of(up_blocks)))
+        pair_own,
+        *pair_arrived,
+    )
+    projected = start_halving(normed_one, projected_gradient, shards, False)
     output.along_second()
     projected.along_first()
-    up_rows = clock(*up_moving)
-    up_spread = spread(side_by_side(up_rows))
-    move_block(0)
-    output_blocks = output.finish()
+    (up_rows,) = clock.wait(up_moving)
+    up_spread = spread(side_by_side(up_blocks[:1] + up_rows))
+    output_blocks = clock(*blocks_of(output.finish()))
+    output_moving = send_blocks(output_blocks)
     projected_gradient, hidden_gradient = clock(projected_gradient, hidden_gradient)
     normed_one_gradient = times_transposed(projected_gradient, input_matrix)
     gain_one_gradient = jnp.sum(normed_one_gradient * unit_one, axis=0)
@@ -947,44 +951,52 @@
         jnp.concatenate([part.reshape(shards, -1) for part in small_parts], axis=1)
     )
     projected.along_second()
-    up_arrived, block_arrived[:1] = together(up_spread.waits(), block_arrived[:1])
-    up_spread.further(*up_arrived)
-    output_moving = shift_blocks(clock(*sends_of(output_blocks)))
-    input_blocks = clock(*sends_of(projected.finish()))
-    output_sum = row_sum(clock(*output_moving))
-    input_moving = shift_blocks(input_blocks)
+    up_spread.further()
+    (output_rows,) = clock.wait(output_moving)
+    output_spread = spread(clock(total_of(output_blocks[:1] + output_rows).astype(bf16))[0])
+    block_first = send_block(0)
+    small_moving = clock.send(core, [small], [1])
+    input_blocks = clock(*blocks_of(projected.finish()))
+    output_spread.further()
+    block_first, small_arrived = clock.wait(block_first, small_moving)
+    small = total_of([small] + small_arrived)
+    (gate_piece,) = clock(gate_piece)
+    gate_blocks = clock(*blocks_of(gate_piece.reshape(shards, part_rows, block_units)))
+    gate_moving = send_blocks(gate_blocks)
+    output_spread.over()
+    (output_total,) = clock.run(widen_pieces, *output_spread.finish())
     up_spread.over()
-    input_sum = row_sum(clock(*input_moving))
-    input_spread = spread(input_sum)
-    up_arrived = clock(*up_spread.waits())
-    (gate_piece,) = clock(gate_piece)
-    gate_moving = shift_blocks(
-        clock(*sends_of(gate_piece.reshape(shards, part_rows, block_units)))
-    )
-    (up_total,) = clock.run(widen_pieces, *up_spread.finish(*up_arrived))
+    small_moving = clock.send(first, [small] * (first.size - 1), range(1, first.size))
+    (gate_rows,) = clock.wait(gate_moving)
+    gate_spread = spread(side_by_side(gate_blocks[:1] + gate_rows))
+    (small_arrived,) = clock.wait(small_moving)
+    small = total_of([small] + small_arrived)
+    input_moving = send_blocks(input_blocks)
+    (up_total,) = clock.run(widen_pieces, *up_spread.finish())
+    gate_spread.further()
+    (input_rows,) = clock.wait(input_moving)
+    input_spread = spread(clock(total_of(input_blocks[:1] + input_rows).astype(bf16))[0])
+    block_moving = []
+    for at in range(1, len(block_partial) - 1):
+        block_moving += send_block(at)
+    small_moving = clock.send(second, [small] * (second.size - 1), range(1, second.size))
     input_spread.further()
-    for at in range(1, len(block_partial) - 1):
-        move_block(at)
+    gate_spread.over()
+    (small_arrived,) = clock.wait(small_moving)
+    small = total_of([small] + small_arrived)
     input_spread.over()
-    gate_spread = spread(side_by_side(clock(*gate_moving)))
-    output_spread = spread(output_sum)
+    block_last = send_block(len(block_partial) - 1) if len(block_partial) > 1 else []
+    (gate_total,) = clock.run(widen_pieces, *gate_spread.finish())
     (input_total,) = clock.run(widen_pieces, *input_spread.finish())
-    block_arrived[1:-1] = clock(*block_arrived[1:-1])
-    output_spread.further()
-    gate_spread.further()
-    move_block(len(block_partial) - 1)
-    output_spread.over()
-    for line in (core, first, second):
-        small = total_of(
-            [small] + clock(*[line.shift(small, step) for step in range(1, line.size)])
-        )
-    small_moving = shift_blocks(clock(*sends_of(small)))
-    gate_spread.over()
-    small = total_of(clock(*small_moving))
-    (output_total,) = clock.run(widen_pieces, *output_spread.finish())
-    down_total = clock(clock(down_gathered)[0].astype(f32))[0]
-    (block_out,) = clock(total_of([hidden, block_own] + clock(*block_arrived)).astype(bf16))
-    (gate_total,) = clock.run(widen_pieces, *gate_spread.finish())
+    small_blocks = clock(*blocks_of(small))
+    small_moving = send_blocks(small_blocks)
+    (down_gathered,) = clock(down_gathered)
+    (down_total,) = clock(down_gathered.astype(f32))
+    small_arrived, block_arrived, block_last = clock.wait(small_moving, block_moving, block_last)
+    small = total_of(small_blocks[:1] + small_arrived)
+    (block_out,) = clock(
+        total_of([hidden, block_own] + block_first + block_arrived + block_last).astype(bf16)
+    )
 
     small = small + clock.token[0, 0]
     small_totals, at = [], 0

time: 771 us -> 717 us (0.930)
  local copies, waits for them, and re-layouts: 86.8 us -> 54.3 us
  waiting for transfers between devices: 299 us -> 282 us
    optimization_barrier x17 -> x5, local copies, waits for them, and re-layouts: 30.7 us -> 13.5 us  [tie(): return lax.optimization_barrier(arrays)]
    ppermute x78 -> x72, waiting for transfers between devices: 299 us -> 282 us  [shift(): return lax.ppermute(value, self.name, self.pairs(step % self.size))]
    reshape x3 -> x0, local copies, waits for them, and re-layouts: 11.3 us -> none  [start_halving(): sent.reshape(shape)]
    unnamed x141, local copies, waits for them, and re-layouts: 20.4 us -> 10.1 us
    concatenate x1 -> x7, other arithmetic: 2.7 us -> 12.2 us  [the longest x6 8.9 us: over(): self.pieces = jnp.concatenate(rows, axis=0)]
    ppermute x78 -> x72, starting transfers between devices: 119 us -> 123 us  [shift(): return lax.ppermute(value, self.name, self.pairs(step % self.size))]
  transfers between devices with their start and end apart: 83 -> 77, of which waited for: 31 -> 31; matrix products, arithmetic and copies ran while one was open for 20% -> 17% of each run, Pallas kernels for 14% -> 16%
where the time goes in v7:
time: 717 us; the launch traced here: 707 us
  waiting for transfers between devices  282 us (39%)
  Pallas kernels  144 us (20%)
  starting transfers between devices  123 us (17%)
  other arithmetic  72.1 us (10%)
  local copies, waits for them, and re-layouts  54.3 us (8%)
  matrix products  16 us (2%)
  between operations  15.7 us (2%)
    ppermute x72, waiting for transfers between devices, shift(): return lax.ppermute(value, self.name, self.pairs(step % self.size))  282 us
    ppermute x72, starting transfers between devices, shift(): return lax.ppermute(value, self.name, self.pairs(step % self.size))  123 us
    pallas_call x1, Pallas kernels, feed_forward(): pl.pallas_call(body, grid=(steps,), out_shape=[jax.ShapeDtypeStruct((coun...  23.7 us
    pallas_call x2, Pallas kernels, rows_product(): pl.pallas_call(body, grid=(pl.cdiv(columns, TILE),), out_shape=[jax.Shape...  23.1 us
    pallas_call x4, Pallas kernels, widen_pieces(): pl.pallas_call(body, out_shape=jax.ShapeDtypeStruct((reps, rows, columns)...  21.3 us
    pallas_call x3, Pallas kernels, split_gradient(): pl.pallas_call(body, grid=(pl.cdiv(columns, TILE),), out_shape=[jax.Shape...  20.6 us
    pallas_call x2, Pallas kernels, ordered_gradient(): pl.pallas_call(body, grid=(pl.cdiv(columns, TILE),), out_shape=[jax.Shape...  19.4 us
    convert_element_type x6, other arithmetic, along(): total_of([pick(term, line.ahead(step), 1) for term in self.terms])  17.1 us
  transfers between devices with their start and end apart: 77, of which 31 were waited for; matrix products, arithmetic and copies ran while one was open for 17% of the time, Pallas kernels for 16%

profile of v7, /device:TPU:0, one launch (start us, length us, event | category | flops | bytes accessed | tf_op | source)
XLA Modules:
  0.0 707.1 jit_solution(18352990724303711086)
XLA Ops:
  43.6 11.4 %collective-permute-done.3 = bf16[1,4,48,2048]{3,2,1,0:T(8,128)(2,1)S(1)} collective-permute-done((bf16[1,4,48,2048]{3,2,1,0:T(8,128)(2,1)}, bf16[1,4,48,2048]{3,2,1,0:T(8,128)(2,1)S(1)}, u32[]{:S(2)}, u32[]{:S(2)}) %collective-permute-start.3) | collective-permute-done | bytes 786464 | tf_op jit(solution)/shard_map/ppermute | solution.py:68
  69.4 12.2 %collective-permute-done.5 = bf16[48,2240]{1,0:T(8,128)(2,1)S(1)} collective-permute-done((bf16[48,2240]{1,0:T(8,128)(2,1)S(1)}, bf16[48,2240]{1,0:T(8,128)(2,1)S(1)}, u32[]{:S(2)}, u32[]{:S(2)}) %collective-permute-start.5) | collective-permute-done | bytes 215072 | tf_op jit(solution)/shard_map/ppermute | solution.py:68
  95.2 6.3 place_blocks.3
  106.3 14.0 %collective-permute-done.10 = bf16[48,2240]{1,0:T(8,128)(2,1)} collective-permute-done((bf16[48,2240]{1,0:T(8,128)(2,1)}, bf16[48,2240]{1,0:T(8,128)(2,1)}, u32[]{:S(2)}, u32[]{:S(2)}) %collective-permute-start.10) | collective-permute-done | bytes 215072 | tf_op jit(solution)/shard_map/ppermute | solution.py:68
  134.4 6.1 collective-permute-done.13
  154.7 29.4 %collective-permute-done.16 = bf16[2,1,4,48,2240]{4,3,2,1,0:T(8,128)(2,1)} collective-permute-done((bf16[2,1,4,48,2240]{4,3,2,1,0:T(8,128)(2,1)}, bf16[2,1,4,48,2240]{4,3,2,1,0:T(8,128)(2,1)}, u32[]{:S(2)}, u32[]{:S(2)}) %collective-permute-start.16) | collective-permute-done | bytes 1720352 | tf_op jit(solution)/shard_map/ppermute | solution.py:68
  194.3 38.8 %collective-permute-done.17 = bf16[160,1536]{1,0:T(8,128)(2,1)S(1)} collective-permute-done((bf16[160,1536]{1,0:T(8,128)(2,1)S(1)}, bf16[160,1536]{1,0:T(8,128)(2,1)S(1)}, u32[]{:S(2)}, u32[]{:S(2)}) %collective-permute-start.17) | collective-permute-done | bytes 491552 | tf_op jit(solution)/shard_map/ppermute | solution.py:68
  233.2 7.0 place_blocks.4
  243.1 7.1 %place_blocks.5 = bf16[4,8,48,2240]{3,2,1,0:T(8,128)(2,1)} custom-call(s32[4]{0:T(128)} %pad_add_fusion.4.order_ref, bf16[8,4,1,48,2240]{4,3,2,1,0:T(8,128)(2,1)} %bitcast.220), custom_call_target="tpu_custom_call" | custom-call | flops 1 | bytes 1 | tf_op jit(solution)/shard_map/place_blocks/pallas_call | solution.py:281
  250.2 14.4 %collective-permute-done.23 = bf16[160,1536]{1,0:T(8,128)(2,1)} collective-permute-done((bf16[160,1536]{1,0:T(8,128)(2,1)S(1)}, bf16[160,1536]{1,0:T(8,128)(2,1)}, u32[]{:S(2)}, u32[]{:S(2)}) %collective-permute-start.23) | collective-permute-done | bytes 491552 | tf_op jit(solution)/shard_map/ppermute | solution.py:68
  270.1 23.7 %feed_forward.1 = (bf16[640,2240]{1,0:T(8,128)(2,1)}, bf16[640,2240]{1,0:T(8,128)(2,1)}, bf16[640,2240]{1,0:T(8,128)(2,1)}, bf16[1536,640]{1,0:T(8,128)(2,1)}, bf16[2240,640]{1,0:T(8,128)(2,1)}) custom-call(bf16[640,1536]{1,0:T(8,128)(2,1)} %pad_maximum_fusion.4.rows_ref, bf16[640,1536]{1,0:T(8,128)(2,1)} %copy-done.5, bf16[1536,2240]{1,0:T(8,128)(2,1)} %bitcast.206, ...), custom_call_target="tpu_custom_call" | custom-call | flops 1 | bytes 1 | tf_op jit(solution)/shard_map/feed_forward/pallas_call | solution.py:419
  293.7 9.3 %ordered_gradient.2 = bf16[8,1,280,1536]{3,2,1,0:T(8,128)(2,1)} custom-call(bf16[2240,640]{1,0:T(8,128)(2,1)} %get-tuple-element.642.left_ref, bf16[640,1536]{1,0:T(8,128)(2,1)} %copy-done.5), custom_call_target="tpu_custom_call" | custom-call | flops 1 | bytes 1 | tf_op jit(solution)/shard_map/ordered_gradient/pallas_call | solution.py:502
  303.1 14.6 %rows_product.2 = (bf16[160,1536]{1,0:T(8,128)(2,1)}, bf16[160,1536]{1,0:T(8,128)(2,1)}, bf16[160,1536]{1,0:T(8,128)(2,1)}, bf16[160,1536]{1,0:T(8,128)(2,1)}) custom-call(bf16[640,2240]{1,0:T(8,128)(2,1)} %get-tuple-element.672.refs_0_.right_ref, bf16[640,2240]{1,0:T(8,128)(2,1)} %get-tuple-element.664.refs_1_.right_ref, bf16[1536,2240]{1,0:T(8,128)(2,1)} %bitcast.207, ...), custom_call_target="tpu_custom_call" | custom-call | flops 1 | bytes 1 | tf_op jit(solution)/shard_map/rows_product/pallas_call | solution.py:542
  317.8 10.5 %split_gradient.3 = (bf16[4,192,2240]{2,1,0:T(8,128)(2,1)}, bf16[4,192,2240]{2,1,0:T(8,128)(2,1)}) custom-call(s32[1]{0:T(128)} %bitcast.44.core_ref, bf16[1536,640]{1,0:T(8,128)(2,1)} %get-tuple-element.671.left_ref, bf16[640,2240]{1,0:T(8,128)(2,1)} %get-tuple-element.664.refs_1_.right_ref), custom_call_target="tpu_custom_call" | custom-call | flops 1 | bytes 1 | tf_op jit(solution)/shard_map/split_gradient/pallas_call | solution.py:472
  332.6 10.1 %ordered_gradient.3 = bf16[8,4,48,2240]{3,2,1,0:T(8,128)(2,1)} custom-call(bf16[1536,640]{1,0:T(8,128)(2,1)} %get-tuple-element.671.left_ref, bf16[640,2240]{1,0:T(8,128)(2,1)} %get-tuple-element.672.refs_0_.right_ref), custom_call_target="tpu_custom_call" | custom-call | flops 1 | bytes 1 | tf_op jit(solution)/shard_map/ordered_gradient/pallas_call | solution.py:502
  350.9 8.7 %collective-permute-start.27 = (bf16[160,1536]{1,0:T(8,128)(2,1)}, bf16[160,1536]{1,0:T(8,128)(2,1)S(1)}, u32[]{:S(2)}, u32[]{:S(2)}) collective-permute-start(bf16[160,1536]{1,0:T(8,128)(2,1)} %get-tuple-element.693), channel_id=1, source_target_pairs={{0,2},{1,3},{2,0},{3,1},{4,6},{5,7},{6,4},{7,5},{8,10},{9,11},{10,... | collective-permute-start | bytes 1474568 | tf_op jit(solution)/shard_map/ppermute | solution.py:68
  359.5 10.4 %collective-permute-start.28 = (bf16[160,1536]{1,0:T(8,128)(2,1)}, bf16[160,1536]{1,0:T(8,128)(2,1)S(1)}, u32[]{:S(2)}, u32[]{:S(2)}) collective-permute-start(bf16[160,1536]{1,0:T(8,128)(2,1)} %get-tuple-element.694), channel_id=1, source_target_pairs={{0,1},{1,2},{2,3},{3,0},{4,5},{5,6},{6,7},{7,4},{8,9},{9,10},{10,1... | collective-permute-start | bytes 1474568 | tf_op jit(solution)/shard_map/ppermute | solution.py:68
  370.8 8.5 %rows_product.3 = (bf16[160,1536]{1,0:T(8,128)(2,1)}, bf16[160,1536]{1,0:T(8,128)(2,1)}, bf16[160,1536]{1,0:T(8,128)(2,1)}, bf16[160,1536]{1,0:T(8,128)(2,1)}) custom-call(bf16[640,2240]{1,0:T(8,128)(2,1)} %get-tuple-element.681.refs_0_, bf16[2240,1536]{1,0:T(8,128)(2,1)} %refs_1_), custom_call_target="tpu_custom_call" | custom-call | flops 1 | bytes 1 | tf_op jit(solution)/shard_map/rows_product/pallas_call | solution.py:542
  379.3 6.8 collective-permute-done.25
  389.3 13.7 %collective-permute-done.27 = bf16[160,1536]{1,0:T(8,128)(2,1)S(1)} collective-permute-done((bf16[160,1536]{1,0:T(8,128)(2,1)}, bf16[160,1536]{1,0:T(8,128)(2,1)S(1)}, u32[]{:S(2)}, u32[]{:S(2)}) %collective-permute-start.27) | collective-permute-done | bytes 491552 | tf_op jit(solution)/shard_map/ppermute | solution.py:68
  408.3 7.5 %attention_backward.1 = (bf16[160,1536]{1,0:T(8,128)(2,1)}, bf16[160,512]{1,0:T(8,128)(2,1)}, bf16[160,512]{1,0:T(8,128)(2,1)}, bf16[160,512]{1,0:T(8,128)(2,1)}, bf16[160,512]{1,0:T(8,128)(2,1)}) custom-call(bf16[2,960,128]{2,1,0:T(8,128)(2,1)} %get-tuple-element.706.queries_ref, bf16[160,1536]{1,0:T(8,128)(2,1)} %convolution_convert_fusion.gradient_ref, ...), custom_call_target="tpu_custom_call" | custom-call | flops 1 | bytes 1 | tf_op jit(solution)/shard_map/attention_backward/pallas_call | solution.py:644
  426.7 10.4 %collective-permute-done.29 = bf16[4,48,2240]{2,1,0:T(8,128)(2,1)} collective-permute-done((bf16[4,48,2240]{2,1,0:T(8,128)(2,1)}, bf16[4,48,2240]{2,1,0:T(8,128)(2,1)}, u32[]{:S(2)}, u32[]{:S(2)}) %collective-permute-start.29) | collective-permute-done | bytes 860192 | tf_op jit(solution)/shard_map/ppermute | solution.py:68
  462.8 17.7 %collective-permute-done.34 = bf16[4,2,48,1536]{3,2,0,1:T(8,128)(2,1)} collective-permute-done((bf16[4,2,48,1536]{3,2,0,1:T(8,128)(2,1)}, bf16[4,2,48,1536]{3,2,0,1:T(8,128)(2,1)}, u32[]{:S(2)}, u32[]{:S(2)}) %collective-permute-start.34) | collective-permute-done | bytes 1179680 | tf_op jit(solution)/shard_map/ppermute | solution.py:68
  491.7 9.1 %collective-permute-done.39 = bf16[4,48,1536]{2,1,0:T(8,128)(2,1)} collective-permute-done((bf16[4,48,1536]{2,1,0:T(8,128)(2,1)}, bf16[4,48,1536]{2,1,0:T(8,128)(2,1)}, u32[]{:S(2)}, u32[]{:S(2)}) %collective-permute-start.39) | collective-permute-done | bytes 589856 | tf_op jit(solution)/shard_map/ppermute | solution.py:68
  519.3 11.4 %collective-permute-done.40 = bf16[4,2,48,2048]{3,2,0,1:T(8,128)(2,1)} collective-permute-done((bf16[4,2,48,2048]{3,2,0,1:T(8,128)(2,1)}, bf16[4,2,48,2048]{3,2,0,1:T(8,128)(2,1)}, u32[]{:S(2)}, u32[]{:S(2)}) %collective-permute-start.40) | collective-permute-done | bytes 1572896 | tf_op jit(solution)/shard_map/ppermute | solution.py:68
  554.5 11.9 %collective-permute-done.49 = bf16[2,48,1536]{2,1,0:T(8,128)(2,1)S(1)} collective-permute-done((bf16[2,48,1536]{2,1,0:T(8,128)(2,1)}, bf16[2,48,1536]{2,1,0:T(8,128)(2,1)S(1)}, u32[]{:S(2)}, u32[]{:S(2)}) %collective-permute-start.49) | collective-permute-done | bytes 294944 | tf_op jit(solution)/shard_map/ppermute | solution.py:68
  586.8 8.7 %collective-permute-done.53 = bf16[48,2240]{1,0:T(8,128)(2,1)S(1)} collective-permute-done((bf16[48,2240]{1,0:T(8,128)(2,1)S(1)}, bf16[48,2240]{1,0:T(8,128)(2,1)S(1)}, u32[]{:S(2)}, u32[]{:S(2)}) %collective-permute-start.53) | collective-permute-done | bytes 215072 | tf_op jit(solution)/shard_map/ppermute | solution.py:68
  600.9 7.4 %widen_pieces.5 = f32[8,48,8960]{2,1,0:T(8,128)} custom-call(s32[8]{0:T(128)} %stack.250.places_ref, bf16[4,48,8960]{2,1,0:T(8,128)(2,1)} %pad_maximum_fusion.1.pieces_ref, bf16[4,48,8960]{2,1,0:T(8,128)(2,1)} %collective-permute-done.56.others_ref), custom_call_target="tpu_custom_call" | custom-call | flops 1 | bytes 1 | tf_op jit(solution)/shard_map/widen_pieces/pallas_call | solution.py:357
  608.4 15.3 %collective-permute-done.57 = bf16[48,8960]{1,0:T(8,128)(2,1)S(1)} collective-permute-done((bf16[48,8960]{1,0:T(8,128)(2,1)S(1)}, bf16[48,8960]{1,0:T(8,128)(2,1)S(1)}, u32[]{:S(2)}, u32[]{:S(2)}) %collective-permute-start.57) | collective-permute-done | bytes 860192 | tf_op jit(solution)/shard_map/ppermute | solution.py:68
  635.1 7.0 collective-permute-done.59
  663.6 7.3 %widen_pieces.6 = f32[8,48,8960]{2,1,0:T(8,128)} custom-call(s32[8]{0:T(128)} %stack.250.places_ref, bf16[4,48,8960]{2,1,0:T(8,128)(2,1)} %copy-done.3, bf16[4,48,8960]{2,1,0:T(8,128)(2,1)} %collective-permute-done.65.others_ref), custom_call_target="tpu_custom_call" | custom-call | flops 1 | bytes 1 | tf_op jit(solution)/shard_map/widen_pieces/pallas_call | solution.py:357
  679.7 10.2 %convert_element_type.347 = f32[2240,1536]{1,0:T(8,128)} convert(bf16[2240,1536]{1,0:T(8,128)(2,1)} %all-gather.7.cloned.1.call-done) | non-fusion elementwise | flops 3440640 | bytes 20643840 | tf_op jit(solution)/shard_map/convert_element_type | solution.py:994
  (422 shorter events, 304.7 us)
Async XLA Ops:
  7.2 143.8 %all-gather.5.cloned.1.call-start = ((), (), s32[]{:S(2)}) async-start(), calls=%async_computation.2 | async-start | bytes 4866048 | tf_op jit(solution)/shard_map/all_gather | solution.py:749
  36.4 206.6 %all-gather.9.cloned.1.call-start = ((), (), s32[]{:S(2)}) async-start(), calls=%async_computation.6 | async-start | bytes 7962624 | tf_op jit(solution)/shard_map/all_gather | solution.py:792
  56.4 26.3 %collective-permute-start.7 = (bf16[2,1,4,48,2048]{4,3,2,1,0:T(8,128)(2,1)}, bf16[2,1,4,48,2048]{4,3,2,1,0:T(8,128)(2,1)}, u32[]{:S(2)}, u32[]{:S(2)}) collective-permute-start(bf16[2,1,4,48,2048]{4,3,2,1,0:T(8,128)(2,1)} %pad_maximum_fusion.8), channel_id=1, source_target_pairs={{0,8},{4,20},{8,0},{12,28},{16,24},{20,4},{24,16},{28,12},{1,9},{5... | collective-permute-start | bytes 4718600 | tf_op jit(solution)/shard_map/ppermute | solution.py:68
  86.0 357.3 %reduce-scatter.3.cloned.1.call-start = ((), (), s32[]{:S(2)}) async-start(), calls=%async_computation.3 | async-start | bytes 7741440 | tf_op jit(solution)/shard_map/reduce_scatter | solution.py:861
  92.8 27.5 %collective-permute-start.10 = (bf16[48,2240]{1,0:T(8,128)(2,1)}, bf16[48,2240]{1,0:T(8,128)(2,1)}, u32[]{:S(2)}, u32[]{:S(2)}) collective-permute-start(bf16[48,2240]{1,0:T(8,128)(2,1)} %bitcast.195), channel_id=1, source_target_pairs={{0,2},{1,3},{2,0},{3,1},{4,6},{5,7},{6,4},{7,5},{8,10},{9,11},{10,... | collective-permute-start | bytes 645128 | tf_op jit(solution)/shard_map/ppermute | solution.py:68
  95.0 25.3 %collective-permute-start.11 = (bf16[48,2240]{1,0:T(8,128)(2,1)}, bf16[48,2240]{1,0:T(8,128)(2,1)}, u32[]{:S(2)}, u32[]{:S(2)}) collective-permute-start(bf16[48,2240]{1,0:T(8,128)(2,1)} %bitcast.194), channel_id=1, source_target_pairs={{0,3},{1,0},{2,1},{3,2},{4,7},{5,4},{6,5},{7,6},{8,11},{9,8},{10,9... | collective-permute-start | bytes 645128 | tf_op jit(solution)/shard_map/ppermute | solution.py:68
  142.8 41.3 %collective-permute-start.16 = (bf16[2,1,4,48,2240]{4,3,2,1,0:T(8,128)(2,1)}, bf16[2,1,4,48,2240]{4,3,2,1,0:T(8,128)(2,1)}, u32[]{:S(2)}, u32[]{:S(2)}) collective-permute-start(bf16[2,1,4,48,2240]{4,3,2,1,0:T(8,128)(2,1)} %pad_maximum_fusion.5), channel_id=1, source_target_pairs={{0,8},{4,20},{8,0},{12,28},{16,24},{20,4},{24,16},{28,12},{1,9},{5... | collective-permute-start | bytes 5160968 | tf_op jit(solution)/shard_map/ppermute | solution.py:68
  185.8 47.4 %collective-permute-start.18 = (bf16[4,1,4,48,2240]{4,3,2,1,0:T(8,128)(2,1)S(1)}, bf16[4,1,4,48,2240]{4,3,2,1,0:T(8,128)(2,1)}, u32[]{:S(2)}, u32[]{:S(2)}) collective-permute-start(bf16[4,1,4,48,2240]{4,3,2,1,0:T(8,128)(2,1)S(1)} %pad_maximum_fusion.pieces_ref), channel_id=1, source_target_pairs={{0,4},{4,0},{8,12},{12,8},{16,20},{20,16},{24,28},{28,24},{1,5},{5... | collective-permute-start | bytes 10321928 | tf_op jit(solution)/shard_map/ppermute | solution.py:68
  185.9 47.3 %collective-permute-start.17 = (bf16[160,1536]{1,0:T(8,128)(2,1)S(1)}, bf16[160,1536]{1,0:T(8,128)(2,1)S(1)}, u32[]{:S(2)}, u32[]{:S(2)}) collective-permute-start(bf16[160,1536]{1,0:T(8,128)(2,1)S(1)} %copy-done.22), channel_id=1, source_target_pairs={{0,2},{1,3},{2,0},{3,1},{4,6},{5,7},{6,4},{7,5},{8,10},{9,11},{10,... | collective-permute-start | bytes 1474568 | tf_op jit(solution)/shard_map/ppermute | solution.py:68
  189.4 60.7 %collective-permute-start.19 = (bf16[160,1536]{1,0:T(8,128)(2,1)S(1)}, bf16[160,1536]{1,0:T(8,128)(2,1)S(1)}, u32[]{:S(2)}, u32[]{:S(2)}) collective-permute-start(bf16[160,1536]{1,0:T(8,128)(2,1)S(1)} %multiply_convert_fusion), channel_id=1, source_target_pairs={{0,1},{1,2},{2,3},{3,0},{4,5},{5,6},{6,7},{7,4},{8,9},{9,10},{10,1... | collective-permute-start | bytes 1474568 | tf_op jit(solution)/shard_map/ppermute | solution.py:68
  191.9 58.2 %collective-permute-start.20 = (bf16[160,1536]{1,0:T(8,128)(2,1)S(1)}, bf16[160,1536]{1,0:T(8,128)(2,1)}, u32[]{:S(2)}, u32[]{:S(2)}) collective-permute-start(bf16[160,1536]{1,0:T(8,128)(2,1)S(1)} %multiply_convert_fusion), channel_id=1, source_target_pairs={{0,2},{1,3},{2,0},{3,1},{4,6},{5,7},{6,4},{7,5},{8,10},{9,11},{10,... | collective-permute-start | bytes 1474568 | tf_op jit(solution)/shard_map/ppermute | solution.py:68
  194.0 56.2 %collective-permute-start.21 = (bf16[160,1536]{1,0:T(8,128)(2,1)S(1)}, bf16[160,1536]{1,0:T(8,128)(2,1)}, u32[]{:S(2)}, u32[]{:S(2)}) collective-permute-start(bf16[160,1536]{1,0:T(8,128)(2,1)S(1)} %multiply_convert_fusion), channel_id=1, source_target_pairs={{0,3},{1,0},{2,1},{3,2},{4,7},{5,4},{6,5},{7,6},{8,11},{9,8},{10,9... | collective-permute-start | bytes 1474568 | tf_op jit(solution)/shard_map/ppermute | solution.py:68
  233.2 31.4 %collective-permute-start.23 = (bf16[160,1536]{1,0:T(8,128)(2,1)S(1)}, bf16[160,1536]{1,0:T(8,128)(2,1)}, u32[]{:S(2)}, u32[]{:S(2)}) collective-permute-start(bf16[160,1536]{1,0:T(8,128)(2,1)S(1)} %copy-done.22), channel_id=1, source_target_pairs={{0,3},{1,0},{2,1},{3,2},{4,7},{5,4},{6,5},{7,6},{8,11},{9,8},{10,9... | collective-permute-start | bytes 1474568 | tf_op jit(solution)/shard_map/ppermute | solution.py:68
  240.2 24.4 %collective-permute-start.22 = (bf16[160,1536]{1,0:T(8,128)(2,1)S(1)}, bf16[160,1536]{1,0:T(8,128)(2,1)}, u32[]{:S(2)}, u32[]{:S(2)}) collective-permute-start(bf16[160,1536]{1,0:T(8,128)(2,1)S(1)} %copy-done.22), channel_id=1, source_target_pairs={{0,1},{1,2},{2,3},{3,0},{4,5},{5,6},{6,7},{7,4},{8,9},{9,10},{10,1... | collective-permute-start | bytes 1474568 | tf_op jit(solution)/shard_map/ppermute | solution.py:68
  303.1 248.7 %reduce-scatter.5.cloned.1.call-start = ((), (), s32[]{:S(2)}) async-start(), calls=%async_computation.4 | async-start | bytes 7962624 | tf_op jit(solution)/shard_map/reduce_scatter | solution.py:861
  345.8 40.3 %collective-permute-start.25 = (bf16[4,2,48,2240]{3,2,0,1:T(8,128)(2,1)}, bf16[4,2,48,2240]{3,2,0,1:T(8,128)(2,1)}, u32[]{:S(2)}, u32[]{:S(2)}) collective-permute-start(bf16[4,2,48,2240]{3,2,0,1:T(8,128)(2,1)} %fusion), channel_id=1, source_target_pairs={{0,8},{4,20},{8,0},{12,28},{16,24},{20,4},{24,16},{28,12},{1,9},{5... | collective-permute-start | bytes 5160968 | tf_op jit(solution)/shard_map/ppermute | solution.py:68
  346.0 43.3 %collective-permute-start.26 = (bf16[160,1536]{1,0:T(8,128)(2,1)}, bf16[160,1536]{1,0:T(8,128)(2,1)S(1)}, u32[]{:S(2)}, u32[]{:S(2)}) collective-permute-start(bf16[160,1536]{1,0:T(8,128)(2,1)} %get-tuple-element.692), channel_id=1, source_target_pairs={{0,3},{1,0},{2,1},{3,2},{4,7},{5,4},{6,5},{7,6},{8,11},{9,8},{10,9... | collective-permute-start | bytes 1474568 | tf_op jit(solution)/shard_map/ppermute | solution.py:68
  350.9 52.2 %collective-permute-start.27 = (bf16[160,1536]{1,0:T(8,128)(2,1)}, bf16[160,1536]{1,0:T(8,128)(2,1)S(1)}, u32[]{:S(2)}, u32[]{:S(2)}) collective-permute-start(bf16[160,1536]{1,0:T(8,128)(2,1)} %get-tuple-element.693), channel_id=1, source_target_pairs={{0,2},{1,3},{2,0},{3,1},{4,6},{5,7},{6,4},{7,5},{8,10},{9,11},{10,... | collective-permute-start | bytes 1474568 | tf_op jit(solution)/shard_map/ppermute | solution.py:68
  359.5 43.5 %collective-permute-start.28 = (bf16[160,1536]{1,0:T(8,128)(2,1)}, bf16[160,1536]{1,0:T(8,128)(2,1)S(1)}, u32[]{:S(2)}, u32[]{:S(2)}) collective-permute-start(bf16[160,1536]{1,0:T(8,128)(2,1)} %get-tuple-element.694), channel_id=1, source_target_pairs={{0,1},{1,2},{2,3},{3,0},{4,5},{5,6},{6,7},{7,4},{8,9},{9,10},{10,1... | collective-permute-start | bytes 1474568 | tf_op jit(solution)/shard_map/ppermute | solution.py:68
  424.5 255.1 %all-gather.7.cloned.1.call-start = ((), (), s32[]{:S(2)}) async-start(), calls=%async_computation.5 | async-start | bytes 7741440 | tf_op jit(solution)/shard_map/all_gather | solution.py:916
  455.9 28.5 %collective-permute-start.35 = (bf16[4,2,2,48,2048]{4,3,0,2,1:T(8,128)(2,1)}, bf16[4,2,2,48,2048]{4,3,0,2,1:T(8,128)(2,1)}, u32[]{:S(2)}, u32[]{:S(2)}) collective-permute-start(bf16[4,2,2,48,2048]{4,3,0,2,1:T(8,128)(2,1)} %copy.91), channel_id=1, source_target_pairs={{0,4},{4,0},{8,12},{12,8},{16,20},{20,16},{24,28},{28,24},{1,5},{5... | collective-permute-start | bytes 9437192 | tf_op jit(solution)/shard_map/ppermute | solution.py:68
  455.9 24.6 %collective-permute-start.34 = (bf16[4,2,48,1536]{3,2,0,1:T(8,128)(2,1)}, bf16[4,2,48,1536]{3,2,0,1:T(8,128)(2,1)}, u32[]{:S(2)}, u32[]{:S(2)}) collective-permute-start(bf16[4,2,48,1536]{3,2,0,1:T(8,128)(2,1)} %fusion.12), channel_id=1, source_target_pairs={{0,8},{4,20},{8,0},{12,28},{16,24},{20,4},{24,16},{28,12},{1,9},{5... | collective-permute-start | bytes 3538952 | tf_op jit(solution)/shard_map/ppermute | solution.py:68
  457.9 30.2 %collective-permute-start.36 = (bf16[48,2240]{1,0:T(8,128)(2,1)S(1)}, bf16[48,2240]{1,0:T(8,128)(2,1)}, u32[]{:S(2)}, u32[]{:S(2)}) collective-permute-start(bf16[48,2240]{1,0:T(8,128)(2,1)S(1)} %copy-done.35), channel_id=1, source_target_pairs={{0,1},{1,2},{2,3},{3,0},{4,5},{5,6},{6,7},{7,4},{8,9},{9,10},{10,1... | collective-permute-start | bytes 645128 | tf_op jit(solution)/shard_map/ppermute | solution.py:68
  458.1 30.0 %collective-permute-start.37 = (bf16[48,2240]{1,0:T(8,128)(2,1)S(1)}, bf16[48,2240]{1,0:T(8,128)(2,1)}, u32[]{:S(2)}, u32[]{:S(2)}) collective-permute-start(bf16[48,2240]{1,0:T(8,128)(2,1)S(1)} %copy-done.34), channel_id=1, source_target_pairs={{0,2},{1,3},{2,0},{3,1},{4,6},{5,7},{6,4},{7,5},{8,10},{9,11},{10,... | collective-permute-start | bytes 645128 | tf_op jit(solution)/shard_map/ppermute | solution.py:68
  458.4 29.7 %collective-permute-start.38 = (bf16[48,2240]{1,0:T(8,128)(2,1)S(1)}, bf16[48,2240]{1,0:T(8,128)(2,1)}, u32[]{:S(2)}, u32[]{:S(2)}) collective-permute-start(bf16[48,2240]{1,0:T(8,128)(2,1)S(1)} %copy-done.33), channel_id=1, source_target_pairs={{0,3},{1,0},{2,1},{3,2},{4,7},{5,4},{6,5},{7,6},{8,11},{9,8},{10,9... | collective-permute-start | bytes 645128 | tf_op jit(solution)/shard_map/ppermute | solution.py:68
  500.8 29.9 %collective-permute-start.40 = (bf16[4,2,48,2048]{3,2,0,1:T(8,128)(2,1)}, bf16[4,2,48,2048]{3,2,0,1:T(8,128)(2,1)}, u32[]{:S(2)}, u32[]{:S(2)}) collective-permute-start(bf16[4,2,48,2048]{3,2,0,1:T(8,128)(2,1)} %fusion.4), channel_id=1, source_target_pairs={{0,8},{4,20},{8,0},{12,28},{16,24},{20,4},{24,16},{28,12},{1,9},{5... | collective-permute-start | bytes 4718600 | tf_op jit(solution)/shard_map/ppermute | solution.py:68
  504.9 27.8 %collective-permute-start.41 = (bf16[48,8960]{1,0:T(8,128)(2,1)S(1)}, bf16[48,8960]{1,0:T(8,128)(2,1)}, u32[]{:S(2)}, u32[]{:S(2)}) collective-permute-start(bf16[48,8960]{1,0:T(8,128)(2,1)S(1)} %concatenate.74), channel_id=1, source_target_pairs={{0,16},{4,12},{8,24},{12,4},{16,0},{20,28},{24,8},{28,20},{1,17},{... | collective-permute-start | bytes 2580488 | tf_op jit(solution)/shard_map/ppermute | solution.py:68
  541.0 31.9 %collective-permute-start.51 = (bf16[2,48,8960]{2,1,0:T(8,128)(2,1)}, bf16[2,48,8960]{2,1,0:T(8,128)(2,1)}, u32[]{:S(2)}, u32[]{:S(2)}) collective-permute-start(bf16[2,48,8960]{2,1,0:T(8,128)(2,1)} %pad_maximum_fusion.6), channel_id=1, source_target_pairs={{0,8},{4,20},{8,0},{12,28},{16,24},{20,4},{24,16},{28,12},{1,9},{5... | collective-permute-start | bytes 5160968 | tf_op jit(solution)/shard_map/ppermute | solution.py:68
  576.2 24.7 %collective-permute-start.56 = (bf16[4,48,8960]{2,1,0:T(8,128)(2,1)}, bf16[4,48,8960]{2,1,0:T(8,128)(2,1)}, u32[]{:S(2)}, u32[]{:S(2)}) collective-permute-start(bf16[4,48,8960]{2,1,0:T(8,128)(2,1)} %pad_maximum_fusion.1.pieces_ref), channel_id=1, source_target_pairs={{0,4},{4,0},{8,12},{12,8},{16,20},{20,16},{24,28},{28,24},{1,5},{5... | collective-permute-start | bytes 10321928 | tf_op jit(solution)/shard_map/ppermute | solution.py:68
  596.1 27.5 %collective-permute-start.57 = (bf16[48,8960]{1,0:T(8,128)(2,1)S(1)}, bf16[48,8960]{1,0:T(8,128)(2,1)S(1)}, u32[]{:S(2)}, u32[]{:S(2)}) collective-permute-start(bf16[48,8960]{1,0:T(8,128)(2,1)S(1)} %concatenate.78), channel_id=1, source_target_pairs={{0,16},{4,12},{8,24},{12,4},{16,0},{20,28},{24,8},{28,20},{1,17},{... | collective-permute-start | bytes 2580488 | tf_op jit(solution)/shard_map/ppermute | solution.py:68
  656.7 37.5 %collective-permute-start.70 = (bf16[160,1536]{1,0:T(8,128)(2,1)}, bf16[160,1536]{1,0:T(8,128)(2,1)}, u32[]{:S(2)}, u32[]{:S(2)}) collective-permute-start(bf16[160,1536]{1,0:T(8,128)(2,1)} %get-tuple-element.960), channel_id=1, source_target_pairs={{0,2},{1,3},{2,0},{3,1},{4,6},{5,7},{6,4},{7,5},{8,10},{9,11},{10,... | collective-permute-start | bytes 1474568 | tf_op jit(solution)/shard_map/ppermute | solution.py:68
  660.4 33.8 %collective-permute-start.71 = (bf16[160,1536]{1,0:T(8,128)(2,1)}, bf16[160,1536]{1,0:T(8,128)(2,1)}, u32[]{:S(2)}, u32[]{:S(2)}) collective-permute-start(bf16[160,1536]{1,0:T(8,128)(2,1)} %get-tuple-element.961), channel_id=1, source_target_pairs={{0,1},{1,2},{2,3},{3,0},{4,5},{5,6},{6,7},{7,4},{8,9},{9,10},{10,1... | collective-permute-start | bytes 1474568 | tf_op jit(solution)/shard_map/ppermute | solution.py:68
  (108 other events, 1622.0 us)
Sparse Core Ops, SparseCore 0:
  36.5 85.3 all-gather.4
  124.4 61.6 all-gather.8
  303.2 83.4 reduce-scatter.2
  424.6 75.6 reduce-scatter.4
  568.1 55.8 all-gather.6

commit v8 on v7

--- a/solution.py
+++ b/solution.py
@@ -66,6 +66,11 @@
 
     def shift(self, value, step):
         return lax.ppermute(value, self.name, self.pairs(step % self.size))
+
+    def pass_on(self, value, up):
+        places = range(self.size - 1)
+        pairs = [(at, at + 1) if up else (at + 1, at) for at in places]
+        return lax.ppermute(value, self.name, pairs)
 
     def behind(self, step):
         return lax.rem(self.place + (self.size - step % self.size), self.size)
@@ -179,6 +184,11 @@
         self.open += len(values)
         return [line.shift(value, step) for value, step in zip(self(*values), steps)]
 
+    def pass_on(self, line, lower, upper):
+        self.open += 2
+        lower, upper = self(lower, upper)
+        return [line.pass_on(lower, True), line.pass_on(upper, False)]
+
     def wait(self, *groups):
         flat = self(*[array for group in groups for array in group])
         self.open -= len(flat)
@@ -202,25 +212,23 @@
         self.terms = [own]
         self.moving = clock.send(core, [sent], [1])
 
-    def along(self, line):
-        (arrived,) = self.clock.wait(self.moving)
+    def along(self, line, arrived):
         self.terms = self.terms + arrived
         steps = range(1, line.size)
         blocks = [
-            total_of([pick(term, line.ahead(step), 1) for term in self.terms]).astype(jnp.bfloat16)
+            total_of([pick(term, line.ahead(step), 0) for term in self.terms]).astype(jnp.bfloat16)
             for step in steps
         ]
         self.moving = self.clock.send(line, blocks, steps)
-        self.terms = [pick(term, line.place, 1) for term in self.terms]
-
-    def along_first(self):
-        self.along(self.first)
-
-    def along_second(self):
-        self.along(self.second)
-
-    def finish(self):
-        (arrived,) = self.clock.wait(self.moving)
+        self.terms = [pick(term, line.place, 0) for term in self.terms]
+
+    def along_first(self, arrived):
+        self.along(self.first, arrived)
+
+    def along_second(self, arrived):
+        self.along(self.second, arrived)
+
+    def finish(self, arrived):
         return self.clock(total_of(self.terms + arrived).astype(jnp.bfloat16))[0]
 
 
@@ -228,26 +236,24 @@
     def __init__(self, clock, piece, core, first, second):
         self.clock, self.lines = clock, (core, first, second)
         self.pieces = [piece]
-        self.moving = clock.send(second, [piece], range(1, 2)) if second.size == 2 else []
-
-    def further(self):
+        steps = range(1, second.size)
+        self.moving = clock.send(second, [piece] * len(steps), steps)
+
+    def along(self, arrived):
         core, first, second = self.lines
-        if self.moving:
-            (arrived,) = self.clock.wait(self.moving)
-            self.pieces = self.pieces + arrived
+        self.pieces = self.pieces + arrived
         steps = range(1, first.size)
         self.moving = self.clock.send(first, [jnp.stack(self.pieces)] * len(steps), steps)
 
-    def over(self):
+    def over(self, arrived):
         core, first, second = self.lines
-        (arrived,) = self.clock.wait(self.moving)
         rows = [jnp.stack(self.pieces)] + arrived
         self.pieces = jnp.concatenate(rows, axis=0)
         self.moving = self.clock.send(core, [self.pieces], [1])
 
-    def finish(self):
+    def finish(self, arrived):
         core, first, second = self.lines
-        ((others,),) = self.clock.wait(self.moving)
+        (others,) = arrived
         offsets = [(one, two) for one in range(first.size) for two in range(second.size)]
         placed = [(core.place, first.behind(one), second.behind(two)) for one, two in offsets]
         far, near = (second, first) if core.crossed else (first, second)
@@ -442,10 +448,11 @@
     )(rows, cotangents, gate_matrix, up_matrix, down_matrix)
 
 
-def split_gradient(left, right, groups, core_place, turned):
+def split_gradient(left, right, groups, places, core_place, turned):
     rows, count = left.shape if turned else left.shape[::-1]
     columns = right.shape[1]
     half = rows // (2 * groups)
+    part = half // places
 
     def body(core_ref, left_ref, right_ref, other_ref, own_ref, *scratch):
         if turned:
@@ -467,18 +474,20 @@
                 jnp.concatenate(halves, axis=0), right_ref[...], preferred_element_type=jnp.float32
             )
             for group in range(groups):
-                out_ref[group] = product[group * half : (group + 1) * half].astype(jnp.bfloat16)
+                for place in range(places):
+                    at = group * half + place * part
+                    out_ref[place, group] = product[at : at + part].astype(jnp.bfloat16)
 
     return pl.pallas_call(
         body,
         grid=(pl.cdiv(columns, TILE),),
-        out_shape=[jax.ShapeDtypeStruct((groups, half, columns), jnp.bfloat16)] * 2,
+        out_shape=[jax.ShapeDtypeStruct((places, groups, part, columns), jnp.bfloat16)] * 2,
         in_specs=[
             pl.BlockSpec(memory_space=pltpu.SMEM),
             resident(left.shape),
             pl.BlockSpec((count, TILE), lambda i: (0, i)),
         ],
-        out_specs=[pl.BlockSpec((groups, half, TILE), lambda i: (0, 0, i))] * 2,
+        out_specs=[pl.BlockSpec((places, groups, part, TILE), lambda i: (0, 0, 0, i))] * 2,
         scratch_shapes=[] if turned else [pltpu.VMEM((rows, count), jnp.bfloat16)],
         compiler_params=pltpu.CompilerParams(vmem_limit_bytes=VMEM_LIMIT),
         cost_estimate=COST,
@@ -735,21 +744,23 @@
         return clock.send(shard, rows, [shards - step for step in steps])
 
     rep_index = lax.axis_index("rep")
+    input_matrix = lax.all_gather(
+        weight_piece(input_weight, rep_index), ("shard", "rep"), axis=0, tiled=True
+    )
     shard_vectors = jnp.concatenate([first_gain, second_gain, input_bias])
-    vector_row = jnp.pad(shard_vectors, (0, input_weight.shape[1] - shard_vectors.shape[0]))
-    own_input = jnp.concatenate([weight_piece(input_weight, rep_place), vector_row[None]], axis=0)
-    input_moving = send_around(own_input)
-    output_piece, *gate_blocks = clock(
-        weight_piece(output_weight, rep_index), *blocks_of(column_piece(gate_weight, rep_index))
-    )
+    vector_row = jnp.pad(shard_vectors, (0, output_weight.shape[1] - shard_vectors.shape[0]))
+    own_output = jnp.concatenate(
+        [weight_piece(output_weight, rep_place), vector_row[None]], axis=0
+    )
+    output_moving = send_around(own_output)
+    gate_blocks = clock(*blocks_of(column_piece(gate_weight, rep_index)))
     up_blocks = clock(*blocks_of(column_piece(up_weight, rep_place)))
-    (input_rows,) = clock.wait(input_moving)
-    input_rows = [own_input] + input_rows
-    input_spread = spread(jnp.stack([rows[:part_rows] for rows in input_rows])[None])
-    output_matrix = lax.all_gather(clock(output_piece)[0], ("shard", "rep"), axis=0, tiled=True)
+    (output_rows,) = clock.wait(output_moving)
+    output_rows = [own_output] + output_rows
+
+    output_spread = spread(jnp.stack([rows[:part_rows] for rows in output_rows])[None])
     gate_moving = send_blocks(gate_blocks)
-
-    vector_rows = jnp.stack(in_place_order([rows[part_rows] for rows in input_rows], shard))
+    vector_rows = jnp.stack(in_place_order([rows[part_rows] for rows in output_rows], shard))
     own_gain = first_gain.shape[0]
     gain_one = vector_rows[:, :own_gain].reshape(width).astype(f32)
     gain_two = vector_rows[:, own_gain : 2 * own_gain].reshape(width).astype(f32)
@@ -786,16 +797,27 @@
         key_marks,
         row_marks,
     ) = clock(normed_one, cosine_table, sine_table, signed_sine, key_marks, row_marks)
-
-    input_spread.further()
-    (gate_rows,) = clock.wait(gate_moving)
+    output_arrived, gate_rows = clock.wait(output_spread.moving, gate_moving)
+
+    output_spread.along(output_arrived)
     gate_gathered = lax.all_gather(
         clock(jnp.stack(gate_blocks[:1] + gate_rows))[0][None, :, None], "rep", axis=0, tiled=True
     )
     up_moving = send_blocks(up_blocks)
-    input_spread.over()
-    (input_matrix,) = clock.run(place_blocks, z_order, *input_spread.finish())
-    input_matrix = input_matrix.reshape(width, -1)
+    output_arrived, up_rows = clock.wait(output_spread.moving, up_moving)
+
+    output_spread.over(output_arrived)
+    up_spread = spread(jnp.stack(up_blocks[:1] + up_rows)[None])
+    passed = [[output_cotangent] * 2]
+    passing = clock.pass_on(shard, *passed[-1])
+    output_arrived, up_arrived, arrived = clock.wait(
+        output_spread.moving, up_spread.moving, passing
+    )
+    passed.append(arrived)
+    (output_matrix,) = clock.run(place_blocks, z_order, *output_spread.finish(output_arrived))
+    output_matrix = output_matrix.reshape(width, width)
+
+    input_matrix, normed_one = clock(input_matrix, normed_one)
     projected = jnp.dot(normed_one, input_matrix, preferred_element_type=f32) + shift_row
     key_part = rotate(
         projected[:, query_width : query_width + pair_width].reshape(own_rows, KVH, HD),
@@ -808,37 +830,42 @@
             axis=1,
         ).astype(bf16)
     )
-    (up_rows,) = clock.wait(up_moving)
     pair_moving = send_around(own_pairs)
-    up_spread = spread(jnp.stack(up_blocks[:1] + up_rows)[None])
-    (pair_rows,) = clock.wait(pair_moving)
+    up_spread.along(up_arrived)
+    pair_rows, up_arrived = clock.wait(pair_moving, up_spread.moving)
+
     pairs = jnp.concatenate([own_pairs] + pair_rows, axis=0)
-    far = list(range(2, shards - 1))
-    near = sorted({1, shards - 1})
-    far_moving = clock.send(shard, [output_cotangent] * len(far), far)
-    up_spread.further()
+    up_spread.over(up_arrived)
+    passing = clock.pass_on(shard, *passed[-1]) if shards > 2 else []
     queries, attention_low = clock.run(
         attention_forward, projected, cosine_table, signed_sine, pairs, row_marks.T, key_marks
     )
-    output_matrix, attention_low = clock(output_matrix, attention_low)
     hidden = wide_tokens + jnp.dot(attention_low, output_matrix, preferred_element_type=f32)
     inverse_two = lax.rsqrt(jnp.mean(hidden * hidden, axis=-1, keepdims=True) + EPSILON)
     unit_two = hidden * inverse_two
     (normed_two,) = clock((unit_two * gain_two).astype(bf16))
+    up_arrived, arrived = clock.wait(up_spread.moving, passing)
+    passed.append(arrived)
+
     normed_moving = send_around(normed_two)
-    up_spread.over()
-    (far_arrived,) = clock.wait(far_moving)
-    near_moving = clock.send(shard, [output_cotangent] * (len(near) - 1), near[1:])
-    (up_matrix,) = clock.run(place_blocks, z_order, *up_spread.finish())
-    near_moving = clock.send(shard, [output_cotangent], near[:1]) + near_moving
+    passing = clock.pass_on(shard, *passed[-1]) if shards > 3 else []
+    (up_matrix,) = clock.run(place_blocks, z_order, *up_spread.finish(up_arrived))
     up_matrix = up_matrix.reshape(width, block_units)
     (gate_matrix,) = clock.run(place_gathered, z_order, gate_gathered)
     gate_matrix = gate_matrix.reshape(width, block_units)
-    normed_arrived, near_arrived = clock.wait(normed_moving, near_moving)
+    normed_arrived, arrived = clock.wait(normed_moving, passing)
+    passed.append(arrived)
+    while len(passed) < shards:
+        (arrived,) = clock.wait(clock.pass_on(shard, *passed[-1]))
+        passed.append(arrived)
     group_normed = jnp.concatenate([normed_two] + normed_arrived, axis=0)
-    cotangent_arrived = dict(zip(near + far, near_arrived + far_arrived))
     cotangents = jnp.concatenate(
-        [output_cotangent] + [cotangent_arrived[step] for step in steps], axis=0
+        [output_cotangent]
+        + [
+            jnp.where(shard.place >= step, passed[step][0], passed[shards - step][1])
+            for step in steps
+        ],
+        axis=0,
     )
 
     inner_act, d_gate, d_up, turned_normed, turned_inner = clock.run(
@@ -846,12 +873,13 @@
     )
 
     def start_halving(left, right, groups, turned):
+        count = first.size * second.size
         sent, own = clock.run(
-            lambda left, right: split_gradient(left, right, groups, core.place, turned),
+            lambda left, right: split_gradient(left, right, groups, count, core.place, turned),
             left,
             right,
         )
-        shape = (groups, first.size, second.size, -1, right.shape[1])
+        shape = (first.size, second.size) + own.shape[1:]
         return Halving(clock, sent.reshape(shape), own.reshape(shape), core, first, second)
 
     def side_by_side(rows):
@@ -859,6 +887,15 @@
 
     def sum_over_rep(blocks):
         return lax.psum_scatter(blocks, "rep", scatter_dimension=0, tiled=True)
+
+    def row_sum(own, arrived):
+        return clock(total_of(own + arrived).astype(bf16))[0]
+
+    def send_some(rows, chosen):
+        return clock.send(shard, [rows[k] for k in chosen], [shards - 1 - k for k in chosen])
+
+    edges = sorted({0, shards - 2})
+    inside = list(range(1, shards - 2))
 
     (down_blocks,) = clock.run(
         lambda left, right: ordered_gradient(left, right, 1, list(range(reps))),
@@ -873,7 +910,8 @@
         gate_matrix,
         up_matrix,
     )
-    normed_moving = send_back(normed_partial)
+
+    normed_moving = send_some(normed_partial, edges)
     up = start_halving(turned_normed, d_up, shards, True)
     (gate_blocks,) = clock.run(
         lambda left, right: ordered_gradient(left, right, shards, rep_places(reps)),
@@ -881,17 +919,17 @@
         d_gate,
     )
     gate_piece = sum_over_rep(gate_blocks.reshape(width, block_units))
-    up.along_first()
+    normed_arrived, up_arrived = clock.wait(normed_moving, up.moving)
+
+    up.along_first(up_arrived)
+    normed_moving = send_some(normed_partial, inside)
     block_own, *block_partial = clock.run(
         lambda left, right: rows_product((left,), (right,), False, shards), inner_act, down_weight
     )
-
-    def send_block(at):
-        return clock.send(shard, [block_partial[at]], [shards - 1 - at])
-
-    up.along_second()
-    (normed_arrived,) = clock.wait(normed_moving)
-    normed_two_gradient = total_of([normed_own] + normed_arrived)
+    more_arrived, up_arrived = clock.wait(normed_moving, up.moving)
+
+    up.along_second(up_arrived)
+    normed_two_gradient = total_of([normed_own] + normed_arrived + more_arrived)
     gain_two_gradient = jnp.sum(normed_two_gradient * unit_two, axis=0)
     hidden_gradient = output_cotangent.astype(f32) + norm_back(
         normed_two_gradient, unit_two, inverse_two, gain_two
@@ -908,14 +946,17 @@
         row_marks,
         key_marks.T,
     )
+    (up_arrived,) = clock.wait(up.moving)
+
     pair_moving = send_back(pair_partial)
     output = start_halving(attention_low, branch_gradient, shards, False)
-    up_blocks = clock(*blocks_of(up.finish()))
-    output.along_first()
+    up_blocks = clock(*blocks_of(up.finish(up_arrived)))
+    pair_arrived, output_arrived = clock.wait(pair_moving, output.moving)
+
+    output.along_first(output_arrived)
+    block_moving = send_some(block_partial, edges[:1])
     (down_piece,) = clock(down_piece)
     down_gathered = lax.all_gather(down_piece, "rep", axis=0, tiled=True)
-    (pair_arrived,) = clock.wait(pair_moving)
-    up_moving = send_blocks(up_blocks)
     projected_gradient, bias_sum = clock.run(
         lambda *operands: join_projected(operands[0], operands[3:], *operands[1:3]),
         d_queries,
@@ -925,12 +966,13 @@
         *pair_arrived,
     )
     projected = start_halving(normed_one, projected_gradient, shards, False)
-    output.along_second()
-    projected.along_first()
-    (up_rows,) = clock.wait(up_moving)
-    up_spread = spread(side_by_side(up_blocks[:1] + up_rows))
-    output_blocks = clock(*blocks_of(output.finish()))
-    output_moving = send_blocks(output_blocks)
+    output_arrived, block_arrived, projected_arrived = clock.wait(
+        output.moving, block_moving, projected.moving
+    )
+
+    projected.along_first(projected_arrived)
+    output.along_second(output_arrived)
+    up_moving = send_blocks(up_blocks)
     projected_gradient, hidden_gradient = clock(projected_gradient, hidden_gradient)
     normed_one_gradient = times_transposed(projected_gradient, input_matrix)
     gain_one_gradient = jnp.sum(normed_one_gradient * unit_one, axis=0)
@@ -950,53 +992,73 @@
     (small,) = clock(
         jnp.concatenate([part.reshape(shards, -1) for part in small_parts], axis=1)
     )
-    projected.along_second()
-    up_spread.further()
-    (output_rows,) = clock.wait(output_moving)
-    output_spread = spread(clock(total_of(output_blocks[:1] + output_rows).astype(bf16))[0])
-    block_first = send_block(0)
-    small_moving = clock.send(core, [small], [1])
-    input_blocks = clock(*blocks_of(projected.finish()))
-    output_spread.further()
-    block_first, small_arrived = clock.wait(block_first, small_moving)
-    small = total_of([small] + small_arrived)
+    projected_arrived, output_arrived, up_rows = clock.wait(
+        projected.moving, output.moving, up_moving
+    )
+
+    projected.along_second(projected_arrived)
+    output_blocks = clock(*blocks_of(output.finish(output_arrived)))
+    output_moving = send_blocks(output_blocks)
+    up_spread = spread(side_by_side(up_blocks[:1] + up_rows))
+    projected_arrived, output_rows, up_arrived = clock.wait(
+        projected.moving, output_moving, up_spread.moving
+    )
+
+    up_spread.along(up_arrived)
+    input_blocks = clock(*blocks_of(projected.finish(projected_arrived)))
+    input_moving = send_blocks(input_blocks)
+    output_spread = spread(row_sum(output_blocks[:1], output_rows))
+    up_arrived, input_rows, output_arrived = clock.wait(
+        up_spread.moving, input_moving, output_spread.moving
+    )
+
     (gate_piece,) = clock(gate_piece)
     gate_blocks = clock(*blocks_of(gate_piece.reshape(shards, part_rows, block_units)))
     gate_moving = send_blocks(gate_blocks)
-    output_spread.over()
-    (output_total,) = clock.run(widen_pieces, *output_spread.finish())
-    up_spread.over()
+    output_spread.along(output_arrived)
+    input_spread = spread(row_sum(input_blocks[:1], input_rows))
+    gate_rows, output_arrived, input_arrived = clock.wait(
+        gate_moving, output_spread.moving, input_spread.moving
+    )
+
+    gate_spread = spread(side_by_side(gate_blocks[:1] + gate_rows))
+    input_spread.along(input_arrived)
+    output_spread.over(output_arrived)
+    up_spread.over(up_arrived)
+    block_moving = send_some(block_partial, edges[1:])
+    gate_arrived, input_arrived, output_arrived, up_arrived, more_arrived = clock.wait(
+        gate_spread.moving, input_spread.moving, output_spread.moving, up_spread.moving, block_moving
+    )
+    block_arrived = block_arrived + more_arrived
+
+    gate_spread.along(gate_arrived)
+    input_spread.over(input_arrived)
+    block_moving = send_some(block_partial, inside)
+    small_moving = clock.send(core, [small], [1])
+    (up_total,) = clock.run(widen_pieces, *up_spread.finish(up_arrived))
+    (output_total,) = clock.run(widen_pieces, *output_spread.finish(output_arrived))
+    gate_arrived, input_arrived, more_arrived, small_arrived = clock.wait(
+        gate_spread.moving, input_spread.moving, block_moving, small_moving
+    )
+    block_arrived = block_arrived + more_arrived
+    small = total_of([small] + small_arrived)
+
+    gate_spread.over(gate_arrived)
     small_moving = clock.send(first, [small] * (first.size - 1), range(1, first.size))
-    (gate_rows,) = clock.wait(gate_moving)
-    gate_spread = spread(side_by_side(gate_blocks[:1] + gate_rows))
+    (input_total,) = clock.run(widen_pieces, *input_spread.finish(input_arrived))
+    down_gathered, hidden, block_own = clock(down_gathered, hidden, block_own)
+    (down_total,) = clock(down_gathered.astype(f32))
+    gate_arrived, small_arrived = clock.wait(gate_spread.moving, small_moving)
+    small = total_of([small] + small_arrived)
+
+    small_moving = clock.send(second, [small] * (second.size - 1), range(1, second.size))
+    (gate_total,) = clock.run(widen_pieces, *gate_spread.finish(gate_arrived))
     (small_arrived,) = clock.wait(small_moving)
-    small = total_of([small] + small_arrived)
-    input_moving = send_blocks(input_blocks)
-    (up_total,) = clock.run(widen_pieces, *up_spread.finish())
-    gate_spread.further()
-    (input_rows,) = clock.wait(input_moving)
-    input_spread = spread(clock(total_of(input_blocks[:1] + input_rows).astype(bf16))[0])
-    block_moving = []
-    for at in range(1, len(block_partial) - 1):
-        block_moving += send_block(at)
-    small_moving = clock.send(second, [small] * (second.size - 1), range(1, second.size))
-    input_spread.further()
-    gate_spread.over()
+    small_blocks = clock(*blocks_of(total_of([small] + small_arrived)))
+    small_moving = send_blocks(small_blocks)
+    (block_out,) = clock(total_of([hidden, block_own] + block_arrived).astype(bf16))
     (small_arrived,) = clock.wait(small_moving)
-    small = total_of([small] + small_arrived)
-    input_spread.over()
-    block_last = send_block(len(block_partial) - 1) if len(block_partial) > 1 else []
-    (gate_total,) = clock.run(widen_pieces, *gate_spread.finish())
-    (input_total,) = clock.run(widen_pieces, *input_spread.finish())
-    small_blocks = clock(*blocks_of(small))
-    small_moving = send_blocks(small_blocks)
-    (down_gathered,) = clock(down_gathered)
-    (down_total,) = clock(down_gathered.astype(f32))
-    small_arrived, block_arrived, block_last = clock.wait(small_moving, block_moving, block_last)
     small = total_of(small_blocks[:1] + small_arrived)
-    (block_out,) = clock(
-        total_of([hidden, block_own] + block_first + block_arrived + block_last).astype(bf16)
-    )
 
     small = small + clock.token[0, 0]
     small_totals, at = [], 0

time: 717 us -> 712 us (level)
  waiting for transfers between devices: 282 us -> 298 us
  starting transfers between devices: 123 us -> 112 us
  local copies, waits for them, and re-layouts: 54.3 us -> 44.1 us
    ppermute x0 -> x6, waiting for transfers between devices: none -> 41.8 us  [pass_on(): return lax.ppermute(value, self.name, pairs)]
    ppermute x72 -> x69, waiting for transfers between devices: 282 us -> 256 us  [shift(): return lax.ppermute(value, self.name, self.pairs(step % self.size))]
    ppermute x72 -> x69, starting transfers between devices: 123 us -> 98.5 us  [shift(): return lax.ppermute(value, self.name, self.pairs(step % self.size))]
    ppermute x0 -> x6, starting transfers between devices: none -> 12.9 us  [pass_on(): return lax.ppermute(value, self.name, pairs)]
    optimization_barrier x5 -> x2, local copies, waits for them, and re-layouts: 13.5 us -> 1.89 us  [tie(): return lax.optimization_barrier(arrays)]
    unnamed x141 -> x132, local copies, waits for them, and re-layouts: 10.1 us -> 15.3 us
  transfers between devices with their start and end apart: 77 -> 80, of which waited for: 31 -> 42; matrix products, arithmetic and copies ran while one was open for 17% -> 17% of each run, Pallas kernels for 16% -> 14%
where the time goes in v8:
time: 712 us; the launch traced here: 702 us
  waiting for transfers between devices  298 us (42%)
  Pallas kernels  143 us (20%)
  starting transfers between devices  112 us (16%)
  other arithmetic  75.4 us (11%)
  local copies, waits for them, and re-layouts  44.1 us (6%)
  between operations  15.6 us (2%)
  matrix products  15.4 us (2%)
    ppermute x69, waiting for transfers between devices, shift(): return lax.ppermute(value, self.name, self.pairs(step % self.size))  256 us
    ppermute x69, starting transfers between devices, shift(): return lax.ppermute(value, self.name, self.pairs(step % self.size))  98.5 us
    ppermute x6, waiting for transfers between devices, pass_on(): return lax.ppermute(value, self.name, pairs)  41.8 us
    pallas_call x1, Pallas kernels, feed_forward(): pl.pallas_call(body, grid=(steps,), out_shape=[jax.ShapeDtypeStruct((coun...  23.7 us
    pallas_call x2, Pallas kernels, rows_product(): pl.pallas_call(body, grid=(pl.cdiv(columns, TILE),), out_shape=[jax.Shape...  23.1 us
    pallas_call x4, Pallas kernels, widen_pieces(): pl.pallas_call(body, out_shape=jax.ShapeDtypeStruct((reps, rows, columns)...  21.3 us
    pallas_call x3, Pallas kernels, split_gradient(): pl.pallas_call(body, grid=(pl.cdiv(columns, TILE),), out_shape=[jax.Shape...  20.6 us
    pallas_call x2, Pallas kernels, ordered_gradient(): pl.pallas_call(body, grid=(pl.cdiv(columns, TILE),), out_shape=[jax.Shape...  19.4 us
  transfers between devices with their start and end apart: 80, of which 42 were waited for; matrix products, arithmetic and copies ran while one was open for 17% of the time, Pallas kernels for 14%

profile of v8, /device:TPU:0, one launch (start us, length us, event | category | flops | bytes accessed | tf_op | source)
XLA Modules:
  0.0 702.5 jit_solution(18086784200582730061)
XLA Ops:
  55.1 8.8 %collective-permute-done.4 = bf16[48,2240]{1,0:T(8,128)(2,1)S(1)} collective-permute-done((bf16[48,2240]{1,0:T(8,128)(2,1)}, bf16[48,2240]{1,0:T(8,128)(2,1)S(1)}, u32[]{:S(2)}, u32[]{:S(2)}) %collective-permute-start.4) | collective-permute-done | bytes 215072 | tf_op jit(solution)/shard_map/ppermute | solution.py:68
  63.9 7.6 %collective-permute-done.5 = bf16[48,2240]{1,0:T(8,128)(2,1)S(1)} collective-permute-done((bf16[48,2240]{1,0:T(8,128)(2,1)}, bf16[48,2240]{1,0:T(8,128)(2,1)S(1)}, u32[]{:S(2)}, u32[]{:S(2)}) %collective-permute-start.5) | collective-permute-done | bytes 215072 | tf_op jit(solution)/shard_map/ppermute | solution.py:68
  83.7 10.4 %collective-permute-done.10 = bf16[48,2240]{1,0:T(8,128)(2,1)S(1)} collective-permute-done((bf16[48,2240]{1,0:T(8,128)(2,1)}, bf16[48,2240]{1,0:T(8,128)(2,1)S(1)}, u32[]{:S(2)}, u32[]{:S(2)}) %collective-permute-start.10) | collective-permute-done | bytes 215072 | tf_op jit(solution)/shard_map/ppermute | solution.py:68
  100.5 11.2 %collective-permute-done.9 = bf16[48,2240]{1,0:T(8,128)(2,1)S(1)} collective-permute-done((bf16[48,2240]{1,0:T(8,128)(2,1)}, bf16[48,2240]{1,0:T(8,128)(2,1)S(1)}, u32[]{:S(2)}, u32[]{:S(2)}) %collective-permute-start.9) | collective-permute-done | bytes 215072 | tf_op jit(solution)/shard_map/ppermute | solution.py:68
  120.5 6.8 collective-permute-done.13
  165.6 14.9 %collective-permute-done.18 = bf16[2,1,4,48,2240]{4,3,2,1,0:T(8,128)(2,1)S(1)} collective-permute-done((bf16[2,1,4,48,2240]{4,3,2,1,0:T(8,128)(2,1)S(1)}, bf16[2,1,4,48,2240]{4,3,2,1,0:T(8,128)(2,1)S(1)}, u32[]{:S(2)}, u32[]{:S(2)}) %collective-permute-start.18) | collective-permute-done | bytes 1720352 | tf_op jit(solution)/shard_map/ppermute | solution.py:68
  210.0 7.0 place_blocks.4
  217.1 7.0 place_blocks.5
  239.2 15.9 %collective-permute-done.26 = bf16[160,1536]{1,0:T(8,128)(2,1)S(1)} collective-permute-done((bf16[160,1536]{1,0:T(8,128)(2,1)S(1)}, bf16[160,1536]{1,0:T(8,128)(2,1)S(1)}, u32[]{:S(2)}, u32[]{:S(2)}) %collective-permute-start.26) | collective-permute-done | bytes 491552 | tf_op jit(solution)/shard_map/ppermute | solution.py:73
  255.1 21.0 %collective-permute-done.23 = bf16[160,1536]{1,0:T(8,128)(2,1)S(1)} collective-permute-done((bf16[160,1536]{1,0:T(8,128)(2,1)S(1)}, bf16[160,1536]{1,0:T(8,128)(2,1)S(1)}, u32[]{:S(2)}, u32[]{:S(2)}) %collective-permute-start.23) | collective-permute-done | bytes 491552 | tf_op jit(solution)/shard_map/ppermute | solution.py:68
  280.2 23.7 %feed_forward.1 = (bf16[640,2240]{1,0:T(8,128)(2,1)}, bf16[640,2240]{1,0:T(8,128)(2,1)}, bf16[640,2240]{1,0:T(8,128)(2,1)}, bf16[1536,640]{1,0:T(8,128)(2,1)}, bf16[2240,640]{1,0:T(8,128)(2,1)}) custom-call(bf16[640,1536]{1,0:T(8,128)(2,1)} %pad_maximum_fusion.4.rows_ref, bf16[640,1536]{1,0:T(8,128)(2,1)} %pad_maximum_fusion.5.cotangents_ref.right_ref, ...), custom_call_target="tpu_custom_call" | custom-call | flops 1 | bytes 1 | tf_op jit(solution)/shard_map/feed_forward/pallas_call | solution.py:425
  303.9 9.3 %ordered_gradient.2 = bf16[8,1,280,1536]{3,2,1,0:T(8,128)(2,1)} custom-call(bf16[2240,640]{1,0:T(8,128)(2,1)} %get-tuple-element.624.left_ref, bf16[640,1536]{1,0:T(8,128)(2,1)} %pad_maximum_fusion.5.cotangents_ref.right_ref), custom_call_target="tpu_custom_call" | custom-call | flops 1 | bytes 1 | tf_op jit(solution)/shard_map/ordered_gradient/pallas_call | solution.py:511
  313.3 14.6 %rows_product.2 = (bf16[160,1536]{1,0:T(8,128)(2,1)}, bf16[160,1536]{1,0:T(8,128)(2,1)}, bf16[160,1536]{1,0:T(8,128)(2,1)}, bf16[160,1536]{1,0:T(8,128)(2,1)}) custom-call(bf16[640,2240]{1,0:T(8,128)(2,1)} %get-tuple-element.653.refs_0_.right_ref, bf16[640,2240]{1,0:T(8,128)(2,1)} %get-tuple-element.645.refs_1_.right_ref, bf16[1536,2240]{1,0:T(8,128)(2,1)} %bitcast.193, ...), custom_call_target="tpu_custom_call" | custom-call | flops 1 | bytes 1 | tf_op jit(solution)/shard_map/rows_product/pallas_call | solution.py:551
  327.9 10.6 %split_gradient.3 = (bf16[4,4,48,2240]{3,2,1,0:T(8,128)(2,1)}, bf16[4,4,48,2240]{3,2,1,0:T(8,128)(2,1)}) custom-call(s32[1]{0:T(128)} %bitcast.44.core_ref, bf16[1536,640]{1,0:T(8,128)(2,1)} %get-tuple-element.652.left_ref, bf16[640,2240]{1,0:T(8,128)(2,1)} %get-tuple-element.645.refs_1_.right_ref), custom_call_target="tpu_custom_call" | custom-call | flops 1 | bytes 1 | tf_op jit(solution)/shard_map/split_gradient/pallas_call | solution.py:481
  338.5 7.7 %collective-permute-start.27 = (bf16[160,1536]{1,0:T(8,128)(2,1)S(1)}, bf16[160,1536]{1,0:T(8,128)(2,1)S(1)}, u32[]{:S(2)}, u32[]{:S(2)}) collective-permute-start(bf16[160,1536]{1,0:T(8,128)(2,1)S(1)} %copy-done.57), channel_id=1, source_target_pairs={{0,3},{1,0},{2,1},{3,2},{4,7},{5,4},{6,5},{7,6},{8,11},{9,8},{10,9... | collective-permute-start | bytes 1474568 | tf_op jit(solution)/shard_map/ppermute | solution.py:68
  348.4 10.1 %ordered_gradient.3 = bf16[8,4,48,2240]{3,2,1,0:T(8,128)(2,1)} custom-call(bf16[1536,640]{1,0:T(8,128)(2,1)} %get-tuple-element.652.left_ref, bf16[640,2240]{1,0:T(8,128)(2,1)} %get-tuple-element.653.refs_0_.right_ref), custom_call_target="tpu_custom_call" | custom-call | flops 1 | bytes 1 | tf_op jit(solution)/shard_map/ordered_gradient/pallas_call | solution.py:511
  360.1 10.8 %collective-permute-done.28 = bf16[160,1536]{1,0:T(8,128)(2,1)S(1)} collective-permute-done((bf16[160,1536]{1,0:T(8,128)(2,1)S(1)}, bf16[160,1536]{1,0:T(8,128)(2,1)S(1)}, u32[]{:S(2)}, u32[]{:S(2)}) %collective-permute-start.28) | collective-permute-done | bytes 491552 | tf_op jit(solution)/shard_map/ppermute | solution.py:68
  375.9 8.5 %rows_product.3 = (bf16[160,1536]{1,0:T(8,128)(2,1)}, bf16[160,1536]{1,0:T(8,128)(2,1)}, bf16[160,1536]{1,0:T(8,128)(2,1)}, bf16[160,1536]{1,0:T(8,128)(2,1)}) custom-call(bf16[640,2240]{1,0:T(8,128)(2,1)} %get-tuple-element.666.refs_0_, bf16[2240,1536]{1,0:T(8,128)(2,1)} %refs_1_), custom_call_target="tpu_custom_call" | custom-call | flops 1 | bytes 1 | tf_op jit(solution)/shard_map/rows_product/pallas_call | solution.py:551
  384.4 15.4 %collective-permute-done.30 = bf16[160,1536]{1,0:T(8,128)(2,1)S(1)} collective-permute-done((bf16[160,1536]{1,0:T(8,128)(2,1)}, bf16[160,1536]{1,0:T(8,128)(2,1)S(1)}, u32[]{:S(2)}, u32[]{:S(2)}) %collective-permute-start.30) | collective-permute-done | bytes 491552 | tf_op jit(solution)/shard_map/ppermute | solution.py:68
  411.1 7.5 %attention_backward.1 = (bf16[160,1536]{1,0:T(8,128)(2,1)}, bf16[160,512]{1,0:T(8,128)(2,1)}, bf16[160,512]{1,0:T(8,128)(2,1)}, bf16[160,512]{1,0:T(8,128)(2,1)}, bf16[160,512]{1,0:T(8,128)(2,1)}) custom-call(bf16[2,960,128]{2,1,0:T(8,128)(2,1)} %get-tuple-element.688.queries_ref, bf16[160,1536]{1,0:T(8,128)(2,1)} %convolution_convert_fusion.gradient_ref, ...), custom_call_target="tpu_custom_call" | custom-call | flops 1 | bytes 1 | tf_op jit(solution)/shard_map/attention_backward/pallas_call | solution.py:653
  434.1 10.1 %collective-permute-done.34.refs_2_ = bf16[160,512]{1,0:T(8,128)(2,1)} collective-permute-done((bf16[160,512]{1,0:T(8,128)(2,1)}, bf16[160,512]{1,0:T(8,128)(2,1)}, u32[]{:S(2)}, u32[]{:S(2)}) %collective-permute-start.34) | collective-permute-done | bytes 163872 | tf_op jit(solution)/shard_map/ppermute | solution.py:68
  456.4 12.8 %collective-permute-done.38 = bf16[160,1536]{1,0:T(8,128)(2,1)S(1)} collective-permute-done((bf16[160,1536]{1,0:T(8,128)(2,1)S(1)}, bf16[160,1536]{1,0:T(8,128)(2,1)S(1)}, u32[]{:S(2)}, u32[]{:S(2)}) %collective-permute-start.38) | collective-permute-done | bytes 491552 | tf_op jit(solution)/shard_map/ppermute | solution.py:68
  495.0 8.0 %collective-permute-done.43 = bf16[48,2240]{1,0:T(8,128)(2,1)} collective-permute-done((bf16[48,2240]{1,0:T(8,128)(2,1)}, bf16[48,2240]{1,0:T(8,128)(2,1)}, u32[]{:S(2)}, u32[]{:S(2)}) %collective-permute-start.43) | collective-permute-done | bytes 215072 | tf_op jit(solution)/shard_map/ppermute | solution.py:68
  507.2 13.7 %collective-permute-done.40 = bf16[2,4,48,2048]{3,2,1,0:T(8,128)(2,1)} collective-permute-done((bf16[2,4,48,2048]{3,2,1,0:T(8,128)(2,1)}, bf16[2,4,48,2048]{3,2,1,0:T(8,128)(2,1)}, u32[]{:S(2)}, u32[]{:S(2)}) %collective-permute-start.40) | collective-permute-done | bytes 1572896 | tf_op jit(solution)/shard_map/ppermute | solution.py:68
  542.9 8.0 %collective-permute-done.45 = bf16[4,48,2048]{2,1,0:T(8,128)(2,1)S(1)} collective-permute-done((bf16[4,48,2048]{2,1,0:T(8,128)(2,1)}, bf16[4,48,2048]{2,1,0:T(8,128)(2,1)S(1)}, u32[]{:S(2)}, u32[]{:S(2)}) %collective-permute-start.45) | collective-permute-done | bytes 786464 | tf_op jit(solution)/shard_map/ppermute | solution.py:68
  573.6 11.7 %collective-permute-done.50 = bf16[2,48,8960]{2,1,0:T(8,128)(2,1)} collective-permute-done((bf16[2,48,8960]{2,1,0:T(8,128)(2,1)}, bf16[2,48,8960]{2,1,0:T(8,128)(2,1)}, u32[]{:S(2)}, u32[]{:S(2)}) %collective-permute-start.50) | collective-permute-done | bytes 1720352 | tf_op jit(solution)/shard_map/ppermute | solution.py:68
  601.1 6.7 collective-permute-done.56
  618.9 8.8 %collective-permute-done.61 = bf16[2,48,2048]{2,1,0:T(8,128)(2,1)S(1)} collective-permute-done((bf16[2,48,2048]{2,1,0:T(8,128)(2,1)S(1)}, bf16[2,48,2048]{2,1,0:T(8,128)(2,1)S(1)}, u32[]{:S(2)}, u32[]{:S(2)}) %collective-permute-start.61) | collective-permute-done | bytes 393248 | tf_op jit(solution)/shard_map/ppermute | solution.py:68
  636.2 7.3 %widen_pieces.4 = f32[8,48,8960]{2,1,0:T(8,128)} custom-call(s32[8]{0:T(128)} %stack.255.places_ref, bf16[4,48,8960]{2,1,0:T(8,128)(2,1)} %pad_maximum_fusion.1.pieces_ref, bf16[4,48,8960]{2,1,0:T(8,128)(2,1)} %copy-done.7), custom_call_target="tpu_custom_call" | custom-call | flops 1 | bytes 1 | tf_op jit(solution)/shard_map/widen_pieces/pallas_call | solution.py:363
  646.6 13.2 %collective-permute-done.67 = bf16[160,1536]{1,0:T(8,128)(2,1)S(1)} collective-permute-done((bf16[160,1536]{1,0:T(8,128)(2,1)}, bf16[160,1536]{1,0:T(8,128)(2,1)S(1)}, u32[]{:S(2)}, u32[]{:S(2)}) %collective-permute-start.67) | collective-permute-done | bytes 491552 | tf_op jit(solution)/shard_map/ppermute | solution.py:68
  668.0 10.1 %convert_element_type.347 = f32[2240,1536]{1,0:T(8,128)} convert(bf16[2240,1536]{1,0:T(8,128)(2,1)} %all-gather.6.cloned.1.call-done) | non-fusion elementwise | flops 3440640 | bytes 20643840 | tf_op jit(solution)/shard_map/convert_element_type | solution.py:1050
  679.0 7.4 %widen_pieces.7 = f32[8,48,8960]{2,1,0:T(8,128)} custom-call(s32[8]{0:T(128)} %stack.255.places_ref, bf16[4,48,8960]{2,1,0:T(8,128)(2,1)} %pad_maximum_fusion.2.pieces_ref, bf16[4,48,8960]{2,1,0:T(8,128)(2,1)} %collective-permute-done.69.others_ref), custom_call_target="tpu_custom_call" | custom-call | flops 1 | bytes 1 | tf_op jit(solution)/shard_map/widen_pieces/pallas_call | solution.py:363
  (419 shorter events, 340.4 us)
Async XLA Ops:
  7.2 136.5 %all-gather.8.cloned.1.call-start = ((), (), s32[]{:S(2)}) async-start(), calls=%async_computation.5 | async-start | bytes 6488064 | tf_op jit(solution)/shard_map/all_gather | solution.py:747
  9.3 207.7 %all-gather.10.cloned.1.call-start = ((), (), s32[]{:S(2)}) async-start(), calls=%async_computation.6 | async-start | bytes 7962624 | tf_op jit(solution)/shard_map/all_gather | solution.py:803
  11.8 31.1 %collective-permute-start = (bf16[49,1536]{1,0:T(8,128)(2,1)}, bf16[49,1536]{1,0:T(8,128)(2,1)}, u32[]{:S(2)}, u32[]{:S(2)}) collective-permute-start(bf16[49,1536]{1,0:T(8,128)(2,1)} %pad_maximum_fusion.17), channel_id=1, source_target_pairs={{0,1},{1,2},{2,3},{3,0},{4,5},{5,6},{6,7},{7,4},{8,9},{9,10},{10,1... | collective-permute-start | bytes 451592 | tf_op jit(solution)/shard_map/ppermute | solution.py:68
  14.8 28.1 %collective-permute-start.1 = (bf16[49,1536]{1,0:T(8,128)(2,1)}, bf16[49,1536]{1,0:T(8,128)(2,1)}, u32[]{:S(2)}, u32[]{:S(2)}) collective-permute-start(bf16[49,1536]{1,0:T(8,128)(2,1)} %pad_maximum_fusion.17), channel_id=1, source_target_pairs={{0,2},{1,3},{2,0},{3,1},{4,6},{5,7},{6,4},{7,5},{8,10},{9,11},{10,... | collective-permute-start | bytes 451592 | tf_op jit(solution)/shard_map/ppermute | solution.py:68
  17.4 25.5 %collective-permute-start.2 = (bf16[49,1536]{1,0:T(8,128)(2,1)}, bf16[49,1536]{1,0:T(8,128)(2,1)}, u32[]{:S(2)}, u32[]{:S(2)}) collective-permute-start(bf16[49,1536]{1,0:T(8,128)(2,1)} %pad_maximum_fusion.17), channel_id=1, source_target_pairs={{0,3},{1,0},{2,1},{3,2},{4,7},{5,4},{6,5},{7,6},{8,11},{9,8},{10,9... | collective-permute-start | bytes 451592 | tf_op jit(solution)/shard_map/ppermute | solution.py:68
  48.2 23.4 %collective-permute-start.3 = (bf16[1,4,48,1536]{3,2,1,0:T(8,128)(2,1)S(1)}, bf16[1,4,48,1536]{3,2,1,0:T(8,128)(2,1)S(1)}, u32[]{:S(2)}, u32[]{:S(2)}) collective-permute-start(bf16[1,4,48,1536]{3,2,1,0:T(8,128)(2,1)S(1)} %get-tuple-element.495), channel_id=1, source_target_pairs={{0,16},{4,12},{8,24},{12,4},{16,0},{20,28},{24,8},{28,20},{1,17},{... | collective-permute-start | bytes 1769480 | tf_op jit(solution)/shard_map/ppermute | solution.py:68
  73.8 373.1 %reduce-scatter.3.cloned.1.call-start = ((), (), s32[]{:S(2)}) async-start(), calls=%async_computation.2 | async-start | bytes 7741440 | tf_op jit(solution)/shard_map/reduce_scatter | solution.py:889
  73.9 37.8 %collective-permute-start.7 = (bf16[2,1,4,48,1536]{4,3,2,1,0:T(8,128)(2,1)S(1)}, bf16[2,1,4,48,1536]{4,3,2,1,0:T(8,128)(2,1)S(1)}, u32[]{:S(2)}, u32[]{:S(2)}) collective-permute-start(bf16[2,1,4,48,1536]{4,3,2,1,0:T(8,128)(2,1)S(1)} %pad_maximum_fusion.9), channel_id=1, source_target_pairs={{0,8},{4,20},{8,0},{12,28},{16,24},{20,4},{24,16},{28,12},{1,9},{5... | collective-permute-start | bytes 3538952 | tf_op jit(solution)/shard_map/ppermute | solution.py:68
  82.3 29.4 %collective-permute-start.9 = (bf16[48,2240]{1,0:T(8,128)(2,1)}, bf16[48,2240]{1,0:T(8,128)(2,1)S(1)}, u32[]{:S(2)}, u32[]{:S(2)}) collective-permute-start(bf16[48,2240]{1,0:T(8,128)(2,1)} %bitcast.246), channel_id=1, source_target_pairs={{0,2},{1,3},{2,0},{3,1},{4,6},{5,7},{6,4},{7,5},{8,10},{9,11},{10,... | collective-permute-start | bytes 645128 | tf_op jit(solution)/shard_map/ppermute | solution.py:68
  113.3 23.8 %collective-permute-start.11 = (bf16[4,1,4,48,1536]{4,3,2,1,0:T(8,128)(2,1)}, bf16[4,1,4,48,1536]{4,3,2,1,0:T(8,128)(2,1)}, u32[]{:S(2)}, u32[]{:S(2)}) collective-permute-start(bf16[4,1,4,48,1536]{4,3,2,1,0:T(8,128)(2,1)} %pad_maximum_fusion.3.pieces_ref), channel_id=1, source_target_pairs={{0,4},{4,0},{8,12},{12,8},{16,20},{20,16},{24,28},{28,24},{1,5},{5... | collective-permute-start | bytes 7077896 | tf_op jit(solution)/shard_map/ppermute | solution.py:68
  114.4 22.7 %collective-permute-start.12 = (bf16[1,4,48,2240]{3,2,1,0:T(8,128)(2,1)}, bf16[1,4,48,2240]{3,2,1,0:T(8,128)(2,1)S(1)}, u32[]{:S(2)}, u32[]{:S(2)}) collective-permute-start(bf16[1,4,48,2240]{3,2,1,0:T(8,128)(2,1)} %get-tuple-element.525), channel_id=1, source_target_pairs={{0,16},{4,12},{8,24},{12,4},{16,0},{20,28},{24,8},{28,20},{1,17},{... | collective-permute-start | bytes 2580488 | tf_op jit(solution)/shard_map/ppermute | solution.py:68
  150.4 30.1 %collective-permute-start.18 = (bf16[2,1,4,48,2240]{4,3,2,1,0:T(8,128)(2,1)S(1)}, bf16[2,1,4,48,2240]{4,3,2,1,0:T(8,128)(2,1)S(1)}, u32[]{:S(2)}, u32[]{:S(2)}) collective-permute-start(bf16[2,1,4,48,2240]{4,3,2,1,0:T(8,128)(2,1)S(1)} %copy-done.20), channel_id=1, source_target_pairs={{0,8},{4,20},{8,0},{12,28},{16,24},{20,4},{24,16},{28,12},{1,9},{5... | collective-permute-start | bytes 5160968 | tf_op jit(solution)/shard_map/ppermute | solution.py:68
  182.5 27.5 %collective-permute-start.19 = (bf16[4,1,4,48,2240]{4,3,2,1,0:T(8,128)(2,1)}, bf16[4,1,4,48,2240]{4,3,2,1,0:T(8,128)(2,1)}, u32[]{:S(2)}, u32[]{:S(2)}) collective-permute-start(bf16[4,1,4,48,2240]{4,3,2,1,0:T(8,128)(2,1)} %pad_maximum_fusion.pieces_ref), channel_id=1, source_target_pairs={{0,4},{4,0},{8,12},{12,8},{16,20},{20,16},{24,28},{28,24},{1,5},{5... | collective-permute-start | bytes 10321928 | tf_op jit(solution)/shard_map/ppermute | solution.py:68
  227.6 27.5 %collective-permute-start.26 = (bf16[160,1536]{1,0:T(8,128)(2,1)S(1)}, bf16[160,1536]{1,0:T(8,128)(2,1)S(1)}, u32[]{:S(2)}, u32[]{:S(2)}) collective-permute-start(bf16[160,1536]{1,0:T(8,128)(2,1)S(1)} %collective-permute-done.21), channel_id=1, source_target_pairs={{1,0},{2,1},{3,2},{5,4},{6,5},{7,6},{9,8},{10,9},{11,10},{13,12},{... | collective-permute-start | bytes 1474568 | tf_op jit(solution)/shard_map/ppermute | solution.py:73
  228.9 26.2 %collective-permute-start.22 = (bf16[160,1536]{1,0:T(8,128)(2,1)S(1)}, bf16[160,1536]{1,0:T(8,128)(2,1)S(1)}, u32[]{:S(2)}, u32[]{:S(2)}) collective-permute-start(bf16[160,1536]{1,0:T(8,128)(2,1)S(1)} %multiply_convert_fusion), channel_id=1, source_target_pairs={{0,1},{1,2},{2,3},{3,0},{4,5},{5,6},{6,7},{7,4},{8,9},{9,10},{10,1... | collective-permute-start | bytes 1474568 | tf_op jit(solution)/shard_map/ppermute | solution.py:68
  231.6 44.5 %collective-permute-start.23 = (bf16[160,1536]{1,0:T(8,128)(2,1)S(1)}, bf16[160,1536]{1,0:T(8,128)(2,1)S(1)}, u32[]{:S(2)}, u32[]{:S(2)}) collective-permute-start(bf16[160,1536]{1,0:T(8,128)(2,1)S(1)} %multiply_convert_fusion), channel_id=1, source_target_pairs={{0,2},{1,3},{2,0},{3,1},{4,6},{5,7},{6,4},{7,5},{8,10},{9,11},{10,... | collective-permute-start | bytes 1474568 | tf_op jit(solution)/shard_map/ppermute | solution.py:68
  232.6 43.6 %collective-permute-start.24 = (bf16[160,1536]{1,0:T(8,128)(2,1)S(1)}, bf16[160,1536]{1,0:T(8,128)(2,1)S(1)}, u32[]{:S(2)}, u32[]{:S(2)}) collective-permute-start(bf16[160,1536]{1,0:T(8,128)(2,1)S(1)} %multiply_convert_fusion), channel_id=1, source_target_pairs={{0,3},{1,0},{2,1},{3,2},{4,7},{5,4},{6,5},{7,6},{8,11},{9,8},{10,9... | collective-permute-start | bytes 1474568 | tf_op jit(solution)/shard_map/ppermute | solution.py:68
  313.2 272.1 %reduce-scatter.5.cloned.1.call-start = ((), (), s32[]{:S(2)}) async-start(), calls=%async_computation.3 | async-start | bytes 7962624 | tf_op jit(solution)/shard_map/reduce_scatter | solution.py:889
  338.5 32.4 %collective-permute-start.29 = (bf16[2,2,4,48,2240]{4,3,2,1,0:T(8,128)(2,1)}, bf16[2,2,4,48,2240]{4,3,2,1,0:T(8,128)(2,1)}, u32[]{:S(2)}, u32[]{:S(2)}) collective-permute-start(bf16[2,2,4,48,2240]{4,3,2,1,0:T(8,128)(2,1)} %bitcast.264), channel_id=1, source_target_pairs={{0,4},{4,0},{8,12},{12,8},{16,20},{20,16},{24,28},{28,24},{1,5},{5... | collective-permute-start | bytes 10321928 | tf_op jit(solution)/shard_map/ppermute | solution.py:68
  338.5 21.6 %collective-permute-start.27 = (bf16[160,1536]{1,0:T(8,128)(2,1)S(1)}, bf16[160,1536]{1,0:T(8,128)(2,1)S(1)}, u32[]{:S(2)}, u32[]{:S(2)}) collective-permute-start(bf16[160,1536]{1,0:T(8,128)(2,1)S(1)} %copy-done.57), channel_id=1, source_target_pairs={{0,3},{1,0},{2,1},{3,2},{4,7},{5,4},{6,5},{7,6},{8,11},{9,8},{10,9... | collective-permute-start | bytes 1474568 | tf_op jit(solution)/shard_map/ppermute | solution.py:68
  346.2 24.8 %collective-permute-start.28 = (bf16[160,1536]{1,0:T(8,128)(2,1)S(1)}, bf16[160,1536]{1,0:T(8,128)(2,1)S(1)}, u32[]{:S(2)}, u32[]{:S(2)}) collective-permute-start(bf16[160,1536]{1,0:T(8,128)(2,1)S(1)} %copy-done.56), channel_id=1, source_target_pairs={{0,1},{1,2},{2,3},{3,0},{4,5},{5,6},{6,7},{7,4},{8,9},{9,10},{10,1... | collective-permute-start | bytes 1474568 | tf_op jit(solution)/shard_map/ppermute | solution.py:68
  374.6 27.9 %collective-permute-start.31 = (bf16[2,4,48,2240]{3,2,1,0:T(8,128)(2,1)}, bf16[2,4,48,2240]{3,2,1,0:T(8,128)(2,1)}, u32[]{:S(2)}, u32[]{:S(2)}) collective-permute-start(bf16[2,4,48,2240]{3,2,1,0:T(8,128)(2,1)} %fusion), channel_id=1, source_target_pairs={{0,8},{4,20},{8,0},{12,28},{16,24},{20,4},{24,16},{28,12},{1,9},{5... | collective-permute-start | bytes 5160968 | tf_op jit(solution)/shard_map/ppermute | solution.py:68
  374.7 25.1 %collective-permute-start.30 = (bf16[160,1536]{1,0:T(8,128)(2,1)}, bf16[160,1536]{1,0:T(8,128)(2,1)S(1)}, u32[]{:S(2)}, u32[]{:S(2)}) collective-permute-start(bf16[160,1536]{1,0:T(8,128)(2,1)} %get-tuple-element.673), channel_id=1, source_target_pairs={{0,2},{1,3},{2,0},{3,1},{4,6},{5,7},{6,4},{7,5},{8,10},{9,11},{10,... | collective-permute-start | bytes 1474568 | tf_op jit(solution)/shard_map/ppermute | solution.py:68
  454.5 213.4 %all-gather.6.cloned.1.call-start = ((), (), s32[]{:S(2)}) async-start(), calls=%async_computation.4 | async-start | bytes 7741440 | tf_op jit(solution)/shard_map/all_gather | solution.py:959
  474.9 46.0 %collective-permute-start.40 = (bf16[2,4,48,2048]{3,2,1,0:T(8,128)(2,1)}, bf16[2,4,48,2048]{3,2,1,0:T(8,128)(2,1)}, u32[]{:S(2)}, u32[]{:S(2)}) collective-permute-start(bf16[2,4,48,2048]{3,2,1,0:T(8,128)(2,1)} %fusion.4), channel_id=1, source_target_pairs={{0,8},{4,20},{8,0},{12,28},{16,24},{20,4},{24,16},{28,12},{1,9},{5... | collective-permute-start | bytes 4718600 | tf_op jit(solution)/shard_map/ppermute | solution.py:68
  478.1 29.1 %collective-permute-start.41 = (bf16[4,48,1536]{2,1,0:T(8,128)(2,1)}, bf16[4,48,1536]{2,1,0:T(8,128)(2,1)}, u32[]{:S(2)}, u32[]{:S(2)}) collective-permute-start(bf16[4,48,1536]{2,1,0:T(8,128)(2,1)} %fusion.15), channel_id=1, source_target_pairs={{0,16},{4,12},{8,24},{12,4},{16,0},{20,28},{24,8},{28,20},{1,17},{... | collective-permute-start | bytes 1769480 | tf_op jit(solution)/shard_map/ppermute | solution.py:68
  528.9 22.0 %collective-permute-start.49 = (bf16[48,8960]{1,0:T(8,128)(2,1)S(1)}, bf16[48,8960]{1,0:T(8,128)(2,1)S(1)}, u32[]{:S(2)}, u32[]{:S(2)}) collective-permute-start(bf16[48,8960]{1,0:T(8,128)(2,1)S(1)} %concatenate.75), channel_id=1, source_target_pairs={{0,16},{4,12},{8,24},{12,4},{16,0},{20,28},{24,8},{28,20},{1,17},{... | collective-permute-start | bytes 2580488 | tf_op jit(solution)/shard_map/ppermute | solution.py:68
  529.1 21.7 %collective-permute-start.45 = (bf16[4,48,2048]{2,1,0:T(8,128)(2,1)}, bf16[4,48,2048]{2,1,0:T(8,128)(2,1)S(1)}, u32[]{:S(2)}, u32[]{:S(2)}) collective-permute-start(bf16[4,48,2048]{2,1,0:T(8,128)(2,1)} %fusion.7), channel_id=1, source_target_pairs={{0,16},{4,12},{8,24},{12,4},{16,0},{20,28},{24,8},{28,20},{1,17},{... | collective-permute-start | bytes 2359304 | tf_op jit(solution)/shard_map/ppermute | solution.py:68
  552.2 33.1 %collective-permute-start.50 = (bf16[2,48,8960]{2,1,0:T(8,128)(2,1)}, bf16[2,48,8960]{2,1,0:T(8,128)(2,1)}, u32[]{:S(2)}, u32[]{:S(2)}) collective-permute-start(bf16[2,48,8960]{2,1,0:T(8,128)(2,1)} %pad_maximum_fusion.7), channel_id=1, source_target_pairs={{0,8},{4,20},{8,0},{12,28},{16,24},{20,4},{24,16},{28,12},{1,9},{5... | collective-permute-start | bytes 5160968 | tf_op jit(solution)/shard_map/ppermute | solution.py:68
  633.7 26.1 %collective-permute-start.65 = (bf16[2,48,8960]{2,1,0:T(8,128)(2,1)}, bf16[2,48,8960]{2,1,0:T(8,128)(2,1)}, u32[]{:S(2)}, u32[]{:S(2)}) collective-permute-start(bf16[2,48,8960]{2,1,0:T(8,128)(2,1)} %pad_maximum_fusion.8), channel_id=1, source_target_pairs={{0,8},{4,20},{8,0},{12,28},{16,24},{20,4},{24,16},{28,12},{1,9},{5... | collective-permute-start | bytes 5160968 | tf_op jit(solution)/shard_map/ppermute | solution.py:68
  634.4 25.4 %collective-permute-start.66 = (bf16[4,48,2048]{2,1,0:T(8,128)(2,1)S(1)}, bf16[4,48,2048]{2,1,0:T(8,128)(2,1)}, u32[]{:S(2)}, u32[]{:S(2)}) collective-permute-start(bf16[4,48,2048]{2,1,0:T(8,128)(2,1)S(1)} %pad_maximum_fusion.12.pieces_ref), channel_id=1, source_target_pairs={{0,4},{4,0},{8,12},{12,8},{16,20},{20,16},{24,28},{28,24},{1,5},{5... | collective-permute-start | bytes 2359304 | tf_op jit(solution)/shard_map/ppermute | solution.py:68
  634.5 25.3 %collective-permute-start.67 = (bf16[160,1536]{1,0:T(8,128)(2,1)}, bf16[160,1536]{1,0:T(8,128)(2,1)S(1)}, u32[]{:S(2)}, u32[]{:S(2)}) collective-permute-start(bf16[160,1536]{1,0:T(8,128)(2,1)} %get-tuple-element.889), channel_id=1, source_target_pairs={{0,2},{1,3},{2,0},{3,1},{4,6},{5,7},{6,4},{7,5},{8,10},{9,11},{10,... | collective-permute-start | bytes 1474568 | tf_op jit(solution)/shard_map/ppermute | solution.py:68
  (108 other events, 1719.5 us)
Sparse Core Ops, SparseCore 0:
  10.9 100.4 all-gather.7
  113.8 54.3 all-gather.9
  313.3 74.8 reduce-scatter.2
  454.7 81.6 reduce-scatter.4
  562.8 55.6 all-gather.5

commit v9 on v8

--- a/solution.py
+++ b/solution.py
@@ -260,6 +260,53 @@
         placed += [(core.behind(1), far.behind(one), near.behind(two)) for one, two in offsets]
         places = [(c * first.size + f) * second.size + s for c, f, s in placed]
         return [jnp.stack(places).astype(jnp.int32), self.pieces, others]
+
+
+def column_blocks(place, shard_place, *weights):
+    count = len(weights)
+    rows, columns = weights[0].shape[1:]
+    shards = lax.axis_size("shard")
+    block = columns // shards
+
+    def body(places_ref, *refs):
+        sources, outs = refs[:count], refs[count : 2 * count]
+        held, cut, in_sems, out_sems = refs[2 * count :]
+        loads = [
+            pltpu.make_async_copy(sources[at].at[places_ref[0]], held.at[at], in_sems.at[at])
+            for at in range(count)
+        ]
+
+        def store(at, z):
+            ahead = lax.rem(z + shards - places_ref[1], shards)
+            return pltpu.make_async_copy(cut.at[at, z], outs[at].at[ahead], out_sems.at[at, z])
+
+        for load in loads:
+            load.start()
+        for at in range(count):
+            loads[at].wait()
+            for z in range(shards):
+                cut[at, z] = held[at, :, z * block : (z + 1) * block]
+                store(at, z).start()
+        for at in range(count):
+            for z in range(shards):
+                store(at, z).wait()
+
+    return pl.pallas_call(
+        body,
+        out_shape=[jax.ShapeDtypeStruct((shards, rows, block), jnp.bfloat16)] * count,
+        in_specs=[pl.BlockSpec(memory_space=pltpu.SMEM)]
+        + [pl.BlockSpec(memory_space=pl.ANY)] * count,
+        out_specs=[pl.BlockSpec(memory_space=pl.ANY)] * count,
+        scratch_shapes=[
+            pltpu.VMEM((count, rows, columns), jnp.bfloat16),
+            pltpu.VMEM((count, shards, rows, block), jnp.bfloat16),
+            pltpu.SemaphoreType.DMA((count,)),
+            pltpu.SemaphoreType.DMA((count, shards)),
+        ],
+        compiler_params=pltpu.CompilerParams(vmem_limit_bytes=VMEM_LIMIT),
+        cost_estimate=COST,
+        name="column_blocks",
+    )(jnp.stack([place, shard_place]).astype(jnp.int32), *weights)
 
 
 def place_blocks(order, places, pieces, others):
@@ -723,9 +770,6 @@
     def weight_piece(weight, place):
         return pick(weight.reshape(reps, part_rows, weight.shape[1]), place, 0)
 
-    def column_piece(weight, place):
-        return weight_piece(weight, place).reshape(part_rows, shards, block_units).transpose(1, 0, 2)
-
     def spread(piece):
         return Spread(clock, piece, core, first, second)
 
@@ -753,8 +797,11 @@
         [weight_piece(output_weight, rep_place), vector_row[None]], axis=0
     )
     output_moving = send_around(own_output)
-    gate_blocks = clock(*blocks_of(column_piece(gate_weight, rep_index)))
-    up_blocks = clock(*blocks_of(column_piece(up_weight, rep_place)))
+    gate_blocks, up_blocks = clock.run(
+        lambda *weights: column_blocks(rep_index, shard.place, *weights),
+        gate_weight.reshape(reps, part_rows, hidden_units),
+        up_weight.reshape(reps, part_rows, hidden_units),
+    )
     (output_rows,) = clock.wait(output_moving)
     output_rows = [own_output] + output_rows
 
@@ -800,23 +847,22 @@
     output_arrived, gate_rows = clock.wait(output_spread.moving, gate_moving)
 
     output_spread.along(output_arrived)
-    gate_gathered = lax.all_gather(
-        clock(jnp.stack(gate_blocks[:1] + gate_rows))[0][None, :, None], "rep", axis=0, tiled=True
-    )
     up_moving = send_blocks(up_blocks)
     output_arrived, up_rows = clock.wait(output_spread.moving, up_moving)
 
+    gate_up = jnp.stack(
+        [jnp.stack([gate_blocks[0]] + gate_rows), jnp.stack([up_blocks[0]] + up_rows)], axis=1
+    )
+    gate_up = lax.all_gather(clock(gate_up)[0][None], "rep", axis=0, tiled=True)
+    passed = [[output_cotangent] * 2]
     output_spread.over(output_arrived)
-    up_spread = spread(jnp.stack(up_blocks[:1] + up_rows)[None])
-    passed = [[output_cotangent] * 2]
     passing = clock.pass_on(shard, *passed[-1])
-    output_arrived, up_arrived, arrived = clock.wait(
-        output_spread.moving, up_spread.moving, passing
-    )
+    output_arrived, arrived = clock.wait(output_spread.moving, passing)
     passed.append(arrived)
+
+    passing = clock.pass_on(shard, *passed[-1]) if shards > 2 else []
     (output_matrix,) = clock.run(place_blocks, z_order, *output_spread.finish(output_arrived))
     output_matrix = output_matrix.reshape(width, width)
-
     input_matrix, normed_one = clock(input_matrix, normed_one)
     projected = jnp.dot(normed_one, input_matrix, preferred_element_type=f32) + shift_row
     key_part = rotate(
@@ -830,13 +876,13 @@
             axis=1,
         ).astype(bf16)
     )
-    pair_moving = send_around(own_pairs)
-    up_spread.along(up_arrived)
-    pair_rows, up_arrived = clock.wait(pair_moving, up_spread.moving)
-
+    (arrived,) = clock.wait(passing)
+    passed.append(arrived)
+
+    (pair_rows,) = clock.wait(send_around(own_pairs))
     pairs = jnp.concatenate([own_pairs] + pair_rows, axis=0)
-    up_spread.over(up_arrived)
-    passing = clock.pass_on(shard, *passed[-1]) if shards > 2 else []
+
+    passing = clock.pass_on(shard, *passed[-1]) if shards > 3 else []
     queries, attention_low = clock.run(
         attention_forward, projected, cosine_table, signed_sine, pairs, row_marks.T, key_marks
     )
@@ -844,17 +890,14 @@
     inverse_two = lax.rsqrt(jnp.mean(hidden * hidden, axis=-1, keepdims=True) + EPSILON)
     unit_two = hidden * inverse_two
     (normed_two,) = clock((unit_two * gain_two).astype(bf16))
-    up_arrived, arrived = clock.wait(up_spread.moving, passing)
+    (arrived,) = clock.wait(passing)
     passed.append(arrived)
 
     normed_moving = send_around(normed_two)
-    passing = clock.pass_on(shard, *passed[-1]) if shards > 3 else []
-    (up_matrix,) = clock.run(place_blocks, z_order, *up_spread.finish(up_arrived))
+    gate_matrix, up_matrix = clock.run(place_gathered, z_order, gate_up)
+    gate_matrix = gate_matrix.reshape(width, block_units)
     up_matrix = up_matrix.reshape(width, block_units)
-    (gate_matrix,) = clock.run(place_gathered, z_order, gate_gathered)
-    gate_matrix = gate_matrix.reshape(width, block_units)
-    normed_arrived, arrived = clock.wait(normed_moving, passing)
-    passed.append(arrived)
+    (normed_arrived,) = clock.wait(normed_moving)
     while len(passed) < shards:
         (arrived,) = clock.wait(clock.pass_on(shard, *passed[-1]))
         passed.append(arrived)
@@ -872,15 +915,14 @@
         feed_forward, group_normed, cotangents, gate_matrix, up_matrix, down_weight
     )
 
-    def start_halving(left, right, groups, turned):
+    def split_halves(left, right, groups, turned):
         count = first.size * second.size
-        sent, own = clock.run(
+        halves = clock.run(
             lambda left, right: split_gradient(left, right, groups, count, core.place, turned),
             left,
             right,
         )
-        shape = (first.size, second.size) + own.shape[1:]
-        return Halving(clock, sent.reshape(shape), own.reshape(shape), core, first, second)
+        return [half.reshape((first.size, second.size) + half.shape[1:]) for half in halves]
 
     def side_by_side(rows):
         return clock(jnp.concatenate(in_place_order(rows, shard), axis=1))[0]
@@ -897,12 +939,6 @@
     edges = sorted({0, shards - 2})
     inside = list(range(1, shards - 2))
 
-    (down_blocks,) = clock.run(
-        lambda left, right: ordered_gradient(left, right, 1, list(range(reps))),
-        turned_inner,
-        cotangents,
-    )
-    down_piece = sum_over_rep(down_blocks.reshape(block_units, width))
     normed_own, *normed_partial = clock.run(
         lambda *operands: rows_product(operands[:2], operands[2:], True, shards),
         d_gate,
@@ -912,23 +948,30 @@
     )
 
     normed_moving = send_some(normed_partial, edges)
-    up = start_halving(turned_normed, d_up, shards, True)
+    (down_blocks,) = clock.run(
+        lambda left, right: ordered_gradient(left, right, 1, list(range(reps))),
+        turned_inner,
+        cotangents,
+    )
+    down_piece = sum_over_rep(down_blocks.reshape(block_units, width))
+    up_halves = split_halves(turned_normed, d_up, shards, True)
+    (normed_arrived,) = clock.wait(normed_moving)
+
+    normed_moving = send_some(normed_partial, inside)
+    up = Halving(clock, *up_halves, core, first, second)
     (gate_blocks,) = clock.run(
         lambda left, right: ordered_gradient(left, right, shards, rep_places(reps)),
         turned_normed,
         d_gate,
     )
     gate_piece = sum_over_rep(gate_blocks.reshape(width, block_units))
-    normed_arrived, up_arrived = clock.wait(normed_moving, up.moving)
-
-    up.along_first(up_arrived)
-    normed_moving = send_some(normed_partial, inside)
     block_own, *block_partial = clock.run(
         lambda left, right: rows_product((left,), (right,), False, shards), inner_act, down_weight
     )
     more_arrived, up_arrived = clock.wait(normed_moving, up.moving)
 
-    up.along_second(up_arrived)
+    up.along_first(up_arrived)
+    block_moving = send_some(block_partial, inside)
     normed_two_gradient = total_of([normed_own] + normed_arrived + more_arrived)
     gain_two_gradient = jnp.sum(normed_two_gradient * unit_two, axis=0)
     hidden_gradient = output_cotangent.astype(f32) + norm_back(
@@ -946,17 +989,16 @@
         row_marks,
         key_marks.T,
     )
-    (up_arrived,) = clock.wait(up.moving)
+    output_halves = split_halves(attention_low, branch_gradient, shards, False)
+    up_arrived, block_arrived = clock.wait(up.moving, block_moving)
 
     pair_moving = send_back(pair_partial)
-    output = start_halving(attention_low, branch_gradient, shards, False)
-    up_blocks = clock(*blocks_of(up.finish(up_arrived)))
+    output = Halving(clock, *output_halves, core, first, second)
     pair_arrived, output_arrived = clock.wait(pair_moving, output.moving)
 
+    up.along_second(up_arrived)
     output.along_first(output_arrived)
     block_moving = send_some(block_partial, edges[:1])
-    (down_piece,) = clock(down_piece)
-    down_gathered = lax.all_gather(down_piece, "rep", axis=0, tiled=True)
     projected_gradient, bias_sum = clock.run(
         lambda *operands: join_projected(operands[0], operands[3:], *operands[1:3]),
         d_queries,
@@ -965,14 +1007,16 @@
         pair_own,
         *pair_arrived,
     )
-    projected = start_halving(normed_one, projected_gradient, shards, False)
-    output_arrived, block_arrived, projected_arrived = clock.wait(
-        output.moving, block_moving, projected.moving
-    )
-
-    projected.along_first(projected_arrived)
+    projected_halves = split_halves(normed_one, projected_gradient, shards, False)
+    up_arrived, output_arrived, more_arrived = clock.wait(up.moving, output.moving, block_moving)
+    block_arrived = block_arrived + more_arrived
+
+    projected = Halving(clock, *projected_halves, core, first, second)
     output.along_second(output_arrived)
-    up_moving = send_blocks(up_blocks)
+    block_moving = send_some(block_partial, edges[1:])
+    (down_piece,) = clock(down_piece)
+    down_gathered = lax.all_gather(down_piece, "rep", axis=0, tiled=True)
+    up_blocks = clock(*blocks_of(up.finish(up_arrived)))
     projected_gradient, hidden_gradient = clock(projected_gradient, hidden_gradient)
     normed_one_gradient = times_transposed(projected_gradient, input_matrix)
     gain_one_gradient = jnp.sum(normed_one_gradient * unit_one, axis=0)
@@ -981,6 +1025,15 @@
             hidden_gradient + norm_back(normed_one_gradient, unit_one, inverse_one, gain_one)
         ).astype(bf16)
     )
+    projected_arrived, output_arrived, more_arrived = clock.wait(
+        projected.moving, output.moving, block_moving
+    )
+    block_arrived = block_arrived + more_arrived
+
+    projected.along_first(projected_arrived)
+    up_moving = send_blocks(up_blocks)
+    output_blocks = clock(*blocks_of(output.finish(output_arrived)))
+    (block_out,) = clock(total_of([hidden, block_own] + block_arrived).astype(bf16))
     bias_gradient = bias_sum[0]
     bias_split = query_width + pair_width
     small_parts = (
@@ -992,71 +1045,62 @@
     (small,) = clock(
         jnp.concatenate([part.reshape(shards, -1) for part in small_parts], axis=1)
     )
-    projected_arrived, output_arrived, up_rows = clock.wait(
-        projected.moving, output.moving, up_moving
-    )
+    projected_arrived, up_rows = clock.wait(projected.moving, up_moving)
 
     projected.along_second(projected_arrived)
-    output_blocks = clock(*blocks_of(output.finish(output_arrived)))
     output_moving = send_blocks(output_blocks)
     up_spread = spread(side_by_side(up_blocks[:1] + up_rows))
     projected_arrived, output_rows, up_arrived = clock.wait(
         projected.moving, output_moving, up_spread.moving
     )
 
-    up_spread.along(up_arrived)
-    input_blocks = clock(*blocks_of(projected.finish(projected_arrived)))
-    input_moving = send_blocks(input_blocks)
-    output_spread = spread(row_sum(output_blocks[:1], output_rows))
-    up_arrived, input_rows, output_arrived = clock.wait(
-        up_spread.moving, input_moving, output_spread.moving
-    )
-
     (gate_piece,) = clock(gate_piece)
     gate_blocks = clock(*blocks_of(gate_piece.reshape(shards, part_rows, block_units)))
     gate_moving = send_blocks(gate_blocks)
+    up_spread.along(up_arrived)
+    output_spread = spread(row_sum(output_blocks[:1], output_rows))
+    input_blocks = clock(*blocks_of(projected.finish(projected_arrived)))
+    gate_rows, up_arrived, output_arrived = clock.wait(
+        gate_moving, up_spread.moving, output_spread.moving
+    )
+
+    input_moving = send_blocks(input_blocks)
+    gate_spread = spread(side_by_side(gate_blocks[:1] + gate_rows))
     output_spread.along(output_arrived)
+    input_rows, gate_arrived, output_arrived = clock.wait(
+        input_moving, gate_spread.moving, output_spread.moving
+    )
+
+    gate_spread.along(gate_arrived)
     input_spread = spread(row_sum(input_blocks[:1], input_rows))
-    gate_rows, output_arrived, input_arrived = clock.wait(
-        gate_moving, output_spread.moving, input_spread.moving
-    )
-
-    gate_spread = spread(side_by_side(gate_blocks[:1] + gate_rows))
+    up_spread.over(up_arrived)
+    output_spread.over(output_arrived)
+    small_moving = clock.send(core, [small], [1])
+    gate_arrived, input_arrived, up_arrived, output_arrived, small_arrived = clock.wait(
+        gate_spread.moving, input_spread.moving, up_spread.moving, output_spread.moving, small_moving
+    )
+    small = total_of([small] + small_arrived)
+
     input_spread.along(input_arrived)
-    output_spread.over(output_arrived)
-    up_spread.over(up_arrived)
-    block_moving = send_some(block_partial, edges[1:])
-    gate_arrived, input_arrived, output_arrived, up_arrived, more_arrived = clock.wait(
-        gate_spread.moving, input_spread.moving, output_spread.moving, up_spread.moving, block_moving
-    )
-    block_arrived = block_arrived + more_arrived
-
-    gate_spread.along(gate_arrived)
-    input_spread.over(input_arrived)
-    block_moving = send_some(block_partial, inside)
-    small_moving = clock.send(core, [small], [1])
+    gate_spread.over(gate_arrived)
+    small_moving = clock.send(first, [small] * (first.size - 1), range(1, first.size))
     (up_total,) = clock.run(widen_pieces, *up_spread.finish(up_arrived))
     (output_total,) = clock.run(widen_pieces, *output_spread.finish(output_arrived))
-    gate_arrived, input_arrived, more_arrived, small_arrived = clock.wait(
-        gate_spread.moving, input_spread.moving, block_moving, small_moving
-    )
-    block_arrived = block_arrived + more_arrived
+    input_arrived, gate_arrived, small_arrived = clock.wait(
+        input_spread.moving, gate_spread.moving, small_moving
+    )
     small = total_of([small] + small_arrived)
 
-    gate_spread.over(gate_arrived)
-    small_moving = clock.send(first, [small] * (first.size - 1), range(1, first.size))
-    (input_total,) = clock.run(widen_pieces, *input_spread.finish(input_arrived))
-    down_gathered, hidden, block_own = clock(down_gathered, hidden, block_own)
-    (down_total,) = clock(down_gathered.astype(f32))
-    gate_arrived, small_arrived = clock.wait(gate_spread.moving, small_moving)
-    small = total_of([small] + small_arrived)
-
+    input_spread.over(input_arrived)
     small_moving = clock.send(second, [small] * (second.size - 1), range(1, second.size))
     (gate_total,) = clock.run(widen_pieces, *gate_spread.finish(gate_arrived))
-    (small_arrived,) = clock.wait(small_moving)
+    input_arrived, small_arrived = clock.wait(input_spread.moving, small_moving)
     small_blocks = clock(*blocks_of(total_of([small] + small_arrived)))
+
     small_moving = send_blocks(small_blocks)
-    (block_out,) = clock(total_of([hidden, block_own] + block_arrived).astype(bf16))
+    (input_total,) = clock.run(widen_pieces, *input_spread.finish(input_arrived))
+    (down_gathered,) = clock(down_gathered)
+    (down_total,) = clock(down_gathered.astype(f32))
     (small_arrived,) = clock.wait(small_moving)
     small = total_of(small_blocks[:1] + small_arrived)
 

time: 712 us -> 651 us (0.914)
  waiting for transfers between devices: 298 us -> 235 us
  starting transfers between devices: 112 us -> 129 us
  other arithmetic: 75.4 us -> 66.5 us
  local copies, waits for them, and re-layouts: 44.1 us -> 36 us
    ppermute x69 -> x66, waiting for transfers between devices: 256 us -> 217 us  [shift(): return lax.ppermute(value, self.name, self.pairs(step % self.size))]
    ppermute x6, waiting for transfers between devices: 41.8 us -> 17.6 us  [pass_on(): return lax.ppermute(value, self.name, pairs)]
    ppermute x6, starting transfers between devices: 12.9 us -> 26.2 us  [pass_on(): return lax.ppermute(value, self.name, pairs)]
    all_gather x0 -> x1, local copies, waits for them, and re-layouts: none -> 10.6 us  [on_device(): gate_up = lax.all_gather(clock(gate_up)[0][None], 'rep', axis=0, tiled=True)]
    unnamed x132 -> x108, local copies, waits for them, and re-layouts: 15.3 us -> 6.84 us
    pallas_call x2 -> x1, Pallas kernels: 12.2 us -> 4.84 us  [place_blocks(): blocks_call(body, 2, 2, groups, shards, 2 * half, pieces.shape[3:])]
    ppermute x69 -> x66, starting transfers between devices: 98.5 us -> 102 us  [shift(): return lax.ppermute(value, self.name, self.pairs(step % self.size))]
  transfers between devices with their start and end apart: 80 -> 77, of which waited for: 42 -> 38; matrix products, arithmetic and copies ran while one was open for 17% -> 16% of each run, Pallas kernels for 14% -> 15%
where the time goes in v9:
time: 651 us; the launch traced here: 641 us
  waiting for transfers between devices  235 us (36%)
  Pallas kernels  143 us (22%)
  starting transfers between devices  129 us (20%)
  other arithmetic  66.5 us (10%)
  local copies, waits for them, and re-layouts  36 us (6%)
  matrix products  15.8 us (2%)
  between operations  15.4 us (2%)
    ppermute x66, waiting for transfers between devices, shift(): return lax.ppermute(value, self.name, self.pairs(step % self.size))  217 us
    ppermute x66, starting transfers between devices, shift(): return lax.ppermute(value, self.name, self.pairs(step % self.size))  102 us
    ppermute x6, starting transfers between devices, pass_on(): return lax.ppermute(value, self.name, pairs)  26.2 us
    pallas_call x1, Pallas kernels, feed_forward(): pl.pallas_call(body, grid=(steps,), out_shape=[jax.ShapeDtypeStruct((coun...  23.8 us
    pallas_call x2, Pallas kernels, rows_product(): pl.pallas_call(body, grid=(pl.cdiv(columns, TILE),), out_shape=[jax.Shape...  23.3 us
    pallas_call x4, Pallas kernels, widen_pieces(): pl.pallas_call(body, out_shape=jax.ShapeDtypeStruct((reps, rows, columns)...  21.1 us
    pallas_call x3, Pallas kernels, split_gradient(): pl.pallas_call(body, grid=(pl.cdiv(columns, TILE),), out_shape=[jax.Shape...  20.1 us
    pallas_call x2, Pallas kernels, ordered_gradient(): pl.pallas_call(body, grid=(pl.cdiv(columns, TILE),), out_shape=[jax.Shape...  19.2 us
  transfers between devices with their start and end apart: 77, of which 38 were waited for; matrix products, arithmetic and copies ran while one was open for 16% of the time, Pallas kernels for 15%

profile of v9, /device:TPU:0, one launch (start us, length us, event | category | flops | bytes accessed | tf_op | source)
XLA Modules:
  0.0 641.0 jit_solution(11258442043049136801)
XLA Ops:
  32.3 6.6 %collective-permute-start.4 = (bf16[48,2240]{1,0:T(8,128)(2,1)}, bf16[48,2240]{1,0:T(8,128)(2,1)S(1)}, u32[]{:S(2)}, u32[]{:S(2)}) collective-permute-start(bf16[48,2240]{1,0:T(8,128)(2,1)} %get-tuple-element.482), channel_id=1, source_target_pairs={{0,1},{1,2},{2,3},{3,0},{4,5},{5,6},{6,7},{7,4},{8,9},{9,10},{10,1... | collective-permute-start | bytes 645128 | tf_op jit(solution)/shard_map/ppermute | solution.py:68
  41.5 6.2 collective-permute-done.4
  47.7 13.6 %collective-permute-done.5 = bf16[48,2240]{1,0:T(8,128)(2,1)S(1)} collective-permute-done((bf16[48,2240]{1,0:T(8,128)(2,1)}, bf16[48,2240]{1,0:T(8,128)(2,1)S(1)}, u32[]{:S(2)}, u32[]{:S(2)}) %collective-permute-start.5) | collective-permute-done | bytes 215072 | tf_op jit(solution)/shard_map/ppermute | solution.py:68
  62.4 5.7 collective-permute-start.8
  70.8 6.3 collective-permute-done.8
  77.1 18.5 %collective-permute-done.9 = bf16[48,2240]{1,0:T(8,128)(2,1)S(1)} collective-permute-done((bf16[48,2240]{1,0:T(8,128)(2,1)S(1)}, bf16[48,2240]{1,0:T(8,128)(2,1)S(1)}, u32[]{:S(2)}, u32[]{:S(2)}) %collective-permute-start.9) | collective-permute-done | bytes 215072 | tf_op jit(solution)/shard_map/ppermute | solution.py:68
  101.2 15.2 %collective-permute-start.12 = (bf16[160,1536]{1,0:T(8,128)(2,1)S(1)}, bf16[160,1536]{1,0:T(8,128)(2,1)}, u32[]{:S(2)}, u32[]{:S(2)}) collective-permute-start(bf16[160,1536]{1,0:T(8,128)(2,1)S(1)} %copy-done.19), channel_id=1, source_target_pairs={{0,1},{1,2},{2,3},{4,5},{5,6},{6,7},{8,9},{9,10},{10,11},{12,13},{... | collective-permute-start | bytes 1474568 | tf_op jit(solution)/shard_map/ppermute | solution.py:73
  120.0 6.7 %collective-permute-done.12 = bf16[160,1536]{1,0:T(8,128)(2,1)} collective-permute-done((bf16[160,1536]{1,0:T(8,128)(2,1)S(1)}, bf16[160,1536]{1,0:T(8,128)(2,1)}, u32[]{:S(2)}, u32[]{:S(2)}) %collective-permute-start.12) | collective-permute-done | bytes 491552 | tf_op jit(solution)/shard_map/ppermute | solution.py:73
  169.4 5.7 attention_forward.1
  188.0 10.6 %copy.34 = bf16[32,2,48,2240]{3,2,1,0:T(8,128)(2,1)} copy(bf16[32,2,48,2240]{3,2,0,1:T(8,128)(2,1)} %all-gather.10.cloned.1.call-done) | data formatting | bytes 27525120 | tf_op jit(solution)/shard_map/all_gather | solution.py:856
  198.6 11.7 %place_blocks.3 = (bf16[4,8,48,2240]{3,2,1,0:T(8,128)(2,1)}, bf16[4,8,48,2240]{3,2,1,0:T(8,128)(2,1)}) custom-call(s32[4]{0:T(128)} %pad_add_fusion.5.order_ref, bf16[8,4,2,48,2240]{4,3,2,1,0:T(8,128)(2,1)} %bitcast.177), custom_call_target="tpu_custom_call" | custom-call | flops 1 | bytes 1 | tf_op jit(solution)/shard_map/place_blocks/pallas_call | solution.py:334
  216.8 23.8 %feed_forward.1 = (bf16[640,2240]{1,0:T(8,128)(2,1)}, bf16[640,2240]{1,0:T(8,128)(2,1)}, bf16[640,2240]{1,0:T(8,128)(2,1)}, bf16[1536,640]{1,0:T(8,128)(2,1)}, bf16[2240,640]{1,0:T(8,128)(2,1)}) custom-call(bf16[640,1536]{1,0:T(8,128)(2,1)} %pad_maximum_fusion.3.rows_ref, bf16[640,1536]{1,0:T(8,128)(2,1)} %pad_maximum_fusion.4.cotangents_ref.right_ref, ...), custom_call_target="tpu_custom_call" | custom-call | flops 1 | bytes 1 | tf_op jit(solution)/shard_map/feed_forward/pallas_call | solution.py:472
  240.7 14.6 %rows_product.2 = (bf16[160,1536]{1,0:T(8,128)(2,1)}, bf16[160,1536]{1,0:T(8,128)(2,1)}, bf16[160,1536]{1,0:T(8,128)(2,1)}, bf16[160,1536]{1,0:T(8,128)(2,1)}) custom-call(bf16[640,2240]{1,0:T(8,128)(2,1)} %get-tuple-element.628.refs_0_.right_ref, bf16[640,2240]{1,0:T(8,128)(2,1)} %get-tuple-element.615.refs_1_.right_ref, bf16[1536,2240]{1,0:T(8,128)(2,1)} %bitcast.183, ...), custom_call_target="tpu_custom_call" | custom-call | flops 1 | bytes 1 | tf_op jit(solution)/shard_map/rows_product/pallas_call | solution.py:598
  255.3 9.3 %ordered_gradient.2 = bf16[8,1,280,1536]{3,2,1,0:T(8,128)(2,1)} custom-call(bf16[2240,640]{1,0:T(8,128)(2,1)} %get-tuple-element.609.left_ref, bf16[640,1536]{1,0:T(8,128)(2,1)} %pad_maximum_fusion.4.cotangents_ref.right_ref), custom_call_target="tpu_custom_call" | custom-call | flops 1 | bytes 1 | tf_op jit(solution)/shard_map/ordered_gradient/pallas_call | solution.py:558
  264.7 10.3 %collective-permute-start.24 = (bf16[160,1536]{1,0:T(8,128)(2,1)}, bf16[160,1536]{1,0:T(8,128)(2,1)S(1)}, u32[]{:S(2)}, u32[]{:S(2)}) collective-permute-start(bf16[160,1536]{1,0:T(8,128)(2,1)} %get-tuple-element.619), channel_id=1, source_target_pairs={{0,3},{1,0},{2,1},{3,2},{4,7},{5,4},{6,5},{7,6},{8,11},{9,8},{10,9... | collective-permute-start | bytes 1474568 | tf_op jit(solution)/shard_map/ppermute | solution.py:68
  276.9 10.2 %split_gradient.3 = (bf16[4,4,48,2240]{3,2,1,0:T(8,128)(2,1)}, bf16[4,4,48,2240]{3,2,1,0:T(8,128)(2,1)}) custom-call(s32[1]{0:T(128)} %bitcast.49.core_ref, bf16[1536,640]{1,0:T(8,128)(2,1)} %get-tuple-element.627.left_ref, bf16[640,2240]{1,0:T(8,128)(2,1)} %get-tuple-element.615.refs_1_.right_ref), custom_call_target="tpu_custom_call" | custom-call | flops 1 | bytes 1 | tf_op jit(solution)/shard_map/split_gradient/pallas_call | solution.py:528
  288.0 10.0 %collective-permute-done.25 = bf16[160,1536]{1,0:T(8,128)(2,1)} collective-permute-done((bf16[160,1536]{1,0:T(8,128)(2,1)S(1)}, bf16[160,1536]{1,0:T(8,128)(2,1)}, u32[]{:S(2)}, u32[]{:S(2)}) %collective-permute-start.25) | collective-permute-done | bytes 491552 | tf_op jit(solution)/shard_map/ppermute | solution.py:68
  298.5 9.9 %ordered_gradient.3 = bf16[8,4,48,2240]{3,2,1,0:T(8,128)(2,1)} custom-call(bf16[1536,640]{1,0:T(8,128)(2,1)} %get-tuple-element.627.left_ref, bf16[640,2240]{1,0:T(8,128)(2,1)} %get-tuple-element.628.refs_0_.right_ref), custom_call_target="tpu_custom_call" | custom-call | flops 1 | bytes 1 | tf_op jit(solution)/shard_map/ordered_gradient/pallas_call | solution.py:558
  308.4 8.7 %rows_product.3 = (bf16[160,1536]{1,0:T(8,128)(2,1)}, bf16[160,1536]{1,0:T(8,128)(2,1)}, bf16[160,1536]{1,0:T(8,128)(2,1)}, bf16[160,1536]{1,0:T(8,128)(2,1)}) custom-call(bf16[640,2240]{1,0:T(8,128)(2,1)} %get-tuple-element.632.refs_0_, bf16[2240,1536]{1,0:T(8,128)(2,1)} %refs_1_), custom_call_target="tpu_custom_call" | custom-call | flops 1 | bytes 1 | tf_op jit(solution)/shard_map/rows_product/pallas_call | solution.py:598
  317.1 5.9 collective-permute-done.26
  334.4 7.6 %attention_backward.1 = (bf16[160,1536]{1,0:T(8,128)(2,1)}, bf16[160,512]{1,0:T(8,128)(2,1)}, bf16[160,512]{1,0:T(8,128)(2,1)}, bf16[160,512]{1,0:T(8,128)(2,1)}, bf16[160,512]{1,0:T(8,128)(2,1)}) custom-call(bf16[2,960,128]{2,1,0:T(8,128)(2,1)} %get-tuple-element.657.queries_ref, bf16[160,1536]{1,0:T(8,128)(2,1)} %convolution_convert_fusion.gradient_ref, ...), custom_call_target="tpu_custom_call" | custom-call | flops 1 | bytes 1 | tf_op jit(solution)/shard_map/attention_backward/pallas_call | solution.py:700
  362.6 10.0 %collective-permute-done.31.refs_2_ = bf16[160,512]{1,0:T(8,128)(2,1)S(1)} collective-permute-done((bf16[160,512]{1,0:T(8,128)(2,1)S(1)}, bf16[160,512]{1,0:T(8,128)(2,1)S(1)}, u32[]{:S(2)}, u32[]{:S(2)}) %collective-permute-start.31) | collective-permute-done | bytes 163872 | tf_op jit(solution)/shard_map/ppermute | solution.py:68
  389.9 27.4 %collective-permute-done.34 = bf16[4,48,2240]{2,1,0:T(8,128)(2,1)} collective-permute-done((bf16[4,48,2240]{2,1,0:T(8,128)(2,1)}, bf16[4,48,2240]{2,1,0:T(8,128)(2,1)}, u32[]{:S(2)}, u32[]{:S(2)}) %collective-permute-start.34) | collective-permute-done | bytes 860192 | tf_op jit(solution)/shard_map/ppermute | solution.py:68
  458.4 7.5 %collective-permute-done.42 = bf16[48,2240]{1,0:T(8,128)(2,1)S(1)} collective-permute-done((bf16[48,2240]{1,0:T(8,128)(2,1)}, bf16[48,2240]{1,0:T(8,128)(2,1)S(1)}, u32[]{:S(2)}, u32[]{:S(2)}) %collective-permute-start.42) | collective-permute-done | bytes 215072 | tf_op jit(solution)/shard_map/ppermute | solution.py:68
  508.2 7.4 %collective-permute-done.53 = bf16[48,1536]{1,0:T(8,128)(2,1)S(1)} collective-permute-done((bf16[48,1536]{1,0:T(8,128)(2,1)S(1)}, bf16[48,1536]{1,0:T(8,128)(2,1)S(1)}, u32[]{:S(2)}, u32[]{:S(2)}) %collective-permute-start.53) | collective-permute-done | bytes 147488 | tf_op jit(solution)/shard_map/ppermute | solution.py:68
  515.6 11.7 %collective-permute-done.52 = bf16[2,48,8960]{2,1,0:T(8,128)(2,1)} collective-permute-done((bf16[2,48,8960]{2,1,0:T(8,128)(2,1)}, bf16[2,48,8960]{2,1,0:T(8,128)(2,1)}, u32[]{:S(2)}, u32[]{:S(2)}) %collective-permute-start.52) | collective-permute-done | bytes 1720352 | tf_op jit(solution)/shard_map/ppermute | solution.py:68
  544.6 9.9 %collective-permute-done.58 = bf16[2,48,1536]{2,1,0:T(8,128)(2,1)S(1)} collective-permute-done((bf16[2,48,1536]{2,1,0:T(8,128)(2,1)S(1)}, bf16[2,48,1536]{2,1,0:T(8,128)(2,1)S(1)}, u32[]{:S(2)}, u32[]{:S(2)}) %collective-permute-start.58) | collective-permute-done | bytes 294944 | tf_op jit(solution)/shard_map/ppermute | solution.py:68
  554.5 8.3 %collective-permute-done.57 = bf16[48,8960]{1,0:T(8,128)(2,1)S(1)} collective-permute-done((bf16[48,8960]{1,0:T(8,128)(2,1)S(1)}, bf16[48,8960]{1,0:T(8,128)(2,1)S(1)}, u32[]{:S(2)}, u32[]{:S(2)}) %collective-permute-start.57) | collective-permute-done | bytes 860192 | tf_op jit(solution)/shard_map/ppermute | solution.py:68
  573.9 14.6 %collective-permute-done.59 = bf16[2,48,8960]{2,1,0:T(8,128)(2,1)S(1)} collective-permute-done((bf16[2,48,8960]{2,1,0:T(8,128)(2,1)S(1)}, bf16[2,48,8960]{2,1,0:T(8,128)(2,1)S(1)}, u32[]{:S(2)}, u32[]{:S(2)}) %collective-permute-start.59) | collective-permute-done | bytes 1720352 | tf_op jit(solution)/shard_map/ppermute | solution.py:68
  592.9 7.3 %widen_pieces.4 = f32[8,48,8960]{2,1,0:T(8,128)} custom-call(s32[8]{0:T(128)} %stack.255.places_ref, bf16[4,48,8960]{2,1,0:T(8,128)(2,1)} %copy-done.2, bf16[4,48,8960]{2,1,0:T(8,128)(2,1)} %copy-done.9), custom_call_target="tpu_custom_call" | custom-call | flops 1 | bytes 1 | tf_op jit(solution)/shard_map/widen_pieces/pallas_call | solution.py:410
  604.8 7.3 %widen_pieces.6 = f32[8,48,8960]{2,1,0:T(8,128)} custom-call(s32[8]{0:T(128)} %stack.255.places_ref, bf16[4,48,8960]{2,1,0:T(8,128)(2,1)} %copy-done.3, bf16[4,48,8960]{2,1,0:T(8,128)(2,1)} %collective-permute-done.65.others_ref), custom_call_target="tpu_custom_call" | custom-call | flops 1 | bytes 1 | tf_op jit(solution)/shard_map/widen_pieces/pallas_call | solution.py:410
  621.1 10.2 %convert_element_type.352 = f32[2240,1536]{1,0:T(8,128)} convert(bf16[2240,1536]{1,0:T(8,128)(2,1)} %all-gather.6.cloned.1.call-done) | non-fusion elementwise | flops 3440640 | bytes 20643840 | tf_op jit(solution)/shard_map/convert_element_type | solution.py:1103
  (384 shorter events, 287.1 us)
Async XLA Ops:
  7.2 132.8 %all-gather.8.cloned.1.call-start = ((), (), s32[]{:S(2)}) async-start(), calls=%async_computation.5 | async-start | bytes 6488064 | tf_op jit(solution)/shard_map/all_gather | solution.py:791
  9.3 178.7 %all-gather.10.cloned.1.call-start = ((), (), s32[]{:S(2)}) async-start(), calls=%async_computation.6 | async-start | bytes 15925248 | tf_op jit(solution)/shard_map/all_gather | solution.py:856
  30.7 31.1 %collective-permute-start.3 = (bf16[1,4,48,1536]{3,2,1,0:T(8,128)(2,1)}, bf16[1,4,48,1536]{3,2,1,0:T(8,128)(2,1)S(1)}, u32[]{:S(2)}, u32[]{:S(2)}) collective-permute-start(bf16[1,4,48,1536]{3,2,1,0:T(8,128)(2,1)} %get-tuple-element.481), channel_id=1, source_target_pairs={{0,16},{4,12},{8,24},{12,4},{16,0},{20,28},{24,8},{28,20},{1,17},{... | collective-permute-start | bytes 1769480 | tf_op jit(solution)/shard_map/ppermute | solution.py:68
  38.9 22.4 %collective-permute-start.5 = (bf16[48,2240]{1,0:T(8,128)(2,1)}, bf16[48,2240]{1,0:T(8,128)(2,1)S(1)}, u32[]{:S(2)}, u32[]{:S(2)}) collective-permute-start(bf16[48,2240]{1,0:T(8,128)(2,1)} %get-tuple-element.483), channel_id=1, source_target_pairs={{0,2},{1,3},{2,0},{3,1},{4,6},{5,7},{6,4},{7,5},{8,10},{9,11},{10,... | collective-permute-start | bytes 645128 | tf_op jit(solution)/shard_map/ppermute | solution.py:68
  40.5 21.3 %collective-permute-start.6 = (bf16[48,2240]{1,0:T(8,128)(2,1)}, bf16[48,2240]{1,0:T(8,128)(2,1)S(1)}, u32[]{:S(2)}, u32[]{:S(2)}) collective-permute-start(bf16[48,2240]{1,0:T(8,128)(2,1)} %get-tuple-element.484), channel_id=1, source_target_pairs={{0,3},{1,0},{2,1},{3,2},{4,7},{5,4},{6,5},{7,6},{8,11},{9,8},{10,9... | collective-permute-start | bytes 645128 | tf_op jit(solution)/shard_map/ppermute | solution.py:68
  61.9 33.7 %collective-permute-start.7 = (bf16[2,1,4,48,1536]{4,3,2,1,0:T(8,128)(2,1)S(1)}, bf16[2,1,4,48,1536]{4,3,2,1,0:T(8,128)(2,1)S(1)}, u32[]{:S(2)}, u32[]{:S(2)}) collective-permute-start(bf16[2,1,4,48,1536]{4,3,2,1,0:T(8,128)(2,1)S(1)} %pad_maximum_fusion.8), channel_id=1, source_target_pairs={{0,8},{4,20},{8,0},{12,28},{16,24},{20,4},{24,16},{28,12},{1,9},{5... | collective-permute-start | bytes 3538952 | tf_op jit(solution)/shard_map/ppermute | solution.py:68
  68.1 27.5 %collective-permute-start.9 = (bf16[48,2240]{1,0:T(8,128)(2,1)S(1)}, bf16[48,2240]{1,0:T(8,128)(2,1)S(1)}, u32[]{:S(2)}, u32[]{:S(2)}) collective-permute-start(bf16[48,2240]{1,0:T(8,128)(2,1)S(1)} %copy-done.30), channel_id=1, source_target_pairs={{0,2},{1,3},{2,0},{3,1},{4,6},{5,7},{6,4},{7,5},{8,10},{9,11},{10,... | collective-permute-start | bytes 645128 | tf_op jit(solution)/shard_map/ppermute | solution.py:68
  70.7 24.9 %collective-permute-start.10 = (bf16[48,2240]{1,0:T(8,128)(2,1)S(1)}, bf16[48,2240]{1,0:T(8,128)(2,1)S(1)}, u32[]{:S(2)}, u32[]{:S(2)}) collective-permute-start(bf16[48,2240]{1,0:T(8,128)(2,1)S(1)} %get-tuple-element.493), channel_id=1, source_target_pairs={{0,3},{1,0},{2,1},{3,2},{4,7},{5,4},{6,5},{7,6},{8,11},{9,8},{10,9... | collective-permute-start | bytes 645128 | tf_op jit(solution)/shard_map/ppermute | solution.py:68
  98.1 329.4 %reduce-scatter.3.cloned.1.call-start = ((), (), s32[]{:S(2)}) async-start(), calls=%async_computation.2 | async-start | bytes 7741440 | tf_op jit(solution)/shard_map/reduce_scatter | solution.py:931
  101.1 30.5 %collective-permute-start.11 = (bf16[4,1,4,48,1536]{4,3,2,1,0:T(8,128)(2,1)}, bf16[4,1,4,48,1536]{4,3,2,1,0:T(8,128)(2,1)}, u32[]{:S(2)}, u32[]{:S(2)}) collective-permute-start(bf16[4,1,4,48,1536]{4,3,2,1,0:T(8,128)(2,1)} %pad_maximum_fusion.2.pieces_ref), channel_id=1, source_target_pairs={{0,4},{4,0},{8,12},{12,8},{16,20},{20,16},{24,28},{28,24},{1,5},{5... | collective-permute-start | bytes 7077896 | tf_op jit(solution)/shard_map/ppermute | solution.py:68
  101.2 25.5 %collective-permute-start.12 = (bf16[160,1536]{1,0:T(8,128)(2,1)S(1)}, bf16[160,1536]{1,0:T(8,128)(2,1)}, u32[]{:S(2)}, u32[]{:S(2)}) collective-permute-start(bf16[160,1536]{1,0:T(8,128)(2,1)S(1)} %copy-done.19), channel_id=1, source_target_pairs={{0,1},{1,2},{2,3},{4,5},{5,6},{6,7},{8,9},{9,10},{10,11},{12,13},{... | collective-permute-start | bytes 1474568 | tf_op jit(solution)/shard_map/ppermute | solution.py:73
  181.2 29.0 %collective-permute-start.21 = (bf16[160,1536]{1,0:T(8,128)(2,1)S(1)}, bf16[160,1536]{1,0:T(8,128)(2,1)S(1)}, u32[]{:S(2)}, u32[]{:S(2)}) collective-permute-start(bf16[160,1536]{1,0:T(8,128)(2,1)S(1)} %multiply_convert_fusion), channel_id=1, source_target_pairs={{0,1},{1,2},{2,3},{3,0},{4,5},{5,6},{6,7},{7,4},{8,9},{9,10},{10,1... | collective-permute-start | bytes 1474568 | tf_op jit(solution)/shard_map/ppermute | solution.py:68
  181.6 33.9 %collective-permute-start.22 = (bf16[160,1536]{1,0:T(8,128)(2,1)S(1)}, bf16[160,1536]{1,0:T(8,128)(2,1)S(1)}, u32[]{:S(2)}, u32[]{:S(2)}) collective-permute-start(bf16[160,1536]{1,0:T(8,128)(2,1)S(1)} %multiply_convert_fusion), channel_id=1, source_target_pairs={{0,2},{1,3},{2,0},{3,1},{4,6},{5,7},{6,4},{7,5},{8,10},{9,11},{10,... | collective-permute-start | bytes 1474568 | tf_op jit(solution)/shard_map/ppermute | solution.py:68
  181.6 33.9 %collective-permute-start.23 = (bf16[160,1536]{1,0:T(8,128)(2,1)S(1)}, bf16[160,1536]{1,0:T(8,128)(2,1)S(1)}, u32[]{:S(2)}, u32[]{:S(2)}) collective-permute-start(bf16[160,1536]{1,0:T(8,128)(2,1)S(1)} %multiply_convert_fusion), channel_id=1, source_target_pairs={{0,3},{1,0},{2,1},{3,2},{4,7},{5,4},{6,5},{7,6},{8,11},{9,8},{10,9... | collective-permute-start | bytes 1474568 | tf_op jit(solution)/shard_map/ppermute | solution.py:68
  264.6 226.1 %reduce-scatter.5.cloned.1.call-start = ((), (), s32[]{:S(2)}) async-start(), calls=%async_computation.3 | async-start | bytes 7962624 | tf_op jit(solution)/shard_map/reduce_scatter | solution.py:931
  264.7 23.3 %collective-permute-start.24 = (bf16[160,1536]{1,0:T(8,128)(2,1)}, bf16[160,1536]{1,0:T(8,128)(2,1)S(1)}, u32[]{:S(2)}, u32[]{:S(2)}) collective-permute-start(bf16[160,1536]{1,0:T(8,128)(2,1)} %get-tuple-element.619), channel_id=1, source_target_pairs={{0,3},{1,0},{2,1},{3,2},{4,7},{5,4},{6,5},{7,6},{8,11},{9,8},{10,9... | collective-permute-start | bytes 1474568 | tf_op jit(solution)/shard_map/ppermute | solution.py:68
  275.0 23.0 %collective-permute-start.25 = (bf16[160,1536]{1,0:T(8,128)(2,1)S(1)}, bf16[160,1536]{1,0:T(8,128)(2,1)}, u32[]{:S(2)}, u32[]{:S(2)}) collective-permute-start(bf16[160,1536]{1,0:T(8,128)(2,1)S(1)} %copy-done.46), channel_id=1, source_target_pairs={{0,1},{1,2},{2,3},{3,0},{4,5},{5,6},{6,7},{7,4},{8,9},{9,10},{10,1... | collective-permute-start | bytes 1474568 | tf_op jit(solution)/shard_map/ppermute | solution.py:68
  297.9 25.1 %collective-permute-start.27 = (bf16[2,2,4,48,2240]{4,3,2,1,0:T(8,128)(2,1)}, bf16[2,2,4,48,2240]{4,3,2,1,0:T(8,128)(2,1)}, u32[]{:S(2)}, u32[]{:S(2)}) collective-permute-start(bf16[2,2,4,48,2240]{4,3,2,1,0:T(8,128)(2,1)} %bitcast.241), channel_id=1, source_target_pairs={{0,4},{4,0},{8,12},{12,8},{16,20},{20,16},{24,28},{28,24},{1,5},{5... | collective-permute-start | bytes 10321928 | tf_op jit(solution)/shard_map/ppermute | solution.py:68
  297.9 25.1 %collective-permute-start.26 = (bf16[160,1536]{1,0:T(8,128)(2,1)S(1)}, bf16[160,1536]{1,0:T(8,128)(2,1)S(1)}, u32[]{:S(2)}, u32[]{:S(2)}) collective-permute-start(bf16[160,1536]{1,0:T(8,128)(2,1)S(1)} %copy-done.45), channel_id=1, source_target_pairs={{0,2},{1,3},{2,0},{3,1},{4,6},{5,7},{6,4},{7,5},{8,10},{9,11},{10,... | collective-permute-start | bytes 1474568 | tf_op jit(solution)/shard_map/ppermute | solution.py:68
  327.0 26.6 %collective-permute-start.28 = (bf16[2,4,48,2240]{3,2,1,0:T(8,128)(2,1)}, bf16[2,4,48,2240]{3,2,1,0:T(8,128)(2,1)}, u32[]{:S(2)}, u32[]{:S(2)}) collective-permute-start(bf16[2,4,48,2240]{3,2,1,0:T(8,128)(2,1)} %fusion), channel_id=1, source_target_pairs={{0,8},{4,20},{8,0},{12,28},{16,24},{20,4},{24,16},{28,12},{1,9},{5... | collective-permute-start | bytes 5160968 | tf_op jit(solution)/shard_map/ppermute | solution.py:68
  327.9 23.2 %collective-permute-start.29 = (bf16[160,1536]{1,0:T(8,128)(2,1)}, bf16[160,1536]{1,0:T(8,128)(2,1)}, u32[]{:S(2)}, u32[]{:S(2)}) collective-permute-start(bf16[160,1536]{1,0:T(8,128)(2,1)} %get-tuple-element.677), channel_id=1, source_target_pairs={{0,2},{1,3},{2,0},{3,1},{4,6},{5,7},{6,4},{7,5},{8,10},{9,11},{10,... | collective-permute-start | bytes 1474568 | tf_op jit(solution)/shard_map/ppermute | solution.py:68
  353.8 267.4 %all-gather.6.cloned.1.call-start = ((), (), s32[]{:S(2)}) async-start(), calls=%async_computation.4 | async-start | bytes 7741440 | tf_op jit(solution)/shard_map/all_gather | solution.py:1018
  375.4 44.9 %collective-permute-start.35 = (bf16[2,4,48,1536]{3,2,1,0:T(8,128)(2,1)}, bf16[2,4,48,1536]{3,2,1,0:T(8,128)(2,1)}, u32[]{:S(2)}, u32[]{:S(2)}) collective-permute-start(bf16[2,4,48,1536]{3,2,1,0:T(8,128)(2,1)} %fusion.12), channel_id=1, source_target_pairs={{0,8},{4,20},{8,0},{12,28},{16,24},{20,4},{24,16},{28,12},{1,9},{5... | collective-permute-start | bytes 3538952 | tf_op jit(solution)/shard_map/ppermute | solution.py:68
  375.9 41.4 %collective-permute-start.34 = (bf16[4,48,2240]{2,1,0:T(8,128)(2,1)}, bf16[4,48,2240]{2,1,0:T(8,128)(2,1)}, u32[]{:S(2)}, u32[]{:S(2)}) collective-permute-start(bf16[4,48,2240]{2,1,0:T(8,128)(2,1)} %fusion.3), channel_id=1, source_target_pairs={{0,16},{4,12},{8,24},{12,4},{16,0},{20,28},{24,8},{28,20},{1,17},{... | collective-permute-start | bytes 2580488 | tf_op jit(solution)/shard_map/ppermute | solution.py:68
  420.3 22.1 %collective-permute-start.37 = (bf16[2,2,4,48,2048]{4,3,2,1,0:T(8,128)(2,1)}, bf16[2,2,4,48,2048]{4,3,2,1,0:T(8,128)(2,1)}, u32[]{:S(2)}, u32[]{:S(2)}) collective-permute-start(bf16[2,2,4,48,2048]{4,3,2,1,0:T(8,128)(2,1)} %bitcast.242), channel_id=1, source_target_pairs={{0,4},{4,0},{8,12},{12,8},{16,20},{20,16},{24,28},{28,24},{1,5},{5... | collective-permute-start | bytes 9437192 | tf_op jit(solution)/shard_map/ppermute | solution.py:68
  444.4 21.5 %collective-permute-start.40 = (bf16[2,4,48,2048]{3,2,1,0:T(8,128)(2,1)S(1)}, bf16[2,4,48,2048]{3,2,1,0:T(8,128)(2,1)}, u32[]{:S(2)}, u32[]{:S(2)}) collective-permute-start(bf16[2,4,48,2048]{3,2,1,0:T(8,128)(2,1)S(1)} %fusion.4), channel_id=1, source_target_pairs={{0,8},{4,20},{8,0},{12,28},{16,24},{20,4},{24,16},{28,12},{1,9},{5... | collective-permute-start | bytes 4718600 | tf_op jit(solution)/shard_map/ppermute | solution.py:68
  469.4 21.3 %collective-permute-start.48 = (bf16[48,8960]{1,0:T(8,128)(2,1)S(1)}, bf16[48,8960]{1,0:T(8,128)(2,1)S(1)}, u32[]{:S(2)}, u32[]{:S(2)}) collective-permute-start(bf16[48,8960]{1,0:T(8,128)(2,1)S(1)} %concatenate.71), channel_id=1, source_target_pairs={{0,16},{4,12},{8,24},{12,4},{16,0},{20,28},{24,8},{28,20},{1,17},{... | collective-permute-start | bytes 2580488 | tf_op jit(solution)/shard_map/ppermute | solution.py:68
  494.1 33.1 %collective-permute-start.52 = (bf16[2,48,8960]{2,1,0:T(8,128)(2,1)}, bf16[2,48,8960]{2,1,0:T(8,128)(2,1)}, u32[]{:S(2)}, u32[]{:S(2)}) collective-permute-start(bf16[2,48,8960]{2,1,0:T(8,128)(2,1)} %pad_maximum_fusion.6), channel_id=1, source_target_pairs={{0,8},{4,20},{8,0},{12,28},{16,24},{20,4},{24,16},{28,12},{1,9},{5... | collective-permute-start | bytes 5160968 | tf_op jit(solution)/shard_map/ppermute | solution.py:68
  494.8 20.7 %collective-permute-start.49 = (bf16[48,2240]{1,0:T(8,128)(2,1)}, bf16[48,2240]{1,0:T(8,128)(2,1)S(1)}, u32[]{:S(2)}, u32[]{:S(2)}) collective-permute-start(bf16[48,2240]{1,0:T(8,128)(2,1)} %get-tuple-element.806), channel_id=1, source_target_pairs={{0,1},{1,2},{2,3},{3,0},{4,5},{5,6},{6,7},{7,4},{8,9},{9,10},{10,1... | collective-permute-start | bytes 645128 | tf_op jit(solution)/shard_map/ppermute | solution.py:68
  539.0 23.8 %collective-permute-start.57 = (bf16[48,8960]{1,0:T(8,128)(2,1)S(1)}, bf16[48,8960]{1,0:T(8,128)(2,1)S(1)}, u32[]{:S(2)}, u32[]{:S(2)}) collective-permute-start(bf16[48,8960]{1,0:T(8,128)(2,1)S(1)} %concatenate.72), channel_id=1, source_target_pairs={{0,16},{4,12},{8,24},{12,4},{16,0},{20,28},{24,8},{28,20},{1,17},{... | collective-permute-start | bytes 2580488 | tf_op jit(solution)/shard_map/ppermute | solution.py:68
  564.2 24.3 %collective-permute-start.61 = (bf16[4,48,8960]{2,1,0:T(8,128)(2,1)S(1)}, bf16[4,48,8960]{2,1,0:T(8,128)(2,1)S(1)}, u32[]{:S(2)}, u32[]{:S(2)}) collective-permute-start(bf16[4,48,8960]{2,1,0:T(8,128)(2,1)S(1)} %pad_maximum_fusion.pieces_ref), channel_id=1, source_target_pairs={{0,4},{4,0},{8,12},{12,8},{16,20},{20,16},{24,28},{28,24},{1,5},{5... | collective-permute-start | bytes 10321928 | tf_op jit(solution)/shard_map/ppermute | solution.py:68
  564.4 24.1 %collective-permute-start.59 = (bf16[2,48,8960]{2,1,0:T(8,128)(2,1)S(1)}, bf16[2,48,8960]{2,1,0:T(8,128)(2,1)S(1)}, u32[]{:S(2)}, u32[]{:S(2)}) collective-permute-start(bf16[2,48,8960]{2,1,0:T(8,128)(2,1)S(1)} %pad_maximum_fusion.7), channel_id=1, source_target_pairs={{0,8},{4,20},{8,0},{12,28},{16,24},{20,4},{24,16},{28,12},{1,9},{5... | collective-permute-start | bytes 5160968 | tf_op jit(solution)/shard_map/ppermute | solution.py:68
  (97 other events, 1491.1 us)
Sparse Core Ops, SparseCore 0:
  10.9 97.0 all-gather.7
  110.5 76.6 all-gather.9
  264.7 73.7 reduce-scatter.2
  353.9 88.2 reduce-scatter.4
  495.0 65.6 all-gather.5

commit v10 on v9

--- a/solution.py
+++ b/solution.py
@@ -323,15 +323,20 @@
     )
 
 
-def place_gathered(order, gathered):
-    reps, shards, groups = gathered.shape[:3]
+def place_gathered(order, gathered, groups):
+    shards = lax.axis_size("shard")
+    reps = gathered.shape[0] // (shards * groups)
 
     def body(order_ref, source, *rest):
         move_blocks(
-            lambda g, k, r: source.at[r, k, g], lambda r: r, order_ref, rest[:groups], *rest[groups:]
+            lambda g, k, r: source.at[(r * shards + k) * groups + g],
+            lambda r: r,
+            order_ref,
+            rest[:groups],
+            *rest[groups:],
         )
 
-    return blocks_call(body, 1, 1, groups, shards, reps, gathered.shape[3:])(order, gathered)
+    return blocks_call(body, 1, 1, groups, shards, reps, gathered.shape[1:])(order, gathered)
 
 
 def move_blocks(source_of, place_of, order_ref, outs, held, in_sems, out_sems):
@@ -851,18 +856,12 @@
     output_arrived, up_rows = clock.wait(output_spread.moving, up_moving)
 
     gate_up = jnp.stack(
-        [jnp.stack([gate_blocks[0]] + gate_rows), jnp.stack([up_blocks[0]] + up_rows)], axis=1
-    )
-    gate_up = lax.all_gather(clock(gate_up)[0][None], "rep", axis=0, tiled=True)
+        [row for pair in zip([gate_blocks[0]] + gate_rows, [up_blocks[0]] + up_rows) for row in pair]
+    )
+    gate_up = lax.all_gather(clock(gate_up)[0], "rep", axis=0, tiled=True)
     passed = [[output_cotangent] * 2]
+    passing = clock.pass_on(shard, *passed[-1])
     output_spread.over(output_arrived)
-    passing = clock.pass_on(shard, *passed[-1])
-    output_arrived, arrived = clock.wait(output_spread.moving, passing)
-    passed.append(arrived)
-
-    passing = clock.pass_on(shard, *passed[-1]) if shards > 2 else []
-    (output_matrix,) = clock.run(place_blocks, z_order, *output_spread.finish(output_arrived))
-    output_matrix = output_matrix.reshape(width, width)
     input_matrix, normed_one = clock(input_matrix, normed_one)
     projected = jnp.dot(normed_one, input_matrix, preferred_element_type=f32) + shift_row
     key_part = rotate(
@@ -876,13 +875,18 @@
             axis=1,
         ).astype(bf16)
     )
-    (arrived,) = clock.wait(passing)
+    arrived, output_arrived = clock.wait(passing, output_spread.moving)
     passed.append(arrived)
 
-    (pair_rows,) = clock.wait(send_around(own_pairs))
+    pair_moving = send_around(own_pairs)
+    passing = clock.pass_on(shard, *passed[-1]) if shards > 2 else []
+    pair_rows, arrived = clock.wait(pair_moving, passing)
+    passed.append(arrived)
     pairs = jnp.concatenate([own_pairs] + pair_rows, axis=0)
 
     passing = clock.pass_on(shard, *passed[-1]) if shards > 3 else []
+    (output_matrix,) = clock.run(place_blocks, z_order, *output_spread.finish(output_arrived))
+    output_matrix = output_matrix.reshape(width, width)
     queries, attention_low = clock.run(
         attention_forward, projected, cosine_table, signed_sine, pairs, row_marks.T, key_marks
     )
@@ -894,7 +898,9 @@
     passed.append(arrived)
 
     normed_moving = send_around(normed_two)
-    gate_matrix, up_matrix = clock.run(place_gathered, z_order, gate_up)
+    gate_matrix, up_matrix = clock.run(
+        lambda order, gathered: place_gathered(order, gathered, 2), z_order, gate_up
+    )
     gate_matrix = gate_matrix.reshape(width, block_units)
     up_matrix = up_matrix.reshape(width, block_units)
     (normed_arrived,) = clock.wait(normed_moving)
@@ -939,6 +945,9 @@
     edges = sorted({0, shards - 2})
     inside = list(range(1, shards - 2))
 
+    up_halves = split_halves(turned_normed, d_up, shards, True)
+
+    up = Halving(clock, *up_halves, core, first, second)
     normed_own, *normed_partial = clock.run(
         lambda *operands: rows_product(operands[:2], operands[2:], True, shards),
         d_gate,
@@ -946,32 +955,32 @@
         gate_matrix,
         up_matrix,
     )
-
+    (up_arrived,) = clock.wait(up.moving)
+
+    up.along_first(up_arrived)
     normed_moving = send_some(normed_partial, edges)
+    (gate_blocks,) = clock.run(
+        lambda left, right: ordered_gradient(left, right, shards, rep_places(reps)),
+        turned_normed,
+        d_gate,
+    )
+    gate_piece = sum_over_rep(gate_blocks.reshape(width, block_units))
     (down_blocks,) = clock.run(
         lambda left, right: ordered_gradient(left, right, 1, list(range(reps))),
         turned_inner,
         cotangents,
     )
-    down_piece = sum_over_rep(down_blocks.reshape(block_units, width))
-    up_halves = split_halves(turned_normed, d_up, shards, True)
-    (normed_arrived,) = clock.wait(normed_moving)
-
+    up_arrived, normed_arrived = clock.wait(up.moving, normed_moving)
+
+    up.along_second(up_arrived)
     normed_moving = send_some(normed_partial, inside)
-    up = Halving(clock, *up_halves, core, first, second)
-    (gate_blocks,) = clock.run(
-        lambda left, right: ordered_gradient(left, right, shards, rep_places(reps)),
-        turned_normed,
-        d_gate,
-    )
-    gate_piece = sum_over_rep(gate_blocks.reshape(width, block_units))
     block_own, *block_partial = clock.run(
         lambda left, right: rows_product((left,), (right,), False, shards), inner_act, down_weight
     )
-    more_arrived, up_arrived = clock.wait(normed_moving, up.moving)
-
-    up.along_first(up_arrived)
-    block_moving = send_some(block_partial, inside)
+    up_arrived, more_arrived = clock.wait(up.moving, normed_moving)
+
+    up_blocks = clock(*blocks_of(up.finish(up_arrived)))
+    up_moving = send_blocks(up_blocks)
     normed_two_gradient = total_of([normed_own] + normed_arrived + more_arrived)
     gain_two_gradient = jnp.sum(normed_two_gradient * unit_two, axis=0)
     hidden_gradient = output_cotangent.astype(f32) + norm_back(
@@ -990,15 +999,16 @@
         key_marks.T,
     )
     output_halves = split_halves(attention_low, branch_gradient, shards, False)
-    up_arrived, block_arrived = clock.wait(up.moving, block_moving)
+    (up_rows,) = clock.wait(up_moving)
 
     pair_moving = send_back(pair_partial)
     output = Halving(clock, *output_halves, core, first, second)
+    up_piece = side_by_side(up_blocks[:1] + up_rows)
     pair_arrived, output_arrived = clock.wait(pair_moving, output.moving)
 
-    up.along_second(up_arrived)
+    up_spread = spread(up_piece)
     output.along_first(output_arrived)
-    block_moving = send_some(block_partial, edges[:1])
+    block_moving = send_some(block_partial, inside)
     projected_gradient, bias_sum = clock.run(
         lambda *operands: join_projected(operands[0], operands[3:], *operands[1:3]),
         d_queries,
@@ -1008,15 +1018,16 @@
         *pair_arrived,
     )
     projected_halves = split_halves(normed_one, projected_gradient, shards, False)
-    up_arrived, output_arrived, more_arrived = clock.wait(up.moving, output.moving, block_moving)
-    block_arrived = block_arrived + more_arrived
+    up_arrived, output_arrived, block_arrived = clock.wait(
+        up_spread.moving, output.moving, block_moving
+    )
 
     projected = Halving(clock, *projected_halves, core, first, second)
     output.along_second(output_arrived)
-    block_moving = send_some(block_partial, edges[1:])
-    (down_piece,) = clock(down_piece)
-    down_gathered = lax.all_gather(down_piece, "rep", axis=0, tiled=True)
-    up_blocks = clock(*blocks_of(up.finish(up_arrived)))
+    up_spread.along(up_arrived)
+    block_moving = send_some(block_partial, edges)
+    (gate_piece,) = clock(gate_piece)
+    down_piece = sum_over_rep(clock(down_blocks)[0].reshape(block_units, width))
     projected_gradient, hidden_gradient = clock(projected_gradient, hidden_gradient)
     normed_one_gradient = times_transposed(projected_gradient, input_matrix)
     gain_one_gradient = jnp.sum(normed_one_gradient * unit_one, axis=0)
@@ -1031,7 +1042,8 @@
     block_arrived = block_arrived + more_arrived
 
     projected.along_first(projected_arrived)
-    up_moving = send_blocks(up_blocks)
+    gate_blocks = clock(*blocks_of(gate_piece.reshape(shards, part_rows, block_units)))
+    gate_moving = send_blocks(gate_blocks)
     output_blocks = clock(*blocks_of(output.finish(output_arrived)))
     (block_out,) = clock(total_of([hidden, block_own] + block_arrived).astype(bf16))
     bias_gradient = bias_sum[0]
@@ -1045,49 +1057,43 @@
     (small,) = clock(
         jnp.concatenate([part.reshape(shards, -1) for part in small_parts], axis=1)
     )
-    projected_arrived, up_rows = clock.wait(projected.moving, up_moving)
+    projected_arrived, up_arrived, gate_rows = clock.wait(
+        projected.moving, up_spread.moving, gate_moving
+    )
 
     projected.along_second(projected_arrived)
+    gate_spread = spread(side_by_side(gate_blocks[:1] + gate_rows))
     output_moving = send_blocks(output_blocks)
-    up_spread = spread(side_by_side(up_blocks[:1] + up_rows))
-    projected_arrived, output_rows, up_arrived = clock.wait(
-        projected.moving, output_moving, up_spread.moving
-    )
-
-    (gate_piece,) = clock(gate_piece)
-    gate_blocks = clock(*blocks_of(gate_piece.reshape(shards, part_rows, block_units)))
-    gate_moving = send_blocks(gate_blocks)
-    up_spread.along(up_arrived)
+    projected_arrived, gate_arrived, output_rows = clock.wait(
+        projected.moving, gate_spread.moving, output_moving
+    )
+
+    input_blocks = clock(*blocks_of(projected.finish(projected_arrived)))
+    input_moving = send_blocks(input_blocks)
+    gate_spread.along(gate_arrived)
     output_spread = spread(row_sum(output_blocks[:1], output_rows))
-    input_blocks = clock(*blocks_of(projected.finish(projected_arrived)))
-    gate_rows, up_arrived, output_arrived = clock.wait(
-        gate_moving, up_spread.moving, output_spread.moving
-    )
-
-    input_moving = send_blocks(input_blocks)
-    gate_spread = spread(side_by_side(gate_blocks[:1] + gate_rows))
-    output_spread.along(output_arrived)
     input_rows, gate_arrived, output_arrived = clock.wait(
         input_moving, gate_spread.moving, output_spread.moving
     )
 
-    gate_spread.along(gate_arrived)
     input_spread = spread(row_sum(input_blocks[:1], input_rows))
+    output_spread.along(output_arrived)
     up_spread.over(up_arrived)
+    gate_spread.over(gate_arrived)
+    small_moving = clock.send(core, [small], [1])
+    (down_piece,) = clock(down_piece)
+    down_gathered = lax.all_gather(down_piece, "rep", axis=0, tiled=True)
+    input_arrived, output_arrived, up_arrived, gate_arrived, small_arrived = clock.wait(
+        input_spread.moving, output_spread.moving, up_spread.moving, gate_spread.moving, small_moving
+    )
+    small = total_of([small] + small_arrived)
+
+    input_spread.along(input_arrived)
     output_spread.over(output_arrived)
-    small_moving = clock.send(core, [small], [1])
-    gate_arrived, input_arrived, up_arrived, output_arrived, small_arrived = clock.wait(
-        gate_spread.moving, input_spread.moving, up_spread.moving, output_spread.moving, small_moving
-    )
-    small = total_of([small] + small_arrived)
-
-    input_spread.along(input_arrived)
-    gate_spread.over(gate_arrived)
     small_moving = clock.send(first, [small] * (first.size - 1), range(1, first.size))
     (up_total,) = clock.run(widen_pieces, *up_spread.finish(up_arrived))
-    (output_total,) = clock.run(widen_pieces, *output_spread.finish(output_arrived))
-    input_arrived, gate_arrived, small_arrived = clock.wait(
-        input_spread.moving, gate_spread.moving, small_moving
+    input_arrived, output_arrived, small_arrived = clock.wait(
+        input_spread.moving, output_spread.moving, small_moving
     )
     small = total_of([small] + small_arrived)
 
@@ -1098,11 +1104,12 @@
     small_blocks = clock(*blocks_of(total_of([small] + small_arrived)))
 
     small_moving = send_blocks(small_blocks)
+    (output_total,) = clock.run(widen_pieces, *output_spread.finish(output_arrived))
     (input_total,) = clock.run(widen_pieces, *input_spread.finish(input_arrived))
+    (small_arrived,) = clock.wait(small_moving)
+    small = total_of(small_blocks[:1] + small_arrived)
     (down_gathered,) = clock(down_gathered)
     (down_total,) = clock(down_gathered.astype(f32))
-    (small_arrived,) = clock.wait(small_moving)
-    small = total_of(small_blocks[:1] + small_arrived)
 
     small = small + clock.token[0, 0]
     small_totals, at = [], 0

time: 651 us -> 632 us (0.971)
  waiting for transfers between devices: 235 us -> 225 us
  local copies, waits for them, and re-layouts: 36 us -> 27.6 us
    all_gather x1 -> x0, local copies, waits for them, and re-layouts: 10.6 us -> none  [on_device(): gate_up = lax.all_gather(clock(gate_up)[0][None], 'rep', axis=0, tiled=True)]
    ppermute x6, waiting for transfers between devices: 17.6 us -> 9.13 us  [pass_on(): return lax.ppermute(value, self.name, pairs)]
    ppermute x66, waiting for transfers between devices: 217 us -> 210 us  [shift(): return lax.ppermute(value, self.name, self.pairs(step % self.size))]
  transfers between devices with their start and end apart: 77 -> 77, of which waited for: 38 -> 35; matrix products, arithmetic and copies ran while one was open for 16% -> 14% of each run, Pallas kernels for 15% -> 18%
where the time goes in v10:
time: 632 us; the launch traced here: 622 us
  waiting for transfers between devices  225 us (36%)
  Pallas kernels  143 us (23%)
  starting transfers between devices  129 us (20%)
  other arithmetic  67.6 us (11%)
  local copies, waits for them, and re-layouts  27.6 us (4%)
  matrix products  15.6 us (2%)
  between operations  15.2 us (2%)
    ppermute x66, waiting for transfers between devices, shift(): return lax.ppermute(value, self.name, self.pairs(step % self.size))  210 us
    ppermute x66, starting transfers between devices, shift(): return lax.ppermute(value, self.name, self.pairs(step % self.size))  103 us
    ppermute x6, starting transfers between devices, pass_on(): return lax.ppermute(value, self.name, pairs)  25.4 us
    pallas_call x1, Pallas kernels, feed_forward(): pl.pallas_call(body, grid=(steps,), out_shape=[jax.ShapeDtypeStruct((coun...  23.7 us
    pallas_call x2, Pallas kernels, rows_product(): pl.pallas_call(body, grid=(pl.cdiv(columns, TILE),), out_shape=[jax.Shape...  23.2 us
    pallas_call x4, Pallas kernels, widen_pieces(): pl.pallas_call(body, out_shape=jax.ShapeDtypeStruct((reps, rows, columns)...  21.3 us
    pallas_call x3, Pallas kernels, split_gradient(): pl.pallas_call(body, grid=(pl.cdiv(columns, TILE),), out_shape=[jax.Shape...  20 us
    pallas_call x2, Pallas kernels, ordered_gradient(): pl.pallas_call(body, grid=(pl.cdiv(columns, TILE),), out_shape=[jax.Shape...  19.2 us
  transfers between devices with their start and end apart: 77, of which 35 were waited for; matrix products, arithmetic and copies ran while one was open for 14% of the time, Pallas kernels for 18%

profile of v10, /device:TPU:0, one launch (start us, length us, event | category | flops | bytes accessed | tf_op | source)
XLA Modules:
  0.0 622.4 jit_solution(17217172250743203986)
XLA Ops:
  32.1 6.5 %collective-permute-start.4 = (bf16[48,2240]{1,0:T(8,128)(2,1)S(1)}, bf16[48,2240]{1,0:T(8,128)(2,1)S(1)}, u32[]{:S(2)}, u32[]{:S(2)}) collective-permute-start(bf16[48,2240]{1,0:T(8,128)(2,1)S(1)} %get-tuple-element.483), channel_id=1, source_target_pairs={{0,1},{1,2},{2,3},{3,0},{4,5},{5,6},{6,7},{7,4},{8,9},{9,10},{10,1... | collective-permute-start | bytes 645128 | tf_op jit(solution)/shard_map/ppermute | solution.py:68
  46.9 13.9 %collective-permute-done.5 = bf16[48,2240]{1,0:T(8,128)(2,1)S(1)} collective-permute-done((bf16[48,2240]{1,0:T(8,128)(2,1)S(1)}, bf16[48,2240]{1,0:T(8,128)(2,1)S(1)}, u32[]{:S(2)}, u32[]{:S(2)}) %collective-permute-start.5) | collective-permute-done | bytes 215072 | tf_op jit(solution)/shard_map/ppermute | solution.py:68
  63.8 5.6 collective-permute-start.8
  72.7 7.1 %collective-permute-done.8 = bf16[48,2240]{1,0:T(8,128)(2,1)S(1)} collective-permute-done((bf16[48,2240]{1,0:T(8,128)(2,1)S(1)}, bf16[48,2240]{1,0:T(8,128)(2,1)S(1)}, u32[]{:S(2)}, u32[]{:S(2)}) %collective-permute-start.8) | collective-permute-done | bytes 215072 | tf_op jit(solution)/shard_map/ppermute | solution.py:68
  79.8 17.8 %collective-permute-done.9 = bf16[48,2240]{1,0:T(8,128)(2,1)S(1)} collective-permute-done((bf16[48,2240]{1,0:T(8,128)(2,1)S(1)}, bf16[48,2240]{1,0:T(8,128)(2,1)S(1)}, u32[]{:S(2)}, u32[]{:S(2)}) %collective-permute-start.9) | collective-permute-done | bytes 215072 | tf_op jit(solution)/shard_map/ppermute | solution.py:68
  105.3 14.5 %collective-permute-start.11 = (bf16[160,1536]{1,0:T(8,128)(2,1)S(1)}, bf16[160,1536]{1,0:T(8,128)(2,1)}, u32[]{:S(2)}, u32[]{:S(2)}) collective-permute-start(bf16[160,1536]{1,0:T(8,128)(2,1)S(1)} %copy-done.16), channel_id=1, source_target_pairs={{0,1},{1,2},{2,3},{4,5},{5,6},{6,7},{8,9},{9,10},{10,11},{12,13},{... | collective-permute-start | bytes 1474568 | tf_op jit(solution)/shard_map/ppermute | solution.py:73
  146.1 8.7 %collective-permute-done.14 = bf16[160,512]{1,0:T(8,128)(2,1)S(1)} collective-permute-done((bf16[160,512]{1,0:T(8,128)(2,1)S(1)}, bf16[160,512]{1,0:T(8,128)(2,1)S(1)}, u32[]{:S(2)}, u32[]{:S(2)}) %collective-permute-start.14) | collective-permute-done | bytes 163872 | tf_op jit(solution)/shard_map/ppermute | solution.py:68
  154.8 7.9 %collective-permute-done.15 = bf16[160,512]{1,0:T(8,128)(2,1)S(1)} collective-permute-done((bf16[160,512]{1,0:T(8,128)(2,1)S(1)}, bf16[160,512]{1,0:T(8,128)(2,1)S(1)}, u32[]{:S(2)}, u32[]{:S(2)}) %collective-permute-start.15) | collective-permute-done | bytes 163872 | tf_op jit(solution)/shard_map/ppermute | solution.py:68
  175.4 5.7 attention_forward.1
  194.0 11.7 %place_blocks.3 = (bf16[4,8,48,2240]{3,2,1,0:T(8,128)(2,1)}, bf16[4,8,48,2240]{3,2,1,0:T(8,128)(2,1)}) custom-call(s32[4]{0:T(128)} %pad_add_fusion.5.order_ref, bf16[64,48,2240]{2,1,0:T(8,128)(2,1)} %all-gather.5.cloned.1.call-done.source), custom_call_target="tpu_custom_call" | custom-call | flops 1 | bytes 1 | tf_op jit(solution)/shard_map/place_blocks/pallas_call | solution.py:339
  205.6 15.1 %collective-permute-done.22 = bf16[160,1536]{1,0:T(8,128)(2,1)} collective-permute-done((bf16[160,1536]{1,0:T(8,128)(2,1)S(1)}, bf16[160,1536]{1,0:T(8,128)(2,1)}, u32[]{:S(2)}, u32[]{:S(2)}) %collective-permute-start.22) | collective-permute-done | bytes 491552 | tf_op jit(solution)/shard_map/ppermute | solution.py:68
  223.5 23.7 %feed_forward.1 = (bf16[640,2240]{1,0:T(8,128)(2,1)}, bf16[640,2240]{1,0:T(8,128)(2,1)}, bf16[640,2240]{1,0:T(8,128)(2,1)}, bf16[1536,640]{1,0:T(8,128)(2,1)}, bf16[2240,640]{1,0:T(8,128)(2,1)}) custom-call(bf16[640,1536]{1,0:T(8,128)(2,1)} %pad_maximum_fusion.3.rows_ref, bf16[640,1536]{1,0:T(8,128)(2,1)} %pad_maximum_fusion.4.cotangents_ref.right_ref, ...), custom_call_target="tpu_custom_call" | custom-call | flops 1 | bytes 1 | tf_op jit(solution)/shard_map/feed_forward/pallas_call | solution.py:477
  247.2 9.9 %split_gradient.3 = (bf16[4,4,48,2240]{3,2,1,0:T(8,128)(2,1)}, bf16[4,4,48,2240]{3,2,1,0:T(8,128)(2,1)}) custom-call(s32[1]{0:T(128)} %bitcast.46.core_ref, bf16[1536,640]{1,0:T(8,128)(2,1)} %get-tuple-element.622.left_ref, bf16[640,2240]{1,0:T(8,128)(2,1)} %get-tuple-element.605.right_ref.refs_1_), custom_call_target="tpu_custom_call" | custom-call | flops 1 | bytes 1 | tf_op jit(solution)/shard_map/split_gradient/pallas_call | solution.py:533
  257.1 14.8 %rows_product.2 = (bf16[160,1536]{1,0:T(8,128)(2,1)}, bf16[160,1536]{1,0:T(8,128)(2,1)}, bf16[160,1536]{1,0:T(8,128)(2,1)}, bf16[160,1536]{1,0:T(8,128)(2,1)}) custom-call(bf16[640,2240]{1,0:T(8,128)(2,1)} %get-tuple-element.623.refs_0_.right_ref, bf16[640,2240]{1,0:T(8,128)(2,1)} %get-tuple-element.605.right_ref.refs_1_, bf16[1536,2240]{1,0:T(8,128)(2,1)} %bitcast.183, ...), custom_call_target="tpu_custom_call" | custom-call | flops 1 | bytes 1 | tf_op jit(solution)/shard_map/rows_product/pallas_call | solution.py:603
  275.0 9.9 %ordered_gradient.2 = bf16[8,4,48,2240]{3,2,1,0:T(8,128)(2,1)} custom-call(bf16[1536,640]{1,0:T(8,128)(2,1)} %get-tuple-element.622.left_ref, bf16[640,2240]{1,0:T(8,128)(2,1)} %get-tuple-element.623.refs_0_.right_ref), custom_call_target="tpu_custom_call" | custom-call | flops 1 | bytes 1 | tf_op jit(solution)/shard_map/ordered_gradient/pallas_call | solution.py:563
  285.0 11.8 %collective-permute-start.26 = (bf16[160,1536]{1,0:T(8,128)(2,1)}, bf16[160,1536]{1,0:T(8,128)(2,1)S(1)}, u32[]{:S(2)}, u32[]{:S(2)}) collective-permute-start(bf16[160,1536]{1,0:T(8,128)(2,1)} %get-tuple-element.631), channel_id=1, source_target_pairs={{0,3},{1,0},{2,1},{3,2},{4,7},{5,4},{6,5},{7,6},{8,11},{9,8},{10,9... | collective-permute-start | bytes 1474568 | tf_op jit(solution)/shard_map/ppermute | solution.py:68
  297.4 9.3 %ordered_gradient.3 = bf16[8,1,280,1536]{3,2,1,0:T(8,128)(2,1)} custom-call(bf16[2240,640]{1,0:T(8,128)(2,1)} %get-tuple-element.627.left_ref, bf16[640,1536]{1,0:T(8,128)(2,1)} %pad_maximum_fusion.4.cotangents_ref.right_ref), custom_call_target="tpu_custom_call" | custom-call | flops 1 | bytes 1 | tf_op jit(solution)/shard_map/ordered_gradient/pallas_call | solution.py:563
  308.7 10.8 %collective-permute-done.27 = bf16[160,1536]{1,0:T(8,128)(2,1)S(1)} collective-permute-done((bf16[160,1536]{1,0:T(8,128)(2,1)S(1)}, bf16[160,1536]{1,0:T(8,128)(2,1)S(1)}, u32[]{:S(2)}, u32[]{:S(2)}) %collective-permute-start.27) | collective-permute-done | bytes 491552 | tf_op jit(solution)/shard_map/ppermute | solution.py:68
  327.5 8.4 %rows_product.3 = (bf16[160,1536]{1,0:T(8,128)(2,1)}, bf16[160,1536]{1,0:T(8,128)(2,1)}, bf16[160,1536]{1,0:T(8,128)(2,1)}, bf16[160,1536]{1,0:T(8,128)(2,1)}) custom-call(bf16[640,2240]{1,0:T(8,128)(2,1)} %get-tuple-element.640.refs_0_, bf16[2240,1536]{1,0:T(8,128)(2,1)} %refs_1_), custom_call_target="tpu_custom_call" | custom-call | flops 1 | bytes 1 | tf_op jit(solution)/shard_map/rows_product/pallas_call | solution.py:603
  335.9 11.6 %collective-permute-done.29 = bf16[160,1536]{1,0:T(8,128)(2,1)S(1)} collective-permute-done((bf16[160,1536]{1,0:T(8,128)(2,1)S(1)}, bf16[160,1536]{1,0:T(8,128)(2,1)S(1)}, u32[]{:S(2)}, u32[]{:S(2)}) %collective-permute-start.29) | collective-permute-done | bytes 491552 | tf_op jit(solution)/shard_map/ppermute | solution.py:68
  362.9 7.6 %attention_backward.1 = (bf16[160,1536]{1,0:T(8,128)(2,1)}, bf16[160,512]{1,0:T(8,128)(2,1)}, bf16[160,512]{1,0:T(8,128)(2,1)}, bf16[160,512]{1,0:T(8,128)(2,1)}, bf16[160,512]{1,0:T(8,128)(2,1)}) custom-call(bf16[2,960,128]{2,1,0:T(8,128)(2,1)} %get-tuple-element.668.queries_ref, bf16[160,1536]{1,0:T(8,128)(2,1)} %convolution_convert_fusion.gradient_ref, ...), custom_call_target="tpu_custom_call" | custom-call | flops 1 | bytes 1 | tf_op jit(solution)/shard_map/attention_backward/pallas_call | solution.py:705
  384.9 11.1 %collective-permute-done.34.refs_2_ = bf16[160,512]{1,0:T(8,128)(2,1)} collective-permute-done((bf16[160,512]{1,0:T(8,128)(2,1)}, bf16[160,512]{1,0:T(8,128)(2,1)}, u32[]{:S(2)}, u32[]{:S(2)}) %collective-permute-start.34) | collective-permute-done | bytes 163872 | tf_op jit(solution)/shard_map/ppermute | solution.py:68
  410.1 13.9 %collective-permute-done.39 = bf16[160,1536]{1,0:T(8,128)(2,1)} collective-permute-done((bf16[160,1536]{1,0:T(8,128)(2,1)}, bf16[160,1536]{1,0:T(8,128)(2,1)}, u32[]{:S(2)}, u32[]{:S(2)}) %collective-permute-start.39) | collective-permute-done | bytes 491552 | tf_op jit(solution)/shard_map/ppermute | solution.py:68
  445.4 11.2 %collective-permute-done.43 = bf16[160,1536]{1,0:T(8,128)(2,1)} collective-permute-done((bf16[160,1536]{1,0:T(8,128)(2,1)}, bf16[160,1536]{1,0:T(8,128)(2,1)}, u32[]{:S(2)}, u32[]{:S(2)}) %collective-permute-start.43) | collective-permute-done | bytes 491552 | tf_op jit(solution)/shard_map/ppermute | solution.py:68
  474.3 6.8 %collective-permute-done.47 = bf16[48,2240]{1,0:T(8,128)(2,1)S(1)} collective-permute-done((bf16[48,2240]{1,0:T(8,128)(2,1)}, bf16[48,2240]{1,0:T(8,128)(2,1)S(1)}, u32[]{:S(2)}, u32[]{:S(2)}) %collective-permute-start.47) | collective-permute-done | bytes 215072 | tf_op jit(solution)/shard_map/ppermute | solution.py:68
  481.9 13.2 %collective-permute-done.44 = bf16[2,4,48,2048]{3,2,1,0:T(8,128)(2,1)} collective-permute-done((bf16[2,4,48,2048]{3,2,1,0:T(8,128)(2,1)}, bf16[2,4,48,2048]{3,2,1,0:T(8,128)(2,1)}, u32[]{:S(2)}, u32[]{:S(2)}) %collective-permute-start.44) | collective-permute-done | bytes 1572896 | tf_op jit(solution)/shard_map/ppermute | solution.py:68
  514.6 8.8 %collective-permute-done.49 = bf16[4,48,2048]{2,1,0:T(8,128)(2,1)S(1)} collective-permute-done((bf16[4,48,2048]{2,1,0:T(8,128)(2,1)S(1)}, bf16[4,48,2048]{2,1,0:T(8,128)(2,1)S(1)}, u32[]{:S(2)}, u32[]{:S(2)}) %collective-permute-start.49) | collective-permute-done | bytes 786464 | tf_op jit(solution)/shard_map/ppermute | solution.py:68
  554.1 7.7 %collective-permute-done.63 = f32[4,1280]{1,0:T(4,128)S(1)} collective-permute-done((f32[4,1280]{1,0:T(4,128)S(1)}, f32[4,1280]{1,0:T(4,128)S(1)}, u32[]{:S(2)}, u32[]{:S(2)}) %collective-permute-start.63) | collective-permute-done | bytes 20512 | tf_op jit(solution)/shard_map/ppermute | solution.py:68
  565.3 7.3 %widen_pieces.4 = f32[8,48,8960]{2,1,0:T(8,128)} custom-call(s32[8]{0:T(128)} %stack.239.places_ref, bf16[4,48,8960]{2,1,0:T(8,128)(2,1)} %pad_maximum_fusion.pieces_ref, bf16[4,48,8960]{2,1,0:T(8,128)(2,1)} %collective-permute-done.61.others_ref), custom_call_target="tpu_custom_call" | custom-call | flops 1 | bytes 1 | tf_op jit(solution)/shard_map/widen_pieces/pallas_call | solution.py:415
  577.4 7.5 %widen_pieces.5 = f32[8,48,8960]{2,1,0:T(8,128)} custom-call(s32[8]{0:T(128)} %stack.239.places_ref, bf16[4,48,8960]{2,1,0:T(8,128)(2,1)} %pad_maximum_fusion.1.pieces_ref, bf16[4,48,8960]{2,1,0:T(8,128)(2,1)} %copy-done.7), custom_call_target="tpu_custom_call" | custom-call | flops 1 | bytes 1 | tf_op jit(solution)/shard_map/widen_pieces/pallas_call | solution.py:415
  597.0 5.6 all-gather.7.cloned.1.call-done
  602.6 10.2 %convert_element_type.352 = f32[2240,1536]{1,0:T(8,128)} convert(bf16[2240,1536]{1,0:T(8,128)(2,1)} %all-gather.7.cloned.1.call-done) | non-fusion elementwise | flops 3440640 | bytes 20643840 | tf_op jit(solution)/shard_map/convert_element_type | solution.py:1112
  (369 shorter events, 271.7 us)
Async XLA Ops:
  7.2 113.9 %all-gather.9.cloned.1.call-start = ((), (), s32[]{:S(2)}) async-start(), calls=%async_computation.6 | async-start | bytes 6488064 | tf_op jit(solution)/shard_map/all_gather | solution.py:796
  9.3 184.7 %all-gather.5.cloned.1.call-start = ((), (), s32[]{:S(2)}) async-start(), calls=%async_computation.2 | async-start | bytes 15925248 | tf_op jit(solution)/shard_map/all_gather | solution.py:861
  29.9 31.1 %collective-permute-start.3 = (bf16[1,4,48,1536]{3,2,1,0:T(8,128)(2,1)S(1)}, bf16[1,4,48,1536]{3,2,1,0:T(8,128)(2,1)S(1)}, u32[]{:S(2)}, u32[]{:S(2)}) collective-permute-start(bf16[1,4,48,1536]{3,2,1,0:T(8,128)(2,1)S(1)} %get-tuple-element.482), channel_id=1, source_target_pairs={{0,16},{4,12},{8,24},{12,4},{16,0},{20,28},{24,8},{28,20},{1,17},{... | collective-permute-start | bytes 1769480 | tf_op jit(solution)/shard_map/ppermute | solution.py:68
  61.0 36.6 %collective-permute-start.7 = (bf16[2,1,4,48,1536]{4,3,2,1,0:T(8,128)(2,1)S(1)}, bf16[2,1,4,48,1536]{4,3,2,1,0:T(8,128)(2,1)S(1)}, u32[]{:S(2)}, u32[]{:S(2)}) collective-permute-start(bf16[2,1,4,48,1536]{4,3,2,1,0:T(8,128)(2,1)S(1)} %pad_maximum_fusion.7), channel_id=1, source_target_pairs={{0,8},{4,20},{8,0},{12,28},{16,24},{20,4},{24,16},{28,12},{1,9},{5... | collective-permute-start | bytes 3538952 | tf_op jit(solution)/shard_map/ppermute | solution.py:68
  69.3 28.3 %collective-permute-start.9 = (bf16[48,2240]{1,0:T(8,128)(2,1)S(1)}, bf16[48,2240]{1,0:T(8,128)(2,1)S(1)}, u32[]{:S(2)}, u32[]{:S(2)}) collective-permute-start(bf16[48,2240]{1,0:T(8,128)(2,1)S(1)} %get-tuple-element.493), channel_id=1, source_target_pairs={{0,2},{1,3},{2,0},{3,1},{4,6},{5,7},{6,4},{7,5},{8,10},{9,11},{10,... | collective-permute-start | bytes 645128 | tf_op jit(solution)/shard_map/ppermute | solution.py:68
  72.0 25.6 %collective-permute-start.10 = (bf16[48,2240]{1,0:T(8,128)(2,1)S(1)}, bf16[48,2240]{1,0:T(8,128)(2,1)S(1)}, u32[]{:S(2)}, u32[]{:S(2)}) collective-permute-start(bf16[48,2240]{1,0:T(8,128)(2,1)S(1)} %get-tuple-element.494), channel_id=1, source_target_pairs={{0,3},{1,0},{2,1},{3,2},{4,7},{5,4},{6,5},{7,6},{8,11},{9,8},{10,9... | collective-permute-start | bytes 645128 | tf_op jit(solution)/shard_map/ppermute | solution.py:68
  102.2 332.5 %reduce-scatter.3.cloned.1.call-start = ((), (), s32[]{:S(2)}) async-start(), calls=%async_computation.3 | async-start | bytes 7962624 | tf_op jit(solution)/shard_map/reduce_scatter | solution.py:937
  105.2 29.9 %collective-permute-start.13 = (bf16[4,1,4,48,1536]{4,3,2,1,0:T(8,128)(2,1)}, bf16[4,1,4,48,1536]{4,3,2,1,0:T(8,128)(2,1)}, u32[]{:S(2)}, u32[]{:S(2)}) collective-permute-start(bf16[4,1,4,48,1536]{4,3,2,1,0:T(8,128)(2,1)} %pad_maximum_fusion.2.pieces_ref), channel_id=1, source_target_pairs={{0,4},{4,0},{8,12},{12,8},{16,20},{20,16},{24,28},{28,24},{1,5},{5... | collective-permute-start | bytes 7077896 | tf_op jit(solution)/shard_map/ppermute | solution.py:68
  105.3 24.8 %collective-permute-start.11 = (bf16[160,1536]{1,0:T(8,128)(2,1)S(1)}, bf16[160,1536]{1,0:T(8,128)(2,1)}, u32[]{:S(2)}, u32[]{:S(2)}) collective-permute-start(bf16[160,1536]{1,0:T(8,128)(2,1)S(1)} %copy-done.16), channel_id=1, source_target_pairs={{0,1},{1,2},{2,3},{4,5},{5,6},{6,7},{8,9},{9,10},{10,11},{12,13},{... | collective-permute-start | bytes 1474568 | tf_op jit(solution)/shard_map/ppermute | solution.py:73
  135.0 27.7 %collective-permute-start.17 = (bf16[160,1536]{1,0:T(8,128)(2,1)}, bf16[160,1536]{1,0:T(8,128)(2,1)}, u32[]{:S(2)}, u32[]{:S(2)}) collective-permute-start(bf16[160,1536]{1,0:T(8,128)(2,1)} %collective-permute-done.11), channel_id=1, source_target_pairs={{0,1},{1,2},{2,3},{4,5},{5,6},{6,7},{8,9},{9,10},{10,11},{12,13},{... | collective-permute-start | bytes 1474568 | tf_op jit(solution)/shard_map/ppermute | solution.py:73
  137.3 25.4 %collective-permute-start.18 = (bf16[160,1536]{1,0:T(8,128)(2,1)}, bf16[160,1536]{1,0:T(8,128)(2,1)}, u32[]{:S(2)}, u32[]{:S(2)}) collective-permute-start(bf16[160,1536]{1,0:T(8,128)(2,1)} %collective-permute-done.12), channel_id=1, source_target_pairs={{1,0},{2,1},{3,2},{5,4},{6,5},{7,6},{9,8},{10,9},{11,10},{13,12},{... | collective-permute-start | bytes 1474568 | tf_op jit(solution)/shard_map/ppermute | solution.py:73
  162.7 23.3 %collective-permute-start.19 = (bf16[160,1536]{1,0:T(8,128)(2,1)}, bf16[160,1536]{1,0:T(8,128)(2,1)S(1)}, u32[]{:S(2)}, u32[]{:S(2)}) collective-permute-start(bf16[160,1536]{1,0:T(8,128)(2,1)} %collective-permute-done.17), channel_id=1, source_target_pairs={{0,1},{1,2},{2,3},{4,5},{5,6},{6,7},{8,9},{9,10},{10,11},{12,13},{... | collective-permute-start | bytes 1474568 | tf_op jit(solution)/shard_map/ppermute | solution.py:73
  188.7 32.0 %collective-permute-start.22 = (bf16[160,1536]{1,0:T(8,128)(2,1)S(1)}, bf16[160,1536]{1,0:T(8,128)(2,1)}, u32[]{:S(2)}, u32[]{:S(2)}) collective-permute-start(bf16[160,1536]{1,0:T(8,128)(2,1)S(1)} %multiply_convert_fusion), channel_id=1, source_target_pairs={{0,2},{1,3},{2,0},{3,1},{4,6},{5,7},{6,4},{7,5},{8,10},{9,11},{10,... | collective-permute-start | bytes 1474568 | tf_op jit(solution)/shard_map/ppermute | solution.py:68
  188.7 32.0 %collective-permute-start.23 = (bf16[160,1536]{1,0:T(8,128)(2,1)S(1)}, bf16[160,1536]{1,0:T(8,128)(2,1)}, u32[]{:S(2)}, u32[]{:S(2)}) collective-permute-start(bf16[160,1536]{1,0:T(8,128)(2,1)S(1)} %multiply_convert_fusion), channel_id=1, source_target_pairs={{0,3},{1,0},{2,1},{3,2},{4,7},{5,4},{6,5},{7,6},{8,11},{9,8},{10,9... | collective-permute-start | bytes 1474568 | tf_op jit(solution)/shard_map/ppermute | solution.py:68
  275.0 44.5 %collective-permute-start.25 = (bf16[2,4,48,2240]{3,2,1,0:T(8,128)(2,1)}, bf16[2,4,48,2240]{3,2,1,0:T(8,128)(2,1)}, u32[]{:S(2)}, u32[]{:S(2)}) collective-permute-start(bf16[2,4,48,2240]{3,2,1,0:T(8,128)(2,1)} %fusion), channel_id=1, source_target_pairs={{0,8},{4,20},{8,0},{12,28},{16,24},{20,4},{24,16},{28,12},{1,9},{5... | collective-permute-start | bytes 5160968 | tf_op jit(solution)/shard_map/ppermute | solution.py:68
  285.0 266.5 %reduce-scatter.5.cloned.1.call-start = ((), (), s32[]{:S(2)}) async-start(), calls=%async_computation.4 | async-start | bytes 7741440 | tf_op jit(solution)/shard_map/reduce_scatter | solution.py:937
  285.0 23.7 %collective-permute-start.26 = (bf16[160,1536]{1,0:T(8,128)(2,1)}, bf16[160,1536]{1,0:T(8,128)(2,1)S(1)}, u32[]{:S(2)}, u32[]{:S(2)}) collective-permute-start(bf16[160,1536]{1,0:T(8,128)(2,1)} %get-tuple-element.631), channel_id=1, source_target_pairs={{0,3},{1,0},{2,1},{3,2},{4,7},{5,4},{6,5},{7,6},{8,11},{9,8},{10,9... | collective-permute-start | bytes 1474568 | tf_op jit(solution)/shard_map/ppermute | solution.py:68
  296.8 22.6 %collective-permute-start.27 = (bf16[160,1536]{1,0:T(8,128)(2,1)S(1)}, bf16[160,1536]{1,0:T(8,128)(2,1)S(1)}, u32[]{:S(2)}, u32[]{:S(2)}) collective-permute-start(bf16[160,1536]{1,0:T(8,128)(2,1)S(1)} %copy-done.40), channel_id=1, source_target_pairs={{0,1},{1,2},{2,3},{3,0},{4,5},{5,6},{6,7},{7,4},{8,9},{9,10},{10,1... | collective-permute-start | bytes 1474568 | tf_op jit(solution)/shard_map/ppermute | solution.py:68
  322.6 26.6 %collective-permute-start.28 = (bf16[4,48,2240]{2,1,0:T(8,128)(2,1)}, bf16[4,48,2240]{2,1,0:T(8,128)(2,1)}, u32[]{:S(2)}, u32[]{:S(2)}) collective-permute-start(bf16[4,48,2240]{2,1,0:T(8,128)(2,1)} %fusion.3), channel_id=1, source_target_pairs={{0,16},{4,12},{8,24},{12,4},{16,0},{20,28},{24,8},{28,20},{1,17},{... | collective-permute-start | bytes 2580488 | tf_op jit(solution)/shard_map/ppermute | solution.py:68
  323.8 23.7 %collective-permute-start.29 = (bf16[160,1536]{1,0:T(8,128)(2,1)S(1)}, bf16[160,1536]{1,0:T(8,128)(2,1)S(1)}, u32[]{:S(2)}, u32[]{:S(2)}) collective-permute-start(bf16[160,1536]{1,0:T(8,128)(2,1)S(1)} %copy-done.39), channel_id=1, source_target_pairs={{0,2},{1,3},{2,0},{3,1},{4,6},{5,7},{6,4},{7,5},{8,10},{9,11},{10,... | collective-permute-start | bytes 1474568 | tf_op jit(solution)/shard_map/ppermute | solution.py:68
  399.0 25.1 %collective-permute-start.38 = (bf16[2,4,48,1536]{3,2,1,0:T(8,128)(2,1)}, bf16[2,4,48,1536]{3,2,1,0:T(8,128)(2,1)}, u32[]{:S(2)}, u32[]{:S(2)}) collective-permute-start(bf16[2,4,48,1536]{3,2,1,0:T(8,128)(2,1)} %fusion.12), channel_id=1, source_target_pairs={{0,8},{4,20},{8,0},{12,28},{16,24},{20,4},{24,16},{28,12},{1,9},{5... | collective-permute-start | bytes 3538952 | tf_op jit(solution)/shard_map/ppermute | solution.py:68
  399.4 24.6 %collective-permute-start.37 = (bf16[48,8960]{1,0:T(8,128)(2,1)S(1)}, bf16[48,8960]{1,0:T(8,128)(2,1)}, u32[]{:S(2)}, u32[]{:S(2)}) collective-permute-start(bf16[48,8960]{1,0:T(8,128)(2,1)S(1)} %concatenate.70), channel_id=1, source_target_pairs={{0,16},{4,12},{8,24},{12,4},{16,0},{20,28},{24,8},{28,20},{1,17},{... | collective-permute-start | bytes 2580488 | tf_op jit(solution)/shard_map/ppermute | solution.py:68
  401.0 23.0 %collective-permute-start.39 = (bf16[160,1536]{1,0:T(8,128)(2,1)}, bf16[160,1536]{1,0:T(8,128)(2,1)}, u32[]{:S(2)}, u32[]{:S(2)}) collective-permute-start(bf16[160,1536]{1,0:T(8,128)(2,1)} %get-tuple-element.739), channel_id=1, source_target_pairs={{0,2},{1,3},{2,0},{3,1},{4,6},{5,7},{6,4},{7,5},{8,10},{9,11},{10,... | collective-permute-start | bytes 1474568 | tf_op jit(solution)/shard_map/ppermute | solution.py:68
  424.1 32.6 %collective-permute-start.40 = (bf16[2,2,4,48,2048]{4,3,2,1,0:T(8,128)(2,1)}, bf16[2,2,4,48,2048]{4,3,2,1,0:T(8,128)(2,1)}, u32[]{:S(2)}, u32[]{:S(2)}) collective-permute-start(bf16[2,2,4,48,2048]{4,3,2,1,0:T(8,128)(2,1)} %bitcast.234), channel_id=1, source_target_pairs={{0,4},{4,0},{8,12},{12,8},{16,20},{20,16},{24,28},{28,24},{1,5},{5... | collective-permute-start | bytes 9437192 | tf_op jit(solution)/shard_map/ppermute | solution.py:68
  428.1 28.5 %collective-permute-start.41 = (bf16[4,48,1536]{2,1,0:T(8,128)(2,1)}, bf16[4,48,1536]{2,1,0:T(8,128)(2,1)}, u32[]{:S(2)}, u32[]{:S(2)}) collective-permute-start(bf16[4,48,1536]{2,1,0:T(8,128)(2,1)} %fusion.15), channel_id=1, source_target_pairs={{0,16},{4,12},{8,24},{12,4},{16,0},{20,28},{24,8},{28,20},{1,17},{... | collective-permute-start | bytes 1769480 | tf_op jit(solution)/shard_map/ppermute | solution.py:68
  431.5 25.1 %collective-permute-start.43 = (bf16[160,1536]{1,0:T(8,128)(2,1)}, bf16[160,1536]{1,0:T(8,128)(2,1)}, u32[]{:S(2)}, u32[]{:S(2)}) collective-permute-start(bf16[160,1536]{1,0:T(8,128)(2,1)} %get-tuple-element.761), channel_id=1, source_target_pairs={{0,1},{1,2},{2,3},{3,0},{4,5},{5,6},{6,7},{7,4},{8,9},{9,10},{10,1... | collective-permute-start | bytes 1474568 | tf_op jit(solution)/shard_map/ppermute | solution.py:68
  433.6 38.1 %collective-permute-start.45 = (bf16[2,48,8960]{2,1,0:T(8,128)(2,1)}, bf16[2,48,8960]{2,1,0:T(8,128)(2,1)}, u32[]{:S(2)}, u32[]{:S(2)}) collective-permute-start(bf16[2,48,8960]{2,1,0:T(8,128)(2,1)} %pad_maximum_fusion.5), channel_id=1, source_target_pairs={{0,8},{4,20},{8,0},{12,28},{16,24},{20,4},{24,16},{28,12},{1,9},{5... | collective-permute-start | bytes 5160968 | tf_op jit(solution)/shard_map/ppermute | solution.py:68
  434.6 167.9 %all-gather.7.cloned.1.call-start = ((), (), s32[]{:S(2)}) async-start(), calls=%async_computation.5 | async-start | bytes 7741440 | tf_op jit(solution)/shard_map/all_gather | solution.py:1085
  460.3 34.8 %collective-permute-start.44 = (bf16[2,4,48,2048]{3,2,1,0:T(8,128)(2,1)}, bf16[2,4,48,2048]{3,2,1,0:T(8,128)(2,1)}, u32[]{:S(2)}, u32[]{:S(2)}) collective-permute-start(bf16[2,4,48,2048]{3,2,1,0:T(8,128)(2,1)} %fusion.4), channel_id=1, source_target_pairs={{0,8},{4,20},{8,0},{12,28},{16,24},{20,4},{24,16},{28,12},{1,9},{5... | collective-permute-start | bytes 4718600 | tf_op jit(solution)/shard_map/ppermute | solution.py:68
  498.8 24.6 %collective-permute-start.50 = (bf16[48,8960]{1,0:T(8,128)(2,1)S(1)}, bf16[48,8960]{1,0:T(8,128)(2,1)S(1)}, u32[]{:S(2)}, u32[]{:S(2)}) collective-permute-start(bf16[48,8960]{1,0:T(8,128)(2,1)S(1)} %concatenate.72), channel_id=1, source_target_pairs={{0,16},{4,12},{8,24},{12,4},{16,0},{20,28},{24,8},{28,20},{1,17},{... | collective-permute-start | bytes 2580488 | tf_op jit(solution)/shard_map/ppermute | solution.py:68
  500.3 23.1 %collective-permute-start.49 = (bf16[4,48,2048]{2,1,0:T(8,128)(2,1)S(1)}, bf16[4,48,2048]{2,1,0:T(8,128)(2,1)S(1)}, u32[]{:S(2)}, u32[]{:S(2)}) collective-permute-start(bf16[4,48,2048]{2,1,0:T(8,128)(2,1)S(1)} %fusion.7), channel_id=1, source_target_pairs={{0,16},{4,12},{8,24},{12,4},{16,0},{20,28},{24,8},{28,20},{1,17},{... | collective-permute-start | bytes 2359304 | tf_op jit(solution)/shard_map/ppermute | solution.py:68
  525.8 23.6 %collective-permute-start.57 = (bf16[2,48,8960]{2,1,0:T(8,128)(2,1)S(1)}, bf16[2,48,8960]{2,1,0:T(8,128)(2,1)S(1)}, u32[]{:S(2)}, u32[]{:S(2)}) collective-permute-start(bf16[2,48,8960]{2,1,0:T(8,128)(2,1)S(1)} %pad_maximum_fusion.6), channel_id=1, source_target_pairs={{0,8},{4,20},{8,0},{12,28},{16,24},{20,4},{24,16},{28,12},{1,9},{5... | collective-permute-start | bytes 5160968 | tf_op jit(solution)/shard_map/ppermute | solution.py:68
  (88 other events, 1300.1 us)
Sparse Core Ops, SparseCore 0:
  11.5 99.5 all-gather.8
  113.6 75.0 all-gather.4
  285.1 83.0 reduce-scatter.2
  434.8 74.5 reduce-scatter.4
  551.7 50.8 all-gather.6

commit v11 on v10

--- a/solution.py
+++ b/solution.py
@@ -793,26 +793,24 @@
         return clock.send(shard, rows, [shards - step for step in steps])
 
     rep_index = lax.axis_index("rep")
-    input_matrix = lax.all_gather(
-        weight_piece(input_weight, rep_index), ("shard", "rep"), axis=0, tiled=True
-    )
     shard_vectors = jnp.concatenate([first_gain, second_gain, input_bias])
-    vector_row = jnp.pad(shard_vectors, (0, output_weight.shape[1] - shard_vectors.shape[0]))
-    own_output = jnp.concatenate(
-        [weight_piece(output_weight, rep_place), vector_row[None]], axis=0
-    )
-    output_moving = send_around(own_output)
+    vector_row = jnp.pad(shard_vectors, (0, input_weight.shape[1] - shard_vectors.shape[0]))
+    own_input = jnp.concatenate([weight_piece(input_weight, rep_place), vector_row[None]], axis=0)
+    input_moving = send_around(own_input)
     gate_blocks, up_blocks = clock.run(
         lambda *weights: column_blocks(rep_index, shard.place, *weights),
         gate_weight.reshape(reps, part_rows, hidden_units),
         up_weight.reshape(reps, part_rows, hidden_units),
     )
-    (output_rows,) = clock.wait(output_moving)
-    output_rows = [own_output] + output_rows
-
-    output_spread = spread(jnp.stack([rows[:part_rows] for rows in output_rows])[None])
-    gate_moving = send_blocks(gate_blocks)
-    vector_rows = jnp.stack(in_place_order([rows[part_rows] for rows in output_rows], shard))
+    (output_piece,) = clock(weight_piece(output_weight, rep_index))
+    (input_rows,) = clock.wait(input_moving)
+    input_rows = [own_input] + input_rows
+
+    input_spread = spread(jnp.stack([rows[:part_rows] for rows in input_rows])[None])
+    passed = [[output_cotangent] * 2]
+    passing = clock.pass_on(shard, *passed[-1])
+    output_matrix = lax.all_gather(clock(output_piece)[0], ("shard", "rep"), axis=0, tiled=True)
+    vector_rows = jnp.stack(in_place_order([rows[part_rows] for rows in input_rows], shard))
     own_gain = first_gain.shape[0]
     gain_one = vector_rows[:, :own_gain].reshape(width).astype(f32)
     gain_two = vector_rows[:, own_gain : 2 * own_gain].reshape(width).astype(f32)
@@ -849,20 +847,22 @@
         key_marks,
         row_marks,
     ) = clock(normed_one, cosine_table, sine_table, signed_sine, key_marks, row_marks)
-    output_arrived, gate_rows = clock.wait(output_spread.moving, gate_moving)
-
-    output_spread.along(output_arrived)
+    input_arrived, arrived = clock.wait(input_spread.moving, passing)
+    passed.append(arrived)
+
+    input_spread.along(input_arrived)
+    gate_moving = send_blocks(gate_blocks)
+    input_arrived, gate_rows = clock.wait(input_spread.moving, gate_moving)
+
+    input_spread.over(input_arrived)
     up_moving = send_blocks(up_blocks)
-    output_arrived, up_rows = clock.wait(output_spread.moving, up_moving)
-
+    input_arrived, up_rows = clock.wait(input_spread.moving, up_moving)
+
+    (input_matrix,) = clock.run(place_blocks, z_order, *input_spread.finish(input_arrived))
+    input_matrix = input_matrix.reshape(width, -1)
     gate_up = jnp.stack(
         [row for pair in zip([gate_blocks[0]] + gate_rows, [up_blocks[0]] + up_rows) for row in pair]
     )
-    gate_up = lax.all_gather(clock(gate_up)[0], "rep", axis=0, tiled=True)
-    passed = [[output_cotangent] * 2]
-    passing = clock.pass_on(shard, *passed[-1])
-    output_spread.over(output_arrived)
-    input_matrix, normed_one = clock(input_matrix, normed_one)
     projected = jnp.dot(normed_one, input_matrix, preferred_element_type=f32) + shift_row
     key_part = rotate(
         projected[:, query_width : query_width + pair_width].reshape(own_rows, KVH, HD),
@@ -875,21 +875,18 @@
             axis=1,
         ).astype(bf16)
     )
-    arrived, output_arrived = clock.wait(passing, output_spread.moving)
-    passed.append(arrived)
-
     pair_moving = send_around(own_pairs)
     passing = clock.pass_on(shard, *passed[-1]) if shards > 2 else []
+    gate_up = lax.all_gather(clock(gate_up)[0], "rep", axis=0, tiled=True)
     pair_rows, arrived = clock.wait(pair_moving, passing)
     passed.append(arrived)
     pairs = jnp.concatenate([own_pairs] + pair_rows, axis=0)
 
     passing = clock.pass_on(shard, *passed[-1]) if shards > 3 else []
-    (output_matrix,) = clock.run(place_blocks, z_order, *output_spread.finish(output_arrived))
-    output_matrix = output_matrix.reshape(width, width)
     queries, attention_low = clock.run(
         attention_forward, projected, cosine_table, signed_sine, pairs, row_marks.T, key_marks
     )
+    output_matrix, attention_low = clock(output_matrix, attention_low)
     hidden = wide_tokens + jnp.dot(attention_low, output_matrix, preferred_element_type=f32)
     inverse_two = lax.rsqrt(jnp.mean(hidden * hidden, axis=-1, keepdims=True) + EPSILON)
     unit_two = hidden * inverse_two
@@ -931,13 +928,13 @@
         return [half.reshape((first.size, second.size) + half.shape[1:]) for half in halves]
 
     def side_by_side(rows):
-        return clock(jnp.concatenate(in_place_order(rows, shard), axis=1))[0]
+        return clock(jnp.concatenate(list(rows), axis=1))[0]
 
     def sum_over_rep(blocks):
         return lax.psum_scatter(blocks, "rep", scatter_dimension=0, tiled=True)
 
-    def row_sum(own, arrived):
-        return clock(total_of(own + arrived).astype(bf16))[0]
+    def row_sum(rows):
+        return clock(total_of(list(rows)).astype(bf16))[0]
 
     def send_some(rows, chosen):
         return clock.send(shard, [rows[k] for k in chosen], [shards - 1 - k for k in chosen])
@@ -945,9 +942,9 @@
     edges = sorted({0, shards - 2})
     inside = list(range(1, shards - 2))
 
-    up_halves = split_halves(turned_normed, d_up, shards, True)
-
-    up = Halving(clock, *up_halves, core, first, second)
+    def exchange(blocks):
+        return clock(lax.all_to_all(blocks, "shard", 0, 0, tiled=True))[0]
+
     normed_own, *normed_partial = clock.run(
         lambda *operands: rows_product(operands[:2], operands[2:], True, shards),
         d_gate,
@@ -955,32 +952,28 @@
         gate_matrix,
         up_matrix,
     )
-    (up_arrived,) = clock.wait(up.moving)
-
-    up.along_first(up_arrived)
+    up_halves = split_halves(turned_normed, d_up, shards, True)
+
+    up = Halving(clock, *up_halves, core, first, second)
     normed_moving = send_some(normed_partial, edges)
     (gate_blocks,) = clock.run(
         lambda left, right: ordered_gradient(left, right, shards, rep_places(reps)),
         turned_normed,
         d_gate,
     )
-    gate_piece = sum_over_rep(gate_blocks.reshape(width, block_units))
+    up_arrived, normed_arrived = clock.wait(up.moving, normed_moving)
+    gate_piece = sum_over_rep(clock(gate_blocks)[0].reshape(width, block_units))
+
+    up.along_first(up_arrived)
+    normed_moving = send_some(normed_partial, inside)
     (down_blocks,) = clock.run(
         lambda left, right: ordered_gradient(left, right, 1, list(range(reps))),
         turned_inner,
         cotangents,
     )
-    up_arrived, normed_arrived = clock.wait(up.moving, normed_moving)
+    up_arrived, more_arrived = clock.wait(up.moving, normed_moving)
 
     up.along_second(up_arrived)
-    normed_moving = send_some(normed_partial, inside)
-    block_own, *block_partial = clock.run(
-        lambda left, right: rows_product((left,), (right,), False, shards), inner_act, down_weight
-    )
-    up_arrived, more_arrived = clock.wait(up.moving, normed_moving)
-
-    up_blocks = clock(*blocks_of(up.finish(up_arrived)))
-    up_moving = send_blocks(up_blocks)
     normed_two_gradient = total_of([normed_own] + normed_arrived + more_arrived)
     gain_two_gradient = jnp.sum(normed_two_gradient * unit_two, axis=0)
     hidden_gradient = output_cotangent.astype(f32) + norm_back(
@@ -999,16 +992,15 @@
         key_marks.T,
     )
     output_halves = split_halves(attention_low, branch_gradient, shards, False)
-    (up_rows,) = clock.wait(up_moving)
+    (up_arrived,) = clock.wait(up.moving)
 
     pair_moving = send_back(pair_partial)
     output = Halving(clock, *output_halves, core, first, second)
-    up_piece = side_by_side(up_blocks[:1] + up_rows)
+    up_blocks = clock(*blocks_of(up.finish(up_arrived)))
     pair_arrived, output_arrived = clock.wait(pair_moving, output.moving)
 
-    up_spread = spread(up_piece)
     output.along_first(output_arrived)
-    block_moving = send_some(block_partial, inside)
+    up_moving = send_blocks(up_blocks)
     projected_gradient, bias_sum = clock.run(
         lambda *operands: join_projected(operands[0], operands[3:], *operands[1:3]),
         d_queries,
@@ -1018,16 +1010,16 @@
         *pair_arrived,
     )
     projected_halves = split_halves(normed_one, projected_gradient, shards, False)
-    up_arrived, output_arrived, block_arrived = clock.wait(
-        up_spread.moving, output.moving, block_moving
-    )
+    output_arrived, up_rows = clock.wait(output.moving, up_moving)
 
     projected = Halving(clock, *projected_halves, core, first, second)
     output.along_second(output_arrived)
-    up_spread.along(up_arrived)
-    block_moving = send_some(block_partial, edges)
+    up_spread = spread(side_by_side(in_place_order(up_blocks[:1] + up_rows, shard)))
     (gate_piece,) = clock(gate_piece)
     down_piece = sum_over_rep(clock(down_blocks)[0].reshape(block_units, width))
+    block_own, *block_partial = clock.run(
+        lambda left, right: rows_product((left,), (right,), False, shards), inner_act, down_weight
+    )
     projected_gradient, hidden_gradient = clock(projected_gradient, hidden_gradient)
     normed_one_gradient = times_transposed(projected_gradient, input_matrix)
     gain_one_gradient = jnp.sum(normed_one_gradient * unit_one, axis=0)
@@ -1036,16 +1028,15 @@
             hidden_gradient + norm_back(normed_one_gradient, unit_one, inverse_one, gain_one)
         ).astype(bf16)
     )
-    projected_arrived, output_arrived, more_arrived = clock.wait(
-        projected.moving, output.moving, block_moving
-    )
-    block_arrived = block_arrived + more_arrived
+    projected_arrived, output_arrived, up_arrived = clock.wait(
+        projected.moving, output.moving, up_spread.moving
+    )
 
     projected.along_first(projected_arrived)
-    gate_blocks = clock(*blocks_of(gate_piece.reshape(shards, part_rows, block_units)))
-    gate_moving = send_blocks(gate_blocks)
-    output_blocks = clock(*blocks_of(output.finish(output_arrived)))
-    (block_out,) = clock(total_of([hidden, block_own] + block_arrived).astype(bf16))
+    up_spread.along(up_arrived)
+    block_moving = send_some(block_partial, edges[:1])
+    output_sum = output.finish(output_arrived)
+    gate_sum = exchange(gate_piece.reshape(shards, part_rows, block_units))
     bias_gradient = bias_sum[0]
     bias_split = query_width + pair_width
     small_parts = (
@@ -1057,59 +1048,63 @@
     (small,) = clock(
         jnp.concatenate([part.reshape(shards, -1) for part in small_parts], axis=1)
     )
-    projected_arrived, up_arrived, gate_rows = clock.wait(
-        projected.moving, up_spread.moving, gate_moving
+    projected_arrived, up_arrived, block_arrived = clock.wait(
+        projected.moving, up_spread.moving, block_moving
     )
 
     projected.along_second(projected_arrived)
-    gate_spread = spread(side_by_side(gate_blocks[:1] + gate_rows))
-    output_moving = send_blocks(output_blocks)
-    projected_arrived, gate_arrived, output_rows = clock.wait(
-        projected.moving, gate_spread.moving, output_moving
-    )
-
-    input_blocks = clock(*blocks_of(projected.finish(projected_arrived)))
-    input_moving = send_blocks(input_blocks)
+    gate_spread = spread(side_by_side(gate_sum))
+    up_spread.over(up_arrived)
+    block_moving = send_some(block_partial, edges[1:])
+    output_sum = row_sum(exchange(output_sum))
+    projected_arrived, gate_arrived, up_arrived, more_arrived = clock.wait(
+        projected.moving, gate_spread.moving, up_spread.moving, block_moving
+    )
+    block_arrived = block_arrived + more_arrived
+
+    input_sum = projected.finish(projected_arrived)
     gate_spread.along(gate_arrived)
-    output_spread = spread(row_sum(output_blocks[:1], output_rows))
-    input_rows, gate_arrived, output_arrived = clock.wait(
-        input_moving, gate_spread.moving, output_spread.moving
-    )
-
-    input_spread = spread(row_sum(input_blocks[:1], input_rows))
+    output_spread = spread(output_sum)
+    small_moving = clock.send(core, [small], [1])
+    input_sum = row_sum(exchange(input_sum))
+    gate_arrived, output_arrived, small_arrived = clock.wait(
+        gate_spread.moving, output_spread.moving, small_moving
+    )
+    small = total_of([small] + small_arrived)
+
+    input_spread = spread(input_sum)
     output_spread.along(output_arrived)
-    up_spread.over(up_arrived)
     gate_spread.over(gate_arrived)
-    small_moving = clock.send(core, [small], [1])
+    small_moving = clock.send(first, [small] * (first.size - 1), range(1, first.size))
     (down_piece,) = clock(down_piece)
     down_gathered = lax.all_gather(down_piece, "rep", axis=0, tiled=True)
-    input_arrived, output_arrived, up_arrived, gate_arrived, small_arrived = clock.wait(
-        input_spread.moving, output_spread.moving, up_spread.moving, gate_spread.moving, small_moving
+    (up_total,) = clock.run(widen_pieces, *up_spread.finish(up_arrived))
+    input_arrived, output_arrived, gate_arrived, small_arrived = clock.wait(
+        input_spread.moving, output_spread.moving, gate_spread.moving, small_moving
     )
     small = total_of([small] + small_arrived)
 
     input_spread.along(input_arrived)
     output_spread.over(output_arrived)
-    small_moving = clock.send(first, [small] * (first.size - 1), range(1, first.size))
-    (up_total,) = clock.run(widen_pieces, *up_spread.finish(up_arrived))
-    input_arrived, output_arrived, small_arrived = clock.wait(
-        input_spread.moving, output_spread.moving, small_moving
+    small_moving = clock.send(second, [small] * (second.size - 1), range(1, second.size))
+    block_moving = send_some(block_partial, inside)
+    (gate_total,) = clock.run(widen_pieces, *gate_spread.finish(gate_arrived))
+    input_arrived, output_arrived, small_arrived, more_arrived = clock.wait(
+        input_spread.moving, output_spread.moving, small_moving, block_moving
     )
     small = total_of([small] + small_arrived)
+    block_arrived = block_arrived + more_arrived
 
     input_spread.over(input_arrived)
-    small_moving = clock.send(second, [small] * (second.size - 1), range(1, second.size))
-    (gate_total,) = clock.run(widen_pieces, *gate_spread.finish(gate_arrived))
-    input_arrived, small_arrived = clock.wait(input_spread.moving, small_moving)
-    small_blocks = clock(*blocks_of(total_of([small] + small_arrived)))
-
+    small_blocks = clock(*blocks_of(small))
     small_moving = send_blocks(small_blocks)
     (output_total,) = clock.run(widen_pieces, *output_spread.finish(output_arrived))
-    (input_total,) = clock.run(widen_pieces, *input_spread.finish(input_arrived))
-    (small_arrived,) = clock.wait(small_moving)
+    input_arrived, small_arrived = clock.wait(input_spread.moving, small_moving)
     small = total_of(small_blocks[:1] + small_arrived)
+    (block_out,) = clock(total_of([hidden, block_own] + block_arrived).astype(bf16))
     (down_gathered,) = clock(down_gathered)
     (down_total,) = clock(down_gathered.astype(f32))
+    (input_total,) = clock.run(widen_pieces, *input_spread.finish(input_arrived))
 
     small = small + clock.token[0, 0]
     small_totals, at = [], 0

time: 632 us -> 654 us (1.035)
  waiting for transfers between devices: 225 us -> 251 us
  starting transfers between devices: 129 us -> 114 us
  other arithmetic: 67.6 us -> 76.2 us
    ppermute x66 -> x57, waiting for transfers between devices: 210 us -> 164 us  [shift(): return lax.ppermute(value, self.name, self.pairs(step % self.size))]
    all_to_all x0 -> x3, waiting for transfers between devices: none -> 41 us  [exchange(): return clock(lax.all_to_all(blocks, 'shard', 0, 0, tiled=True))[0]]
    ppermute x66 -> x57, starting transfers between devices: 103 us -> 71.8 us  [shift(): return lax.ppermute(value, self.name, self.pairs(step % self.size))]
    all_gather x1, waiting for transfers between devices: 0.01 us -> 26.2 us  [on_device(): gate_up = lax.all_gather(clock(gate_up)[0], 'rep', axis=0, tiled=True)]
    all_to_all x0 -> x3, starting transfers between devices: none -> 16.2 us  [exchange(): return clock(lax.all_to_all(blocks, 'shard', 0, 0, tiled=True))[0]]
  transfers between devices with their start and end apart: 77 -> 71, of which waited for: 35 -> 26; matrix products, arithmetic and copies ran while one was open for 14% -> 15% of each run, Pallas kernels for 18% -> 15%
where the time goes in v11:
time: 654 us; the launch traced here: 643 us
  waiting for transfers between devices  251 us (38%)
  Pallas kernels  145 us (22%)
  starting transfers between devices  114 us (17%)
  other arithmetic  76.2 us (12%)
  local copies, waits for them, and re-layouts  27.6 us (4%)
  matrix products  15.2 us (2%)
  between operations  15.2 us (2%)
    ppermute x57, waiting for transfers between devices, shift(): return lax.ppermute(value, self.name, self.pairs(step % self.size))  164 us
    ppermute x57, starting transfers between devices, shift(): return lax.ppermute(value, self.name, self.pairs(step % self.size))  71.8 us
    all_to_all x3, waiting for transfers between devices, exchange(): return clock(lax.all_to_all(blocks, 'shard', 0, 0, tiled=True))[0]  41 us
    all_gather x1, waiting for transfers between devices, on_device(): gate_up = lax.all_gather(clock(gate_up)[0], 'rep', axis=0, tiled=True)  26.2 us
    ppermute x6, starting transfers between devices, pass_on(): return lax.ppermute(value, self.name, pairs)  25.2 us
    pallas_call x1, Pallas kernels, feed_forward(): pl.pallas_call(body, grid=(steps,), out_shape=[jax.ShapeDtypeStruct((coun...  23.6 us
    pallas_call x2, Pallas kernels, rows_product(): pl.pallas_call(body, grid=(pl.cdiv(columns, TILE),), out_shape=[jax.Shape...  23.1 us
    pallas_call x4, Pallas kernels, widen_pieces(): pl.pallas_call(body, out_shape=jax.ShapeDtypeStruct((reps, rows, columns)...  21.8 us
  transfers between devices with their start and end apart: 71, of which 26 were waited for; matrix products, arithmetic and copies ran while one was open for 15% of the time, Pallas kernels for 15%

profile of v11, /device:TPU:0, one launch (start us, length us, event | category | flops | bytes accessed | tf_op | source)
XLA Modules:
  0.0 643.5 jit_solution(15647710408762132205)
XLA Ops:
  32.2 8.1 %collective-permute-start.4 = (bf16[160,1536]{1,0:T(8,128)(2,1)S(1)}, bf16[160,1536]{1,0:T(8,128)(2,1)}, u32[]{:S(2)}, u32[]{:S(2)}) collective-permute-start(bf16[160,1536]{1,0:T(8,128)(2,1)S(1)} %copy-done.16), channel_id=1, source_target_pairs={{0,1},{1,2},{2,3},{4,5},{5,6},{6,7},{8,9},{9,10},{10,11},{12,13},{... | collective-permute-start | bytes 1474568 | tf_op jit(solution)/shard_map/ppermute | solution.py:73
  41.8 8.0 %collective-permute-done.4 = bf16[160,1536]{1,0:T(8,128)(2,1)} collective-permute-done((bf16[160,1536]{1,0:T(8,128)(2,1)S(1)}, bf16[160,1536]{1,0:T(8,128)(2,1)}, u32[]{:S(2)}, u32[]{:S(2)}) %collective-permute-start.4) | collective-permute-done | bytes 491552 | tf_op jit(solution)/shard_map/ppermute | solution.py:73
  62.5 6.8 %collective-permute-done.7 = bf16[48,2240]{1,0:T(8,128)(2,1)S(1)} collective-permute-done((bf16[48,2240]{1,0:T(8,128)(2,1)S(1)}, bf16[48,2240]{1,0:T(8,128)(2,1)S(1)}, u32[]{:S(2)}, u32[]{:S(2)}) %collective-permute-start.7) | collective-permute-done | bytes 215072 | tf_op jit(solution)/shard_map/ppermute | solution.py:68
  69.4 10.2 %collective-permute-done.8 = bf16[48,2240]{1,0:T(8,128)(2,1)S(1)} collective-permute-done((bf16[48,2240]{1,0:T(8,128)(2,1)S(1)}, bf16[48,2240]{1,0:T(8,128)(2,1)S(1)}, u32[]{:S(2)}, u32[]{:S(2)}) %collective-permute-start.8) | collective-permute-done | bytes 215072 | tf_op jit(solution)/shard_map/ppermute | solution.py:68
  86.3 5.8 collective-permute-start.11
  95.2 6.6 %collective-permute-done.11 = bf16[48,2240]{1,0:T(8,128)(2,1)} collective-permute-done((bf16[48,2240]{1,0:T(8,128)(2,1)S(1)}, bf16[48,2240]{1,0:T(8,128)(2,1)}, u32[]{:S(2)}, u32[]{:S(2)}) %collective-permute-start.11) | collective-permute-done | bytes 215072 | tf_op jit(solution)/shard_map/ppermute | solution.py:68
  101.8 10.6 %collective-permute-done.12 = bf16[48,2240]{1,0:T(8,128)(2,1)} collective-permute-done((bf16[48,2240]{1,0:T(8,128)(2,1)S(1)}, bf16[48,2240]{1,0:T(8,128)(2,1)}, u32[]{:S(2)}, u32[]{:S(2)}) %collective-permute-start.12) | collective-permute-done | bytes 215072 | tf_op jit(solution)/shard_map/ppermute | solution.py:68
  112.4 6.3 place_blocks.2
  129.8 7.7 %collective-permute-start.17 = (bf16[160,1536]{1,0:T(8,128)(2,1)}, bf16[160,1536]{1,0:T(8,128)(2,1)S(1)}, u32[]{:S(2)}, u32[]{:S(2)}) collective-permute-start(bf16[160,1536]{1,0:T(8,128)(2,1)} %collective-permute-done.4), channel_id=1, source_target_pairs={{0,1},{1,2},{2,3},{4,5},{5,6},{6,7},{8,9},{9,10},{10,11},{12,13},{... | collective-permute-start | bytes 1474568 | tf_op jit(solution)/shard_map/ppermute | solution.py:73
  145.2 13.4 %collective-permute-done.14 = bf16[160,512]{1,0:T(8,128)(2,1)S(1)} collective-permute-done((bf16[160,512]{1,0:T(8,128)(2,1)S(1)}, bf16[160,512]{1,0:T(8,128)(2,1)S(1)}, u32[]{:S(2)}, u32[]{:S(2)}) %collective-permute-start.14) | collective-permute-done | bytes 163872 | tf_op jit(solution)/shard_map/ppermute | solution.py:68
  171.9 5.7 attention_forward.1
  191.3 26.2 %all-gather.6.cloned.1.call-done.source = bf16[64,48,2240]{2,1,0:T(8,128)(2,1)} async-done(((bf16[8,48,2240]{2,1,0:T(8,128)(2,1)}), bf16[64,48,2240]{2,1,0:T(8,128)(2,1)}) %all-gather.6.cloned.1.call-update) | async-done | bytes 13762576 | tf_op jit(solution)/shard_map/all_gather | solution.py:880
  217.5 11.7 %place_blocks.3 = (bf16[4,8,48,2240]{3,2,1,0:T(8,128)(2,1)}, bf16[4,8,48,2240]{3,2,1,0:T(8,128)(2,1)}) custom-call(s32[4]{0:T(128)} %pad_add_fusion.5.order_ref, bf16[64,48,2240]{2,1,0:T(8,128)(2,1)} %all-gather.6.cloned.1.call-done.source), custom_call_target="tpu_custom_call" | custom-call | flops 1 | bytes 1 | tf_op jit(solution)/shard_map/place_blocks/pallas_call | solution.py:339
  231.6 23.6 %feed_forward.1 = (bf16[640,2240]{1,0:T(8,128)(2,1)}, bf16[640,2240]{1,0:T(8,128)(2,1)}, bf16[640,2240]{1,0:T(8,128)(2,1)}, bf16[1536,640]{1,0:T(8,128)(2,1)}, bf16[2240,640]{1,0:T(8,128)(2,1)}) custom-call(bf16[640,1536]{1,0:T(8,128)(2,1)} %pad_maximum_fusion.3.rows_ref, bf16[640,1536]{1,0:T(8,128)(2,1)} %pad_maximum_fusion.4.cotangents_ref.right_ref, ...), custom_call_target="tpu_custom_call" | custom-call | flops 1 | bytes 1 | tf_op jit(solution)/shard_map/feed_forward/pallas_call | solution.py:477
  255.2 14.6 %rows_product.2 = (bf16[160,1536]{1,0:T(8,128)(2,1)}, bf16[160,1536]{1,0:T(8,128)(2,1)}, bf16[160,1536]{1,0:T(8,128)(2,1)}, bf16[160,1536]{1,0:T(8,128)(2,1)}) custom-call(bf16[640,2240]{1,0:T(8,128)(2,1)} %get-tuple-element.598.refs_0_.right_ref, bf16[640,2240]{1,0:T(8,128)(2,1)} %get-tuple-element.587.refs_1_.right_ref, bf16[1536,2240]{1,0:T(8,128)(2,1)} %bitcast.171, ...), custom_call_target="tpu_custom_call" | custom-call | flops 1 | bytes 1 | tf_op jit(solution)/shard_map/rows_product/pallas_call | solution.py:603
  269.8 10.0 %split_gradient.3 = (bf16[4,4,48,2240]{3,2,1,0:T(8,128)(2,1)}, bf16[4,4,48,2240]{3,2,1,0:T(8,128)(2,1)}) custom-call(s32[1]{0:T(128)} %bitcast.46.core_ref, bf16[1536,640]{1,0:T(8,128)(2,1)} %get-tuple-element.597.left_ref, bf16[640,2240]{1,0:T(8,128)(2,1)} %get-tuple-element.587.refs_1_.right_ref), custom_call_target="tpu_custom_call" | custom-call | flops 1 | bytes 1 | tf_op jit(solution)/shard_map/split_gradient/pallas_call | solution.py:533
  283.5 9.9 %ordered_gradient.2 = bf16[8,4,48,2240]{3,2,1,0:T(8,128)(2,1)} custom-call(bf16[1536,640]{1,0:T(8,128)(2,1)} %get-tuple-element.597.left_ref, bf16[640,2240]{1,0:T(8,128)(2,1)} %get-tuple-element.598.refs_0_.right_ref), custom_call_target="tpu_custom_call" | custom-call | flops 1 | bytes 1 | tf_op jit(solution)/shard_map/ordered_gradient/pallas_call | solution.py:563
  295.1 10.8 %collective-permute-done.26 = bf16[160,1536]{1,0:T(8,128)(2,1)S(1)} collective-permute-done((bf16[160,1536]{1,0:T(8,128)(2,1)S(1)}, bf16[160,1536]{1,0:T(8,128)(2,1)S(1)}, u32[]{:S(2)}, u32[]{:S(2)}) %collective-permute-start.26) | collective-permute-done | bytes 491552 | tf_op jit(solution)/shard_map/ppermute | solution.py:68
  313.0 9.9 %ordered_gradient.3 = bf16[8,1,280,1536]{3,2,1,0:T(8,128)(2,1)} custom-call(bf16[2240,640]{1,0:T(8,128)(2,1)} %get-tuple-element.613.left_ref, bf16[640,1536]{1,0:T(8,128)(2,1)} %pad_maximum_fusion.4.cotangents_ref.right_ref), custom_call_target="tpu_custom_call" | custom-call | flops 1 | bytes 1 | tf_op jit(solution)/shard_map/ordered_gradient/pallas_call | solution.py:563
  322.8 11.5 %collective-permute-done.28 = bf16[160,1536]{1,0:T(8,128)(2,1)S(1)} collective-permute-done((bf16[160,1536]{1,0:T(8,128)(2,1)S(1)}, bf16[160,1536]{1,0:T(8,128)(2,1)S(1)}, u32[]{:S(2)}, u32[]{:S(2)}) %collective-permute-start.28) | collective-permute-done | bytes 491552 | tf_op jit(solution)/shard_map/ppermute | solution.py:68
  344.6 7.6 %attention_backward.1 = (bf16[160,1536]{1,0:T(8,128)(2,1)}, bf16[160,512]{1,0:T(8,128)(2,1)}, bf16[160,512]{1,0:T(8,128)(2,1)}, bf16[160,512]{1,0:T(8,128)(2,1)}, bf16[160,512]{1,0:T(8,128)(2,1)}) custom-call(bf16[2,960,128]{2,1,0:T(8,128)(2,1)} %get-tuple-element.631.queries_ref, bf16[160,1536]{1,0:T(8,128)(2,1)} %convolution_convert_fusion.gradient_ref, ...), custom_call_target="tpu_custom_call" | custom-call | flops 1 | bytes 1 | tf_op jit(solution)/shard_map/attention_backward/pallas_call | solution.py:705
  370.2 11.0 %collective-permute-done.31.refs_2_ = bf16[160,512]{1,0:T(8,128)(2,1)S(1)} collective-permute-done((bf16[160,512]{1,0:T(8,128)(2,1)S(1)}, bf16[160,512]{1,0:T(8,128)(2,1)S(1)}, u32[]{:S(2)}, u32[]{:S(2)}) %collective-permute-start.31) | collective-permute-done | bytes 163872 | tf_op jit(solution)/shard_map/ppermute | solution.py:68
  410.8 6.6 %all-to-all-start = ((bf16[4,48,2240]{2,1,0:T(8,128)(2,1)}), bf16[4,48,2240]{2,1,0:T(8,128)(2,1)}, u32[]{:S(2)}, u32[]{:S(2)}) async-start(bf16[4,48,2240]{2,1,0:T(8,128)(2,1)} %bitcast.207), calls=%async_computation.1 | async-start | bytes 1769472 | tf_op jit(solution)/shard_map/all_to_all | solution.py:946
  417.4 8.5 %rows_product.3 = (bf16[160,1536]{1,0:T(8,128)(2,1)}, bf16[160,1536]{1,0:T(8,128)(2,1)}, bf16[160,1536]{1,0:T(8,128)(2,1)}, bf16[160,1536]{1,0:T(8,128)(2,1)}) custom-call(bf16[640,2240]{1,0:T(8,128)(2,1)} %get-tuple-element.717.refs_0_, bf16[2240,1536]{1,0:T(8,128)(2,1)} %refs_1_), custom_call_target="tpu_custom_call" | custom-call | flops 1 | bytes 1 | tf_op jit(solution)/shard_map/rows_product/pallas_call | solution.py:603
  450.4 6.3 collective-permute-done.43
  456.7 38.9 %collective-permute-done.41 = bf16[2,4,48,2048]{3,2,1,0:T(8,128)(2,1)} collective-permute-done((bf16[2,4,48,2048]{3,2,1,0:T(8,128)(2,1)}, bf16[2,4,48,2048]{3,2,1,0:T(8,128)(2,1)}, u32[]{:S(2)}, u32[]{:S(2)}) %collective-permute-start.41) | collective-permute-done | bytes 1572896 | tf_op jit(solution)/shard_map/ppermute | solution.py:68
  511.1 23.2 %all-to-all-done.1 = bf16[4,48,1536]{2,1,0:T(8,128)(2,1)} async-done(((bf16[4,48,1536]{2,1,0:T(8,128)(2,1)}), bf16[4,48,1536]{2,1,0:T(8,128)(2,1)}, u32[]{:S(2)}, u32[]{:S(2)}) %all-to-all-start.1) | async-done | bytes 589856 | tf_op jit(solution)/shard_map/all_to_all | solution.py:946
  547.4 17.9 %all-to-all-done.2 = bf16[4,48,2048]{2,1,0:T(8,128)(2,1)} async-done(((bf16[4,48,2048]{2,1,0:T(8,128)(2,1)}), bf16[4,48,2048]{2,1,0:T(8,128)(2,1)}, u32[]{:S(2)}, u32[]{:S(2)}) %all-to-all-start.2) | async-done | bytes 786464 | tf_op jit(solution)/shard_map/all_to_all | solution.py:946
  573.5 8.0 %widen_pieces.4 = f32[8,48,8960]{2,1,0:T(8,128)} custom-call(s32[8]{0:T(128)} %stack.232.places_ref, bf16[4,48,8960]{2,1,0:T(8,128)(2,1)} %pad_maximum_fusion.pieces_ref, bf16[4,48,8960]{2,1,0:T(8,128)(2,1)} %collective-permute-done.46.others_ref), custom_call_target="tpu_custom_call" | custom-call | flops 1 | bytes 1 | tf_op jit(solution)/shard_map/widen_pieces/pallas_call | solution.py:415
  585.1 7.3 %widen_pieces.5 = f32[8,48,8960]{2,1,0:T(8,128)} custom-call(s32[8]{0:T(128)} %stack.232.places_ref, bf16[4,48,8960]{2,1,0:T(8,128)(2,1)} %pad_maximum_fusion.1.pieces_ref, bf16[4,48,8960]{2,1,0:T(8,128)(2,1)} %copy-done.6), custom_call_target="tpu_custom_call" | custom-call | flops 1 | bytes 1 | tf_op jit(solution)/shard_map/widen_pieces/pallas_call | solution.py:415
  593.3 12.8 %collective-permute-done.58 = bf16[160,1536]{1,0:T(8,128)(2,1)S(1)} collective-permute-done((bf16[160,1536]{1,0:T(8,128)(2,1)S(1)}, bf16[160,1536]{1,0:T(8,128)(2,1)S(1)}, u32[]{:S(2)}, u32[]{:S(2)}) %collective-permute-start.58) | collective-permute-done | bytes 491552 | tf_op jit(solution)/shard_map/ppermute | solution.py:68
  620.2 10.2 %convert_element_type.354 = f32[2240,1536]{1,0:T(8,128)} convert(bf16[2240,1536]{1,0:T(8,128)(2,1)} %all-gather.8.cloned.1.call-done) | non-fusion elementwise | flops 3440640 | bytes 20643840 | tf_op jit(solution)/shard_map/convert_element_type | solution.py:1106
  (354 shorter events, 252.8 us)
Async XLA Ops:
  7.2 170.5 %all-gather.4.cloned.1.call-start = ((), (), s32[]{:S(2)}) async-start(), calls=%async_computation.5 | async-start | bytes 4866048 | tf_op jit(solution)/shard_map/all_gather | solution.py:812
  30.6 24.2 %collective-permute-start.3 = (bf16[1,4,48,2048]{3,2,1,0:T(8,128)(2,1)}, bf16[1,4,48,2048]{3,2,1,0:T(8,128)(2,1)S(1)}, u32[]{:S(2)}, u32[]{:S(2)}) collective-permute-start(bf16[1,4,48,2048]{3,2,1,0:T(8,128)(2,1)} %get-tuple-element.460), channel_id=1, source_target_pairs={{0,16},{4,12},{8,24},{12,4},{16,0},{20,28},{24,8},{28,20},{1,17},{... | collective-permute-start | bytes 2359304 | tf_op jit(solution)/shard_map/ppermute | solution.py:68
  56.1 23.5 %collective-permute-start.6 = (bf16[2,1,4,48,2048]{4,3,2,1,0:T(8,128)(2,1)}, bf16[2,1,4,48,2048]{4,3,2,1,0:T(8,128)(2,1)}, u32[]{:S(2)}, u32[]{:S(2)}) collective-permute-start(bf16[2,1,4,48,2048]{4,3,2,1,0:T(8,128)(2,1)} %pad_maximum_fusion.7), channel_id=1, source_target_pairs={{0,8},{4,20},{8,0},{12,28},{16,24},{20,4},{24,16},{28,12},{1,9},{5... | collective-permute-start | bytes 4718600 | tf_op jit(solution)/shard_map/ppermute | solution.py:68
  56.6 160.9 %all-gather.6.cloned.1.call-start = ((), (), s32[]{:S(2)}) async-start(), calls=%async_computation.6 | async-start | bytes 15925248 | tf_op jit(solution)/shard_map/all_gather | solution.py:880
  83.0 29.4 %collective-permute-start.10 = (bf16[4,1,4,48,2048]{4,3,2,1,0:T(8,128)(2,1)}, bf16[4,1,4,48,2048]{4,3,2,1,0:T(8,128)(2,1)}, u32[]{:S(2)}, u32[]{:S(2)}) collective-permute-start(bf16[4,1,4,48,2048]{4,3,2,1,0:T(8,128)(2,1)} %pad_maximum_fusion.2.pieces_ref), channel_id=1, source_target_pairs={{0,4},{4,0},{8,12},{12,8},{16,20},{20,16},{24,28},{28,24},{1,5},{5... | collective-permute-start | bytes 9437192 | tf_op jit(solution)/shard_map/ppermute | solution.py:68
  129.8 281.0 %reduce-scatter.3.cloned.1.call-start = ((), (), s32[]{:S(2)}) async-start(), calls=%async_computation.7 | async-start | bytes 7962624 | tf_op jit(solution)/shard_map/reduce_scatter | solution.py:934
  129.8 34.2 %collective-permute-start.17 = (bf16[160,1536]{1,0:T(8,128)(2,1)}, bf16[160,1536]{1,0:T(8,128)(2,1)S(1)}, u32[]{:S(2)}, u32[]{:S(2)}) collective-permute-start(bf16[160,1536]{1,0:T(8,128)(2,1)} %collective-permute-done.4), channel_id=1, source_target_pairs={{0,1},{1,2},{2,3},{4,5},{5,6},{6,7},{8,9},{9,10},{10,11},{12,13},{... | collective-permute-start | bytes 1474568 | tf_op jit(solution)/shard_map/ppermute | solution.py:73
  137.5 26.5 %collective-permute-start.18 = (bf16[160,1536]{1,0:T(8,128)(2,1)}, bf16[160,1536]{1,0:T(8,128)(2,1)S(1)}, u32[]{:S(2)}, u32[]{:S(2)}) collective-permute-start(bf16[160,1536]{1,0:T(8,128)(2,1)} %collective-permute-done.5), channel_id=1, source_target_pairs={{1,0},{2,1},{3,2},{5,4},{6,5},{7,6},{9,8},{10,9},{11,10},{13,12},{... | collective-permute-start | bytes 1474568 | tf_op jit(solution)/shard_map/ppermute | solution.py:73
  141.5 22.5 %collective-permute-start.15 = (bf16[160,512]{1,0:T(8,128)(2,1)S(1)}, bf16[160,512]{1,0:T(8,128)(2,1)S(1)}, u32[]{:S(2)}, u32[]{:S(2)}) collective-permute-start(bf16[160,512]{1,0:T(8,128)(2,1)S(1)} %pad_maximum_fusion.14), channel_id=1, source_target_pairs={{0,2},{1,3},{2,0},{3,1},{4,6},{5,7},{6,4},{7,5},{8,10},{9,11},{10,... | collective-permute-start | bytes 491528 | tf_op jit(solution)/shard_map/ppermute | solution.py:68
  183.5 45.6 %collective-permute-start.21 = (bf16[160,1536]{1,0:T(8,128)(2,1)S(1)}, bf16[160,1536]{1,0:T(8,128)(2,1)S(1)}, u32[]{:S(2)}, u32[]{:S(2)}) collective-permute-start(bf16[160,1536]{1,0:T(8,128)(2,1)S(1)} %multiply_convert_fusion), channel_id=1, source_target_pairs={{0,1},{1,2},{2,3},{3,0},{4,5},{5,6},{6,7},{7,4},{8,9},{9,10},{10,1... | collective-permute-start | bytes 1474568 | tf_op jit(solution)/shard_map/ppermute | solution.py:68
  184.1 45.1 %collective-permute-start.22 = (bf16[160,1536]{1,0:T(8,128)(2,1)S(1)}, bf16[160,1536]{1,0:T(8,128)(2,1)S(1)}, u32[]{:S(2)}, u32[]{:S(2)}) collective-permute-start(bf16[160,1536]{1,0:T(8,128)(2,1)S(1)} %multiply_convert_fusion), channel_id=1, source_target_pairs={{0,2},{1,3},{2,0},{3,1},{4,6},{5,7},{6,4},{7,5},{8,10},{9,11},{10,... | collective-permute-start | bytes 1474568 | tf_op jit(solution)/shard_map/ppermute | solution.py:68
  184.8 44.4 %collective-permute-start.23 = (bf16[160,1536]{1,0:T(8,128)(2,1)S(1)}, bf16[160,1536]{1,0:T(8,128)(2,1)}, u32[]{:S(2)}, u32[]{:S(2)}) collective-permute-start(bf16[160,1536]{1,0:T(8,128)(2,1)S(1)} %multiply_convert_fusion), channel_id=1, source_target_pairs={{0,3},{1,0},{2,1},{3,2},{4,7},{5,4},{6,5},{7,6},{8,11},{9,8},{10,9... | collective-permute-start | bytes 1474568 | tf_op jit(solution)/shard_map/ppermute | solution.py:68
  279.9 26.0 %collective-permute-start.24 = (bf16[2,2,4,48,2240]{4,3,2,1,0:T(8,128)(2,1)}, bf16[2,2,4,48,2240]{4,3,2,1,0:T(8,128)(2,1)}, u32[]{:S(2)}, u32[]{:S(2)}) collective-permute-start(bf16[2,2,4,48,2240]{4,3,2,1,0:T(8,128)(2,1)} %bitcast.220), channel_id=1, source_target_pairs={{0,4},{4,0},{8,12},{12,8},{16,20},{20,16},{24,28},{28,24},{1,5},{5... | collective-permute-start | bytes 10321928 | tf_op jit(solution)/shard_map/ppermute | solution.py:68
  283.5 22.4 %collective-permute-start.26 = (bf16[160,1536]{1,0:T(8,128)(2,1)S(1)}, bf16[160,1536]{1,0:T(8,128)(2,1)S(1)}, u32[]{:S(2)}, u32[]{:S(2)}) collective-permute-start(bf16[160,1536]{1,0:T(8,128)(2,1)S(1)} %copy-done.36), channel_id=1, source_target_pairs={{0,1},{1,2},{2,3},{3,0},{4,5},{5,6},{6,7},{7,4},{8,9},{9,10},{10,1... | collective-permute-start | bytes 1474568 | tf_op jit(solution)/shard_map/ppermute | solution.py:68
  309.7 27.4 %collective-permute-start.27 = (bf16[2,4,48,2240]{3,2,1,0:T(8,128)(2,1)}, bf16[2,4,48,2240]{3,2,1,0:T(8,128)(2,1)}, u32[]{:S(2)}, u32[]{:S(2)}) collective-permute-start(bf16[2,4,48,2240]{3,2,1,0:T(8,128)(2,1)} %fusion), channel_id=1, source_target_pairs={{0,8},{4,20},{8,0},{12,28},{16,24},{20,4},{24,16},{28,12},{1,9},{5... | collective-permute-start | bytes 5160968 | tf_op jit(solution)/shard_map/ppermute | solution.py:68
  311.2 23.1 %collective-permute-start.28 = (bf16[160,1536]{1,0:T(8,128)(2,1)S(1)}, bf16[160,1536]{1,0:T(8,128)(2,1)S(1)}, u32[]{:S(2)}, u32[]{:S(2)}) collective-permute-start(bf16[160,1536]{1,0:T(8,128)(2,1)S(1)} %copy-done.35), channel_id=1, source_target_pairs={{0,2},{1,3},{2,0},{3,1},{4,6},{5,7},{6,4},{7,5},{8,10},{9,11},{10,... | collective-permute-start | bytes 1474568 | tf_op jit(solution)/shard_map/ppermute | solution.py:68
  402.8 29.5 %collective-permute-start.38 = (bf16[2,2,4,48,2048]{4,3,2,1,0:T(8,128)(2,1)}, bf16[2,2,4,48,2048]{4,3,2,1,0:T(8,128)(2,1)}, u32[]{:S(2)}, u32[]{:S(2)}) collective-permute-start(bf16[2,2,4,48,2048]{4,3,2,1,0:T(8,128)(2,1)} %bitcast.221), channel_id=1, source_target_pairs={{0,4},{4,0},{8,12},{12,8},{16,20},{20,16},{24,28},{28,24},{1,5},{5... | collective-permute-start | bytes 9437192 | tf_op jit(solution)/shard_map/ppermute | solution.py:68
  405.3 27.0 %collective-permute-start.39 = (bf16[4,48,1536]{2,1,0:T(8,128)(2,1)}, bf16[4,48,1536]{2,1,0:T(8,128)(2,1)}, u32[]{:S(2)}, u32[]{:S(2)}) collective-permute-start(bf16[4,48,1536]{2,1,0:T(8,128)(2,1)} %fusion.15), channel_id=1, source_target_pairs={{0,16},{4,12},{8,24},{12,4},{16,0},{20,28},{24,8},{28,20},{1,17},{... | collective-permute-start | bytes 1769480 | tf_op jit(solution)/shard_map/ppermute | solution.py:68
  410.8 36.2 %all-to-all-start = ((bf16[4,48,2240]{2,1,0:T(8,128)(2,1)}), bf16[4,48,2240]{2,1,0:T(8,128)(2,1)}, u32[]{:S(2)}, u32[]{:S(2)}) async-start(bf16[4,48,2240]{2,1,0:T(8,128)(2,1)} %bitcast.207), calls=%async_computation.1 | async-start | bytes 1769472 | tf_op jit(solution)/shard_map/all_to_all | solution.py:946
  417.4 153.1 %reduce-scatter.5.cloned.1.call-start = ((), (), s32[]{:S(2)}) async-start(), calls=%async_computation.8 | async-start | bytes 7741440 | tf_op jit(solution)/shard_map/reduce_scatter | solution.py:934
  438.1 57.4 %collective-permute-start.42 = (bf16[2,48,8960]{2,1,0:T(8,128)(2,1)}, bf16[2,48,8960]{2,1,0:T(8,128)(2,1)}, u32[]{:S(2)}, u32[]{:S(2)}) collective-permute-start(bf16[2,48,8960]{2,1,0:T(8,128)(2,1)} %pad_maximum_fusion.5), channel_id=1, source_target_pairs={{0,8},{4,20},{8,0},{12,28},{16,24},{20,4},{24,16},{28,12},{1,9},{5... | collective-permute-start | bytes 5160968 | tf_op jit(solution)/shard_map/ppermute | solution.py:68
  439.4 56.2 %collective-permute-start.41 = (bf16[2,4,48,2048]{3,2,1,0:T(8,128)(2,1)}, bf16[2,4,48,2048]{3,2,1,0:T(8,128)(2,1)}, u32[]{:S(2)}, u32[]{:S(2)}) collective-permute-start(bf16[2,4,48,2048]{3,2,1,0:T(8,128)(2,1)} %fusion.4), channel_id=1, source_target_pairs={{0,8},{4,20},{8,0},{12,28},{16,24},{20,4},{24,16},{28,12},{1,9},{5... | collective-permute-start | bytes 4718600 | tf_op jit(solution)/shard_map/ppermute | solution.py:68
  501.6 33.8 %collective-permute-start.46 = (bf16[4,48,8960]{2,1,0:T(8,128)(2,1)}, bf16[4,48,8960]{2,1,0:T(8,128)(2,1)}, u32[]{:S(2)}, u32[]{:S(2)}) collective-permute-start(bf16[4,48,8960]{2,1,0:T(8,128)(2,1)} %pad_maximum_fusion.pieces_ref), channel_id=1, source_target_pairs={{0,4},{4,0},{8,12},{12,8},{16,20},{20,16},{24,28},{28,24},{1,5},{5... | collective-permute-start | bytes 10321928 | tf_op jit(solution)/shard_map/ppermute | solution.py:68
  501.6 32.6 %all-to-all-start.1 = ((bf16[4,48,1536]{2,1,0:T(8,128)(2,1)}), bf16[4,48,1536]{2,1,0:T(8,128)(2,1)}, u32[]{:S(2)}, u32[]{:S(2)}) async-start(bf16[4,48,1536]{2,1,0:T(8,128)(2,1)} %fusion.14), calls=%async_computation.2 | async-start | bytes 1179648 | tf_op jit(solution)/shard_map/all_to_all | solution.py:946
  507.0 28.4 %collective-permute-start.45 = (bf16[48,8960]{1,0:T(8,128)(2,1)S(1)}, bf16[48,8960]{1,0:T(8,128)(2,1)S(1)}, u32[]{:S(2)}, u32[]{:S(2)}) collective-permute-start(bf16[48,8960]{1,0:T(8,128)(2,1)S(1)} %concatenate.72), channel_id=1, source_target_pairs={{0,16},{4,12},{8,24},{12,4},{16,0},{20,28},{24,8},{28,20},{1,17},{... | collective-permute-start | bytes 2580488 | tf_op jit(solution)/shard_map/ppermute | solution.py:68
  508.3 27.2 %collective-permute-start.44 = (bf16[4,48,2048]{2,1,0:T(8,128)(2,1)}, bf16[4,48,2048]{2,1,0:T(8,128)(2,1)}, u32[]{:S(2)}, u32[]{:S(2)}) collective-permute-start(bf16[4,48,2048]{2,1,0:T(8,128)(2,1)} %fusion.7), channel_id=1, source_target_pairs={{0,16},{4,12},{8,24},{12,4},{16,0},{20,28},{24,8},{28,20},{1,17},{... | collective-permute-start | bytes 2359304 | tf_op jit(solution)/shard_map/ppermute | solution.py:68
  509.0 26.4 %collective-permute-start.47 = (bf16[160,1536]{1,0:T(8,128)(2,1)}, bf16[160,1536]{1,0:T(8,128)(2,1)}, u32[]{:S(2)}, u32[]{:S(2)}) collective-permute-start(bf16[160,1536]{1,0:T(8,128)(2,1)} %get-tuple-element.765), channel_id=1, source_target_pairs={{0,1},{1,2},{2,3},{3,0},{4,5},{5,6},{6,7},{7,4},{8,9},{9,10},{10,1... | collective-permute-start | bytes 1474568 | tf_op jit(solution)/shard_map/ppermute | solution.py:68
  540.1 26.6 %collective-permute-start.48 = (bf16[2,48,8960]{2,1,0:T(8,128)(2,1)}, bf16[2,48,8960]{2,1,0:T(8,128)(2,1)}, u32[]{:S(2)}, u32[]{:S(2)}) collective-permute-start(bf16[2,48,8960]{2,1,0:T(8,128)(2,1)} %pad_maximum_fusion.6), channel_id=1, source_target_pairs={{0,8},{4,20},{8,0},{12,28},{16,24},{20,4},{24,16},{28,12},{1,9},{5... | collective-permute-start | bytes 5160968 | tf_op jit(solution)/shard_map/ppermute | solution.py:68
  541.3 24.0 %all-to-all-start.2 = ((bf16[4,48,2048]{2,1,0:T(8,128)(2,1)}), bf16[4,48,2048]{2,1,0:T(8,128)(2,1)}, u32[]{:S(2)}, u32[]{:S(2)}) async-start(bf16[4,48,2048]{2,1,0:T(8,128)(2,1)} %fusion.6), calls=%async_computation.3 | async-start | bytes 1572864 | tf_op jit(solution)/shard_map/all_to_all | solution.py:946
  545.5 74.7 %all-gather.8.cloned.1.call-start = ((), (), s32[]{:S(2)}) async-start(), calls=%async_computation.9 | async-start | bytes 7741440 | tf_op jit(solution)/shard_map/all_gather | solution.py:1080
  581.7 25.3 %collective-permute-start.56 = (bf16[4,48,1536]{2,1,0:T(8,128)(2,1)S(1)}, bf16[4,48,1536]{2,1,0:T(8,128)(2,1)}, u32[]{:S(2)}, u32[]{:S(2)}) collective-permute-start(bf16[4,48,1536]{2,1,0:T(8,128)(2,1)S(1)} %pad_maximum_fusion.10.pieces_ref), channel_id=1, source_target_pairs={{0,4},{4,0},{8,12},{12,8},{16,20},{20,16},{24,28},{28,24},{1,5},{5... | collective-permute-start | bytes 1769480 | tf_op jit(solution)/shard_map/ppermute | solution.py:68
  582.7 23.5 %collective-permute-start.58 = (bf16[160,1536]{1,0:T(8,128)(2,1)S(1)}, bf16[160,1536]{1,0:T(8,128)(2,1)S(1)}, u32[]{:S(2)}, u32[]{:S(2)}) collective-permute-start(bf16[160,1536]{1,0:T(8,128)(2,1)S(1)} %copy-done.34), channel_id=1, source_target_pairs={{0,2},{1,3},{2,0},{3,1},{4,6},{5,7},{6,4},{7,5},{8,10},{9,11},{10,... | collective-permute-start | bytes 1474568 | tf_op jit(solution)/shard_map/ppermute | solution.py:68
  (82 other events, 1237.2 us)
Sparse Core Ops, SparseCore 0:
  56.8 80.6 all-gather.3
  139.9 77.5 all-gather.5
  306.0 71.0 reduce-scatter.2
  440.5 77.1 reduce-scatter.4
  570.6 49.4 all-gather.7

commit v12 on v11

--- a/solution.py
+++ b/solution.py
@@ -793,24 +793,26 @@
         return clock.send(shard, rows, [shards - step for step in steps])
 
     rep_index = lax.axis_index("rep")
+    input_matrix = lax.all_gather(
+        weight_piece(input_weight, rep_index), ("shard", "rep"), axis=0, tiled=True
+    )
     shard_vectors = jnp.concatenate([first_gain, second_gain, input_bias])
-    vector_row = jnp.pad(shard_vectors, (0, input_weight.shape[1] - shard_vectors.shape[0]))
-    own_input = jnp.concatenate([weight_piece(input_weight, rep_place), vector_row[None]], axis=0)
-    input_moving = send_around(own_input)
+    vector_row = jnp.pad(shard_vectors, (0, output_weight.shape[1] - shard_vectors.shape[0]))
+    own_output = jnp.concatenate(
+        [weight_piece(output_weight, rep_place), vector_row[None]], axis=0
+    )
+    output_moving = send_around(own_output)
     gate_blocks, up_blocks = clock.run(
         lambda *weights: column_blocks(rep_index, shard.place, *weights),
         gate_weight.reshape(reps, part_rows, hidden_units),
         up_weight.reshape(reps, part_rows, hidden_units),
     )
-    (output_piece,) = clock(weight_piece(output_weight, rep_index))
-    (input_rows,) = clock.wait(input_moving)
-    input_rows = [own_input] + input_rows
-
-    input_spread = spread(jnp.stack([rows[:part_rows] for rows in input_rows])[None])
-    passed = [[output_cotangent] * 2]
-    passing = clock.pass_on(shard, *passed[-1])
-    output_matrix = lax.all_gather(clock(output_piece)[0], ("shard", "rep"), axis=0, tiled=True)
-    vector_rows = jnp.stack(in_place_order([rows[part_rows] for rows in input_rows], shard))
+    (output_rows,) = clock.wait(output_moving)
+    output_rows = [own_output] + output_rows
+
+    output_spread = spread(jnp.stack([rows[:part_rows] for rows in output_rows])[None])
+    gate_moving = send_blocks(gate_blocks)
+    vector_rows = jnp.stack(in_place_order([rows[part_rows] for rows in output_rows], shard))
     own_gain = first_gain.shape[0]
     gain_one = vector_rows[:, :own_gain].reshape(width).astype(f32)
     gain_two = vector_rows[:, own_gain : 2 * own_gain].reshape(width).astype(f32)
@@ -847,22 +849,20 @@
         key_marks,
         row_marks,
     ) = clock(normed_one, cosine_table, sine_table, signed_sine, key_marks, row_marks)
-    input_arrived, arrived = clock.wait(input_spread.moving, passing)
-    passed.append(arrived)
-
-    input_spread.along(input_arrived)
-    gate_moving = send_blocks(gate_blocks)
-    input_arrived, gate_rows = clock.wait(input_spread.moving, gate_moving)
-
-    input_spread.over(input_arrived)
+    output_arrived, gate_rows = clock.wait(output_spread.moving, gate_moving)
+
+    output_spread.along(output_arrived)
     up_moving = send_blocks(up_blocks)
-    input_arrived, up_rows = clock.wait(input_spread.moving, up_moving)
-
-    (input_matrix,) = clock.run(place_blocks, z_order, *input_spread.finish(input_arrived))
-    input_matrix = input_matrix.reshape(width, -1)
+    output_arrived, up_rows = clock.wait(output_spread.moving, up_moving)
+
     gate_up = jnp.stack(
         [row for pair in zip([gate_blocks[0]] + gate_rows, [up_blocks[0]] + up_rows) for row in pair]
     )
+    gate_up = lax.all_gather(clock(gate_up)[0], "rep", axis=0, tiled=True)
+    passed = [[output_cotangent] * 2]
+    passing = clock.pass_on(shard, *passed[-1])
+    output_spread.over(output_arrived)
+    input_matrix, normed_one = clock(input_matrix, normed_one)
     projected = jnp.dot(normed_one, input_matrix, preferred_element_type=f32) + shift_row
     key_part = rotate(
         projected[:, query_width : query_width + pair_width].reshape(own_rows, KVH, HD),
@@ -875,18 +875,21 @@
             axis=1,
         ).astype(bf16)
     )
+    arrived, output_arrived = clock.wait(passing, output_spread.moving)
+    passed.append(arrived)
+
     pair_moving = send_around(own_pairs)
     passing = clock.pass_on(shard, *passed[-1]) if shards > 2 else []
-    gate_up = lax.all_gather(clock(gate_up)[0], "rep", axis=0, tiled=True)
     pair_rows, arrived = clock.wait(pair_moving, passing)
     passed.append(arrived)
     pairs = jnp.concatenate([own_pairs] + pair_rows, axis=0)
 
     passing = clock.pass_on(shard, *passed[-1]) if shards > 3 else []
+    (output_matrix,) = clock.run(place_blocks, z_order, *output_spread.finish(output_arrived))
+    output_matrix = output_matrix.reshape(width, width)
     queries, attention_low = clock.run(
         attention_forward, projected, cosine_table, signed_sine, pairs, row_marks.T, key_marks
     )
-    output_matrix, attention_low = clock(output_matrix, attention_low)
     hidden = wide_tokens + jnp.dot(attention_low, output_matrix, preferred_element_type=f32)
     inverse_two = lax.rsqrt(jnp.mean(hidden * hidden, axis=-1, keepdims=True) + EPSILON)
     unit_two = hidden * inverse_two
@@ -943,7 +946,7 @@
     inside = list(range(1, shards - 2))
 
     def exchange(blocks):
-        return clock(lax.all_to_all(blocks, "shard", 0, 0, tiled=True))[0]
+        return lax.all_to_all(clock(blocks)[0], "shard", 0, 0, tiled=True)
 
     normed_own, *normed_partial = clock.run(
         lambda *operands: rows_product(operands[:2], operands[2:], True, shards),
@@ -996,11 +999,14 @@
 
     pair_moving = send_back(pair_partial)
     output = Halving(clock, *output_halves, core, first, second)
-    up_blocks = clock(*blocks_of(up.finish(up_arrived)))
+    up_sum = exchange(up.finish(up_arrived))
+    block_own, *block_partial = clock.run(
+        lambda left, right: rows_product((left,), (right,), False, shards), inner_act, down_weight
+    )
     pair_arrived, output_arrived = clock.wait(pair_moving, output.moving)
 
-    output.along_first(output_arrived)
-    up_moving = send_blocks(up_blocks)
+    (gate_piece,) = clock(gate_piece)
+    down_piece = sum_over_rep(clock(down_blocks)[0].reshape(block_units, width))
     projected_gradient, bias_sum = clock.run(
         lambda *operands: join_projected(operands[0], operands[3:], *operands[1:3]),
         d_queries,
@@ -1010,16 +1016,12 @@
         *pair_arrived,
     )
     projected_halves = split_halves(normed_one, projected_gradient, shards, False)
-    output_arrived, up_rows = clock.wait(output.moving, up_moving)
+    (up_sum,) = clock(up_sum)
+    gate_sum = exchange(gate_piece.reshape(shards, part_rows, block_units))
 
     projected = Halving(clock, *projected_halves, core, first, second)
-    output.along_second(output_arrived)
-    up_spread = spread(side_by_side(in_place_order(up_blocks[:1] + up_rows, shard)))
-    (gate_piece,) = clock(gate_piece)
-    down_piece = sum_over_rep(clock(down_blocks)[0].reshape(block_units, width))
-    block_own, *block_partial = clock.run(
-        lambda left, right: rows_product((left,), (right,), False, shards), inner_act, down_weight
-    )
+    output.along_first(output_arrived)
+    up_spread = spread(side_by_side(up_sum))
     projected_gradient, hidden_gradient = clock(projected_gradient, hidden_gradient)
     normed_one_gradient = times_transposed(projected_gradient, input_matrix)
     gain_one_gradient = jnp.sum(normed_one_gradient * unit_one, axis=0)
@@ -1033,10 +1035,8 @@
     )
 
     projected.along_first(projected_arrived)
-    up_spread.along(up_arrived)
-    block_moving = send_some(block_partial, edges[:1])
-    output_sum = output.finish(output_arrived)
-    gate_sum = exchange(gate_piece.reshape(shards, part_rows, block_units))
+    output.along_second(output_arrived)
+    gate_spread = spread(side_by_side(clock(gate_sum)[0]))
     bias_gradient = bias_sum[0]
     bias_split = query_width + pair_width
     small_parts = (
@@ -1048,36 +1048,36 @@
     (small,) = clock(
         jnp.concatenate([part.reshape(shards, -1) for part in small_parts], axis=1)
     )
+    projected_arrived, output_arrived, gate_arrived = clock.wait(
+        projected.moving, output.moving, gate_spread.moving
+    )
+
+    projected.along_second(projected_arrived)
+    up_spread.along(up_arrived)
+    output_sum = exchange(output.finish(output_arrived))
+    block_moving = send_some(block_partial, edges[:1])
     projected_arrived, up_arrived, block_arrived = clock.wait(
         projected.moving, up_spread.moving, block_moving
     )
 
-    projected.along_second(projected_arrived)
-    gate_spread = spread(side_by_side(gate_sum))
+    (output_sum,) = clock(output_sum)
+    input_sum = exchange(projected.finish(projected_arrived))
+    gate_spread.along(gate_arrived)
+    output_spread = spread(row_sum(output_sum))
     up_spread.over(up_arrived)
-    block_moving = send_some(block_partial, edges[1:])
-    output_sum = row_sum(exchange(output_sum))
-    projected_arrived, gate_arrived, up_arrived, more_arrived = clock.wait(
-        projected.moving, gate_spread.moving, up_spread.moving, block_moving
-    )
-    block_arrived = block_arrived + more_arrived
-
-    input_sum = projected.finish(projected_arrived)
-    gate_spread.along(gate_arrived)
-    output_spread = spread(output_sum)
     small_moving = clock.send(core, [small], [1])
-    input_sum = row_sum(exchange(input_sum))
-    gate_arrived, output_arrived, small_arrived = clock.wait(
-        gate_spread.moving, output_spread.moving, small_moving
+    gate_arrived, output_arrived, up_arrived, small_arrived = clock.wait(
+        gate_spread.moving, output_spread.moving, up_spread.moving, small_moving
     )
     small = total_of([small] + small_arrived)
 
-    input_spread = spread(input_sum)
+    (input_sum,) = clock(input_sum)
+    (down_piece,) = clock(down_piece)
+    down_gathered = lax.all_gather(down_piece, "rep", axis=0, tiled=True)
+    input_spread = spread(row_sum(input_sum))
     output_spread.along(output_arrived)
     gate_spread.over(gate_arrived)
     small_moving = clock.send(first, [small] * (first.size - 1), range(1, first.size))
-    (down_piece,) = clock(down_piece)
-    down_gathered = lax.all_gather(down_piece, "rep", axis=0, tiled=True)
     (up_total,) = clock.run(widen_pieces, *up_spread.finish(up_arrived))
     input_arrived, output_arrived, gate_arrived, small_arrived = clock.wait(
         input_spread.moving, output_spread.moving, gate_spread.moving, small_moving
@@ -1087,7 +1087,7 @@
     input_spread.along(input_arrived)
     output_spread.over(output_arrived)
     small_moving = clock.send(second, [small] * (second.size - 1), range(1, second.size))
-    block_moving = send_some(block_partial, inside)
+    block_moving = send_some(block_partial, edges[1:])
     (gate_total,) = clock.run(widen_pieces, *gate_spread.finish(gate_arrived))
     input_arrived, output_arrived, small_arrived, more_arrived = clock.wait(
         input_spread.moving, output_spread.moving, small_moving, block_moving
@@ -1096,15 +1096,16 @@
     block_arrived = block_arrived + more_arrived
 
     input_spread.over(input_arrived)
-    small_blocks = clock(*blocks_of(small))
-    small_moving = send_blocks(small_blocks)
+    small_sum = exchange(small)
+    block_moving = send_some(block_partial, inside)
     (output_total,) = clock.run(widen_pieces, *output_spread.finish(output_arrived))
-    input_arrived, small_arrived = clock.wait(input_spread.moving, small_moving)
-    small = total_of(small_blocks[:1] + small_arrived)
-    (block_out,) = clock(total_of([hidden, block_own] + block_arrived).astype(bf16))
     (down_gathered,) = clock(down_gathered)
     (down_total,) = clock(down_gathered.astype(f32))
+    input_arrived, more_arrived = clock.wait(input_spread.moving, block_moving)
+    block_arrived = block_arrived + more_arrived
+    (block_out,) = clock(total_of([hidden, block_own] + block_arrived).astype(bf16))
     (input_total,) = clock.run(widen_pieces, *input_spread.finish(input_arrived))
+    small = total_of(list(clock(small_sum)[0]))
 
     small = small + clock.token[0, 0]
     small_totals, at = [], 0

time: 654 us -> 683 us (1.044)
  waiting for transfers between devices: 251 us -> 271 us
  starting transfers between devices: 114 us -> 123 us
    ppermute x57 -> x51, waiting for transfers between devices: 164 us -> 229 us  [shift(): return lax.ppermute(value, self.name, self.pairs(step % self.size))]
    all_gather x1, waiting for transfers between devices: 26.2 us -> 0.01 us  [on_device(): gate_up = lax.all_gather(clock(gate_up)[0], 'rep', axis=0, tiled=True)]
    all_to_all x3 -> x5, waiting for transfers between devices: 41 us -> 21.3 us  [exchange(): return lax.all_to_all(clock(blocks)[0], 'shard', 0, 0, tiled=True)]
    ppermute x57 -> x51, starting transfers between devices: 71.8 us -> 78.8 us  [shift(): return lax.ppermute(value, self.name, self.pairs(step % self.size))]
    all_to_all x3 -> x5, starting transfers between devices: 16.2 us -> 20.1 us  [exchange(): return lax.all_to_all(clock(blocks)[0], 'shard', 0, 0, tiled=True)]
  transfers between devices with their start and end apart: 71 -> 67, of which waited for: 26 -> 33; matrix products, arithmetic and copies ran while one was open for 15% -> 15% of each run, Pallas kernels for 15% -> 14%
where the time goes in v12:
time: 683 us; the launch traced here: 673 us
  waiting for transfers between devices  271 us (40%)
  Pallas kernels  144 us (21%)
  starting transfers between devices  123 us (18%)
  other arithmetic  73.1 us (11%)
  local copies, waits for them, and re-layouts  29 us (4%)
  matrix products  16.3 us (2%)
  between operations  15.2 us (2%)
    ppermute x51, waiting for transfers between devices, shift(): return lax.ppermute(value, self.name, self.pairs(step % self.size))  229 us
    ppermute x51, starting transfers between devices, shift(): return lax.ppermute(value, self.name, self.pairs(step % self.size))  78.8 us
    ppermute x6, starting transfers between devices, pass_on(): return lax.ppermute(value, self.name, pairs)  24.2 us
    pallas_call x1, Pallas kernels, feed_forward(): pl.pallas_call(body, grid=(steps,), out_shape=[jax.ShapeDtypeStruct((coun...  23.6 us
    pallas_call x2, Pallas kernels, rows_product(): pl.pallas_call(body, grid=(pl.cdiv(columns, TILE),), out_shape=[jax.Shape...  23 us
    pallas_call x4, Pallas kernels, widen_pieces(): pl.pallas_call(body, out_shape=jax.ShapeDtypeStruct((reps, rows, columns)...  22.3 us
    all_to_all x5, waiting for transfers between devices, exchange(): return lax.all_to_all(clock(blocks)[0], 'shard', 0, 0, tiled=True)  21.3 us
    ppermute x6, waiting for transfers between devices, pass_on(): return lax.ppermute(value, self.name, pairs)  20.2 us
  transfers between devices with their start and end apart: 67, of which 33 were waited for; matrix products, arithmetic and copies ran while one was open for 15% of the time, Pallas kernels for 14%

profile of v12, /device:TPU:0, one launch (start us, length us, event | category | flops | bytes accessed | tf_op | source)
XLA Modules:
  0.0 672.6 jit_solution(1260452144321765451)
XLA Ops:
  42.5 6.9 %collective-permute-done.4 = bf16[48,2240]{1,0:T(8,128)(2,1)S(1)} collective-permute-done((bf16[48,2240]{1,0:T(8,128)(2,1)}, bf16[48,2240]{1,0:T(8,128)(2,1)S(1)}, u32[]{:S(2)}, u32[]{:S(2)}) %collective-permute-start.4) | collective-permute-done | bytes 215072 | tf_op jit(solution)/shard_map/ppermute | solution.py:68
  49.4 13.6 %collective-permute-done.5 = bf16[48,2240]{1,0:T(8,128)(2,1)S(1)} collective-permute-done((bf16[48,2240]{1,0:T(8,128)(2,1)}, bf16[48,2240]{1,0:T(8,128)(2,1)S(1)}, u32[]{:S(2)}, u32[]{:S(2)}) %collective-permute-start.5) | collective-permute-done | bytes 215072 | tf_op jit(solution)/shard_map/ppermute | solution.py:68
  74.3 7.8 %collective-permute-done.8 = bf16[48,2240]{1,0:T(8,128)(2,1)S(1)} collective-permute-done((bf16[48,2240]{1,0:T(8,128)(2,1)S(1)}, bf16[48,2240]{1,0:T(8,128)(2,1)S(1)}, u32[]{:S(2)}, u32[]{:S(2)}) %collective-permute-start.8) | collective-permute-done | bytes 215072 | tf_op jit(solution)/shard_map/ppermute | solution.py:68
  82.1 17.6 %collective-permute-done.9 = bf16[48,2240]{1,0:T(8,128)(2,1)S(1)} collective-permute-done((bf16[48,2240]{1,0:T(8,128)(2,1)S(1)}, bf16[48,2240]{1,0:T(8,128)(2,1)S(1)}, u32[]{:S(2)}, u32[]{:S(2)}) %collective-permute-start.9) | collective-permute-done | bytes 215072 | tf_op jit(solution)/shard_map/ppermute | solution.py:68
  107.5 13.9 %collective-permute-start.11 = (bf16[160,1536]{1,0:T(8,128)(2,1)S(1)}, bf16[160,1536]{1,0:T(8,128)(2,1)}, u32[]{:S(2)}, u32[]{:S(2)}) collective-permute-start(bf16[160,1536]{1,0:T(8,128)(2,1)S(1)} %copy-done.15), channel_id=1, source_target_pairs={{0,1},{1,2},{2,3},{4,5},{5,6},{6,7},{8,9},{9,10},{10,11},{12,13},{... | collective-permute-start | bytes 1474568 | tf_op jit(solution)/shard_map/ppermute | solution.py:73
  146.8 9.6 %collective-permute-done.14 = bf16[160,512]{1,0:T(8,128)(2,1)S(1)} collective-permute-done((bf16[160,512]{1,0:T(8,128)(2,1)S(1)}, bf16[160,512]{1,0:T(8,128)(2,1)S(1)}, u32[]{:S(2)}, u32[]{:S(2)}) %collective-permute-start.14) | collective-permute-done | bytes 163872 | tf_op jit(solution)/shard_map/ppermute | solution.py:68
  156.3 7.9 %collective-permute-done.15 = bf16[160,512]{1,0:T(8,128)(2,1)S(1)} collective-permute-done((bf16[160,512]{1,0:T(8,128)(2,1)S(1)}, bf16[160,512]{1,0:T(8,128)(2,1)S(1)}, u32[]{:S(2)}, u32[]{:S(2)}) %collective-permute-start.15) | collective-permute-done | bytes 163872 | tf_op jit(solution)/shard_map/ppermute | solution.py:68
  188.0 6.7 collective-permute-done.19
  205.7 11.7 %place_blocks.3 = (bf16[4,8,48,2240]{3,2,1,0:T(8,128)(2,1)}, bf16[4,8,48,2240]{3,2,1,0:T(8,128)(2,1)}) custom-call(s32[4]{0:T(128)} %pad_add_fusion.5.order_ref, bf16[64,48,2240]{2,1,0:T(8,128)(2,1)} %all-gather.5.cloned.1.call-done.source), custom_call_target="tpu_custom_call" | custom-call | flops 1 | bytes 1 | tf_op jit(solution)/shard_map/place_blocks/pallas_call | solution.py:339
  217.4 15.2 %collective-permute-done.22 = bf16[160,1536]{1,0:T(8,128)(2,1)S(1)} collective-permute-done((bf16[160,1536]{1,0:T(8,128)(2,1)S(1)}, bf16[160,1536]{1,0:T(8,128)(2,1)S(1)}, u32[]{:S(2)}, u32[]{:S(2)}) %collective-permute-start.22) | collective-permute-done | bytes 491552 | tf_op jit(solution)/shard_map/ppermute | solution.py:68
  235.0 23.6 %feed_forward.1 = (bf16[640,2240]{1,0:T(8,128)(2,1)}, bf16[640,2240]{1,0:T(8,128)(2,1)}, bf16[640,2240]{1,0:T(8,128)(2,1)}, bf16[1536,640]{1,0:T(8,128)(2,1)}, bf16[2240,640]{1,0:T(8,128)(2,1)}) custom-call(bf16[640,1536]{1,0:T(8,128)(2,1)} %pad_maximum_fusion.3.rows_ref, bf16[640,1536]{1,0:T(8,128)(2,1)} %pad_maximum_fusion.4.cotangents_ref.right_ref, ...), custom_call_target="tpu_custom_call" | custom-call | flops 1 | bytes 1 | tf_op jit(solution)/shard_map/feed_forward/pallas_call | solution.py:477
  258.6 14.6 %rows_product.2 = (bf16[160,1536]{1,0:T(8,128)(2,1)}, bf16[160,1536]{1,0:T(8,128)(2,1)}, bf16[160,1536]{1,0:T(8,128)(2,1)}, bf16[160,1536]{1,0:T(8,128)(2,1)}) custom-call(bf16[640,2240]{1,0:T(8,128)(2,1)} %get-tuple-element.571.refs_0_.right_ref, bf16[640,2240]{1,0:T(8,128)(2,1)} %get-tuple-element.560.refs_1_.right_ref, bf16[1536,2240]{1,0:T(8,128)(2,1)} %bitcast.177, ...), custom_call_target="tpu_custom_call" | custom-call | flops 1 | bytes 1 | tf_op jit(solution)/shard_map/rows_product/pallas_call | solution.py:603
  273.2 10.0 %split_gradient.3 = (bf16[4,4,48,2240]{3,2,1,0:T(8,128)(2,1)}, bf16[4,4,48,2240]{3,2,1,0:T(8,128)(2,1)}) custom-call(s32[1]{0:T(128)} %bitcast.46.core_ref, bf16[1536,640]{1,0:T(8,128)(2,1)} %get-tuple-element.570.left_ref, bf16[640,2240]{1,0:T(8,128)(2,1)} %get-tuple-element.560.refs_1_.right_ref), custom_call_target="tpu_custom_call" | custom-call | flops 1 | bytes 1 | tf_op jit(solution)/shard_map/split_gradient/pallas_call | solution.py:533
  283.3 9.7 %collective-permute-start.25 = (bf16[160,1536]{1,0:T(8,128)(2,1)S(1)}, bf16[160,1536]{1,0:T(8,128)(2,1)S(1)}, u32[]{:S(2)}, u32[]{:S(2)}) collective-permute-start(bf16[160,1536]{1,0:T(8,128)(2,1)S(1)} %copy-done.42), channel_id=1, source_target_pairs={{0,3},{1,0},{2,1},{3,2},{4,7},{5,4},{6,5},{7,6},{8,11},{9,8},{10,9... | collective-permute-start | bytes 1474568 | tf_op jit(solution)/shard_map/ppermute | solution.py:68
  293.8 9.9 %ordered_gradient.2 = bf16[8,4,48,2240]{3,2,1,0:T(8,128)(2,1)} custom-call(bf16[1536,640]{1,0:T(8,128)(2,1)} %get-tuple-element.570.left_ref, bf16[640,2240]{1,0:T(8,128)(2,1)} %get-tuple-element.571.refs_0_.right_ref), custom_call_target="tpu_custom_call" | custom-call | flops 1 | bytes 1 | tf_op jit(solution)/shard_map/ordered_gradient/pallas_call | solution.py:563
  306.0 10.3 %collective-permute-done.26 = bf16[160,1536]{1,0:T(8,128)(2,1)S(1)} collective-permute-done((bf16[160,1536]{1,0:T(8,128)(2,1)S(1)}, bf16[160,1536]{1,0:T(8,128)(2,1)S(1)}, u32[]{:S(2)}, u32[]{:S(2)}) %collective-permute-start.26) | collective-permute-done | bytes 491552 | tf_op jit(solution)/shard_map/ppermute | solution.py:68
  322.7 9.9 %ordered_gradient.3 = bf16[8,1,280,1536]{3,2,1,0:T(8,128)(2,1)} custom-call(bf16[2240,640]{1,0:T(8,128)(2,1)} %get-tuple-element.586.left_ref, bf16[640,1536]{1,0:T(8,128)(2,1)} %pad_maximum_fusion.4.cotangents_ref.right_ref), custom_call_target="tpu_custom_call" | custom-call | flops 1 | bytes 1 | tf_op jit(solution)/shard_map/ordered_gradient/pallas_call | solution.py:563
  332.6 12.2 %collective-permute-done.28 = bf16[160,1536]{1,0:T(8,128)(2,1)S(1)} collective-permute-done((bf16[160,1536]{1,0:T(8,128)(2,1)S(1)}, bf16[160,1536]{1,0:T(8,128)(2,1)S(1)}, u32[]{:S(2)}, u32[]{:S(2)}) %collective-permute-start.28) | collective-permute-done | bytes 491552 | tf_op jit(solution)/shard_map/ppermute | solution.py:68
  352.9 7.5 %attention_backward.1 = (bf16[160,1536]{1,0:T(8,128)(2,1)}, bf16[160,512]{1,0:T(8,128)(2,1)}, bf16[160,512]{1,0:T(8,128)(2,1)}, bf16[160,512]{1,0:T(8,128)(2,1)}, bf16[160,512]{1,0:T(8,128)(2,1)}) custom-call(bf16[2,960,128]{2,1,0:T(8,128)(2,1)} %get-tuple-element.604.queries_ref, bf16[160,1536]{1,0:T(8,128)(2,1)} %convolution_convert_fusion.gradient_ref, ...), custom_call_target="tpu_custom_call" | custom-call | flops 1 | bytes 1 | tf_op jit(solution)/shard_map/attention_backward/pallas_call | solution.py:705
  378.2 13.4 %collective-permute-start.30 = (bf16[160,512]{1,0:T(8,128)(2,1)}, bf16[160,512]{1,0:T(8,128)(2,1)}, u32[]{:S(2)}, u32[]{:S(2)}) collective-permute-start(bf16[160,512]{1,0:T(8,128)(2,1)} %get-tuple-element.642), channel_id=1, source_target_pairs={{0,3},{1,0},{2,1},{3,2},{4,7},{5,4},{6,5},{7,6},{8,11},{9,8},{10,9... | collective-permute-start | bytes 491528 | tf_op jit(solution)/shard_map/ppermute | solution.py:68
  392.7 8.4 %rows_product.3 = (bf16[160,1536]{1,0:T(8,128)(2,1)}, bf16[160,1536]{1,0:T(8,128)(2,1)}, bf16[160,1536]{1,0:T(8,128)(2,1)}, bf16[160,1536]{1,0:T(8,128)(2,1)}) custom-call(bf16[640,2240]{1,0:T(8,128)(2,1)} %get-tuple-element.635.refs_0_, bf16[2240,1536]{1,0:T(8,128)(2,1)} %refs_1_), custom_call_target="tpu_custom_call" | custom-call | flops 1 | bytes 1 | tf_op jit(solution)/shard_map/rows_product/pallas_call | solution.py:603
  401.1 13.7 %collective-permute-done.31.refs_2_ = bf16[160,512]{1,0:T(8,128)(2,1)} collective-permute-done((bf16[160,512]{1,0:T(8,128)(2,1)}, bf16[160,512]{1,0:T(8,128)(2,1)}, u32[]{:S(2)}, u32[]{:S(2)}) %collective-permute-start.31) | collective-permute-done | bytes 163872 | tf_op jit(solution)/shard_map/ppermute | solution.py:68
  443.9 9.3 %collective-permute-done.36 = bf16[48,8960]{1,0:T(8,128)(2,1)} collective-permute-done((bf16[48,8960]{1,0:T(8,128)(2,1)S(1)}, bf16[48,8960]{1,0:T(8,128)(2,1)}, u32[]{:S(2)}, u32[]{:S(2)}) %collective-permute-start.36) | collective-permute-done | bytes 860192 | tf_op jit(solution)/shard_map/ppermute | solution.py:68
  472.2 23.4 %collective-permute-done.38 = bf16[4,48,1536]{2,1,0:T(8,128)(2,1)S(1)} collective-permute-done((bf16[4,48,1536]{2,1,0:T(8,128)(2,1)}, bf16[4,48,1536]{2,1,0:T(8,128)(2,1)S(1)}, u32[]{:S(2)}, u32[]{:S(2)}) %collective-permute-start.38) | collective-permute-done | bytes 589856 | tf_op jit(solution)/shard_map/ppermute | solution.py:68
  495.6 20.5 %collective-permute-done.39 = bf16[48,8960]{1,0:T(8,128)(2,1)S(1)} collective-permute-done((bf16[48,8960]{1,0:T(8,128)(2,1)S(1)}, bf16[48,8960]{1,0:T(8,128)(2,1)S(1)}, u32[]{:S(2)}, u32[]{:S(2)}) %collective-permute-start.39) | collective-permute-done | bytes 860192 | tf_op jit(solution)/shard_map/ppermute | solution.py:68
  531.9 10.7 %collective-permute-done.42 = bf16[160,1536]{1,0:T(8,128)(2,1)} collective-permute-done((bf16[160,1536]{1,0:T(8,128)(2,1)}, bf16[160,1536]{1,0:T(8,128)(2,1)}, u32[]{:S(2)}, u32[]{:S(2)}) %collective-permute-start.42) | collective-permute-done | bytes 491552 | tf_op jit(solution)/shard_map/ppermute | solution.py:68
  545.6 8.9 %collective-permute-done.41 = bf16[2,48,8960]{2,1,0:T(8,128)(2,1)} collective-permute-done((bf16[2,48,8960]{2,1,0:T(8,128)(2,1)}, bf16[2,48,8960]{2,1,0:T(8,128)(2,1)}, u32[]{:S(2)}, u32[]{:S(2)}) %collective-permute-start.41) | collective-permute-done | bytes 1720352 | tf_op jit(solution)/shard_map/ppermute | solution.py:68
  574.5 11.3 %collective-permute-done.43 = bf16[2,48,8960]{2,1,0:T(8,128)(2,1)} collective-permute-done((bf16[2,48,8960]{2,1,0:T(8,128)(2,1)}, bf16[2,48,8960]{2,1,0:T(8,128)(2,1)}, u32[]{:S(2)}, u32[]{:S(2)}) %collective-permute-start.43) | collective-permute-done | bytes 1720352 | tf_op jit(solution)/shard_map/ppermute | solution.py:68
  594.2 7.3 %widen_pieces.4 = f32[8,48,8960]{2,1,0:T(8,128)} custom-call(s32[8]{0:T(128)} %stack.239.places_ref, bf16[4,48,8960]{2,1,0:T(8,128)(2,1)} %pad_maximum_fusion.pieces_ref, bf16[4,48,8960]{2,1,0:T(8,128)(2,1)} %collective-permute-done.45.others_ref), custom_call_target="tpu_custom_call" | custom-call | flops 1 | bytes 1 | tf_op jit(solution)/shard_map/widen_pieces/pallas_call | solution.py:415
  607.4 8.4 %widen_pieces.5 = f32[8,48,8960]{2,1,0:T(8,128)} custom-call(s32[8]{0:T(128)} %stack.239.places_ref, bf16[4,48,8960]{2,1,0:T(8,128)(2,1)} %copy-done.2, bf16[4,48,8960]{2,1,0:T(8,128)(2,1)} %collective-permute-done.49.others_ref), custom_call_target="tpu_custom_call" | custom-call | flops 1 | bytes 1 | tf_op jit(solution)/shard_map/widen_pieces/pallas_call | solution.py:415
  630.5 15.6 %all-to-all-done.4 = f32[4,1,1280]{2,1,0:T(1,128)S(1)} async-done(((f32[4,1,1280]{2,1,0:T(1,128)}), f32[4,1,1280]{2,1,0:T(1,128)S(1)}, u32[]{:S(2)}, u32[]{:S(2)}) %all-to-all-start.4) | async-done | bytes 20512 | tf_op jit(solution)/shard_map/all_to_all | solution.py:949
  646.1 10.2 %convert_element_type.349 = f32[2240,1536]{1,0:T(8,128)} convert(bf16[2240,1536]{1,0:T(8,128)(2,1)} %all-gather.7.cloned.1.call-done) | non-fusion elementwise | flops 3440640 | bytes 20643840 | tf_op jit(solution)/shard_map/convert_element_type | solution.py:1103
  (350 shorter events, 277.5 us)
Async XLA Ops:
  7.2 115.5 %all-gather.9.cloned.1.call-start = ((), (), s32[]{:S(2)}) async-start(), calls=%async_computation.11 | async-start | bytes 6488064 | tf_op jit(solution)/shard_map/all_gather | solution.py:796
  9.3 196.4 %all-gather.5.cloned.1.call-start = ((), (), s32[]{:S(2)}) async-start(), calls=%async_computation.7 | async-start | bytes 15925248 | tf_op jit(solution)/shard_map/all_gather | solution.py:861
  31.2 31.8 %collective-permute-start.3 = (bf16[1,4,48,1536]{3,2,1,0:T(8,128)(2,1)S(1)}, bf16[1,4,48,1536]{3,2,1,0:T(8,128)(2,1)S(1)}, u32[]{:S(2)}, u32[]{:S(2)}) collective-permute-start(bf16[1,4,48,1536]{3,2,1,0:T(8,128)(2,1)S(1)} %get-tuple-element.435), channel_id=1, source_target_pairs={{0,16},{4,12},{8,24},{12,4},{16,0},{20,28},{24,8},{28,20},{1,17},{... | collective-permute-start | bytes 1769480 | tf_op jit(solution)/shard_map/ppermute | solution.py:68
  63.2 36.5 %collective-permute-start.7 = (bf16[2,1,4,48,1536]{4,3,2,1,0:T(8,128)(2,1)S(1)}, bf16[2,1,4,48,1536]{4,3,2,1,0:T(8,128)(2,1)S(1)}, u32[]{:S(2)}, u32[]{:S(2)}) collective-permute-start(bf16[2,1,4,48,1536]{4,3,2,1,0:T(8,128)(2,1)S(1)} %pad_maximum_fusion.7), channel_id=1, source_target_pairs={{0,8},{4,20},{8,0},{12,28},{16,24},{20,4},{24,16},{28,12},{1,9},{5... | collective-permute-start | bytes 3538952 | tf_op jit(solution)/shard_map/ppermute | solution.py:68
  70.9 28.8 %collective-permute-start.9 = (bf16[48,2240]{1,0:T(8,128)(2,1)S(1)}, bf16[48,2240]{1,0:T(8,128)(2,1)S(1)}, u32[]{:S(2)}, u32[]{:S(2)}) collective-permute-start(bf16[48,2240]{1,0:T(8,128)(2,1)S(1)} %get-tuple-element.446), channel_id=1, source_target_pairs={{0,2},{1,3},{2,0},{3,1},{4,6},{5,7},{6,4},{7,5},{8,10},{9,11},{10,... | collective-permute-start | bytes 645128 | tf_op jit(solution)/shard_map/ppermute | solution.py:68
  73.5 26.1 %collective-permute-start.10 = (bf16[48,2240]{1,0:T(8,128)(2,1)S(1)}, bf16[48,2240]{1,0:T(8,128)(2,1)S(1)}, u32[]{:S(2)}, u32[]{:S(2)}) collective-permute-start(bf16[48,2240]{1,0:T(8,128)(2,1)S(1)} %get-tuple-element.447), channel_id=1, source_target_pairs={{0,3},{1,0},{2,1},{3,2},{4,7},{5,4},{6,5},{7,6},{8,11},{9,8},{10,9... | collective-permute-start | bytes 645128 | tf_op jit(solution)/shard_map/ppermute | solution.py:68
  104.2 310.6 %reduce-scatter.3.cloned.1.call-start = ((), (), s32[]{:S(2)}) async-start(), calls=%async_computation.8 | async-start | bytes 7962624 | tf_op jit(solution)/shard_map/reduce_scatter | solution.py:937
  107.2 29.4 %collective-permute-start.13 = (bf16[4,1,4,48,1536]{4,3,2,1,0:T(8,128)(2,1)}, bf16[4,1,4,48,1536]{4,3,2,1,0:T(8,128)(2,1)}, u32[]{:S(2)}, u32[]{:S(2)}) collective-permute-start(bf16[4,1,4,48,1536]{4,3,2,1,0:T(8,128)(2,1)} %pad_maximum_fusion.2.pieces_ref), channel_id=1, source_target_pairs={{0,4},{4,0},{8,12},{12,8},{16,20},{20,16},{24,28},{28,24},{1,5},{5... | collective-permute-start | bytes 7077896 | tf_op jit(solution)/shard_map/ppermute | solution.py:68
  107.5 24.1 %collective-permute-start.11 = (bf16[160,1536]{1,0:T(8,128)(2,1)S(1)}, bf16[160,1536]{1,0:T(8,128)(2,1)}, u32[]{:S(2)}, u32[]{:S(2)}) collective-permute-start(bf16[160,1536]{1,0:T(8,128)(2,1)S(1)} %copy-done.15), channel_id=1, source_target_pairs={{0,1},{1,2},{2,3},{4,5},{5,6},{6,7},{8,9},{9,10},{10,11},{12,13},{... | collective-permute-start | bytes 1474568 | tf_op jit(solution)/shard_map/ppermute | solution.py:73
  136.6 27.7 %collective-permute-start.17 = (bf16[160,1536]{1,0:T(8,128)(2,1)}, bf16[160,1536]{1,0:T(8,128)(2,1)S(1)}, u32[]{:S(2)}, u32[]{:S(2)}) collective-permute-start(bf16[160,1536]{1,0:T(8,128)(2,1)} %collective-permute-done.11), channel_id=1, source_target_pairs={{0,1},{1,2},{2,3},{4,5},{5,6},{6,7},{8,9},{9,10},{10,11},{12,13},{... | collective-permute-start | bytes 1474568 | tf_op jit(solution)/shard_map/ppermute | solution.py:73
  138.1 26.2 %collective-permute-start.18 = (bf16[160,1536]{1,0:T(8,128)(2,1)}, bf16[160,1536]{1,0:T(8,128)(2,1)}, u32[]{:S(2)}, u32[]{:S(2)}) collective-permute-start(bf16[160,1536]{1,0:T(8,128)(2,1)} %collective-permute-done.12), channel_id=1, source_target_pairs={{1,0},{2,1},{3,2},{5,4},{6,5},{7,6},{9,8},{10,9},{11,10},{13,12},{... | collective-permute-start | bytes 1474568 | tf_op jit(solution)/shard_map/ppermute | solution.py:73
  199.3 33.2 %collective-permute-start.22 = (bf16[160,1536]{1,0:T(8,128)(2,1)S(1)}, bf16[160,1536]{1,0:T(8,128)(2,1)S(1)}, u32[]{:S(2)}, u32[]{:S(2)}) collective-permute-start(bf16[160,1536]{1,0:T(8,128)(2,1)S(1)} %multiply_convert_fusion), channel_id=1, source_target_pairs={{0,2},{1,3},{2,0},{3,1},{4,6},{5,7},{6,4},{7,5},{8,10},{9,11},{10,... | collective-permute-start | bytes 1474568 | tf_op jit(solution)/shard_map/ppermute | solution.py:68
  199.3 33.2 %collective-permute-start.23 = (bf16[160,1536]{1,0:T(8,128)(2,1)S(1)}, bf16[160,1536]{1,0:T(8,128)(2,1)}, u32[]{:S(2)}, u32[]{:S(2)}) collective-permute-start(bf16[160,1536]{1,0:T(8,128)(2,1)S(1)} %multiply_convert_fusion), channel_id=1, source_target_pairs={{0,3},{1,0},{2,1},{3,2},{4,7},{5,4},{6,5},{7,6},{8,11},{9,8},{10,9... | collective-permute-start | bytes 1474568 | tf_op jit(solution)/shard_map/ppermute | solution.py:68
  283.3 33.0 %collective-permute-start.24 = (bf16[2,2,4,48,2240]{4,3,2,1,0:T(8,128)(2,1)}, bf16[2,2,4,48,2240]{4,3,2,1,0:T(8,128)(2,1)}, u32[]{:S(2)}, u32[]{:S(2)}) collective-permute-start(bf16[2,2,4,48,2240]{4,3,2,1,0:T(8,128)(2,1)} %bitcast.229), channel_id=1, source_target_pairs={{0,4},{4,0},{8,12},{12,8},{16,20},{20,16},{24,28},{28,24},{1,5},{5... | collective-permute-start | bytes 10321928 | tf_op jit(solution)/shard_map/ppermute | solution.py:68
  320.0 25.6 %collective-permute-start.27 = (bf16[2,4,48,2240]{3,2,1,0:T(8,128)(2,1)}, bf16[2,4,48,2240]{3,2,1,0:T(8,128)(2,1)}, u32[]{:S(2)}, u32[]{:S(2)}) collective-permute-start(bf16[2,4,48,2240]{3,2,1,0:T(8,128)(2,1)} %fusion), channel_id=1, source_target_pairs={{0,8},{4,20},{8,0},{12,28},{16,24},{20,4},{24,16},{28,12},{1,9},{5... | collective-permute-start | bytes 5160968 | tf_op jit(solution)/shard_map/ppermute | solution.py:68
  320.0 24.8 %collective-permute-start.28 = (bf16[160,1536]{1,0:T(8,128)(2,1)S(1)}, bf16[160,1536]{1,0:T(8,128)(2,1)S(1)}, u32[]{:S(2)}, u32[]{:S(2)}) collective-permute-start(bf16[160,1536]{1,0:T(8,128)(2,1)S(1)} %copy-done.40), channel_id=1, source_target_pairs={{0,2},{1,3},{2,0},{3,1},{4,6},{5,7},{6,4},{7,5},{8,10},{9,11},{10,... | collective-permute-start | bytes 1474568 | tf_op jit(solution)/shard_map/ppermute | solution.py:68
  369.9 44.9 %collective-permute-start.33 = (bf16[2,2,4,48,1536]{4,3,2,1,0:T(8,128)(2,1)}, bf16[2,2,4,48,1536]{4,3,2,1,0:T(8,128)(2,1)}, u32[]{:S(2)}, u32[]{:S(2)}) collective-permute-start(bf16[2,2,4,48,1536]{4,3,2,1,0:T(8,128)(2,1)} %bitcast.231), channel_id=1, source_target_pairs={{0,4},{4,0},{8,12},{12,8},{16,20},{20,16},{24,28},{28,24},{1,5},{5... | collective-permute-start | bytes 7077896 | tf_op jit(solution)/shard_map/ppermute | solution.py:68
  374.4 48.1 %all-to-all-start = ((bf16[4,48,2240]{2,1,0:T(8,128)(2,1)}), bf16[4,48,2240]{2,1,0:T(8,128)(2,1)S(1)}, u32[]{:S(2)}, u32[]{:S(2)}) async-start(bf16[4,48,2240]{2,1,0:T(8,128)(2,1)} %fusion.2), calls=%async_computation.1 | async-start | bytes 1769472 | tf_op jit(solution)/shard_map/all_to_all | solution.py:949
  422.5 30.7 %collective-permute-start.34 = (bf16[2,2,4,48,2048]{4,3,2,1,0:T(8,128)(2,1)}, bf16[2,2,4,48,2048]{4,3,2,1,0:T(8,128)(2,1)}, u32[]{:S(2)}, u32[]{:S(2)}) collective-permute-start(bf16[2,2,4,48,2048]{4,3,2,1,0:T(8,128)(2,1)} %bitcast.230), channel_id=1, source_target_pairs={{0,4},{4,0},{8,12},{12,8},{16,20},{20,16},{24,28},{28,24},{1,5},{5... | collective-permute-start | bytes 9437192 | tf_op jit(solution)/shard_map/ppermute | solution.py:68
  427.9 25.3 %collective-permute-start.35 = (bf16[2,4,48,1536]{3,2,1,0:T(8,128)(2,1)}, bf16[2,4,48,1536]{3,2,1,0:T(8,128)(2,1)}, u32[]{:S(2)}, u32[]{:S(2)}) collective-permute-start(bf16[2,4,48,1536]{3,2,1,0:T(8,128)(2,1)} %fusion.12), channel_id=1, source_target_pairs={{0,8},{4,20},{8,0},{12,28},{16,24},{20,4},{24,16},{28,12},{1,9},{5... | collective-permute-start | bytes 3538952 | tf_op jit(solution)/shard_map/ppermute | solution.py:68
  436.4 26.9 %all-to-all-start.1 = ((bf16[4,48,2240]{2,1,0:T(8,128)(2,1)}), bf16[4,48,2240]{2,1,0:T(8,128)(2,1)}, u32[]{:S(2)}, u32[]{:S(2)}) async-start(bf16[4,48,2240]{2,1,0:T(8,128)(2,1)} %bitcast.213), calls=%async_computation.2 | async-start | bytes 1769472 | tf_op jit(solution)/shard_map/all_to_all | solution.py:949
  440.7 147.8 %reduce-scatter.5.cloned.1.call-start = ((), (), s32[]{:S(2)}) async-start(), calls=%async_computation.9 | async-start | bytes 7741440 | tf_op jit(solution)/shard_map/reduce_scatter | solution.py:937
  463.3 53.3 %collective-permute-start.37 = (bf16[2,4,48,2048]{3,2,1,0:T(8,128)(2,1)}, bf16[2,4,48,2048]{3,2,1,0:T(8,128)(2,1)}, u32[]{:S(2)}, u32[]{:S(2)}) collective-permute-start(bf16[2,4,48,2048]{3,2,1,0:T(8,128)(2,1)} %fusion.4), channel_id=1, source_target_pairs={{0,8},{4,20},{8,0},{12,28},{16,24},{20,4},{24,16},{28,12},{1,9},{5... | collective-permute-start | bytes 4718600 | tf_op jit(solution)/shard_map/ppermute | solution.py:68
  467.3 28.2 %collective-permute-start.38 = (bf16[4,48,1536]{2,1,0:T(8,128)(2,1)}, bf16[4,48,1536]{2,1,0:T(8,128)(2,1)S(1)}, u32[]{:S(2)}, u32[]{:S(2)}) collective-permute-start(bf16[4,48,1536]{2,1,0:T(8,128)(2,1)} %fusion.15), channel_id=1, source_target_pairs={{0,16},{4,12},{8,24},{12,4},{16,0},{20,28},{24,8},{28,20},{1,17},{... | collective-permute-start | bytes 1769480 | tf_op jit(solution)/shard_map/ppermute | solution.py:68
  468.6 47.4 %collective-permute-start.39 = (bf16[48,8960]{1,0:T(8,128)(2,1)S(1)}, bf16[48,8960]{1,0:T(8,128)(2,1)S(1)}, u32[]{:S(2)}, u32[]{:S(2)}) collective-permute-start(bf16[48,8960]{1,0:T(8,128)(2,1)S(1)} %concatenate.71), channel_id=1, source_target_pairs={{0,16},{4,12},{8,24},{12,4},{16,0},{20,28},{24,8},{28,20},{1,17},{... | collective-permute-start | bytes 2580488 | tf_op jit(solution)/shard_map/ppermute | solution.py:68
  519.5 35.0 %collective-permute-start.41 = (bf16[2,48,8960]{2,1,0:T(8,128)(2,1)}, bf16[2,48,8960]{2,1,0:T(8,128)(2,1)}, u32[]{:S(2)}, u32[]{:S(2)}) collective-permute-start(bf16[2,48,8960]{2,1,0:T(8,128)(2,1)} %pad_maximum_fusion.5), channel_id=1, source_target_pairs={{0,8},{4,20},{8,0},{12,28},{16,24},{20,4},{24,16},{28,12},{1,9},{5... | collective-permute-start | bytes 5160968 | tf_op jit(solution)/shard_map/ppermute | solution.py:68
  525.9 28.6 %all-to-all-start.2 = ((bf16[4,48,1536]{2,1,0:T(8,128)(2,1)}), bf16[4,48,1536]{2,1,0:T(8,128)(2,1)S(1)}, u32[]{:S(2)}, u32[]{:S(2)}) async-start(bf16[4,48,1536]{2,1,0:T(8,128)(2,1)} %fusion.14), calls=%async_computation.3 | async-start | bytes 1179648 | tf_op jit(solution)/shard_map/all_to_all | solution.py:949
  561.8 24.0 %collective-permute-start.45 = (bf16[4,48,8960]{2,1,0:T(8,128)(2,1)}, bf16[4,48,8960]{2,1,0:T(8,128)(2,1)}, u32[]{:S(2)}, u32[]{:S(2)}) collective-permute-start(bf16[4,48,8960]{2,1,0:T(8,128)(2,1)} %pad_maximum_fusion.pieces_ref), channel_id=1, source_target_pairs={{0,4},{4,0},{8,12},{12,8},{16,20},{20,16},{24,28},{28,24},{1,5},{5... | collective-permute-start | bytes 10321928 | tf_op jit(solution)/shard_map/ppermute | solution.py:68
  563.1 25.4 %all-to-all-start.3 = ((bf16[4,48,2048]{2,1,0:T(8,128)(2,1)}), bf16[4,48,2048]{2,1,0:T(8,128)(2,1)}, u32[]{:S(2)}, u32[]{:S(2)}) async-start(bf16[4,48,2048]{2,1,0:T(8,128)(2,1)} %fusion.6), calls=%async_computation.4 | async-start | bytes 1572864 | tf_op jit(solution)/shard_map/all_to_all | solution.py:949
  567.7 78.5 %all-gather.7.cloned.1.call-start = ((), (), s32[]{:S(2)}) async-start(), calls=%async_computation.10 | async-start | bytes 7741440 | tf_op jit(solution)/shard_map/all_gather | solution.py:1076
  622.4 34.6 %collective-permute-start.55 = (bf16[4,48,2048]{2,1,0:T(8,128)(2,1)S(1)}, bf16[4,48,2048]{2,1,0:T(8,128)(2,1)}, u32[]{:S(2)}, u32[]{:S(2)}) collective-permute-start(bf16[4,48,2048]{2,1,0:T(8,128)(2,1)S(1)} %pad_maximum_fusion.8.pieces_ref), channel_id=1, source_target_pairs={{0,4},{4,0},{8,12},{12,8},{16,20},{20,16},{24,28},{28,24},{1,5},{5... | collective-permute-start | bytes 2359304 | tf_op jit(solution)/shard_map/ppermute | solution.py:68
  622.4 33.8 %collective-permute-start.56 = (bf16[160,1536]{1,0:T(8,128)(2,1)}, bf16[160,1536]{1,0:T(8,128)(2,1)S(1)}, u32[]{:S(2)}, u32[]{:S(2)}) collective-permute-start(bf16[160,1536]{1,0:T(8,128)(2,1)} %get-tuple-element.800), channel_id=1, source_target_pairs={{0,2},{1,3},{2,0},{3,1},{4,6},{5,7},{6,4},{7,5},{8,10},{9,11},{10,... | collective-permute-start | bytes 1474568 | tf_op jit(solution)/shard_map/ppermute | solution.py:68
  (80 other events, 1248.6 us)
Sparse Core Ops, SparseCore 0:
  11.5 101.3 all-gather.8
  115.3 75.1 all-gather.4
  316.4 70.4 reduce-scatter.2
  445.6 86.2 reduce-scatter.4
  588.6 46.7 all-gather.6

commit v13 on v10

--- a/solution.py
+++ b/solution.py
@@ -945,9 +945,6 @@
     edges = sorted({0, shards - 2})
     inside = list(range(1, shards - 2))
 
-    up_halves = split_halves(turned_normed, d_up, shards, True)
-
-    up = Halving(clock, *up_halves, core, first, second)
     normed_own, *normed_partial = clock.run(
         lambda *operands: rows_product(operands[:2], operands[2:], True, shards),
         d_gate,
@@ -955,32 +952,28 @@
         gate_matrix,
         up_matrix,
     )
-    (up_arrived,) = clock.wait(up.moving)
-
-    up.along_first(up_arrived)
+    up_halves = split_halves(turned_normed, d_up, shards, True)
+
+    up = Halving(clock, *up_halves, core, first, second)
     normed_moving = send_some(normed_partial, edges)
     (gate_blocks,) = clock.run(
         lambda left, right: ordered_gradient(left, right, shards, rep_places(reps)),
         turned_normed,
         d_gate,
     )
-    gate_piece = sum_over_rep(gate_blocks.reshape(width, block_units))
+    up_arrived, normed_arrived = clock.wait(up.moving, normed_moving)
+    gate_piece = sum_over_rep(clock(gate_blocks)[0].reshape(width, block_units))
+
+    up.along_first(up_arrived)
+    normed_moving = send_some(normed_partial, inside)
     (down_blocks,) = clock.run(
         lambda left, right: ordered_gradient(left, right, 1, list(range(reps))),
         turned_inner,
         cotangents,
     )
-    up_arrived, normed_arrived = clock.wait(up.moving, normed_moving)
+    up_arrived, more_arrived = clock.wait(up.moving, normed_moving)
 
     up.along_second(up_arrived)
-    normed_moving = send_some(normed_partial, inside)
-    block_own, *block_partial = clock.run(
-        lambda left, right: rows_product((left,), (right,), False, shards), inner_act, down_weight
-    )
-    up_arrived, more_arrived = clock.wait(up.moving, normed_moving)
-
-    up_blocks = clock(*blocks_of(up.finish(up_arrived)))
-    up_moving = send_blocks(up_blocks)
     normed_two_gradient = total_of([normed_own] + normed_arrived + more_arrived)
     gain_two_gradient = jnp.sum(normed_two_gradient * unit_two, axis=0)
     hidden_gradient = output_cotangent.astype(f32) + norm_back(
@@ -999,16 +992,20 @@
         key_marks.T,
     )
     output_halves = split_halves(attention_low, branch_gradient, shards, False)
-    (up_rows,) = clock.wait(up_moving)
+    (up_arrived,) = clock.wait(up.moving)
 
     pair_moving = send_back(pair_partial)
     output = Halving(clock, *output_halves, core, first, second)
-    up_piece = side_by_side(up_blocks[:1] + up_rows)
+    up_blocks = clock(*blocks_of(up.finish(up_arrived)))
+    block_own, *block_partial = clock.run(
+        lambda left, right: rows_product((left,), (right,), False, shards), inner_act, down_weight
+    )
     pair_arrived, output_arrived = clock.wait(pair_moving, output.moving)
 
-    up_spread = spread(up_piece)
+    (gate_piece,) = clock(gate_piece)
+    down_piece = sum_over_rep(clock(down_blocks)[0].reshape(block_units, width))
     output.along_first(output_arrived)
-    block_moving = send_some(block_partial, inside)
+    up_moving = send_blocks(up_blocks)
     projected_gradient, bias_sum = clock.run(
         lambda *operands: join_projected(operands[0], operands[3:], *operands[1:3]),
         d_queries,
@@ -1018,16 +1015,12 @@
         *pair_arrived,
     )
     projected_halves = split_halves(normed_one, projected_gradient, shards, False)
-    up_arrived, output_arrived, block_arrived = clock.wait(
-        up_spread.moving, output.moving, block_moving
-    )
+    output_arrived, up_rows = clock.wait(output.moving, up_moving)
 
     projected = Halving(clock, *projected_halves, core, first, second)
     output.along_second(output_arrived)
-    up_spread.along(up_arrived)
-    block_moving = send_some(block_partial, edges)
-    (gate_piece,) = clock(gate_piece)
-    down_piece = sum_over_rep(clock(down_blocks)[0].reshape(block_units, width))
+    up_spread = spread(side_by_side(up_blocks[:1] + up_rows))
+    block_moving = send_some(block_partial, inside)
     projected_gradient, hidden_gradient = clock(projected_gradient, hidden_gradient)
     normed_one_gradient = times_transposed(projected_gradient, input_matrix)
     gain_one_gradient = jnp.sum(normed_one_gradient * unit_one, axis=0)
@@ -1036,16 +1029,15 @@
             hidden_gradient + norm_back(normed_one_gradient, unit_one, inverse_one, gain_one)
         ).astype(bf16)
     )
-    projected_arrived, output_arrived, more_arrived = clock.wait(
-        projected.moving, output.moving, block_moving
-    )
-    block_arrived = block_arrived + more_arrived
+    projected_arrived, output_arrived, up_arrived, block_arrived = clock.wait(
+        projected.moving, output.moving, up_spread.moving, block_moving
+    )
 
     projected.along_first(projected_arrived)
+    up_spread.along(up_arrived)
     gate_blocks = clock(*blocks_of(gate_piece.reshape(shards, part_rows, block_units)))
     gate_moving = send_blocks(gate_blocks)
     output_blocks = clock(*blocks_of(output.finish(output_arrived)))
-    (block_out,) = clock(total_of([hidden, block_own] + block_arrived).astype(bf16))
     bias_gradient = bias_sum[0]
     bias_split = query_width + pair_width
     small_parts = (
@@ -1072,6 +1064,8 @@
     input_moving = send_blocks(input_blocks)
     gate_spread.along(gate_arrived)
     output_spread = spread(row_sum(output_blocks[:1], output_rows))
+    (down_piece,) = clock(down_piece)
+    down_gathered = lax.all_gather(down_piece, "rep", axis=0, tiled=True)
     input_rows, gate_arrived, output_arrived = clock.wait(
         input_moving, gate_spread.moving, output_spread.moving
     )
@@ -1081,8 +1075,6 @@
     up_spread.over(up_arrived)
     gate_spread.over(gate_arrived)
     small_moving = clock.send(core, [small], [1])
-    (down_piece,) = clock(down_piece)
-    down_gathered = lax.all_gather(down_piece, "rep", axis=0, tiled=True)
     input_arrived, output_arrived, up_arrived, gate_arrived, small_arrived = clock.wait(
         input_spread.moving, output_spread.moving, up_spread.moving, gate_spread.moving, small_moving
     )
@@ -1091,25 +1083,32 @@
     input_spread.along(input_arrived)
     output_spread.over(output_arrived)
     small_moving = clock.send(first, [small] * (first.size - 1), range(1, first.size))
+    block_moving = send_some(block_partial, edges[:1])
     (up_total,) = clock.run(widen_pieces, *up_spread.finish(up_arrived))
-    input_arrived, output_arrived, small_arrived = clock.wait(
-        input_spread.moving, output_spread.moving, small_moving
+    input_arrived, output_arrived, small_arrived, more_arrived = clock.wait(
+        input_spread.moving, output_spread.moving, small_moving, block_moving
     )
     small = total_of([small] + small_arrived)
+    block_arrived = block_arrived + more_arrived
 
     input_spread.over(input_arrived)
     small_moving = clock.send(second, [small] * (second.size - 1), range(1, second.size))
+    block_moving = send_some(block_partial, edges[1:])
     (gate_total,) = clock.run(widen_pieces, *gate_spread.finish(gate_arrived))
-    input_arrived, small_arrived = clock.wait(input_spread.moving, small_moving)
+    input_arrived, small_arrived, more_arrived = clock.wait(
+        input_spread.moving, small_moving, block_moving
+    )
+    block_arrived = block_arrived + more_arrived
     small_blocks = clock(*blocks_of(total_of([small] + small_arrived)))
 
     small_moving = send_blocks(small_blocks)
     (output_total,) = clock.run(widen_pieces, *output_spread.finish(output_arrived))
     (input_total,) = clock.run(widen_pieces, *input_spread.finish(input_arrived))
+    (down_gathered,) = clock(down_gathered)
+    (down_total,) = clock(down_gathered.astype(f32))
+    (block_out,) = clock(total_of([hidden, block_own] + block_arrived).astype(bf16))
     (small_arrived,) = clock.wait(small_moving)
     small = total_of(small_blocks[:1] + small_arrived)
-    (down_gathered,) = clock(down_gathered)
-    (down_total,) = clock(down_gathered.astype(f32))
 
     small = small + clock.token[0, 0]
     small_totals, at = [], 0

time: 632 us -> 652 us (1.032)
  waiting for transfers between devices: 225 us -> 247 us
    ppermute x66, waiting for transfers between devices: 210 us -> 238 us  [shift(): return lax.ppermute(value, self.name, self.pairs(step % self.size))]
    unnamed x97 -> x121, local copies, waits for them, and re-layouts: 11.9 us -> 14.4 us
  transfers between devices with their start and end apart: 77 -> 77, of which waited for: 35 -> 32; matrix products, arithmetic and copies ran while one was open for 14% -> 15% of each run, Pallas kernels for 18% -> 15%
where the time goes in v13:
time: 652 us; the launch traced here: 643 us
  waiting for transfers between devices  247 us (38%)
  Pallas kernels  143 us (22%)
  starting transfers between devices  129 us (20%)
  other arithmetic  62.3 us (10%)
  local copies, waits for them, and re-layouts  28.9 us (4%)
  matrix products  16.6 us (3%)
  between operations  15.4 us (2%)
    ppermute x66, waiting for transfers between devices, shift(): return lax.ppermute(value, self.name, self.pairs(step % self.size))  238 us
    ppermute x66, starting transfers between devices, shift(): return lax.ppermute(value, self.name, self.pairs(step % self.size))  103 us
    ppermute x6, starting transfers between devices, pass_on(): return lax.ppermute(value, self.name, pairs)  25.3 us
    pallas_call x1, Pallas kernels, feed_forward(): pl.pallas_call(body, grid=(steps,), out_shape=[jax.ShapeDtypeStruct((coun...  23.6 us
    pallas_call x2, Pallas kernels, rows_product(): pl.pallas_call(body, grid=(pl.cdiv(columns, TILE),), out_shape=[jax.Shape...  23.2 us
    pallas_call x4, Pallas kernels, widen_pieces(): pl.pallas_call(body, out_shape=jax.ShapeDtypeStruct((reps, rows, columns)...  21.1 us
    pallas_call x3, Pallas kernels, split_gradient(): pl.pallas_call(body, grid=(pl.cdiv(columns, TILE),), out_shape=[jax.Shape...  20.2 us
    pallas_call x2, Pallas kernels, ordered_gradient(): pl.pallas_call(body, grid=(pl.cdiv(columns, TILE),), out_shape=[jax.Shape...  19.8 us
  transfers between devices with their start and end apart: 77, of which 32 were waited for; matrix products, arithmetic and copies ran while one was open for 15% of the time, Pallas kernels for 15%

profile of v13, /device:TPU:0, one launch (start us, length us, event | category | flops | bytes accessed | tf_op | source)
XLA Modules:
  0.0 642.7 jit_solution(15878840243611940886)
XLA Ops:
  32.1 6.5 %collective-permute-start.4 = (bf16[48,2240]{1,0:T(8,128)(2,1)}, bf16[48,2240]{1,0:T(8,128)(2,1)S(1)}, u32[]{:S(2)}, u32[]{:S(2)}) collective-permute-start(bf16[48,2240]{1,0:T(8,128)(2,1)} %get-tuple-element.484), channel_id=1, source_target_pairs={{0,1},{1,2},{2,3},{3,0},{4,5},{5,6},{6,7},{7,4},{8,9},{9,10},{10,1... | collective-permute-start | bytes 645128 | tf_op jit(solution)/shard_map/ppermute | solution.py:68
  41.1 6.3 collective-permute-done.4
  47.4 13.9 %collective-permute-done.5 = bf16[48,2240]{1,0:T(8,128)(2,1)S(1)} collective-permute-done((bf16[48,2240]{1,0:T(8,128)(2,1)}, bf16[48,2240]{1,0:T(8,128)(2,1)S(1)}, u32[]{:S(2)}, u32[]{:S(2)}) %collective-permute-start.5) | collective-permute-done | bytes 215072 | tf_op jit(solution)/shard_map/ppermute | solution.py:68
  63.8 5.8 collective-permute-start.8
  72.9 7.4 %collective-permute-done.8 = bf16[48,2240]{1,0:T(8,128)(2,1)S(1)} collective-permute-done((bf16[48,2240]{1,0:T(8,128)(2,1)S(1)}, bf16[48,2240]{1,0:T(8,128)(2,1)S(1)}, u32[]{:S(2)}, u32[]{:S(2)}) %collective-permute-start.8) | collective-permute-done | bytes 215072 | tf_op jit(solution)/shard_map/ppermute | solution.py:68
  80.3 17.5 %collective-permute-done.9 = bf16[48,2240]{1,0:T(8,128)(2,1)S(1)} collective-permute-done((bf16[48,2240]{1,0:T(8,128)(2,1)S(1)}, bf16[48,2240]{1,0:T(8,128)(2,1)S(1)}, u32[]{:S(2)}, u32[]{:S(2)}) %collective-permute-start.9) | collective-permute-done | bytes 215072 | tf_op jit(solution)/shard_map/ppermute | solution.py:68
  105.4 14.6 %collective-permute-start.11 = (bf16[160,1536]{1,0:T(8,128)(2,1)S(1)}, bf16[160,1536]{1,0:T(8,128)(2,1)}, u32[]{:S(2)}, u32[]{:S(2)}) collective-permute-start(bf16[160,1536]{1,0:T(8,128)(2,1)S(1)} %copy-done.21), channel_id=1, source_target_pairs={{0,1},{1,2},{2,3},{4,5},{5,6},{6,7},{8,9},{9,10},{10,11},{12,13},{... | collective-permute-start | bytes 1474568 | tf_op jit(solution)/shard_map/ppermute | solution.py:73
  146.3 8.7 %collective-permute-done.14 = bf16[160,512]{1,0:T(8,128)(2,1)S(1)} collective-permute-done((bf16[160,512]{1,0:T(8,128)(2,1)S(1)}, bf16[160,512]{1,0:T(8,128)(2,1)S(1)}, u32[]{:S(2)}, u32[]{:S(2)}) %collective-permute-start.14) | collective-permute-done | bytes 163872 | tf_op jit(solution)/shard_map/ppermute | solution.py:68
  155.0 7.9 %collective-permute-done.15 = bf16[160,512]{1,0:T(8,128)(2,1)S(1)} collective-permute-done((bf16[160,512]{1,0:T(8,128)(2,1)S(1)}, bf16[160,512]{1,0:T(8,128)(2,1)S(1)}, u32[]{:S(2)}, u32[]{:S(2)}) %collective-permute-start.15) | collective-permute-done | bytes 163872 | tf_op jit(solution)/shard_map/ppermute | solution.py:68
  174.6 5.7 attention_forward.1
  193.2 11.7 %place_blocks.3 = (bf16[4,8,48,2240]{3,2,1,0:T(8,128)(2,1)}, bf16[4,8,48,2240]{3,2,1,0:T(8,128)(2,1)}) custom-call(s32[4]{0:T(128)} %pad_add_fusion.5.order_ref, bf16[64,48,2240]{2,1,0:T(8,128)(2,1)} %all-gather.5.cloned.1.call-done.source), custom_call_target="tpu_custom_call" | custom-call | flops 1 | bytes 1 | tf_op jit(solution)/shard_map/place_blocks/pallas_call | solution.py:339
  204.9 15.1 %collective-permute-done.22 = bf16[160,1536]{1,0:T(8,128)(2,1)S(1)} collective-permute-done((bf16[160,1536]{1,0:T(8,128)(2,1)S(1)}, bf16[160,1536]{1,0:T(8,128)(2,1)S(1)}, u32[]{:S(2)}, u32[]{:S(2)}) %collective-permute-start.22) | collective-permute-done | bytes 491552 | tf_op jit(solution)/shard_map/ppermute | solution.py:68
  221.4 23.6 %feed_forward.1 = (bf16[640,2240]{1,0:T(8,128)(2,1)}, bf16[640,2240]{1,0:T(8,128)(2,1)}, bf16[640,2240]{1,0:T(8,128)(2,1)}, bf16[1536,640]{1,0:T(8,128)(2,1)}, bf16[2240,640]{1,0:T(8,128)(2,1)}) custom-call(bf16[640,1536]{1,0:T(8,128)(2,1)} %pad_maximum_fusion.3.rows_ref, bf16[640,1536]{1,0:T(8,128)(2,1)} %pad_maximum_fusion.4.cotangents_ref.right_ref, ...), custom_call_target="tpu_custom_call" | custom-call | flops 1 | bytes 1 | tf_op jit(solution)/shard_map/feed_forward/pallas_call | solution.py:477
  245.0 14.6 %rows_product.2 = (bf16[160,1536]{1,0:T(8,128)(2,1)}, bf16[160,1536]{1,0:T(8,128)(2,1)}, bf16[160,1536]{1,0:T(8,128)(2,1)}, bf16[160,1536]{1,0:T(8,128)(2,1)}) custom-call(bf16[640,2240]{1,0:T(8,128)(2,1)} %get-tuple-element.619.refs_0_.right_ref, bf16[640,2240]{1,0:T(8,128)(2,1)} %get-tuple-element.608.refs_1_.right_ref, bf16[1536,2240]{1,0:T(8,128)(2,1)} %bitcast.183, ...), custom_call_target="tpu_custom_call" | custom-call | flops 1 | bytes 1 | tf_op jit(solution)/shard_map/rows_product/pallas_call | solution.py:603
  259.7 10.1 %split_gradient.3 = (bf16[4,4,48,2240]{3,2,1,0:T(8,128)(2,1)}, bf16[4,4,48,2240]{3,2,1,0:T(8,128)(2,1)}) custom-call(s32[1]{0:T(128)} %bitcast.46.core_ref, bf16[1536,640]{1,0:T(8,128)(2,1)} %get-tuple-element.618.left_ref, bf16[640,2240]{1,0:T(8,128)(2,1)} %get-tuple-element.608.refs_1_.right_ref), custom_call_target="tpu_custom_call" | custom-call | flops 1 | bytes 1 | tf_op jit(solution)/shard_map/split_gradient/pallas_call | solution.py:533
  269.7 11.8 %collective-permute-start.25 = (bf16[160,1536]{1,0:T(8,128)(2,1)S(1)}, bf16[160,1536]{1,0:T(8,128)(2,1)S(1)}, u32[]{:S(2)}, u32[]{:S(2)}) collective-permute-start(bf16[160,1536]{1,0:T(8,128)(2,1)S(1)} %copy-done.49), channel_id=1, source_target_pairs={{0,3},{1,0},{2,1},{3,2},{4,7},{5,4},{6,5},{7,6},{8,11},{9,8},{10,9... | collective-permute-start | bytes 1474568 | tf_op jit(solution)/shard_map/ppermute | solution.py:68
  281.5 9.9 %ordered_gradient.2 = bf16[8,4,48,2240]{3,2,1,0:T(8,128)(2,1)} custom-call(bf16[1536,640]{1,0:T(8,128)(2,1)} %get-tuple-element.618.left_ref, bf16[640,2240]{1,0:T(8,128)(2,1)} %get-tuple-element.619.refs_0_.right_ref), custom_call_target="tpu_custom_call" | custom-call | flops 1 | bytes 1 | tf_op jit(solution)/shard_map/ordered_gradient/pallas_call | solution.py:563
  293.1 10.9 %collective-permute-done.26 = bf16[160,1536]{1,0:T(8,128)(2,1)S(1)} collective-permute-done((bf16[160,1536]{1,0:T(8,128)(2,1)S(1)}, bf16[160,1536]{1,0:T(8,128)(2,1)S(1)}, u32[]{:S(2)}, u32[]{:S(2)}) %collective-permute-start.26) | collective-permute-done | bytes 491552 | tf_op jit(solution)/shard_map/ppermute | solution.py:68
  311.2 9.8 %ordered_gradient.3 = bf16[8,1,280,1536]{3,2,1,0:T(8,128)(2,1)} custom-call(bf16[2240,640]{1,0:T(8,128)(2,1)} %get-tuple-element.634.left_ref, bf16[640,1536]{1,0:T(8,128)(2,1)} %pad_maximum_fusion.4.cotangents_ref.right_ref), custom_call_target="tpu_custom_call" | custom-call | flops 1 | bytes 1 | tf_op jit(solution)/shard_map/ordered_gradient/pallas_call | solution.py:563
  321.0 12.0 %collective-permute-done.28 = bf16[160,1536]{1,0:T(8,128)(2,1)S(1)} collective-permute-done((bf16[160,1536]{1,0:T(8,128)(2,1)S(1)}, bf16[160,1536]{1,0:T(8,128)(2,1)S(1)}, u32[]{:S(2)}, u32[]{:S(2)}) %collective-permute-start.28) | collective-permute-done | bytes 491552 | tf_op jit(solution)/shard_map/ppermute | solution.py:68
  343.0 7.6 %attention_backward.1 = (bf16[160,1536]{1,0:T(8,128)(2,1)}, bf16[160,512]{1,0:T(8,128)(2,1)}, bf16[160,512]{1,0:T(8,128)(2,1)}, bf16[160,512]{1,0:T(8,128)(2,1)}, bf16[160,512]{1,0:T(8,128)(2,1)}) custom-call(bf16[2,960,128]{2,1,0:T(8,128)(2,1)} %get-tuple-element.652.queries_ref, bf16[160,1536]{1,0:T(8,128)(2,1)} %convolution_convert_fusion.gradient_ref, ...), custom_call_target="tpu_custom_call" | custom-call | flops 1 | bytes 1 | tf_op jit(solution)/shard_map/attention_backward/pallas_call | solution.py:705
  366.1 8.6 %rows_product.3 = (bf16[160,1536]{1,0:T(8,128)(2,1)}, bf16[160,1536]{1,0:T(8,128)(2,1)}, bf16[160,1536]{1,0:T(8,128)(2,1)}, bf16[160,1536]{1,0:T(8,128)(2,1)}) custom-call(bf16[640,2240]{1,0:T(8,128)(2,1)} %get-tuple-element.685.refs_0_, bf16[2240,1536]{1,0:T(8,128)(2,1)} %refs_1_), custom_call_target="tpu_custom_call" | custom-call | flops 1 | bytes 1 | tf_op jit(solution)/shard_map/rows_product/pallas_call | solution.py:603
  409.2 6.7 %fusion.22 = (f32[1536]{0:T(1024)S(1)}, f32[160]{0:T(256)S(1)}, f32[160,1536]{1,0:T(8,128)S(1)}) fusion(bf16[160,1536]{1,0:T(8,128)(2,1)S(1)} %copy-done.4, f32[160]{0:T(256)S(1)} %copy-done.40, f32[1536]{0:T(1024)S(1)} %reshape.278, bf16[160,2048]{1,0:T(8,128)(2,1)} %get-tuple-element.749.right_ref, bf16[1536,2048]{1,0:T(8,128)(2,1)} %bitcast.189), kind=kOutput, calls=%fused_computation.44 | convolution fusion | flops 1008351616 | bytes 8434944 | tf_op jit(solution)/shard_map/dot_general | solution.py:52
  420.3 20.7 %collective-permute-done.41 = bf16[160,1536]{1,0:T(8,128)(2,1)S(1)} collective-permute-done((bf16[160,1536]{1,0:T(8,128)(2,1)S(1)}, bf16[160,1536]{1,0:T(8,128)(2,1)S(1)}, u32[]{:S(2)}, u32[]{:S(2)}) %collective-permute-start.41) | collective-permute-done | bytes 491552 | tf_op jit(solution)/shard_map/ppermute | solution.py:68
  463.8 7.8 %collective-permute-done.45 = bf16[48,2240]{1,0:T(8,128)(2,1)S(1)} collective-permute-done((bf16[48,2240]{1,0:T(8,128)(2,1)S(1)}, bf16[48,2240]{1,0:T(8,128)(2,1)S(1)}, u32[]{:S(2)}, u32[]{:S(2)}) %collective-permute-start.45) | collective-permute-done | bytes 215072 | tf_op jit(solution)/shard_map/ppermute | solution.py:68
  471.6 22.9 %collective-permute-done.42 = bf16[2,4,48,2048]{3,2,1,0:T(8,128)(2,1)} collective-permute-done((bf16[2,4,48,2048]{3,2,1,0:T(8,128)(2,1)}, bf16[2,4,48,2048]{3,2,1,0:T(8,128)(2,1)}, u32[]{:S(2)}, u32[]{:S(2)}) %collective-permute-start.42) | collective-permute-done | bytes 1572896 | tf_op jit(solution)/shard_map/ppermute | solution.py:68
  542.5 17.4 %collective-permute-done.55 = bf16[2,48,8960]{2,1,0:T(8,128)(2,1)S(1)} collective-permute-done((bf16[2,48,8960]{2,1,0:T(8,128)(2,1)}, bf16[2,48,8960]{2,1,0:T(8,128)(2,1)S(1)}, u32[]{:S(2)}, u32[]{:S(2)}) %collective-permute-start.55) | collective-permute-done | bytes 1720352 | tf_op jit(solution)/shard_map/ppermute | solution.py:68
  562.6 9.6 %collective-permute-done.61 = f32[4,1280]{1,0:T(4,128)S(1)} collective-permute-done((f32[4,1280]{1,0:T(4,128)S(1)}, f32[4,1280]{1,0:T(4,128)S(1)}, u32[]{:S(2)}, u32[]{:S(2)}) %collective-permute-start.61) | collective-permute-done | bytes 20512 | tf_op jit(solution)/shard_map/ppermute | solution.py:68
  585.2 7.3 %widen_pieces.4 = f32[8,48,8960]{2,1,0:T(8,128)} custom-call(s32[8]{0:T(128)} %stack.239.places_ref, bf16[4,48,8960]{2,1,0:T(8,128)(2,1)} %copy-done.3, bf16[4,48,8960]{2,1,0:T(8,128)(2,1)} %copy-done.9), custom_call_target="tpu_custom_call" | custom-call | flops 1 | bytes 1 | tf_op jit(solution)/shard_map/widen_pieces/pallas_call | solution.py:415
  596.9 7.3 %widen_pieces.5 = f32[8,48,8960]{2,1,0:T(8,128)} custom-call(s32[8]{0:T(128)} %stack.239.places_ref, bf16[4,48,8960]{2,1,0:T(8,128)(2,1)} %copy-done.2, bf16[4,48,8960]{2,1,0:T(8,128)(2,1)} %copy-done.8), custom_call_target="tpu_custom_call" | custom-call | flops 1 | bytes 1 | tf_op jit(solution)/shard_map/widen_pieces/pallas_call | solution.py:415
  604.2 6.9 %collective-permute-done.68 = bf16[160,1536]{1,0:T(8,128)(2,1)S(1)} collective-permute-done((bf16[160,1536]{1,0:T(8,128)(2,1)S(1)}, bf16[160,1536]{1,0:T(8,128)(2,1)S(1)}, u32[]{:S(2)}, u32[]{:S(2)}) %collective-permute-start.68) | collective-permute-done | bytes 491552 | tf_op jit(solution)/shard_map/ppermute | solution.py:68
  622.8 10.2 %convert_element_type.347 = f32[2240,1536]{1,0:T(8,128)} convert(bf16[2240,1536]{1,0:T(8,128)(2,1)} %all-gather.7.cloned.1.call-done) | non-fusion elementwise | flops 3440640 | bytes 20643840 | tf_op jit(solution)/shard_map/convert_element_type | solution.py:1108
  (393 shorter events, 270.4 us)
Async XLA Ops:
  7.2 114.1 %all-gather.9.cloned.1.call-start = ((), (), s32[]{:S(2)}) async-start(), calls=%async_computation.6 | async-start | bytes 6488064 | tf_op jit(solution)/shard_map/all_gather | solution.py:796
  9.3 183.9 %all-gather.5.cloned.1.call-start = ((), (), s32[]{:S(2)}) async-start(), calls=%async_computation.2 | async-start | bytes 15925248 | tf_op jit(solution)/shard_map/all_gather | solution.py:861
  29.9 31.5 %collective-permute-start.3 = (bf16[1,4,48,1536]{3,2,1,0:T(8,128)(2,1)S(1)}, bf16[1,4,48,1536]{3,2,1,0:T(8,128)(2,1)S(1)}, u32[]{:S(2)}, u32[]{:S(2)}) collective-permute-start(bf16[1,4,48,1536]{3,2,1,0:T(8,128)(2,1)S(1)} %get-tuple-element.483), channel_id=1, source_target_pairs={{0,16},{4,12},{8,24},{12,4},{16,0},{20,28},{24,8},{28,20},{1,17},{... | collective-permute-start | bytes 1769480 | tf_op jit(solution)/shard_map/ppermute | solution.py:68
  38.6 22.8 %collective-permute-start.5 = (bf16[48,2240]{1,0:T(8,128)(2,1)}, bf16[48,2240]{1,0:T(8,128)(2,1)S(1)}, u32[]{:S(2)}, u32[]{:S(2)}) collective-permute-start(bf16[48,2240]{1,0:T(8,128)(2,1)} %get-tuple-element.485), channel_id=1, source_target_pairs={{0,2},{1,3},{2,0},{3,1},{4,6},{5,7},{6,4},{7,5},{8,10},{9,11},{10,... | collective-permute-start | bytes 645128 | tf_op jit(solution)/shard_map/ppermute | solution.py:68
  61.5 36.4 %collective-permute-start.7 = (bf16[2,1,4,48,1536]{4,3,2,1,0:T(8,128)(2,1)S(1)}, bf16[2,1,4,48,1536]{4,3,2,1,0:T(8,128)(2,1)S(1)}, u32[]{:S(2)}, u32[]{:S(2)}) collective-permute-start(bf16[2,1,4,48,1536]{4,3,2,1,0:T(8,128)(2,1)S(1)} %pad_maximum_fusion.7), channel_id=1, source_target_pairs={{0,8},{4,20},{8,0},{12,28},{16,24},{20,4},{24,16},{28,12},{1,9},{5... | collective-permute-start | bytes 3538952 | tf_op jit(solution)/shard_map/ppermute | solution.py:68
  69.5 28.3 %collective-permute-start.9 = (bf16[48,2240]{1,0:T(8,128)(2,1)S(1)}, bf16[48,2240]{1,0:T(8,128)(2,1)S(1)}, u32[]{:S(2)}, u32[]{:S(2)}) collective-permute-start(bf16[48,2240]{1,0:T(8,128)(2,1)S(1)} %get-tuple-element.494), channel_id=1, source_target_pairs={{0,2},{1,3},{2,0},{3,1},{4,6},{5,7},{6,4},{7,5},{8,10},{9,11},{10,... | collective-permute-start | bytes 645128 | tf_op jit(solution)/shard_map/ppermute | solution.py:68
  72.2 25.6 %collective-permute-start.10 = (bf16[48,2240]{1,0:T(8,128)(2,1)S(1)}, bf16[48,2240]{1,0:T(8,128)(2,1)S(1)}, u32[]{:S(2)}, u32[]{:S(2)}) collective-permute-start(bf16[48,2240]{1,0:T(8,128)(2,1)S(1)} %get-tuple-element.495), channel_id=1, source_target_pairs={{0,3},{1,0},{2,1},{3,2},{4,7},{5,4},{6,5},{7,6},{8,11},{9,8},{10,9... | collective-permute-start | bytes 645128 | tf_op jit(solution)/shard_map/ppermute | solution.py:68
  102.4 279.9 %reduce-scatter.3.cloned.1.call-start = ((), (), s32[]{:S(2)}) async-start(), calls=%async_computation.3 | async-start | bytes 7962624 | tf_op jit(solution)/shard_map/reduce_scatter | solution.py:937
  105.4 29.9 %collective-permute-start.13 = (bf16[4,1,4,48,1536]{4,3,2,1,0:T(8,128)(2,1)}, bf16[4,1,4,48,1536]{4,3,2,1,0:T(8,128)(2,1)}, u32[]{:S(2)}, u32[]{:S(2)}) collective-permute-start(bf16[4,1,4,48,1536]{4,3,2,1,0:T(8,128)(2,1)} %pad_maximum_fusion.2.pieces_ref), channel_id=1, source_target_pairs={{0,4},{4,0},{8,12},{12,8},{16,20},{20,16},{24,28},{28,24},{1,5},{5... | collective-permute-start | bytes 7077896 | tf_op jit(solution)/shard_map/ppermute | solution.py:68
  105.4 24.8 %collective-permute-start.11 = (bf16[160,1536]{1,0:T(8,128)(2,1)S(1)}, bf16[160,1536]{1,0:T(8,128)(2,1)}, u32[]{:S(2)}, u32[]{:S(2)}) collective-permute-start(bf16[160,1536]{1,0:T(8,128)(2,1)S(1)} %copy-done.21), channel_id=1, source_target_pairs={{0,1},{1,2},{2,3},{4,5},{5,6},{6,7},{8,9},{9,10},{10,11},{12,13},{... | collective-permute-start | bytes 1474568 | tf_op jit(solution)/shard_map/ppermute | solution.py:73
  135.3 27.6 %collective-permute-start.17 = (bf16[160,1536]{1,0:T(8,128)(2,1)}, bf16[160,1536]{1,0:T(8,128)(2,1)}, u32[]{:S(2)}, u32[]{:S(2)}) collective-permute-start(bf16[160,1536]{1,0:T(8,128)(2,1)} %collective-permute-done.11), channel_id=1, source_target_pairs={{0,1},{1,2},{2,3},{4,5},{5,6},{6,7},{8,9},{9,10},{10,11},{12,13},{... | collective-permute-start | bytes 1474568 | tf_op jit(solution)/shard_map/ppermute | solution.py:73
  137.5 25.4 %collective-permute-start.18 = (bf16[160,1536]{1,0:T(8,128)(2,1)}, bf16[160,1536]{1,0:T(8,128)(2,1)}, u32[]{:S(2)}, u32[]{:S(2)}) collective-permute-start(bf16[160,1536]{1,0:T(8,128)(2,1)} %collective-permute-done.12), channel_id=1, source_target_pairs={{1,0},{2,1},{3,2},{5,4},{6,5},{7,6},{9,8},{10,9},{11,10},{13,12},{... | collective-permute-start | bytes 1474568 | tf_op jit(solution)/shard_map/ppermute | solution.py:73
  141.5 21.4 %collective-permute-start.15 = (bf16[160,512]{1,0:T(8,128)(2,1)S(1)}, bf16[160,512]{1,0:T(8,128)(2,1)S(1)}, u32[]{:S(2)}, u32[]{:S(2)}) collective-permute-start(bf16[160,512]{1,0:T(8,128)(2,1)S(1)} %pad_maximum_fusion.14), channel_id=1, source_target_pairs={{0,2},{1,3},{2,0},{3,1},{4,6},{5,7},{6,4},{7,5},{8,10},{9,11},{10,... | collective-permute-start | bytes 491528 | tf_op jit(solution)/shard_map/ppermute | solution.py:68
  162.9 22.3 %collective-permute-start.19 = (bf16[160,1536]{1,0:T(8,128)(2,1)}, bf16[160,1536]{1,0:T(8,128)(2,1)S(1)}, u32[]{:S(2)}, u32[]{:S(2)}) collective-permute-start(bf16[160,1536]{1,0:T(8,128)(2,1)} %collective-permute-done.17), channel_id=1, source_target_pairs={{0,1},{1,2},{2,3},{4,5},{5,6},{6,7},{8,9},{9,10},{10,11},{12,13},{... | collective-permute-start | bytes 1474568 | tf_op jit(solution)/shard_map/ppermute | solution.py:73
  188.0 32.0 %collective-permute-start.22 = (bf16[160,1536]{1,0:T(8,128)(2,1)S(1)}, bf16[160,1536]{1,0:T(8,128)(2,1)S(1)}, u32[]{:S(2)}, u32[]{:S(2)}) collective-permute-start(bf16[160,1536]{1,0:T(8,128)(2,1)S(1)} %multiply_convert_fusion), channel_id=1, source_target_pairs={{0,2},{1,3},{2,0},{3,1},{4,6},{5,7},{6,4},{7,5},{8,10},{9,11},{10,... | collective-permute-start | bytes 1474568 | tf_op jit(solution)/shard_map/ppermute | solution.py:68
  188.0 32.0 %collective-permute-start.23 = (bf16[160,1536]{1,0:T(8,128)(2,1)S(1)}, bf16[160,1536]{1,0:T(8,128)(2,1)S(1)}, u32[]{:S(2)}, u32[]{:S(2)}) collective-permute-start(bf16[160,1536]{1,0:T(8,128)(2,1)S(1)} %multiply_convert_fusion), channel_id=1, source_target_pairs={{0,3},{1,0},{2,1},{3,2},{4,7},{5,4},{6,5},{7,6},{8,11},{9,8},{10,9... | collective-permute-start | bytes 1474568 | tf_op jit(solution)/shard_map/ppermute | solution.py:68
  269.7 34.3 %collective-permute-start.24 = (bf16[2,2,4,48,2240]{4,3,2,1,0:T(8,128)(2,1)}, bf16[2,2,4,48,2240]{4,3,2,1,0:T(8,128)(2,1)}, u32[]{:S(2)}, u32[]{:S(2)}) collective-permute-start(bf16[2,2,4,48,2240]{4,3,2,1,0:T(8,128)(2,1)} %bitcast.235), channel_id=1, source_target_pairs={{0,4},{4,0},{8,12},{12,8},{16,20},{20,16},{24,28},{28,24},{1,5},{5... | collective-permute-start | bytes 10321928 | tf_op jit(solution)/shard_map/ppermute | solution.py:68
  269.7 23.4 %collective-permute-start.25 = (bf16[160,1536]{1,0:T(8,128)(2,1)S(1)}, bf16[160,1536]{1,0:T(8,128)(2,1)S(1)}, u32[]{:S(2)}, u32[]{:S(2)}) collective-permute-start(bf16[160,1536]{1,0:T(8,128)(2,1)S(1)} %copy-done.49), channel_id=1, source_target_pairs={{0,3},{1,0},{2,1},{3,2},{4,7},{5,4},{6,5},{7,6},{8,11},{9,8},{10,9... | collective-permute-start | bytes 1474568 | tf_op jit(solution)/shard_map/ppermute | solution.py:68
  281.5 22.5 %collective-permute-start.26 = (bf16[160,1536]{1,0:T(8,128)(2,1)S(1)}, bf16[160,1536]{1,0:T(8,128)(2,1)S(1)}, u32[]{:S(2)}, u32[]{:S(2)}) collective-permute-start(bf16[160,1536]{1,0:T(8,128)(2,1)S(1)} %copy-done.48), channel_id=1, source_target_pairs={{0,1},{1,2},{2,3},{3,0},{4,5},{5,6},{6,7},{7,4},{8,9},{9,10},{10,1... | collective-permute-start | bytes 1474568 | tf_op jit(solution)/shard_map/ppermute | solution.py:68
  304.0 221.7 %reduce-scatter.5.cloned.1.call-start = ((), (), s32[]{:S(2)}) async-start(), calls=%async_computation.4 | async-start | bytes 7741440 | tf_op jit(solution)/shard_map/reduce_scatter | solution.py:937
  308.2 27.5 %collective-permute-start.27 = (bf16[2,4,48,2240]{3,2,1,0:T(8,128)(2,1)}, bf16[2,4,48,2240]{3,2,1,0:T(8,128)(2,1)}, u32[]{:S(2)}, u32[]{:S(2)}) collective-permute-start(bf16[2,4,48,2240]{3,2,1,0:T(8,128)(2,1)} %fusion), channel_id=1, source_target_pairs={{0,8},{4,20},{8,0},{12,28},{16,24},{20,4},{24,16},{28,12},{1,9},{5... | collective-permute-start | bytes 5160968 | tf_op jit(solution)/shard_map/ppermute | solution.py:68
  308.2 24.8 %collective-permute-start.28 = (bf16[160,1536]{1,0:T(8,128)(2,1)S(1)}, bf16[160,1536]{1,0:T(8,128)(2,1)S(1)}, u32[]{:S(2)}, u32[]{:S(2)}) collective-permute-start(bf16[160,1536]{1,0:T(8,128)(2,1)S(1)} %copy-done.47), channel_id=1, source_target_pairs={{0,2},{1,3},{2,0},{3,1},{4,6},{5,7},{6,4},{7,5},{8,10},{9,11},{10,... | collective-permute-start | bytes 1474568 | tf_op jit(solution)/shard_map/ppermute | solution.py:68
  387.5 235.3 %all-gather.7.cloned.1.call-start = ((), (), s32[]{:S(2)}) async-start(), calls=%async_computation.5 | async-start | bytes 7741440 | tf_op jit(solution)/shard_map/all_gather | solution.py:1068
  400.8 41.0 %collective-permute-start.38 = (bf16[2,2,4,48,2048]{4,3,2,1,0:T(8,128)(2,1)}, bf16[2,2,4,48,2048]{4,3,2,1,0:T(8,128)(2,1)}, u32[]{:S(2)}, u32[]{:S(2)}) collective-permute-start(bf16[2,2,4,48,2048]{4,3,2,1,0:T(8,128)(2,1)} %bitcast.236), channel_id=1, source_target_pairs={{0,4},{4,0},{8,12},{12,8},{16,20},{20,16},{24,28},{28,24},{1,5},{5... | collective-permute-start | bytes 9437192 | tf_op jit(solution)/shard_map/ppermute | solution.py:68
  403.4 37.7 %collective-permute-start.39 = (bf16[4,48,1536]{2,1,0:T(8,128)(2,1)}, bf16[4,48,1536]{2,1,0:T(8,128)(2,1)}, u32[]{:S(2)}, u32[]{:S(2)}) collective-permute-start(bf16[4,48,1536]{2,1,0:T(8,128)(2,1)} %fusion.15), channel_id=1, source_target_pairs={{0,16},{4,12},{8,24},{12,4},{16,0},{20,28},{24,8},{28,20},{1,17},{... | collective-permute-start | bytes 1769480 | tf_op jit(solution)/shard_map/ppermute | solution.py:68
  408.3 32.8 %collective-permute-start.40 = (bf16[48,8960]{1,0:T(8,128)(2,1)S(1)}, bf16[48,8960]{1,0:T(8,128)(2,1)S(1)}, u32[]{:S(2)}, u32[]{:S(2)}) collective-permute-start(bf16[48,8960]{1,0:T(8,128)(2,1)S(1)} %concatenate.70), channel_id=1, source_target_pairs={{0,16},{4,12},{8,24},{12,4},{16,0},{20,28},{24,8},{28,20},{1,17},{... | collective-permute-start | bytes 2580488 | tf_op jit(solution)/shard_map/ppermute | solution.py:68
  415.9 25.2 %collective-permute-start.41 = (bf16[160,1536]{1,0:T(8,128)(2,1)S(1)}, bf16[160,1536]{1,0:T(8,128)(2,1)S(1)}, u32[]{:S(2)}, u32[]{:S(2)}) collective-permute-start(bf16[160,1536]{1,0:T(8,128)(2,1)S(1)} %copy-done.46), channel_id=1, source_target_pairs={{0,2},{1,3},{2,0},{3,1},{4,6},{5,7},{6,4},{7,5},{8,10},{9,11},{10,... | collective-permute-start | bytes 1474568 | tf_op jit(solution)/shard_map/ppermute | solution.py:68
  446.7 47.8 %collective-permute-start.43 = (bf16[2,48,8960]{2,1,0:T(8,128)(2,1)}, bf16[2,48,8960]{2,1,0:T(8,128)(2,1)}, u32[]{:S(2)}, u32[]{:S(2)}) collective-permute-start(bf16[2,48,8960]{2,1,0:T(8,128)(2,1)} %pad_maximum_fusion.5), channel_id=1, source_target_pairs={{0,8},{4,20},{8,0},{12,28},{16,24},{20,4},{24,16},{28,12},{1,9},{5... | collective-permute-start | bytes 5160968 | tf_op jit(solution)/shard_map/ppermute | solution.py:68
  446.7 47.8 %collective-permute-start.42 = (bf16[2,4,48,2048]{3,2,1,0:T(8,128)(2,1)}, bf16[2,4,48,2048]{3,2,1,0:T(8,128)(2,1)}, u32[]{:S(2)}, u32[]{:S(2)}) collective-permute-start(bf16[2,4,48,2048]{3,2,1,0:T(8,128)(2,1)} %fusion.4), channel_id=1, source_target_pairs={{0,8},{4,20},{8,0},{12,28},{16,24},{20,4},{24,16},{28,12},{1,9},{5... | collective-permute-start | bytes 4718600 | tf_op jit(solution)/shard_map/ppermute | solution.py:68
  525.8 34.1 %collective-permute-start.55 = (bf16[2,48,8960]{2,1,0:T(8,128)(2,1)}, bf16[2,48,8960]{2,1,0:T(8,128)(2,1)S(1)}, u32[]{:S(2)}, u32[]{:S(2)}) collective-permute-start(bf16[2,48,8960]{2,1,0:T(8,128)(2,1)} %pad_maximum_fusion.6), channel_id=1, source_target_pairs={{0,8},{4,20},{8,0},{12,28},{16,24},{20,4},{24,16},{28,12},{1,9},{5... | collective-permute-start | bytes 5160968 | tf_op jit(solution)/shard_map/ppermute | solution.py:68
  611.2 21.8 %collective-permute-start.69 = (f32[1280]{0:T(1024)S(1)}, f32[1280]{0:T(1024)S(1)}, u32[]{:S(2)}, u32[]{:S(2)}) collective-permute-start(f32[1280]{0:T(1024)S(1)} %get-tuple-element.907), channel_id=1, source_target_pairs={{0,1},{1,2},{2,3},{3,0},{4,5},{5,6},{6,7},{7,4},{8,9},{9,10},{10,1... | collective-permute-start | bytes 15368 | tf_op jit(solution)/shard_map/ppermute | solution.py:68
  611.3 21.7 %collective-permute-start.70 = (f32[1280]{0:T(1024)S(1)}, f32[1280]{0:T(1024)S(1)}, u32[]{:S(2)}, u32[]{:S(2)}) collective-permute-start(f32[1280]{0:T(1024)S(1)} %get-tuple-element.908), channel_id=1, source_target_pairs={{0,2},{1,3},{2,0},{3,1},{4,6},{5,7},{6,4},{7,5},{8,10},{9,11},{10,... | collective-permute-start | bytes 15368 | tf_op jit(solution)/shard_map/ppermute | solution.py:68
  (100 other events, 1451.0 us)
Sparse Core Ops, SparseCore 0:
  11.5 99.7 all-gather.8
  113.8 75.0 all-gather.4
  304.1 70.6 reduce-scatter.2
  387.6 77.4 reduce-scatter.4
  525.9 58.2 all-gather.6

commit v14 on v13

--- a/solution.py
+++ b/solution.py
@@ -807,7 +807,10 @@
         gate_weight.reshape(reps, part_rows, hidden_units),
         up_weight.reshape(reps, part_rows, hidden_units),
     )
-    (output_rows,) = clock.wait(output_moving)
+    passed = [[output_cotangent] * 2]
+    passing = clock.pass_on(shard, *passed[-1])
+    output_rows, arrived = clock.wait(output_moving, passing)
+    passed.append(arrived)
     output_rows = [own_output] + output_rows
 
     output_spread = spread(jnp.stack([rows[:part_rows] for rows in output_rows])[None])
@@ -859,9 +862,6 @@
         [row for pair in zip([gate_blocks[0]] + gate_rows, [up_blocks[0]] + up_rows) for row in pair]
     )
     gate_up = lax.all_gather(clock(gate_up)[0], "rep", axis=0, tiled=True)
-    passed = [[output_cotangent] * 2]
-    passing = clock.pass_on(shard, *passed[-1])
-    output_spread.over(output_arrived)
     input_matrix, normed_one = clock(input_matrix, normed_one)
     projected = jnp.dot(normed_one, input_matrix, preferred_element_type=f32) + shift_row
     key_part = rotate(
@@ -875,9 +875,6 @@
             axis=1,
         ).astype(bf16)
     )
-    arrived, output_arrived = clock.wait(passing, output_spread.moving)
-    passed.append(arrived)
-
     pair_moving = send_around(own_pairs)
     passing = clock.pass_on(shard, *passed[-1]) if shards > 2 else []
     pair_rows, arrived = clock.wait(pair_moving, passing)
@@ -885,18 +882,19 @@
     pairs = jnp.concatenate([own_pairs] + pair_rows, axis=0)
 
     passing = clock.pass_on(shard, *passed[-1]) if shards > 3 else []
+    output_spread.over(output_arrived)
+    queries, attention_low = clock.run(
+        attention_forward, projected, cosine_table, signed_sine, pairs, row_marks.T, key_marks
+    )
+    arrived, output_arrived = clock.wait(passing, output_spread.moving)
+    passed.append(arrived)
+
     (output_matrix,) = clock.run(place_blocks, z_order, *output_spread.finish(output_arrived))
     output_matrix = output_matrix.reshape(width, width)
-    queries, attention_low = clock.run(
-        attention_forward, projected, cosine_table, signed_sine, pairs, row_marks.T, key_marks
-    )
     hidden = wide_tokens + jnp.dot(attention_low, output_matrix, preferred_element_type=f32)
     inverse_two = lax.rsqrt(jnp.mean(hidden * hidden, axis=-1, keepdims=True) + EPSILON)
     unit_two = hidden * inverse_two
     (normed_two,) = clock((unit_two * gain_two).astype(bf16))
-    (arrived,) = clock.wait(passing)
-    passed.append(arrived)
-
     normed_moving = send_around(normed_two)
     gate_matrix, up_matrix = clock.run(
         lambda order, gathered: place_gathered(order, gathered, 2), z_order, gate_up
@@ -945,6 +943,12 @@
     edges = sorted({0, shards - 2})
     inside = list(range(1, shards - 2))
 
+    (gate_blocks,) = clock.run(
+        lambda left, right: ordered_gradient(left, right, shards, rep_places(reps)),
+        turned_normed,
+        d_gate,
+    )
+    gate_piece = sum_over_rep(gate_blocks.reshape(width, block_units))
     normed_own, *normed_partial = clock.run(
         lambda *operands: rows_product(operands[:2], operands[2:], True, shards),
         d_gate,
@@ -956,13 +960,10 @@
 
     up = Halving(clock, *up_halves, core, first, second)
     normed_moving = send_some(normed_partial, edges)
-    (gate_blocks,) = clock.run(
-        lambda left, right: ordered_gradient(left, right, shards, rep_places(reps)),
-        turned_normed,
-        d_gate,
+    block_own, *block_partial = clock.run(
+        lambda left, right: rows_product((left,), (right,), False, shards), inner_act, down_weight
     )
     up_arrived, normed_arrived = clock.wait(up.moving, normed_moving)
-    gate_piece = sum_over_rep(clock(gate_blocks)[0].reshape(width, block_units))
 
     up.along_first(up_arrived)
     normed_moving = send_some(normed_partial, inside)
@@ -973,7 +974,10 @@
     )
     up_arrived, more_arrived = clock.wait(up.moving, normed_moving)
 
+    (gate_piece,) = clock(gate_piece)
+    down_piece = sum_over_rep(clock(down_blocks)[0].reshape(block_units, width))
     up.along_second(up_arrived)
+    block_moving = send_some(block_partial, inside)
     normed_two_gradient = total_of([normed_own] + normed_arrived + more_arrived)
     gain_two_gradient = jnp.sum(normed_two_gradient * unit_two, axis=0)
     hidden_gradient = output_cotangent.astype(f32) + norm_back(
@@ -992,18 +996,13 @@
         key_marks.T,
     )
     output_halves = split_halves(attention_low, branch_gradient, shards, False)
-    (up_arrived,) = clock.wait(up.moving)
+    up_arrived, block_arrived = clock.wait(up.moving, block_moving)
 
     pair_moving = send_back(pair_partial)
     output = Halving(clock, *output_halves, core, first, second)
     up_blocks = clock(*blocks_of(up.finish(up_arrived)))
-    block_own, *block_partial = clock.run(
-        lambda left, right: rows_product((left,), (right,), False, shards), inner_act, down_weight
-    )
     pair_arrived, output_arrived = clock.wait(pair_moving, output.moving)
 
-    (gate_piece,) = clock(gate_piece)
-    down_piece = sum_over_rep(clock(down_blocks)[0].reshape(block_units, width))
     output.along_first(output_arrived)
     up_moving = send_blocks(up_blocks)
     projected_gradient, bias_sum = clock.run(
@@ -1020,7 +1019,7 @@
     projected = Halving(clock, *projected_halves, core, first, second)
     output.along_second(output_arrived)
     up_spread = spread(side_by_side(up_blocks[:1] + up_rows))
-    block_moving = send_some(block_partial, inside)
+    block_moving = send_some(block_partial, edges[:1])
     projected_gradient, hidden_gradient = clock(projected_gradient, hidden_gradient)
     normed_one_gradient = times_transposed(projected_gradient, input_matrix)
     gain_one_gradient = jnp.sum(normed_one_gradient * unit_one, axis=0)
@@ -1029,15 +1028,18 @@
             hidden_gradient + norm_back(normed_one_gradient, unit_one, inverse_one, gain_one)
         ).astype(bf16)
     )
-    projected_arrived, output_arrived, up_arrived, block_arrived = clock.wait(
+    projected_arrived, output_arrived, up_arrived, more_arrived = clock.wait(
         projected.moving, output.moving, up_spread.moving, block_moving
     )
-
+    block_arrived = block_arrived + more_arrived
+
+    (down_piece,) = clock(down_piece)
+    down_gathered = lax.all_gather(down_piece, "rep", axis=0, tiled=True)
     projected.along_first(projected_arrived)
     up_spread.along(up_arrived)
     gate_blocks = clock(*blocks_of(gate_piece.reshape(shards, part_rows, block_units)))
     gate_moving = send_blocks(gate_blocks)
-    output_blocks = clock(*blocks_of(output.finish(output_arrived)))
+    (output_blocks,) = clock(output.finish(output_arrived))
     bias_gradient = bias_sum[0]
     bias_split = query_width + pair_width
     small_parts = (
@@ -1055,36 +1057,35 @@
 
     projected.along_second(projected_arrived)
     gate_spread = spread(side_by_side(gate_blocks[:1] + gate_rows))
-    output_moving = send_blocks(output_blocks)
-    projected_arrived, gate_arrived, output_rows = clock.wait(
-        projected.moving, gate_spread.moving, output_moving
+    up_spread.over(up_arrived)
+    output_rows = lax.all_to_all(output_blocks, "shard", 0, 0, tiled=True)
+    projected_arrived, gate_arrived, up_arrived = clock.wait(
+        projected.moving, gate_spread.moving, up_spread.moving
     )
 
     input_blocks = clock(*blocks_of(projected.finish(projected_arrived)))
     input_moving = send_blocks(input_blocks)
     gate_spread.along(gate_arrived)
-    output_spread = spread(row_sum(output_blocks[:1], output_rows))
-    (down_piece,) = clock(down_piece)
-    down_gathered = lax.all_gather(down_piece, "rep", axis=0, tiled=True)
-    input_rows, gate_arrived, output_arrived = clock.wait(
-        input_moving, gate_spread.moving, output_spread.moving
-    )
-
+    (up_total,) = clock.run(widen_pieces, *up_spread.finish(up_arrived))
+    input_rows, gate_arrived = clock.wait(input_moving, gate_spread.moving)
+
+    (output_rows,) = clock(output_rows)
     input_spread = spread(row_sum(input_blocks[:1], input_rows))
-    output_spread.along(output_arrived)
-    up_spread.over(up_arrived)
+    output_spread = spread(row_sum(list(output_rows), []))
     gate_spread.over(gate_arrived)
     small_moving = clock.send(core, [small], [1])
-    input_arrived, output_arrived, up_arrived, gate_arrived, small_arrived = clock.wait(
-        input_spread.moving, output_spread.moving, up_spread.moving, gate_spread.moving, small_moving
+    (down_gathered,) = clock(down_gathered)
+    (down_total,) = clock(down_gathered.astype(f32))
+    input_arrived, output_arrived, gate_arrived, small_arrived = clock.wait(
+        input_spread.moving, output_spread.moving, gate_spread.moving, small_moving
     )
     small = total_of([small] + small_arrived)
 
     input_spread.along(input_arrived)
-    output_spread.over(output_arrived)
+    output_spread.along(output_arrived)
     small_moving = clock.send(first, [small] * (first.size - 1), range(1, first.size))
-    block_moving = send_some(block_partial, edges[:1])
-    (up_total,) = clock.run(widen_pieces, *up_spread.finish(up_arrived))
+    block_moving = send_some(block_partial, edges[1:])
+    (gate_total,) = clock.run(widen_pieces, *gate_spread.finish(gate_arrived))
     input_arrived, output_arrived, small_arrived, more_arrived = clock.wait(
         input_spread.moving, output_spread.moving, small_moving, block_moving
     )
@@ -1092,21 +1093,17 @@
     block_arrived = block_arrived + more_arrived
 
     input_spread.over(input_arrived)
+    output_spread.over(output_arrived)
     small_moving = clock.send(second, [small] * (second.size - 1), range(1, second.size))
-    block_moving = send_some(block_partial, edges[1:])
-    (gate_total,) = clock.run(widen_pieces, *gate_spread.finish(gate_arrived))
-    input_arrived, small_arrived, more_arrived = clock.wait(
-        input_spread.moving, small_moving, block_moving
-    )
-    block_arrived = block_arrived + more_arrived
+    (block_out,) = clock(total_of([hidden, block_own] + block_arrived).astype(bf16))
+    input_arrived, output_arrived, small_arrived = clock.wait(
+        input_spread.moving, output_spread.moving, small_moving
+    )
     small_blocks = clock(*blocks_of(total_of([small] + small_arrived)))
 
     small_moving = send_blocks(small_blocks)
     (output_total,) = clock.run(widen_pieces, *output_spread.finish(output_arrived))
     (input_total,) = clock.run(widen_pieces, *input_spread.finish(input_arrived))
-    (down_gathered,) = clock(down_gathered)
-    (down_total,) = clock(down_gathered.astype(f32))
-    (block_out,) = clock(total_of([hidden, block_own] + block_arrived).astype(bf16))
     (small_arrived,) = clock.wait(small_moving)
     small = total_of(small_blocks[:1] + small_arrived)
 

time: 652 us -> 650 us (level)
  waiting for transfers between devices: 247 us -> 240 us
    ppermute x66 -> x63, waiting for transfers between devices: 238 us -> 219 us  [shift(): return lax.ppermute(value, self.name, self.pairs(step % self.size))]
    ppermute x6, waiting for transfers between devices: 9.2 us -> 16.2 us  [pass_on(): return lax.ppermute(value, self.name, pairs)]
    ppermute x66 -> x63, starting transfers between devices: 103 us -> 98.3 us  [shift(): return lax.ppermute(value, self.name, self.pairs(step % self.size))]
    unnamed x121 -> x169, local copies, waits for them, and re-layouts: 14.4 us -> 15.9 us
  transfers between devices with their start and end apart: 77 -> 75, of which waited for: 32 -> 32; matrix products, arithmetic and copies ran while one was open for 15% -> 15% of each run, Pallas kernels for 15% -> 17%
where the time goes in v14:
time: 650 us; the launch traced here: 640 us
  waiting for transfers between devices  240 us (37%)
  Pallas kernels  144 us (22%)
  starting transfers between devices  124 us (19%)
  other arithmetic  68.3 us (11%)
  local copies, waits for them, and re-layouts  32.4 us (5%)
  between operations  15.6 us (2%)
  matrix products  15.4 us (2%)
    ppermute x63, waiting for transfers between devices, shift(): return lax.ppermute(value, self.name, self.pairs(step % self.size))  219 us
    ppermute x63, starting transfers between devices, shift(): return lax.ppermute(value, self.name, self.pairs(step % self.size))  98.3 us
    pallas_call x1, Pallas kernels, feed_forward(): pl.pallas_call(body, grid=(steps,), out_shape=[jax.ShapeDtypeStruct((coun...  23.7 us
    pallas_call x2, Pallas kernels, rows_product(): pl.pallas_call(body, grid=(pl.cdiv(columns, TILE),), out_shape=[jax.Shape...  23.3 us
    pallas_call x4, Pallas kernels, widen_pieces(): pl.pallas_call(body, out_shape=jax.ShapeDtypeStruct((reps, rows, columns)...  21.4 us
    pallas_call x3, Pallas kernels, split_gradient(): pl.pallas_call(body, grid=(pl.cdiv(columns, TILE),), out_shape=[jax.Shape...  20.6 us
    ppermute x6, starting transfers between devices, pass_on(): return lax.ppermute(value, self.name, pairs)  19.6 us
    pallas_call x2, Pallas kernels, ordered_gradient(): pl.pallas_call(body, grid=(pl.cdiv(columns, TILE),), out_shape=[jax.Shape...  19.3 us
  transfers between devices with their start and end apart: 75, of which 32 were waited for; matrix products, arithmetic and copies ran while one was open for 15% of the time, Pallas kernels for 17%

profile of v14, /device:TPU:0, one launch (start us, length us, event | category | flops | bytes accessed | tf_op | source)
XLA Modules:
  0.0 640.1 jit_solution(8833269721359397430)
XLA Ops:
  33.0 6.9 %collective-permute-done.3 = bf16[160,1536]{1,0:T(8,128)(2,1)S(1)} collective-permute-done((bf16[160,1536]{1,0:T(8,128)(2,1)S(1)}, bf16[160,1536]{1,0:T(8,128)(2,1)S(1)}, u32[]{:S(2)}, u32[]{:S(2)}) %collective-permute-start.3) | collective-permute-done | bytes 491552 | tf_op jit(solution)/shard_map/ppermute | solution.py:73
  60.0 11.4 %collective-permute-done.7 = bf16[48,2240]{1,0:T(8,128)(2,1)S(1)} collective-permute-done((bf16[48,2240]{1,0:T(8,128)(2,1)}, bf16[48,2240]{1,0:T(8,128)(2,1)S(1)}, u32[]{:S(2)}, u32[]{:S(2)}) %collective-permute-start.7) | collective-permute-done | bytes 215072 | tf_op jit(solution)/shard_map/ppermute | solution.py:68
  82.0 8.5 %collective-permute-done.10 = bf16[48,2240]{1,0:T(8,128)(2,1)S(1)} collective-permute-done((bf16[48,2240]{1,0:T(8,128)(2,1)S(1)}, bf16[48,2240]{1,0:T(8,128)(2,1)S(1)}, u32[]{:S(2)}, u32[]{:S(2)}) %collective-permute-start.10) | collective-permute-done | bytes 215072 | tf_op jit(solution)/shard_map/ppermute | solution.py:68
  90.4 16.5 %collective-permute-done.11 = bf16[48,2240]{1,0:T(8,128)(2,1)S(1)} collective-permute-done((bf16[48,2240]{1,0:T(8,128)(2,1)S(1)}, bf16[48,2240]{1,0:T(8,128)(2,1)S(1)}, u32[]{:S(2)}, u32[]{:S(2)}) %collective-permute-start.11) | collective-permute-done | bytes 215072 | tf_op jit(solution)/shard_map/ppermute | solution.py:68
  123.2 8.0 %collective-permute-start.16 = (bf16[160,1536]{1,0:T(8,128)(2,1)S(1)}, bf16[160,1536]{1,0:T(8,128)(2,1)S(1)}, u32[]{:S(2)}, u32[]{:S(2)}) collective-permute-start(bf16[160,1536]{1,0:T(8,128)(2,1)S(1)} %copy-done.36), channel_id=1, source_target_pairs={{0,1},{1,2},{2,3},{4,5},{5,6},{6,7},{8,9},{9,10},{10,11},{12,13},{... | collective-permute-start | bytes 1474568 | tf_op jit(solution)/shard_map/ppermute | solution.py:73
  139.3 11.9 %collective-permute-done.13 = bf16[160,512]{1,0:T(8,128)(2,1)S(1)} collective-permute-done((bf16[160,512]{1,0:T(8,128)(2,1)S(1)}, bf16[160,512]{1,0:T(8,128)(2,1)S(1)}, u32[]{:S(2)}, u32[]{:S(2)}) %collective-permute-start.13) | collective-permute-done | bytes 163872 | tf_op jit(solution)/shard_map/ppermute | solution.py:68
  151.2 6.0 collective-permute-done.14
  169.4 5.7 attention_forward.1
  197.6 11.7 %place_blocks.3 = (bf16[4,8,48,2240]{3,2,1,0:T(8,128)(2,1)}, bf16[4,8,48,2240]{3,2,1,0:T(8,128)(2,1)}) custom-call(s32[4]{0:T(128)} %pad_add_fusion.5.order_ref, bf16[64,48,2240]{2,1,0:T(8,128)(2,1)} %all-gather.5.cloned.1.call-done.source), custom_call_target="tpu_custom_call" | custom-call | flops 1 | bytes 1 | tf_op jit(solution)/shard_map/place_blocks/pallas_call | solution.py:339
  209.3 16.8 %collective-permute-done.22 = bf16[160,1536]{1,0:T(8,128)(2,1)S(1)} collective-permute-done((bf16[160,1536]{1,0:T(8,128)(2,1)S(1)}, bf16[160,1536]{1,0:T(8,128)(2,1)S(1)}, u32[]{:S(2)}, u32[]{:S(2)}) %collective-permute-start.22) | collective-permute-done | bytes 491552 | tf_op jit(solution)/shard_map/ppermute | solution.py:68
  227.5 23.7 %feed_forward.1 = (bf16[640,2240]{1,0:T(8,128)(2,1)}, bf16[640,2240]{1,0:T(8,128)(2,1)}, bf16[640,2240]{1,0:T(8,128)(2,1)}, bf16[1536,640]{1,0:T(8,128)(2,1)}, bf16[2240,640]{1,0:T(8,128)(2,1)}) custom-call(bf16[640,1536]{1,0:T(8,128)(2,1)} %pad_maximum_fusion.3.rows_ref, bf16[640,1536]{1,0:T(8,128)(2,1)} %pad_maximum_fusion.4.cotangents_ref.right_ref, ...), custom_call_target="tpu_custom_call" | custom-call | flops 1 | bytes 1 | tf_op jit(solution)/shard_map/feed_forward/pallas_call | solution.py:477
  251.2 9.9 %ordered_gradient.2 = bf16[8,4,48,2240]{3,2,1,0:T(8,128)(2,1)} custom-call(bf16[1536,640]{1,0:T(8,128)(2,1)} %get-tuple-element.597.left_ref, bf16[640,2240]{1,0:T(8,128)(2,1)} %get-tuple-element.587.right_ref.refs_0_), custom_call_target="tpu_custom_call" | custom-call | flops 1 | bytes 1 | tf_op jit(solution)/shard_map/ordered_gradient/pallas_call | solution.py:563
  261.2 14.6 %rows_product.2 = (bf16[160,1536]{1,0:T(8,128)(2,1)}, bf16[160,1536]{1,0:T(8,128)(2,1)}, bf16[160,1536]{1,0:T(8,128)(2,1)}, bf16[160,1536]{1,0:T(8,128)(2,1)}) custom-call(bf16[640,2240]{1,0:T(8,128)(2,1)} %get-tuple-element.587.right_ref.refs_0_, bf16[640,2240]{1,0:T(8,128)(2,1)} %get-tuple-element.598.refs_1_.right_ref, bf16[1536,2240]{1,0:T(8,128)(2,1)} %bitcast.177, ...), custom_call_target="tpu_custom_call" | custom-call | flops 1 | bytes 1 | tf_op jit(solution)/shard_map/rows_product/pallas_call | solution.py:603
  275.9 10.6 %split_gradient.3 = (bf16[4,4,48,2240]{3,2,1,0:T(8,128)(2,1)}, bf16[4,4,48,2240]{3,2,1,0:T(8,128)(2,1)}) custom-call(s32[1]{0:T(128)} %bitcast.46.core_ref, bf16[1536,640]{1,0:T(8,128)(2,1)} %get-tuple-element.597.left_ref, bf16[640,2240]{1,0:T(8,128)(2,1)} %get-tuple-element.598.refs_1_.right_ref), custom_call_target="tpu_custom_call" | custom-call | flops 1 | bytes 1 | tf_op jit(solution)/shard_map/split_gradient/pallas_call | solution.py:533
  286.5 9.7 %collective-permute-start.25 = (bf16[160,1536]{1,0:T(8,128)(2,1)S(1)}, bf16[160,1536]{1,0:T(8,128)(2,1)S(1)}, u32[]{:S(2)}, u32[]{:S(2)}) collective-permute-start(bf16[160,1536]{1,0:T(8,128)(2,1)S(1)} %copy-done.73), channel_id=1, source_target_pairs={{0,3},{1,0},{2,1},{3,2},{4,7},{5,4},{6,5},{7,6},{8,11},{9,8},{10,9... | collective-permute-start | bytes 1474568 | tf_op jit(solution)/shard_map/ppermute | solution.py:68
  296.7 8.6 %rows_product.3 = (bf16[160,1536]{1,0:T(8,128)(2,1)}, bf16[160,1536]{1,0:T(8,128)(2,1)}, bf16[160,1536]{1,0:T(8,128)(2,1)}, bf16[160,1536]{1,0:T(8,128)(2,1)}) custom-call(bf16[640,2240]{1,0:T(8,128)(2,1)} %get-tuple-element.609.refs_0_, bf16[2240,1536]{1,0:T(8,128)(2,1)} %refs_1_), custom_call_target="tpu_custom_call" | custom-call | flops 1 | bytes 1 | tf_op jit(solution)/shard_map/rows_product/pallas_call | solution.py:603
  308.5 10.9 %collective-permute-done.26 = bf16[160,1536]{1,0:T(8,128)(2,1)S(1)} collective-permute-done((bf16[160,1536]{1,0:T(8,128)(2,1)S(1)}, bf16[160,1536]{1,0:T(8,128)(2,1)S(1)}, u32[]{:S(2)}, u32[]{:S(2)}) %collective-permute-start.26) | collective-permute-done | bytes 491552 | tf_op jit(solution)/shard_map/ppermute | solution.py:68
  326.0 9.4 %ordered_gradient.3 = bf16[8,1,280,1536]{3,2,1,0:T(8,128)(2,1)} custom-call(bf16[2240,640]{1,0:T(8,128)(2,1)} %get-tuple-element.627.left_ref, bf16[640,1536]{1,0:T(8,128)(2,1)} %pad_maximum_fusion.4.cotangents_ref.right_ref), custom_call_target="tpu_custom_call" | custom-call | flops 1 | bytes 1 | tf_op jit(solution)/shard_map/ordered_gradient/pallas_call | solution.py:563
  335.4 12.2 %collective-permute-done.28 = bf16[160,1536]{1,0:T(8,128)(2,1)S(1)} collective-permute-done((bf16[160,1536]{1,0:T(8,128)(2,1)S(1)}, bf16[160,1536]{1,0:T(8,128)(2,1)S(1)}, u32[]{:S(2)}, u32[]{:S(2)}) %collective-permute-start.28) | collective-permute-done | bytes 491552 | tf_op jit(solution)/shard_map/ppermute | solution.py:68
  363.4 7.8 %attention_backward.1 = (bf16[160,1536]{1,0:T(8,128)(2,1)}, bf16[160,512]{1,0:T(8,128)(2,1)}, bf16[160,512]{1,0:T(8,128)(2,1)}, bf16[160,512]{1,0:T(8,128)(2,1)}, bf16[160,512]{1,0:T(8,128)(2,1)}) custom-call(bf16[2,960,128]{2,1,0:T(8,128)(2,1)} %get-tuple-element.651.queries_ref, bf16[160,1536]{1,0:T(8,128)(2,1)} %convolution_convert_fusion.gradient_ref, ...), custom_call_target="tpu_custom_call" | custom-call | flops 1 | bytes 1 | tf_op jit(solution)/shard_map/attention_backward/pallas_call | solution.py:705
  392.5 9.8 %collective-permute-done.32.refs_2_ = bf16[160,512]{1,0:T(8,128)(2,1)} collective-permute-done((bf16[160,512]{1,0:T(8,128)(2,1)S(1)}, bf16[160,512]{1,0:T(8,128)(2,1)}, u32[]{:S(2)}, u32[]{:S(2)}) %collective-permute-start.32) | collective-permute-done | bytes 163872 | tf_op jit(solution)/shard_map/ppermute | solution.py:68
  436.2 5.5 fusion.22
  446.2 9.4 %collective-permute-done.42 = bf16[160,1536]{1,0:T(8,128)(2,1)S(1)} collective-permute-done((bf16[160,1536]{1,0:T(8,128)(2,1)S(1)}, bf16[160,1536]{1,0:T(8,128)(2,1)S(1)}, u32[]{:S(2)}, u32[]{:S(2)}) %collective-permute-start.42) | collective-permute-done | bytes 491552 | tf_op jit(solution)/shard_map/ppermute | solution.py:68
  475.4 7.3 %collective-permute-done.46 = bf16[48,2240]{1,0:T(8,128)(2,1)S(1)} collective-permute-done((bf16[48,2240]{1,0:T(8,128)(2,1)}, bf16[48,2240]{1,0:T(8,128)(2,1)S(1)}, u32[]{:S(2)}, u32[]{:S(2)}) %collective-permute-start.46) | collective-permute-done | bytes 215072 | tf_op jit(solution)/shard_map/ppermute | solution.py:68
  482.6 17.8 %collective-permute-done.43 = bf16[2,4,48,2048]{3,2,1,0:T(8,128)(2,1)} collective-permute-done((bf16[2,4,48,2048]{3,2,1,0:T(8,128)(2,1)}, bf16[2,4,48,2048]{3,2,1,0:T(8,128)(2,1)}, u32[]{:S(2)}, u32[]{:S(2)}) %collective-permute-start.43) | collective-permute-done | bytes 1572896 | tf_op jit(solution)/shard_map/ppermute | solution.py:68
  511.0 28.4 %collective-permute-done.48 = bf16[4,48,2048]{2,1,0:T(8,128)(2,1)S(1)} collective-permute-done((bf16[4,48,2048]{2,1,0:T(8,128)(2,1)}, bf16[4,48,2048]{2,1,0:T(8,128)(2,1)S(1)}, u32[]{:S(2)}, u32[]{:S(2)}) %collective-permute-start.48) | collective-permute-done | bytes 786464 | tf_op jit(solution)/shard_map/ppermute | solution.py:68
  544.5 6.0 all-to-all-start
  556.3 7.4 %widen_pieces.4 = f32[8,48,8960]{2,1,0:T(8,128)} custom-call(s32[8]{0:T(128)} %stack.239.places_ref, bf16[4,48,8960]{2,1,0:T(8,128)(2,1)} %pad_maximum_fusion.pieces_ref, bf16[4,48,8960]{2,1,0:T(8,128)(2,1)} %collective-permute-done.50.others_ref), custom_call_target="tpu_custom_call" | custom-call | flops 1 | bytes 1 | tf_op jit(solution)/shard_map/widen_pieces/pallas_call | solution.py:415
  563.8 6.1 collective-permute-done.51
  569.9 9.3 %collective-permute-done.52 = bf16[48,2048]{1,0:T(8,128)(2,1)S(1)} collective-permute-done((bf16[48,2048]{1,0:T(8,128)(2,1)S(1)}, bf16[48,2048]{1,0:T(8,128)(2,1)S(1)}, u32[]{:S(2)}, u32[]{:S(2)}) %collective-permute-start.52) | collective-permute-done | bytes 196640 | tf_op jit(solution)/shard_map/ppermute | solution.py:68
  588.1 10.1 %convert_element_type.348 = f32[2240,1536]{1,0:T(8,128)} convert(bf16[2240,1536]{1,0:T(8,128)(2,1)} %all-gather.7.cloned.1.call-done) | non-fusion elementwise | flops 3440640 | bytes 20643840 | tf_op jit(solution)/shard_map/convert_element_type | solution.py:1078
  604.6 7.3 %widen_pieces.5 = f32[8,48,8960]{2,1,0:T(8,128)} custom-call(s32[8]{0:T(128)} %stack.239.places_ref, bf16[4,48,8960]{2,1,0:T(8,128)(2,1)} %pad_maximum_fusion.1.pieces_ref, bf16[4,48,8960]{2,1,0:T(8,128)(2,1)} %collective-permute-done.57.others_ref), custom_call_target="tpu_custom_call" | custom-call | flops 1 | bytes 1 | tf_op jit(solution)/shard_map/widen_pieces/pallas_call | solution.py:415
  (436 shorter events, 279.2 us)
Async XLA Ops:
  7.2 108.6 %all-gather.9.cloned.1.call-start = ((), (), s32[]{:S(2)}) async-start(), calls=%async_computation.7 | async-start | bytes 6488064 | tf_op jit(solution)/shard_map/all_gather | solution.py:796
  9.3 188.3 %all-gather.5.cloned.1.call-start = ((), (), s32[]{:S(2)}) async-start(), calls=%async_computation.3 | async-start | bytes 15925248 | tf_op jit(solution)/shard_map/all_gather | solution.py:864
  44.5 27.0 %collective-permute-start.5 = (bf16[1,4,48,1536]{3,2,1,0:T(8,128)(2,1)}, bf16[1,4,48,1536]{3,2,1,0:T(8,128)(2,1)S(1)}, u32[]{:S(2)}, u32[]{:S(2)}) collective-permute-start(bf16[1,4,48,1536]{3,2,1,0:T(8,128)(2,1)} %get-tuple-element.473), channel_id=1, source_target_pairs={{0,16},{4,12},{8,24},{12,4},{16,0},{20,28},{24,8},{28,20},{1,17},{... | collective-permute-start | bytes 1769480 | tf_op jit(solution)/shard_map/ppermute | solution.py:68
  71.6 35.4 %collective-permute-start.9 = (bf16[2,1,4,48,1536]{4,3,2,1,0:T(8,128)(2,1)S(1)}, bf16[2,1,4,48,1536]{4,3,2,1,0:T(8,128)(2,1)S(1)}, u32[]{:S(2)}, u32[]{:S(2)}) collective-permute-start(bf16[2,1,4,48,1536]{4,3,2,1,0:T(8,128)(2,1)S(1)} %pad_maximum_fusion.7), channel_id=1, source_target_pairs={{0,8},{4,20},{8,0},{12,28},{16,24},{20,4},{24,16},{28,12},{1,9},{5... | collective-permute-start | bytes 3538952 | tf_op jit(solution)/shard_map/ppermute | solution.py:68
  78.9 28.0 %collective-permute-start.11 = (bf16[48,2240]{1,0:T(8,128)(2,1)S(1)}, bf16[48,2240]{1,0:T(8,128)(2,1)S(1)}, u32[]{:S(2)}, u32[]{:S(2)}) collective-permute-start(bf16[48,2240]{1,0:T(8,128)(2,1)S(1)} %get-tuple-element.484), channel_id=1, source_target_pairs={{0,2},{1,3},{2,0},{3,1},{4,6},{5,7},{6,4},{7,5},{8,10},{9,11},{10,... | collective-permute-start | bytes 645128 | tf_op jit(solution)/shard_map/ppermute | solution.py:68
  80.5 26.5 %collective-permute-start.12 = (bf16[48,2240]{1,0:T(8,128)(2,1)S(1)}, bf16[48,2240]{1,0:T(8,128)(2,1)S(1)}, u32[]{:S(2)}, u32[]{:S(2)}) collective-permute-start(bf16[48,2240]{1,0:T(8,128)(2,1)S(1)} %get-tuple-element.485), channel_id=1, source_target_pairs={{0,3},{1,0},{2,1},{3,2},{4,7},{5,4},{6,5},{7,6},{8,11},{9,8},{10,9... | collective-permute-start | bytes 645128 | tf_op jit(solution)/shard_map/ppermute | solution.py:68
  111.5 240.4 %reduce-scatter.3.cloned.1.call-start = ((), (), s32[]{:S(2)}) async-start(), calls=%async_computation.4 | async-start | bytes 7962624 | tf_op jit(solution)/shard_map/reduce_scatter | solution.py:935
  123.2 34.0 %collective-permute-start.16 = (bf16[160,1536]{1,0:T(8,128)(2,1)S(1)}, bf16[160,1536]{1,0:T(8,128)(2,1)S(1)}, u32[]{:S(2)}, u32[]{:S(2)}) collective-permute-start(bf16[160,1536]{1,0:T(8,128)(2,1)S(1)} %copy-done.36), channel_id=1, source_target_pairs={{0,1},{1,2},{2,3},{4,5},{5,6},{6,7},{8,9},{9,10},{10,11},{12,13},{... | collective-permute-start | bytes 1474568 | tf_op jit(solution)/shard_map/ppermute | solution.py:73
  131.2 26.0 %collective-permute-start.17 = (bf16[160,1536]{1,0:T(8,128)(2,1)S(1)}, bf16[160,1536]{1,0:T(8,128)(2,1)S(1)}, u32[]{:S(2)}, u32[]{:S(2)}) collective-permute-start(bf16[160,1536]{1,0:T(8,128)(2,1)S(1)} %copy-done.39), channel_id=1, source_target_pairs={{1,0},{2,1},{3,2},{5,4},{6,5},{7,6},{9,8},{10,9},{11,10},{13,12},{... | collective-permute-start | bytes 1474568 | tf_op jit(solution)/shard_map/ppermute | solution.py:73
  158.8 22.9 %collective-permute-start.20 = (bf16[4,1,4,48,1536]{4,3,2,1,0:T(8,128)(2,1)}, bf16[4,1,4,48,1536]{4,3,2,1,0:T(8,128)(2,1)}, u32[]{:S(2)}, u32[]{:S(2)}) collective-permute-start(bf16[4,1,4,48,1536]{4,3,2,1,0:T(8,128)(2,1)} %pad_maximum_fusion.2.pieces_ref), channel_id=1, source_target_pairs={{0,4},{4,0},{8,12},{12,8},{16,20},{20,16},{24,28},{28,24},{1,5},{5... | collective-permute-start | bytes 7077896 | tf_op jit(solution)/shard_map/ppermute | solution.py:68
  191.1 35.0 %collective-permute-start.22 = (bf16[160,1536]{1,0:T(8,128)(2,1)S(1)}, bf16[160,1536]{1,0:T(8,128)(2,1)S(1)}, u32[]{:S(2)}, u32[]{:S(2)}) collective-permute-start(bf16[160,1536]{1,0:T(8,128)(2,1)S(1)} %multiply_convert_fusion), channel_id=1, source_target_pairs={{0,2},{1,3},{2,0},{3,1},{4,6},{5,7},{6,4},{7,5},{8,10},{9,11},{10,... | collective-permute-start | bytes 1474568 | tf_op jit(solution)/shard_map/ppermute | solution.py:68
  191.1 35.0 %collective-permute-start.23 = (bf16[160,1536]{1,0:T(8,128)(2,1)S(1)}, bf16[160,1536]{1,0:T(8,128)(2,1)S(1)}, u32[]{:S(2)}, u32[]{:S(2)}) collective-permute-start(bf16[160,1536]{1,0:T(8,128)(2,1)S(1)} %multiply_convert_fusion), channel_id=1, source_target_pairs={{0,3},{1,0},{2,1},{3,2},{4,7},{5,4},{6,5},{7,6},{8,11},{9,8},{10,9... | collective-permute-start | bytes 1474568 | tf_op jit(solution)/shard_map/ppermute | solution.py:68
  261.2 200.1 %reduce-scatter.5.cloned.1.call-start = ((), (), s32[]{:S(2)}) async-start(), calls=%async_computation.5 | async-start | bytes 7741440 | tf_op jit(solution)/shard_map/reduce_scatter | solution.py:935
  286.5 32.9 %collective-permute-start.24 = (bf16[2,2,4,48,2240]{4,3,2,1,0:T(8,128)(2,1)}, bf16[2,2,4,48,2240]{4,3,2,1,0:T(8,128)(2,1)}, u32[]{:S(2)}, u32[]{:S(2)}) collective-permute-start(bf16[2,2,4,48,2240]{4,3,2,1,0:T(8,128)(2,1)} %bitcast.229), channel_id=1, source_target_pairs={{0,4},{4,0},{8,12},{12,8},{16,20},{20,16},{24,28},{28,24},{1,5},{5... | collective-permute-start | bytes 10321928 | tf_op jit(solution)/shard_map/ppermute | solution.py:68
  296.2 23.2 %collective-permute-start.26 = (bf16[160,1536]{1,0:T(8,128)(2,1)S(1)}, bf16[160,1536]{1,0:T(8,128)(2,1)S(1)}, u32[]{:S(2)}, u32[]{:S(2)}) collective-permute-start(bf16[160,1536]{1,0:T(8,128)(2,1)S(1)} %copy-done.72), channel_id=1, source_target_pairs={{0,1},{1,2},{2,3},{3,0},{4,5},{5,6},{6,7},{7,4},{8,9},{9,10},{10,1... | collective-permute-start | bytes 1474568 | tf_op jit(solution)/shard_map/ppermute | solution.py:68
  322.7 29.2 %collective-permute-start.27 = (bf16[2,4,48,2240]{3,2,1,0:T(8,128)(2,1)}, bf16[2,4,48,2240]{3,2,1,0:T(8,128)(2,1)}, u32[]{:S(2)}, u32[]{:S(2)}) collective-permute-start(bf16[2,4,48,2240]{3,2,1,0:T(8,128)(2,1)} %fusion), channel_id=1, source_target_pairs={{0,8},{4,20},{8,0},{12,28},{16,24},{20,4},{24,16},{28,12},{1,9},{5... | collective-permute-start | bytes 5160968 | tf_op jit(solution)/shard_map/ppermute | solution.py:68
  324.2 23.4 %collective-permute-start.28 = (bf16[160,1536]{1,0:T(8,128)(2,1)S(1)}, bf16[160,1536]{1,0:T(8,128)(2,1)S(1)}, u32[]{:S(2)}, u32[]{:S(2)}) collective-permute-start(bf16[160,1536]{1,0:T(8,128)(2,1)S(1)} %copy-done.71), channel_id=1, source_target_pairs={{0,2},{1,3},{2,0},{3,1},{4,6},{5,7},{6,4},{7,5},{8,10},{9,11},{10,... | collective-permute-start | bytes 1474568 | tf_op jit(solution)/shard_map/ppermute | solution.py:68
  351.9 236.2 %all-gather.7.cloned.1.call-start = ((), (), s32[]{:S(2)}) async-start(), calls=%async_computation.6 | async-start | bytes 7741440 | tf_op jit(solution)/shard_map/all_gather | solution.py:1037
  356.4 24.7 %collective-permute-start.30 = (bf16[160,1536]{1,0:T(8,128)(2,1)S(1)}, bf16[160,1536]{1,0:T(8,128)(2,1)S(1)}, u32[]{:S(2)}, u32[]{:S(2)}) collective-permute-start(bf16[160,1536]{1,0:T(8,128)(2,1)S(1)} %copy-done.70), channel_id=1, source_target_pairs={{0,2},{1,3},{2,0},{3,1},{4,6},{5,7},{6,4},{7,5},{8,10},{9,11},{10,... | collective-permute-start | bytes 1474568 | tf_op jit(solution)/shard_map/ppermute | solution.py:68
  358.9 22.3 %collective-permute-start.29 = (bf16[4,48,2240]{2,1,0:T(8,128)(2,1)S(1)}, bf16[4,48,2240]{2,1,0:T(8,128)(2,1)}, u32[]{:S(2)}, u32[]{:S(2)}) collective-permute-start(bf16[4,48,2240]{2,1,0:T(8,128)(2,1)S(1)} %fusion.3), channel_id=1, source_target_pairs={{0,16},{4,12},{8,24},{12,4},{16,0},{20,28},{24,8},{28,20},{1,17},{... | collective-permute-start | bytes 2580488 | tf_op jit(solution)/shard_map/ppermute | solution.py:68
  404.9 23.1 %collective-permute-start.35 = (bf16[2,4,48,1536]{3,2,1,0:T(8,128)(2,1)}, bf16[2,4,48,1536]{3,2,1,0:T(8,128)(2,1)}, u32[]{:S(2)}, u32[]{:S(2)}) collective-permute-start(bf16[2,4,48,1536]{3,2,1,0:T(8,128)(2,1)} %fusion.12), channel_id=1, source_target_pairs={{0,8},{4,20},{8,0},{12,28},{16,24},{20,4},{24,16},{28,12},{1,9},{5... | collective-permute-start | bytes 3538952 | tf_op jit(solution)/shard_map/ppermute | solution.py:68
  428.0 28.5 %collective-permute-start.39 = (bf16[2,2,4,48,2048]{4,3,2,1,0:T(8,128)(2,1)}, bf16[2,2,4,48,2048]{4,3,2,1,0:T(8,128)(2,1)}, u32[]{:S(2)}, u32[]{:S(2)}) collective-permute-start(bf16[2,2,4,48,2048]{4,3,2,1,0:T(8,128)(2,1)} %bitcast.230), channel_id=1, source_target_pairs={{0,4},{4,0},{8,12},{12,8},{16,20},{20,16},{24,28},{28,24},{1,5},{5... | collective-permute-start | bytes 9437192 | tf_op jit(solution)/shard_map/ppermute | solution.py:68
  430.5 25.1 %collective-permute-start.40 = (bf16[4,48,1536]{2,1,0:T(8,128)(2,1)}, bf16[4,48,1536]{2,1,0:T(8,128)(2,1)}, u32[]{:S(2)}, u32[]{:S(2)}) collective-permute-start(bf16[4,48,1536]{2,1,0:T(8,128)(2,1)} %fusion.15), channel_id=1, source_target_pairs={{0,16},{4,12},{8,24},{12,4},{16,0},{20,28},{24,8},{28,20},{1,17},{... | collective-permute-start | bytes 1769480 | tf_op jit(solution)/shard_map/ppermute | solution.py:68
  461.3 39.2 %collective-permute-start.44 = (bf16[2,48,8960]{2,1,0:T(8,128)(2,1)}, bf16[2,48,8960]{2,1,0:T(8,128)(2,1)}, u32[]{:S(2)}, u32[]{:S(2)}) collective-permute-start(bf16[2,48,8960]{2,1,0:T(8,128)(2,1)} %pad_maximum_fusion.5), channel_id=1, source_target_pairs={{0,8},{4,20},{8,0},{12,28},{16,24},{20,4},{24,16},{28,12},{1,9},{5... | collective-permute-start | bytes 5160968 | tf_op jit(solution)/shard_map/ppermute | solution.py:68
  462.1 38.3 %collective-permute-start.43 = (bf16[2,4,48,2048]{3,2,1,0:T(8,128)(2,1)}, bf16[2,4,48,2048]{3,2,1,0:T(8,128)(2,1)}, u32[]{:S(2)}, u32[]{:S(2)}) collective-permute-start(bf16[2,4,48,2048]{3,2,1,0:T(8,128)(2,1)} %fusion.4), channel_id=1, source_target_pairs={{0,8},{4,20},{8,0},{12,28},{16,24},{20,4},{24,16},{28,12},{1,9},{5... | collective-permute-start | bytes 4718600 | tf_op jit(solution)/shard_map/ppermute | solution.py:68
  508.9 30.5 %collective-permute-start.50 = (bf16[4,48,8960]{2,1,0:T(8,128)(2,1)}, bf16[4,48,8960]{2,1,0:T(8,128)(2,1)}, u32[]{:S(2)}, u32[]{:S(2)}) collective-permute-start(bf16[4,48,8960]{2,1,0:T(8,128)(2,1)} %pad_maximum_fusion.pieces_ref), channel_id=1, source_target_pairs={{0,4},{4,0},{8,12},{12,8},{16,20},{20,16},{24,28},{28,24},{1,5},{5... | collective-permute-start | bytes 10321928 | tf_op jit(solution)/shard_map/ppermute | solution.py:68
  509.0 30.5 %collective-permute-start.49 = (bf16[48,8960]{1,0:T(8,128)(2,1)S(1)}, bf16[48,8960]{1,0:T(8,128)(2,1)S(1)}, u32[]{:S(2)}, u32[]{:S(2)}) collective-permute-start(bf16[48,8960]{1,0:T(8,128)(2,1)S(1)} %concatenate.72), channel_id=1, source_target_pairs={{0,16},{4,12},{8,24},{12,4},{16,0},{20,28},{24,8},{28,20},{1,17},{... | collective-permute-start | bytes 2580488 | tf_op jit(solution)/shard_map/ppermute | solution.py:68
  509.9 29.6 %collective-permute-start.48 = (bf16[4,48,2048]{2,1,0:T(8,128)(2,1)}, bf16[4,48,2048]{2,1,0:T(8,128)(2,1)S(1)}, u32[]{:S(2)}, u32[]{:S(2)}) collective-permute-start(bf16[4,48,2048]{2,1,0:T(8,128)(2,1)} %fusion.7), channel_id=1, source_target_pairs={{0,16},{4,12},{8,24},{12,4},{16,0},{20,28},{24,8},{28,20},{1,17},{... | collective-permute-start | bytes 2359304 | tf_op jit(solution)/shard_map/ppermute | solution.py:68
  544.1 36.4 %collective-permute-start.54 = (bf16[2,48,8960]{2,1,0:T(8,128)(2,1)}, bf16[2,48,8960]{2,1,0:T(8,128)(2,1)}, u32[]{:S(2)}, u32[]{:S(2)}) collective-permute-start(bf16[2,48,8960]{2,1,0:T(8,128)(2,1)} %pad_maximum_fusion.6), channel_id=1, source_target_pairs={{0,8},{4,20},{8,0},{12,28},{16,24},{20,4},{24,16},{28,12},{1,9},{5... | collective-permute-start | bytes 5160968 | tf_op jit(solution)/shard_map/ppermute | solution.py:68
  544.5 36.0 %all-to-all-start = ((bf16[4,48,1536]{2,1,0:T(8,128)(2,1)}), bf16[4,48,1536]{2,1,0:T(8,128)(2,1)}, u32[]{:S(2)}, u32[]{:S(2)}) async-start(bf16[4,48,1536]{2,1,0:T(8,128)(2,1)} %fusion.14), calls=%async_computation.2 | async-start | bytes 1179648 | tf_op jit(solution)/shard_map/all_to_all | solution.py:1061
  552.5 26.7 %collective-permute-start.52 = (bf16[48,2048]{1,0:T(8,128)(2,1)S(1)}, bf16[48,2048]{1,0:T(8,128)(2,1)S(1)}, u32[]{:S(2)}, u32[]{:S(2)}) collective-permute-start(bf16[48,2048]{1,0:T(8,128)(2,1)S(1)} %get-tuple-element.798), channel_id=1, source_target_pairs={{0,2},{1,3},{2,0},{3,1},{4,6},{5,7},{6,4},{7,5},{8,10},{9,11},{10,... | collective-permute-start | bytes 589832 | tf_op jit(solution)/shard_map/ppermute | solution.py:68
  554.9 24.3 %collective-permute-start.53 = (bf16[48,2048]{1,0:T(8,128)(2,1)S(1)}, bf16[48,2048]{1,0:T(8,128)(2,1)S(1)}, u32[]{:S(2)}, u32[]{:S(2)}) collective-permute-start(bf16[48,2048]{1,0:T(8,128)(2,1)S(1)} %get-tuple-element.799), channel_id=1, source_target_pairs={{0,3},{1,0},{2,1},{3,2},{4,7},{5,4},{6,5},{7,6},{8,11},{9,8},{10,9... | collective-permute-start | bytes 589832 | tf_op jit(solution)/shard_map/ppermute | solution.py:68
  (122 other events, 1571.6 us)
Sparse Core Ops, SparseCore 0:
  11.5 104.2 all-gather.8
  118.2 79.3 all-gather.4
  261.3 76.7 reduce-scatter.2
  352.0 68.8 reduce-scatter.4
  509.1 61.3 all-gather.6

commit v15 on v10

--- a/solution.py
+++ b/solution.py
@@ -428,6 +428,52 @@
         cost_estimate=COST,
         name="widen_pieces",
     )(places, pieces, others)
+    return (result.reshape(reps * rows, columns),)
+
+
+def widen_gathered(gathered, order):
+    reps, rows, columns = gathered.shape
+    strip = next(size for size in (16, 8, rows) if rows % size == 0)
+
+    def body(source_ref, out_ref, narrow, wide, in_sems, out_sems):
+        loads = [
+            pltpu.make_async_copy(source_ref.at[r], narrow.at[r], in_sems.at[r])
+            for r in range(reps)
+        ]
+        stores = [
+            pltpu.make_async_copy(wide.at[r], out_ref.at[order[r]], out_sems.at[r])
+            for r in range(reps)
+        ]
+        for load in loads:
+            load.start()
+        for r in range(reps):
+            loads[r].wait()
+
+            def convert(at, carry):
+                cut = pl.ds(pl.multiple_of(at * strip, strip), strip)
+                wide[r, cut, :] = narrow[r, cut, :].astype(jnp.float32)
+                return carry
+
+            lax.fori_loop(0, rows // strip, convert, 0)
+            stores[r].start()
+        for store in stores:
+            store.wait()
+
+    result = pl.pallas_call(
+        body,
+        out_shape=jax.ShapeDtypeStruct((reps, rows, columns), jnp.float32),
+        in_specs=[pl.BlockSpec(memory_space=pl.ANY)],
+        out_specs=pl.BlockSpec(memory_space=pl.ANY),
+        scratch_shapes=[
+            pltpu.VMEM((reps, rows, columns), jnp.bfloat16),
+            pltpu.VMEM((reps, rows, columns), jnp.float32),
+            pltpu.SemaphoreType.DMA((reps,)),
+            pltpu.SemaphoreType.DMA((reps,)),
+        ],
+        compiler_params=pltpu.CompilerParams(vmem_limit_bytes=VMEM_LIMIT),
+        cost_estimate=COST,
+        name="widen_gathered",
+    )(gathered)
     return (result.reshape(reps * rows, columns),)
 
 
@@ -945,9 +991,21 @@
     edges = sorted({0, shards - 2})
     inside = list(range(1, shards - 2))
 
+    def gather_rep(piece):
+        return lax.all_gather(piece[None], "rep", axis=0, tiled=True)
+
     up_halves = split_halves(turned_normed, d_up, shards, True)
 
     up = Halving(clock, *up_halves, core, first, second)
+    (gate_blocks,) = clock.run(
+        lambda left, right: ordered_gradient(left, right, shards, rep_places(reps)),
+        turned_normed,
+        d_gate,
+    )
+    (up_arrived,) = clock.wait(up.moving)
+
+    gate_piece = sum_over_rep(clock(gate_blocks)[0].reshape(width, block_units))
+    up.along_first(up_arrived)
     normed_own, *normed_partial = clock.run(
         lambda *operands: rows_product(operands[:2], operands[2:], True, shards),
         d_gate,
@@ -955,30 +1013,19 @@
         gate_matrix,
         up_matrix,
     )
-    (up_arrived,) = clock.wait(up.moving)
-
-    up.along_first(up_arrived)
     normed_moving = send_some(normed_partial, edges)
-    (gate_blocks,) = clock.run(
-        lambda left, right: ordered_gradient(left, right, shards, rep_places(reps)),
-        turned_normed,
-        d_gate,
-    )
-    gate_piece = sum_over_rep(gate_blocks.reshape(width, block_units))
-    (down_blocks,) = clock.run(
-        lambda left, right: ordered_gradient(left, right, 1, list(range(reps))),
-        turned_inner,
-        cotangents,
-    )
+    down_halves = split_halves(turned_inner, cotangents, 1, True)
     up_arrived, normed_arrived = clock.wait(up.moving, normed_moving)
 
     up.along_second(up_arrived)
+    down = Halving(clock, *down_halves, core, first, second)
     normed_moving = send_some(normed_partial, inside)
     block_own, *block_partial = clock.run(
         lambda left, right: rows_product((left,), (right,), False, shards), inner_act, down_weight
     )
-    up_arrived, more_arrived = clock.wait(up.moving, normed_moving)
-
+    up_arrived, down_arrived, more_arrived = clock.wait(up.moving, down.moving, normed_moving)
+
+    down.along_first(down_arrived)
     up_blocks = clock(*blocks_of(up.finish(up_arrived)))
     up_moving = send_blocks(up_blocks)
     normed_two_gradient = total_of([normed_own] + normed_arrived + more_arrived)
@@ -999,16 +1046,21 @@
         key_marks.T,
     )
     output_halves = split_halves(attention_low, branch_gradient, shards, False)
-    (up_rows,) = clock.wait(up_moving)
+    down_arrived, up_rows = clock.wait(down.moving, up_moving)
 
     pair_moving = send_back(pair_partial)
     output = Halving(clock, *output_halves, core, first, second)
+    down.along_second(down_arrived)
     up_piece = side_by_side(up_blocks[:1] + up_rows)
-    pair_arrived, output_arrived = clock.wait(pair_moving, output.moving)
-
-    up_spread = spread(up_piece)
+    pair_arrived, output_arrived, down_arrived = clock.wait(
+        pair_moving, output.moving, down.moving
+    )
+
+    (gate_piece,) = clock(gate_piece)
+    down_gathered = gather_rep(down.finish(down_arrived)[0])
     output.along_first(output_arrived)
-    block_moving = send_some(block_partial, inside)
+    gate_blocks = clock(*blocks_of(gate_piece.reshape(shards, part_rows, block_units)))
+    gate_moving = send_blocks(gate_blocks)
     projected_gradient, bias_sum = clock.run(
         lambda *operands: join_projected(operands[0], operands[3:], *operands[1:3]),
         d_queries,
@@ -1018,16 +1070,12 @@
         *pair_arrived,
     )
     projected_halves = split_halves(normed_one, projected_gradient, shards, False)
-    up_arrived, output_arrived, block_arrived = clock.wait(
-        up_spread.moving, output.moving, block_moving
-    )
+    output_arrived, gate_rows = clock.wait(output.moving, gate_moving)
 
     projected = Halving(clock, *projected_halves, core, first, second)
     output.along_second(output_arrived)
-    up_spread.along(up_arrived)
-    block_moving = send_some(block_partial, edges)
-    (gate_piece,) = clock(gate_piece)
-    down_piece = sum_over_rep(clock(down_blocks)[0].reshape(block_units, width))
+    gate_spread = spread(side_by_side(gate_blocks[:1] + gate_rows))
+    block_moving = send_some(block_partial, edges[:1])
     projected_gradient, hidden_gradient = clock(projected_gradient, hidden_gradient)
     normed_one_gradient = times_transposed(projected_gradient, input_matrix)
     gain_one_gradient = jnp.sum(normed_one_gradient * unit_one, axis=0)
@@ -1036,16 +1084,14 @@
             hidden_gradient + norm_back(normed_one_gradient, unit_one, inverse_one, gain_one)
         ).astype(bf16)
     )
-    projected_arrived, output_arrived, more_arrived = clock.wait(
-        projected.moving, output.moving, block_moving
-    )
-    block_arrived = block_arrived + more_arrived
+    projected_arrived, output_arrived, gate_arrived, block_arrived = clock.wait(
+        projected.moving, output.moving, gate_spread.moving, block_moving
+    )
 
     projected.along_first(projected_arrived)
-    gate_blocks = clock(*blocks_of(gate_piece.reshape(shards, part_rows, block_units)))
-    gate_moving = send_blocks(gate_blocks)
+    gate_spread.along(gate_arrived)
     output_blocks = clock(*blocks_of(output.finish(output_arrived)))
-    (block_out,) = clock(total_of([hidden, block_own] + block_arrived).astype(bf16))
+    output_moving = send_blocks(output_blocks)
     bias_gradient = bias_sum[0]
     bias_split = query_width + pair_width
     small_parts = (
@@ -1057,59 +1103,56 @@
     (small,) = clock(
         jnp.concatenate([part.reshape(shards, -1) for part in small_parts], axis=1)
     )
-    projected_arrived, up_arrived, gate_rows = clock.wait(
-        projected.moving, up_spread.moving, gate_moving
-    )
-
-    projected.along_second(projected_arrived)
-    gate_spread = spread(side_by_side(gate_blocks[:1] + gate_rows))
-    output_moving = send_blocks(output_blocks)
     projected_arrived, gate_arrived, output_rows = clock.wait(
         projected.moving, gate_spread.moving, output_moving
     )
 
+    projected.along_second(projected_arrived)
+    gate_spread.over(gate_arrived)
+    output_spread = spread(row_sum(output_blocks[:1], output_rows))
+    block_moving = send_some(block_partial, inside)
+    (down_gathered,) = clock(down_gathered)
+    up_gathered = gather_rep(clock(up_piece)[0])
+    projected_arrived, gate_arrived, output_arrived, more_arrived = clock.wait(
+        projected.moving, gate_spread.moving, output_spread.moving, block_moving
+    )
+    block_arrived = block_arrived + more_arrived
+
     input_blocks = clock(*blocks_of(projected.finish(projected_arrived)))
     input_moving = send_blocks(input_blocks)
-    gate_spread.along(gate_arrived)
-    output_spread = spread(row_sum(output_blocks[:1], output_rows))
-    input_rows, gate_arrived, output_arrived = clock.wait(
-        input_moving, gate_spread.moving, output_spread.moving
-    )
+    output_spread.along(output_arrived)
+    (gate_total,) = clock.run(widen_pieces, *gate_spread.finish(gate_arrived))
+    input_rows, output_arrived = clock.wait(input_moving, output_spread.moving)
 
     input_spread = spread(row_sum(input_blocks[:1], input_rows))
-    output_spread.along(output_arrived)
-    up_spread.over(up_arrived)
-    gate_spread.over(gate_arrived)
+    output_spread.over(output_arrived)
     small_moving = clock.send(core, [small], [1])
-    (down_piece,) = clock(down_piece)
-    down_gathered = lax.all_gather(down_piece, "rep", axis=0, tiled=True)
-    input_arrived, output_arrived, up_arrived, gate_arrived, small_arrived = clock.wait(
-        input_spread.moving, output_spread.moving, up_spread.moving, gate_spread.moving, small_moving
+    block_moving = send_some(block_partial, edges[1:])
+    (down_total,) = clock.run(lambda gathered: widen_gathered(gathered, rep_places(reps)), down_gathered)
+    input_arrived, output_arrived, small_arrived, more_arrived = clock.wait(
+        input_spread.moving, output_spread.moving, small_moving, block_moving
     )
     small = total_of([small] + small_arrived)
+    block_arrived = block_arrived + more_arrived
 
     input_spread.along(input_arrived)
-    output_spread.over(output_arrived)
     small_moving = clock.send(first, [small] * (first.size - 1), range(1, first.size))
-    (up_total,) = clock.run(widen_pieces, *up_spread.finish(up_arrived))
-    input_arrived, output_arrived, small_arrived = clock.wait(
-        input_spread.moving, output_spread.moving, small_moving
-    )
+    (output_total,) = clock.run(widen_pieces, *output_spread.finish(output_arrived))
+    (block_out,) = clock(total_of([hidden, block_own] + block_arrived).astype(bf16))
+    input_arrived, small_arrived = clock.wait(input_spread.moving, small_moving)
     small = total_of([small] + small_arrived)
 
     input_spread.over(input_arrived)
     small_moving = clock.send(second, [small] * (second.size - 1), range(1, second.size))
-    (gate_total,) = clock.run(widen_pieces, *gate_spread.finish(gate_arrived))
     input_arrived, small_arrived = clock.wait(input_spread.moving, small_moving)
     small_blocks = clock(*blocks_of(total_of([small] + small_arrived)))
 
     small_moving = send_blocks(small_blocks)
-    (output_total,) = clock.run(widen_pieces, *output_spread.finish(output_arrived))
     (input_total,) = clock.run(widen_pieces, *input_spread.finish(input_arrived))
+    (up_gathered,) = clock(up_gathered)
+    (up_total,) = clock.run(lambda gathered: widen_gathered(gathered, rep_places(reps)), up_gathered)
     (small_arrived,) = clock.wait(small_moving)
     small = total_of(small_blocks[:1] + small_arrived)
-    (down_gathered,) = clock(down_gathered)
-    (down_total,) = clock(down_gathered.astype(f32))
 
     small = small + clock.token[0, 0]
     small_totals, at = [], 0

time: 632 us -> 632 us (level)
    pallas_call x0 -> x2, Pallas kernels: none -> 13.8 us  [widen_gathered(): pl.pallas_call(body, out_shape=jax.ShapeDtypeStruct((reps, rows, columns)...]
    convert_element_type x1 -> x0, other arithmetic: 10.2 us -> none  [on_device(): down_total, = clock(down_gathered.astype(f32))]
    pallas_call x2 -> x1, Pallas kernels: 19.2 us -> 10.1 us  [ordered_gradient(): pl.pallas_call(body, grid=(pl.cdiv(columns, TILE),), out_shape=[jax.Shape...]
    pallas_call x3 -> x4, Pallas kernels: 20 us -> 28.8 us  [split_gradient(): pl.pallas_call(body, grid=(pl.cdiv(columns, TILE),), out_shape=[jax.Shape...]
    pallas_call x4 -> x3, Pallas kernels: 21.3 us -> 13.9 us  [widen_pieces(): pl.pallas_call(body, out_shape=jax.ShapeDtypeStruct((reps, rows, columns)...]
    convert_element_type x6 -> x8, other arithmetic: 17.3 us -> 23.7 us  [along(): total_of([pick(term, line.ahead(step), 0) for term in self.terms])]
  transfers between devices with their start and end apart: 77 -> 77, of which waited for: 35 -> 28; matrix products, arithmetic and copies ran while one was open for 14% -> 15% of each run, Pallas kernels for 18% -> 19%
where the time goes in v15:
time: 632 us; the launch traced here: 622 us
  waiting for transfers between devices  225 us (36%)
  Pallas kernels  149 us (24%)
  starting transfers between devices  128 us (20%)
  other arithmetic  63.1 us (10%)
  local copies, waits for them, and re-layouts  26.3 us (4%)
  matrix products  15.6 us (2%)
  between operations  15.5 us (2%)
    ppermute x66, waiting for transfers between devices, shift(): return lax.ppermute(value, self.name, self.pairs(step % self.size))  216 us
    ppermute x66, starting transfers between devices, shift(): return lax.ppermute(value, self.name, self.pairs(step % self.size))  102 us
    pallas_call x4, Pallas kernels, split_gradient(): pl.pallas_call(body, grid=(pl.cdiv(columns, TILE),), out_shape=[jax.Shape...  28.8 us
    ppermute x6, starting transfers between devices, pass_on(): return lax.ppermute(value, self.name, pairs)  25.2 us
    convert_element_type x8, other arithmetic, along(): total_of([pick(term, line.ahead(step), 0) for term in self.terms])  23.7 us
    pallas_call x1, Pallas kernels, feed_forward(): pl.pallas_call(body, grid=(steps,), out_shape=[jax.ShapeDtypeStruct((coun...  23.7 us
    pallas_call x2, Pallas kernels, rows_product(): pl.pallas_call(body, grid=(pl.cdiv(columns, TILE),), out_shape=[jax.Shape...  23.2 us
    pallas_call x3, Pallas kernels, widen_pieces(): pl.pallas_call(body, out_shape=jax.ShapeDtypeStruct((reps, rows, columns)...  13.9 us
  transfers between devices with their start and end apart: 77, of which 28 were waited for; matrix products, arithmetic and copies ran while one was open for 15% of the time, Pallas kernels for 19%

profile of v15, /device:TPU:0, one launch (start us, length us, event | category | flops | bytes accessed | tf_op | source)
XLA Modules:
  0.0 622.1 jit_solution(3744303629715188653)
XLA Ops:
  32.1 6.5 %collective-permute-start.4 = (bf16[48,2240]{1,0:T(8,128)(2,1)}, bf16[48,2240]{1,0:T(8,128)(2,1)S(1)}, u32[]{:S(2)}, u32[]{:S(2)}) collective-permute-start(bf16[48,2240]{1,0:T(8,128)(2,1)} %get-tuple-element.489), channel_id=1, source_target_pairs={{0,1},{1,2},{2,3},{3,0},{4,5},{5,6},{6,7},{7,4},{8,9},{9,10},{10,1... | collective-permute-start | bytes 645128 | tf_op jit(solution)/shard_map/ppermute | solution.py:68
  41.1 6.3 %collective-permute-done.4 = bf16[48,2240]{1,0:T(8,128)(2,1)S(1)} collective-permute-done((bf16[48,2240]{1,0:T(8,128)(2,1)}, bf16[48,2240]{1,0:T(8,128)(2,1)S(1)}, u32[]{:S(2)}, u32[]{:S(2)}) %collective-permute-start.4) | collective-permute-done | bytes 215072 | tf_op jit(solution)/shard_map/ppermute | solution.py:68
  47.4 13.8 %collective-permute-done.5 = bf16[48,2240]{1,0:T(8,128)(2,1)S(1)} collective-permute-done((bf16[48,2240]{1,0:T(8,128)(2,1)}, bf16[48,2240]{1,0:T(8,128)(2,1)S(1)}, u32[]{:S(2)}, u32[]{:S(2)}) %collective-permute-start.5) | collective-permute-done | bytes 215072 | tf_op jit(solution)/shard_map/ppermute | solution.py:68
  63.8 5.8 collective-permute-start.8
  72.9 7.6 %collective-permute-done.8 = bf16[48,2240]{1,0:T(8,128)(2,1)S(1)} collective-permute-done((bf16[48,2240]{1,0:T(8,128)(2,1)S(1)}, bf16[48,2240]{1,0:T(8,128)(2,1)S(1)}, u32[]{:S(2)}, u32[]{:S(2)}) %collective-permute-start.8) | collective-permute-done | bytes 215072 | tf_op jit(solution)/shard_map/ppermute | solution.py:68
  80.5 17.3 %collective-permute-done.9 = bf16[48,2240]{1,0:T(8,128)(2,1)S(1)} collective-permute-done((bf16[48,2240]{1,0:T(8,128)(2,1)S(1)}, bf16[48,2240]{1,0:T(8,128)(2,1)S(1)}, u32[]{:S(2)}, u32[]{:S(2)}) %collective-permute-start.9) | collective-permute-done | bytes 215072 | tf_op jit(solution)/shard_map/ppermute | solution.py:68
  105.4 14.6 %collective-permute-start.11 = (bf16[160,1536]{1,0:T(8,128)(2,1)S(1)}, bf16[160,1536]{1,0:T(8,128)(2,1)}, u32[]{:S(2)}, u32[]{:S(2)}) collective-permute-start(bf16[160,1536]{1,0:T(8,128)(2,1)S(1)} %copy-done.18), channel_id=1, source_target_pairs={{0,1},{1,2},{2,3},{4,5},{5,6},{6,7},{8,9},{9,10},{10,11},{12,13},{... | collective-permute-start | bytes 1474568 | tf_op jit(solution)/shard_map/ppermute | solution.py:73
  146.0 8.9 %collective-permute-done.14 = bf16[160,512]{1,0:T(8,128)(2,1)S(1)} collective-permute-done((bf16[160,512]{1,0:T(8,128)(2,1)S(1)}, bf16[160,512]{1,0:T(8,128)(2,1)S(1)}, u32[]{:S(2)}, u32[]{:S(2)}) %collective-permute-start.14) | collective-permute-done | bytes 163872 | tf_op jit(solution)/shard_map/ppermute | solution.py:68
  155.0 8.0 %collective-permute-done.15 = bf16[160,512]{1,0:T(8,128)(2,1)} collective-permute-done((bf16[160,512]{1,0:T(8,128)(2,1)S(1)}, bf16[160,512]{1,0:T(8,128)(2,1)}, u32[]{:S(2)}, u32[]{:S(2)}) %collective-permute-start.15) | collective-permute-done | bytes 163872 | tf_op jit(solution)/shard_map/ppermute | solution.py:68
  176.5 5.8 attention_forward.1
  195.2 11.7 %place_blocks.3 = (bf16[4,8,48,2240]{3,2,1,0:T(8,128)(2,1)}, bf16[4,8,48,2240]{3,2,1,0:T(8,128)(2,1)}) custom-call(s32[4]{0:T(128)} %pad_add_fusion.5.order_ref, bf16[64,48,2240]{2,1,0:T(8,128)(2,1)} %all-gather.7.cloned.1.call-done.source), custom_call_target="tpu_custom_call" | custom-call | flops 1 | bytes 1 | tf_op jit(solution)/shard_map/place_blocks/pallas_call | solution.py:339
  206.8 15.1 %collective-permute-done.22 = bf16[160,1536]{1,0:T(8,128)(2,1)} collective-permute-done((bf16[160,1536]{1,0:T(8,128)(2,1)S(1)}, bf16[160,1536]{1,0:T(8,128)(2,1)}, u32[]{:S(2)}, u32[]{:S(2)}) %collective-permute-start.22) | collective-permute-done | bytes 491552 | tf_op jit(solution)/shard_map/ppermute | solution.py:68
  224.7 23.7 %feed_forward.1 = (bf16[640,2240]{1,0:T(8,128)(2,1)}, bf16[640,2240]{1,0:T(8,128)(2,1)}, bf16[640,2240]{1,0:T(8,128)(2,1)}, bf16[1536,640]{1,0:T(8,128)(2,1)}, bf16[2240,640]{1,0:T(8,128)(2,1)}) custom-call(bf16[640,1536]{1,0:T(8,128)(2,1)} %pad_maximum_fusion.2.rows_ref, bf16[640,1536]{1,0:T(8,128)(2,1)} %pad_maximum_fusion.3.cotangents_ref.right_ref, ...), custom_call_target="tpu_custom_call" | custom-call | flops 1 | bytes 1 | tf_op jit(solution)/shard_map/feed_forward/pallas_call | solution.py:523
  248.4 10.0 %split_gradient.4 = (bf16[4,4,48,2240]{3,2,1,0:T(8,128)(2,1)}, bf16[4,4,48,2240]{3,2,1,0:T(8,128)(2,1)}) custom-call(s32[1]{0:T(128)} %bitcast.46.core_ref, bf16[1536,640]{1,0:T(8,128)(2,1)} %get-tuple-element.610.left_ref, bf16[640,2240]{1,0:T(8,128)(2,1)} %get-tuple-element.622.right_ref.refs_1_), custom_call_target="tpu_custom_call" | custom-call | flops 1 | bytes 1 | tf_op jit(solution)/shard_map/split_gradient/pallas_call | solution.py:579
  258.4 10.1 %ordered_gradient.1 = bf16[8,4,48,2240]{3,2,1,0:T(8,128)(2,1)} custom-call(bf16[1536,640]{1,0:T(8,128)(2,1)} %get-tuple-element.610.left_ref, bf16[640,2240]{1,0:T(8,128)(2,1)} %get-tuple-element.621.right_ref.refs_0_), custom_call_target="tpu_custom_call" | custom-call | flops 1 | bytes 1 | tf_op jit(solution)/shard_map/ordered_gradient/pallas_call | solution.py:609
  271.6 14.6 %rows_product.2 = (bf16[160,1536]{1,0:T(8,128)(2,1)}, bf16[160,1536]{1,0:T(8,128)(2,1)}, bf16[160,1536]{1,0:T(8,128)(2,1)}, bf16[160,1536]{1,0:T(8,128)(2,1)}) custom-call(bf16[640,2240]{1,0:T(8,128)(2,1)} %get-tuple-element.621.right_ref.refs_0_, bf16[640,2240]{1,0:T(8,128)(2,1)} %get-tuple-element.622.right_ref.refs_1_, bf16[1536,2240]{1,0:T(8,128)(2,1)} %bitcast.202, ...), custom_call_target="tpu_custom_call" | custom-call | flops 1 | bytes 1 | tf_op jit(solution)/shard_map/rows_product/pallas_call | solution.py:649
  286.2 11.8 %collective-permute-start.26 = (bf16[160,1536]{1,0:T(8,128)(2,1)}, bf16[160,1536]{1,0:T(8,128)(2,1)S(1)}, u32[]{:S(2)}, u32[]{:S(2)}) collective-permute-start(bf16[160,1536]{1,0:T(8,128)(2,1)} %get-tuple-element.641), channel_id=1, source_target_pairs={{0,3},{1,0},{2,1},{3,2},{4,7},{5,4},{6,5},{7,6},{8,11},{9,8},{10,9... | collective-permute-start | bytes 1474568 | tf_op jit(solution)/shard_map/ppermute | solution.py:68
  298.0 8.9 %split_gradient.5 = (bf16[4,1,280,1536]{3,2,1,0:T(8,128)(2,1)}, bf16[4,1,280,1536]{3,2,1,0:T(8,128)(2,1)}) custom-call(s32[1]{0:T(128)} %bitcast.46.core_ref, bf16[2240,640]{1,0:T(8,128)(2,1)} %get-tuple-element.635.left_ref, bf16[640,1536]{1,0:T(8,128)(2,1)} %pad_maximum_fusion.3.cotangents_ref.right_ref), custom_call_target="tpu_custom_call" | custom-call | flops 1 | bytes 1 | tf_op jit(solution)/shard_map/split_gradient/pallas_call | solution.py:579
  310.0 10.7 %collective-permute-done.27 = bf16[160,1536]{1,0:T(8,128)(2,1)S(1)} collective-permute-done((bf16[160,1536]{1,0:T(8,128)(2,1)}, bf16[160,1536]{1,0:T(8,128)(2,1)S(1)}, u32[]{:S(2)}, u32[]{:S(2)}) %collective-permute-start.27) | collective-permute-done | bytes 491552 | tf_op jit(solution)/shard_map/ppermute | solution.py:68
  328.4 8.6 %rows_product.3 = (bf16[160,1536]{1,0:T(8,128)(2,1)}, bf16[160,1536]{1,0:T(8,128)(2,1)}, bf16[160,1536]{1,0:T(8,128)(2,1)}, bf16[160,1536]{1,0:T(8,128)(2,1)}) custom-call(bf16[640,2240]{1,0:T(8,128)(2,1)} %get-tuple-element.652.refs_0_, bf16[2240,1536]{1,0:T(8,128)(2,1)} %refs_1_), custom_call_target="tpu_custom_call" | custom-call | flops 1 | bytes 1 | tf_op jit(solution)/shard_map/rows_product/pallas_call | solution.py:649
  337.0 11.7 %collective-permute-done.30 = bf16[160,1536]{1,0:T(8,128)(2,1)S(1)} collective-permute-done((bf16[160,1536]{1,0:T(8,128)(2,1)S(1)}, bf16[160,1536]{1,0:T(8,128)(2,1)S(1)}, u32[]{:S(2)}, u32[]{:S(2)}) %collective-permute-start.30) | collective-permute-done | bytes 491552 | tf_op jit(solution)/shard_map/ppermute | solution.py:68
  365.7 7.5 %attention_backward.1 = (bf16[160,1536]{1,0:T(8,128)(2,1)}, bf16[160,512]{1,0:T(8,128)(2,1)}, bf16[160,512]{1,0:T(8,128)(2,1)}, bf16[160,512]{1,0:T(8,128)(2,1)}, bf16[160,512]{1,0:T(8,128)(2,1)}) custom-call(bf16[2,960,128]{2,1,0:T(8,128)(2,1)} %get-tuple-element.684.queries_ref, bf16[160,1536]{1,0:T(8,128)(2,1)} %convolution_convert_fusion.gradient_ref, ...), custom_call_target="tpu_custom_call" | custom-call | flops 1 | bytes 1 | tf_op jit(solution)/shard_map/attention_backward/pallas_call | solution.py:751
  389.7 12.3 %collective-permute-done.36.refs_2_ = bf16[160,512]{1,0:T(8,128)(2,1)} collective-permute-done((bf16[160,512]{1,0:T(8,128)(2,1)}, bf16[160,512]{1,0:T(8,128)(2,1)}, u32[]{:S(2)}, u32[]{:S(2)}) %collective-permute-start.36) | collective-permute-done | bytes 163872 | tf_op jit(solution)/shard_map/ppermute | solution.py:68
  421.2 7.2 %collective-permute-done.42 = bf16[48,2240]{1,0:T(8,128)(2,1)S(1)} collective-permute-done((bf16[48,2240]{1,0:T(8,128)(2,1)}, bf16[48,2240]{1,0:T(8,128)(2,1)S(1)}, u32[]{:S(2)}, u32[]{:S(2)}) %collective-permute-start.42) | collective-permute-done | bytes 215072 | tf_op jit(solution)/shard_map/ppermute | solution.py:68
  448.0 11.9 %collective-permute-done.47 = bf16[160,1536]{1,0:T(8,128)(2,1)S(1)} collective-permute-done((bf16[160,1536]{1,0:T(8,128)(2,1)S(1)}, bf16[160,1536]{1,0:T(8,128)(2,1)S(1)}, u32[]{:S(2)}, u32[]{:S(2)}) %collective-permute-start.47) | collective-permute-done | bytes 491552 | tf_op jit(solution)/shard_map/ppermute | solution.py:68
  459.9 9.2 %collective-permute-done.46 = bf16[48,8960]{1,0:T(8,128)(2,1)S(1)} collective-permute-done((bf16[48,8960]{1,0:T(8,128)(2,1)S(1)}, bf16[48,8960]{1,0:T(8,128)(2,1)S(1)}, u32[]{:S(2)}, u32[]{:S(2)}) %collective-permute-start.46) | collective-permute-done | bytes 860192 | tf_op jit(solution)/shard_map/ppermute | solution.py:68
  492.5 20.7 %collective-permute-done.48 = bf16[2,4,48,2048]{3,2,1,0:T(8,128)(2,1)} collective-permute-done((bf16[2,4,48,2048]{3,2,1,0:T(8,128)(2,1)}, bf16[2,4,48,2048]{3,2,1,0:T(8,128)(2,1)}, u32[]{:S(2)}, u32[]{:S(2)}) %collective-permute-start.48) | collective-permute-done | bytes 1572896 | tf_op jit(solution)/shard_map/ppermute | solution.py:68
  524.9 15.1 %collective-permute-done.55 = bf16[48,1536]{1,0:T(8,128)(2,1)S(1)} collective-permute-done((bf16[48,1536]{1,0:T(8,128)(2,1)S(1)}, bf16[48,1536]{1,0:T(8,128)(2,1)S(1)}, u32[]{:S(2)}, u32[]{:S(2)}) %collective-permute-start.55) | collective-permute-done | bytes 147488 | tf_op jit(solution)/shard_map/ppermute | solution.py:68
  540.0 6.2 %collective-permute-done.56 = bf16[160,1536]{1,0:T(8,128)(2,1)S(1)} collective-permute-done((bf16[160,1536]{1,0:T(8,128)(2,1)}, bf16[160,1536]{1,0:T(8,128)(2,1)S(1)}, u32[]{:S(2)}, u32[]{:S(2)}) %collective-permute-start.56) | collective-permute-done | bytes 491552 | tf_op jit(solution)/shard_map/ppermute | solution.py:68
  554.9 7.4 %widen_pieces.3 = f32[8,48,8960]{2,1,0:T(8,128)} custom-call(s32[8]{0:T(128)} %stack.219.places_ref, bf16[4,48,8960]{2,1,0:T(8,128)(2,1)} %pad_maximum_fusion.pieces_ref, bf16[4,48,8960]{2,1,0:T(8,128)(2,1)} %copy-done.8), custom_call_target="tpu_custom_call" | custom-call | flops 1 | bytes 1 | tf_op jit(solution)/shard_map/widen_pieces/pallas_call | solution.py:415
  574.4 6.6 %widen_gathered.2 = f32[8,280,1536]{2,1,0:T(8,128)} custom-call(bf16[8,280,1536]{2,1,0:T(8,128)(2,1)} %all-gather.9.cloned.1.call-done.source_ref), custom_call_target="tpu_custom_call" | custom-call | flops 1 | bytes 1 | tf_op jit(solution)/shard_map/widen_gathered/pallas_call | solution.py:462
  605.0 7.2 %widen_gathered.3 = f32[8,48,8960]{2,1,0:T(8,128)} custom-call(bf16[8,48,8960]{2,1,0:T(8,128)(2,1)} %bitcast.213), custom_call_target="tpu_custom_call" | custom-call | flops 1 | bytes 1 | tf_op jit(solution)/shard_map/widen_gathered/pallas_call | solution.py:462
  (372 shorter events, 263.9 us)
Async XLA Ops:
  7.2 114.1 %all-gather.11.cloned.1.call-start = ((), (), s32[]{:S(2)}) async-start(), calls=%async_computation.4 | async-start | bytes 6488064 | tf_op jit(solution)/shard_map/all_gather | solution.py:842
  9.3 185.8 %all-gather.7.cloned.1.call-start = ((), (), s32[]{:S(2)}) async-start(), calls=%async_computation.1 | async-start | bytes 15925248 | tf_op jit(solution)/shard_map/all_gather | solution.py:907
  29.9 31.4 %collective-permute-start.3 = (bf16[1,4,48,1536]{3,2,1,0:T(8,128)(2,1)S(1)}, bf16[1,4,48,1536]{3,2,1,0:T(8,128)(2,1)S(1)}, u32[]{:S(2)}, u32[]{:S(2)}) collective-permute-start(bf16[1,4,48,1536]{3,2,1,0:T(8,128)(2,1)S(1)} %get-tuple-element.488), channel_id=1, source_target_pairs={{0,16},{4,12},{8,24},{12,4},{16,0},{20,28},{24,8},{28,20},{1,17},{... | collective-permute-start | bytes 1769480 | tf_op jit(solution)/shard_map/ppermute | solution.py:68
  61.4 36.4 %collective-permute-start.7 = (bf16[2,1,4,48,1536]{4,3,2,1,0:T(8,128)(2,1)S(1)}, bf16[2,1,4,48,1536]{4,3,2,1,0:T(8,128)(2,1)S(1)}, u32[]{:S(2)}, u32[]{:S(2)}) collective-permute-start(bf16[2,1,4,48,1536]{4,3,2,1,0:T(8,128)(2,1)S(1)} %pad_maximum_fusion.5), channel_id=1, source_target_pairs={{0,8},{4,20},{8,0},{12,28},{16,24},{20,4},{24,16},{28,12},{1,9},{5... | collective-permute-start | bytes 3538952 | tf_op jit(solution)/shard_map/ppermute | solution.py:68
  69.5 28.3 %collective-permute-start.9 = (bf16[48,2240]{1,0:T(8,128)(2,1)S(1)}, bf16[48,2240]{1,0:T(8,128)(2,1)S(1)}, u32[]{:S(2)}, u32[]{:S(2)}) collective-permute-start(bf16[48,2240]{1,0:T(8,128)(2,1)S(1)} %get-tuple-element.499), channel_id=1, source_target_pairs={{0,2},{1,3},{2,0},{3,1},{4,6},{5,7},{6,4},{7,5},{8,10},{9,11},{10,... | collective-permute-start | bytes 645128 | tf_op jit(solution)/shard_map/ppermute | solution.py:68
  72.2 25.6 %collective-permute-start.10 = (bf16[48,2240]{1,0:T(8,128)(2,1)S(1)}, bf16[48,2240]{1,0:T(8,128)(2,1)S(1)}, u32[]{:S(2)}, u32[]{:S(2)}) collective-permute-start(bf16[48,2240]{1,0:T(8,128)(2,1)S(1)} %get-tuple-element.500), channel_id=1, source_target_pairs={{0,3},{1,0},{2,1},{3,2},{4,7},{5,4},{6,5},{7,6},{8,11},{9,8},{10,9... | collective-permute-start | bytes 645128 | tf_op jit(solution)/shard_map/ppermute | solution.py:68
  102.4 302.9 %reduce-scatter.2.cloned.1.call-start = ((), (), s32[]{:S(2)}) async-start(), calls=%async_computation.2 | async-start | bytes 7962624 | tf_op jit(solution)/shard_map/reduce_scatter | solution.py:983
  105.4 29.9 %collective-permute-start.13 = (bf16[4,1,4,48,1536]{4,3,2,1,0:T(8,128)(2,1)}, bf16[4,1,4,48,1536]{4,3,2,1,0:T(8,128)(2,1)}, u32[]{:S(2)}, u32[]{:S(2)}) collective-permute-start(bf16[4,1,4,48,1536]{4,3,2,1,0:T(8,128)(2,1)} %pad_maximum_fusion.1.pieces_ref), channel_id=1, source_target_pairs={{0,4},{4,0},{8,12},{12,8},{16,20},{20,16},{24,28},{28,24},{1,5},{5... | collective-permute-start | bytes 7077896 | tf_op jit(solution)/shard_map/ppermute | solution.py:68
  105.4 24.8 %collective-permute-start.11 = (bf16[160,1536]{1,0:T(8,128)(2,1)S(1)}, bf16[160,1536]{1,0:T(8,128)(2,1)}, u32[]{:S(2)}, u32[]{:S(2)}) collective-permute-start(bf16[160,1536]{1,0:T(8,128)(2,1)S(1)} %copy-done.18), channel_id=1, source_target_pairs={{0,1},{1,2},{2,3},{4,5},{5,6},{6,7},{8,9},{9,10},{10,11},{12,13},{... | collective-permute-start | bytes 1474568 | tf_op jit(solution)/shard_map/ppermute | solution.py:73
  135.2 27.7 %collective-permute-start.17 = (bf16[160,1536]{1,0:T(8,128)(2,1)}, bf16[160,1536]{1,0:T(8,128)(2,1)}, u32[]{:S(2)}, u32[]{:S(2)}) collective-permute-start(bf16[160,1536]{1,0:T(8,128)(2,1)} %collective-permute-done.11), channel_id=1, source_target_pairs={{0,1},{1,2},{2,3},{4,5},{5,6},{6,7},{8,9},{9,10},{10,11},{12,13},{... | collective-permute-start | bytes 1474568 | tf_op jit(solution)/shard_map/ppermute | solution.py:73
  137.4 25.5 %collective-permute-start.18 = (bf16[160,1536]{1,0:T(8,128)(2,1)}, bf16[160,1536]{1,0:T(8,128)(2,1)}, u32[]{:S(2)}, u32[]{:S(2)}) collective-permute-start(bf16[160,1536]{1,0:T(8,128)(2,1)} %collective-permute-done.12), channel_id=1, source_target_pairs={{1,0},{2,1},{3,2},{5,4},{6,5},{7,6},{9,8},{10,9},{11,10},{13,12},{... | collective-permute-start | bytes 1474568 | tf_op jit(solution)/shard_map/ppermute | solution.py:73
  163.0 24.2 %collective-permute-start.19 = (bf16[160,1536]{1,0:T(8,128)(2,1)}, bf16[160,1536]{1,0:T(8,128)(2,1)S(1)}, u32[]{:S(2)}, u32[]{:S(2)}) collective-permute-start(bf16[160,1536]{1,0:T(8,128)(2,1)} %collective-permute-done.17), channel_id=1, source_target_pairs={{0,1},{1,2},{2,3},{4,5},{5,6},{6,7},{8,9},{9,10},{10,11},{12,13},{... | collective-permute-start | bytes 1474568 | tf_op jit(solution)/shard_map/ppermute | solution.py:73
  190.0 32.0 %collective-permute-start.22 = (bf16[160,1536]{1,0:T(8,128)(2,1)S(1)}, bf16[160,1536]{1,0:T(8,128)(2,1)}, u32[]{:S(2)}, u32[]{:S(2)}) collective-permute-start(bf16[160,1536]{1,0:T(8,128)(2,1)S(1)} %multiply_convert_fusion), channel_id=1, source_target_pairs={{0,2},{1,3},{2,0},{3,1},{4,6},{5,7},{6,4},{7,5},{8,10},{9,11},{10,... | collective-permute-start | bytes 1474568 | tf_op jit(solution)/shard_map/ppermute | solution.py:68
  190.0 32.0 %collective-permute-start.23 = (bf16[160,1536]{1,0:T(8,128)(2,1)S(1)}, bf16[160,1536]{1,0:T(8,128)(2,1)}, u32[]{:S(2)}, u32[]{:S(2)}) collective-permute-start(bf16[160,1536]{1,0:T(8,128)(2,1)S(1)} %multiply_convert_fusion), channel_id=1, source_target_pairs={{0,3},{1,0},{2,1},{3,2},{4,7},{5,4},{6,5},{7,6},{8,11},{9,8},{10,9... | collective-permute-start | bytes 1474568 | tf_op jit(solution)/shard_map/ppermute | solution.py:68
  271.5 49.2 %collective-permute-start.25 = (bf16[2,4,48,2240]{3,2,1,0:T(8,128)(2,1)}, bf16[2,4,48,2240]{3,2,1,0:T(8,128)(2,1)}, u32[]{:S(2)}, u32[]{:S(2)}) collective-permute-start(bf16[2,4,48,2240]{3,2,1,0:T(8,128)(2,1)} %fusion), channel_id=1, source_target_pairs={{0,8},{4,20},{8,0},{12,28},{16,24},{20,4},{24,16},{28,12},{1,9},{5... | collective-permute-start | bytes 5160968 | tf_op jit(solution)/shard_map/ppermute | solution.py:68
  271.6 248.7 %all-gather.9.cloned.1.call-start = ((), (), s32[]{:S(2)}) async-start(), calls=%async_computation.3 | async-start | bytes 7741440 | tf_op jit(solution)/shard_map/all_gather | solution.py:995
  286.2 23.8 %collective-permute-start.26 = (bf16[160,1536]{1,0:T(8,128)(2,1)}, bf16[160,1536]{1,0:T(8,128)(2,1)S(1)}, u32[]{:S(2)}, u32[]{:S(2)}) collective-permute-start(bf16[160,1536]{1,0:T(8,128)(2,1)} %get-tuple-element.641), channel_id=1, source_target_pairs={{0,3},{1,0},{2,1},{3,2},{4,7},{5,4},{6,5},{7,6},{8,11},{9,8},{10,9... | collective-permute-start | bytes 1474568 | tf_op jit(solution)/shard_map/ppermute | solution.py:68
  323.7 25.1 %collective-permute-start.29 = (bf16[2,2,1,280,1536]{4,3,2,1,0:T(8,128)(2,1)}, bf16[2,2,1,280,1536]{4,3,2,1,0:T(8,128)(2,1)}, u32[]{:S(2)}, u32[]{:S(2)}) collective-permute-start(bf16[2,2,1,280,1536]{4,3,2,1,0:T(8,128)(2,1)} %bitcast.53), channel_id=1, source_target_pairs={{0,4},{4,0},{8,12},{12,8},{16,20},{20,16},{24,28},{28,24},{1,5},{5... | collective-permute-start | bytes 10321928 | tf_op jit(solution)/shard_map/ppermute | solution.py:68
  323.7 25.0 %collective-permute-start.28 = (bf16[4,48,2240]{2,1,0:T(8,128)(2,1)}, bf16[4,48,2240]{2,1,0:T(8,128)(2,1)}, u32[]{:S(2)}, u32[]{:S(2)}) collective-permute-start(bf16[4,48,2240]{2,1,0:T(8,128)(2,1)} %fusion.3), channel_id=1, source_target_pairs={{0,16},{4,12},{8,24},{12,4},{16,0},{20,28},{24,8},{28,20},{1,17},{... | collective-permute-start | bytes 2580488 | tf_op jit(solution)/shard_map/ppermute | solution.py:68
  324.4 24.4 %collective-permute-start.30 = (bf16[160,1536]{1,0:T(8,128)(2,1)S(1)}, bf16[160,1536]{1,0:T(8,128)(2,1)S(1)}, u32[]{:S(2)}, u32[]{:S(2)}) collective-permute-start(bf16[160,1536]{1,0:T(8,128)(2,1)S(1)} %copy-done.41), channel_id=1, source_target_pairs={{0,2},{1,3},{2,0},{3,1},{4,6},{5,7},{6,4},{7,5},{8,10},{9,11},{10,... | collective-permute-start | bytes 1474568 | tf_op jit(solution)/shard_map/ppermute | solution.py:68
  354.6 23.2 %collective-permute-start.31 = (bf16[2,1,280,1536]{3,2,1,0:T(8,128)(2,1)}, bf16[2,1,280,1536]{3,2,1,0:T(8,128)(2,1)}, u32[]{:S(2)}, u32[]{:S(2)}) collective-permute-start(bf16[2,1,280,1536]{3,2,1,0:T(8,128)(2,1)} %bitcast.64), channel_id=1, source_target_pairs={{0,8},{4,20},{8,0},{12,28},{16,24},{20,4},{24,16},{28,12},{1,9},{5... | collective-permute-start | bytes 5160968 | tf_op jit(solution)/shard_map/ppermute | solution.py:68
  377.8 24.2 %collective-permute-start.38 = (bf16[2,2,4,48,1536]{4,3,2,1,0:T(8,128)(2,1)}, bf16[2,2,4,48,1536]{4,3,2,1,0:T(8,128)(2,1)}, u32[]{:S(2)}, u32[]{:S(2)}) collective-permute-start(bf16[2,2,4,48,1536]{4,3,2,1,0:T(8,128)(2,1)} %bitcast.256), channel_id=1, source_target_pairs={{0,4},{4,0},{8,12},{12,8},{16,20},{20,16},{24,28},{28,24},{1,5},{5... | collective-permute-start | bytes 7077896 | tf_op jit(solution)/shard_map/ppermute | solution.py:68
  405.3 199.7 %all-gather.13.cloned.1.call-start = ((), (), s32[]{:S(2)}) async-start(), calls=%async_computation.5 | async-start | bytes 7741440 | tf_op jit(solution)/shard_map/all_gather | solution.py:995
  408.4 25.7 %collective-permute-start.40 = (bf16[2,4,48,1536]{3,2,1,0:T(8,128)(2,1)}, bf16[2,4,48,1536]{3,2,1,0:T(8,128)(2,1)}, u32[]{:S(2)}, u32[]{:S(2)}) collective-permute-start(bf16[2,4,48,1536]{3,2,1,0:T(8,128)(2,1)} %fusion.16), channel_id=1, source_target_pairs={{0,8},{4,20},{8,0},{12,28},{16,24},{20,4},{24,16},{28,12},{1,9},{5... | collective-permute-start | bytes 3538952 | tf_op jit(solution)/shard_map/ppermute | solution.py:68
  434.1 35.1 %collective-permute-start.44 = (bf16[2,2,4,48,2048]{4,3,2,1,0:T(8,128)(2,1)}, bf16[2,2,4,48,2048]{4,3,2,1,0:T(8,128)(2,1)}, u32[]{:S(2)}, u32[]{:S(2)}) collective-permute-start(bf16[2,2,4,48,2048]{4,3,2,1,0:T(8,128)(2,1)} %bitcast.255), channel_id=1, source_target_pairs={{0,4},{4,0},{8,12},{12,8},{16,20},{20,16},{24,28},{28,24},{1,5},{5... | collective-permute-start | bytes 9437192 | tf_op jit(solution)/shard_map/ppermute | solution.py:68
  436.6 23.4 %collective-permute-start.45 = (bf16[4,48,1536]{2,1,0:T(8,128)(2,1)}, bf16[4,48,1536]{2,1,0:T(8,128)(2,1)}, u32[]{:S(2)}, u32[]{:S(2)}) collective-permute-start(bf16[4,48,1536]{2,1,0:T(8,128)(2,1)} %fusion.19), channel_id=1, source_target_pairs={{0,16},{4,12},{8,24},{12,4},{16,0},{20,28},{24,8},{28,20},{1,17},{... | collective-permute-start | bytes 1769480 | tf_op jit(solution)/shard_map/ppermute | solution.py:68
  439.8 29.4 %collective-permute-start.46 = (bf16[48,8960]{1,0:T(8,128)(2,1)S(1)}, bf16[48,8960]{1,0:T(8,128)(2,1)S(1)}, u32[]{:S(2)}, u32[]{:S(2)}) collective-permute-start(bf16[48,8960]{1,0:T(8,128)(2,1)S(1)} %concatenate.68), channel_id=1, source_target_pairs={{0,16},{4,12},{8,24},{12,4},{16,0},{20,28},{24,8},{28,20},{1,17},{... | collective-permute-start | bytes 2580488 | tf_op jit(solution)/shard_map/ppermute | solution.py:68
  474.0 39.2 %collective-permute-start.49 = (bf16[2,48,8960]{2,1,0:T(8,128)(2,1)}, bf16[2,48,8960]{2,1,0:T(8,128)(2,1)}, u32[]{:S(2)}, u32[]{:S(2)}) collective-permute-start(bf16[2,48,8960]{2,1,0:T(8,128)(2,1)} %pad_maximum_fusion.4), channel_id=1, source_target_pairs={{0,8},{4,20},{8,0},{12,28},{16,24},{20,4},{24,16},{28,12},{1,9},{5... | collective-permute-start | bytes 5160968 | tf_op jit(solution)/shard_map/ppermute | solution.py:68
  475.5 37.7 %collective-permute-start.48 = (bf16[2,4,48,2048]{3,2,1,0:T(8,128)(2,1)}, bf16[2,4,48,2048]{3,2,1,0:T(8,128)(2,1)}, u32[]{:S(2)}, u32[]{:S(2)}) collective-permute-start(bf16[2,4,48,2048]{3,2,1,0:T(8,128)(2,1)} %fusion.8), channel_id=1, source_target_pairs={{0,8},{4,20},{8,0},{12,28},{16,24},{20,4},{24,16},{28,12},{1,9},{5... | collective-permute-start | bytes 4718600 | tf_op jit(solution)/shard_map/ppermute | solution.py:68
  520.3 26.0 %collective-permute-start.54 = (bf16[4,48,8960]{2,1,0:T(8,128)(2,1)}, bf16[4,48,8960]{2,1,0:T(8,128)(2,1)S(1)}, u32[]{:S(2)}, u32[]{:S(2)}) collective-permute-start(bf16[4,48,8960]{2,1,0:T(8,128)(2,1)} %pad_maximum_fusion.pieces_ref), channel_id=1, source_target_pairs={{0,4},{4,0},{8,12},{12,8},{16,20},{20,16},{24,28},{28,24},{1,5},{5... | collective-permute-start | bytes 10321928 | tf_op jit(solution)/shard_map/ppermute | solution.py:68
  520.4 25.9 %collective-permute-start.53 = (bf16[4,48,2048]{2,1,0:T(8,128)(2,1)}, bf16[4,48,2048]{2,1,0:T(8,128)(2,1)S(1)}, u32[]{:S(2)}, u32[]{:S(2)}) collective-permute-start(bf16[4,48,2048]{2,1,0:T(8,128)(2,1)} %fusion.11), channel_id=1, source_target_pairs={{0,16},{4,12},{8,24},{12,4},{16,0},{20,28},{24,8},{28,20},{1,17},{... | collective-permute-start | bytes 2359304 | tf_op jit(solution)/shard_map/ppermute | solution.py:68
  520.8 25.4 %collective-permute-start.56 = (bf16[160,1536]{1,0:T(8,128)(2,1)}, bf16[160,1536]{1,0:T(8,128)(2,1)S(1)}, u32[]{:S(2)}, u32[]{:S(2)}) collective-permute-start(bf16[160,1536]{1,0:T(8,128)(2,1)} %get-tuple-element.828), channel_id=1, source_target_pairs={{0,2},{1,3},{2,0},{3,1},{4,6},{5,7},{6,4},{7,5},{8,10},{9,11},{10,... | collective-permute-start | bytes 1474568 | tf_op jit(solution)/shard_map/ppermute | solution.py:68
  (89 other events, 1358.2 us)
Sparse Core Ops, SparseCore 0:
  11.5 99.7 all-gather.10
  113.8 74.9 all-gather.6
  271.7 76.1 reduce-scatter.1
  405.4 56.8 all-gather.8
  520.4 54.1 all-gather.12

commit v16 on v15

--- a/solution.py
+++ b/solution.py
@@ -1058,9 +1058,6 @@
 
     (gate_piece,) = clock(gate_piece)
     down_gathered = gather_rep(down.finish(down_arrived)[0])
-    output.along_first(output_arrived)
-    gate_blocks = clock(*blocks_of(gate_piece.reshape(shards, part_rows, block_units)))
-    gate_moving = send_blocks(gate_blocks)
     projected_gradient, bias_sum = clock.run(
         lambda *operands: join_projected(operands[0], operands[3:], *operands[1:3]),
         d_queries,
@@ -1070,12 +1067,11 @@
         *pair_arrived,
     )
     projected_halves = split_halves(normed_one, projected_gradient, shards, False)
-    output_arrived, gate_rows = clock.wait(output.moving, gate_moving)
 
     projected = Halving(clock, *projected_halves, core, first, second)
-    output.along_second(output_arrived)
-    gate_spread = spread(side_by_side(gate_blocks[:1] + gate_rows))
-    block_moving = send_some(block_partial, edges[:1])
+    output.along_first(output_arrived)
+    gate_blocks = clock(*blocks_of(gate_piece.reshape(shards, part_rows, block_units)))
+    gate_moving = send_blocks(gate_blocks)
     projected_gradient, hidden_gradient = clock(projected_gradient, hidden_gradient)
     normed_one_gradient = times_transposed(projected_gradient, input_matrix)
     gain_one_gradient = jnp.sum(normed_one_gradient * unit_one, axis=0)
@@ -1084,14 +1080,14 @@
             hidden_gradient + norm_back(normed_one_gradient, unit_one, inverse_one, gain_one)
         ).astype(bf16)
     )
-    projected_arrived, output_arrived, gate_arrived, block_arrived = clock.wait(
-        projected.moving, output.moving, gate_spread.moving, block_moving
+    projected_arrived, output_arrived, gate_rows = clock.wait(
+        projected.moving, output.moving, gate_moving
     )
 
     projected.along_first(projected_arrived)
-    gate_spread.along(gate_arrived)
-    output_blocks = clock(*blocks_of(output.finish(output_arrived)))
-    output_moving = send_blocks(output_blocks)
+    output.along_second(output_arrived)
+    gate_spread = spread(side_by_side(gate_blocks[:1] + gate_rows))
+    block_moving = send_some(block_partial, inside)
     bias_gradient = bias_sum[0]
     bias_split = query_width + pair_width
     small_parts = (
@@ -1103,30 +1099,42 @@
     (small,) = clock(
         jnp.concatenate([part.reshape(shards, -1) for part in small_parts], axis=1)
     )
+    projected_arrived, output_arrived, gate_arrived, block_arrived = clock.wait(
+        projected.moving, output.moving, gate_spread.moving, block_moving
+    )
+
+    projected.along_second(projected_arrived)
+    gate_spread.along(gate_arrived)
+    output_blocks = clock(*blocks_of(output.finish(output_arrived)))
+    output_moving = send_blocks(output_blocks)
+    (down_gathered,) = clock(down_gathered)
+    up_gathered = gather_rep(clock(up_piece)[0])
     projected_arrived, gate_arrived, output_rows = clock.wait(
         projected.moving, gate_spread.moving, output_moving
     )
 
-    projected.along_second(projected_arrived)
-    gate_spread.over(gate_arrived)
-    output_spread = spread(row_sum(output_blocks[:1], output_rows))
-    block_moving = send_some(block_partial, inside)
-    (down_gathered,) = clock(down_gathered)
-    up_gathered = gather_rep(clock(up_piece)[0])
-    projected_arrived, gate_arrived, output_arrived, more_arrived = clock.wait(
-        projected.moving, gate_spread.moving, output_spread.moving, block_moving
-    )
-    block_arrived = block_arrived + more_arrived
-
     input_blocks = clock(*blocks_of(projected.finish(projected_arrived)))
     input_moving = send_blocks(input_blocks)
+    output_spread = spread(row_sum(output_blocks[:1], output_rows))
+    gate_spread.over(gate_arrived)
+    input_rows, output_arrived, gate_arrived = clock.wait(
+        input_moving, output_spread.moving, gate_spread.moving
+    )
+
+    input_spread = spread(row_sum(input_blocks[:1], input_rows))
     output_spread.along(output_arrived)
+    small_moving = clock.send(core, [small], [1])
+    block_moving = send_some(block_partial, edges[:1])
     (gate_total,) = clock.run(widen_pieces, *gate_spread.finish(gate_arrived))
-    input_rows, output_arrived = clock.wait(input_moving, output_spread.moving)
-
-    input_spread = spread(row_sum(input_blocks[:1], input_rows))
+    input_arrived, output_arrived, small_arrived, more_arrived = clock.wait(
+        input_spread.moving, output_spread.moving, small_moving, block_moving
+    )
+    small = total_of([small] + small_arrived)
+    block_arrived = block_arrived + more_arrived
+
+    input_spread.along(input_arrived)
     output_spread.over(output_arrived)
-    small_moving = clock.send(core, [small], [1])
+    small_moving = clock.send(first, [small] * (first.size - 1), range(1, first.size))
     block_moving = send_some(block_partial, edges[1:])
     (down_total,) = clock.run(lambda gathered: widen_gathered(gathered, rep_places(reps)), down_gathered)
     input_arrived, output_arrived, small_arrived, more_arrived = clock.wait(
@@ -1135,22 +1143,17 @@
     small = total_of([small] + small_arrived)
     block_arrived = block_arrived + more_arrived
 
-    input_spread.along(input_arrived)
-    small_moving = clock.send(first, [small] * (first.size - 1), range(1, first.size))
+    input_spread.over(input_arrived)
+    small_moving = clock.send(second, [small] * (second.size - 1), range(1, second.size))
     (output_total,) = clock.run(widen_pieces, *output_spread.finish(output_arrived))
     (block_out,) = clock(total_of([hidden, block_own] + block_arrived).astype(bf16))
     input_arrived, small_arrived = clock.wait(input_spread.moving, small_moving)
-    small = total_of([small] + small_arrived)
-
-    input_spread.over(input_arrived)
-    small_moving = clock.send(second, [small] * (second.size - 1), range(1, second.size))
-    input_arrived, small_arrived = clock.wait(input_spread.moving, small_moving)
     small_blocks = clock(*blocks_of(total_of([small] + small_arrived)))
 
     small_moving = send_blocks(small_blocks)
-    (input_total,) = clock.run(widen_pieces, *input_spread.finish(input_arrived))
     (up_gathered,) = clock(up_gathered)
     (up_total,) = clock.run(lambda gathered: widen_gathered(gathered, rep_places(reps)), up_gathered)
+    (input_total,) = clock.run(widen_pieces, *input_spread.finish(input_arrived))
     (small_arrived,) = clock.wait(small_moving)
     small = total_of(small_blocks[:1] + small_arrived)
 

time: 632 us -> 629 us (level)
  waiting for transfers between devices: 225 us -> 234 us
  other arithmetic: 63.1 us -> 54.8 us
    ppermute x66, waiting for transfers between devices: 216 us -> 225 us  [shift(): return lax.ppermute(value, self.name, self.pairs(step % self.size))]
  transfers between devices with their start and end apart: 77 -> 77, of which waited for: 28 -> 29; matrix products, arithmetic and copies ran while one was open for 15% -> 13% of each run, Pallas kernels for 19% -> 19%
where the time goes in v16:
time: 629 us; the launch traced here: 620 us
  waiting for transfers between devices  234 us (37%)
  Pallas kernels  149 us (24%)
  starting transfers between devices  127 us (20%)
  other arithmetic  54.8 us (9%)
  local copies, waits for them, and re-layouts  24.8 us (4%)
  between operations  15.5 us (2%)
  matrix products  15.4 us (2%)
    ppermute x66, waiting for transfers between devices, shift(): return lax.ppermute(value, self.name, self.pairs(step % self.size))  225 us
    ppermute x66, starting transfers between devices, shift(): return lax.ppermute(value, self.name, self.pairs(step % self.size))  101 us
    pallas_call x4, Pallas kernels, split_gradient(): pl.pallas_call(body, grid=(pl.cdiv(columns, TILE),), out_shape=[jax.Shape...  29.1 us
    ppermute x6, starting transfers between devices, pass_on(): return lax.ppermute(value, self.name, pairs)  25.2 us
    pallas_call x1, Pallas kernels, feed_forward(): pl.pallas_call(body, grid=(steps,), out_shape=[jax.ShapeDtypeStruct((coun...  23.6 us
    pallas_call x2, Pallas kernels, rows_product(): pl.pallas_call(body, grid=(pl.cdiv(columns, TILE),), out_shape=[jax.Shape...  23.2 us
    convert_element_type x8, other arithmetic, along(): total_of([pick(term, line.ahead(step), 0) for term in self.terms])  21.4 us
    pallas_call x3, Pallas kernels, widen_pieces(): pl.pallas_call(body, out_shape=jax.ShapeDtypeStruct((reps, rows, columns)...  14 us
  transfers between devices with their start and end apart: 77, of which 29 were waited for; matrix products, arithmetic and copies ran while one was open for 13% of the time, Pallas kernels for 19%

profile of v16, /device:TPU:0, one launch (start us, length us, event | category | flops | bytes accessed | tf_op | source)
XLA Modules:
  0.0 619.7 jit_solution(3565076227553306188)
XLA Ops:
  32.1 6.5 %collective-permute-start.4 = (bf16[48,2240]{1,0:T(8,128)(2,1)}, bf16[48,2240]{1,0:T(8,128)(2,1)S(1)}, u32[]{:S(2)}, u32[]{:S(2)}) collective-permute-start(bf16[48,2240]{1,0:T(8,128)(2,1)} %get-tuple-element.488), channel_id=1, source_target_pairs={{0,1},{1,2},{2,3},{3,0},{4,5},{5,6},{6,7},{7,4},{8,9},{9,10},{10,1... | collective-permute-start | bytes 645128 | tf_op jit(solution)/shard_map/ppermute | solution.py:68
  41.1 6.3 %collective-permute-done.4 = bf16[48,2240]{1,0:T(8,128)(2,1)S(1)} collective-permute-done((bf16[48,2240]{1,0:T(8,128)(2,1)}, bf16[48,2240]{1,0:T(8,128)(2,1)S(1)}, u32[]{:S(2)}, u32[]{:S(2)}) %collective-permute-start.4) | collective-permute-done | bytes 215072 | tf_op jit(solution)/shard_map/ppermute | solution.py:68
  47.4 13.9 %collective-permute-done.5 = bf16[48,2240]{1,0:T(8,128)(2,1)S(1)} collective-permute-done((bf16[48,2240]{1,0:T(8,128)(2,1)}, bf16[48,2240]{1,0:T(8,128)(2,1)S(1)}, u32[]{:S(2)}, u32[]{:S(2)}) %collective-permute-start.5) | collective-permute-done | bytes 215072 | tf_op jit(solution)/shard_map/ppermute | solution.py:68
  63.8 5.8 collective-permute-start.8
  72.9 7.6 %collective-permute-done.8 = bf16[48,2240]{1,0:T(8,128)(2,1)S(1)} collective-permute-done((bf16[48,2240]{1,0:T(8,128)(2,1)S(1)}, bf16[48,2240]{1,0:T(8,128)(2,1)S(1)}, u32[]{:S(2)}, u32[]{:S(2)}) %collective-permute-start.8) | collective-permute-done | bytes 215072 | tf_op jit(solution)/shard_map/ppermute | solution.py:68
  80.5 17.2 %collective-permute-done.9 = bf16[48,2240]{1,0:T(8,128)(2,1)S(1)} collective-permute-done((bf16[48,2240]{1,0:T(8,128)(2,1)S(1)}, bf16[48,2240]{1,0:T(8,128)(2,1)S(1)}, u32[]{:S(2)}, u32[]{:S(2)}) %collective-permute-start.9) | collective-permute-done | bytes 215072 | tf_op jit(solution)/shard_map/ppermute | solution.py:68
  105.4 14.6 %collective-permute-start.11 = (bf16[160,1536]{1,0:T(8,128)(2,1)S(1)}, bf16[160,1536]{1,0:T(8,128)(2,1)}, u32[]{:S(2)}, u32[]{:S(2)}) collective-permute-start(bf16[160,1536]{1,0:T(8,128)(2,1)S(1)} %copy-done.17), channel_id=1, source_target_pairs={{0,1},{1,2},{2,3},{4,5},{5,6},{6,7},{8,9},{9,10},{10,11},{12,13},{... | collective-permute-start | bytes 1474568 | tf_op jit(solution)/shard_map/ppermute | solution.py:73
  146.1 8.9 %collective-permute-done.14 = bf16[160,512]{1,0:T(8,128)(2,1)S(1)} collective-permute-done((bf16[160,512]{1,0:T(8,128)(2,1)S(1)}, bf16[160,512]{1,0:T(8,128)(2,1)S(1)}, u32[]{:S(2)}, u32[]{:S(2)}) %collective-permute-start.14) | collective-permute-done | bytes 163872 | tf_op jit(solution)/shard_map/ppermute | solution.py:68
  155.0 8.0 %collective-permute-done.15 = bf16[160,512]{1,0:T(8,128)(2,1)} collective-permute-done((bf16[160,512]{1,0:T(8,128)(2,1)S(1)}, bf16[160,512]{1,0:T(8,128)(2,1)}, u32[]{:S(2)}, u32[]{:S(2)}) %collective-permute-start.15) | collective-permute-done | bytes 163872 | tf_op jit(solution)/shard_map/ppermute | solution.py:68
  195.1 11.7 %place_blocks.3 = (bf16[4,8,48,2240]{3,2,1,0:T(8,128)(2,1)}, bf16[4,8,48,2240]{3,2,1,0:T(8,128)(2,1)}) custom-call(s32[4]{0:T(128)} %pad_add_fusion.5.order_ref, bf16[64,48,2240]{2,1,0:T(8,128)(2,1)} %all-gather.7.cloned.1.call-done.source), custom_call_target="tpu_custom_call" | custom-call | flops 1 | bytes 1 | tf_op jit(solution)/shard_map/place_blocks/pallas_call | solution.py:339
  206.8 15.2 %collective-permute-done.22 = bf16[160,1536]{1,0:T(8,128)(2,1)} collective-permute-done((bf16[160,1536]{1,0:T(8,128)(2,1)S(1)}, bf16[160,1536]{1,0:T(8,128)(2,1)}, u32[]{:S(2)}, u32[]{:S(2)}) %collective-permute-start.22) | collective-permute-done | bytes 491552 | tf_op jit(solution)/shard_map/ppermute | solution.py:68
  224.7 23.6 %feed_forward.1 = (bf16[640,2240]{1,0:T(8,128)(2,1)}, bf16[640,2240]{1,0:T(8,128)(2,1)}, bf16[640,2240]{1,0:T(8,128)(2,1)}, bf16[1536,640]{1,0:T(8,128)(2,1)}, bf16[2240,640]{1,0:T(8,128)(2,1)}) custom-call(bf16[640,1536]{1,0:T(8,128)(2,1)} %pad_maximum_fusion.2.rows_ref, bf16[640,1536]{1,0:T(8,128)(2,1)} %pad_maximum_fusion.3.cotangents_ref.right_ref, ...), custom_call_target="tpu_custom_call" | custom-call | flops 1 | bytes 1 | tf_op jit(solution)/shard_map/feed_forward/pallas_call | solution.py:523
  248.3 10.0 %split_gradient.4 = (bf16[4,4,48,2240]{3,2,1,0:T(8,128)(2,1)}, bf16[4,4,48,2240]{3,2,1,0:T(8,128)(2,1)}) custom-call(s32[1]{0:T(128)} %bitcast.46.core_ref, bf16[1536,640]{1,0:T(8,128)(2,1)} %get-tuple-element.609.left_ref, bf16[640,2240]{1,0:T(8,128)(2,1)} %get-tuple-element.621.right_ref.refs_1_), custom_call_target="tpu_custom_call" | custom-call | flops 1 | bytes 1 | tf_op jit(solution)/shard_map/split_gradient/pallas_call | solution.py:579
  258.4 10.1 %ordered_gradient.1 = bf16[8,4,48,2240]{3,2,1,0:T(8,128)(2,1)} custom-call(bf16[1536,640]{1,0:T(8,128)(2,1)} %get-tuple-element.609.left_ref, bf16[640,2240]{1,0:T(8,128)(2,1)} %get-tuple-element.620.right_ref.refs_0_), custom_call_target="tpu_custom_call" | custom-call | flops 1 | bytes 1 | tf_op jit(solution)/shard_map/ordered_gradient/pallas_call | solution.py:609
  271.6 14.6 %rows_product.2 = (bf16[160,1536]{1,0:T(8,128)(2,1)}, bf16[160,1536]{1,0:T(8,128)(2,1)}, bf16[160,1536]{1,0:T(8,128)(2,1)}, bf16[160,1536]{1,0:T(8,128)(2,1)}) custom-call(bf16[640,2240]{1,0:T(8,128)(2,1)} %get-tuple-element.620.right_ref.refs_0_, bf16[640,2240]{1,0:T(8,128)(2,1)} %get-tuple-element.621.right_ref.refs_1_, bf16[1536,2240]{1,0:T(8,128)(2,1)} %bitcast.202, ...), custom_call_target="tpu_custom_call" | custom-call | flops 1 | bytes 1 | tf_op jit(solution)/shard_map/rows_product/pallas_call | solution.py:649
  286.3 11.7 %collective-permute-start.26 = (bf16[160,1536]{1,0:T(8,128)(2,1)}, bf16[160,1536]{1,0:T(8,128)(2,1)S(1)}, u32[]{:S(2)}, u32[]{:S(2)}) collective-permute-start(bf16[160,1536]{1,0:T(8,128)(2,1)} %get-tuple-element.640), channel_id=1, source_target_pairs={{0,3},{1,0},{2,1},{3,2},{4,7},{5,4},{6,5},{7,6},{8,11},{9,8},{10,9... | collective-permute-start | bytes 1474568 | tf_op jit(solution)/shard_map/ppermute | solution.py:68
  298.0 8.9 %split_gradient.5 = (bf16[4,1,280,1536]{3,2,1,0:T(8,128)(2,1)}, bf16[4,1,280,1536]{3,2,1,0:T(8,128)(2,1)}) custom-call(s32[1]{0:T(128)} %bitcast.46.core_ref, bf16[2240,640]{1,0:T(8,128)(2,1)} %get-tuple-element.634.left_ref, bf16[640,1536]{1,0:T(8,128)(2,1)} %pad_maximum_fusion.3.cotangents_ref.right_ref), custom_call_target="tpu_custom_call" | custom-call | flops 1 | bytes 1 | tf_op jit(solution)/shard_map/split_gradient/pallas_call | solution.py:579
  310.0 10.7 %collective-permute-done.27 = bf16[160,1536]{1,0:T(8,128)(2,1)S(1)} collective-permute-done((bf16[160,1536]{1,0:T(8,128)(2,1)}, bf16[160,1536]{1,0:T(8,128)(2,1)S(1)}, u32[]{:S(2)}, u32[]{:S(2)}) %collective-permute-start.27) | collective-permute-done | bytes 491552 | tf_op jit(solution)/shard_map/ppermute | solution.py:68
  328.4 8.6 %rows_product.3 = (bf16[160,1536]{1,0:T(8,128)(2,1)}, bf16[160,1536]{1,0:T(8,128)(2,1)}, bf16[160,1536]{1,0:T(8,128)(2,1)}, bf16[160,1536]{1,0:T(8,128)(2,1)}) custom-call(bf16[640,2240]{1,0:T(8,128)(2,1)} %get-tuple-element.651.refs_0_, bf16[2240,1536]{1,0:T(8,128)(2,1)} %refs_1_), custom_call_target="tpu_custom_call" | custom-call | flops 1 | bytes 1 | tf_op jit(solution)/shard_map/rows_product/pallas_call | solution.py:649
  337.0 11.7 %collective-permute-done.30 = bf16[160,1536]{1,0:T(8,128)(2,1)S(1)} collective-permute-done((bf16[160,1536]{1,0:T(8,128)(2,1)S(1)}, bf16[160,1536]{1,0:T(8,128)(2,1)S(1)}, u32[]{:S(2)}, u32[]{:S(2)}) %collective-permute-start.30) | collective-permute-done | bytes 491552 | tf_op jit(solution)/shard_map/ppermute | solution.py:68
  364.6 7.5 %attention_backward.1 = (bf16[160,1536]{1,0:T(8,128)(2,1)}, bf16[160,512]{1,0:T(8,128)(2,1)}, bf16[160,512]{1,0:T(8,128)(2,1)}, bf16[160,512]{1,0:T(8,128)(2,1)}, bf16[160,512]{1,0:T(8,128)(2,1)}) custom-call(bf16[2,960,128]{2,1,0:T(8,128)(2,1)} %get-tuple-element.683.queries_ref, bf16[160,1536]{1,0:T(8,128)(2,1)} %convolution_convert_fusion.gradient_ref, ...), custom_call_target="tpu_custom_call" | custom-call | flops 1 | bytes 1 | tf_op jit(solution)/shard_map/attention_backward/pallas_call | solution.py:751
  389.7 11.7 %collective-permute-done.36.refs_2_ = bf16[160,512]{1,0:T(8,128)(2,1)} collective-permute-done((bf16[160,512]{1,0:T(8,128)(2,1)}, bf16[160,512]{1,0:T(8,128)(2,1)}, u32[]{:S(2)}, u32[]{:S(2)}) %collective-permute-start.36) | collective-permute-done | bytes 163872 | tf_op jit(solution)/shard_map/ppermute | solution.py:68
  426.1 7.4 %collective-permute-done.43 = bf16[48,2240]{1,0:T(8,128)(2,1)S(1)} collective-permute-done((bf16[48,2240]{1,0:T(8,128)(2,1)S(1)}, bf16[48,2240]{1,0:T(8,128)(2,1)S(1)}, u32[]{:S(2)}, u32[]{:S(2)}) %collective-permute-start.43) | collective-permute-done | bytes 215072 | tf_op jit(solution)/shard_map/ppermute | solution.py:68
  433.5 7.3 %collective-permute-done.41 = bf16[2,4,48,1536]{3,2,1,0:T(8,128)(2,1)S(1)} collective-permute-done((bf16[2,4,48,1536]{3,2,1,0:T(8,128)(2,1)S(1)}, bf16[2,4,48,1536]{3,2,1,0:T(8,128)(2,1)S(1)}, u32[]{:S(2)}, u32[]{:S(2)}) %collective-permute-start.41) | collective-permute-done | bytes 1179680 | tf_op jit(solution)/shard_map/ppermute | solution.py:68
  451.1 22.3 %collective-permute-done.48 = bf16[160,1536]{1,0:T(8,128)(2,1)S(1)} collective-permute-done((bf16[160,1536]{1,0:T(8,128)(2,1)}, bf16[160,1536]{1,0:T(8,128)(2,1)S(1)}, u32[]{:S(2)}, u32[]{:S(2)}) %collective-permute-start.48) | collective-permute-done | bytes 491552 | tf_op jit(solution)/shard_map/ppermute | solution.py:68
  473.4 12.2 %collective-permute-done.46 = bf16[4,48,1536]{2,1,0:T(8,128)(2,1)} collective-permute-done((bf16[4,48,1536]{2,1,0:T(8,128)(2,1)}, bf16[4,48,1536]{2,1,0:T(8,128)(2,1)}, u32[]{:S(2)}, u32[]{:S(2)}) %collective-permute-start.46) | collective-permute-done | bytes 589856 | tf_op jit(solution)/shard_map/ppermute | solution.py:68
  507.9 15.3 %collective-permute-done.49 = bf16[4,48,2048]{2,1,0:T(8,128)(2,1)S(1)} collective-permute-done((bf16[4,48,2048]{2,1,0:T(8,128)(2,1)}, bf16[4,48,2048]{2,1,0:T(8,128)(2,1)S(1)}, u32[]{:S(2)}, u32[]{:S(2)}) %collective-permute-start.49) | collective-permute-done | bytes 786464 | tf_op jit(solution)/shard_map/ppermute | solution.py:68
  523.2 14.9 %collective-permute-done.50 = bf16[2,48,8960]{2,1,0:T(8,128)(2,1)S(1)} collective-permute-done((bf16[2,48,8960]{2,1,0:T(8,128)(2,1)}, bf16[2,48,8960]{2,1,0:T(8,128)(2,1)S(1)}, u32[]{:S(2)}, u32[]{:S(2)}) %collective-permute-start.50) | collective-permute-done | bytes 1720352 | tf_op jit(solution)/shard_map/ppermute | solution.py:68
  551.3 6.8 %collective-permute-done.55 = bf16[48,2048]{1,0:T(8,128)(2,1)S(1)} collective-permute-done((bf16[48,2048]{1,0:T(8,128)(2,1)S(1)}, bf16[48,2048]{1,0:T(8,128)(2,1)S(1)}, u32[]{:S(2)}, u32[]{:S(2)}) %collective-permute-start.55) | collective-permute-done | bytes 196640 | tf_op jit(solution)/shard_map/ppermute | solution.py:68
  565.8 7.3 %widen_pieces.3 = f32[8,48,8960]{2,1,0:T(8,128)} custom-call(s32[8]{0:T(128)} %stack.219.places_ref, bf16[4,48,8960]{2,1,0:T(8,128)(2,1)} %copy-done.2, bf16[4,48,8960]{2,1,0:T(8,128)(2,1)} %collective-permute-done.58.others_ref), custom_call_target="tpu_custom_call" | custom-call | flops 1 | bytes 1 | tf_op jit(solution)/shard_map/widen_pieces/pallas_call | solution.py:415
  577.9 6.6 %widen_gathered.2 = f32[8,280,1536]{2,1,0:T(8,128)} custom-call(bf16[8,280,1536]{2,1,0:T(8,128)(2,1)} %all-gather.9.cloned.1.call-done.source_ref), custom_call_target="tpu_custom_call" | custom-call | flops 1 | bytes 1 | tf_op jit(solution)/shard_map/widen_gathered/pallas_call | solution.py:462
  599.6 6.6 %widen_gathered.3 = f32[8,48,8960]{2,1,0:T(8,128)} custom-call(bf16[8,48,8960]{2,1,0:T(8,128)(2,1)} %bitcast.213), custom_call_target="tpu_custom_call" | custom-call | flops 1 | bytes 1 | tf_op jit(solution)/shard_map/widen_gathered/pallas_call | solution.py:462
  (376 shorter events, 252.6 us)
Async XLA Ops:
  7.2 114.1 %all-gather.11.cloned.1.call-start = ((), (), s32[]{:S(2)}) async-start(), calls=%async_computation.4 | async-start | bytes 6488064 | tf_op jit(solution)/shard_map/all_gather | solution.py:842
  9.3 185.8 %all-gather.7.cloned.1.call-start = ((), (), s32[]{:S(2)}) async-start(), calls=%async_computation.1 | async-start | bytes 15925248 | tf_op jit(solution)/shard_map/all_gather | solution.py:907
  29.9 31.5 %collective-permute-start.3 = (bf16[1,4,48,1536]{3,2,1,0:T(8,128)(2,1)S(1)}, bf16[1,4,48,1536]{3,2,1,0:T(8,128)(2,1)S(1)}, u32[]{:S(2)}, u32[]{:S(2)}) collective-permute-start(bf16[1,4,48,1536]{3,2,1,0:T(8,128)(2,1)S(1)} %get-tuple-element.487), channel_id=1, source_target_pairs={{0,16},{4,12},{8,24},{12,4},{16,0},{20,28},{24,8},{28,20},{1,17},{... | collective-permute-start | bytes 1769480 | tf_op jit(solution)/shard_map/ppermute | solution.py:68
  38.6 22.8 %collective-permute-start.5 = (bf16[48,2240]{1,0:T(8,128)(2,1)}, bf16[48,2240]{1,0:T(8,128)(2,1)S(1)}, u32[]{:S(2)}, u32[]{:S(2)}) collective-permute-start(bf16[48,2240]{1,0:T(8,128)(2,1)} %get-tuple-element.489), channel_id=1, source_target_pairs={{0,2},{1,3},{2,0},{3,1},{4,6},{5,7},{6,4},{7,5},{8,10},{9,11},{10,... | collective-permute-start | bytes 645128 | tf_op jit(solution)/shard_map/ppermute | solution.py:68
  61.5 36.3 %collective-permute-start.7 = (bf16[2,1,4,48,1536]{4,3,2,1,0:T(8,128)(2,1)S(1)}, bf16[2,1,4,48,1536]{4,3,2,1,0:T(8,128)(2,1)S(1)}, u32[]{:S(2)}, u32[]{:S(2)}) collective-permute-start(bf16[2,1,4,48,1536]{4,3,2,1,0:T(8,128)(2,1)S(1)} %pad_maximum_fusion.5), channel_id=1, source_target_pairs={{0,8},{4,20},{8,0},{12,28},{16,24},{20,4},{24,16},{28,12},{1,9},{5... | collective-permute-start | bytes 3538952 | tf_op jit(solution)/shard_map/ppermute | solution.py:68
  69.6 28.2 %collective-permute-start.9 = (bf16[48,2240]{1,0:T(8,128)(2,1)S(1)}, bf16[48,2240]{1,0:T(8,128)(2,1)S(1)}, u32[]{:S(2)}, u32[]{:S(2)}) collective-permute-start(bf16[48,2240]{1,0:T(8,128)(2,1)S(1)} %get-tuple-element.498), channel_id=1, source_target_pairs={{0,2},{1,3},{2,0},{3,1},{4,6},{5,7},{6,4},{7,5},{8,10},{9,11},{10,... | collective-permute-start | bytes 645128 | tf_op jit(solution)/shard_map/ppermute | solution.py:68
  72.2 25.6 %collective-permute-start.10 = (bf16[48,2240]{1,0:T(8,128)(2,1)S(1)}, bf16[48,2240]{1,0:T(8,128)(2,1)S(1)}, u32[]{:S(2)}, u32[]{:S(2)}) collective-permute-start(bf16[48,2240]{1,0:T(8,128)(2,1)S(1)} %get-tuple-element.499), channel_id=1, source_target_pairs={{0,3},{1,0},{2,1},{3,2},{4,7},{5,4},{6,5},{7,6},{8,11},{9,8},{10,9... | collective-permute-start | bytes 645128 | tf_op jit(solution)/shard_map/ppermute | solution.py:68
  102.4 302.4 %reduce-scatter.2.cloned.1.call-start = ((), (), s32[]{:S(2)}) async-start(), calls=%async_computation.2 | async-start | bytes 7962624 | tf_op jit(solution)/shard_map/reduce_scatter | solution.py:983
  105.4 29.9 %collective-permute-start.13 = (bf16[4,1,4,48,1536]{4,3,2,1,0:T(8,128)(2,1)}, bf16[4,1,4,48,1536]{4,3,2,1,0:T(8,128)(2,1)}, u32[]{:S(2)}, u32[]{:S(2)}) collective-permute-start(bf16[4,1,4,48,1536]{4,3,2,1,0:T(8,128)(2,1)} %pad_maximum_fusion.1.pieces_ref), channel_id=1, source_target_pairs={{0,4},{4,0},{8,12},{12,8},{16,20},{20,16},{24,28},{28,24},{1,5},{5... | collective-permute-start | bytes 7077896 | tf_op jit(solution)/shard_map/ppermute | solution.py:68
  105.4 24.8 %collective-permute-start.11 = (bf16[160,1536]{1,0:T(8,128)(2,1)S(1)}, bf16[160,1536]{1,0:T(8,128)(2,1)}, u32[]{:S(2)}, u32[]{:S(2)}) collective-permute-start(bf16[160,1536]{1,0:T(8,128)(2,1)S(1)} %copy-done.17), channel_id=1, source_target_pairs={{0,1},{1,2},{2,3},{4,5},{5,6},{6,7},{8,9},{9,10},{10,11},{12,13},{... | collective-permute-start | bytes 1474568 | tf_op jit(solution)/shard_map/ppermute | solution.py:73
  135.2 27.7 %collective-permute-start.17 = (bf16[160,1536]{1,0:T(8,128)(2,1)}, bf16[160,1536]{1,0:T(8,128)(2,1)}, u32[]{:S(2)}, u32[]{:S(2)}) collective-permute-start(bf16[160,1536]{1,0:T(8,128)(2,1)} %collective-permute-done.11), channel_id=1, source_target_pairs={{0,1},{1,2},{2,3},{4,5},{5,6},{6,7},{8,9},{9,10},{10,11},{12,13},{... | collective-permute-start | bytes 1474568 | tf_op jit(solution)/shard_map/ppermute | solution.py:73
  137.4 25.6 %collective-permute-start.18 = (bf16[160,1536]{1,0:T(8,128)(2,1)}, bf16[160,1536]{1,0:T(8,128)(2,1)}, u32[]{:S(2)}, u32[]{:S(2)}) collective-permute-start(bf16[160,1536]{1,0:T(8,128)(2,1)} %collective-permute-done.12), channel_id=1, source_target_pairs={{1,0},{2,1},{3,2},{5,4},{6,5},{7,6},{9,8},{10,9},{11,10},{13,12},{... | collective-permute-start | bytes 1474568 | tf_op jit(solution)/shard_map/ppermute | solution.py:73
  163.0 24.2 %collective-permute-start.19 = (bf16[160,1536]{1,0:T(8,128)(2,1)}, bf16[160,1536]{1,0:T(8,128)(2,1)S(1)}, u32[]{:S(2)}, u32[]{:S(2)}) collective-permute-start(bf16[160,1536]{1,0:T(8,128)(2,1)} %collective-permute-done.17), channel_id=1, source_target_pairs={{0,1},{1,2},{2,3},{4,5},{5,6},{6,7},{8,9},{9,10},{10,11},{12,13},{... | collective-permute-start | bytes 1474568 | tf_op jit(solution)/shard_map/ppermute | solution.py:73
  190.0 32.0 %collective-permute-start.22 = (bf16[160,1536]{1,0:T(8,128)(2,1)S(1)}, bf16[160,1536]{1,0:T(8,128)(2,1)}, u32[]{:S(2)}, u32[]{:S(2)}) collective-permute-start(bf16[160,1536]{1,0:T(8,128)(2,1)S(1)} %multiply_convert_fusion), channel_id=1, source_target_pairs={{0,2},{1,3},{2,0},{3,1},{4,6},{5,7},{6,4},{7,5},{8,10},{9,11},{10,... | collective-permute-start | bytes 1474568 | tf_op jit(solution)/shard_map/ppermute | solution.py:68
  190.0 32.0 %collective-permute-start.23 = (bf16[160,1536]{1,0:T(8,128)(2,1)S(1)}, bf16[160,1536]{1,0:T(8,128)(2,1)}, u32[]{:S(2)}, u32[]{:S(2)}) collective-permute-start(bf16[160,1536]{1,0:T(8,128)(2,1)S(1)} %multiply_convert_fusion), channel_id=1, source_target_pairs={{0,3},{1,0},{2,1},{3,2},{4,7},{5,4},{6,5},{7,6},{8,11},{9,8},{10,9... | collective-permute-start | bytes 1474568 | tf_op jit(solution)/shard_map/ppermute | solution.py:68
  271.6 49.1 %collective-permute-start.25 = (bf16[2,4,48,2240]{3,2,1,0:T(8,128)(2,1)}, bf16[2,4,48,2240]{3,2,1,0:T(8,128)(2,1)}, u32[]{:S(2)}, u32[]{:S(2)}) collective-permute-start(bf16[2,4,48,2240]{3,2,1,0:T(8,128)(2,1)} %fusion), channel_id=1, source_target_pairs={{0,8},{4,20},{8,0},{12,28},{16,24},{20,4},{24,16},{28,12},{1,9},{5... | collective-permute-start | bytes 5160968 | tf_op jit(solution)/shard_map/ppermute | solution.py:68
  271.6 220.8 %all-gather.9.cloned.1.call-start = ((), (), s32[]{:S(2)}) async-start(), calls=%async_computation.3 | async-start | bytes 7741440 | tf_op jit(solution)/shard_map/all_gather | solution.py:995
  286.3 23.7 %collective-permute-start.26 = (bf16[160,1536]{1,0:T(8,128)(2,1)}, bf16[160,1536]{1,0:T(8,128)(2,1)S(1)}, u32[]{:S(2)}, u32[]{:S(2)}) collective-permute-start(bf16[160,1536]{1,0:T(8,128)(2,1)} %get-tuple-element.640), channel_id=1, source_target_pairs={{0,3},{1,0},{2,1},{3,2},{4,7},{5,4},{6,5},{7,6},{8,11},{9,8},{10,9... | collective-permute-start | bytes 1474568 | tf_op jit(solution)/shard_map/ppermute | solution.py:68
  298.0 22.7 %collective-permute-start.27 = (bf16[160,1536]{1,0:T(8,128)(2,1)}, bf16[160,1536]{1,0:T(8,128)(2,1)S(1)}, u32[]{:S(2)}, u32[]{:S(2)}) collective-permute-start(bf16[160,1536]{1,0:T(8,128)(2,1)} %get-tuple-element.641), channel_id=1, source_target_pairs={{0,1},{1,2},{2,3},{3,0},{4,5},{5,6},{6,7},{7,4},{8,9},{9,10},{10,1... | collective-permute-start | bytes 1474568 | tf_op jit(solution)/shard_map/ppermute | solution.py:68
  323.6 25.1 %collective-permute-start.29 = (bf16[2,2,1,280,1536]{4,3,2,1,0:T(8,128)(2,1)}, bf16[2,2,1,280,1536]{4,3,2,1,0:T(8,128)(2,1)}, u32[]{:S(2)}, u32[]{:S(2)}) collective-permute-start(bf16[2,2,1,280,1536]{4,3,2,1,0:T(8,128)(2,1)} %bitcast.53), channel_id=1, source_target_pairs={{0,4},{4,0},{8,12},{12,8},{16,20},{20,16},{24,28},{28,24},{1,5},{5... | collective-permute-start | bytes 10321928 | tf_op jit(solution)/shard_map/ppermute | solution.py:68
  323.7 25.0 %collective-permute-start.28 = (bf16[4,48,2240]{2,1,0:T(8,128)(2,1)}, bf16[4,48,2240]{2,1,0:T(8,128)(2,1)}, u32[]{:S(2)}, u32[]{:S(2)}) collective-permute-start(bf16[4,48,2240]{2,1,0:T(8,128)(2,1)} %fusion.3), channel_id=1, source_target_pairs={{0,16},{4,12},{8,24},{12,4},{16,0},{20,28},{24,8},{28,20},{1,17},{... | collective-permute-start | bytes 2580488 | tf_op jit(solution)/shard_map/ppermute | solution.py:68
  324.3 24.3 %collective-permute-start.30 = (bf16[160,1536]{1,0:T(8,128)(2,1)S(1)}, bf16[160,1536]{1,0:T(8,128)(2,1)S(1)}, u32[]{:S(2)}, u32[]{:S(2)}) collective-permute-start(bf16[160,1536]{1,0:T(8,128)(2,1)S(1)} %copy-done.43), channel_id=1, source_target_pairs={{0,2},{1,3},{2,0},{3,1},{4,6},{5,7},{6,4},{7,5},{8,10},{9,11},{10,... | collective-permute-start | bytes 1474568 | tf_op jit(solution)/shard_map/ppermute | solution.py:68
  354.5 22.4 %collective-permute-start.31 = (bf16[2,1,280,1536]{3,2,1,0:T(8,128)(2,1)}, bf16[2,1,280,1536]{3,2,1,0:T(8,128)(2,1)}, u32[]{:S(2)}, u32[]{:S(2)}) collective-permute-start(bf16[2,1,280,1536]{3,2,1,0:T(8,128)(2,1)} %bitcast.64), channel_id=1, source_target_pairs={{0,8},{4,20},{8,0},{12,28},{16,24},{20,4},{24,16},{28,12},{1,9},{5... | collective-permute-start | bytes 5160968 | tf_op jit(solution)/shard_map/ppermute | solution.py:68
  376.9 24.5 %collective-permute-start.38 = (bf16[2,2,4,48,1536]{4,3,2,1,0:T(8,128)(2,1)}, bf16[2,2,4,48,1536]{4,3,2,1,0:T(8,128)(2,1)}, u32[]{:S(2)}, u32[]{:S(2)}) collective-permute-start(bf16[2,2,4,48,1536]{4,3,2,1,0:T(8,128)(2,1)} %bitcast.256), channel_id=1, source_target_pairs={{0,4},{4,0},{8,12},{12,8},{16,20},{20,16},{24,28},{28,24},{1,5},{5... | collective-permute-start | bytes 7077896 | tf_op jit(solution)/shard_map/ppermute | solution.py:68
  404.7 194.9 %all-gather.13.cloned.1.call-start = ((), (), s32[]{:S(2)}) async-start(), calls=%async_computation.5 | async-start | bytes 7741440 | tf_op jit(solution)/shard_map/all_gather | solution.py:995
  412.6 28.2 %collective-permute-start.40 = (bf16[2,2,4,48,2048]{4,3,2,1,0:T(8,128)(2,1)}, bf16[2,2,4,48,2048]{4,3,2,1,0:T(8,128)(2,1)S(1)}, u32[]{:S(2)}, u32[]{:S(2)}) collective-permute-start(bf16[2,2,4,48,2048]{4,3,2,1,0:T(8,128)(2,1)} %bitcast.255), channel_id=1, source_target_pairs={{0,4},{4,0},{8,12},{12,8},{16,20},{20,16},{24,28},{28,24},{1,5},{5... | collective-permute-start | bytes 9437192 | tf_op jit(solution)/shard_map/ppermute | solution.py:68
  445.6 40.4 %collective-permute-start.45 = (bf16[2,4,48,2048]{3,2,1,0:T(8,128)(2,1)}, bf16[2,4,48,2048]{3,2,1,0:T(8,128)(2,1)}, u32[]{:S(2)}, u32[]{:S(2)}) collective-permute-start(bf16[2,4,48,2048]{3,2,1,0:T(8,128)(2,1)} %fusion.8), channel_id=1, source_target_pairs={{0,8},{4,20},{8,0},{12,28},{16,24},{20,4},{24,16},{28,12},{1,9},{5... | collective-permute-start | bytes 4718600 | tf_op jit(solution)/shard_map/ppermute | solution.py:68
  447.9 37.7 %collective-permute-start.47 = (bf16[48,8960]{1,0:T(8,128)(2,1)S(1)}, bf16[48,8960]{1,0:T(8,128)(2,1)S(1)}, u32[]{:S(2)}, u32[]{:S(2)}) collective-permute-start(bf16[48,8960]{1,0:T(8,128)(2,1)S(1)} %concatenate.68), channel_id=1, source_target_pairs={{0,16},{4,12},{8,24},{12,4},{16,0},{20,28},{24,8},{28,20},{1,17},{... | collective-permute-start | bytes 2580488 | tf_op jit(solution)/shard_map/ppermute | solution.py:68
  448.4 37.3 %collective-permute-start.46 = (bf16[4,48,1536]{2,1,0:T(8,128)(2,1)}, bf16[4,48,1536]{2,1,0:T(8,128)(2,1)}, u32[]{:S(2)}, u32[]{:S(2)}) collective-permute-start(bf16[4,48,1536]{2,1,0:T(8,128)(2,1)} %fusion.19), channel_id=1, source_target_pairs={{0,16},{4,12},{8,24},{12,4},{16,0},{20,28},{24,8},{28,20},{1,17},{... | collective-permute-start | bytes 1769480 | tf_op jit(solution)/shard_map/ppermute | solution.py:68
  450.0 23.4 %collective-permute-start.48 = (bf16[160,1536]{1,0:T(8,128)(2,1)}, bf16[160,1536]{1,0:T(8,128)(2,1)S(1)}, u32[]{:S(2)}, u32[]{:S(2)}) collective-permute-start(bf16[160,1536]{1,0:T(8,128)(2,1)} %get-tuple-element.791), channel_id=1, source_target_pairs={{0,2},{1,3},{2,0},{3,1},{4,6},{5,7},{6,4},{7,5},{8,10},{9,11},{10,... | collective-permute-start | bytes 1474568 | tf_op jit(solution)/shard_map/ppermute | solution.py:68
  492.4 45.7 %collective-permute-start.50 = (bf16[2,48,8960]{2,1,0:T(8,128)(2,1)}, bf16[2,48,8960]{2,1,0:T(8,128)(2,1)S(1)}, u32[]{:S(2)}, u32[]{:S(2)}) collective-permute-start(bf16[2,48,8960]{2,1,0:T(8,128)(2,1)} %pad_maximum_fusion.4), channel_id=1, source_target_pairs={{0,8},{4,20},{8,0},{12,28},{16,24},{20,4},{24,16},{28,12},{1,9},{5... | collective-permute-start | bytes 5160968 | tf_op jit(solution)/shard_map/ppermute | solution.py:68
  493.3 29.9 %collective-permute-start.49 = (bf16[4,48,2048]{2,1,0:T(8,128)(2,1)}, bf16[4,48,2048]{2,1,0:T(8,128)(2,1)S(1)}, u32[]{:S(2)}, u32[]{:S(2)}) collective-permute-start(bf16[4,48,2048]{2,1,0:T(8,128)(2,1)} %fusion.11), channel_id=1, source_target_pairs={{0,16},{4,12},{8,24},{12,4},{16,0},{20,28},{24,8},{28,20},{1,17},{... | collective-permute-start | bytes 2359304 | tf_op jit(solution)/shard_map/ppermute | solution.py:68
  (91 other events, 1306.7 us)
Sparse Core Ops, SparseCore 0:
  11.5 99.7 all-gather.10
  113.8 75.0 all-gather.6
  271.7 76.0 reduce-scatter.1
  404.9 54.4 all-gather.8
  492.6 60.4 all-gather.12

commit v17 on v16

--- a/solution.py
+++ b/solution.py
@@ -1099,6 +1099,9 @@
     (small,) = clock(
         jnp.concatenate([part.reshape(shards, -1) for part in small_parts], axis=1)
     )
+    (down_gathered,) = clock(down_gathered)
+    up_gathered = gather_rep(clock(up_piece)[0])
+    (down_total,) = clock.run(lambda gathered: widen_gathered(gathered, rep_places(reps)), down_gathered)
     projected_arrived, output_arrived, gate_arrived, block_arrived = clock.wait(
         projected.moving, output.moving, gate_spread.moving, block_moving
     )
@@ -1107,8 +1110,6 @@
     gate_spread.along(gate_arrived)
     output_blocks = clock(*blocks_of(output.finish(output_arrived)))
     output_moving = send_blocks(output_blocks)
-    (down_gathered,) = clock(down_gathered)
-    up_gathered = gather_rep(clock(up_piece)[0])
     projected_arrived, gate_arrived, output_rows = clock.wait(
         projected.moving, gate_spread.moving, output_moving
     )
@@ -1125,7 +1126,8 @@
     output_spread.along(output_arrived)
     small_moving = clock.send(core, [small], [1])
     block_moving = send_some(block_partial, edges[:1])
-    (gate_total,) = clock.run(widen_pieces, *gate_spread.finish(gate_arrived))
+    (up_gathered,) = clock(up_gathered)
+    (up_total,) = clock.run(lambda gathered: widen_gathered(gathered, rep_places(reps)), up_gathered)
     input_arrived, output_arrived, small_arrived, more_arrived = clock.wait(
         input_spread.moving, output_spread.moving, small_moving, block_moving
     )
@@ -1136,7 +1138,7 @@
     output_spread.over(output_arrived)
     small_moving = clock.send(first, [small] * (first.size - 1), range(1, first.size))
     block_moving = send_some(block_partial, edges[1:])
-    (down_total,) = clock.run(lambda gathered: widen_gathered(gathered, rep_places(reps)), down_gathered)
+    (gate_total,) = clock.run(widen_pieces, *gate_spread.finish(gate_arrived))
     input_arrived, output_arrived, small_arrived, more_arrived = clock.wait(
         input_spread.moving, output_spread.moving, small_moving, block_moving
     )
@@ -1151,8 +1153,6 @@
     small_blocks = clock(*blocks_of(total_of([small] + small_arrived)))
 
     small_moving = send_blocks(small_blocks)
-    (up_gathered,) = clock(up_gathered)
-    (up_total,) = clock.run(lambda gathered: widen_gathered(gathered, rep_places(reps)), up_gathered)
     (input_total,) = clock.run(widen_pieces, *input_spread.finish(input_arrived))
     (small_arrived,) = clock.wait(small_moving)
     small = total_of(small_blocks[:1] + small_arrived)

time: 629 us -> 636 us (1.011)
  starting transfers between devices: 127 us -> 138 us
    ppermute x66, starting transfers between devices: 101 us -> 113 us  [shift(): return lax.ppermute(value, self.name, self.pairs(step % self.size))]
    ppermute x66, waiting for transfers between devices: 225 us -> 213 us  [shift(): return lax.ppermute(value, self.name, self.pairs(step % self.size))]
    unnamed x103 -> x95, local copies, waits for them, and re-layouts: 12 us -> 13 us
  transfers between devices with their start and end apart: 77 -> 77, of which waited for: 29 -> 29; matrix products, arithmetic and copies ran while one was open for 13% -> 13% of each run, Pallas kernels for 19% -> 18%
where the time goes in v17:
time: 636 us; the launch traced here: 629 us
  waiting for transfers between devices  229 us (36%)
  Pallas kernels  149 us (23%)
  starting transfers between devices  138 us (22%)
  other arithmetic  56 us (9%)
  local copies, waits for them, and re-layouts  26.5 us (4%)
  between operations  15.3 us (2%)
  matrix products  15.2 us (2%)
    ppermute x66, waiting for transfers between devices, shift(): return lax.ppermute(value, self.name, self.pairs(step % self.size))  213 us
    ppermute x66, starting transfers between devices, shift(): return lax.ppermute(value, self.name, self.pairs(step % self.size))  113 us
    pallas_call x4, Pallas kernels, split_gradient(): pl.pallas_call(body, grid=(pl.cdiv(columns, TILE),), out_shape=[jax.Shape...  29.2 us
    ppermute x6, starting transfers between devices, pass_on(): return lax.ppermute(value, self.name, pairs)  25.2 us
    pallas_call x1, Pallas kernels, feed_forward(): pl.pallas_call(body, grid=(steps,), out_shape=[jax.ShapeDtypeStruct((coun...  23.7 us
    pallas_call x2, Pallas kernels, rows_product(): pl.pallas_call(body, grid=(pl.cdiv(columns, TILE),), out_shape=[jax.Shape...  23.2 us
    convert_element_type x8, other arithmetic, along(): total_of([pick(term, line.ahead(step), 0) for term in self.terms])  23 us
    pallas_call x3, Pallas kernels, widen_pieces(): pl.pallas_call(body, out_shape=jax.ShapeDtypeStruct((reps, rows, columns)...  13.8 us
  transfers between devices with their start and end apart: 77, of which 29 were waited for; matrix products, arithmetic and copies ran while one was open for 13% of the time, Pallas kernels for 18%

profile of v17, /device:TPU:0, one launch (start us, length us, event | category | flops | bytes accessed | tf_op | source)
XLA Modules:
  0.0 628.8 jit_solution(15893349109185087276)
XLA Ops:
  32.1 6.5 %collective-permute-start.4 = (bf16[48,2240]{1,0:T(8,128)(2,1)}, bf16[48,2240]{1,0:T(8,128)(2,1)S(1)}, u32[]{:S(2)}, u32[]{:S(2)}) collective-permute-start(bf16[48,2240]{1,0:T(8,128)(2,1)} %get-tuple-element.488), channel_id=1, source_target_pairs={{0,1},{1,2},{2,3},{3,0},{4,5},{5,6},{6,7},{7,4},{8,9},{9,10},{10,1... | collective-permute-start | bytes 645128 | tf_op jit(solution)/shard_map/ppermute | solution.py:68
  41.1 6.3 %collective-permute-done.4 = bf16[48,2240]{1,0:T(8,128)(2,1)S(1)} collective-permute-done((bf16[48,2240]{1,0:T(8,128)(2,1)}, bf16[48,2240]{1,0:T(8,128)(2,1)S(1)}, u32[]{:S(2)}, u32[]{:S(2)}) %collective-permute-start.4) | collective-permute-done | bytes 215072 | tf_op jit(solution)/shard_map/ppermute | solution.py:68
  47.4 13.9 %collective-permute-done.5 = bf16[48,2240]{1,0:T(8,128)(2,1)S(1)} collective-permute-done((bf16[48,2240]{1,0:T(8,128)(2,1)}, bf16[48,2240]{1,0:T(8,128)(2,1)S(1)}, u32[]{:S(2)}, u32[]{:S(2)}) %collective-permute-start.5) | collective-permute-done | bytes 215072 | tf_op jit(solution)/shard_map/ppermute | solution.py:68
  72.9 7.7 %collective-permute-done.8 = bf16[48,2240]{1,0:T(8,128)(2,1)S(1)} collective-permute-done((bf16[48,2240]{1,0:T(8,128)(2,1)S(1)}, bf16[48,2240]{1,0:T(8,128)(2,1)S(1)}, u32[]{:S(2)}, u32[]{:S(2)}) %collective-permute-start.8) | collective-permute-done | bytes 215072 | tf_op jit(solution)/shard_map/ppermute | solution.py:68
  80.6 17.2 %collective-permute-done.9 = bf16[48,2240]{1,0:T(8,128)(2,1)S(1)} collective-permute-done((bf16[48,2240]{1,0:T(8,128)(2,1)S(1)}, bf16[48,2240]{1,0:T(8,128)(2,1)S(1)}, u32[]{:S(2)}, u32[]{:S(2)}) %collective-permute-start.9) | collective-permute-done | bytes 215072 | tf_op jit(solution)/shard_map/ppermute | solution.py:68
  105.4 14.6 %collective-permute-start.11 = (bf16[160,1536]{1,0:T(8,128)(2,1)S(1)}, bf16[160,1536]{1,0:T(8,128)(2,1)}, u32[]{:S(2)}, u32[]{:S(2)}) collective-permute-start(bf16[160,1536]{1,0:T(8,128)(2,1)S(1)} %copy-done.16), channel_id=1, source_target_pairs={{0,1},{1,2},{2,3},{4,5},{5,6},{6,7},{8,9},{9,10},{10,11},{12,13},{... | collective-permute-start | bytes 1474568 | tf_op jit(solution)/shard_map/ppermute | solution.py:73
  146.2 8.8 %collective-permute-done.14 = bf16[160,512]{1,0:T(8,128)(2,1)S(1)} collective-permute-done((bf16[160,512]{1,0:T(8,128)(2,1)S(1)}, bf16[160,512]{1,0:T(8,128)(2,1)S(1)}, u32[]{:S(2)}, u32[]{:S(2)}) %collective-permute-start.14) | collective-permute-done | bytes 163872 | tf_op jit(solution)/shard_map/ppermute | solution.py:68
  155.0 8.0 %collective-permute-done.15 = bf16[160,512]{1,0:T(8,128)(2,1)} collective-permute-done((bf16[160,512]{1,0:T(8,128)(2,1)S(1)}, bf16[160,512]{1,0:T(8,128)(2,1)}, u32[]{:S(2)}, u32[]{:S(2)}) %collective-permute-start.15) | collective-permute-done | bytes 163872 | tf_op jit(solution)/shard_map/ppermute | solution.py:68
  195.2 11.7 %place_blocks.3 = (bf16[4,8,48,2240]{3,2,1,0:T(8,128)(2,1)}, bf16[4,8,48,2240]{3,2,1,0:T(8,128)(2,1)}) custom-call(s32[4]{0:T(128)} %pad_add_fusion.5.order_ref, bf16[64,48,2240]{2,1,0:T(8,128)(2,1)} %all-gather.7.cloned.1.call-done.source), custom_call_target="tpu_custom_call" | custom-call | flops 1 | bytes 1 | tf_op jit(solution)/shard_map/place_blocks/pallas_call | solution.py:339
  206.9 15.1 %collective-permute-done.22 = bf16[160,1536]{1,0:T(8,128)(2,1)} collective-permute-done((bf16[160,1536]{1,0:T(8,128)(2,1)S(1)}, bf16[160,1536]{1,0:T(8,128)(2,1)}, u32[]{:S(2)}, u32[]{:S(2)}) %collective-permute-start.22) | collective-permute-done | bytes 491552 | tf_op jit(solution)/shard_map/ppermute | solution.py:68
  224.7 23.7 %feed_forward.1 = (bf16[640,2240]{1,0:T(8,128)(2,1)}, bf16[640,2240]{1,0:T(8,128)(2,1)}, bf16[640,2240]{1,0:T(8,128)(2,1)}, bf16[1536,640]{1,0:T(8,128)(2,1)}, bf16[2240,640]{1,0:T(8,128)(2,1)}) custom-call(bf16[640,1536]{1,0:T(8,128)(2,1)} %pad_maximum_fusion.2.rows_ref, bf16[640,1536]{1,0:T(8,128)(2,1)} %pad_maximum_fusion.3.cotangents_ref.right_ref, ...), custom_call_target="tpu_custom_call" | custom-call | flops 1 | bytes 1 | tf_op jit(solution)/shard_map/feed_forward/pallas_call | solution.py:523
  248.4 10.1 %split_gradient.4 = (bf16[4,4,48,2240]{3,2,1,0:T(8,128)(2,1)}, bf16[4,4,48,2240]{3,2,1,0:T(8,128)(2,1)}) custom-call(s32[1]{0:T(128)} %bitcast.46.core_ref, bf16[1536,640]{1,0:T(8,128)(2,1)} %get-tuple-element.609.left_ref, bf16[640,2240]{1,0:T(8,128)(2,1)} %get-tuple-element.621.right_ref.refs_1_), custom_call_target="tpu_custom_call" | custom-call | flops 1 | bytes 1 | tf_op jit(solution)/shard_map/split_gradient/pallas_call | solution.py:579
  258.5 10.1 %ordered_gradient.1 = bf16[8,4,48,2240]{3,2,1,0:T(8,128)(2,1)} custom-call(bf16[1536,640]{1,0:T(8,128)(2,1)} %get-tuple-element.609.left_ref, bf16[640,2240]{1,0:T(8,128)(2,1)} %get-tuple-element.620.right_ref.refs_0_), custom_call_target="tpu_custom_call" | custom-call | flops 1 | bytes 1 | tf_op jit(solution)/shard_map/ordered_gradient/pallas_call | solution.py:609
  271.7 14.6 %rows_product.2 = (bf16[160,1536]{1,0:T(8,128)(2,1)}, bf16[160,1536]{1,0:T(8,128)(2,1)}, bf16[160,1536]{1,0:T(8,128)(2,1)}, bf16[160,1536]{1,0:T(8,128)(2,1)}) custom-call(bf16[640,2240]{1,0:T(8,128)(2,1)} %get-tuple-element.620.right_ref.refs_0_, bf16[640,2240]{1,0:T(8,128)(2,1)} %get-tuple-element.621.right_ref.refs_1_, bf16[1536,2240]{1,0:T(8,128)(2,1)} %bitcast.202, ...), custom_call_target="tpu_custom_call" | custom-call | flops 1 | bytes 1 | tf_op jit(solution)/shard_map/rows_product/pallas_call | solution.py:649
  286.3 11.8 %collective-permute-start.26 = (bf16[160,1536]{1,0:T(8,128)(2,1)}, bf16[160,1536]{1,0:T(8,128)(2,1)S(1)}, u32[]{:S(2)}, u32[]{:S(2)}) collective-permute-start(bf16[160,1536]{1,0:T(8,128)(2,1)} %get-tuple-element.640), channel_id=1, source_target_pairs={{0,3},{1,0},{2,1},{3,2},{4,7},{5,4},{6,5},{7,6},{8,11},{9,8},{10,9... | collective-permute-start | bytes 1474568 | tf_op jit(solution)/shard_map/ppermute | solution.py:68
  298.1 8.9 %split_gradient.5 = (bf16[4,1,280,1536]{3,2,1,0:T(8,128)(2,1)}, bf16[4,1,280,1536]{3,2,1,0:T(8,128)(2,1)}) custom-call(s32[1]{0:T(128)} %bitcast.46.core_ref, bf16[2240,640]{1,0:T(8,128)(2,1)} %get-tuple-element.634.left_ref, bf16[640,1536]{1,0:T(8,128)(2,1)} %pad_maximum_fusion.3.cotangents_ref.right_ref), custom_call_target="tpu_custom_call" | custom-call | flops 1 | bytes 1 | tf_op jit(solution)/shard_map/split_gradient/pallas_call | solution.py:579
  310.1 10.7 %collective-permute-done.27 = bf16[160,1536]{1,0:T(8,128)(2,1)S(1)} collective-permute-done((bf16[160,1536]{1,0:T(8,128)(2,1)}, bf16[160,1536]{1,0:T(8,128)(2,1)S(1)}, u32[]{:S(2)}, u32[]{:S(2)}) %collective-permute-start.27) | collective-permute-done | bytes 491552 | tf_op jit(solution)/shard_map/ppermute | solution.py:68
  328.5 8.6 %rows_product.3 = (bf16[160,1536]{1,0:T(8,128)(2,1)}, bf16[160,1536]{1,0:T(8,128)(2,1)}, bf16[160,1536]{1,0:T(8,128)(2,1)}, bf16[160,1536]{1,0:T(8,128)(2,1)}) custom-call(bf16[640,2240]{1,0:T(8,128)(2,1)} %get-tuple-element.651.refs_0_, bf16[2240,1536]{1,0:T(8,128)(2,1)} %refs_1_), custom_call_target="tpu_custom_call" | custom-call | flops 1 | bytes 1 | tf_op jit(solution)/shard_map/rows_product/pallas_call | solution.py:649
  337.1 11.7 %collective-permute-done.30 = bf16[160,1536]{1,0:T(8,128)(2,1)S(1)} collective-permute-done((bf16[160,1536]{1,0:T(8,128)(2,1)S(1)}, bf16[160,1536]{1,0:T(8,128)(2,1)S(1)}, u32[]{:S(2)}, u32[]{:S(2)}) %collective-permute-start.30) | collective-permute-done | bytes 491552 | tf_op jit(solution)/shard_map/ppermute | solution.py:68
  361.1 9.3 %collective-permute-start.34 = (bf16[48,2240]{1,0:T(8,128)(2,1)}, bf16[48,2240]{1,0:T(8,128)(2,1)S(1)}, u32[]{:S(2)}, u32[]{:S(2)}) collective-permute-start(bf16[48,2240]{1,0:T(8,128)(2,1)} %get-tuple-element.705), channel_id=1, source_target_pairs={{0,3},{1,0},{2,1},{3,2},{4,7},{5,4},{6,5},{7,6},{8,11},{9,8},{10,9... | collective-permute-start | bytes 645128 | tf_op jit(solution)/shard_map/ppermute | solution.py:68
  372.9 7.5 %attention_backward.1 = (bf16[160,1536]{1,0:T(8,128)(2,1)}, bf16[160,512]{1,0:T(8,128)(2,1)}, bf16[160,512]{1,0:T(8,128)(2,1)}, bf16[160,512]{1,0:T(8,128)(2,1)}, bf16[160,512]{1,0:T(8,128)(2,1)}) custom-call(bf16[2,960,128]{2,1,0:T(8,128)(2,1)} %get-tuple-element.683.queries_ref, bf16[160,1536]{1,0:T(8,128)(2,1)} %convolution_convert_fusion.gradient_ref, ...), custom_call_target="tpu_custom_call" | custom-call | flops 1 | bytes 1 | tf_op jit(solution)/shard_map/attention_backward/pallas_call | solution.py:751
  395.7 10.7 %collective-permute-done.36.refs_2_ = bf16[160,512]{1,0:T(8,128)(2,1)} collective-permute-done((bf16[160,512]{1,0:T(8,128)(2,1)}, bf16[160,512]{1,0:T(8,128)(2,1)}, u32[]{:S(2)}, u32[]{:S(2)}) %collective-permute-start.36) | collective-permute-done | bytes 163872 | tf_op jit(solution)/shard_map/ppermute | solution.py:68
  438.4 8.6 %collective-permute-done.43 = bf16[48,2240]{1,0:T(8,128)(2,1)S(1)} collective-permute-done((bf16[48,2240]{1,0:T(8,128)(2,1)}, bf16[48,2240]{1,0:T(8,128)(2,1)S(1)}, u32[]{:S(2)}, u32[]{:S(2)}) %collective-permute-start.43) | collective-permute-done | bytes 215072 | tf_op jit(solution)/shard_map/ppermute | solution.py:68
  455.0 6.0 all-gather.9.cloned.1.call-done.source_ref
  467.0 7.0 %widen_gathered.2 = f32[8,280,1536]{2,1,0:T(8,128)} custom-call(bf16[8,280,1536]{2,1,0:T(8,128)(2,1)} %all-gather.9.cloned.1.call-done.source_ref), custom_call_target="tpu_custom_call" | custom-call | flops 1 | bytes 1 | tf_op jit(solution)/shard_map/widen_gathered/pallas_call | solution.py:462
  474.1 14.0 %collective-permute-done.48 = bf16[160,1536]{1,0:T(8,128)(2,1)S(1)} collective-permute-done((bf16[160,1536]{1,0:T(8,128)(2,1)}, bf16[160,1536]{1,0:T(8,128)(2,1)S(1)}, u32[]{:S(2)}, u32[]{:S(2)}) %collective-permute-start.48) | collective-permute-done | bytes 491552 | tf_op jit(solution)/shard_map/ppermute | solution.py:68
  488.0 24.2 %collective-permute-done.46 = bf16[4,48,1536]{2,1,0:T(8,128)(2,1)S(1)} collective-permute-done((bf16[4,48,1536]{2,1,0:T(8,128)(2,1)}, bf16[4,48,1536]{2,1,0:T(8,128)(2,1)S(1)}, u32[]{:S(2)}, u32[]{:S(2)}) %collective-permute-start.46) | collective-permute-done | bytes 589856 | tf_op jit(solution)/shard_map/ppermute | solution.py:68
  532.1 11.3 %collective-permute-done.49 = bf16[4,48,2048]{2,1,0:T(8,128)(2,1)S(1)} collective-permute-done((bf16[4,48,2048]{2,1,0:T(8,128)(2,1)S(1)}, bf16[4,48,2048]{2,1,0:T(8,128)(2,1)S(1)}, u32[]{:S(2)}, u32[]{:S(2)}) %collective-permute-start.49) | collective-permute-done | bytes 786464 | tf_op jit(solution)/shard_map/ppermute | solution.py:68
  543.4 7.9 %collective-permute-done.50 = bf16[2,48,8960]{2,1,0:T(8,128)(2,1)S(1)} collective-permute-done((bf16[2,48,8960]{2,1,0:T(8,128)(2,1)S(1)}, bf16[2,48,8960]{2,1,0:T(8,128)(2,1)S(1)}, u32[]{:S(2)}, u32[]{:S(2)}) %collective-permute-start.50) | collective-permute-done | bytes 1720352 | tf_op jit(solution)/shard_map/ppermute | solution.py:68
  566.0 7.2 %collective-permute-done.55 = bf16[48,2048]{1,0:T(8,128)(2,1)S(1)} collective-permute-done((bf16[48,2048]{1,0:T(8,128)(2,1)S(1)}, bf16[48,2048]{1,0:T(8,128)(2,1)S(1)}, u32[]{:S(2)}, u32[]{:S(2)}) %collective-permute-start.55) | collective-permute-done | bytes 196640 | tf_op jit(solution)/shard_map/ppermute | solution.py:68
  581.5 6.6 %widen_gathered.3 = f32[8,48,8960]{2,1,0:T(8,128)} custom-call(bf16[8,48,8960]{2,1,0:T(8,128)(2,1)} %bitcast.213), custom_call_target="tpu_custom_call" | custom-call | flops 1 | bytes 1 | tf_op jit(solution)/shard_map/widen_gathered/pallas_call | solution.py:462
  593.7 7.3 %widen_pieces.3 = f32[8,48,8960]{2,1,0:T(8,128)} custom-call(s32[8]{0:T(128)} %stack.219.places_ref, bf16[4,48,8960]{2,1,0:T(8,128)(2,1)} %copy-done.2, bf16[4,48,8960]{2,1,0:T(8,128)(2,1)} %collective-permute-done.58.others_ref), custom_call_target="tpu_custom_call" | custom-call | flops 1 | bytes 1 | tf_op jit(solution)/shard_map/widen_pieces/pallas_call | solution.py:415
  (368 shorter events, 266.1 us)
Async XLA Ops:
  7.2 114.1 %all-gather.11.cloned.1.call-start = ((), (), s32[]{:S(2)}) async-start(), calls=%async_computation.4 | async-start | bytes 6488064 | tf_op jit(solution)/shard_map/all_gather | solution.py:842
  9.3 185.9 %all-gather.7.cloned.1.call-start = ((), (), s32[]{:S(2)}) async-start(), calls=%async_computation.1 | async-start | bytes 15925248 | tf_op jit(solution)/shard_map/all_gather | solution.py:907
  29.9 31.5 %collective-permute-start.3 = (bf16[1,4,48,1536]{3,2,1,0:T(8,128)(2,1)S(1)}, bf16[1,4,48,1536]{3,2,1,0:T(8,128)(2,1)S(1)}, u32[]{:S(2)}, u32[]{:S(2)}) collective-permute-start(bf16[1,4,48,1536]{3,2,1,0:T(8,128)(2,1)S(1)} %get-tuple-element.487), channel_id=1, source_target_pairs={{0,16},{4,12},{8,24},{12,4},{16,0},{20,28},{24,8},{28,20},{1,17},{... | collective-permute-start | bytes 1769480 | tf_op jit(solution)/shard_map/ppermute | solution.py:68
  61.5 36.3 %collective-permute-start.7 = (bf16[2,1,4,48,1536]{4,3,2,1,0:T(8,128)(2,1)S(1)}, bf16[2,1,4,48,1536]{4,3,2,1,0:T(8,128)(2,1)S(1)}, u32[]{:S(2)}, u32[]{:S(2)}) collective-permute-start(bf16[2,1,4,48,1536]{4,3,2,1,0:T(8,128)(2,1)S(1)} %pad_maximum_fusion.5), channel_id=1, source_target_pairs={{0,8},{4,20},{8,0},{12,28},{16,24},{20,4},{24,16},{28,12},{1,9},{5... | collective-permute-start | bytes 3538952 | tf_op jit(solution)/shard_map/ppermute | solution.py:68
  69.5 28.3 %collective-permute-start.9 = (bf16[48,2240]{1,0:T(8,128)(2,1)S(1)}, bf16[48,2240]{1,0:T(8,128)(2,1)S(1)}, u32[]{:S(2)}, u32[]{:S(2)}) collective-permute-start(bf16[48,2240]{1,0:T(8,128)(2,1)S(1)} %get-tuple-element.498), channel_id=1, source_target_pairs={{0,2},{1,3},{2,0},{3,1},{4,6},{5,7},{6,4},{7,5},{8,10},{9,11},{10,... | collective-permute-start | bytes 645128 | tf_op jit(solution)/shard_map/ppermute | solution.py:68
  72.2 25.6 %collective-permute-start.10 = (bf16[48,2240]{1,0:T(8,128)(2,1)S(1)}, bf16[48,2240]{1,0:T(8,128)(2,1)S(1)}, u32[]{:S(2)}, u32[]{:S(2)}) collective-permute-start(bf16[48,2240]{1,0:T(8,128)(2,1)S(1)} %get-tuple-element.499), channel_id=1, source_target_pairs={{0,3},{1,0},{2,1},{3,2},{4,7},{5,4},{6,5},{7,6},{8,11},{9,8},{10,9... | collective-permute-start | bytes 645128 | tf_op jit(solution)/shard_map/ppermute | solution.py:68
  102.4 307.3 %reduce-scatter.2.cloned.1.call-start = ((), (), s32[]{:S(2)}) async-start(), calls=%async_computation.2 | async-start | bytes 7962624 | tf_op jit(solution)/shard_map/reduce_scatter | solution.py:983
  105.4 29.9 %collective-permute-start.13 = (bf16[4,1,4,48,1536]{4,3,2,1,0:T(8,128)(2,1)}, bf16[4,1,4,48,1536]{4,3,2,1,0:T(8,128)(2,1)}, u32[]{:S(2)}, u32[]{:S(2)}) collective-permute-start(bf16[4,1,4,48,1536]{4,3,2,1,0:T(8,128)(2,1)} %pad_maximum_fusion.1.pieces_ref), channel_id=1, source_target_pairs={{0,4},{4,0},{8,12},{12,8},{16,20},{20,16},{24,28},{28,24},{1,5},{5... | collective-permute-start | bytes 7077896 | tf_op jit(solution)/shard_map/ppermute | solution.py:68
  105.4 24.8 %collective-permute-start.11 = (bf16[160,1536]{1,0:T(8,128)(2,1)S(1)}, bf16[160,1536]{1,0:T(8,128)(2,1)}, u32[]{:S(2)}, u32[]{:S(2)}) collective-permute-start(bf16[160,1536]{1,0:T(8,128)(2,1)S(1)} %copy-done.16), channel_id=1, source_target_pairs={{0,1},{1,2},{2,3},{4,5},{5,6},{6,7},{8,9},{9,10},{10,11},{12,13},{... | collective-permute-start | bytes 1474568 | tf_op jit(solution)/shard_map/ppermute | solution.py:73
  135.3 27.7 %collective-permute-start.17 = (bf16[160,1536]{1,0:T(8,128)(2,1)}, bf16[160,1536]{1,0:T(8,128)(2,1)}, u32[]{:S(2)}, u32[]{:S(2)}) collective-permute-start(bf16[160,1536]{1,0:T(8,128)(2,1)} %collective-permute-done.11), channel_id=1, source_target_pairs={{0,1},{1,2},{2,3},{4,5},{5,6},{6,7},{8,9},{9,10},{10,11},{12,13},{... | collective-permute-start | bytes 1474568 | tf_op jit(solution)/shard_map/ppermute | solution.py:73
  137.4 25.6 %collective-permute-start.18 = (bf16[160,1536]{1,0:T(8,128)(2,1)}, bf16[160,1536]{1,0:T(8,128)(2,1)}, u32[]{:S(2)}, u32[]{:S(2)}) collective-permute-start(bf16[160,1536]{1,0:T(8,128)(2,1)} %collective-permute-done.12), channel_id=1, source_target_pairs={{1,0},{2,1},{3,2},{5,4},{6,5},{7,6},{9,8},{10,9},{11,10},{13,12},{... | collective-permute-start | bytes 1474568 | tf_op jit(solution)/shard_map/ppermute | solution.py:73
  163.0 24.2 %collective-permute-start.19 = (bf16[160,1536]{1,0:T(8,128)(2,1)}, bf16[160,1536]{1,0:T(8,128)(2,1)S(1)}, u32[]{:S(2)}, u32[]{:S(2)}) collective-permute-start(bf16[160,1536]{1,0:T(8,128)(2,1)} %collective-permute-done.17), channel_id=1, source_target_pairs={{0,1},{1,2},{2,3},{4,5},{5,6},{6,7},{8,9},{9,10},{10,11},{12,13},{... | collective-permute-start | bytes 1474568 | tf_op jit(solution)/shard_map/ppermute | solution.py:73
  190.0 32.0 %collective-permute-start.22 = (bf16[160,1536]{1,0:T(8,128)(2,1)S(1)}, bf16[160,1536]{1,0:T(8,128)(2,1)}, u32[]{:S(2)}, u32[]{:S(2)}) collective-permute-start(bf16[160,1536]{1,0:T(8,128)(2,1)S(1)} %multiply_convert_fusion), channel_id=1, source_target_pairs={{0,2},{1,3},{2,0},{3,1},{4,6},{5,7},{6,4},{7,5},{8,10},{9,11},{10,... | collective-permute-start | bytes 1474568 | tf_op jit(solution)/shard_map/ppermute | solution.py:68
  190.0 32.0 %collective-permute-start.23 = (bf16[160,1536]{1,0:T(8,128)(2,1)S(1)}, bf16[160,1536]{1,0:T(8,128)(2,1)}, u32[]{:S(2)}, u32[]{:S(2)}) collective-permute-start(bf16[160,1536]{1,0:T(8,128)(2,1)S(1)} %multiply_convert_fusion), channel_id=1, source_target_pairs={{0,3},{1,0},{2,1},{3,2},{4,7},{5,4},{6,5},{7,6},{8,11},{9,8},{10,9... | collective-permute-start | bytes 1474568 | tf_op jit(solution)/shard_map/ppermute | solution.py:68
  271.6 49.2 %collective-permute-start.25 = (bf16[2,4,48,2240]{3,2,1,0:T(8,128)(2,1)}, bf16[2,4,48,2240]{3,2,1,0:T(8,128)(2,1)}, u32[]{:S(2)}, u32[]{:S(2)}) collective-permute-start(bf16[2,4,48,2240]{3,2,1,0:T(8,128)(2,1)} %fusion), channel_id=1, source_target_pairs={{0,8},{4,20},{8,0},{12,28},{16,24},{20,4},{24,16},{28,12},{1,9},{5... | collective-permute-start | bytes 5160968 | tf_op jit(solution)/shard_map/ppermute | solution.py:68
  271.7 189.4 %all-gather.9.cloned.1.call-start = ((), (), s32[]{:S(2)}) async-start(), calls=%async_computation.3 | async-start | bytes 7741440 | tf_op jit(solution)/shard_map/all_gather | solution.py:995
  286.3 23.8 %collective-permute-start.26 = (bf16[160,1536]{1,0:T(8,128)(2,1)}, bf16[160,1536]{1,0:T(8,128)(2,1)S(1)}, u32[]{:S(2)}, u32[]{:S(2)}) collective-permute-start(bf16[160,1536]{1,0:T(8,128)(2,1)} %get-tuple-element.640), channel_id=1, source_target_pairs={{0,3},{1,0},{2,1},{3,2},{4,7},{5,4},{6,5},{7,6},{8,11},{9,8},{10,9... | collective-permute-start | bytes 1474568 | tf_op jit(solution)/shard_map/ppermute | solution.py:68
  323.7 25.1 %collective-permute-start.29 = (bf16[2,2,1,280,1536]{4,3,2,1,0:T(8,128)(2,1)}, bf16[2,2,1,280,1536]{4,3,2,1,0:T(8,128)(2,1)}, u32[]{:S(2)}, u32[]{:S(2)}) collective-permute-start(bf16[2,2,1,280,1536]{4,3,2,1,0:T(8,128)(2,1)} %bitcast.53), channel_id=1, source_target_pairs={{0,4},{4,0},{8,12},{12,8},{16,20},{20,16},{24,28},{28,24},{1,5},{5... | collective-permute-start | bytes 10321928 | tf_op jit(solution)/shard_map/ppermute | solution.py:68
  323.8 25.0 %collective-permute-start.28 = (bf16[4,48,2240]{2,1,0:T(8,128)(2,1)}, bf16[4,48,2240]{2,1,0:T(8,128)(2,1)}, u32[]{:S(2)}, u32[]{:S(2)}) collective-permute-start(bf16[4,48,2240]{2,1,0:T(8,128)(2,1)} %fusion.3), channel_id=1, source_target_pairs={{0,16},{4,12},{8,24},{12,4},{16,0},{20,28},{24,8},{28,20},{1,17},{... | collective-permute-start | bytes 2580488 | tf_op jit(solution)/shard_map/ppermute | solution.py:68
  324.4 24.4 %collective-permute-start.30 = (bf16[160,1536]{1,0:T(8,128)(2,1)S(1)}, bf16[160,1536]{1,0:T(8,128)(2,1)S(1)}, u32[]{:S(2)}, u32[]{:S(2)}) collective-permute-start(bf16[160,1536]{1,0:T(8,128)(2,1)S(1)} %copy-done.39), channel_id=1, source_target_pairs={{0,2},{1,3},{2,0},{3,1},{4,6},{5,7},{6,4},{7,5},{8,10},{9,11},{10,... | collective-permute-start | bytes 1474568 | tf_op jit(solution)/shard_map/ppermute | solution.py:68
  354.6 30.5 %collective-permute-start.31 = (bf16[2,1,280,1536]{3,2,1,0:T(8,128)(2,1)}, bf16[2,1,280,1536]{3,2,1,0:T(8,128)(2,1)}, u32[]{:S(2)}, u32[]{:S(2)}) collective-permute-start(bf16[2,1,280,1536]{3,2,1,0:T(8,128)(2,1)} %bitcast.64), channel_id=1, source_target_pairs={{0,8},{4,20},{8,0},{12,28},{16,24},{20,4},{24,16},{28,12},{1,9},{5... | collective-permute-start | bytes 5160968 | tf_op jit(solution)/shard_map/ppermute | solution.py:68
  358.2 26.9 %collective-permute-start.32 = (bf16[48,2240]{1,0:T(8,128)(2,1)}, bf16[48,2240]{1,0:T(8,128)(2,1)S(1)}, u32[]{:S(2)}, u32[]{:S(2)}) collective-permute-start(bf16[48,2240]{1,0:T(8,128)(2,1)} %get-tuple-element.703), channel_id=1, source_target_pairs={{0,1},{1,2},{2,3},{3,0},{4,5},{5,6},{6,7},{7,4},{8,9},{9,10},{10,1... | collective-permute-start | bytes 645128 | tf_op jit(solution)/shard_map/ppermute | solution.py:68
  358.3 26.8 %collective-permute-start.33 = (bf16[48,2240]{1,0:T(8,128)(2,1)}, bf16[48,2240]{1,0:T(8,128)(2,1)S(1)}, u32[]{:S(2)}, u32[]{:S(2)}) collective-permute-start(bf16[48,2240]{1,0:T(8,128)(2,1)} %get-tuple-element.704), channel_id=1, source_target_pairs={{0,2},{1,3},{2,0},{3,1},{4,6},{5,7},{6,4},{7,5},{8,10},{9,11},{10,... | collective-permute-start | bytes 645128 | tf_op jit(solution)/shard_map/ppermute | solution.py:68
  361.1 24.0 %collective-permute-start.34 = (bf16[48,2240]{1,0:T(8,128)(2,1)}, bf16[48,2240]{1,0:T(8,128)(2,1)S(1)}, u32[]{:S(2)}, u32[]{:S(2)}) collective-permute-start(bf16[48,2240]{1,0:T(8,128)(2,1)} %get-tuple-element.705), channel_id=1, source_target_pairs={{0,3},{1,0},{2,1},{3,2},{4,7},{5,4},{6,5},{7,6},{8,11},{9,8},{10,9... | collective-permute-start | bytes 645128 | tf_op jit(solution)/shard_map/ppermute | solution.py:68
  409.7 171.8 %all-gather.13.cloned.1.call-start = ((), (), s32[]{:S(2)}) async-start(), calls=%async_computation.5 | async-start | bytes 7741440 | tf_op jit(solution)/shard_map/all_gather | solution.py:995
  417.6 29.4 %collective-permute-start.40 = (bf16[2,2,4,48,2048]{4,3,2,1,0:T(8,128)(2,1)}, bf16[2,2,4,48,2048]{4,3,2,1,0:T(8,128)(2,1)}, u32[]{:S(2)}, u32[]{:S(2)}) collective-permute-start(bf16[2,2,4,48,2048]{4,3,2,1,0:T(8,128)(2,1)} %bitcast.255), channel_id=1, source_target_pairs={{0,4},{4,0},{8,12},{12,8},{16,20},{20,16},{24,28},{28,24},{1,5},{5... | collective-permute-start | bytes 9437192 | tf_op jit(solution)/shard_map/ppermute | solution.py:68
  421.8 25.2 %collective-permute-start.41 = (bf16[2,4,48,1536]{3,2,1,0:T(8,128)(2,1)}, bf16[2,4,48,1536]{3,2,1,0:T(8,128)(2,1)}, u32[]{:S(2)}, u32[]{:S(2)}) collective-permute-start(bf16[2,4,48,1536]{3,2,1,0:T(8,128)(2,1)} %fusion.16), channel_id=1, source_target_pairs={{0,8},{4,20},{8,0},{12,28},{16,24},{20,4},{24,16},{28,12},{1,9},{5... | collective-permute-start | bytes 3538952 | tf_op jit(solution)/shard_map/ppermute | solution.py:68
  461.1 52.7 %collective-permute-start.45 = (bf16[2,4,48,2048]{3,2,1,0:T(8,128)(2,1)}, bf16[2,4,48,2048]{3,2,1,0:T(8,128)(2,1)}, u32[]{:S(2)}, u32[]{:S(2)}) collective-permute-start(bf16[2,4,48,2048]{3,2,1,0:T(8,128)(2,1)} %fusion.8), channel_id=1, source_target_pairs={{0,8},{4,20},{8,0},{12,28},{16,24},{20,4},{24,16},{28,12},{1,9},{5... | collective-permute-start | bytes 4718600 | tf_op jit(solution)/shard_map/ppermute | solution.py:68
  462.6 49.6 %collective-permute-start.47 = (bf16[48,8960]{1,0:T(8,128)(2,1)S(1)}, bf16[48,8960]{1,0:T(8,128)(2,1)S(1)}, u32[]{:S(2)}, u32[]{:S(2)}) collective-permute-start(bf16[48,8960]{1,0:T(8,128)(2,1)S(1)} %concatenate.68), channel_id=1, source_target_pairs={{0,16},{4,12},{8,24},{12,4},{16,0},{20,28},{24,8},{28,20},{1,17},{... | collective-permute-start | bytes 2580488 | tf_op jit(solution)/shard_map/ppermute | solution.py:68
  463.1 49.1 %collective-permute-start.46 = (bf16[4,48,1536]{2,1,0:T(8,128)(2,1)}, bf16[4,48,1536]{2,1,0:T(8,128)(2,1)S(1)}, u32[]{:S(2)}, u32[]{:S(2)}) collective-permute-start(bf16[4,48,1536]{2,1,0:T(8,128)(2,1)} %fusion.19), channel_id=1, source_target_pairs={{0,16},{4,12},{8,24},{12,4},{16,0},{20,28},{24,8},{28,20},{1,17},{... | collective-permute-start | bytes 1769480 | tf_op jit(solution)/shard_map/ppermute | solution.py:68
  515.7 35.6 %collective-permute-start.50 = (bf16[2,48,8960]{2,1,0:T(8,128)(2,1)S(1)}, bf16[2,48,8960]{2,1,0:T(8,128)(2,1)S(1)}, u32[]{:S(2)}, u32[]{:S(2)}) collective-permute-start(bf16[2,48,8960]{2,1,0:T(8,128)(2,1)S(1)} %pad_maximum_fusion.4), channel_id=1, source_target_pairs={{0,8},{4,20},{8,0},{12,28},{16,24},{20,4},{24,16},{28,12},{1,9},{5... | collective-permute-start | bytes 5160968 | tf_op jit(solution)/shard_map/ppermute | solution.py:68
  518.2 25.1 %collective-permute-start.49 = (bf16[4,48,2048]{2,1,0:T(8,128)(2,1)S(1)}, bf16[4,48,2048]{2,1,0:T(8,128)(2,1)S(1)}, u32[]{:S(2)}, u32[]{:S(2)}) collective-permute-start(bf16[4,48,2048]{2,1,0:T(8,128)(2,1)S(1)} %fusion.11), channel_id=1, source_target_pairs={{0,16},{4,12},{8,24},{12,4},{16,0},{20,28},{24,8},{28,20},{1,17},{... | collective-permute-start | bytes 2359304 | tf_op jit(solution)/shard_map/ppermute | solution.py:68
  (87 other events, 1270.0 us)
Sparse Core Ops, SparseCore 0:
  11.5 99.7 all-gather.10
  113.8 75.0 all-gather.6
  271.8 76.1 reduce-scatter.1
  409.8 51.1 all-gather.8
  462.9 70.2 all-gather.12

commit v18 on v17

--- a/solution.py
+++ b/solution.py
@@ -1100,7 +1100,6 @@
         jnp.concatenate([part.reshape(shards, -1) for part in small_parts], axis=1)
     )
     (down_gathered,) = clock(down_gathered)
-    up_gathered = gather_rep(clock(up_piece)[0])
     (down_total,) = clock.run(lambda gathered: widen_gathered(gathered, rep_places(reps)), down_gathered)
     projected_arrived, output_arrived, gate_arrived, block_arrived = clock.wait(
         projected.moving, output.moving, gate_spread.moving, block_moving
@@ -1110,6 +1109,7 @@
     gate_spread.along(gate_arrived)
     output_blocks = clock(*blocks_of(output.finish(output_arrived)))
     output_moving = send_blocks(output_blocks)
+    up_gathered = gather_rep(clock(up_piece)[0])
     projected_arrived, gate_arrived, output_rows = clock.wait(
         projected.moving, gate_spread.moving, output_moving
     )

time: 636 us -> 624 us (0.981)
  starting transfers between devices: 138 us -> 127 us
    ppermute x66, starting transfers between devices: 113 us -> 101 us  [shift(): return lax.ppermute(value, self.name, self.pairs(step % self.size))]
    unnamed x95 -> x101, local copies, waits for them, and re-layouts: 13 us -> 13.1 us
  transfers between devices with their start and end apart: 77 -> 77, of which waited for: 29 -> 31; matrix products, arithmetic and copies ran while one was open for 13% -> 12% of each run, Pallas kernels for 18% -> 19%
where the time goes in v18:
time: 624 us; the launch traced here: 614 us
  waiting for transfers between devices  227 us (36%)
  Pallas kernels  149 us (24%)
  starting transfers between devices  127 us (20%)
  other arithmetic  54.9 us (9%)
  local copies, waits for them, and re-layouts  25.8 us (4%)
  between operations  15.5 us (2%)
  matrix products  15.4 us (2%)
    ppermute x66, waiting for transfers between devices, shift(): return lax.ppermute(value, self.name, self.pairs(step % self.size))  209 us
    ppermute x66, starting transfers between devices, shift(): return lax.ppermute(value, self.name, self.pairs(step % self.size))  101 us
    pallas_call x4, Pallas kernels, split_gradient(): pl.pallas_call(body, grid=(pl.cdiv(columns, TILE),), out_shape=[jax.Shape...  29 us
    ppermute x6, starting transfers between devices, pass_on(): return lax.ppermute(value, self.name, pairs)  25.2 us
    pallas_call x1, Pallas kernels, feed_forward(): pl.pallas_call(body, grid=(steps,), out_shape=[jax.ShapeDtypeStruct((coun...  23.7 us
    pallas_call x2, Pallas kernels, rows_product(): pl.pallas_call(body, grid=(pl.cdiv(columns, TILE),), out_shape=[jax.Shape...  23.2 us
    convert_element_type x8, other arithmetic, along(): total_of([pick(term, line.ahead(step), 0) for term in self.terms])  21.5 us
    pallas_call x3, Pallas kernels, widen_pieces(): pl.pallas_call(body, out_shape=jax.ShapeDtypeStruct((reps, rows, columns)...  13.8 us
  transfers between devices with their start and end apart: 77, of which 31 were waited for; matrix products, arithmetic and copies ran while one was open for 12% of the time, Pallas kernels for 19%

profile of v18, /device:TPU:0, one launch (start us, length us, event | category | flops | bytes accessed | tf_op | source)
XLA Modules:
  0.0 614.1 jit_solution(5509920832466286610)
XLA Ops:
  32.1 6.5 %collective-permute-start.4 = (bf16[48,2240]{1,0:T(8,128)(2,1)}, bf16[48,2240]{1,0:T(8,128)(2,1)S(1)}, u32[]{:S(2)}, u32[]{:S(2)}) collective-permute-start(bf16[48,2240]{1,0:T(8,128)(2,1)} %get-tuple-element.486), channel_id=1, source_target_pairs={{0,1},{1,2},{2,3},{3,0},{4,5},{5,6},{6,7},{7,4},{8,9},{9,10},{10,1... | collective-permute-start | bytes 645128 | tf_op jit(solution)/shard_map/ppermute | solution.py:68
  41.1 6.3 %collective-permute-done.4 = bf16[48,2240]{1,0:T(8,128)(2,1)S(1)} collective-permute-done((bf16[48,2240]{1,0:T(8,128)(2,1)}, bf16[48,2240]{1,0:T(8,128)(2,1)S(1)}, u32[]{:S(2)}, u32[]{:S(2)}) %collective-permute-start.4) | collective-permute-done | bytes 215072 | tf_op jit(solution)/shard_map/ppermute | solution.py:68
  47.4 13.9 %collective-permute-done.5 = bf16[48,2240]{1,0:T(8,128)(2,1)S(1)} collective-permute-done((bf16[48,2240]{1,0:T(8,128)(2,1)}, bf16[48,2240]{1,0:T(8,128)(2,1)S(1)}, u32[]{:S(2)}, u32[]{:S(2)}) %collective-permute-start.5) | collective-permute-done | bytes 215072 | tf_op jit(solution)/shard_map/ppermute | solution.py:68
  72.9 7.6 %collective-permute-done.8 = bf16[48,2240]{1,0:T(8,128)(2,1)S(1)} collective-permute-done((bf16[48,2240]{1,0:T(8,128)(2,1)S(1)}, bf16[48,2240]{1,0:T(8,128)(2,1)S(1)}, u32[]{:S(2)}, u32[]{:S(2)}) %collective-permute-start.8) | collective-permute-done | bytes 215072 | tf_op jit(solution)/shard_map/ppermute | solution.py:68
  80.5 17.2 %collective-permute-done.9 = bf16[48,2240]{1,0:T(8,128)(2,1)S(1)} collective-permute-done((bf16[48,2240]{1,0:T(8,128)(2,1)S(1)}, bf16[48,2240]{1,0:T(8,128)(2,1)S(1)}, u32[]{:S(2)}, u32[]{:S(2)}) %collective-permute-start.9) | collective-permute-done | bytes 215072 | tf_op jit(solution)/shard_map/ppermute | solution.py:68
  105.4 14.6 %collective-permute-start.11 = (bf16[160,1536]{1,0:T(8,128)(2,1)S(1)}, bf16[160,1536]{1,0:T(8,128)(2,1)}, u32[]{:S(2)}, u32[]{:S(2)}) collective-permute-start(bf16[160,1536]{1,0:T(8,128)(2,1)S(1)} %copy-done.17), channel_id=1, source_target_pairs={{0,1},{1,2},{2,3},{4,5},{5,6},{6,7},{8,9},{9,10},{10,11},{12,13},{... | collective-permute-start | bytes 1474568 | tf_op jit(solution)/shard_map/ppermute | solution.py:73
  146.2 8.8 %collective-permute-done.14 = bf16[160,512]{1,0:T(8,128)(2,1)S(1)} collective-permute-done((bf16[160,512]{1,0:T(8,128)(2,1)S(1)}, bf16[160,512]{1,0:T(8,128)(2,1)S(1)}, u32[]{:S(2)}, u32[]{:S(2)}) %collective-permute-start.14) | collective-permute-done | bytes 163872 | tf_op jit(solution)/shard_map/ppermute | solution.py:68
  155.0 8.0 %collective-permute-done.15 = bf16[160,512]{1,0:T(8,128)(2,1)} collective-permute-done((bf16[160,512]{1,0:T(8,128)(2,1)S(1)}, bf16[160,512]{1,0:T(8,128)(2,1)}, u32[]{:S(2)}, u32[]{:S(2)}) %collective-permute-start.15) | collective-permute-done | bytes 163872 | tf_op jit(solution)/shard_map/ppermute | solution.py:68
  195.1 11.7 %place_blocks.3 = (bf16[4,8,48,2240]{3,2,1,0:T(8,128)(2,1)}, bf16[4,8,48,2240]{3,2,1,0:T(8,128)(2,1)}) custom-call(s32[4]{0:T(128)} %pad_add_fusion.5.order_ref, bf16[64,48,2240]{2,1,0:T(8,128)(2,1)} %all-gather.7.cloned.1.call-done.source), custom_call_target="tpu_custom_call" | custom-call | flops 1 | bytes 1 | tf_op jit(solution)/shard_map/place_blocks/pallas_call | solution.py:339
  206.8 15.1 %collective-permute-done.22 = bf16[160,1536]{1,0:T(8,128)(2,1)} collective-permute-done((bf16[160,1536]{1,0:T(8,128)(2,1)S(1)}, bf16[160,1536]{1,0:T(8,128)(2,1)}, u32[]{:S(2)}, u32[]{:S(2)}) %collective-permute-start.22) | collective-permute-done | bytes 491552 | tf_op jit(solution)/shard_map/ppermute | solution.py:68
  224.7 23.7 %feed_forward.1 = (bf16[640,2240]{1,0:T(8,128)(2,1)}, bf16[640,2240]{1,0:T(8,128)(2,1)}, bf16[640,2240]{1,0:T(8,128)(2,1)}, bf16[1536,640]{1,0:T(8,128)(2,1)}, bf16[2240,640]{1,0:T(8,128)(2,1)}) custom-call(bf16[640,1536]{1,0:T(8,128)(2,1)} %pad_maximum_fusion.2.rows_ref, bf16[640,1536]{1,0:T(8,128)(2,1)} %pad_maximum_fusion.3.cotangents_ref.right_ref, ...), custom_call_target="tpu_custom_call" | custom-call | flops 1 | bytes 1 | tf_op jit(solution)/shard_map/feed_forward/pallas_call | solution.py:523
  248.3 10.0 %split_gradient.4 = (bf16[4,4,48,2240]{3,2,1,0:T(8,128)(2,1)}, bf16[4,4,48,2240]{3,2,1,0:T(8,128)(2,1)}) custom-call(s32[1]{0:T(128)} %bitcast.46.core_ref, bf16[1536,640]{1,0:T(8,128)(2,1)} %get-tuple-element.607.left_ref, bf16[640,2240]{1,0:T(8,128)(2,1)} %get-tuple-element.619.right_ref.refs_1_), custom_call_target="tpu_custom_call" | custom-call | flops 1 | bytes 1 | tf_op jit(solution)/shard_map/split_gradient/pallas_call | solution.py:579
  258.3 10.1 %ordered_gradient.1 = bf16[8,4,48,2240]{3,2,1,0:T(8,128)(2,1)} custom-call(bf16[1536,640]{1,0:T(8,128)(2,1)} %get-tuple-element.607.left_ref, bf16[640,2240]{1,0:T(8,128)(2,1)} %get-tuple-element.618.right_ref.refs_0_), custom_call_target="tpu_custom_call" | custom-call | flops 1 | bytes 1 | tf_op jit(solution)/shard_map/ordered_gradient/pallas_call | solution.py:609
  271.6 14.6 %rows_product.2 = (bf16[160,1536]{1,0:T(8,128)(2,1)}, bf16[160,1536]{1,0:T(8,128)(2,1)}, bf16[160,1536]{1,0:T(8,128)(2,1)}, bf16[160,1536]{1,0:T(8,128)(2,1)}) custom-call(bf16[640,2240]{1,0:T(8,128)(2,1)} %get-tuple-element.618.right_ref.refs_0_, bf16[640,2240]{1,0:T(8,128)(2,1)} %get-tuple-element.619.right_ref.refs_1_, bf16[1536,2240]{1,0:T(8,128)(2,1)} %bitcast.202, ...), custom_call_target="tpu_custom_call" | custom-call | flops 1 | bytes 1 | tf_op jit(solution)/shard_map/rows_product/pallas_call | solution.py:649
  286.2 11.8 %collective-permute-start.26 = (bf16[160,1536]{1,0:T(8,128)(2,1)}, bf16[160,1536]{1,0:T(8,128)(2,1)S(1)}, u32[]{:S(2)}, u32[]{:S(2)}) collective-permute-start(bf16[160,1536]{1,0:T(8,128)(2,1)} %get-tuple-element.638), channel_id=1, source_target_pairs={{0,3},{1,0},{2,1},{3,2},{4,7},{5,4},{6,5},{7,6},{8,11},{9,8},{10,9... | collective-permute-start | bytes 1474568 | tf_op jit(solution)/shard_map/ppermute | solution.py:68
  298.0 8.9 %split_gradient.5 = (bf16[4,1,280,1536]{3,2,1,0:T(8,128)(2,1)}, bf16[4,1,280,1536]{3,2,1,0:T(8,128)(2,1)}) custom-call(s32[1]{0:T(128)} %bitcast.46.core_ref, bf16[2240,640]{1,0:T(8,128)(2,1)} %get-tuple-element.632.left_ref, bf16[640,1536]{1,0:T(8,128)(2,1)} %pad_maximum_fusion.3.cotangents_ref.right_ref), custom_call_target="tpu_custom_call" | custom-call | flops 1 | bytes 1 | tf_op jit(solution)/shard_map/split_gradient/pallas_call | solution.py:579
  310.0 10.7 %collective-permute-done.27 = bf16[160,1536]{1,0:T(8,128)(2,1)S(1)} collective-permute-done((bf16[160,1536]{1,0:T(8,128)(2,1)}, bf16[160,1536]{1,0:T(8,128)(2,1)S(1)}, u32[]{:S(2)}, u32[]{:S(2)}) %collective-permute-start.27) | collective-permute-done | bytes 491552 | tf_op jit(solution)/shard_map/ppermute | solution.py:68
  328.4 8.6 %rows_product.3 = (bf16[160,1536]{1,0:T(8,128)(2,1)}, bf16[160,1536]{1,0:T(8,128)(2,1)}, bf16[160,1536]{1,0:T(8,128)(2,1)}, bf16[160,1536]{1,0:T(8,128)(2,1)}) custom-call(bf16[640,2240]{1,0:T(8,128)(2,1)} %get-tuple-element.649.refs_0_, bf16[2240,1536]{1,0:T(8,128)(2,1)} %refs_1_), custom_call_target="tpu_custom_call" | custom-call | flops 1 | bytes 1 | tf_op jit(solution)/shard_map/rows_product/pallas_call | solution.py:649
  337.0 11.7 %collective-permute-done.30 = bf16[160,1536]{1,0:T(8,128)(2,1)S(1)} collective-permute-done((bf16[160,1536]{1,0:T(8,128)(2,1)S(1)}, bf16[160,1536]{1,0:T(8,128)(2,1)S(1)}, u32[]{:S(2)}, u32[]{:S(2)}) %collective-permute-start.30) | collective-permute-done | bytes 491552 | tf_op jit(solution)/shard_map/ppermute | solution.py:68
  364.6 7.6 %attention_backward.1 = (bf16[160,1536]{1,0:T(8,128)(2,1)}, bf16[160,512]{1,0:T(8,128)(2,1)}, bf16[160,512]{1,0:T(8,128)(2,1)}, bf16[160,512]{1,0:T(8,128)(2,1)}, bf16[160,512]{1,0:T(8,128)(2,1)}) custom-call(bf16[2,960,128]{2,1,0:T(8,128)(2,1)} %get-tuple-element.681.queries_ref, bf16[160,1536]{1,0:T(8,128)(2,1)} %convolution_convert_fusion.gradient_ref, ...), custom_call_target="tpu_custom_call" | custom-call | flops 1 | bytes 1 | tf_op jit(solution)/shard_map/attention_backward/pallas_call | solution.py:751
  389.6 11.7 %collective-permute-done.36.refs_2_ = bf16[160,512]{1,0:T(8,128)(2,1)} collective-permute-done((bf16[160,512]{1,0:T(8,128)(2,1)}, bf16[160,512]{1,0:T(8,128)(2,1)}, u32[]{:S(2)}, u32[]{:S(2)}) %collective-permute-start.36) | collective-permute-done | bytes 163872 | tf_op jit(solution)/shard_map/ppermute | solution.py:68
  426.0 7.5 %collective-permute-done.43 = bf16[48,2240]{1,0:T(8,128)(2,1)S(1)} collective-permute-done((bf16[48,2240]{1,0:T(8,128)(2,1)S(1)}, bf16[48,2240]{1,0:T(8,128)(2,1)S(1)}, u32[]{:S(2)}, u32[]{:S(2)}) %collective-permute-start.43) | collective-permute-done | bytes 215072 | tf_op jit(solution)/shard_map/ppermute | solution.py:68
  433.5 7.4 %collective-permute-done.41 = bf16[2,4,48,1536]{3,2,1,0:T(8,128)(2,1)S(1)} collective-permute-done((bf16[2,4,48,1536]{3,2,1,0:T(8,128)(2,1)S(1)}, bf16[2,4,48,1536]{3,2,1,0:T(8,128)(2,1)S(1)}, u32[]{:S(2)}, u32[]{:S(2)}) %collective-permute-start.41) | collective-permute-done | bytes 1179680 | tf_op jit(solution)/shard_map/ppermute | solution.py:68
  451.0 8.2 %all-gather.9.cloned.1.call-done.source_ref = bf16[8,280,1536]{2,1,0:T(8,128)(2,1)} async-done(((bf16[1,280,1536]{2,1,0:T(8,128)(2,1)}), bf16[8,280,1536]{2,1,0:T(8,128)(2,1)}) %all-gather.9.cloned.1.call-update) | async-done | bytes 6881296 | tf_op jit(solution)/shard_map/all_gather | solution.py:995
  459.2 7.0 %widen_gathered.2 = f32[8,280,1536]{2,1,0:T(8,128)} custom-call(bf16[8,280,1536]{2,1,0:T(8,128)(2,1)} %all-gather.9.cloned.1.call-done.source_ref), custom_call_target="tpu_custom_call" | custom-call | flops 1 | bytes 1 | tf_op jit(solution)/shard_map/widen_gathered/pallas_call | solution.py:462
  466.2 7.1 %collective-permute-done.48 = bf16[160,1536]{1,0:T(8,128)(2,1)S(1)} collective-permute-done((bf16[160,1536]{1,0:T(8,128)(2,1)}, bf16[160,1536]{1,0:T(8,128)(2,1)S(1)}, u32[]{:S(2)}, u32[]{:S(2)}) %collective-permute-start.48) | collective-permute-done | bytes 491552 | tf_op jit(solution)/shard_map/ppermute | solution.py:68
  473.3 12.2 %collective-permute-done.46 = bf16[4,48,1536]{2,1,0:T(8,128)(2,1)} collective-permute-done((bf16[4,48,1536]{2,1,0:T(8,128)(2,1)}, bf16[4,48,1536]{2,1,0:T(8,128)(2,1)}, u32[]{:S(2)}, u32[]{:S(2)}) %collective-permute-start.46) | collective-permute-done | bytes 589856 | tf_op jit(solution)/shard_map/ppermute | solution.py:68
  507.3 15.4 %collective-permute-done.49 = bf16[4,48,2048]{2,1,0:T(8,128)(2,1)S(1)} collective-permute-done((bf16[4,48,2048]{2,1,0:T(8,128)(2,1)}, bf16[4,48,2048]{2,1,0:T(8,128)(2,1)S(1)}, u32[]{:S(2)}, u32[]{:S(2)}) %collective-permute-start.49) | collective-permute-done | bytes 786464 | tf_op jit(solution)/shard_map/ppermute | solution.py:68
  522.7 14.9 %collective-permute-done.50 = bf16[2,48,8960]{2,1,0:T(8,128)(2,1)S(1)} collective-permute-done((bf16[2,48,8960]{2,1,0:T(8,128)(2,1)}, bf16[2,48,8960]{2,1,0:T(8,128)(2,1)S(1)}, u32[]{:S(2)}, u32[]{:S(2)}) %collective-permute-start.50) | collective-permute-done | bytes 1720352 | tf_op jit(solution)/shard_map/ppermute | solution.py:68
  551.7 7.5 %collective-permute-done.55 = bf16[48,2048]{1,0:T(8,128)(2,1)S(1)} collective-permute-done((bf16[48,2048]{1,0:T(8,128)(2,1)S(1)}, bf16[48,2048]{1,0:T(8,128)(2,1)S(1)}, u32[]{:S(2)}, u32[]{:S(2)}) %collective-permute-start.55) | collective-permute-done | bytes 196640 | tf_op jit(solution)/shard_map/ppermute | solution.py:68
  567.1 6.6 %widen_gathered.3 = f32[8,48,8960]{2,1,0:T(8,128)} custom-call(bf16[8,48,8960]{2,1,0:T(8,128)(2,1)} %bitcast.213), custom_call_target="tpu_custom_call" | custom-call | flops 1 | bytes 1 | tf_op jit(solution)/shard_map/widen_gathered/pallas_call | solution.py:462
  579.4 7.3 %widen_pieces.3 = f32[8,48,8960]{2,1,0:T(8,128)} custom-call(s32[8]{0:T(128)} %stack.219.places_ref, bf16[4,48,8960]{2,1,0:T(8,128)(2,1)} %copy-done.2, bf16[4,48,8960]{2,1,0:T(8,128)(2,1)} %collective-permute-done.58.others_ref), custom_call_target="tpu_custom_call" | custom-call | flops 1 | bytes 1 | tf_op jit(solution)/shard_map/widen_pieces/pallas_call | solution.py:415
  (374 shorter events, 258.4 us)
Async XLA Ops:
  7.2 114.1 %all-gather.11.cloned.1.call-start = ((), (), s32[]{:S(2)}) async-start(), calls=%async_computation.4 | async-start | bytes 6488064 | tf_op jit(solution)/shard_map/all_gather | solution.py:842
  9.3 185.8 %all-gather.7.cloned.1.call-start = ((), (), s32[]{:S(2)}) async-start(), calls=%async_computation.1 | async-start | bytes 15925248 | tf_op jit(solution)/shard_map/all_gather | solution.py:907
  29.9 31.5 %collective-permute-start.3 = (bf16[1,4,48,1536]{3,2,1,0:T(8,128)(2,1)S(1)}, bf16[1,4,48,1536]{3,2,1,0:T(8,128)(2,1)S(1)}, u32[]{:S(2)}, u32[]{:S(2)}) collective-permute-start(bf16[1,4,48,1536]{3,2,1,0:T(8,128)(2,1)S(1)} %get-tuple-element.485), channel_id=1, source_target_pairs={{0,16},{4,12},{8,24},{12,4},{16,0},{20,28},{24,8},{28,20},{1,17},{... | collective-permute-start | bytes 1769480 | tf_op jit(solution)/shard_map/ppermute | solution.py:68
  38.6 22.8 %collective-permute-start.5 = (bf16[48,2240]{1,0:T(8,128)(2,1)}, bf16[48,2240]{1,0:T(8,128)(2,1)S(1)}, u32[]{:S(2)}, u32[]{:S(2)}) collective-permute-start(bf16[48,2240]{1,0:T(8,128)(2,1)} %get-tuple-element.487), channel_id=1, source_target_pairs={{0,2},{1,3},{2,0},{3,1},{4,6},{5,7},{6,4},{7,5},{8,10},{9,11},{10,... | collective-permute-start | bytes 645128 | tf_op jit(solution)/shard_map/ppermute | solution.py:68
  61.5 36.3 %collective-permute-start.7 = (bf16[2,1,4,48,1536]{4,3,2,1,0:T(8,128)(2,1)S(1)}, bf16[2,1,4,48,1536]{4,3,2,1,0:T(8,128)(2,1)S(1)}, u32[]{:S(2)}, u32[]{:S(2)}) collective-permute-start(bf16[2,1,4,48,1536]{4,3,2,1,0:T(8,128)(2,1)S(1)} %pad_maximum_fusion.5), channel_id=1, source_target_pairs={{0,8},{4,20},{8,0},{12,28},{16,24},{20,4},{24,16},{28,12},{1,9},{5... | collective-permute-start | bytes 3538952 | tf_op jit(solution)/shard_map/ppermute | solution.py:68
  69.5 28.3 %collective-permute-start.9 = (bf16[48,2240]{1,0:T(8,128)(2,1)S(1)}, bf16[48,2240]{1,0:T(8,128)(2,1)S(1)}, u32[]{:S(2)}, u32[]{:S(2)}) collective-permute-start(bf16[48,2240]{1,0:T(8,128)(2,1)S(1)} %get-tuple-element.496), channel_id=1, source_target_pairs={{0,2},{1,3},{2,0},{3,1},{4,6},{5,7},{6,4},{7,5},{8,10},{9,11},{10,... | collective-permute-start | bytes 645128 | tf_op jit(solution)/shard_map/ppermute | solution.py:68
  72.2 25.6 %collective-permute-start.10 = (bf16[48,2240]{1,0:T(8,128)(2,1)S(1)}, bf16[48,2240]{1,0:T(8,128)(2,1)S(1)}, u32[]{:S(2)}, u32[]{:S(2)}) collective-permute-start(bf16[48,2240]{1,0:T(8,128)(2,1)S(1)} %get-tuple-element.497), channel_id=1, source_target_pairs={{0,3},{1,0},{2,1},{3,2},{4,7},{5,4},{6,5},{7,6},{8,11},{9,8},{10,9... | collective-permute-start | bytes 645128 | tf_op jit(solution)/shard_map/ppermute | solution.py:68
  102.4 302.3 %reduce-scatter.2.cloned.1.call-start = ((), (), s32[]{:S(2)}) async-start(), calls=%async_computation.2 | async-start | bytes 7962624 | tf_op jit(solution)/shard_map/reduce_scatter | solution.py:983
  105.4 29.9 %collective-permute-start.13 = (bf16[4,1,4,48,1536]{4,3,2,1,0:T(8,128)(2,1)}, bf16[4,1,4,48,1536]{4,3,2,1,0:T(8,128)(2,1)}, u32[]{:S(2)}, u32[]{:S(2)}) collective-permute-start(bf16[4,1,4,48,1536]{4,3,2,1,0:T(8,128)(2,1)} %pad_maximum_fusion.1.pieces_ref), channel_id=1, source_target_pairs={{0,4},{4,0},{8,12},{12,8},{16,20},{20,16},{24,28},{28,24},{1,5},{5... | collective-permute-start | bytes 7077896 | tf_op jit(solution)/shard_map/ppermute | solution.py:68
  105.4 24.8 %collective-permute-start.11 = (bf16[160,1536]{1,0:T(8,128)(2,1)S(1)}, bf16[160,1536]{1,0:T(8,128)(2,1)}, u32[]{:S(2)}, u32[]{:S(2)}) collective-permute-start(bf16[160,1536]{1,0:T(8,128)(2,1)S(1)} %copy-done.17), channel_id=1, source_target_pairs={{0,1},{1,2},{2,3},{4,5},{5,6},{6,7},{8,9},{9,10},{10,11},{12,13},{... | collective-permute-start | bytes 1474568 | tf_op jit(solution)/shard_map/ppermute | solution.py:73
  135.2 27.7 %collective-permute-start.17 = (bf16[160,1536]{1,0:T(8,128)(2,1)}, bf16[160,1536]{1,0:T(8,128)(2,1)}, u32[]{:S(2)}, u32[]{:S(2)}) collective-permute-start(bf16[160,1536]{1,0:T(8,128)(2,1)} %collective-permute-done.11), channel_id=1, source_target_pairs={{0,1},{1,2},{2,3},{4,5},{5,6},{6,7},{8,9},{9,10},{10,11},{12,13},{... | collective-permute-start | bytes 1474568 | tf_op jit(solution)/shard_map/ppermute | solution.py:73
  137.4 25.6 %collective-permute-start.18 = (bf16[160,1536]{1,0:T(8,128)(2,1)}, bf16[160,1536]{1,0:T(8,128)(2,1)}, u32[]{:S(2)}, u32[]{:S(2)}) collective-permute-start(bf16[160,1536]{1,0:T(8,128)(2,1)} %collective-permute-done.12), channel_id=1, source_target_pairs={{1,0},{2,1},{3,2},{5,4},{6,5},{7,6},{9,8},{10,9},{11,10},{13,12},{... | collective-permute-start | bytes 1474568 | tf_op jit(solution)/shard_map/ppermute | solution.py:73
  163.0 24.2 %collective-permute-start.19 = (bf16[160,1536]{1,0:T(8,128)(2,1)}, bf16[160,1536]{1,0:T(8,128)(2,1)S(1)}, u32[]{:S(2)}, u32[]{:S(2)}) collective-permute-start(bf16[160,1536]{1,0:T(8,128)(2,1)} %collective-permute-done.17), channel_id=1, source_target_pairs={{0,1},{1,2},{2,3},{4,5},{5,6},{6,7},{8,9},{9,10},{10,11},{12,13},{... | collective-permute-start | bytes 1474568 | tf_op jit(solution)/shard_map/ppermute | solution.py:73
  190.0 32.0 %collective-permute-start.22 = (bf16[160,1536]{1,0:T(8,128)(2,1)S(1)}, bf16[160,1536]{1,0:T(8,128)(2,1)}, u32[]{:S(2)}, u32[]{:S(2)}) collective-permute-start(bf16[160,1536]{1,0:T(8,128)(2,1)S(1)} %multiply_convert_fusion), channel_id=1, source_target_pairs={{0,2},{1,3},{2,0},{3,1},{4,6},{5,7},{6,4},{7,5},{8,10},{9,11},{10,... | collective-permute-start | bytes 1474568 | tf_op jit(solution)/shard_map/ppermute | solution.py:68
  190.0 32.0 %collective-permute-start.23 = (bf16[160,1536]{1,0:T(8,128)(2,1)S(1)}, bf16[160,1536]{1,0:T(8,128)(2,1)}, u32[]{:S(2)}, u32[]{:S(2)}) collective-permute-start(bf16[160,1536]{1,0:T(8,128)(2,1)S(1)} %multiply_convert_fusion), channel_id=1, source_target_pairs={{0,3},{1,0},{2,1},{3,2},{4,7},{5,4},{6,5},{7,6},{8,11},{9,8},{10,9... | collective-permute-start | bytes 1474568 | tf_op jit(solution)/shard_map/ppermute | solution.py:68
  271.5 49.2 %collective-permute-start.25 = (bf16[2,4,48,2240]{3,2,1,0:T(8,128)(2,1)}, bf16[2,4,48,2240]{3,2,1,0:T(8,128)(2,1)}, u32[]{:S(2)}, u32[]{:S(2)}) collective-permute-start(bf16[2,4,48,2240]{3,2,1,0:T(8,128)(2,1)} %fusion), channel_id=1, source_target_pairs={{0,8},{4,20},{8,0},{12,28},{16,24},{20,4},{24,16},{28,12},{1,9},{5... | collective-permute-start | bytes 5160968 | tf_op jit(solution)/shard_map/ppermute | solution.py:68
  271.5 187.6 %all-gather.9.cloned.1.call-start = ((), (), s32[]{:S(2)}) async-start(), calls=%async_computation.3 | async-start | bytes 7741440 | tf_op jit(solution)/shard_map/all_gather | solution.py:995
  286.2 23.8 %collective-permute-start.26 = (bf16[160,1536]{1,0:T(8,128)(2,1)}, bf16[160,1536]{1,0:T(8,128)(2,1)S(1)}, u32[]{:S(2)}, u32[]{:S(2)}) collective-permute-start(bf16[160,1536]{1,0:T(8,128)(2,1)} %get-tuple-element.638), channel_id=1, source_target_pairs={{0,3},{1,0},{2,1},{3,2},{4,7},{5,4},{6,5},{7,6},{8,11},{9,8},{10,9... | collective-permute-start | bytes 1474568 | tf_op jit(solution)/shard_map/ppermute | solution.py:68
  298.0 22.7 %collective-permute-start.27 = (bf16[160,1536]{1,0:T(8,128)(2,1)}, bf16[160,1536]{1,0:T(8,128)(2,1)S(1)}, u32[]{:S(2)}, u32[]{:S(2)}) collective-permute-start(bf16[160,1536]{1,0:T(8,128)(2,1)} %get-tuple-element.639), channel_id=1, source_target_pairs={{0,1},{1,2},{2,3},{3,0},{4,5},{5,6},{6,7},{7,4},{8,9},{9,10},{10,1... | collective-permute-start | bytes 1474568 | tf_op jit(solution)/shard_map/ppermute | solution.py:68
  323.6 25.1 %collective-permute-start.29 = (bf16[2,2,1,280,1536]{4,3,2,1,0:T(8,128)(2,1)}, bf16[2,2,1,280,1536]{4,3,2,1,0:T(8,128)(2,1)}, u32[]{:S(2)}, u32[]{:S(2)}) collective-permute-start(bf16[2,2,1,280,1536]{4,3,2,1,0:T(8,128)(2,1)} %bitcast.53), channel_id=1, source_target_pairs={{0,4},{4,0},{8,12},{12,8},{16,20},{20,16},{24,28},{28,24},{1,5},{5... | collective-permute-start | bytes 10321928 | tf_op jit(solution)/shard_map/ppermute | solution.py:68
  323.7 25.0 %collective-permute-start.28 = (bf16[4,48,2240]{2,1,0:T(8,128)(2,1)}, bf16[4,48,2240]{2,1,0:T(8,128)(2,1)}, u32[]{:S(2)}, u32[]{:S(2)}) collective-permute-start(bf16[4,48,2240]{2,1,0:T(8,128)(2,1)} %fusion.3), channel_id=1, source_target_pairs={{0,16},{4,12},{8,24},{12,4},{16,0},{20,28},{24,8},{28,20},{1,17},{... | collective-permute-start | bytes 2580488 | tf_op jit(solution)/shard_map/ppermute | solution.py:68
  324.3 24.4 %collective-permute-start.30 = (bf16[160,1536]{1,0:T(8,128)(2,1)S(1)}, bf16[160,1536]{1,0:T(8,128)(2,1)S(1)}, u32[]{:S(2)}, u32[]{:S(2)}) collective-permute-start(bf16[160,1536]{1,0:T(8,128)(2,1)S(1)} %copy-done.42), channel_id=1, source_target_pairs={{0,2},{1,3},{2,0},{3,1},{4,6},{5,7},{6,4},{7,5},{8,10},{9,11},{10,... | collective-permute-start | bytes 1474568 | tf_op jit(solution)/shard_map/ppermute | solution.py:68
  354.5 22.4 %collective-permute-start.31 = (bf16[2,1,280,1536]{3,2,1,0:T(8,128)(2,1)}, bf16[2,1,280,1536]{3,2,1,0:T(8,128)(2,1)}, u32[]{:S(2)}, u32[]{:S(2)}) collective-permute-start(bf16[2,1,280,1536]{3,2,1,0:T(8,128)(2,1)} %bitcast.64), channel_id=1, source_target_pairs={{0,8},{4,20},{8,0},{12,28},{16,24},{20,4},{24,16},{28,12},{1,9},{5... | collective-permute-start | bytes 5160968 | tf_op jit(solution)/shard_map/ppermute | solution.py:68
  376.9 24.5 %collective-permute-start.38 = (bf16[2,2,4,48,1536]{4,3,2,1,0:T(8,128)(2,1)}, bf16[2,2,4,48,1536]{4,3,2,1,0:T(8,128)(2,1)}, u32[]{:S(2)}, u32[]{:S(2)}) collective-permute-start(bf16[2,2,4,48,1536]{4,3,2,1,0:T(8,128)(2,1)} %bitcast.256), channel_id=1, source_target_pairs={{0,4},{4,0},{8,12},{12,8},{16,20},{20,16},{24,28},{28,24},{1,5},{5... | collective-permute-start | bytes 7077896 | tf_op jit(solution)/shard_map/ppermute | solution.py:68
  404.7 162.4 %all-gather.13.cloned.1.call-start = ((), (), s32[]{:S(2)}) async-start(), calls=%async_computation.5 | async-start | bytes 7741440 | tf_op jit(solution)/shard_map/all_gather | solution.py:995
  412.6 28.3 %collective-permute-start.40 = (bf16[2,2,4,48,2048]{4,3,2,1,0:T(8,128)(2,1)}, bf16[2,2,4,48,2048]{4,3,2,1,0:T(8,128)(2,1)S(1)}, u32[]{:S(2)}, u32[]{:S(2)}) collective-permute-start(bf16[2,2,4,48,2048]{4,3,2,1,0:T(8,128)(2,1)} %bitcast.255), channel_id=1, source_target_pairs={{0,4},{4,0},{8,12},{12,8},{16,20},{20,16},{24,28},{28,24},{1,5},{5... | collective-permute-start | bytes 9437192 | tf_op jit(solution)/shard_map/ppermute | solution.py:68
  445.7 40.2 %collective-permute-start.45 = (bf16[2,4,48,2048]{3,2,1,0:T(8,128)(2,1)}, bf16[2,4,48,2048]{3,2,1,0:T(8,128)(2,1)}, u32[]{:S(2)}, u32[]{:S(2)}) collective-permute-start(bf16[2,4,48,2048]{3,2,1,0:T(8,128)(2,1)} %fusion.8), channel_id=1, source_target_pairs={{0,8},{4,20},{8,0},{12,28},{16,24},{20,4},{24,16},{28,12},{1,9},{5... | collective-permute-start | bytes 4718600 | tf_op jit(solution)/shard_map/ppermute | solution.py:68
  447.8 37.7 %collective-permute-start.47 = (bf16[48,8960]{1,0:T(8,128)(2,1)S(1)}, bf16[48,8960]{1,0:T(8,128)(2,1)S(1)}, u32[]{:S(2)}, u32[]{:S(2)}) collective-permute-start(bf16[48,8960]{1,0:T(8,128)(2,1)S(1)} %concatenate.68), channel_id=1, source_target_pairs={{0,16},{4,12},{8,24},{12,4},{16,0},{20,28},{24,8},{28,20},{1,17},{... | collective-permute-start | bytes 2580488 | tf_op jit(solution)/shard_map/ppermute | solution.py:68
  448.1 37.4 %collective-permute-start.46 = (bf16[4,48,1536]{2,1,0:T(8,128)(2,1)}, bf16[4,48,1536]{2,1,0:T(8,128)(2,1)}, u32[]{:S(2)}, u32[]{:S(2)}) collective-permute-start(bf16[4,48,1536]{2,1,0:T(8,128)(2,1)} %fusion.19), channel_id=1, source_target_pairs={{0,16},{4,12},{8,24},{12,4},{16,0},{20,28},{24,8},{28,20},{1,17},{... | collective-permute-start | bytes 1769480 | tf_op jit(solution)/shard_map/ppermute | solution.py:68
  449.9 23.4 %collective-permute-start.48 = (bf16[160,1536]{1,0:T(8,128)(2,1)}, bf16[160,1536]{1,0:T(8,128)(2,1)S(1)}, u32[]{:S(2)}, u32[]{:S(2)}) collective-permute-start(bf16[160,1536]{1,0:T(8,128)(2,1)} %get-tuple-element.793), channel_id=1, source_target_pairs={{0,2},{1,3},{2,0},{3,1},{4,6},{5,7},{6,4},{7,5},{8,10},{9,11},{10,... | collective-permute-start | bytes 1474568 | tf_op jit(solution)/shard_map/ppermute | solution.py:68
  492.0 45.6 %collective-permute-start.50 = (bf16[2,48,8960]{2,1,0:T(8,128)(2,1)}, bf16[2,48,8960]{2,1,0:T(8,128)(2,1)S(1)}, u32[]{:S(2)}, u32[]{:S(2)}) collective-permute-start(bf16[2,48,8960]{2,1,0:T(8,128)(2,1)} %pad_maximum_fusion.4), channel_id=1, source_target_pairs={{0,8},{4,20},{8,0},{12,28},{16,24},{20,4},{24,16},{28,12},{1,9},{5... | collective-permute-start | bytes 5160968 | tf_op jit(solution)/shard_map/ppermute | solution.py:68
  492.8 29.9 %collective-permute-start.49 = (bf16[4,48,2048]{2,1,0:T(8,128)(2,1)}, bf16[4,48,2048]{2,1,0:T(8,128)(2,1)S(1)}, u32[]{:S(2)}, u32[]{:S(2)}) collective-permute-start(bf16[4,48,2048]{2,1,0:T(8,128)(2,1)} %fusion.11), channel_id=1, source_target_pairs={{0,16},{4,12},{8,24},{12,4},{16,0},{20,28},{24,8},{28,20},{1,17},{... | collective-permute-start | bytes 2359304 | tf_op jit(solution)/shard_map/ppermute | solution.py:68
  (90 other events, 1262.9 us)
Sparse Core Ops, SparseCore 0:
  11.5 99.7 all-gather.10
  113.8 75.0 all-gather.6
  271.7 76.1 reduce-scatter.1
  404.8 54.3 all-gather.8
  492.1 59.3 all-gather.12

commit v19 on v18

--- a/solution.py
+++ b/solution.py
@@ -384,7 +384,7 @@
 def widen_pieces(places, pieces, others):
     half, rows, columns = pieces.shape
     reps = 2 * half
-    strip = next(size for size in (16, 8, rows) if rows % size == 0)
+    strip = 16 if rows % 16 == 0 else rows
 
     def body(places_ref, pieces_ref, others_ref, out_ref, narrow, wide, in_sems, out_sems):
         loads = [
@@ -407,7 +407,10 @@
                 wide[r, cut, :] = narrow[r, cut, :].astype(jnp.float32)
                 return carry
 
-            lax.fori_loop(0, rows // strip, convert, 0)
+            if strip == rows:
+                wide[r] = narrow[r].astype(jnp.float32)
+            else:
+                lax.fori_loop(0, rows // strip, convert, 0)
             stores[r].start()
         for store in stores:
             store.wait()
@@ -433,7 +436,7 @@
 
 def widen_gathered(gathered, order):
     reps, rows, columns = gathered.shape
-    strip = next(size for size in (16, 8, rows) if rows % size == 0)
+    strip = 16 if rows % 16 == 0 else rows
 
     def body(source_ref, out_ref, narrow, wide, in_sems, out_sems):
         loads = [
@@ -454,7 +457,10 @@
                 wide[r, cut, :] = narrow[r, cut, :].astype(jnp.float32)
                 return carry
 
-            lax.fori_loop(0, rows // strip, convert, 0)
+            if strip == rows:
+                wide[r] = narrow[r].astype(jnp.float32)
+            else:
+                lax.fori_loop(0, rows // strip, convert, 0)
             stores[r].start()
         for store in stores:
             store.wait()

time: 624 us -> 624 us (level)
  no operation moved by 1% of the time
where the time goes in v19:
time: 624 us; the launch traced here: 614 us
  waiting for transfers between devices  227 us (36%)
  Pallas kernels  149 us (24%)
  starting transfers between devices  127 us (20%)
  other arithmetic  54.9 us (9%)
  local copies, waits for them, and re-layouts  25.8 us (4%)
  between operations  15.5 us (2%)
  matrix products  15.4 us (2%)
    ppermute x66, waiting for transfers between devices, shift(): return lax.ppermute(value, self.name, self.pairs(step % self.size))  209 us
    ppermute x66, starting transfers between devices, shift(): return lax.ppermute(value, self.name, self.pairs(step % self.size))  101 us
    pallas_call x4, Pallas kernels, split_gradient(): pl.pallas_call(body, grid=(pl.cdiv(columns, TILE),), out_shape=[jax.Shape...  29 us
    ppermute x6, starting transfers between devices, pass_on(): return lax.ppermute(value, self.name, pairs)  25.2 us
    pallas_call x1, Pallas kernels, feed_forward(): pl.pallas_call(body, grid=(steps,), out_shape=[jax.ShapeDtypeStruct((coun...  23.7 us
    pallas_call x2, Pallas kernels, rows_product(): pl.pallas_call(body, grid=(pl.cdiv(columns, TILE),), out_shape=[jax.Shape...  23.2 us
    convert_element_type x8, other arithmetic, along(): total_of([pick(term, line.ahead(step), 0) for term in self.terms])  21.5 us
    pallas_call x3, Pallas kernels, widen_pieces(): pl.pallas_call(body, out_shape=jax.ShapeDtypeStruct((reps, rows, columns)...  13.8 us
  transfers between devices with their start and end apart: 77, of which 31 were waited for; matrix products, arithmetic and copies ran while one was open for 12% of the time, Pallas kernels for 19%

profile of v19, /device:TPU:0, one launch (start us, length us, event | category | flops | bytes accessed | tf_op | source)
XLA Modules:
  0.0 614.1 jit_solution(949022818839234371)
XLA Ops:
  32.1 6.5 %collective-permute-start.4 = (bf16[48,2240]{1,0:T(8,128)(2,1)}, bf16[48,2240]{1,0:T(8,128)(2,1)S(1)}, u32[]{:S(2)}, u32[]{:S(2)}) collective-permute-start(bf16[48,2240]{1,0:T(8,128)(2,1)} %get-tuple-element.486), channel_id=1, source_target_pairs={{0,1},{1,2},{2,3},{3,0},{4,5},{5,6},{6,7},{7,4},{8,9},{9,10},{10,1... | collective-permute-start | bytes 645128 | tf_op jit(solution)/shard_map/ppermute | solution.py:68
  41.1 6.3 %collective-permute-done.4 = bf16[48,2240]{1,0:T(8,128)(2,1)S(1)} collective-permute-done((bf16[48,2240]{1,0:T(8,128)(2,1)}, bf16[48,2240]{1,0:T(8,128)(2,1)S(1)}, u32[]{:S(2)}, u32[]{:S(2)}) %collective-permute-start.4) | collective-permute-done | bytes 215072 | tf_op jit(solution)/shard_map/ppermute | solution.py:68
  47.4 13.9 %collective-permute-done.5 = bf16[48,2240]{1,0:T(8,128)(2,1)S(1)} collective-permute-done((bf16[48,2240]{1,0:T(8,128)(2,1)}, bf16[48,2240]{1,0:T(8,128)(2,1)S(1)}, u32[]{:S(2)}, u32[]{:S(2)}) %collective-permute-start.5) | collective-permute-done | bytes 215072 | tf_op jit(solution)/shard_map/ppermute | solution.py:68
  72.9 7.6 %collective-permute-done.8 = bf16[48,2240]{1,0:T(8,128)(2,1)S(1)} collective-permute-done((bf16[48,2240]{1,0:T(8,128)(2,1)S(1)}, bf16[48,2240]{1,0:T(8,128)(2,1)S(1)}, u32[]{:S(2)}, u32[]{:S(2)}) %collective-permute-start.8) | collective-permute-done | bytes 215072 | tf_op jit(solution)/shard_map/ppermute | solution.py:68
  80.5 17.2 %collective-permute-done.9 = bf16[48,2240]{1,0:T(8,128)(2,1)S(1)} collective-permute-done((bf16[48,2240]{1,0:T(8,128)(2,1)S(1)}, bf16[48,2240]{1,0:T(8,128)(2,1)S(1)}, u32[]{:S(2)}, u32[]{:S(2)}) %collective-permute-start.9) | collective-permute-done | bytes 215072 | tf_op jit(solution)/shard_map/ppermute | solution.py:68
  105.4 14.6 %collective-permute-start.11 = (bf16[160,1536]{1,0:T(8,128)(2,1)S(1)}, bf16[160,1536]{1,0:T(8,128)(2,1)}, u32[]{:S(2)}, u32[]{:S(2)}) collective-permute-start(bf16[160,1536]{1,0:T(8,128)(2,1)S(1)} %copy-done.17), channel_id=1, source_target_pairs={{0,1},{1,2},{2,3},{4,5},{5,6},{6,7},{8,9},{9,10},{10,11},{12,13},{... | collective-permute-start | bytes 1474568 | tf_op jit(solution)/shard_map/ppermute | solution.py:73
  146.2 8.8 %collective-permute-done.14 = bf16[160,512]{1,0:T(8,128)(2,1)S(1)} collective-permute-done((bf16[160,512]{1,0:T(8,128)(2,1)S(1)}, bf16[160,512]{1,0:T(8,128)(2,1)S(1)}, u32[]{:S(2)}, u32[]{:S(2)}) %collective-permute-start.14) | collective-permute-done | bytes 163872 | tf_op jit(solution)/shard_map/ppermute | solution.py:68
  155.0 8.0 %collective-permute-done.15 = bf16[160,512]{1,0:T(8,128)(2,1)} collective-permute-done((bf16[160,512]{1,0:T(8,128)(2,1)S(1)}, bf16[160,512]{1,0:T(8,128)(2,1)}, u32[]{:S(2)}, u32[]{:S(2)}) %collective-permute-start.15) | collective-permute-done | bytes 163872 | tf_op jit(solution)/shard_map/ppermute | solution.py:68
  195.1 11.7 %place_blocks.3 = (bf16[4,8,48,2240]{3,2,1,0:T(8,128)(2,1)}, bf16[4,8,48,2240]{3,2,1,0:T(8,128)(2,1)}) custom-call(s32[4]{0:T(128)} %pad_add_fusion.5.order_ref, bf16[64,48,2240]{2,1,0:T(8,128)(2,1)} %all-gather.7.cloned.1.call-done.source), custom_call_target="tpu_custom_call" | custom-call | flops 1 | bytes 1 | tf_op jit(solution)/shard_map/place_blocks/pallas_call | solution.py:339
  206.8 15.1 %collective-permute-done.22 = bf16[160,1536]{1,0:T(8,128)(2,1)} collective-permute-done((bf16[160,1536]{1,0:T(8,128)(2,1)S(1)}, bf16[160,1536]{1,0:T(8,128)(2,1)}, u32[]{:S(2)}, u32[]{:S(2)}) %collective-permute-start.22) | collective-permute-done | bytes 491552 | tf_op jit(solution)/shard_map/ppermute | solution.py:68
  224.7 23.7 %feed_forward.1 = (bf16[640,2240]{1,0:T(8,128)(2,1)}, bf16[640,2240]{1,0:T(8,128)(2,1)}, bf16[640,2240]{1,0:T(8,128)(2,1)}, bf16[1536,640]{1,0:T(8,128)(2,1)}, bf16[2240,640]{1,0:T(8,128)(2,1)}) custom-call(bf16[640,1536]{1,0:T(8,128)(2,1)} %pad_maximum_fusion.2.rows_ref, bf16[640,1536]{1,0:T(8,128)(2,1)} %pad_maximum_fusion.3.cotangents_ref.right_ref, ...), custom_call_target="tpu_custom_call" | custom-call | flops 1 | bytes 1 | tf_op jit(solution)/shard_map/feed_forward/pallas_call | solution.py:529
  248.3 10.0 %split_gradient.4 = (bf16[4,4,48,2240]{3,2,1,0:T(8,128)(2,1)}, bf16[4,4,48,2240]{3,2,1,0:T(8,128)(2,1)}) custom-call(s32[1]{0:T(128)} %bitcast.46.core_ref, bf16[1536,640]{1,0:T(8,128)(2,1)} %get-tuple-element.607.left_ref, bf16[640,2240]{1,0:T(8,128)(2,1)} %get-tuple-element.619.right_ref.refs_1_), custom_call_target="tpu_custom_call" | custom-call | flops 1 | bytes 1 | tf_op jit(solution)/shard_map/split_gradient/pallas_call | solution.py:585
  258.3 10.1 %ordered_gradient.1 = bf16[8,4,48,2240]{3,2,1,0:T(8,128)(2,1)} custom-call(bf16[1536,640]{1,0:T(8,128)(2,1)} %get-tuple-element.607.left_ref, bf16[640,2240]{1,0:T(8,128)(2,1)} %get-tuple-element.618.right_ref.refs_0_), custom_call_target="tpu_custom_call" | custom-call | flops 1 | bytes 1 | tf_op jit(solution)/shard_map/ordered_gradient/pallas_call | solution.py:615
  271.6 14.6 %rows_product.2 = (bf16[160,1536]{1,0:T(8,128)(2,1)}, bf16[160,1536]{1,0:T(8,128)(2,1)}, bf16[160,1536]{1,0:T(8,128)(2,1)}, bf16[160,1536]{1,0:T(8,128)(2,1)}) custom-call(bf16[640,2240]{1,0:T(8,128)(2,1)} %get-tuple-element.618.right_ref.refs_0_, bf16[640,2240]{1,0:T(8,128)(2,1)} %get-tuple-element.619.right_ref.refs_1_, bf16[1536,2240]{1,0:T(8,128)(2,1)} %bitcast.202, ...), custom_call_target="tpu_custom_call" | custom-call | flops 1 | bytes 1 | tf_op jit(solution)/shard_map/rows_product/pallas_call | solution.py:655
  286.2 11.8 %collective-permute-start.26 = (bf16[160,1536]{1,0:T(8,128)(2,1)}, bf16[160,1536]{1,0:T(8,128)(2,1)S(1)}, u32[]{:S(2)}, u32[]{:S(2)}) collective-permute-start(bf16[160,1536]{1,0:T(8,128)(2,1)} %get-tuple-element.638), channel_id=1, source_target_pairs={{0,3},{1,0},{2,1},{3,2},{4,7},{5,4},{6,5},{7,6},{8,11},{9,8},{10,9... | collective-permute-start | bytes 1474568 | tf_op jit(solution)/shard_map/ppermute | solution.py:68
  298.0 8.9 %split_gradient.5 = (bf16[4,1,280,1536]{3,2,1,0:T(8,128)(2,1)}, bf16[4,1,280,1536]{3,2,1,0:T(8,128)(2,1)}) custom-call(s32[1]{0:T(128)} %bitcast.46.core_ref, bf16[2240,640]{1,0:T(8,128)(2,1)} %get-tuple-element.632.left_ref, bf16[640,1536]{1,0:T(8,128)(2,1)} %pad_maximum_fusion.3.cotangents_ref.right_ref), custom_call_target="tpu_custom_call" | custom-call | flops 1 | bytes 1 | tf_op jit(solution)/shard_map/split_gradient/pallas_call | solution.py:585
  310.0 10.7 %collective-permute-done.27 = bf16[160,1536]{1,0:T(8,128)(2,1)S(1)} collective-permute-done((bf16[160,1536]{1,0:T(8,128)(2,1)}, bf16[160,1536]{1,0:T(8,128)(2,1)S(1)}, u32[]{:S(2)}, u32[]{:S(2)}) %collective-permute-start.27) | collective-permute-done | bytes 491552 | tf_op jit(solution)/shard_map/ppermute | solution.py:68
  328.4 8.6 %rows_product.3 = (bf16[160,1536]{1,0:T(8,128)(2,1)}, bf16[160,1536]{1,0:T(8,128)(2,1)}, bf16[160,1536]{1,0:T(8,128)(2,1)}, bf16[160,1536]{1,0:T(8,128)(2,1)}) custom-call(bf16[640,2240]{1,0:T(8,128)(2,1)} %get-tuple-element.649.refs_0_, bf16[2240,1536]{1,0:T(8,128)(2,1)} %refs_1_), custom_call_target="tpu_custom_call" | custom-call | flops 1 | bytes 1 | tf_op jit(solution)/shard_map/rows_product/pallas_call | solution.py:655
  337.0 11.7 %collective-permute-done.30 = bf16[160,1536]{1,0:T(8,128)(2,1)S(1)} collective-permute-done((bf16[160,1536]{1,0:T(8,128)(2,1)S(1)}, bf16[160,1536]{1,0:T(8,128)(2,1)S(1)}, u32[]{:S(2)}, u32[]{:S(2)}) %collective-permute-start.30) | collective-permute-done | bytes 491552 | tf_op jit(solution)/shard_map/ppermute | solution.py:68
  364.6 7.6 %attention_backward.1 = (bf16[160,1536]{1,0:T(8,128)(2,1)}, bf16[160,512]{1,0:T(8,128)(2,1)}, bf16[160,512]{1,0:T(8,128)(2,1)}, bf16[160,512]{1,0:T(8,128)(2,1)}, bf16[160,512]{1,0:T(8,128)(2,1)}) custom-call(bf16[2,960,128]{2,1,0:T(8,128)(2,1)} %get-tuple-element.681.queries_ref, bf16[160,1536]{1,0:T(8,128)(2,1)} %convolution_convert_fusion.gradient_ref, ...), custom_call_target="tpu_custom_call" | custom-call | flops 1 | bytes 1 | tf_op jit(solution)/shard_map/attention_backward/pallas_call | solution.py:757
  389.6 11.7 %collective-permute-done.36.refs_2_ = bf16[160,512]{1,0:T(8,128)(2,1)} collective-permute-done((bf16[160,512]{1,0:T(8,128)(2,1)}, bf16[160,512]{1,0:T(8,128)(2,1)}, u32[]{:S(2)}, u32[]{:S(2)}) %collective-permute-start.36) | collective-permute-done | bytes 163872 | tf_op jit(solution)/shard_map/ppermute | solution.py:68
  426.0 7.5 %collective-permute-done.43 = bf16[48,2240]{1,0:T(8,128)(2,1)S(1)} collective-permute-done((bf16[48,2240]{1,0:T(8,128)(2,1)S(1)}, bf16[48,2240]{1,0:T(8,128)(2,1)S(1)}, u32[]{:S(2)}, u32[]{:S(2)}) %collective-permute-start.43) | collective-permute-done | bytes 215072 | tf_op jit(solution)/shard_map/ppermute | solution.py:68
  433.5 7.4 %collective-permute-done.41 = bf16[2,4,48,1536]{3,2,1,0:T(8,128)(2,1)S(1)} collective-permute-done((bf16[2,4,48,1536]{3,2,1,0:T(8,128)(2,1)S(1)}, bf16[2,4,48,1536]{3,2,1,0:T(8,128)(2,1)S(1)}, u32[]{:S(2)}, u32[]{:S(2)}) %collective-permute-start.41) | collective-permute-done | bytes 1179680 | tf_op jit(solution)/shard_map/ppermute | solution.py:68
  451.0 8.2 %all-gather.9.cloned.1.call-done.source_ref = bf16[8,280,1536]{2,1,0:T(8,128)(2,1)} async-done(((bf16[1,280,1536]{2,1,0:T(8,128)(2,1)}), bf16[8,280,1536]{2,1,0:T(8,128)(2,1)}) %all-gather.9.cloned.1.call-update) | async-done | bytes 6881296 | tf_op jit(solution)/shard_map/all_gather | solution.py:1001
  459.2 7.0 %widen_gathered.2 = f32[8,280,1536]{2,1,0:T(8,128)} custom-call(bf16[8,280,1536]{2,1,0:T(8,128)(2,1)} %all-gather.9.cloned.1.call-done.source_ref), custom_call_target="tpu_custom_call" | custom-call | flops 1 | bytes 1 | tf_op jit(solution)/shard_map/widen_gathered/pallas_call | solution.py:468
  466.2 7.0 %collective-permute-done.48 = bf16[160,1536]{1,0:T(8,128)(2,1)S(1)} collective-permute-done((bf16[160,1536]{1,0:T(8,128)(2,1)}, bf16[160,1536]{1,0:T(8,128)(2,1)S(1)}, u32[]{:S(2)}, u32[]{:S(2)}) %collective-permute-start.48) | collective-permute-done | bytes 491552 | tf_op jit(solution)/shard_map/ppermute | solution.py:68
  473.3 12.2 %collective-permute-done.46 = bf16[4,48,1536]{2,1,0:T(8,128)(2,1)} collective-permute-done((bf16[4,48,1536]{2,1,0:T(8,128)(2,1)}, bf16[4,48,1536]{2,1,0:T(8,128)(2,1)}, u32[]{:S(2)}, u32[]{:S(2)}) %collective-permute-start.46) | collective-permute-done | bytes 589856 | tf_op jit(solution)/shard_map/ppermute | solution.py:68
  507.3 15.4 %collective-permute-done.49 = bf16[4,48,2048]{2,1,0:T(8,128)(2,1)S(1)} collective-permute-done((bf16[4,48,2048]{2,1,0:T(8,128)(2,1)}, bf16[4,48,2048]{2,1,0:T(8,128)(2,1)S(1)}, u32[]{:S(2)}, u32[]{:S(2)}) %collective-permute-start.49) | collective-permute-done | bytes 786464 | tf_op jit(solution)/shard_map/ppermute | solution.py:68
  522.7 14.9 %collective-permute-done.50 = bf16[2,48,8960]{2,1,0:T(8,128)(2,1)S(1)} collective-permute-done((bf16[2,48,8960]{2,1,0:T(8,128)(2,1)}, bf16[2,48,8960]{2,1,0:T(8,128)(2,1)S(1)}, u32[]{:S(2)}, u32[]{:S(2)}) %collective-permute-start.50) | collective-permute-done | bytes 1720352 | tf_op jit(solution)/shard_map/ppermute | solution.py:68
  551.7 7.5 %collective-permute-done.55 = bf16[48,2048]{1,0:T(8,128)(2,1)S(1)} collective-permute-done((bf16[48,2048]{1,0:T(8,128)(2,1)S(1)}, bf16[48,2048]{1,0:T(8,128)(2,1)S(1)}, u32[]{:S(2)}, u32[]{:S(2)}) %collective-permute-start.55) | collective-permute-done | bytes 196640 | tf_op jit(solution)/shard_map/ppermute | solution.py:68
  567.1 6.6 %widen_gathered.3 = f32[8,48,8960]{2,1,0:T(8,128)} custom-call(bf16[8,48,8960]{2,1,0:T(8,128)(2,1)} %bitcast.213), custom_call_target="tpu_custom_call" | custom-call | flops 1 | bytes 1 | tf_op jit(solution)/shard_map/widen_gathered/pallas_call | solution.py:468
  579.4 7.3 %widen_pieces.3 = f32[8,48,8960]{2,1,0:T(8,128)} custom-call(s32[8]{0:T(128)} %stack.219.places_ref, bf16[4,48,8960]{2,1,0:T(8,128)(2,1)} %copy-done.2, bf16[4,48,8960]{2,1,0:T(8,128)(2,1)} %collective-permute-done.58.others_ref), custom_call_target="tpu_custom_call" | custom-call | flops 1 | bytes 1 | tf_op jit(solution)/shard_map/widen_pieces/pallas_call | solution.py:418
  (374 shorter events, 258.4 us)
Async XLA Ops:
  7.2 114.1 %all-gather.11.cloned.1.call-start = ((), (), s32[]{:S(2)}) async-start(), calls=%async_computation.4 | async-start | bytes 6488064 | tf_op jit(solution)/shard_map/all_gather | solution.py:848
  9.3 185.8 %all-gather.7.cloned.1.call-start = ((), (), s32[]{:S(2)}) async-start(), calls=%async_computation.1 | async-start | bytes 15925248 | tf_op jit(solution)/shard_map/all_gather | solution.py:913
  29.9 31.5 %collective-permute-start.3 = (bf16[1,4,48,1536]{3,2,1,0:T(8,128)(2,1)S(1)}, bf16[1,4,48,1536]{3,2,1,0:T(8,128)(2,1)S(1)}, u32[]{:S(2)}, u32[]{:S(2)}) collective-permute-start(bf16[1,4,48,1536]{3,2,1,0:T(8,128)(2,1)S(1)} %get-tuple-element.485), channel_id=1, source_target_pairs={{0,16},{4,12},{8,24},{12,4},{16,0},{20,28},{24,8},{28,20},{1,17},{... | collective-permute-start | bytes 1769480 | tf_op jit(solution)/shard_map/ppermute | solution.py:68
  38.6 22.8 %collective-permute-start.5 = (bf16[48,2240]{1,0:T(8,128)(2,1)}, bf16[48,2240]{1,0:T(8,128)(2,1)S(1)}, u32[]{:S(2)}, u32[]{:S(2)}) collective-permute-start(bf16[48,2240]{1,0:T(8,128)(2,1)} %get-tuple-element.487), channel_id=1, source_target_pairs={{0,2},{1,3},{2,0},{3,1},{4,6},{5,7},{6,4},{7,5},{8,10},{9,11},{10,... | collective-permute-start | bytes 645128 | tf_op jit(solution)/shard_map/ppermute | solution.py:68
  61.5 36.3 %collective-permute-start.7 = (bf16[2,1,4,48,1536]{4,3,2,1,0:T(8,128)(2,1)S(1)}, bf16[2,1,4,48,1536]{4,3,2,1,0:T(8,128)(2,1)S(1)}, u32[]{:S(2)}, u32[]{:S(2)}) collective-permute-start(bf16[2,1,4,48,1536]{4,3,2,1,0:T(8,128)(2,1)S(1)} %pad_maximum_fusion.5), channel_id=1, source_target_pairs={{0,8},{4,20},{8,0},{12,28},{16,24},{20,4},{24,16},{28,12},{1,9},{5... | collective-permute-start | bytes 3538952 | tf_op jit(solution)/shard_map/ppermute | solution.py:68
  69.5 28.3 %collective-permute-start.9 = (bf16[48,2240]{1,0:T(8,128)(2,1)S(1)}, bf16[48,2240]{1,0:T(8,128)(2,1)S(1)}, u32[]{:S(2)}, u32[]{:S(2)}) collective-permute-start(bf16[48,2240]{1,0:T(8,128)(2,1)S(1)} %get-tuple-element.496), channel_id=1, source_target_pairs={{0,2},{1,3},{2,0},{3,1},{4,6},{5,7},{6,4},{7,5},{8,10},{9,11},{10,... | collective-permute-start | bytes 645128 | tf_op jit(solution)/shard_map/ppermute | solution.py:68
  72.2 25.6 %collective-permute-start.10 = (bf16[48,2240]{1,0:T(8,128)(2,1)S(1)}, bf16[48,2240]{1,0:T(8,128)(2,1)S(1)}, u32[]{:S(2)}, u32[]{:S(2)}) collective-permute-start(bf16[48,2240]{1,0:T(8,128)(2,1)S(1)} %get-tuple-element.497), channel_id=1, source_target_pairs={{0,3},{1,0},{2,1},{3,2},{4,7},{5,4},{6,5},{7,6},{8,11},{9,8},{10,9... | collective-permute-start | bytes 645128 | tf_op jit(solution)/shard_map/ppermute | solution.py:68
  102.4 302.3 %reduce-scatter.2.cloned.1.call-start = ((), (), s32[]{:S(2)}) async-start(), calls=%async_computation.2 | async-start | bytes 7962624 | tf_op jit(solution)/shard_map/reduce_scatter | solution.py:989
  105.4 29.9 %collective-permute-start.13 = (bf16[4,1,4,48,1536]{4,3,2,1,0:T(8,128)(2,1)}, bf16[4,1,4,48,1536]{4,3,2,1,0:T(8,128)(2,1)}, u32[]{:S(2)}, u32[]{:S(2)}) collective-permute-start(bf16[4,1,4,48,1536]{4,3,2,1,0:T(8,128)(2,1)} %pad_maximum_fusion.1.pieces_ref), channel_id=1, source_target_pairs={{0,4},{4,0},{8,12},{12,8},{16,20},{20,16},{24,28},{28,24},{1,5},{5... | collective-permute-start | bytes 7077896 | tf_op jit(solution)/shard_map/ppermute | solution.py:68
  105.4 24.8 %collective-permute-start.11 = (bf16[160,1536]{1,0:T(8,128)(2,1)S(1)}, bf16[160,1536]{1,0:T(8,128)(2,1)}, u32[]{:S(2)}, u32[]{:S(2)}) collective-permute-start(bf16[160,1536]{1,0:T(8,128)(2,1)S(1)} %copy-done.17), channel_id=1, source_target_pairs={{0,1},{1,2},{2,3},{4,5},{5,6},{6,7},{8,9},{9,10},{10,11},{12,13},{... | collective-permute-start | bytes 1474568 | tf_op jit(solution)/shard_map/ppermute | solution.py:73
  135.2 27.7 %collective-permute-start.17 = (bf16[160,1536]{1,0:T(8,128)(2,1)}, bf16[160,1536]{1,0:T(8,128)(2,1)}, u32[]{:S(2)}, u32[]{:S(2)}) collective-permute-start(bf16[160,1536]{1,0:T(8,128)(2,1)} %collective-permute-done.11), channel_id=1, source_target_pairs={{0,1},{1,2},{2,3},{4,5},{5,6},{6,7},{8,9},{9,10},{10,11},{12,13},{... | collective-permute-start | bytes 1474568 | tf_op jit(solution)/shard_map/ppermute | solution.py:73
  137.4 25.6 %collective-permute-start.18 = (bf16[160,1536]{1,0:T(8,128)(2,1)}, bf16[160,1536]{1,0:T(8,128)(2,1)}, u32[]{:S(2)}, u32[]{:S(2)}) collective-permute-start(bf16[160,1536]{1,0:T(8,128)(2,1)} %collective-permute-done.12), channel_id=1, source_target_pairs={{1,0},{2,1},{3,2},{5,4},{6,5},{7,6},{9,8},{10,9},{11,10},{13,12},{... | collective-permute-start | bytes 1474568 | tf_op jit(solution)/shard_map/ppermute | solution.py:73
  163.0 24.2 %collective-permute-start.19 = (bf16[160,1536]{1,0:T(8,128)(2,1)}, bf16[160,1536]{1,0:T(8,128)(2,1)S(1)}, u32[]{:S(2)}, u32[]{:S(2)}) collective-permute-start(bf16[160,1536]{1,0:T(8,128)(2,1)} %collective-permute-done.17), channel_id=1, source_target_pairs={{0,1},{1,2},{2,3},{4,5},{5,6},{6,7},{8,9},{9,10},{10,11},{12,13},{... | collective-permute-start | bytes 1474568 | tf_op jit(solution)/shard_map/ppermute | solution.py:73
  190.0 32.0 %collective-permute-start.22 = (bf16[160,1536]{1,0:T(8,128)(2,1)S(1)}, bf16[160,1536]{1,0:T(8,128)(2,1)}, u32[]{:S(2)}, u32[]{:S(2)}) collective-permute-start(bf16[160,1536]{1,0:T(8,128)(2,1)S(1)} %multiply_convert_fusion), channel_id=1, source_target_pairs={{0,2},{1,3},{2,0},{3,1},{4,6},{5,7},{6,4},{7,5},{8,10},{9,11},{10,... | collective-permute-start | bytes 1474568 | tf_op jit(solution)/shard_map/ppermute | solution.py:68
  190.0 32.0 %collective-permute-start.23 = (bf16[160,1536]{1,0:T(8,128)(2,1)S(1)}, bf16[160,1536]{1,0:T(8,128)(2,1)}, u32[]{:S(2)}, u32[]{:S(2)}) collective-permute-start(bf16[160,1536]{1,0:T(8,128)(2,1)S(1)} %multiply_convert_fusion), channel_id=1, source_target_pairs={{0,3},{1,0},{2,1},{3,2},{4,7},{5,4},{6,5},{7,6},{8,11},{9,8},{10,9... | collective-permute-start | bytes 1474568 | tf_op jit(solution)/shard_map/ppermute | solution.py:68
  271.5 49.2 %collective-permute-start.25 = (bf16[2,4,48,2240]{3,2,1,0:T(8,128)(2,1)}, bf16[2,4,48,2240]{3,2,1,0:T(8,128)(2,1)}, u32[]{:S(2)}, u32[]{:S(2)}) collective-permute-start(bf16[2,4,48,2240]{3,2,1,0:T(8,128)(2,1)} %fusion), channel_id=1, source_target_pairs={{0,8},{4,20},{8,0},{12,28},{16,24},{20,4},{24,16},{28,12},{1,9},{5... | collective-permute-start | bytes 5160968 | tf_op jit(solution)/shard_map/ppermute | solution.py:68
  271.5 187.6 %all-gather.9.cloned.1.call-start = ((), (), s32[]{:S(2)}) async-start(), calls=%async_computation.3 | async-start | bytes 7741440 | tf_op jit(solution)/shard_map/all_gather | solution.py:1001
  286.2 23.8 %collective-permute-start.26 = (bf16[160,1536]{1,0:T(8,128)(2,1)}, bf16[160,1536]{1,0:T(8,128)(2,1)S(1)}, u32[]{:S(2)}, u32[]{:S(2)}) collective-permute-start(bf16[160,1536]{1,0:T(8,128)(2,1)} %get-tuple-element.638), channel_id=1, source_target_pairs={{0,3},{1,0},{2,1},{3,2},{4,7},{5,4},{6,5},{7,6},{8,11},{9,8},{10,9... | collective-permute-start | bytes 1474568 | tf_op jit(solution)/shard_map/ppermute | solution.py:68
  298.0 22.7 %collective-permute-start.27 = (bf16[160,1536]{1,0:T(8,128)(2,1)}, bf16[160,1536]{1,0:T(8,128)(2,1)S(1)}, u32[]{:S(2)}, u32[]{:S(2)}) collective-permute-start(bf16[160,1536]{1,0:T(8,128)(2,1)} %get-tuple-element.639), channel_id=1, source_target_pairs={{0,1},{1,2},{2,3},{3,0},{4,5},{5,6},{6,7},{7,4},{8,9},{9,10},{10,1... | collective-permute-start | bytes 1474568 | tf_op jit(solution)/shard_map/ppermute | solution.py:68
  323.6 25.1 %collective-permute-start.29 = (bf16[2,2,1,280,1536]{4,3,2,1,0:T(8,128)(2,1)}, bf16[2,2,1,280,1536]{4,3,2,1,0:T(8,128)(2,1)}, u32[]{:S(2)}, u32[]{:S(2)}) collective-permute-start(bf16[2,2,1,280,1536]{4,3,2,1,0:T(8,128)(2,1)} %bitcast.53), channel_id=1, source_target_pairs={{0,4},{4,0},{8,12},{12,8},{16,20},{20,16},{24,28},{28,24},{1,5},{5... | collective-permute-start | bytes 10321928 | tf_op jit(solution)/shard_map/ppermute | solution.py:68
  323.7 25.0 %collective-permute-start.28 = (bf16[4,48,2240]{2,1,0:T(8,128)(2,1)}, bf16[4,48,2240]{2,1,0:T(8,128)(2,1)}, u32[]{:S(2)}, u32[]{:S(2)}) collective-permute-start(bf16[4,48,2240]{2,1,0:T(8,128)(2,1)} %fusion.3), channel_id=1, source_target_pairs={{0,16},{4,12},{8,24},{12,4},{16,0},{20,28},{24,8},{28,20},{1,17},{... | collective-permute-start | bytes 2580488 | tf_op jit(solution)/shard_map/ppermute | solution.py:68
  324.3 24.4 %collective-permute-start.30 = (bf16[160,1536]{1,0:T(8,128)(2,1)S(1)}, bf16[160,1536]{1,0:T(8,128)(2,1)S(1)}, u32[]{:S(2)}, u32[]{:S(2)}) collective-permute-start(bf16[160,1536]{1,0:T(8,128)(2,1)S(1)} %copy-done.42), channel_id=1, source_target_pairs={{0,2},{1,3},{2,0},{3,1},{4,6},{5,7},{6,4},{7,5},{8,10},{9,11},{10,... | collective-permute-start | bytes 1474568 | tf_op jit(solution)/shard_map/ppermute | solution.py:68
  354.5 22.4 %collective-permute-start.31 = (bf16[2,1,280,1536]{3,2,1,0:T(8,128)(2,1)}, bf16[2,1,280,1536]{3,2,1,0:T(8,128)(2,1)}, u32[]{:S(2)}, u32[]{:S(2)}) collective-permute-start(bf16[2,1,280,1536]{3,2,1,0:T(8,128)(2,1)} %bitcast.64), channel_id=1, source_target_pairs={{0,8},{4,20},{8,0},{12,28},{16,24},{20,4},{24,16},{28,12},{1,9},{5... | collective-permute-start | bytes 5160968 | tf_op jit(solution)/shard_map/ppermute | solution.py:68
  376.9 24.5 %collective-permute-start.38 = (bf16[2,2,4,48,1536]{4,3,2,1,0:T(8,128)(2,1)}, bf16[2,2,4,48,1536]{4,3,2,1,0:T(8,128)(2,1)}, u32[]{:S(2)}, u32[]{:S(2)}) collective-permute-start(bf16[2,2,4,48,1536]{4,3,2,1,0:T(8,128)(2,1)} %bitcast.256), channel_id=1, source_target_pairs={{0,4},{4,0},{8,12},{12,8},{16,20},{20,16},{24,28},{28,24},{1,5},{5... | collective-permute-start | bytes 7077896 | tf_op jit(solution)/shard_map/ppermute | solution.py:68
  404.7 162.4 %all-gather.13.cloned.1.call-start = ((), (), s32[]{:S(2)}) async-start(), calls=%async_computation.5 | async-start | bytes 7741440 | tf_op jit(solution)/shard_map/all_gather | solution.py:1001
  412.6 28.3 %collective-permute-start.40 = (bf16[2,2,4,48,2048]{4,3,2,1,0:T(8,128)(2,1)}, bf16[2,2,4,48,2048]{4,3,2,1,0:T(8,128)(2,1)S(1)}, u32[]{:S(2)}, u32[]{:S(2)}) collective-permute-start(bf16[2,2,4,48,2048]{4,3,2,1,0:T(8,128)(2,1)} %bitcast.255), channel_id=1, source_target_pairs={{0,4},{4,0},{8,12},{12,8},{16,20},{20,16},{24,28},{28,24},{1,5},{5... | collective-permute-start | bytes 9437192 | tf_op jit(solution)/shard_map/ppermute | solution.py:68
  445.7 40.2 %collective-permute-start.45 = (bf16[2,4,48,2048]{3,2,1,0:T(8,128)(2,1)}, bf16[2,4,48,2048]{3,2,1,0:T(8,128)(2,1)}, u32[]{:S(2)}, u32[]{:S(2)}) collective-permute-start(bf16[2,4,48,2048]{3,2,1,0:T(8,128)(2,1)} %fusion.8), channel_id=1, source_target_pairs={{0,8},{4,20},{8,0},{12,28},{16,24},{20,4},{24,16},{28,12},{1,9},{5... | collective-permute-start | bytes 4718600 | tf_op jit(solution)/shard_map/ppermute | solution.py:68
  447.8 37.7 %collective-permute-start.47 = (bf16[48,8960]{1,0:T(8,128)(2,1)S(1)}, bf16[48,8960]{1,0:T(8,128)(2,1)S(1)}, u32[]{:S(2)}, u32[]{:S(2)}) collective-permute-start(bf16[48,8960]{1,0:T(8,128)(2,1)S(1)} %concatenate.68), channel_id=1, source_target_pairs={{0,16},{4,12},{8,24},{12,4},{16,0},{20,28},{24,8},{28,20},{1,17},{... | collective-permute-start | bytes 2580488 | tf_op jit(solution)/shard_map/ppermute | solution.py:68
  448.1 37.4 %collective-permute-start.46 = (bf16[4,48,1536]{2,1,0:T(8,128)(2,1)}, bf16[4,48,1536]{2,1,0:T(8,128)(2,1)}, u32[]{:S(2)}, u32[]{:S(2)}) collective-permute-start(bf16[4,48,1536]{2,1,0:T(8,128)(2,1)} %fusion.19), channel_id=1, source_target_pairs={{0,16},{4,12},{8,24},{12,4},{16,0},{20,28},{24,8},{28,20},{1,17},{... | collective-permute-start | bytes 1769480 | tf_op jit(solution)/shard_map/ppermute | solution.py:68
  449.9 23.4 %collective-permute-start.48 = (bf16[160,1536]{1,0:T(8,128)(2,1)}, bf16[160,1536]{1,0:T(8,128)(2,1)S(1)}, u32[]{:S(2)}, u32[]{:S(2)}) collective-permute-start(bf16[160,1536]{1,0:T(8,128)(2,1)} %get-tuple-element.793), channel_id=1, source_target_pairs={{0,2},{1,3},{2,0},{3,1},{4,6},{5,7},{6,4},{7,5},{8,10},{9,11},{10,... | collective-permute-start | bytes 1474568 | tf_op jit(solution)/shard_map/ppermute | solution.py:68
  492.0 45.6 %collective-permute-start.50 = (bf16[2,48,8960]{2,1,0:T(8,128)(2,1)}, bf16[2,48,8960]{2,1,0:T(8,128)(2,1)S(1)}, u32[]{:S(2)}, u32[]{:S(2)}) collective-permute-start(bf16[2,48,8960]{2,1,0:T(8,128)(2,1)} %pad_maximum_fusion.4), channel_id=1, source_target_pairs={{0,8},{4,20},{8,0},{12,28},{16,24},{20,4},{24,16},{28,12},{1,9},{5... | collective-permute-start | bytes 5160968 | tf_op jit(solution)/shard_map/ppermute | solution.py:68
  492.8 29.9 %collective-permute-start.49 = (bf16[4,48,2048]{2,1,0:T(8,128)(2,1)}, bf16[4,48,2048]{2,1,0:T(8,128)(2,1)S(1)}, u32[]{:S(2)}, u32[]{:S(2)}) collective-permute-start(bf16[4,48,2048]{2,1,0:T(8,128)(2,1)} %fusion.11), channel_id=1, source_target_pairs={{0,16},{4,12},{8,24},{12,4},{16,0},{20,28},{24,8},{28,20},{1,17},{... | collective-permute-start | bytes 2359304 | tf_op jit(solution)/shard_map/ppermute | solution.py:68
  (90 other events, 1262.9 us)
Sparse Core Ops, SparseCore 0:
  11.5 99.7 all-gather.10
  113.8 75.0 all-gather.6
  271.7 76.1 reduce-scatter.1
  404.8 54.3 all-gather.8
  492.1 59.3 all-gather.12
